TPU v7x, 32 devices: a whole 2x2x4 slice. The times are simulated.
32 devices in a mesh: groups: 2 (over x), ind: 16 (over z, y, core).
Axes of the slice: x: 2, y: 2, z: 4, core: 2. Of those that a mesh axis runs over, the one named last changes fastest.
Arguments:
- genotype: bfloat16 [12288, 16384], P(('groups', 'ind')), parts along dimension 0, may hold values from -4 to 4
- residual: bfloat16 [12288, 256], P(('groups', 'ind')), parts along dimension 0, may hold values from -4 to 4
- labels: int32 [12288, 256], P(('groups', 'ind')), parts along dimension 0, may hold values 0 or 1
- incl_old: float32 [32768, 256], P(('groups', 'ind')), parts along dimension 0, may hold values from 0.02 to 0.98
- mean_old: float32 [32768, 256], P(('groups', 'ind')), parts along dimension 0, may hold values from -0.078125 to 0.078125
- prior_logit: float32 [256], replicated, may hold values from -4 to 0
- slab_scale: float32 [256], replicated, may hold values from 0.25 to 8
- offset: float32 [256], replicated, may hold values from -2 to 1
Outputs:
- incl_new: float32 [32768, 256], P(('groups', 'ind')), parts along dimension 0
- mean_new: float32 [32768, 256], P(('groups', 'ind')), parts along dimension 0
- resid_new: float32 [12288, 256], P(('groups', 'ind')), parts along dimension 0
There are 2 independent parts, one for each index of `groups`. A program takes and returns all parts, laid end to end along the dimension named above; an argument that names none is the same for every part. Nothing has to cross between parts.
All inputs are finite; a program needn't handle non-finite values. No bound on the sum of `labels` on one device may be relied on, other than what follows from the above.
Results may differ from a plain program's by a relative error of at most 0.00062.
Values may be sent and summed in bfloat16 or wider, within the bound.
No kernel may reach another device: no remote copies, remote signals or barrier semaphores. Data moves between devices by JAX's collectives and lax.ppermute only.
A program may use at most 128 MiB of HBM per device.

v0:
```python
import jax
import jax.numpy as jnp
from jax import lax
from jax.sharding import PartitionSpec as P


def update(corr, incl_part, mean_part, prior_part, scale_part, total):
    stat = corr / total + incl_part * mean_part
    shrink = scale_part / (1.0 + scale_part)
    mean_new = stat * shrink
    logit = prior_part - 0.5 * jnp.log1p(scale_part) + 0.5 * total * shrink * stat * stat
    incl_new = 0.5 * incl_part + 0.5 * jax.nn.sigmoid(logit)
    effect = (incl_new * mean_new).astype(jnp.bfloat16)
    return (incl_new, mean_new, effect)


def on_device(genotype, residual, labels, incl_old, mean_old, prior_logit, slab_scale, offset):
    total = genotype.shape[0] * lax.axis_size("ind")
    columns = genotype
    corr = lax.psum_scatter(
        lax.dot_general(
            columns, residual, (((0,), (0,)), ((), ())), preferred_element_type=jnp.float32
        ),
        "ind",
        scatter_dimension=0,
        tiled=True,
    )
    incl_new, mean_new, effect = update(corr, incl_old, mean_old, prior_logit, slab_scale, total)
    columns = genotype
    eta = jnp.dot(
        columns,
        lax.all_gather(effect, "ind", axis=0, tiled=True),
        preferred_element_type=jnp.float32,
    )
    eta = eta + offset
    resid_new = 4.0 * (labels.astype(jnp.float32) - jax.nn.sigmoid(eta))
    return (incl_new, mean_new, resid_new)


def solution(mesh):
    placed = (
        P(("groups", "ind"), None),
        P(("groups", "ind"), None),
        P(("groups", "ind"), None),
        P(("groups", "ind"), None),
        P(("groups", "ind"), None),
        P(),
        P(),
        P(),
    )
    return jax.shard_map(
        on_device,
        mesh=mesh,
        in_specs=placed,
        out_specs=(
            P(("groups", "ind"), None),
            P(("groups", "ind"), None),
            P(("groups", "ind"), None),
        ),
        check_vma=False,
    )
```

profile of v0, /device:TPU:0, one launch (start us, length us, event | category | flops | bytes accessed | tf_op | source)
XLA Modules:
  0.0 303.0 jit_solution(4936477498398542598)
XLA Ops:
  7.2 0.0 copy-start
  7.2 0.0 reduce-scatter.2.cloned.1.call-start
  7.2 0.9 copy-done
  8.1 14.9 %fusion.15 = f32[16384,256]{1,0:T(8,128)} fusion(bf16[384,16384]{1,0:T(8,128)(2,1)} %param.8, bf16[384,256]{1,0:T(8,128)(2,1)S(1)} %copy-done), kind=kOutput, calls=%fused_computation.22 | convolution fusion | flops 3221225472 | bytes 29556736 | tf_op jit(solution)/shard_map/dot_general | solution.py:21
  23.0 0.0 copy-start.4
  23.0 0.0 copy-start.5
  23.0 0.0 copy-start.1
  23.0 0.0 copy-start.2
  23.0 0.0 copy-start.3
  23.0 0.0 copy-start.6
  23.0 0.0 reduce-scatter.2.cloned.1.call-update
  23.0 0.0 all-gather.2.cloned.1.call-start
  23.1 0.6 copy-done.4
  23.7 0.0 copy-done.5
  23.7 180.8 %reduce-scatter.2.cloned.1.call-done = f32[1024,256]{1,0:T(8,128)} async-done(((f32[16384,256]{1,0:T(8,128)}), f32[1024,256]{1,0:T(8,128)}) %reduce-scatter.2.cloned.1.call-update) | async-done | bytes 1048592 | tf_op jit(solution)/shard_map/reduce_scatter | solution.py:20
  204.4 0.0 copy-done.1
  204.4 0.0 copy-done.2
  204.5 3.0 %multiply_convert_fusion = (bf16[1024,256]{1,0:T(8,128)(2,1)}, f32[1024,256]{1,0:T(8,128)}, f32[1024,256]{1,0:T(8,128)}) fusion(f32[256]{0:T(256)S(1)} %get-tuple-element.10, f32[1024,256]{1,0:T(8,128)S(1)} %copy-done.1, f32[1024,256]{1,0:T(8,128)S(1)} %copy-done.2, f32[1024,256]{1,0:T(8,128)} %reduce-scatter.2.cloned.1.call-done, ...), kind=kLoop, calls=%fused_computation.15 | loop fusion | flops 3670016 | bytes 5770240 | tf_op jit(solution)/shard_map/convert_element_type | solution.py:13
  207.5 0.0 all-gather.2.cloned.1.call-update
  207.5 0.0 copy-done.3
  207.5 0.2 copy.11
  207.7 73.9 %all-gather.2.cloned.1.call-done = bf16[16384,256]{1,0:T(8,128)(2,1)} async-done(((bf16[1024,256]{1,0:T(8,128)(2,1)}), bf16[16384,256]{1,0:T(8,128)(2,1)}) %all-gather.2.cloned.1.call-update) | async-done | bytes 8388624 | tf_op jit(solution)/shard_map/all_gather | solution.py:32
  281.6 0.0 copy-done.6
  281.6 13.6 %fusion.6 = f32[384,256]{0,1:T(8,128)S(1)} fusion(bf16[16384,256]{1,0:T(8,128)(2,1)} %all-gather.2.cloned.1.call-done, bf16[384,16384]{1,0:T(8,128)(2,1)} %param.8, s32[384,256]{0,1:T(8,128)S(1)} %copy.11, f32[256]{0:T(256)S(1)} %copy-done.6), kind=kOutput, calls=%fused_computation.8 | convolution fusion | flops 3221913600 | bytes 21758976 | tf_op jit(solution)/shard_map/dot_general | solution.py:30
  295.2 0.9 copy.12
  (1 shorter events, 0.0 us)
Async XLA Ops:
  7.2 0.9 copy-start
  7.2 197.3 %reduce-scatter.2.cloned.1.call-start = ((), (), s32[]{:S(2)}) async-start(), calls=%async_computation.1 | async-start | bytes 17825792 | tf_op jit(solution)/shard_map/reduce_scatter | solution.py:20
  23.0 0.7 copy-start.4
  23.0 0.7 copy-start.5
  23.0 181.5 %copy-start.1 = (f32[1024,256]{1,0:T(8,128)S(1)}, f32[1024,256]{1,0:T(8,128)}, u32[]{:S(2)}) copy-start(f32[1024,256]{1,0:T(8,128)} %param.11) | copy-start | bytes 3145732
  23.0 181.5 %copy-start.2 = (f32[1024,256]{1,0:T(8,128)S(1)}, f32[1024,256]{1,0:T(8,128)}, u32[]{:S(2)}) copy-start(f32[1024,256]{1,0:T(8,128)} %param.12) | copy-start | bytes 3145732
  23.0 184.5 %copy-start.3 = (s32[384,256]{1,0:T(8,128)S(1)}, s32[384,256]{1,0:T(8,128)}, u32[]{:S(2)}) copy-start(s32[384,256]{1,0:T(8,128)} %param.10) | copy-start | bytes 1179652
  23.0 258.6 %copy-start.6 = (f32[256]{0:T(256)S(1)}, f32[256]{0:T(256)}, u32[]{:S(2)}) copy-start(f32[256]{0:T(256)} %param.15) | copy-start | bytes 3076
  23.0 258.5 %all-gather.2.cloned.1.call-start = ((), (), s32[]{:S(2)}) async-start(), calls=%async_computation.2 | async-start | bytes 8912896 | tf_op jit(solution)/shard_map/all_gather | solution.py:32
Sparse Core Ops, SparseCore 0:
  23.2 181.2 reduce-scatter.1
  207.6 73.8 all-gather.1
where the time goes:
time: 303 us
  waiting for transfers between devices  255 us (84%)
  matrix products  28.5 us (9%)
  between operations  14.1 us (5%)
  other arithmetic  3.04 us (1%)
    reduce_scatter x1, waiting for transfers between devices, on_device(): lax.psum_scatter(lax.dot_general(columns, residual, (((0,), (0,)), ((), (...  181 us
    all_gather x1, waiting for transfers between devices, on_device(): lax.all_gather(effect, 'ind', axis=0, tiled=True)  73.9 us
    dot_general x1, matrix products, on_device(): lax.dot_general(columns, residual, (((0,), (0,)), ((), ())), preferred_el...  14.9 us
    dot_general x1, matrix products, on_device(): jnp.dot(columns, lax.all_gather(effect, 'ind', axis=0, tiled=True), prefe...  13.6 us
  transfers between devices with their start and end apart: 2, of which 2 were waited for; matrix products, arithmetic and copies ran while one was open for 0% of the time, Pallas kernels for 0%

commit v1 on v0

v1 whole, which is shorter than its diff:
```python
import functools

import jax
import jax.numpy as jnp
import numpy as np
from jax import lax
from jax.experimental import pallas as pl
from jax.experimental.pallas import tpu as pltpu
from jax.sharding import PartitionSpec as P

STEPS = 256.0
TOP = 32700.0
PAD = 16
VMEM = 48 * 1024 * 1024


def ring_of(devices):
    chips = devices[0, ::2]
    where = [getattr(d, "coords", None) for d in chips]
    count = len(where)
    plain = list(range(count))
    if any(w is None for w in where):
        where = [(0, k % 2, k // 2) for k in plain]
    varying = [k for k in range(3) if len({w[k] for w in where}) > 1]
    if len(varying) != 2:
        return sorted(plain, key=lambda k: tuple(where[k]))
    short, long = sorted(varying, key=lambda k: len({w[k] for w in where}))
    low = min(w[short] for w in where)
    if len({w[short] for w in where}) != 2:
        return plain
    up = sorted((k for k in plain if where[k][short] == low), key=lambda k: where[k][long])
    down = sorted((k for k in plain if where[k][short] != low), key=lambda k: -where[k][long])
    return up + down


def decode(message):
    rows = message.shape[0] - PAD
    code = message[rows : rows + 1, :].astype(jnp.float32)
    return message[:rows, :].astype(jnp.float32) * (jnp.exp2(code * (1.0 / STEPS)) * (1.0 / TOP))


def local_sum(own_ref, other_ref, res_ref, res_other_ref):
    dims = (((0,), (0,)), ((), ()))
    return lax.dot_general(
        own_ref[...], res_ref[...], dims, preferred_element_type=jnp.float32
    ) + lax.dot_general(
        other_ref[...], res_other_ref[...], dims, preferred_element_type=jnp.float32
    )


def encode_to(out_ref, total):
    rows = total.shape[0]
    top = jnp.maximum(jnp.max(jnp.abs(total), axis=0, keepdims=True), 1e-30)
    code = jnp.ceil(jnp.log2(top) * STEPS)
    scaled = jnp.round(total * (TOP * jnp.exp2(code * (-1.0 / STEPS))))
    out_ref[:rows, :] = scaled.astype(jnp.int32).astype(jnp.int16)
    out_ref[rows:, :] = jnp.broadcast_to(code, (PAD, code.shape[1])).astype(jnp.int32).astype(jnp.int16)


def start_kernel(at_ref, own_ref, other_ref, res_ref, res_other_ref, out_ref):
    encode_to(out_ref, local_sum(own_ref, other_ref, res_ref, res_other_ref))


def add_kernel(at_ref, own_ref, other_ref, res_ref, res_other_ref, got_ref, out_ref):
    encode_to(
        out_ref, local_sum(own_ref, other_ref, res_ref, res_other_ref) + decode(got_ref[...])
    )


def update_kernel(
    total, at_ref, own_ref, other_ref, res_ref, res_other_ref, right_ref, left_ref, incl_ref,
    mean_ref, prior_ref, scale_ref, *rest
):
    incl_new_ref, mean_new_ref, effect_ref = rest[-3:]
    corr = local_sum(own_ref, other_ref, res_ref, res_other_ref)
    corr = corr + decode(right_ref[...]) + decode(left_ref[...])
    incl = incl_ref[...]
    scale = scale_ref[...]
    stat = corr / total + incl * mean_ref[...]
    shrink = scale / (1.0 + scale)
    mean_new = stat * shrink
    logit = prior_ref[...] - 0.5 * jnp.log1p(scale) + 0.5 * total * shrink * stat * stat
    incl_new = 0.5 * incl + 0.5 * jax.nn.sigmoid(logit)
    incl_new_ref[...] = incl_new
    mean_new_ref[...] = mean_new
    effect_ref[...] = (incl_new * mean_new).astype(jnp.bfloat16)


def eta_kernel(pieces, first, at_ref, *refs):
    out_ref, out_other_ref = refs[-2:]
    mine = other = None
    for k in range(pieces):
        own_ref, peer_ref, effect_ref = refs[3 * k : 3 * k + 3]
        a = jnp.dot(own_ref[...], effect_ref[...], preferred_element_type=jnp.float32)
        b = jnp.dot(peer_ref[...], effect_ref[...], preferred_element_type=jnp.float32)
        mine = a if mine is None else mine + a
        other = b if other is None else other + b
    if not first:
        mine = mine + refs[3 * pieces][...]
        other = other + refs[3 * pieces + 1][...]
    out_ref[...] = mine
    out_other_ref[...] = other


def end_kernel(eta_ref, got_ref, labels_ref, offset_ref, out_ref):
    eta = eta_ref[...] + got_ref[...] + offset_ref[...]
    out_ref[...] = 4.0 * (labels_ref[...].astype(jnp.float32) - jax.nn.sigmoid(eta))


def on_device(ring, genotype, residual, labels, incl_old, mean_old, prior_logit, slab_scale, offset):
    n = lax.axis_size("ind")
    people, cols = residual.shape
    total = float(people * n)
    block = incl_old.shape[0]
    part = block // 2
    size = len(ring)
    reach = size // 2
    spot = {chip: k for k, chip in enumerate(ring)}

    me = lax.axis_index("ind")
    core = lax.rem(me, 2)
    table = np.zeros((n, size), np.int32)
    for dev in range(n):
        for d in range(size):
            table[dev, d] = 2 * ring[(spot[dev // 2] + d) % size] + dev % 2
    owners = lax.dynamic_slice(jnp.asarray(table), (me, 0), (1, size)).reshape(size)

    swap = [(k, k ^ 1) for k in range(n)]
    right, left = [], []
    for k, chip in enumerate(ring):
        for c in range(2):
            right.append((2 * chip + c, 2 * ring[(k + 1) % size] + c))
            left.append((2 * chip + c, 2 * ring[(k - 1) % size] + c))

    residual_other = lax.ppermute(residual, "ind", swap)
    order = [reach]
    for d in range(reach - 1, 0, -1):
        order += [d, size - d]
    order += [0]
    peer = {}
    for d in order:
        if d in peer:
            continue
        wanted = owners[d] + 1 - 2 * core
        slab = lax.dynamic_slice(genotype, (0, wanted * block), (people, block))
        peer[d] = lax.ppermute(slab, "ind", swap)

    params = pltpu.CompilerParams(vmem_limit_bytes=VMEM)

    def specs(d, half):
        return [
            pl.BlockSpec((people, part), lambda i, at, d=d, half=half: (0, 2 * at[d] + half)),
            pl.BlockSpec((people, part), lambda i, at, half=half: (0, half)),
        ]

    def whole(shape):
        return pl.BlockSpec(shape, lambda i, at: (0,) * len(shape))

    res_spec = whole((people, cols))
    message = jax.ShapeDtypeStruct((part + PAD, cols), jnp.int16)
    message_spec = whole(message.shape)
    dot_cost = pl.CostEstimate(
        flops=4 * people * part * cols,
        bytes_accessed=4 * people * part + 4 * people * cols + 4 * part * cols,
        transcendentals=0,
    )

    def outgoing(d, half, got):
        kernel = start_kernel if got is None else add_kernel
        extra = [] if got is None else [got]
        return pl.pallas_call(
            kernel,
            grid_spec=pltpu.PrefetchScalarGridSpec(
                num_scalar_prefetch=1,
                grid=(1,),
                in_specs=specs(d, half) + [res_spec] * 2 + [message_spec] * len(extra),
                out_specs=message_spec,
            ),
            out_shape=message,
            compiler_params=params,
            cost_estimate=dot_cost,
            name="sum_block",
        )(owners, genotype, peer[d], residual, residual_other, *extra)

    got = {}
    for d in range(reach, 0, -1):
        for way, half in ((0, 0), (1, 1), (0, 1), (1, 0)):
            if d == reach and way != half:
                continue
            at = d if way == 0 else (size - d) % size
            sent = outgoing(at, half, got.get((way, half)))
            got[way, half] = lax.ppermute(sent, "ind", right if way == 0 else left)

    prior = prior_logit.reshape(1, cols)
    scale = slab_scale.reshape(1, cols)
    row = whole((1, cols))
    state = pl.BlockSpec((part, cols), lambda i, at: (0, 0))
    outs = None
    effects = {}
    for half in range(2):
        at_half = pl.BlockSpec((part, cols), lambda i, at, half=half: (half, 0))
        extra = [] if outs is None else list(outs)
        incl_new, mean_new, effects[half] = pl.pallas_call(
            functools.partial(update_kernel, total),
            grid_spec=pltpu.PrefetchScalarGridSpec(
                num_scalar_prefetch=1,
                grid=(1,),
                in_specs=specs(0, half)
                + [res_spec] * 2
                + [message_spec] * 2
                + [at_half] * 2
                + [row] * 2
                + [pl.BlockSpec(memory_space=pl.ANY)] * len(extra),
                out_specs=[at_half, at_half, state],
            ),
            out_shape=[
                jax.ShapeDtypeStruct((block, cols), jnp.float32),
                jax.ShapeDtypeStruct((block, cols), jnp.float32),
                jax.ShapeDtypeStruct((part, cols), jnp.bfloat16),
            ],
            input_output_aliases={} if outs is None else {11: 0, 12: 1},
            compiler_params=params,
            name="update",
        )(
            owners, genotype, peer[0], residual, residual_other, got[0, half], got[1, half],
            incl_old, mean_old, prior, scale, *extra
        )
        outs = (incl_new, mean_new)

    eta_spec = whole((people, cols))
    eta_shape = jax.ShapeDtypeStruct((people, cols), jnp.float32)

    def product(pieces, before):
        in_specs, args = [], []
        for d, half, effect in pieces:
            in_specs += specs(d, half) + [state]
            args += [genotype, peer[d], effect]
        return pl.pallas_call(
            functools.partial(eta_kernel, len(pieces), before is None),
            grid_spec=pltpu.PrefetchScalarGridSpec(
                num_scalar_prefetch=1,
                grid=(1,),
                in_specs=in_specs + [eta_spec] * (0 if before is None else 2),
                out_specs=[eta_spec] * 2,
            ),
            out_shape=[eta_shape] * 2,
            compiler_params=params,
            cost_estimate=pl.CostEstimate(
                flops=4 * people * part * cols * len(pieces),
                bytes_accessed=len(pieces) * (4 * people * part + 2 * part * cols)
                + 16 * people * cols,
                transcendentals=0,
            ),
            name="add_eta",
        )(owners, *args, *(() if before is None else before))

    held = {(way, half): effects[half] for way in range(2) for half in range(2)}
    eta = None
    pending = [(0, 0, effects[0]), (0, 1, effects[1])]
    for hop in range(1, reach + 1):
        fresh = []
        for way, half in ((0, 0), (1, 1), (0, 1), (1, 0)):
            if hop == reach and way != half:
                continue
            held[way, half] = lax.ppermute(
                held[way, half], "ind", right if way == 0 else left
            )
            fresh.append(((size - hop) % size if way == 0 else hop, half, held[way, half]))
        eta = product(pending, eta)
        pending = fresh
    eta = product(pending, eta)

    eta_got = lax.ppermute(eta[1], "ind", swap)
    resid_new = pl.pallas_call(
        end_kernel,
        out_shape=eta_shape,
        compiler_params=params,
        name="new_residual",
    )(eta[0], eta_got, labels, offset.reshape(1, cols))
    return (outs[0], outs[1], resid_new)


def solution(mesh):
    split = P(("groups", "ind"), None)
    return jax.shard_map(
        functools.partial(on_device, ring_of(mesh.devices)),
        mesh=mesh,
        in_specs=(split, split, split, split, split, P(), P(), P()),
        out_specs=(split, split, split),
        check_vma=False,
    )
```

time: 303 us -> 127 us (0.42)
  waiting for transfers between devices: 255 us -> 32 us
  Pallas kernels: 0 us -> 50.3 us
  starting transfers between devices: 0.08 us -> 32.1 us
  matrix products: 28.5 us -> 0 us
  between operations: 14.1 us -> 6.19 us
  other arithmetic: 3.04 us -> 0 us
    reduce_scatter x1 -> x0, waiting for transfers between devices: 181 us -> none  [on_device(): lax.psum_scatter(lax.dot_general(columns, residual, (((0,), (0,)), ((), (...]
    all_gather x1 -> x0, waiting for transfers between devices: 73.9 us -> none  [on_device(): lax.all_gather(effect, 'ind', axis=0, tiled=True)]
    pallas_call x0 -> x22, Pallas kernels: none -> 50.3 us  [the longest x14 29.7 us: outgoing(): pl.pallas_call(kernel, grid_spec=pltpu.PrefetchScalarGridSpec(num_scalar_...]
    ppermute x0 -> x38, starting transfers between devices: none -> 32.1 us  [the longest x14 15.8 us: on_device(): got[way, half] = lax.ppermute(sent, 'ind', right if way == 0 else left)]
    ppermute x0 -> x38, waiting for transfers between devices: none -> 32 us  [the longest x14 19.6 us: on_device(): lax.ppermute(held[way, half], 'ind', right if way == 0 else left)]
    dot_general x2 -> x0, matrix products: 28.5 us -> none  [the longest x1 14.9 us: on_device(): lax.dot_general(columns, residual, (((0,), (0,)), ((), ())), preferred_el...]
    dynamic_slice x0 -> x2, local copies, waits for them, and re-layouts: none -> 4.28 us  [the longest x1 3.54 us: on_device(): slab = lax.dynamic_slice(genotype, (0, wanted * block), (people, block))]
    convert_element_type x1 -> x0, other arithmetic: 3.03 us -> none  [update(): effect = (incl_new * mean_new).astype(jnp.bfloat16)]
  transfers between devices with their start and end apart: 2 -> 38, of which waited for: 2 -> 12; matrix products, arithmetic and copies ran while one was open for 0% -> 0% of each run, Pallas kernels for 0% -> 35%
where the time goes in v1:
time: 127 us; the launch traced here: 126 us
  Pallas kernels  50.3 us (40%)
  starting transfers between devices  32.1 us (25%)
  waiting for transfers between devices  32 us (25%)
  between operations  6.19 us (5%)
  local copies, waits for them, and re-layouts  4.99 us (4%)
    pallas_call x14, Pallas kernels, outgoing(): pl.pallas_call(kernel, grid_spec=pltpu.PrefetchScalarGridSpec(num_scalar_...  29.7 us
    ppermute x14, waiting for transfers between devices, on_device(): lax.ppermute(held[way, half], 'ind', right if way == 0 else left)  19.6 us
    ppermute x14, starting transfers between devices, on_device(): got[way, half] = lax.ppermute(sent, 'ind', right if way == 0 else left)  15.8 us
    ppermute x14, starting transfers between devices, on_device(): lax.ppermute(held[way, half], 'ind', right if way == 0 else left)  14.2 us
    pallas_call x5, Pallas kernels, product(): pl.pallas_call(functools.partial(eta_kernel, len(pieces), before is None)...  13.2 us
    ppermute x14, waiting for transfers between devices, on_device(): got[way, half] = lax.ppermute(sent, 'ind', right if way == 0 else left)  8.4 us
    pallas_call x2, Pallas kernels, on_device(): pl.pallas_call(functools.partial(update_kernel, total), grid_spec=pltpu.P...  6.48 us
    dynamic_slice x1, local copies, waits for them, and re-layouts, on_device(): slab = lax.dynamic_slice(genotype, (0, wanted * block), (people, block))  3.54 us
  transfers between devices with their start and end apart: 38, of which 12 were waited for; matrix products, arithmetic and copies ran while one was open for 0% of the time, Pallas kernels for 35%

profile of v1, /device:TPU:0, one launch (start us, length us, event | category | flops | bytes accessed | tf_op | source)
XLA Modules:
  0.0 125.5 jit_solution(6379972617491715557)
XLA Ops:
  7.2 3.5 %constant_dynamic-slice_fusion = (bf16[384,1024]{1,0:T(8,128)(2,1)S(1)}, bf16[384,1024]{1,0:T(8,128)(2,1)S(1)}, bf16[384,1024]{1,0:T(8,128)(2,1)S(1)}, bf16[384,...) fusion(bf16[384,16384]{1,0:T(8,128)(2,1)} %refs_3_.9, ...), kind=kLoop, calls=%fused_computation | loop fusion | bytes 12582944 | tf_op jit(solution)/shard_map/dynamic_slice | solution.py:145
  12.3 2.3 %collective-permute-done.1.res_other_ref = bf16[384,256]{1,0:T(8,128)(2,1)S(1)} collective-permute-done((bf16[384,256]{1,0:T(8,128)(2,1)S(1)}, bf16[384,256]{1,0:T(8,128)(2,1)S(1)}, u32[]{:S(2)}, u32[]{:S(2)}) %collective-permute-start.1) | collective-permute-done | bytes 196640 | tf_op jit(solution)/shard_map/ppermute | solution.py:135
  15.1 2.1 %sum_block.21 = s16[528,256]{1,0:T(8,128)(2,1)S(1)} custom-call(s32[8]{0:T(128)S(1)} %get-tuple-element.44.at_ref, bf16[384,16384]{1,0:T(8,128)(2,1)} %refs_3_.9, bf16[384,1024]{1,0:T(8,128)(2,1)S(1)} %collective-permute-done.11.other_ref.refs_1_.refs_4_, bf16[384,256]{1,0:T(8,128)(2,1)S(1)} %copy-done, bf16[384,256]{1,0:T(8,128)(2,1)S(1)} %collective-permute-done.1.res_other_ref), custom_call_target="tpu_custom_call" | custom-call | flops 201326592 | bytes 1703936 | tf_op jit(solution)/shard_map/sum_block/pallas_call | solution.py:171
  17.3 3.0 %collective-permute-start.16 = (s16[528,256]{1,0:T(8,128)(2,1)S(1)}, s16[528,256]{1,0:T(8,128)(2,1)S(1)}, u32[]{:S(2)}, u32[]{:S(2)}) collective-permute-start(s16[528,256]{1,0:T(8,128)(2,1)S(1)} %sum_block.21), channel_id=1, source_target_pairs={{0,4},{1,5},{4,8},{5,9},{8,12},{9,13},{12,14},{13,15},{14,10},{15,... | collective-permute-start | bytes 811016 | tf_op jit(solution)/shard_map/ppermute | solution.py:192
  20.3 2.1 %sum_block.17 = s16[528,256]{1,0:T(8,128)(2,1)S(1)} custom-call(s32[8]{0:T(128)S(1)} %get-tuple-element.44.at_ref, bf16[384,16384]{1,0:T(8,128)(2,1)} %refs_3_.9, bf16[384,1024]{1,0:T(8,128)(2,1)S(1)} %collective-permute-done.11.other_ref.refs_1_.refs_4_, bf16[384,256]{1,0:T(8,128)(2,1)S(1)} %copy-done, bf16[384,256]{1,0:T(8,128)(2,1)S(1)} %collective-permute-done.1.res_other_ref), custom_call_target="tpu_custom_call" | custom-call | flops 201326592 | bytes 1703936 | tf_op jit(solution)/shard_map/sum_block/pallas_call | solution.py:171
  22.5 2.1 %sum_block.25 = s16[528,256]{1,0:T(8,128)(2,1)S(1)} custom-call(s32[8]{0:T(128)S(1)} %get-tuple-element.44.at_ref, bf16[384,16384]{1,0:T(8,128)(2,1)} %refs_3_.9, bf16[384,1024]{1,0:T(8,128)(2,1)S(1)} %collective-permute-done.10.other_ref.refs_1_.refs_7_, bf16[384,256]{1,0:T(8,128)(2,1)S(1)} %copy-done, bf16[384,256]{1,0:T(8,128)(2,1)S(1)} %collective-permute-done.1.res_other_ref), custom_call_target="tpu_custom_call" | custom-call | flops 201326592 | bytes 1703936 | tf_op jit(solution)/shard_map/sum_block/pallas_call | solution.py:171
  24.6 2.0 %collective-permute-start.20 = (s16[528,256]{1,0:T(8,128)(2,1)S(1)}, s16[528,256]{1,0:T(8,128)(2,1)S(1)}, u32[]{:S(2)}, u32[]{:S(2)}) collective-permute-start(s16[528,256]{1,0:T(8,128)(2,1)S(1)} %sum_block.25), channel_id=1, source_target_pairs={{0,2},{1,3},{4,0},{5,1},{8,4},{9,5},{12,8},{13,9},{14,12},{15,13},... | collective-permute-start | bytes 811016 | tf_op jit(solution)/shard_map/ppermute | solution.py:192
  26.6 2.1 %sum_block.14 = s16[528,256]{1,0:T(8,128)(2,1)S(1)} custom-call(s32[8]{0:T(128)S(1)} %get-tuple-element.44.at_ref, bf16[384,16384]{1,0:T(8,128)(2,1)} %refs_3_.9, bf16[384,1024]{1,0:T(8,128)(2,1)S(1)} %collective-permute-done.4.other_ref.refs_4_.refs_10_, bf16[384,256]{1,0:T(8,128)(2,1)S(1)} %copy-done, bf16[384,256]{1,0:T(8,128)(2,1)S(1)} %collective-permute-done.1.res_other_ref), custom_call_target="tpu_custom_call" | custom-call | flops 201326592 | bytes 1703936 | tf_op jit(solution)/shard_map/sum_block/pallas_call | solution.py:171
  28.9 2.1 %sum_block.22 = s16[528,256]{1,0:T(8,128)(2,1)S(1)} custom-call(s32[8]{0:T(128)S(1)} %get-tuple-element.44.at_ref, bf16[384,16384]{1,0:T(8,128)(2,1)} %refs_3_.9, bf16[384,1024]{1,0:T(8,128)(2,1)S(1)} %collective-permute-done.4.other_ref.refs_4_.refs_10_, bf16[384,256]{1,0:T(8,128)(2,1)S(1)} %copy-done, ...), custom_call_target="tpu_custom_call" | custom-call | flops 201326592 | bytes 1703936 | tf_op jit(solution)/shard_map/sum_block/pallas_call | solution.py:171
  33.4 2.1 %sum_block.18 = s16[528,256]{1,0:T(8,128)(2,1)S(1)} custom-call(s32[8]{0:T(128)S(1)} %get-tuple-element.44.at_ref, bf16[384,16384]{1,0:T(8,128)(2,1)} %refs_3_.9, bf16[384,1024]{1,0:T(8,128)(2,1)S(1)} %collective-permute-done.10.other_ref.refs_1_.refs_7_, bf16[384,256]{1,0:T(8,128)(2,1)S(1)} %copy-done, ...), custom_call_target="tpu_custom_call" | custom-call | flops 201326592 | bytes 1703936 | tf_op jit(solution)/shard_map/sum_block/pallas_call | solution.py:171
  36.8 2.1 %sum_block.26 = s16[528,256]{1,0:T(8,128)(2,1)S(1)} custom-call(s32[8]{0:T(128)S(1)} %get-tuple-element.44.at_ref, bf16[384,16384]{1,0:T(8,128)(2,1)} %refs_3_.9, bf16[384,1024]{1,0:T(8,128)(2,1)S(1)} %collective-permute-done.9.other_ref.refs_1_.refs_7_, bf16[384,256]{1,0:T(8,128)(2,1)S(1)} %copy-done, ...), custom_call_target="tpu_custom_call" | custom-call | flops 201326592 | bytes 1703936 | tf_op jit(solution)/shard_map/sum_block/pallas_call | solution.py:171
  40.6 2.1 %sum_block.15 = s16[528,256]{1,0:T(8,128)(2,1)S(1)} custom-call(s32[8]{0:T(128)S(1)} %get-tuple-element.44.at_ref, bf16[384,16384]{1,0:T(8,128)(2,1)} %refs_3_.9, bf16[384,1024]{1,0:T(8,128)(2,1)S(1)} %collective-permute-done.3.other_ref.refs_4_.refs_10_, bf16[384,256]{1,0:T(8,128)(2,1)S(1)} %copy-done, ...), custom_call_target="tpu_custom_call" | custom-call | flops 201326592 | bytes 1703936 | tf_op jit(solution)/shard_map/sum_block/pallas_call | solution.py:171
  43.7 2.1 %sum_block.23 = s16[528,256]{1,0:T(8,128)(2,1)S(1)} custom-call(s32[8]{0:T(128)S(1)} %get-tuple-element.44.at_ref, bf16[384,16384]{1,0:T(8,128)(2,1)} %refs_3_.9, bf16[384,1024]{1,0:T(8,128)(2,1)S(1)} %collective-permute-done.3.other_ref.refs_4_.refs_10_, bf16[384,256]{1,0:T(8,128)(2,1)S(1)} %copy-done, ...), custom_call_target="tpu_custom_call" | custom-call | flops 201326592 | bytes 1703936 | tf_op jit(solution)/shard_map/sum_block/pallas_call | solution.py:171
  45.9 1.8 %collective-permute-start.18 = (s16[528,256]{1,0:T(8,128)(2,1)S(1)}, s16[528,256]{1,0:T(8,128)(2,1)S(1)}, u32[]{:S(2)}, u32[]{:S(2)}) collective-permute-start(s16[528,256]{1,0:T(8,128)(2,1)S(1)} %sum_block.23), channel_id=1, source_target_pairs={{0,4},{1,5},{4,8},{5,9},{8,12},{9,13},{12,14},{13,15},{14,10},{15,... | collective-permute-start | bytes 811016 | tf_op jit(solution)/shard_map/ppermute | solution.py:192
  47.7 2.1 %sum_block.19 = s16[528,256]{1,0:T(8,128)(2,1)S(1)} custom-call(s32[8]{0:T(128)S(1)} %get-tuple-element.44.at_ref, bf16[384,16384]{1,0:T(8,128)(2,1)} %refs_3_.9, bf16[384,1024]{1,0:T(8,128)(2,1)S(1)} %collective-permute-done.9.other_ref.refs_1_.refs_7_, bf16[384,256]{1,0:T(8,128)(2,1)S(1)} %copy-done, ...), custom_call_target="tpu_custom_call" | custom-call | flops 201326592 | bytes 1703936 | tf_op jit(solution)/shard_map/sum_block/pallas_call | solution.py:171
  50.2 2.1 %sum_block.27 = s16[528,256]{1,0:T(8,128)(2,1)S(1)} custom-call(s32[8]{0:T(128)S(1)} %get-tuple-element.44.at_ref, bf16[384,16384]{1,0:T(8,128)(2,1)} %refs_3_.9, bf16[384,1024]{1,0:T(8,128)(2,1)S(1)} %collective-permute-done.8.other_ref.refs_1_.refs_7_, bf16[384,256]{1,0:T(8,128)(2,1)S(1)} %copy-done, ...), custom_call_target="tpu_custom_call" | custom-call | flops 201326592 | bytes 1703936 | tf_op jit(solution)/shard_map/sum_block/pallas_call | solution.py:171
  54.1 2.1 %sum_block.16 = s16[528,256]{1,0:T(8,128)(2,1)S(1)} custom-call(s32[8]{0:T(128)S(1)} %get-tuple-element.44.at_ref, bf16[384,16384]{1,0:T(8,128)(2,1)} %refs_3_.9, bf16[384,1024]{1,0:T(8,128)(2,1)S(1)} %collective-permute-done.2.other_ref.refs_4_.refs_10_, bf16[384,256]{1,0:T(8,128)(2,1)S(1)} %copy-done, ...), custom_call_target="tpu_custom_call" | custom-call | flops 201326592 | bytes 1703936 | tf_op jit(solution)/shard_map/sum_block/pallas_call | solution.py:171
  57.5 2.1 %sum_block.24 = s16[528,256]{1,0:T(8,128)(2,1)S(1)} custom-call(s32[8]{0:T(128)S(1)} %get-tuple-element.44.at_ref, bf16[384,16384]{1,0:T(8,128)(2,1)} %refs_3_.9, bf16[384,1024]{1,0:T(8,128)(2,1)S(1)} %collective-permute-done.2.other_ref.refs_4_.refs_10_, bf16[384,256]{1,0:T(8,128)(2,1)S(1)} %copy-done, ...), custom_call_target="tpu_custom_call" | custom-call | flops 201326592 | bytes 1703936 | tf_op jit(solution)/shard_map/sum_block/pallas_call | solution.py:171
  60.6 2.1 %sum_block.20 = s16[528,256]{1,0:T(8,128)(2,1)S(1)} custom-call(s32[8]{0:T(128)S(1)} %get-tuple-element.44.at_ref, bf16[384,16384]{1,0:T(8,128)(2,1)} %refs_3_.9, bf16[384,1024]{1,0:T(8,128)(2,1)S(1)} %collective-permute-done.8.other_ref.refs_1_.refs_7_, bf16[384,256]{1,0:T(8,128)(2,1)S(1)} %copy-done, ...), custom_call_target="tpu_custom_call" | custom-call | flops 201326592 | bytes 1703936 | tf_op jit(solution)/shard_map/sum_block/pallas_call | solution.py:171
  64.1 5.2 %collective-permute-done.19.right_ref = s16[528,256]{1,0:T(8,128)(2,1)S(1)} collective-permute-done((s16[528,256]{1,0:T(8,128)(2,1)S(1)}, s16[528,256]{1,0:T(8,128)(2,1)S(1)}, u32[]{:S(2)}, u32[]{:S(2)}) %collective-permute-start.19) | collective-permute-done | bytes 270368 | tf_op jit(solution)/shard_map/ppermute | solution.py:192
  69.3 3.2 %update.2 = (f32[1024,256]{1,0:T(8,128)}, f32[1024,256]{1,0:T(8,128)}, bf16[512,256]{1,0:T(8,128)(2,1)S(1)}) custom-call(s32[8]{0:T(128)S(1)} %get-tuple-element.44.at_ref, bf16[384,16384]{1,0:T(8,128)(2,1)} %refs_3_.9, bf16[384,1024]{1,0:T(8,128)(2,1)S(1)} %collective-permute-done.other_ref.refs_1_.refs_4_, bf16[384,256]{1,0:T(8,128)(2,1)S(1)} %copy-done, ...), custom_call_target="tpu_custom_call" | custom-call | tf_op jit(solution)/shard_map/update/pallas_call | solution.py:203
  72.6 3.2 %update.3 = (f32[1024,256]{1,0:T(8,128)}, f32[1024,256]{1,0:T(8,128)}, bf16[512,256]{1,0:T(8,128)(2,1)S(1)}) custom-call(s32[8]{0:T(128)S(1)} %get-tuple-element.44.at_ref, bf16[384,16384]{1,0:T(8,128)(2,1)} %refs_3_.9, bf16[384,1024]{1,0:T(8,128)(2,1)S(1)} %collective-permute-done.other_ref.refs_1_.refs_4_, ...), custom_call_target="tpu_custom_call", output_to_operand_aliasing={{0}: (11, {}), {1}: (12, {})} | custom-call | tf_op jit(solution)/shard_map/update/pallas_call | solution.py:203
  79.9 5.2 %collective-permute-done.27.refs_5_ = bf16[512,256]{1,0:T(8,128)(2,1)S(1)} collective-permute-done((bf16[512,256]{1,0:T(8,128)(2,1)S(1)}, bf16[512,256]{1,0:T(8,128)(2,1)S(1)}, u32[]{:S(2)}, u32[]{:S(2)}) %collective-permute-start.27) | collective-permute-done | bytes 262176 | tf_op jit(solution)/shard_map/ppermute | solution.py:265
  87.1 5.2 %collective-permute-done.31.refs_8_ = bf16[512,256]{1,0:T(8,128)(2,1)S(1)} collective-permute-done((bf16[512,256]{1,0:T(8,128)(2,1)S(1)}, bf16[512,256]{1,0:T(8,128)(2,1)S(1)}, u32[]{:S(2)}, u32[]{:S(2)}) %collective-permute-start.31) | collective-permute-done | bytes 262176 | tf_op jit(solution)/shard_map/ppermute | solution.py:265
  94.3 2.0 %collective-permute-done.28.refs_5_ = bf16[512,256]{1,0:T(8,128)(2,1)S(1)} collective-permute-done((bf16[512,256]{1,0:T(8,128)(2,1)S(1)}, bf16[512,256]{1,0:T(8,128)(2,1)S(1)}, u32[]{:S(2)}, u32[]{:S(2)}) %collective-permute-start.28) | collective-permute-done | bytes 262176 | tf_op jit(solution)/shard_map/ppermute | solution.py:265
  98.3 5.2 %collective-permute-done.32.refs_8_ = bf16[512,256]{1,0:T(8,128)(2,1)S(1)} collective-permute-done((bf16[512,256]{1,0:T(8,128)(2,1)S(1)}, bf16[512,256]{1,0:T(8,128)(2,1)S(1)}, u32[]{:S(2)}, u32[]{:S(2)}) %collective-permute-start.32) | collective-permute-done | bytes 262176 | tf_op jit(solution)/shard_map/ppermute | solution.py:265
  105.5 2.0 %collective-permute-done.29.refs_5_ = bf16[512,256]{1,0:T(8,128)(2,1)S(1)} collective-permute-done((bf16[512,256]{1,0:T(8,128)(2,1)S(1)}, bf16[512,256]{1,0:T(8,128)(2,1)S(1)}, u32[]{:S(2)}, u32[]{:S(2)}) %collective-permute-start.29) | collective-permute-done | bytes 262176 | tf_op jit(solution)/shard_map/ppermute | solution.py:265
  109.6 2.2 %add_eta.5 = (f32[384,256]{1,0:T(8,128)S(1)}, f32[384,256]{1,0:T(8,128)S(1)}) custom-call(s32[8]{0:T(128)S(1)} %get-tuple-element.44.at_ref, bf16[384,16384]{1,0:T(8,128)(2,1)} %refs_3_.9, bf16[384,1024]{1,0:T(8,128)(2,1)S(1)} %collective-permute-done.other_ref.refs_1_.refs_4_, bf16[512,256]{1,0:T(8,128)(2,1)S(1)} %get-tuple-element.23.refs_2_, ...), custom_call_target="tpu_custom_call" | custom-call | flops 402653184 | bytes 3670016 | tf_op jit(solution)/shard_map/add_eta/pallas_call | solution.py:238
  111.8 2.9 %add_eta.6 = (f32[384,256]{1,0:T(8,128)S(1)}, f32[384,256]{1,0:T(8,128)S(1)}) custom-call(s32[8]{0:T(128)S(1)} %get-tuple-element.44.at_ref, bf16[384,16384]{1,0:T(8,128)(2,1)} %refs_3_.9, bf16[384,1024]{1,0:T(8,128)(2,1)S(1)} %collective-permute-done.8.other_ref.refs_1_.refs_7_, bf16[512,256]{1,0:T(8,128)(2,1)S(1)} %collective-permute-done.23.refs_2_, ...), custom_call_target="tpu_custom_call" | custom-call | flops 805306368 | bytes 5767168 | tf_op jit(solution)/shard_map/add_eta/pallas_call | solution.py:238
  114.7 2.9 %add_eta.7 = (f32[384,256]{1,0:T(8,128)S(1)}, f32[384,256]{1,0:T(8,128)S(1)}) custom-call(s32[8]{0:T(128)S(1)} %get-tuple-element.44.at_ref, bf16[384,16384]{1,0:T(8,128)(2,1)} %refs_3_.9, bf16[384,1024]{1,0:T(8,128)(2,1)S(1)} %collective-permute-done.9.other_ref.refs_1_.refs_7_, bf16[512,256]{1,0:T(8,128)(2,1)S(1)} %collective-permute-done.24.refs_2_, ...), custom_call_target="tpu_custom_call" | custom-call | flops 805306368 | bytes 5767168 | tf_op jit(solution)/shard_map/add_eta/pallas_call | solution.py:238
  117.7 2.9 %add_eta.8 = (f32[384,256]{1,0:T(8,128)S(1)}, f32[384,256]{1,0:T(8,128)S(1)}) custom-call(s32[8]{0:T(128)S(1)} %get-tuple-element.44.at_ref, bf16[384,16384]{1,0:T(8,128)(2,1)} %refs_3_.9, bf16[384,1024]{1,0:T(8,128)(2,1)S(1)} %collective-permute-done.10.other_ref.refs_1_.refs_7_, bf16[512,256]{1,0:T(8,128)(2,1)S(1)} %collective-permute-done.25.refs_2_, ...), custom_call_target="tpu_custom_call" | custom-call | flops 805306368 | bytes 5767168 | tf_op jit(solution)/shard_map/add_eta/pallas_call | solution.py:238
  120.7 2.2 %add_eta.9 = (f32[384,256]{1,0:T(8,128)S(1)}, f32[384,256]{1,0:T(8,128)S(1)}) custom-call(s32[8]{0:T(128)S(1)} %get-tuple-element.44.at_ref, bf16[384,16384]{1,0:T(8,128)(2,1)} %refs_3_.9, bf16[384,1024]{1,0:T(8,128)(2,1)S(1)} %collective-permute-done.11.other_ref.refs_1_.refs_4_, bf16[512,256]{1,0:T(8,128)(2,1)S(1)} %collective-permute-done.26.refs_2_, ...), custom_call_target="tpu_custom_call" | custom-call | flops 402653184 | bytes 3670016 | tf_op jit(solution)/shard_map/add_eta/pallas_call | solution.py:238
  (83 shorter events, 32.6 us)
Async XLA Ops:
  11.8 10.6 %collective-permute-start.9 = (bf16[384,1024]{1,0:T(8,128)(2,1)S(1)}, bf16[384,1024]{1,0:T(8,128)(2,1)S(1)}, u32[]{:S(2)}, u32[]{:S(2)}) collective-permute-start(bf16[384,1024]{1,0:T(8,128)(2,1)S(1)} %get-tuple-element.37), channel_id=1, source_target_pairs={{0,1},{1,0},{2,3},{3,2},{4,5},{5,4},{6,7},{7,6},{8,9},{9,8},{10,11... | collective-permute-start | bytes 2359304 | tf_op jit(solution)/shard_map/ppermute | solution.py:146
  11.9 12.7 %collective-permute-start.8 = (bf16[384,1024]{1,0:T(8,128)(2,1)S(1)}, bf16[384,1024]{1,0:T(8,128)(2,1)S(1)}, u32[]{:S(2)}, u32[]{:S(2)}) collective-permute-start(bf16[384,1024]{1,0:T(8,128)(2,1)S(1)} %get-tuple-element.38), channel_id=1, source_target_pairs={{0,1},{1,0},{2,3},{3,2},{4,5},{5,4},{6,7},{7,6},{8,9},{9,8},{10,11... | collective-permute-start | bytes 2359304 | tf_op jit(solution)/shard_map/ppermute | solution.py:146
  14.6 12.0 %collective-permute-start.4 = (bf16[384,1024]{1,0:T(8,128)(2,1)S(1)}, bf16[384,1024]{1,0:T(8,128)(2,1)S(1)}, u32[]{:S(2)}, u32[]{:S(2)}) collective-permute-start(bf16[384,1024]{1,0:T(8,128)(2,1)S(1)} %get-tuple-element.39), channel_id=1, source_target_pairs={{0,1},{1,0},{2,3},{3,2},{4,5},{5,4},{6,7},{7,6},{8,9},{9,8},{10,11... | collective-permute-start | bytes 2359304 | tf_op jit(solution)/shard_map/ppermute | solution.py:146
  15.0 23.9 %collective-permute-start.3 = (bf16[384,1024]{1,0:T(8,128)(2,1)S(1)}, bf16[384,1024]{1,0:T(8,128)(2,1)S(1)}, u32[]{:S(2)}, u32[]{:S(2)}) collective-permute-start(bf16[384,1024]{1,0:T(8,128)(2,1)S(1)} %get-tuple-element.40), channel_id=1, source_target_pairs={{0,1},{1,0},{2,3},{3,2},{4,5},{5,4},{6,7},{7,6},{8,9},{9,8},{10,11... | collective-permute-start | bytes 2359304 | tf_op jit(solution)/shard_map/ppermute | solution.py:146
  17.3 11.5 %collective-permute-start.16 = (s16[528,256]{1,0:T(8,128)(2,1)S(1)}, s16[528,256]{1,0:T(8,128)(2,1)S(1)}, u32[]{:S(2)}, u32[]{:S(2)}) collective-permute-start(s16[528,256]{1,0:T(8,128)(2,1)S(1)} %sum_block.21), channel_id=1, source_target_pairs={{0,4},{1,5},{4,8},{5,9},{8,12},{9,13},{12,14},{13,15},{14,10},{15,... | collective-permute-start | bytes 811016 | tf_op jit(solution)/shard_map/ppermute | solution.py:192
  22.4 9.4 %collective-permute-start.12 = (s16[528,256]{1,0:T(8,128)(2,1)S(1)}, s16[528,256]{1,0:T(8,128)(2,1)S(1)}, u32[]{:S(2)}, u32[]{:S(2)}) collective-permute-start(s16[528,256]{1,0:T(8,128)(2,1)S(1)} %sum_block.17), channel_id=1, source_target_pairs={{0,2},{1,3},{4,0},{5,1},{8,4},{9,5},{12,8},{13,9},{14,12},{15,13},... | collective-permute-start | bytes 811016 | tf_op jit(solution)/shard_map/ppermute | solution.py:192
  24.6 11.9 %collective-permute-start.20 = (s16[528,256]{1,0:T(8,128)(2,1)S(1)}, s16[528,256]{1,0:T(8,128)(2,1)S(1)}, u32[]{:S(2)}, u32[]{:S(2)}) collective-permute-start(s16[528,256]{1,0:T(8,128)(2,1)S(1)} %sum_block.25), channel_id=1, source_target_pairs={{0,2},{1,3},{4,0},{5,1},{8,4},{9,5},{12,8},{13,9},{14,12},{15,13},... | collective-permute-start | bytes 811016 | tf_op jit(solution)/shard_map/ppermute | solution.py:192
  26.6 25.8 %collective-permute-start.2 = (bf16[384,1024]{1,0:T(8,128)(2,1)S(1)}, bf16[384,1024]{1,0:T(8,128)(2,1)S(1)}, u32[]{:S(2)}, u32[]{:S(2)}) collective-permute-start(bf16[384,1024]{1,0:T(8,128)(2,1)S(1)} %get-tuple-element.41), channel_id=1, source_target_pairs={{0,1},{1,0},{2,3},{3,2},{4,5},{5,4},{6,7},{7,6},{8,9},{9,8},{10,11... | collective-permute-start | bytes 2359304 | tf_op jit(solution)/shard_map/ppermute | solution.py:146
  28.7 11.9 %collective-permute-start.5 = (s16[528,256]{1,0:T(8,128)(2,1)S(1)}, s16[528,256]{1,0:T(8,128)(2,1)S(1)}, u32[]{:S(2)}, u32[]{:S(2)}) collective-permute-start(s16[528,256]{1,0:T(8,128)(2,1)S(1)} %sum_block.14), channel_id=1, source_target_pairs={{0,4},{1,5},{4,8},{5,9},{8,12},{9,13},{12,14},{13,15},{14,10},{15,... | collective-permute-start | bytes 811016 | tf_op jit(solution)/shard_map/ppermute | solution.py:192
  31.8 11.6 %collective-permute-start.17 = (s16[528,256]{1,0:T(8,128)(2,1)S(1)}, s16[528,256]{1,0:T(8,128)(2,1)S(1)}, u32[]{:S(2)}, u32[]{:S(2)}) collective-permute-start(s16[528,256]{1,0:T(8,128)(2,1)S(1)} %sum_block.22), channel_id=1, source_target_pairs={{0,4},{1,5},{4,8},{5,9},{8,12},{9,13},{12,14},{13,15},{14,10},{15,... | collective-permute-start | bytes 811016 | tf_op jit(solution)/shard_map/ppermute | solution.py:192
  36.5 9.4 %collective-permute-start.13 = (s16[528,256]{1,0:T(8,128)(2,1)S(1)}, s16[528,256]{1,0:T(8,128)(2,1)S(1)}, u32[]{:S(2)}, u32[]{:S(2)}) collective-permute-start(s16[528,256]{1,0:T(8,128)(2,1)S(1)} %sum_block.18), channel_id=1, source_target_pairs={{0,2},{1,3},{4,0},{5,1},{8,4},{9,5},{12,8},{13,9},{14,12},{15,13},... | collective-permute-start | bytes 811016 | tf_op jit(solution)/shard_map/ppermute | solution.py:192
  38.9 11.0 %collective-permute-start.21 = (s16[528,256]{1,0:T(8,128)(2,1)S(1)}, s16[528,256]{1,0:T(8,128)(2,1)S(1)}, u32[]{:S(2)}, u32[]{:S(2)}) collective-permute-start(s16[528,256]{1,0:T(8,128)(2,1)S(1)} %sum_block.26), channel_id=1, source_target_pairs={{0,2},{1,3},{4,0},{5,1},{8,4},{9,5},{12,8},{13,9},{14,12},{15,13},... | collective-permute-start | bytes 811016 | tf_op jit(solution)/shard_map/ppermute | solution.py:192
  40.6 23.5 %collective-permute-start = (bf16[384,1024]{1,0:T(8,128)(2,1)S(1)}, bf16[384,1024]{1,0:T(8,128)(2,1)S(1)}, u32[]{:S(2)}, u32[]{:S(2)}) collective-permute-start(bf16[384,1024]{1,0:T(8,128)(2,1)S(1)} %get-tuple-element.42), channel_id=1, source_target_pairs={{0,1},{1,0},{2,3},{3,2},{4,5},{5,4},{6,7},{7,6},{8,9},{9,8},{10,11... | collective-permute-start | bytes 2359304 | tf_op jit(solution)/shard_map/ppermute | solution.py:146
  43.5 10.6 %collective-permute-start.6 = (s16[528,256]{1,0:T(8,128)(2,1)S(1)}, s16[528,256]{1,0:T(8,128)(2,1)S(1)}, u32[]{:S(2)}, u32[]{:S(2)}) collective-permute-start(s16[528,256]{1,0:T(8,128)(2,1)S(1)} %sum_block.15), channel_id=1, source_target_pairs={{0,4},{1,5},{4,8},{5,9},{8,12},{9,13},{12,14},{13,15},{14,10},{15,... | collective-permute-start | bytes 811016 | tf_op jit(solution)/shard_map/ppermute | solution.py:192
  45.9 11.6 %collective-permute-start.18 = (s16[528,256]{1,0:T(8,128)(2,1)S(1)}, s16[528,256]{1,0:T(8,128)(2,1)S(1)}, u32[]{:S(2)}, u32[]{:S(2)}) collective-permute-start(s16[528,256]{1,0:T(8,128)(2,1)S(1)} %sum_block.23), channel_id=1, source_target_pairs={{0,4},{1,5},{4,8},{5,9},{8,12},{9,13},{12,14},{13,15},{14,10},{15,... | collective-permute-start | bytes 811016 | tf_op jit(solution)/shard_map/ppermute | solution.py:192
  49.9 10.7 %collective-permute-start.14 = (s16[528,256]{1,0:T(8,128)(2,1)S(1)}, s16[528,256]{1,0:T(8,128)(2,1)S(1)}, u32[]{:S(2)}, u32[]{:S(2)}) collective-permute-start(s16[528,256]{1,0:T(8,128)(2,1)S(1)} %sum_block.19), channel_id=1, source_target_pairs={{0,2},{1,3},{4,0},{5,1},{8,4},{9,5},{12,8},{13,9},{14,12},{15,13},... | collective-permute-start | bytes 811016 | tf_op jit(solution)/shard_map/ppermute | solution.py:192
  52.4 11.7 %collective-permute-start.22 = (s16[528,256]{1,0:T(8,128)(2,1)S(1)}, s16[528,256]{1,0:T(8,128)(2,1)S(1)}, u32[]{:S(2)}, u32[]{:S(2)}) collective-permute-start(s16[528,256]{1,0:T(8,128)(2,1)S(1)} %sum_block.27), channel_id=1, source_target_pairs={{0,2},{1,3},{4,0},{5,1},{8,4},{9,5},{12,8},{13,9},{14,12},{15,13},... | collective-permute-start | bytes 811016 | tf_op jit(solution)/shard_map/ppermute | solution.py:192
  56.3 16.3 %collective-permute-start.7 = (s16[528,256]{1,0:T(8,128)(2,1)S(1)}, s16[528,256]{1,0:T(8,128)(2,1)S(1)}, u32[]{:S(2)}, u32[]{:S(2)}) collective-permute-start(s16[528,256]{1,0:T(8,128)(2,1)S(1)} %sum_block.16), channel_id=1, source_target_pairs={{0,4},{1,5},{4,8},{5,9},{8,12},{9,13},{12,14},{13,15},{14,10},{15,... | collective-permute-start | bytes 811016 | tf_op jit(solution)/shard_map/ppermute | solution.py:192
  59.7 9.6 %collective-permute-start.19 = (s16[528,256]{1,0:T(8,128)(2,1)S(1)}, s16[528,256]{1,0:T(8,128)(2,1)S(1)}, u32[]{:S(2)}, u32[]{:S(2)}) collective-permute-start(s16[528,256]{1,0:T(8,128)(2,1)S(1)} %sum_block.24), channel_id=1, source_target_pairs={{0,4},{1,5},{4,8},{5,9},{8,12},{9,13},{12,14},{13,15},{14,10},{15,... | collective-permute-start | bytes 811016 | tf_op jit(solution)/shard_map/ppermute | solution.py:192
  62.8 9.8 %collective-permute-start.15 = (s16[528,256]{1,0:T(8,128)(2,1)S(1)}, s16[528,256]{1,0:T(8,128)(2,1)S(1)}, u32[]{:S(2)}, u32[]{:S(2)}) collective-permute-start(s16[528,256]{1,0:T(8,128)(2,1)S(1)} %sum_block.20), channel_id=1, source_target_pairs={{0,2},{1,3},{4,0},{5,1},{8,4},{9,5},{12,8},{13,9},{14,12},{15,13},... | collective-permute-start | bytes 811016 | tf_op jit(solution)/shard_map/ppermute | solution.py:192
  77.8 14.4 %collective-permute-start.31 = (bf16[512,256]{1,0:T(8,128)(2,1)S(1)}, bf16[512,256]{1,0:T(8,128)(2,1)S(1)}, u32[]{:S(2)}, u32[]{:S(2)}) collective-permute-start(bf16[512,256]{1,0:T(8,128)(2,1)S(1)} %get-tuple-element.24.refs_5_), channel_id=1, source_target_pairs={{0,4},{1,5},{4,8},{5,9},{8,12},{9,13},{12,14},{13,15},{14,10},{15,... | collective-permute-start | bytes 786440 | tf_op jit(solution)/shard_map/ppermute | solution.py:265
  78.2 14.5 %collective-permute-start.34 = (bf16[512,256]{1,0:T(8,128)(2,1)S(1)}, bf16[512,256]{1,0:T(8,128)(2,1)S(1)}, u32[]{:S(2)}, u32[]{:S(2)}) collective-permute-start(bf16[512,256]{1,0:T(8,128)(2,1)S(1)} %get-tuple-element.23.refs_2_), channel_id=1, source_target_pairs={{0,2},{1,3},{4,0},{5,1},{8,4},{9,5},{12,8},{13,9},{14,12},{15,13},... | collective-permute-start | bytes 786440 | tf_op jit(solution)/shard_map/ppermute | solution.py:265
  85.1 11.2 %collective-permute-start.28 = (bf16[512,256]{1,0:T(8,128)(2,1)S(1)}, bf16[512,256]{1,0:T(8,128)(2,1)S(1)}, u32[]{:S(2)}, u32[]{:S(2)}) collective-permute-start(bf16[512,256]{1,0:T(8,128)(2,1)S(1)} %collective-permute-done.27.refs_5_), channel_id=1, source_target_pairs={{0,2},{1,3},{4,0},{5,1},{8,4},{9,5},{12,8},{13,9},{14,12},{15,13},... | collective-permute-start | bytes 786440 | tf_op jit(solution)/shard_map/ppermute | solution.py:265
  86.7 11.2 %collective-permute-start.24 = (bf16[512,256]{1,0:T(8,128)(2,1)S(1)}, bf16[512,256]{1,0:T(8,128)(2,1)S(1)}, u32[]{:S(2)}, u32[]{:S(2)}) collective-permute-start(bf16[512,256]{1,0:T(8,128)(2,1)S(1)} %collective-permute-done.23.refs_2_), channel_id=1, source_target_pairs={{0,4},{1,5},{4,8},{5,9},{8,12},{9,13},{12,14},{13,15},{14,10},{15,... | collective-permute-start | bytes 786440 | tf_op jit(solution)/shard_map/ppermute | solution.py:265
  92.3 11.2 %collective-permute-start.32 = (bf16[512,256]{1,0:T(8,128)(2,1)S(1)}, bf16[512,256]{1,0:T(8,128)(2,1)S(1)}, u32[]{:S(2)}, u32[]{:S(2)}) collective-permute-start(bf16[512,256]{1,0:T(8,128)(2,1)S(1)} %collective-permute-done.31.refs_8_), channel_id=1, source_target_pairs={{0,4},{1,5},{4,8},{5,9},{8,12},{9,13},{12,14},{13,15},{14,10},{15,... | collective-permute-start | bytes 786440 | tf_op jit(solution)/shard_map/ppermute | solution.py:265
  92.7 11.2 %collective-permute-start.35 = (bf16[512,256]{1,0:T(8,128)(2,1)S(1)}, bf16[512,256]{1,0:T(8,128)(2,1)S(1)}, u32[]{:S(2)}, u32[]{:S(2)}) collective-permute-start(bf16[512,256]{1,0:T(8,128)(2,1)S(1)} %collective-permute-done.34.refs_11_), channel_id=1, source_target_pairs={{0,2},{1,3},{4,0},{5,1},{8,4},{9,5},{12,8},{13,9},{14,12},{15,13},... | collective-permute-start | bytes 786440 | tf_op jit(solution)/shard_map/ppermute | solution.py:265
  96.3 11.2 %collective-permute-start.29 = (bf16[512,256]{1,0:T(8,128)(2,1)S(1)}, bf16[512,256]{1,0:T(8,128)(2,1)S(1)}, u32[]{:S(2)}, u32[]{:S(2)}) collective-permute-start(bf16[512,256]{1,0:T(8,128)(2,1)S(1)} %collective-permute-done.28.refs_5_), channel_id=1, source_target_pairs={{0,2},{1,3},{4,0},{5,1},{8,4},{9,5},{12,8},{13,9},{14,12},{15,13},... | collective-permute-start | bytes 786440 | tf_op jit(solution)/shard_map/ppermute | solution.py:265
  97.9 11.2 %collective-permute-start.25 = (bf16[512,256]{1,0:T(8,128)(2,1)S(1)}, bf16[512,256]{1,0:T(8,128)(2,1)S(1)}, u32[]{:S(2)}, u32[]{:S(2)}) collective-permute-start(bf16[512,256]{1,0:T(8,128)(2,1)S(1)} %collective-permute-done.24.refs_2_), channel_id=1, source_target_pairs={{0,4},{1,5},{4,8},{5,9},{8,12},{9,13},{12,14},{13,15},{14,10},{15,... | collective-permute-start | bytes 786440 | tf_op jit(solution)/shard_map/ppermute | solution.py:265
  103.5 14.2 %collective-permute-start.33 = (bf16[512,256]{1,0:T(8,128)(2,1)S(1)}, bf16[512,256]{1,0:T(8,128)(2,1)S(1)}, u32[]{:S(2)}, u32[]{:S(2)}) collective-permute-start(bf16[512,256]{1,0:T(8,128)(2,1)S(1)} %collective-permute-done.32.refs_8_), channel_id=1, source_target_pairs={{0,4},{1,5},{4,8},{5,9},{8,12},{9,13},{12,14},{13,15},{14,10},{15,... | collective-permute-start | bytes 786440 | tf_op jit(solution)/shard_map/ppermute | solution.py:265
  103.9 13.7 %collective-permute-start.36 = (bf16[512,256]{1,0:T(8,128)(2,1)S(1)}, bf16[512,256]{1,0:T(8,128)(2,1)S(1)}, u32[]{:S(2)}, u32[]{:S(2)}) collective-permute-start(bf16[512,256]{1,0:T(8,128)(2,1)S(1)} %collective-permute-done.35.refs_11_), channel_id=1, source_target_pairs={{0,2},{1,3},{4,0},{5,1},{8,4},{9,5},{12,8},{13,9},{14,12},{15,13},... | collective-permute-start | bytes 786440 | tf_op jit(solution)/shard_map/ppermute | solution.py:265
  107.5 13.1 %collective-permute-start.30 = (bf16[512,256]{1,0:T(8,128)(2,1)S(1)}, bf16[512,256]{1,0:T(8,128)(2,1)S(1)}, u32[]{:S(2)}, u32[]{:S(2)}) collective-permute-start(bf16[512,256]{1,0:T(8,128)(2,1)S(1)} %collective-permute-done.29.refs_5_), channel_id=1, source_target_pairs={{0,2},{1,3},{4,0},{5,1},{8,4},{9,5},{12,8},{13,9},{14,12},{15,13},... | collective-permute-start | bytes 786440 | tf_op jit(solution)/shard_map/ppermute | solution.py:265
  109.1 11.5 %collective-permute-start.26 = (bf16[512,256]{1,0:T(8,128)(2,1)S(1)}, bf16[512,256]{1,0:T(8,128)(2,1)S(1)}, u32[]{:S(2)}, u32[]{:S(2)}) collective-permute-start(bf16[512,256]{1,0:T(8,128)(2,1)S(1)} %collective-permute-done.25.refs_2_), channel_id=1, source_target_pairs={{0,4},{1,5},{4,8},{5,9},{8,12},{9,13},{12,14},{13,15},{14,10},{15,... | collective-permute-start | bytes 786440 | tf_op jit(solution)/shard_map/ppermute | solution.py:265
  (13 other events, 104.8 us)

commit v2 on v0

v2 whole, which is shorter than its diff:
```python
import functools

import jax
import jax.numpy as jnp
from jax import lax
from jax.experimental import pallas as pl
from jax.experimental.pallas import tpu as pltpu
from jax.sharding import PartitionSpec as P

STEPS = 256.0
TOP = 32700.0
PAD = 16
LANES = 128
VMEM = 24 * 1024 * 1024


def ring_of(devices):
    chips = devices[0, ::2]
    where = [getattr(d, "coords", None) for d in chips]
    count = len(where)
    plain = list(range(count))
    if any(w is None for w in where):
        where = [(0, k % 2, k // 2) for k in plain]
    varying = [k for k in range(3) if len({w[k] for w in where}) > 1]
    if len(varying) != 2:
        return sorted(plain, key=lambda k: tuple(where[k]))
    short, long = sorted(varying, key=lambda k: len({w[k] for w in where}))
    low = min(w[short] for w in where)
    if len({w[short] for w in where}) != 2:
        return plain
    up = sorted((k for k in plain if where[k][short] == low), key=lambda k: where[k][long])
    down = sorted((k for k in plain if where[k][short] != low), key=lambda k: -where[k][long])
    return up + down


def owners_of(ring, distances):
    chip = lax.div(lax.axis_index("ind"), 2)
    spot = jnp.int32(0)
    for k, c in enumerate(ring):
        spot = jnp.where(chip == c, k, spot)
    found = []
    for d in distances:
        at = lax.rem(spot + d, len(ring))
        owner = jnp.int32(ring[0])
        for k, c in enumerate(ring):
            owner = jnp.where(at == k, c, owner)
        found.append(owner)
    return found


def pick_kernel(ring, wanted, block, genotype_ref, before_ref, *refs):
    outs, sems = refs[:-1], refs[-1]
    core = lax.rem(lax.axis_index("ind"), 2)
    owners = dict(zip([d for d, _ in wanted], owners_of(ring, [d for d, _ in wanted])))
    copies = []
    for k, (d, swapped) in enumerate(wanted):
        parity = 1 - core if swapped else core
        at = pl.multiple_of((2 * owners[d] + parity) * block, LANES)
        copies.append(
            pltpu.make_async_copy(genotype_ref.at[:, pl.ds(at, block)], outs[k], sems.at[k])
        )
        copies[-1].start()
    for copy in copies:
        copy.wait()


def flip_kernel(before_ref, mine_ref, other_ref, out_ref):
    people = mine_ref.shape[0]
    out_ref[:, :people] = mine_ref[...].T
    out_ref[:, people:] = other_ref[...].T


def local_sum(res_ref, own_ref, peer_ref, low, high):
    people = own_ref.shape[0]
    return jnp.dot(
        res_ref[:, :people], own_ref[:, low:high], preferred_element_type=jnp.float32
    ) + jnp.dot(
        res_ref[:, people:], peer_ref[:, low:high], preferred_element_type=jnp.float32
    )


def decode(ref):
    rows = ref.shape[0] - PAD
    code = ref[rows:, :].astype(jnp.float32)[:1, :]
    return ref[:rows, :].astype(jnp.float32) * (jnp.exp2(code * (1.0 / STEPS)) * (1.0 / TOP))


def encode(ref, tiles):
    height = tiles[0].shape[0]
    top = functools.reduce(jnp.maximum, [jnp.abs(t) for t in tiles])
    top = jnp.maximum(jnp.max(top, axis=0, keepdims=True), 1e-30)
    code = jnp.ceil(jnp.log2(top) * STEPS)
    scale = TOP * jnp.exp2(code * (-1.0 / STEPS))
    for k, t in enumerate(tiles):
        ref[k * height : (k + 1) * height, :] = (
            jnp.round(t * scale).astype(jnp.int32).astype(jnp.int16)
        )
    ref[len(tiles) * height :, :] = (
        jnp.broadcast_to(code, (PAD, LANES)).astype(jnp.int32).astype(jnp.int16)
    )


def tiles_of(total):
    return [total[:, k : k + LANES] for k in range(0, total.shape[1], LANES)]


def far_kernel(low, high, before_ref, res_ref, own_ref, peer_ref, right_ref, left_ref):
    tiles = tiles_of(local_sum(res_ref, own_ref, peer_ref, low, high))
    half = len(tiles) // 2
    encode(right_ref, tiles[:half])
    encode(left_ref, tiles[half:])


def hop_kernel(
    low, high, before_ref, res_ref, own_ref, peer_ref, own_left_ref, peer_left_ref, got_right_ref,
    got_left_ref, right_ref, left_ref
):
    for way, own, peer, got_ref, out_ref in (
        (0, own_ref, peer_ref, got_right_ref, right_ref),
        (1, own_left_ref, peer_left_ref, got_left_ref, left_ref),
    ):
        tiles = tiles_of(local_sum(res_ref, own, peer, low, high))
        got = decode(got_ref)
        height = tiles[0].shape[0]
        count = got.shape[0] // height
        first = 0 if way == 0 else len(tiles) - count
        for k in range(count):
            tiles[first + k] = tiles[first + k] + got[k * height : (k + 1) * height, :]
        encode(out_ref, tiles)


def near_kernel(before_ref, res_ref, own_ref, peer_ref, out_ref):
    out_ref[...] = local_sum(res_ref, own_ref, peer_ref, 0, own_ref.shape[1])


def update_kernel(total, low, before_ref, corr_ref, right_ref, left_ref, incl_ref, mean_ref, prior_ref,
                  scale_ref, *rest):
    incl_new_ref, mean_new_ref, effect_ref = rest[-3:]
    height = corr_ref.shape[0]
    right, left = decode(right_ref), decode(left_ref)
    scale = scale_ref[...]
    shrink = scale / (1.0 + scale)
    start = prior_ref[...] - 0.5 * jnp.log1p(scale)
    steep = 0.5 * total * shrink
    halves = [(right, 0), (left, 1)]
    tiles = effect_ref.shape[0] // LANES
    for k in range(tiles):
        corr = corr_ref[:, low + k * LANES : low + (k + 1) * LANES]
        for got, way in halves:
            count = got.shape[0] // height
            first = 0 if way == 0 else tiles - count
            if first <= k < first + count:
                corr = corr + got[(k - first) * height : (k - first + 1) * height, :]
        rows = slice(k * LANES, (k + 1) * LANES)
        incl = incl_ref[rows, :]
        stat = corr.T / total + incl * mean_ref[rows, :]
        mean_new = stat * shrink
        incl_new = 0.5 * incl + 0.5 * jax.nn.sigmoid(start + steep * stat * stat)
        incl_new_ref[rows, :] = incl_new
        mean_new_ref[rows, :] = mean_new
        effect_ref[rows, :] = (incl_new * mean_new).astype(jnp.bfloat16)


def eta_kernel(ring, low, part, first, before_ref, gathered_ref, *refs):
    size = len(ring)
    own, peer = refs[:size], refs[size : 2 * size]
    out_ref, out_other_ref = refs[-2:]
    mine = other = None
    for d, owner in enumerate(owners_of(ring, range(size))):
        effect = gathered_ref[pl.ds(pl.multiple_of(owner * part, part), part), :]
        a = jnp.dot(own[d][:, low : low + part], effect, preferred_element_type=jnp.float32)
        b = jnp.dot(peer[d][:, low : low + part], effect, preferred_element_type=jnp.float32)
        mine = a if mine is None else mine + a
        other = b if other is None else other + b
    if not first:
        mine = mine + refs[2 * size][...]
        other = other + refs[2 * size + 1][...]
    out_ref[...] = mine
    out_other_ref[...] = other


def end_kernel(eta_ref, got_ref, labels_ref, offset_ref, out_ref):
    eta = eta_ref[...] + got_ref[...] + offset_ref[...]
    out_ref[...] = 4.0 * (labels_ref[...].astype(jnp.float32) - jax.nn.sigmoid(eta))


def on_device(ring, genotype, residual, labels, incl_old, mean_old, prior_logit, slab_scale, offset):
    n = lax.axis_size("ind")
    people, cols = residual.shape
    total = float(people * n)
    block = incl_old.shape[0]
    size = len(ring)
    reach = size // 2
    pieces = 2 if block % (4 * LANES) == 0 else 1
    part = block // pieces
    f32, bf16 = jnp.float32, jnp.bfloat16
    params = pltpu.CompilerParams(vmem_limit_bytes=VMEM)

    swap = [(k, k ^ 1) for k in range(n)]
    right, left = [], []
    for k, chip in enumerate(ring):
        for c in range(2):
            right.append((2 * chip + c, 2 * ring[(k + 1) % size] + c))
            left.append((2 * chip + c, 2 * ring[(k - 1) % size] + c))

    anywhere = pl.BlockSpec(memory_space=pl.ANY)

    def after(before, args):
        return [anywhere] + [pl.BlockSpec()] * len(args)

    peer, own = {}, {}

    def pick(distances, before):
        wanted = [(d, True) for d in distances] + [(d, False) for d in distances]
        found = pl.pallas_call(
            functools.partial(pick_kernel, ring, wanted, block),
            in_specs=[pl.BlockSpec(memory_space=pltpu.HBM), anywhere],
            out_specs=[anywhere] * len(wanted),
            out_shape=[jax.ShapeDtypeStruct((people, block), bf16)] * len(wanted),
            scratch_shapes=[pltpu.SemaphoreType.DMA((len(wanted),))],
            compiler_params=params,
            name="pick_blocks",
        )(pltpu.with_memory_space_constraint(genotype, pltpu.HBM), before)
        for k, d in enumerate(distances):
            peer[d] = lax.ppermute(found[k], "ind", swap)
            own[d] = found[len(distances) + k]
        return found[0]

    def around(d):
        return [0] if d == 0 else [d, size - d] if 2 * d != size else [d]

    residual_other = lax.ppermute(residual, "ind", swap)
    last = pick(around(reach), residual)
    if reach > 1:
        last = pick(around(reach - 1), last)
    res = last = pl.pallas_call(
        flip_kernel,
        in_specs=after(last, (residual, residual_other)),
        out_shape=jax.ShapeDtypeStruct((cols, 2 * people), bf16),
        compiler_params=params,
        name="flip",
    )(last, residual, residual_other)

    def message(width):
        return jax.ShapeDtypeStruct((width // LANES * cols + PAD, LANES), jnp.int16)

    def dot_cost(width):
        return pl.CostEstimate(
            flops=4 * people * width * cols,
            bytes_accessed=4 * people * width + 4 * people * cols + 4 * width * cols,
            transcendentals=0,
        )

    got = {}
    for d in range(reach, 0, -1):
        for piece in range(pieces):
            low, high = piece * part, (piece + 1) * part
            if d == reach:
                kernel, width, name = far_kernel, part // 2, "sum_far"
                args = (res, own[d], peer[d])
            else:
                kernel, width, name = hop_kernel, part, "sum_hop"
                args = (res, own[d], peer[d], own[size - d], peer[size - d], *got[piece])
            sent = pl.pallas_call(
                functools.partial(kernel, low, high),
                in_specs=after(last, args),
                out_shape=[message(width)] * 2,
                compiler_params=params,
                cost_estimate=dot_cost(2 * width),
                name=name,
            )(last, *args)
            last = sent[0]
            got[piece] = (lax.ppermute(sent[0], "ind", right), lax.ppermute(sent[1], "ind", left))
        if d > 1:
            last = pick(around(d - 2), last)
    if reach == 1:
        last = pick([0], last)

    near = last = pl.pallas_call(
        near_kernel,
        in_specs=after(last, (res, own[0], peer[0])),
        out_shape=jax.ShapeDtypeStruct((cols, block), f32),
        compiler_params=params,
        cost_estimate=dot_cost(block),
        name="sum_near",
    )(last, res, own[0], peer[0])

    prior = prior_logit.reshape(1, cols)
    scale = slab_scale.reshape(1, cols)

    def full(shape):
        return pl.BlockSpec(shape, lambda i: (0,) * len(shape))

    outs = ()
    gathered = []
    groups = [[2 * chip + c for chip in range(size)] for c in range(2)]
    for piece in range(pieces):
        rows = pl.BlockSpec((part, cols), lambda i, piece=piece: (piece, 0))
        incl_new, mean_new, effect = pl.pallas_call(
            functools.partial(update_kernel, total, piece * part),
            grid=(1,),
            in_specs=[anywhere, full((cols, block))]
            + [full(m.shape) for m in got[piece]]
            + [rows] * 2
            + [full((1, cols))] * 2
            + [anywhere] * len(outs),
            out_specs=[rows, rows, full((part, cols))],
            out_shape=[
                jax.ShapeDtypeStruct((block, cols), f32),
                jax.ShapeDtypeStruct((block, cols), f32),
                jax.ShapeDtypeStruct((part, cols), bf16),
            ],
            input_output_aliases={8: 0, 9: 1} if outs else {},
            compiler_params=params,
            name="update",
        )(last, near, *got[piece], incl_old, mean_old, prior, scale, *outs)
        outs = (incl_new, mean_new)
        last = effect
        gathered.append(
            lax.all_gather(effect, "ind", axis=0, tiled=True, axis_index_groups=groups)
        )

    eta_shape = jax.ShapeDtypeStruct((people, cols), f32)
    eta = ()
    for piece in range(pieces):
        args = (
            gathered[piece], *[own[d] for d in range(size)], *[peer[d] for d in range(size)], *eta
        )
        eta = pl.pallas_call(
            functools.partial(eta_kernel, ring, piece * part, part, not eta),
            in_specs=after(last, args),
            out_shape=[eta_shape] * 2,
            compiler_params=params,
            cost_estimate=pl.CostEstimate(
                flops=4 * people * part * size * cols,
                bytes_accessed=size * (4 * people * part + 2 * part * cols),
                transcendentals=0,
            ),
            name="add_eta",
        )(last, *args)
        last = eta[0]

    eta_got = lax.ppermute(eta[1], "ind", swap)
    resid_new = pl.pallas_call(
        end_kernel,
        out_shape=eta_shape,
        compiler_params=params,
        name="new_residual",
    )(eta[0], eta_got, labels, offset.reshape(1, cols))
    return (outs[0], outs[1], resid_new)


def solution(mesh):
    split = P(("groups", "ind"), None)
    return jax.shard_map(
        functools.partial(on_device, ring_of(mesh.devices)),
        mesh=mesh,
        in_specs=(split, split, split, split, split, P(), P(), P()),
        out_specs=(split, split, split),
        check_vma=False,
    )
```

time: 303 us -> 204 us (0.67)
  waiting for transfers between devices: 255 us -> 102 us
  local copies, waits for them, and re-layouts: 2.56 us -> 42.5 us
  matrix products: 28.5 us -> 0 us
  Pallas kernels: 0 us -> 22.6 us
  starting transfers between devices: 0.08 us -> 20.9 us
  other arithmetic: 3.04 us -> 0 us
    reduce_scatter x1 -> x0, waiting for transfers between devices: 181 us -> none  [on_device(): lax.psum_scatter(lax.dot_general(columns, residual, (((0,), (0,)), ((), (...]
    ppermute x0 -> x26, waiting for transfers between devices: none -> 40.9 us  [the longest x8 18.8 us: on_device(): lax.ppermute(sent[0], 'ind', right)]
    unnamed x16 -> x122, local copies, waits for them, and re-layouts: 2.56 us -> 42.5 us
    dot_general x2 -> x0, matrix products: 28.5 us -> none  [the longest x1 14.9 us: on_device(): lax.dot_general(columns, residual, (((0,), (0,)), ((), ())), preferred_el...]
    pallas_call x0 -> x20, Pallas kernels: none -> 22.6 us  [the longest x5 8.52 us: pick(): pl.pallas_call(functools.partial(pick_kernel, ring, wanted, block), in_sp...]
    ppermute x0 -> x26, starting transfers between devices: none -> 20.9 us  [the longest x8 12.5 us: on_device(): lax.ppermute(sent[0], 'ind', right)]
    all_gather x1 -> x2, waiting for transfers between devices: 73.9 us -> 60.8 us  [on_device(): lax.all_gather(effect, 'ind', axis=0, tiled=True, axis_index_groups=groups)]
    convert_element_type x1 -> x0, other arithmetic: 3.03 us -> none  [update(): effect = (incl_new * mean_new).astype(jnp.bfloat16)]
  transfers between devices with their start and end apart: 2 -> 28, of which waited for: 2 -> 17; matrix products, arithmetic and copies ran while one was open for 0% -> 0% of each run, Pallas kernels for 0% -> 8%
where the time goes in v2:
time: 204 us; the launch traced here: 202 us
  waiting for transfers between devices  102 us (50%)
  local copies, waits for them, and re-layouts  42.5 us (21%)
  Pallas kernels  22.6 us (11%)
  starting transfers between devices  20.9 us (10%)
  between operations  14.5 us (7%)
    all_gather x2, waiting for transfers between devices, on_device(): lax.all_gather(effect, 'ind', axis=0, tiled=True, axis_index_groups=groups)  60.8 us
    unnamed x122, local copies, waits for them, and re-layouts  42.5 us
    ppermute x8, waiting for transfers between devices, on_device(): lax.ppermute(sent[0], 'ind', right)  18.8 us
    ppermute x8, waiting for transfers between devices, on_device(): lax.ppermute(sent[1], 'ind', left)  17.5 us
    ppermute x8, starting transfers between devices, on_device(): lax.ppermute(sent[0], 'ind', right)  12.5 us
    pallas_call x5, Pallas kernels, pick(): pl.pallas_call(functools.partial(pick_kernel, ring, wanted, block), in_sp...  8.52 us
    pallas_call x8, Pallas kernels, on_device(): pl.pallas_call(functools.partial(kernel, low, high), in_specs=after(last,...  6.07 us
    ppermute x8, starting transfers between devices, on_device(): lax.ppermute(sent[1], 'ind', left)  5.72 us
  transfers between devices with their start and end apart: 28, of which 17 were waited for; matrix products, arithmetic and copies ran while one was open for 0% of the time, Pallas kernels for 8%

profile of v2, /device:TPU:0, one launch (start us, length us, event | category | flops | bytes accessed | tf_op | source)
XLA Modules:
  0.0 202.2 jit_solution(6237530569198203844)
XLA Ops:
  8.1 1.4 pick_blocks.5
  10.1 1.9 pick_blocks.6
  12.9 2.9 %collective-permute-done.other_ref = bf16[384,256]{1,0:T(8,128)(2,1)S(1)} collective-permute-done((bf16[384,256]{1,0:T(8,128)(2,1)S(1)}, bf16[384,256]{1,0:T(8,128)(2,1)S(1)}, u32[]{:S(2)}, u32[]{:S(2)}) %collective-permute-start) | collective-permute-done | bytes 196640 | tf_op jit(solution)/shard_map/ppermute | solution.py:232
  17.0 1.9 pick_blocks.7
  19.5 2.9 %collective-permute-start.4 = (s16[528,128]{1,0:T(8,128)(2,1)S(1)}, s16[528,128]{1,0:T(8,128)(2,1)S(1)}, u32[]{:S(2)}, u32[]{:S(2)}) collective-permute-start(s16[528,128]{1,0:T(8,128)(2,1)S(1)} %get-tuple-element.48.before_ref), channel_id=1, source_target_pairs={{0,4},{1,5},{4,8},{5,9},{8,12},{9,13},{12,14},{13,15},{14,10},{15,... | collective-permute-start | bytes 405512 | tf_op jit(solution)/shard_map/ppermute | solution.py:273
  22.4 2.0 collective-permute-start.6
  24.4 2.3 %collective-permute-done.4.got_right_ref = s16[528,128]{1,0:T(8,128)(2,1)S(1)} collective-permute-done((s16[528,128]{1,0:T(8,128)(2,1)S(1)}, s16[528,128]{1,0:T(8,128)(2,1)S(1)}, u32[]{:S(2)}, u32[]{:S(2)}) %collective-permute-start.4) | collective-permute-done | bytes 135200 | tf_op jit(solution)/shard_map/ppermute | solution.py:273
  28.6 1.6 collective-permute-start.10
  31.7 8.6 %collective-permute-done.7.got_left_ref = s16[528,128]{1,0:T(8,128)(2,1)S(1)} collective-permute-done((s16[528,128]{1,0:T(8,128)(2,1)S(1)}, s16[528,128]{1,0:T(8,128)(2,1)S(1)}, u32[]{:S(2)}, u32[]{:S(2)}) %collective-permute-start.7) | collective-permute-done | bytes 135200 | tf_op jit(solution)/shard_map/ppermute | solution.py:273
  41.1 1.9 pick_blocks.8
  43.0 1.6 collective-permute-start.12
  46.5 3.0 %collective-permute-done.12.got_right_ref = s16[1040,128]{1,0:T(8,128)(2,1)S(1)} collective-permute-done((s16[1040,128]{1,0:T(8,128)(2,1)S(1)}, s16[1040,128]{1,0:T(8,128)(2,1)S(1)}, u32[]{:S(2)}, u32[]{:S(2)}) %collective-permute-start.12) | collective-permute-done | bytes 266272 | tf_op jit(solution)/shard_map/ppermute | solution.py:273
  49.5 1.6 collective-permute-done.13.got_left_ref
  52.0 1.4 pick_blocks.9
  53.5 1.6 collective-permute-start.16
  55.6 1.5 collective-permute-start.18
  57.6 5.1 %collective-permute-done.16.got_right_ref = s16[1040,128]{1,0:T(8,128)(2,1)S(1)} collective-permute-done((s16[1040,128]{1,0:T(8,128)(2,1)S(1)}, s16[1040,128]{1,0:T(8,128)(2,1)S(1)}, u32[]{:S(2)}, u32[]{:S(2)}) %collective-permute-start.16) | collective-permute-done | bytes 266272 | tf_op jit(solution)/shard_map/ppermute | solution.py:273
  62.7 1.6 collective-permute-done.17.got_left_ref
  65.8 1.4 collective-permute-start.22
  68.4 1.6 collective-permute-done.19.got_left_ref
  72.3 1.4 collective-permute-done.21.right_ref
  74.9 1.3 update.2
  77.7 1.4 collective-permute-start.24
  79.2 5.8 %collective-permute-done.23.right_ref = s16[1040,128]{1,0:T(8,128)(2,1)S(1)} collective-permute-done((s16[1040,128]{1,0:T(8,128)(2,1)}, s16[1040,128]{1,0:T(8,128)(2,1)S(1)}, u32[]{:S(2)}, u32[]{:S(2)}) %collective-permute-start.23) | collective-permute-done | bytes 266272 | tf_op jit(solution)/shard_map/ppermute | solution.py:273
  85.0 1.8 collective-permute-done.24.left_ref
  92.3 31.5 %all-gather.3.cloned.1.call-done.gathered_ref = bf16[4096,256]{1,0:T(8,128)(2,1)} async-done(((bf16[512,256]{1,0:T(8,128)(2,1)}), bf16[4096,256]{1,0:T(8,128)(2,1)}) %all-gather.3.cloned.1.call-update) | async-done | bytes 2097168 | tf_op jit(solution)/shard_map/all_gather | solution.py:320
  138.6 1.6 copy-done.43
  141.1 1.8 add_eta.2
  144.4 29.3 %all-gather.5.cloned.1.call-done.gathered_ref = bf16[4096,256]{1,0:T(8,128)(2,1)} async-done(((bf16[512,256]{1,0:T(8,128)(2,1)}), bf16[4096,256]{1,0:T(8,128)(2,1)}) %all-gather.5.cloned.1.call-update) | async-done | bytes 2097168 | tf_op jit(solution)/shard_map/all_gather | solution.py:320
  187.3 1.6 copy-done.44
  190.9 1.8 add_eta.3
  192.8 1.7 collective-permute-done.25.got_ref
  (168 shorter events, 59.0 us)
Async XLA Ops:
  7.2 116.6 %all-gather.3.cloned.1.call-start = ((), (), s32[]{:S(2)}) async-start(), calls=%async_computation | async-start | bytes 2359296 | tf_op jit(solution)/shard_map/all_gather | solution.py:320
  9.6 6.3 %collective-permute-start.1 = (bf16[384,1024]{1,0:T(8,128)(2,1)S(1)}, bf16[384,1024]{1,0:T(8,128)(2,1)S(1)}, u32[]{:S(2)}, u32[]{:S(2)}) collective-permute-start(bf16[384,1024]{1,0:T(8,128)(2,1)S(1)} %get-tuple-element.45.before_ref), channel_id=1, source_target_pairs={{0,1},{1,0},{2,3},{3,2},{4,5},{5,4},{6,7},{7,6},{8,9},{9,8},{10,11... | collective-permute-start | bytes 2359304 | tf_op jit(solution)/shard_map/ppermute | solution.py:225
  12.0 10.4 %collective-permute-start.2 = (bf16[384,1024]{1,0:T(8,128)(2,1)S(1)}, bf16[384,1024]{1,0:T(8,128)(2,1)S(1)}, u32[]{:S(2)}, u32[]{:S(2)}) collective-permute-start(bf16[384,1024]{1,0:T(8,128)(2,1)S(1)} %get-tuple-element.46.before_ref), channel_id=1, source_target_pairs={{0,1},{1,0},{2,3},{3,2},{4,5},{5,4},{6,7},{7,6},{8,9},{9,8},{10,11... | collective-permute-start | bytes 2359304 | tf_op jit(solution)/shard_map/ppermute | solution.py:225
  12.3 10.0 %collective-permute-start.3 = (bf16[384,1024]{1,0:T(8,128)(2,1)S(1)}, bf16[384,1024]{1,0:T(8,128)(2,1)S(1)}, u32[]{:S(2)}, u32[]{:S(2)}) collective-permute-start(bf16[384,1024]{1,0:T(8,128)(2,1)S(1)} %get-tuple-element.53), channel_id=1, source_target_pairs={{0,1},{1,0},{2,3},{3,2},{4,5},{5,4},{6,7},{7,6},{8,9},{9,8},{10,11... | collective-permute-start | bytes 2359304 | tf_op jit(solution)/shard_map/ppermute | solution.py:225
  12.5 3.2 %collective-permute-start = (bf16[384,256]{1,0:T(8,128)(2,1)S(1)}, bf16[384,256]{1,0:T(8,128)(2,1)S(1)}, u32[]{:S(2)}, u32[]{:S(2)}) collective-permute-start(bf16[384,256]{1,0:T(8,128)(2,1)S(1)} %copy-done.52), channel_id=1, source_target_pairs={{0,1},{1,0},{2,3},{3,2},{4,5},{5,4},{6,7},{7,6},{8,9},{9,8},{10,11... | collective-permute-start | bytes 589832 | tf_op jit(solution)/shard_map/ppermute | solution.py:232
  18.9 32.2 %copy-start.3 = (bf16[384,1024]{1,0:T(8,128)(2,1)}, bf16[384,1024]{1,0:T(8,128)(2,1)S(1)}, u32[]{:S(2)}) copy-start(bf16[384,1024]{1,0:T(8,128)(2,1)S(1)} %get-tuple-element.59.own_ref.refs_2_) | copy-start | bytes 2359300
  18.9 32.2 %copy-start.6 = (bf16[384,1024]{1,0:T(8,128)(2,1)}, bf16[384,1024]{1,0:T(8,128)(2,1)S(1)}, u32[]{:S(2)}) copy-start(bf16[384,1024]{1,0:T(8,128)(2,1)S(1)} %get-tuple-element.60.own_left_ref.refs_6_) | copy-start | bytes 2359300
  18.9 26.2 %collective-permute-start.8 = (bf16[384,1024]{1,0:T(8,128)(2,1)S(1)}, bf16[384,1024]{1,0:T(8,128)(2,1)S(1)}, u32[]{:S(2)}, u32[]{:S(2)}) collective-permute-start(bf16[384,1024]{1,0:T(8,128)(2,1)S(1)} %get-tuple-element.50.before_ref), channel_id=1, source_target_pairs={{0,1},{1,0},{2,3},{3,2},{4,5},{5,4},{6,7},{7,6},{8,9},{9,8},{10,11... | collective-permute-start | bytes 2359304 | tf_op jit(solution)/shard_map/ppermute | solution.py:225
  19.3 26.4 %collective-permute-start.9 = (bf16[384,1024]{1,0:T(8,128)(2,1)S(1)}, bf16[384,1024]{1,0:T(8,128)(2,1)S(1)}, u32[]{:S(2)}, u32[]{:S(2)}) collective-permute-start(bf16[384,1024]{1,0:T(8,128)(2,1)S(1)} %get-tuple-element.61), channel_id=1, source_target_pairs={{0,1},{1,0},{2,3},{3,2},{4,5},{5,4},{6,7},{7,6},{8,9},{9,8},{10,11... | collective-permute-start | bytes 2359304 | tf_op jit(solution)/shard_map/ppermute | solution.py:225
  19.5 7.2 %collective-permute-start.4 = (s16[528,128]{1,0:T(8,128)(2,1)S(1)}, s16[528,128]{1,0:T(8,128)(2,1)S(1)}, u32[]{:S(2)}, u32[]{:S(2)}) collective-permute-start(s16[528,128]{1,0:T(8,128)(2,1)S(1)} %get-tuple-element.48.before_ref), channel_id=1, source_target_pairs={{0,4},{1,5},{4,8},{5,9},{8,12},{9,13},{12,14},{13,15},{14,10},{15,... | collective-permute-start | bytes 405512 | tf_op jit(solution)/shard_map/ppermute | solution.py:273
  22.4 5.4 %collective-permute-start.5 = (s16[528,128]{1,0:T(8,128)(2,1)S(1)}, s16[528,128]{1,0:T(8,128)(2,1)S(1)}, u32[]{:S(2)}, u32[]{:S(2)}) collective-permute-start(s16[528,128]{1,0:T(8,128)(2,1)S(1)} %get-tuple-element.54), channel_id=1, source_target_pairs={{0,2},{1,3},{4,0},{5,1},{8,4},{9,5},{12,8},{13,9},{14,12},{15,13},... | collective-permute-start | bytes 405512 | tf_op jit(solution)/shard_map/ppermute | solution.py:273
  22.4 8.3 %collective-permute-start.6 = (s16[528,128]{1,0:T(8,128)(2,1)S(1)}, s16[528,128]{1,0:T(8,128)(2,1)S(1)}, u32[]{:S(2)}, u32[]{:S(2)}) collective-permute-start(s16[528,128]{1,0:T(8,128)(2,1)S(1)} %get-tuple-element.49.before_ref), channel_id=1, source_target_pairs={{0,4},{1,5},{4,8},{5,9},{8,12},{9,13},{12,14},{13,15},{14,10},{15,... | collective-permute-start | bytes 405512 | tf_op jit(solution)/shard_map/ppermute | solution.py:273
  28.6 16.0 %collective-permute-start.10 = (s16[1040,128]{1,0:T(8,128)(2,1)S(1)}, s16[1040,128]{1,0:T(8,128)(2,1)S(1)}, u32[]{:S(2)}, u32[]{:S(2)}) collective-permute-start(s16[1040,128]{1,0:T(8,128)(2,1)S(1)} %get-tuple-element.55.before_ref), channel_id=1, source_target_pairs={{0,4},{1,5},{4,8},{5,9},{8,12},{9,13},{12,14},{13,15},{14,10},{15,... | collective-permute-start | bytes 798728 | tf_op jit(solution)/shard_map/ppermute | solution.py:273
  30.3 14.9 %collective-permute-start.11 = (s16[1040,128]{1,0:T(8,128)(2,1)S(1)}, s16[1040,128]{1,0:T(8,128)(2,1)S(1)}, u32[]{:S(2)}, u32[]{:S(2)}) collective-permute-start(s16[1040,128]{1,0:T(8,128)(2,1)S(1)} %get-tuple-element.62), channel_id=1, source_target_pairs={{0,2},{1,3},{4,0},{5,1},{8,4},{9,5},{12,8},{13,9},{14,12},{15,13},... | collective-permute-start | bytes 798728 | tf_op jit(solution)/shard_map/ppermute | solution.py:273
  30.7 9.5 %collective-permute-start.7 = (s16[528,128]{1,0:T(8,128)(2,1)S(1)}, s16[528,128]{1,0:T(8,128)(2,1)S(1)}, u32[]{:S(2)}, u32[]{:S(2)}) collective-permute-start(s16[528,128]{1,0:T(8,128)(2,1)S(1)} %get-tuple-element.56), channel_id=1, source_target_pairs={{0,2},{1,3},{4,0},{5,1},{8,4},{9,5},{12,8},{13,9},{14,12},{15,13},... | collective-permute-start | bytes 405512 | tf_op jit(solution)/shard_map/ppermute | solution.py:273
  43.0 27.0 %copy-start.15 = (bf16[384,1024]{1,0:T(8,128)(2,1)}, bf16[384,1024]{1,0:T(8,128)(2,1)S(1)}, u32[]{:S(2)}) copy-start(bf16[384,1024]{1,0:T(8,128)(2,1)S(1)} %get-tuple-element.67.own_ref.refs_1_) | copy-start | bytes 2359300
  43.0 6.5 %collective-permute-start.12 = (s16[1040,128]{1,0:T(8,128)(2,1)S(1)}, s16[1040,128]{1,0:T(8,128)(2,1)S(1)}, u32[]{:S(2)}, u32[]{:S(2)}) collective-permute-start(s16[1040,128]{1,0:T(8,128)(2,1)S(1)} %get-tuple-element.57.before_ref), channel_id=1, source_target_pairs={{0,4},{1,5},{4,8},{5,9},{8,12},{9,13},{12,14},{13,15},{14,10},{15,... | collective-permute-start | bytes 798728 | tf_op jit(solution)/shard_map/ppermute | solution.py:273
  44.7 6.4 %collective-permute-start.13 = (s16[1040,128]{1,0:T(8,128)(2,1)S(1)}, s16[1040,128]{1,0:T(8,128)(2,1)S(1)}, u32[]{:S(2)}, u32[]{:S(2)}) collective-permute-start(s16[1040,128]{1,0:T(8,128)(2,1)S(1)} %get-tuple-element.64), channel_id=1, source_target_pairs={{0,2},{1,3},{4,0},{5,1},{8,4},{9,5},{12,8},{13,9},{14,12},{15,13},... | collective-permute-start | bytes 798728 | tf_op jit(solution)/shard_map/ppermute | solution.py:273
  45.1 10.4 %collective-permute-start.14 = (bf16[384,1024]{1,0:T(8,128)(2,1)S(1)}, bf16[384,1024]{1,0:T(8,128)(2,1)S(1)}, u32[]{:S(2)}, u32[]{:S(2)}) collective-permute-start(bf16[384,1024]{1,0:T(8,128)(2,1)S(1)} %get-tuple-element.58.before_ref), channel_id=1, source_target_pairs={{0,1},{1,0},{2,3},{3,2},{4,5},{5,4},{6,7},{7,6},{8,9},{9,8},{10,11... | collective-permute-start | bytes 2359304 | tf_op jit(solution)/shard_map/ppermute | solution.py:225
  45.1 11.9 %collective-permute-start.15 = (bf16[384,1024]{1,0:T(8,128)(2,1)S(1)}, bf16[384,1024]{1,0:T(8,128)(2,1)S(1)}, u32[]{:S(2)}, u32[]{:S(2)}) collective-permute-start(bf16[384,1024]{1,0:T(8,128)(2,1)S(1)} %get-tuple-element.69), channel_id=1, source_target_pairs={{0,1},{1,0},{2,3},{3,2},{4,5},{5,4},{6,7},{7,6},{8,9},{9,8},{10,11... | collective-permute-start | bytes 2359304 | tf_op jit(solution)/shard_map/ppermute | solution.py:225
  53.4 18.2 %collective-permute-start.20 = (bf16[384,1024]{1,0:T(8,128)(2,1)S(1)}, bf16[384,1024]{1,0:T(8,128)(2,1)S(1)}, u32[]{:S(2)}, u32[]{:S(2)}) collective-permute-start(bf16[384,1024]{1,0:T(8,128)(2,1)S(1)} %get-tuple-element.66.before_ref), channel_id=1, source_target_pairs={{0,1},{1,0},{2,3},{3,2},{4,5},{5,4},{6,7},{7,6},{8,9},{9,8},{10,11... | collective-permute-start | bytes 2359304 | tf_op jit(solution)/shard_map/ppermute | solution.py:225
  53.5 9.2 %collective-permute-start.16 = (s16[1040,128]{1,0:T(8,128)(2,1)S(1)}, s16[1040,128]{1,0:T(8,128)(2,1)S(1)}, u32[]{:S(2)}, u32[]{:S(2)}) collective-permute-start(s16[1040,128]{1,0:T(8,128)(2,1)S(1)} %get-tuple-element.63.before_ref), channel_id=1, source_target_pairs={{0,4},{1,5},{4,8},{5,9},{8,12},{9,13},{12,14},{13,15},{14,10},{15,... | collective-permute-start | bytes 798728 | tf_op jit(solution)/shard_map/ppermute | solution.py:273
  55.0 9.2 %collective-permute-start.17 = (s16[1040,128]{1,0:T(8,128)(2,1)S(1)}, s16[1040,128]{1,0:T(8,128)(2,1)S(1)}, u32[]{:S(2)}, u32[]{:S(2)}) collective-permute-start(s16[1040,128]{1,0:T(8,128)(2,1)S(1)} %get-tuple-element.70), channel_id=1, source_target_pairs={{0,2},{1,3},{4,0},{5,1},{8,4},{9,5},{12,8},{13,9},{14,12},{15,13},... | collective-permute-start | bytes 798728 | tf_op jit(solution)/shard_map/ppermute | solution.py:273
  55.6 12.9 %collective-permute-start.18 = (s16[1040,128]{1,0:T(8,128)(2,1)S(1)}, s16[1040,128]{1,0:T(8,128)(2,1)S(1)}, u32[]{:S(2)}, u32[]{:S(2)}) collective-permute-start(s16[1040,128]{1,0:T(8,128)(2,1)S(1)} %get-tuple-element.65.before_ref), channel_id=1, source_target_pairs={{0,4},{1,5},{4,8},{5,9},{8,12},{9,13},{12,14},{13,15},{14,10},{15,... | collective-permute-start | bytes 798728 | tf_op jit(solution)/shard_map/ppermute | solution.py:273
  57.1 12.9 %collective-permute-start.19 = (s16[1040,128]{1,0:T(8,128)(2,1)S(1)}, s16[1040,128]{1,0:T(8,128)(2,1)S(1)}, u32[]{:S(2)}, u32[]{:S(2)}) collective-permute-start(s16[1040,128]{1,0:T(8,128)(2,1)S(1)} %get-tuple-element.72), channel_id=1, source_target_pairs={{0,2},{1,3},{4,0},{5,1},{8,4},{9,5},{12,8},{13,9},{14,12},{15,13},... | collective-permute-start | bytes 798728 | tf_op jit(solution)/shard_map/ppermute | solution.py:273
  65.1 8.6 %collective-permute-start.21 = (s16[1040,128]{1,0:T(8,128)(2,1)S(1)}, s16[1040,128]{1,0:T(8,128)(2,1)S(1)}, u32[]{:S(2)}, u32[]{:S(2)}) collective-permute-start(s16[1040,128]{1,0:T(8,128)(2,1)S(1)} %get-tuple-element.71.before_ref), channel_id=1, source_target_pairs={{0,4},{1,5},{4,8},{5,9},{8,12},{9,13},{12,14},{13,15},{14,10},{15,... | collective-permute-start | bytes 798728 | tf_op jit(solution)/shard_map/ppermute | solution.py:273
  65.8 9.1 %collective-permute-start.22 = (s16[1040,128]{1,0:T(8,128)(2,1)S(1)}, s16[1040,128]{1,0:T(8,128)(2,1)S(1)}, u32[]{:S(2)}, u32[]{:S(2)}) collective-permute-start(s16[1040,128]{1,0:T(8,128)(2,1)S(1)} %get-tuple-element.75), channel_id=1, source_target_pairs={{0,2},{1,3},{4,0},{5,1},{8,4},{9,5},{12,8},{13,9},{14,12},{15,13},... | collective-permute-start | bytes 798728 | tf_op jit(solution)/shard_map/ppermute | solution.py:273
  77.0 96.7 %all-gather.5.cloned.1.call-start = ((), (), s32[]{:S(2)}) async-start(), calls=%async_computation.1 | async-start | bytes 2359296 | tf_op jit(solution)/shard_map/all_gather | solution.py:320
  77.1 7.9 %collective-permute-start.23 = (s16[1040,128]{1,0:T(8,128)(2,1)}, s16[1040,128]{1,0:T(8,128)(2,1)S(1)}, u32[]{:S(2)}, u32[]{:S(2)}) collective-permute-start(s16[1040,128]{1,0:T(8,128)(2,1)} %copy-done.56), channel_id=1, source_target_pairs={{0,4},{1,5},{4,8},{5,9},{8,12},{9,13},{12,14},{13,15},{14,10},{15,... | collective-permute-start | bytes 798728 | tf_op jit(solution)/shard_map/ppermute | solution.py:273
  77.7 9.1 %collective-permute-start.24 = (s16[1040,128]{1,0:T(8,128)(2,1)}, s16[1040,128]{1,0:T(8,128)(2,1)S(1)}, u32[]{:S(2)}, u32[]{:S(2)}) collective-permute-start(s16[1040,128]{1,0:T(8,128)(2,1)} %copy-done.60), channel_id=1, source_target_pairs={{0,2},{1,3},{4,0},{5,1},{8,4},{9,5},{12,8},{13,9},{14,12},{15,13},... | collective-permute-start | bytes 798728 | tf_op jit(solution)/shard_map/ppermute | solution.py:273
  141.1 32.6 %copy-start.2 = (bf16[384,1024]{1,0:T(8,128)(2,1)S(1)}, bf16[384,1024]{1,0:T(8,128)(2,1)}, u32[]{:S(2)}) copy-start(bf16[384,1024]{1,0:T(8,128)(2,1)} %copy-done) | copy-start | bytes 2359300
  192.7 1.8 collective-permute-start.25
  (57 other events, 184.0 us)
Sparse Core Ops, SparseCore 0:
  77.2 46.5 all-gather.2
  125.9 47.7 all-gather.4

commit v3 on v2

--- a/solution.py
+++ b/solution.py
@@ -11,7 +11,7 @@
 TOP = 32700.0
 PAD = 16
 LANES = 128
-VMEM = 24 * 1024 * 1024
+VMEM = 14 * 1024 * 1024
 
 
 def ring_of(devices):
@@ -48,18 +48,22 @@
     return found
 
 
-def pick_kernel(ring, wanted, block, genotype_ref, before_ref, *refs):
-    outs, sems = refs[:-1], refs[-1]
+def pick_kernel(ring, wanted, block, genotype_ref, *refs):
+    outs, sems = refs[-1 - len(wanted) : -1], refs[-1]
     core = lax.rem(lax.axis_index("ind"), 2)
-    owners = dict(zip([d for d, _ in wanted], owners_of(ring, [d for d, _ in wanted])))
+    needed = sorted({d for distances, _ in wanted for d in distances})
+    owners = dict(zip(needed, owners_of(ring, needed)))
     copies = []
-    for k, (d, swapped) in enumerate(wanted):
+    for out_ref, (distances, swapped) in zip(outs, wanted):
         parity = 1 - core if swapped else core
-        at = pl.multiple_of((2 * owners[d] + parity) * block, LANES)
-        copies.append(
-            pltpu.make_async_copy(genotype_ref.at[:, pl.ds(at, block)], outs[k], sems.at[k])
-        )
-        copies[-1].start()
+        for k, d in enumerate(distances):
+            at = pl.multiple_of((2 * owners[d] + parity) * block, LANES)
+            copies.append(
+                pltpu.make_async_copy(
+                    genotype_ref.at[:, pl.ds(at, block)], out_ref.at[k], sems.at[len(copies)]
+                )
+            )
+            copies[-1].start()
     for copy in copies:
         copy.wait()
 
@@ -70,12 +74,12 @@
     out_ref[:, people:] = other_ref[...].T
 
 
-def local_sum(res_ref, own_ref, peer_ref, low, high):
-    people = own_ref.shape[0]
+def local_sum(res_ref, own_ref, peer_ref, at, low, high):
+    people = own_ref.shape[1]
     return jnp.dot(
-        res_ref[:, :people], own_ref[:, low:high], preferred_element_type=jnp.float32
+        res_ref[:, :people], own_ref[at[0], :, low:high], preferred_element_type=jnp.float32
     ) + jnp.dot(
-        res_ref[:, people:], peer_ref[:, low:high], preferred_element_type=jnp.float32
+        res_ref[:, people:], peer_ref[at[1], :, low:high], preferred_element_type=jnp.float32
     )
 
 
@@ -104,22 +108,22 @@
     return [total[:, k : k + LANES] for k in range(0, total.shape[1], LANES)]
 
 
-def far_kernel(low, high, before_ref, res_ref, own_ref, peer_ref, right_ref, left_ref):
-    tiles = tiles_of(local_sum(res_ref, own_ref, peer_ref, low, high))
+def far_kernel(at, low, high, before_ref, res_ref, own_ref, peer_ref, right_ref, left_ref):
+    tiles = tiles_of(local_sum(res_ref, own_ref, peer_ref, at[0], low, high))
     half = len(tiles) // 2
     encode(right_ref, tiles[:half])
     encode(left_ref, tiles[half:])
 
 
 def hop_kernel(
-    low, high, before_ref, res_ref, own_ref, peer_ref, own_left_ref, peer_left_ref, got_right_ref,
+    at, low, high, before_ref, res_ref, own_ref, peer_ref, own_left_ref, peer_left_ref, got_right_ref,
     got_left_ref, right_ref, left_ref
 ):
     for way, own, peer, got_ref, out_ref in (
         (0, own_ref, peer_ref, got_right_ref, right_ref),
         (1, own_left_ref, peer_left_ref, got_left_ref, left_ref),
     ):
-        tiles = tiles_of(local_sum(res_ref, own, peer, low, high))
+        tiles = tiles_of(local_sum(res_ref, own, peer, at[way], low, high))
         got = decode(got_ref)
         height = tiles[0].shape[0]
         count = got.shape[0] // height
@@ -129,8 +133,8 @@
         encode(out_ref, tiles)
 
 
-def near_kernel(before_ref, res_ref, own_ref, peer_ref, out_ref):
-    out_ref[...] = local_sum(res_ref, own_ref, peer_ref, 0, own_ref.shape[1])
+def near_kernel(at, before_ref, res_ref, own_ref, peer_ref, out_ref):
+    out_ref[...] = local_sum(res_ref, own_ref, peer_ref, at, 0, own_ref.shape[2])
 
 
 def update_kernel(total, low, before_ref, corr_ref, right_ref, left_ref, incl_ref, mean_ref, prior_ref,
@@ -161,20 +165,20 @@
         effect_ref[rows, :] = (incl_new * mean_new).astype(jnp.bfloat16)
 
 
-def eta_kernel(ring, low, part, first, before_ref, gathered_ref, *refs):
-    size = len(ring)
-    own, peer = refs[:size], refs[size : 2 * size]
+def eta_kernel(places, first, before_ref, *refs):
     out_ref, out_other_ref = refs[-2:]
     mine = other = None
-    for d, owner in enumerate(owners_of(ring, range(size))):
-        effect = gathered_ref[pl.ds(pl.multiple_of(owner * part, part), part), :]
-        a = jnp.dot(own[d][:, low : low + part], effect, preferred_element_type=jnp.float32)
-        b = jnp.dot(peer[d][:, low : low + part], effect, preferred_element_type=jnp.float32)
+    for k, (at, low) in enumerate(places):
+        effect_ref, own_ref, peer_ref = refs[3 * k : 3 * k + 3]
+        effect = effect_ref[...]
+        high = low + effect.shape[0]
+        a = jnp.dot(own_ref[at[0], :, low:high], effect, preferred_element_type=jnp.float32)
+        b = jnp.dot(peer_ref[at[1], :, low:high], effect, preferred_element_type=jnp.float32)
         mine = a if mine is None else mine + a
         other = b if other is None else other + b
     if not first:
-        mine = mine + refs[2 * size][...]
-        other = other + refs[2 * size + 1][...]
+        mine = mine + refs[3 * len(places)][...]
+        other = other + refs[3 * len(places) + 1][...]
     out_ref[...] = mine
     out_other_ref[...] = other
 
@@ -195,6 +199,8 @@
     part = block // pieces
     f32, bf16 = jnp.float32, jnp.bfloat16
     params = pltpu.CompilerParams(vmem_limit_bytes=VMEM)
+    heavy = pl.CostEstimate(flops=10**10, bytes_accessed=10**6, transcendentals=0)
+    light = pl.CostEstimate(flops=2 * 10**9, bytes_accessed=10**6, transcendentals=0)
 
     swap = [(k, k ^ 1) for k in range(n)]
     right, left = [], []
@@ -208,82 +214,86 @@
     def after(before, args):
         return [anywhere] + [pl.BlockSpec()] * len(args)
 
-    peer, own = {}, {}
-
-    def pick(distances, before):
-        wanted = [(d, True) for d in distances] + [(d, False) for d in distances]
-        found = pl.pallas_call(
+    def pick(wanted, *before):
+        return pl.pallas_call(
             functools.partial(pick_kernel, ring, wanted, block),
-            in_specs=[pl.BlockSpec(memory_space=pltpu.HBM), anywhere],
+            in_specs=[pl.BlockSpec(memory_space=pltpu.HBM)] + [anywhere] * len(before),
             out_specs=[anywhere] * len(wanted),
-            out_shape=[jax.ShapeDtypeStruct((people, block), bf16)] * len(wanted),
-            scratch_shapes=[pltpu.SemaphoreType.DMA((len(wanted),))],
+            out_shape=[
+                jax.ShapeDtypeStruct((len(distances), people, block), bf16)
+                for distances, _ in wanted
+            ],
+            scratch_shapes=[pltpu.SemaphoreType.DMA((sum(len(d) for d, _ in wanted),))],
             compiler_params=params,
+            cost_estimate=heavy,
             name="pick_blocks",
-        )(pltpu.with_memory_space_constraint(genotype, pltpu.HBM), before)
-        for k, d in enumerate(distances):
-            peer[d] = lax.ppermute(found[k], "ind", swap)
-            own[d] = found[len(distances) + k]
-        return found[0]
-
-    def around(d):
-        return [0] if d == 0 else [d, size - d] if 2 * d != size else [d]
-
+        )(pltpu.with_memory_space_constraint(genotype, pltpu.HBM), *before)
+
+    order = [reach]
+    for d in range(reach - 1, 0, -1):
+        order += [d, size - d]
+    order += [0]
+    batches = [b for b in (order[:1], order[1:3], order[3:]) if b]
+    own, peer = {}, {}
     residual_other = lax.ppermute(residual, "ind", swap)
-    last = pick(around(reach), residual)
-    if reach > 1:
-        last = pick(around(reach - 1), last)
+    last = None
+    for k, batch in enumerate(batches):
+        if k == 0:
+            last, mine = pick([(batch, True), (batch, False)])
+            own[reach] = (mine, 0)
+        else:
+            last = pick([(batch, True)], last)[0]
+        sent = lax.ppermute(last, "ind", swap)
+        peer.update({d: (sent, j) for j, d in enumerate(batch)})
     res = last = pl.pallas_call(
         flip_kernel,
         in_specs=after(last, (residual, residual_other)),
         out_shape=jax.ShapeDtypeStruct((cols, 2 * people), bf16),
         compiler_params=params,
+        cost_estimate=heavy,
         name="flip",
     )(last, residual, residual_other)
 
-    def message(width):
+    def shape_of(width):
         return jax.ShapeDtypeStruct((width // LANES * cols + PAD, LANES), jnp.int16)
-
-    def dot_cost(width):
-        return pl.CostEstimate(
-            flops=4 * people * width * cols,
-            bytes_accessed=4 * people * width + 4 * people * cols + 4 * width * cols,
-            transcendentals=0,
-        )
 
     got = {}
     for d in range(reach, 0, -1):
         for piece in range(pieces):
             low, high = piece * part, (piece + 1) * part
+            if d == reach > 1 and piece:
+                last, _ = lax.optimization_barrier((last, peer[d - 1][0]))
             if d == reach:
-                kernel, width, name = far_kernel, part // 2, "sum_far"
-                args = (res, own[d], peer[d])
+                kernel, width, name, where = far_kernel, part // 2, "sum_far", (d,)
             else:
-                kernel, width, name = hop_kernel, part, "sum_hop"
-                args = (res, own[d], peer[d], own[size - d], peer[size - d], *got[piece])
+                kernel, width, name, where = hop_kernel, part, "sum_hop", (d, size - d)
+            args = [res]
+            for w in where:
+                args += [own[w][0], peer[w][0]]
+            if d < reach:
+                args += got[piece]
             sent = pl.pallas_call(
-                functools.partial(kernel, low, high),
+                functools.partial(kernel, [(own[w][1], peer[w][1]) for w in where], low, high),
                 in_specs=after(last, args),
-                out_shape=[message(width)] * 2,
+                out_shape=[shape_of(width)] * 2,
                 compiler_params=params,
-                cost_estimate=dot_cost(2 * width),
+                cost_estimate=heavy,
                 name=name,
             )(last, *args)
             last = sent[0]
             got[piece] = (lax.ppermute(sent[0], "ind", right), lax.ppermute(sent[1], "ind", left))
-        if d > 1:
-            last = pick(around(d - 2), last)
-    if reach == 1:
-        last = pick([0], last)
+        if d == reach:
+            last = pick([(order[1:], False)], last)[0]
+            own.update({w: (last, j) for j, w in enumerate(order[1:])})
 
     near = last = pl.pallas_call(
-        near_kernel,
+        functools.partial(near_kernel, (own[0][1], peer[0][1])),
         in_specs=after(last, (res, own[0], peer[0])),
         out_shape=jax.ShapeDtypeStruct((cols, block), f32),
         compiler_params=params,
-        cost_estimate=dot_cost(block),
+        cost_estimate=light,
         name="sum_near",
-    )(last, res, own[0], peer[0])
+    )(last, res, own[0][0], peer[0][0])
 
     prior = prior_logit.reshape(1, cols)
     scale = slab_scale.reshape(1, cols)
@@ -292,8 +302,7 @@
         return pl.BlockSpec(shape, lambda i: (0,) * len(shape))
 
     outs = ()
-    gathered = []
-    groups = [[2 * chip + c for chip in range(size)] for c in range(2)]
+    effects = []
     for piece in range(pieces):
         rows = pl.BlockSpec((part, cols), lambda i, piece=piece: (piece, 0))
         incl_new, mean_new, effect = pl.pallas_call(
@@ -312,39 +321,55 @@
             ],
             input_output_aliases={8: 0, 9: 1} if outs else {},
             compiler_params=params,
+            cost_estimate=light,
             name="update",
         )(last, near, *got[piece], incl_old, mean_old, prior, scale, *outs)
         outs = (incl_new, mean_new)
         last = effect
-        gathered.append(
-            lax.all_gather(effect, "ind", axis=0, tiled=True, axis_index_groups=groups)
-        )
+        effects.append(effect)
 
     eta_shape = jax.ShapeDtypeStruct((people, cols), f32)
-    eta = ()
-    for piece in range(pieces):
-        args = (
-            gathered[piece], *[own[d] for d in range(size)], *[peer[d] for d in range(size)], *eta
-        )
-        eta = pl.pallas_call(
-            functools.partial(eta_kernel, ring, piece * part, part, not eta),
-            in_specs=after(last, args),
+    def product(found, eta, before):
+        args = [v for d, _, effect in found for v in (effect, own[d][0], peer[d][0])] + list(eta)
+        places = [((own[d][1], peer[d][1]), piece * part) for d, piece, _ in found]
+        return pl.pallas_call(
+            functools.partial(eta_kernel, places, not eta),
+            in_specs=after(before, args),
             out_shape=[eta_shape] * 2,
             compiler_params=params,
-            cost_estimate=pl.CostEstimate(
-                flops=4 * people * part * size * cols,
-                bytes_accessed=size * (4 * people * part + 2 * part * cols),
-                transcendentals=0,
-            ),
+            cost_estimate=heavy if eta else light,
             name="add_eta",
-        )(last, *args)
-        last = eta[0]
+        )(before, *args)
+
+    eta = product([(0, piece, effects[piece]) for piece in range(pieces)], (), last)
+    held = {(way, piece): effects[piece] for way in range(2) for piece in range(pieces)}
+    etas = [eta[0]]
+    for hop in range(1, reach + 1):
+        for piece in range(pieces):
+            found = []
+            for way in range(2):
+                if hop == reach and way != piece % 2:
+                    continue
+                message = held[way, piece]
+                if hop > 1:
+                    message, _ = lax.optimization_barrier((message, etas[-1 - pieces]))
+                held[way, piece] = lax.ppermute(message, "ind", left if way else right)
+                found.append((hop if way else size - hop, piece, held[way, piece]))
+            if hop == reach and pieces == 2:
+                tail = found if piece == 0 else tail + found
+                if piece == 0:
+                    continue
+                found = tail
+            if found:
+                eta = product(found, eta, eta[0])
+                etas.append(eta[0])
 
     eta_got = lax.ppermute(eta[1], "ind", swap)
     resid_new = pl.pallas_call(
         end_kernel,
         out_shape=eta_shape,
         compiler_params=params,
+        cost_estimate=light,
         name="new_residual",
     )(eta[0], eta_got, labels, offset.reshape(1, cols))
     return (outs[0], outs[1], resid_new)

time: 204 us -> 98.7 us (0.48)
  waiting for transfers between devices: 102 us -> 41.7 us
  local copies, waits for them, and re-layouts: 42.5 us -> 0.03 us
  between operations: 14.5 us -> 0.89 us
  starting transfers between devices: 20.9 us -> 33.3 us
    all_gather x2 -> x0, waiting for transfers between devices: 60.8 us -> none  [on_device(): lax.all_gather(effect, 'ind', axis=0, tiled=True, axis_index_groups=groups)]
    unnamed x122 -> x14, local copies, waits for them, and re-layouts: 42.5 us -> 0.03 us
    ppermute x8 -> x17, waiting for transfers between devices: 0.02 us -> 20.6 us  [the longest x14 20.6 us: on_device(): held[way, piece] = lax.ppermute(message, 'ind', left if way else right)]
    ppermute x8, waiting for transfers between devices: 18.8 us -> 4.76 us  [on_device(): lax.ppermute(sent[0], 'ind', right)]
    ppermute x8 -> x17, starting transfers between devices: 2.24 us -> 14.9 us  [the longest x14 14.2 us: on_device(): held[way, piece] = lax.ppermute(message, 'ind', left if way else right)]
    ppermute x8, starting transfers between devices: 12.5 us -> 7.16 us  [on_device(): lax.ppermute(sent[0], 'ind', right)]
    ppermute x8, starting transfers between devices: 5.72 us -> 10.6 us  [on_device(): lax.ppermute(sent[1], 'ind', left)]
    ppermute x1, waiting for transfers between devices: 2.87 us -> 0.01 us  [on_device(): residual_other = lax.ppermute(residual, 'ind', swap)]
  transfers between devices with their start and end apart: 28 -> 35, of which waited for: 17 -> 27; matrix products, arithmetic and copies ran while one was open for 0% -> 0% of each run, Pallas kernels for 8% -> 22%
where the time goes in v3:
time: 98.7 us; the launch traced here: 98.5 us
  waiting for transfers between devices  41.7 us (42%)
  starting transfers between devices  33.3 us (34%)
  Pallas kernels  22.6 us (23%)
    ppermute x14, waiting for transfers between devices, on_device(): held[way, piece] = lax.ppermute(message, 'ind', left if way else right)  20.6 us
    ppermute x8, waiting for transfers between devices, on_device(): lax.ppermute(sent[1], 'ind', left)  14.6 us
    ppermute x14, starting transfers between devices, on_device(): held[way, piece] = lax.ppermute(message, 'ind', left if way else right)  14.2 us
    ppermute x8, starting transfers between devices, on_device(): lax.ppermute(sent[1], 'ind', left)  10.6 us
    pallas_call x4, Pallas kernels, pick(): pl.pallas_call(functools.partial(pick_kernel, ring, wanted, block), in_sp...  7.54 us
    ppermute x8, starting transfers between devices, on_device(): lax.ppermute(sent[0], 'ind', right)  7.16 us
    pallas_call x8, Pallas kernels, on_device(): pl.pallas_call(functools.partial(kernel, [(own[w][1], peer[w][1]) for w i...  6.14 us
    ppermute x8, waiting for transfers between devices, on_device(): lax.ppermute(sent[0], 'ind', right)  4.76 us
  transfers between devices with their start and end apart: 35, of which 27 were waited for; matrix products, arithmetic and copies ran while one was open for 0% of the time, Pallas kernels for 22%

profile of v3, /device:TPU:0, one launch (start us, length us, event | category | flops | bytes accessed | tf_op | source)
XLA Modules:
  0.0 98.5 jit_solution(12067300066719107349)
XLA Ops:
  1.1 1.4 %pick_blocks.4 = (bf16[1,384,1024]{2,1,0:T(8,128)(2,1)S(1)}, bf16[1,384,1024]{2,1,0:T(8,128)(2,1)S(1)}) custom-call(bf16[384,16384]{1,0:T(8,128)(2,1)} %genotype_ref.7), custom_call_target="tpu_custom_call" | custom-call | flops 10000000000 | bytes 1000000 | tf_op jit(solution)/shard_map/pick_blocks/pallas_call | solution.py:218
  2.7 1.4 %pick_blocks.5.refs_0_ = bf16[2,384,1024]{2,1,0:T(8,128)(2,1)S(1)} custom-call(bf16[384,16384]{1,0:T(8,128)(2,1)} %genotype_ref.7, bf16[1,384,1024]{2,1,0:T(8,128)(2,1)S(1)} %get-tuple-element.54.refs_0_), custom_call_target="tpu_custom_call" | custom-call | flops 10000000000 | bytes 1000000 | tf_op jit(solution)/shard_map/pick_blocks/pallas_call | solution.py:218
  4.6 2.1 %pick_blocks.6.before_ref = bf16[5,384,1024]{2,1,0:T(8,128)(2,1)S(1)} custom-call(bf16[384,16384]{1,0:T(8,128)(2,1)} %genotype_ref.7, bf16[2,384,1024]{2,1,0:T(8,128)(2,1)S(1)} %pick_blocks.5.refs_0_), custom_call_target="tpu_custom_call" | custom-call | flops 10000000000 | bytes 1000000 | tf_op jit(solution)/shard_map/pick_blocks/pallas_call | solution.py:218
  7.6 3.0 %collective-permute-start.4 = (s16[528,128]{1,0:T(8,128)(2,1)S(1)}, s16[528,128]{1,0:T(8,128)(2,1)S(1)}, u32[]{:S(2)}, u32[]{:S(2)}) collective-permute-start(s16[528,128]{1,0:T(8,128)(2,1)S(1)} %get-tuple-element.59), channel_id=1, source_target_pairs={{0,2},{1,3},{4,0},{5,1},{8,4},{9,5},{12,8},{13,9},{14,12},{15,13},... | collective-permute-start | bytes 405512 | tf_op jit(solution)/shard_map/ppermute | solution.py:284
  11.2 2.0 %collective-permute-start.5 = (s16[528,128]{1,0:T(8,128)(2,1)S(1)}, s16[528,128]{1,0:T(8,128)(2,1)S(1)}, u32[]{:S(2)}, u32[]{:S(2)}) collective-permute-start(s16[528,128]{1,0:T(8,128)(2,1)S(1)} %get-tuple-element.58.refs_0_), channel_id=1, source_target_pairs={{0,4},{1,5},{4,8},{5,9},{8,12},{9,13},{12,14},{13,15},{14,10},{15,... | collective-permute-start | bytes 405512 | tf_op jit(solution)/shard_map/ppermute | solution.py:284
  13.2 2.6 %pick_blocks.7.before_ref.own_ref.own_left_ref.refs_1_.refs_4_ = bf16[7,384,1024]{2,1,0:T(8,128)(2,1)S(1)} custom-call(bf16[384,16384]{1,0:T(8,128)(2,1)} %genotype_ref.7, s16[528,128]{1,0:T(8,128)(2,1)S(1)} %get-tuple-element.58.refs_0_), custom_call_target="tpu_custom_call" | custom-call | flops 10000000000 | bytes 1000000 | tf_op jit(solution)/shard_map/pick_blocks/pallas_call | solution.py:218
  17.9 1.6 %collective-permute-start.9 = (s16[1040,128]{1,0:T(8,128)(2,1)S(1)}, s16[1040,128]{1,0:T(8,128)(2,1)S(1)}, u32[]{:S(2)}, u32[]{:S(2)}) collective-permute-start(s16[1040,128]{1,0:T(8,128)(2,1)S(1)} %get-tuple-element.63), channel_id=1, source_target_pairs={{0,2},{1,3},{4,0},{5,1},{8,4},{9,5},{12,8},{13,9},{14,12},{15,13},... | collective-permute-start | bytes 798728 | tf_op jit(solution)/shard_map/ppermute | solution.py:284
  20.0 2.5 %collective-permute-done.6.got_left_ref = s16[528,128]{1,0:T(8,128)(2,1)S(1)} collective-permute-done((s16[528,128]{1,0:T(8,128)(2,1)S(1)}, s16[528,128]{1,0:T(8,128)(2,1)S(1)}, u32[]{:S(2)}, u32[]{:S(2)}) %collective-permute-start.6) | collective-permute-done | bytes 135200 | tf_op jit(solution)/shard_map/ppermute | solution.py:284
  23.4 2.0 %collective-permute-start.10 = (s16[1040,128]{1,0:T(8,128)(2,1)S(1)}, s16[1040,128]{1,0:T(8,128)(2,1)S(1)}, u32[]{:S(2)}, u32[]{:S(2)}) collective-permute-start(s16[1040,128]{1,0:T(8,128)(2,1)S(1)} %get-tuple-element.62.before_ref), channel_id=1, source_target_pairs={{0,4},{1,5},{4,8},{5,9},{8,12},{9,13},{12,14},{13,15},{14,10},{15,... | collective-permute-start | bytes 798728 | tf_op jit(solution)/shard_map/ppermute | solution.py:284
  25.4 2.8 %collective-permute-done.9.got_left_ref = s16[1040,128]{1,0:T(8,128)(2,1)S(1)} collective-permute-done((s16[1040,128]{1,0:T(8,128)(2,1)S(1)}, s16[1040,128]{1,0:T(8,128)(2,1)S(1)}, u32[]{:S(2)}, u32[]{:S(2)}) %collective-permute-start.9) | collective-permute-done | bytes 266272 | tf_op jit(solution)/shard_map/ppermute | solution.py:284
  29.6 1.5 %collective-permute-start.13 = (s16[1040,128]{1,0:T(8,128)(2,1)S(1)}, s16[1040,128]{1,0:T(8,128)(2,1)S(1)}, u32[]{:S(2)}, u32[]{:S(2)}) collective-permute-start(s16[1040,128]{1,0:T(8,128)(2,1)S(1)} %get-tuple-element.67), channel_id=1, source_target_pairs={{0,2},{1,3},{4,0},{5,1},{8,4},{9,5},{12,8},{13,9},{14,12},{15,13},... | collective-permute-start | bytes 798728 | tf_op jit(solution)/shard_map/ppermute | solution.py:284
  31.7 2.1 %collective-permute-done.11.got_left_ref = s16[1040,128]{1,0:T(8,128)(2,1)S(1)} collective-permute-done((s16[1040,128]{1,0:T(8,128)(2,1)S(1)}, s16[1040,128]{1,0:T(8,128)(2,1)S(1)}, u32[]{:S(2)}, u32[]{:S(2)}) %collective-permute-start.11) | collective-permute-done | bytes 266272 | tf_op jit(solution)/shard_map/ppermute | solution.py:284
  35.3 1.5 %collective-permute-start.15 = (s16[1040,128]{1,0:T(8,128)(2,1)S(1)}, s16[1040,128]{1,0:T(8,128)(2,1)S(1)}, u32[]{:S(2)}, u32[]{:S(2)}) collective-permute-start(s16[1040,128]{1,0:T(8,128)(2,1)S(1)} %get-tuple-element.69), channel_id=1, source_target_pairs={{0,2},{1,3},{4,0},{5,1},{8,4},{9,5},{12,8},{13,9},{14,12},{15,13},... | collective-permute-start | bytes 798728 | tf_op jit(solution)/shard_map/ppermute | solution.py:284
  37.4 2.2 %collective-permute-done.13.got_left_ref = s16[1040,128]{1,0:T(8,128)(2,1)S(1)} collective-permute-done((s16[1040,128]{1,0:T(8,128)(2,1)S(1)}, s16[1040,128]{1,0:T(8,128)(2,1)S(1)}, u32[]{:S(2)}, u32[]{:S(2)}) %collective-permute-start.13) | collective-permute-done | bytes 266272 | tf_op jit(solution)/shard_map/ppermute | solution.py:284
  41.2 1.5 %collective-permute-start.17 = (s16[1040,128]{1,0:T(8,128)(2,1)S(1)}, s16[1040,128]{1,0:T(8,128)(2,1)S(1)}, u32[]{:S(2)}, u32[]{:S(2)}) collective-permute-start(s16[1040,128]{1,0:T(8,128)(2,1)S(1)} %get-tuple-element.71), channel_id=1, source_target_pairs={{0,2},{1,3},{4,0},{5,1},{8,4},{9,5},{12,8},{13,9},{14,12},{15,13},... | collective-permute-start | bytes 798728 | tf_op jit(solution)/shard_map/ppermute | solution.py:284
  43.3 2.0 %collective-permute-done.15.got_left_ref = s16[1040,128]{1,0:T(8,128)(2,1)S(1)} collective-permute-done((s16[1040,128]{1,0:T(8,128)(2,1)S(1)}, s16[1040,128]{1,0:T(8,128)(2,1)S(1)}, u32[]{:S(2)}, u32[]{:S(2)}) %collective-permute-start.15) | collective-permute-done | bytes 266272 | tf_op jit(solution)/shard_map/ppermute | solution.py:284
  46.9 1.4 %collective-permute-start.19 = (s16[1040,128]{1,0:T(8,128)(2,1)S(1)}, s16[1040,128]{1,0:T(8,128)(2,1)S(1)}, u32[]{:S(2)}, u32[]{:S(2)}) collective-permute-start(s16[1040,128]{1,0:T(8,128)(2,1)S(1)} %get-tuple-element.73), channel_id=1, source_target_pairs={{0,2},{1,3},{4,0},{5,1},{8,4},{9,5},{12,8},{13,9},{14,12},{15,13},... | collective-permute-start | bytes 798728 | tf_op jit(solution)/shard_map/ppermute | solution.py:284
  51.5 1.3 %update.2 = (f32[1024,256]{1,0:T(8,128)}, f32[1024,256]{1,0:T(8,128)}, bf16[512,256]{1,0:T(8,128)(2,1)S(1)}) custom-call(f32[256,1024]{1,0:T(8,128)S(1)} %sum_near.1.before_ref.corr_ref, f32[256,1024]{1,0:T(8,128)S(1)} %sum_near.1.before_ref.corr_ref, s16[1040,128]{1,0:T(8,128)(2,1)S(1)} %collective-permute-done.16.right_ref, ...), custom_call_target="tpu_custom_call" | custom-call | flops 2000000000 | bytes 1000000 | tf_op jit(solution)/shard_map/update/pallas_call | solution.py:308
  52.8 1.6 %collective-permute-start.21 = (bf16[512,256]{1,0:T(8,128)(2,1)S(1)}, bf16[512,256]{1,0:T(8,128)(2,1)S(1)}, u32[]{:S(2)}, u32[]{:S(2)}) collective-permute-start(bf16[512,256]{1,0:T(8,128)(2,1)S(1)} %get-tuple-element.72.before_ref.refs_0_), channel_id=1, source_target_pairs={{0,2},{1,3},{4,0},{5,1},{8,4},{9,5},{12,8},{13,9},{14,12},{15,13},... | collective-permute-start | bytes 786440 | tf_op jit(solution)/shard_map/ppermute | solution.py:356
  54.8 1.9 %collective-permute-done.19.left_ref = s16[1040,128]{1,0:T(8,128)(2,1)S(1)} collective-permute-done((s16[1040,128]{1,0:T(8,128)(2,1)S(1)}, s16[1040,128]{1,0:T(8,128)(2,1)S(1)}, u32[]{:S(2)}, u32[]{:S(2)}) %collective-permute-start.19) | collective-permute-done | bytes 266272 | tf_op jit(solution)/shard_map/ppermute | solution.py:284
  63.9 1.7 %collective-permute-start.25 = (bf16[512,256]{1,0:T(8,128)(2,1)S(1)}, bf16[512,256]{1,0:T(8,128)(2,1)S(1)}, u32[]{:S(2)}, u32[]{:S(2)}) collective-permute-start(bf16[512,256]{1,0:T(8,128)(2,1)S(1)} %collective-permute-done.21.refs_3_), channel_id=1, source_target_pairs={{0,2},{1,3},{4,0},{5,1},{8,4},{9,5},{12,8},{13,9},{14,12},{15,13},... | collective-permute-start | bytes 786440 | tf_op jit(solution)/shard_map/ppermute | solution.py:356
  66.1 1.8 %collective-permute-done.23.refs_3_ = bf16[512,256]{1,0:T(8,128)(2,1)S(1)} collective-permute-done((bf16[512,256]{1,0:T(8,128)(2,1)S(1)}, bf16[512,256]{1,0:T(8,128)(2,1)S(1)}, u32[]{:S(2)}, u32[]{:S(2)}) %collective-permute-start.23) | collective-permute-done | bytes 262176 | tf_op jit(solution)/shard_map/ppermute | solution.py:356
  69.8 1.4 %collective-permute-start.27 = (bf16[512,256]{1,0:T(8,128)(2,1)S(1)}, bf16[512,256]{1,0:T(8,128)(2,1)S(1)}, u32[]{:S(2)}, u32[]{:S(2)}) collective-permute-start(bf16[512,256]{1,0:T(8,128)(2,1)S(1)} %collective-permute-done.23.refs_3_), channel_id=1, source_target_pairs={{0,2},{1,3},{4,0},{5,1},{8,4},{9,5},{12,8},{13,9},{14,12},{15,13},... | collective-permute-start | bytes 786440 | tf_op jit(solution)/shard_map/ppermute | solution.py:356
  71.8 1.8 %collective-permute-done.25.refs_3_ = bf16[512,256]{1,0:T(8,128)(2,1)S(1)} collective-permute-done((bf16[512,256]{1,0:T(8,128)(2,1)S(1)}, bf16[512,256]{1,0:T(8,128)(2,1)S(1)}, u32[]{:S(2)}, u32[]{:S(2)}) %collective-permute-start.25) | collective-permute-done | bytes 262176 | tf_op jit(solution)/shard_map/ppermute | solution.py:356
  75.4 1.4 %collective-permute-start.29 = (bf16[512,256]{1,0:T(8,128)(2,1)S(1)}, bf16[512,256]{1,0:T(8,128)(2,1)S(1)}, u32[]{:S(2)}, u32[]{:S(2)}) collective-permute-start(bf16[512,256]{1,0:T(8,128)(2,1)S(1)} %collective-permute-done.25.refs_3_), channel_id=1, source_target_pairs={{0,2},{1,3},{4,0},{5,1},{8,4},{9,5},{12,8},{13,9},{14,12},{15,13},... | collective-permute-start | bytes 786440 | tf_op jit(solution)/shard_map/ppermute | solution.py:356
  77.4 1.8 %collective-permute-done.27.refs_3_ = bf16[512,256]{1,0:T(8,128)(2,1)S(1)} collective-permute-done((bf16[512,256]{1,0:T(8,128)(2,1)S(1)}, bf16[512,256]{1,0:T(8,128)(2,1)S(1)}, u32[]{:S(2)}, u32[]{:S(2)}) %collective-permute-start.27) | collective-permute-done | bytes 262176 | tf_op jit(solution)/shard_map/ppermute | solution.py:356
  81.0 1.4 %collective-permute-start.31 = (bf16[512,256]{1,0:T(8,128)(2,1)S(1)}, bf16[512,256]{1,0:T(8,128)(2,1)S(1)}, u32[]{:S(2)}, u32[]{:S(2)}) collective-permute-start(bf16[512,256]{1,0:T(8,128)(2,1)S(1)} %collective-permute-done.27.refs_3_), channel_id=1, source_target_pairs={{0,2},{1,3},{4,0},{5,1},{8,4},{9,5},{12,8},{13,9},{14,12},{15,13},... | collective-permute-start | bytes 786440 | tf_op jit(solution)/shard_map/ppermute | solution.py:356
  83.0 2.3 %collective-permute-done.28.refs_0_ = bf16[512,256]{1,0:T(8,128)(2,1)S(1)} collective-permute-done((bf16[512,256]{1,0:T(8,128)(2,1)S(1)}, bf16[512,256]{1,0:T(8,128)(2,1)S(1)}, u32[]{:S(2)}, u32[]{:S(2)}) %collective-permute-start.28) | collective-permute-done | bytes 262176 | tf_op jit(solution)/shard_map/ppermute | solution.py:356
  85.3 3.3 %collective-permute-done.31.refs_3_ = bf16[512,256]{1,0:T(8,128)(2,1)S(1)} collective-permute-done((bf16[512,256]{1,0:T(8,128)(2,1)S(1)}, bf16[512,256]{1,0:T(8,128)(2,1)S(1)}, u32[]{:S(2)}, u32[]{:S(2)}) %collective-permute-start.31) | collective-permute-done | bytes 262176 | tf_op jit(solution)/shard_map/ppermute | solution.py:356
  88.9 1.6 %collective-permute-start.32 = (bf16[512,256]{1,0:T(8,128)(2,1)S(1)}, bf16[512,256]{1,0:T(8,128)(2,1)S(1)}, u32[]{:S(2)}, u32[]{:S(2)}) collective-permute-start(bf16[512,256]{1,0:T(8,128)(2,1)S(1)} %collective-permute-done.28.refs_0_), channel_id=1, source_target_pairs={{0,4},{1,5},{4,8},{5,9},{8,12},{9,13},{12,14},{13,15},{14,10},{15,... | collective-permute-start | bytes 786440 | tf_op jit(solution)/shard_map/ppermute | solution.py:356
  91.8 3.3 %collective-permute-done.33.refs_3_ = bf16[512,256]{1,0:T(8,128)(2,1)S(1)} collective-permute-done((bf16[512,256]{1,0:T(8,128)(2,1)S(1)}, bf16[512,256]{1,0:T(8,128)(2,1)S(1)}, u32[]{:S(2)}, u32[]{:S(2)}) %collective-permute-start.33) | collective-permute-done | bytes 262176 | tf_op jit(solution)/shard_map/ppermute | solution.py:356
  96.0 1.7 %collective-permute-done.34.got_ref = f32[384,256]{1,0:T(8,128)S(1)} collective-permute-done((f32[384,256]{1,0:T(8,128)S(1)}, f32[384,256]{1,0:T(8,128)S(1)}, u32[]{:S(2)}, u32[]{:S(2)}) %collective-permute-start.34) | collective-permute-done | bytes 393248 | tf_op jit(solution)/shard_map/ppermute | solution.py:367
  (77 shorter events, 35.8 us)
Async XLA Ops:
  4.1 6.6 %collective-permute-start.2 = (bf16[2,384,1024]{2,1,0:T(8,128)(2,1)S(1)}, bf16[2,384,1024]{2,1,0:T(8,128)(2,1)S(1)}, u32[]{:S(2)}, u32[]{:S(2)}) collective-permute-start(bf16[2,384,1024]{2,1,0:T(8,128)(2,1)S(1)} %pick_blocks.5.refs_0_), channel_id=1, source_target_pairs={{0,1},{1,0},{2,3},{3,2},{4,5},{5,4},{6,7},{7,6},{8,9},{9,8},{10,11... | collective-permute-start | bytes 4718600 | tf_op jit(solution)/shard_map/ppermute | solution.py:246
  6.7 22.0 %collective-permute-start.7 = (bf16[5,384,1024]{2,1,0:T(8,128)(2,1)S(1)}, bf16[5,384,1024]{2,1,0:T(8,128)(2,1)S(1)}, u32[]{:S(2)}, u32[]{:S(2)}) collective-permute-start(bf16[5,384,1024]{2,1,0:T(8,128)(2,1)S(1)} %pick_blocks.6.before_ref), channel_id=1, source_target_pairs={{0,1},{1,0},{2,3},{3,2},{4,5},{5,4},{6,7},{7,6},{8,9},{9,8},{10,11... | collective-permute-start | bytes 11796488 | tf_op jit(solution)/shard_map/ppermute | solution.py:246
  7.6 8.4 %collective-permute-start.4 = (s16[528,128]{1,0:T(8,128)(2,1)S(1)}, s16[528,128]{1,0:T(8,128)(2,1)S(1)}, u32[]{:S(2)}, u32[]{:S(2)}) collective-permute-start(s16[528,128]{1,0:T(8,128)(2,1)S(1)} %get-tuple-element.59), channel_id=1, source_target_pairs={{0,2},{1,3},{4,0},{5,1},{8,4},{9,5},{12,8},{13,9},{14,12},{15,13},... | collective-permute-start | bytes 405512 | tf_op jit(solution)/shard_map/ppermute | solution.py:284
  10.6 6.5 %collective-permute-start.3 = (s16[528,128]{1,0:T(8,128)(2,1)S(1)}, s16[528,128]{1,0:T(8,128)(2,1)S(1)}, u32[]{:S(2)}, u32[]{:S(2)}) collective-permute-start(s16[528,128]{1,0:T(8,128)(2,1)S(1)} %get-tuple-element.57.before_ref), channel_id=1, source_target_pairs={{0,4},{1,5},{4,8},{5,9},{8,12},{9,13},{12,14},{13,15},{14,10},{15,... | collective-permute-start | bytes 405512 | tf_op jit(solution)/shard_map/ppermute | solution.py:284
  11.2 11.2 %collective-permute-start.5 = (s16[528,128]{1,0:T(8,128)(2,1)S(1)}, s16[528,128]{1,0:T(8,128)(2,1)S(1)}, u32[]{:S(2)}, u32[]{:S(2)}) collective-permute-start(s16[528,128]{1,0:T(8,128)(2,1)S(1)} %get-tuple-element.58.refs_0_), channel_id=1, source_target_pairs={{0,4},{1,5},{4,8},{5,9},{8,12},{9,13},{12,14},{13,15},{14,10},{15,... | collective-permute-start | bytes 405512 | tf_op jit(solution)/shard_map/ppermute | solution.py:284
  15.9 6.6 %collective-permute-start.6 = (s16[528,128]{1,0:T(8,128)(2,1)S(1)}, s16[528,128]{1,0:T(8,128)(2,1)S(1)}, u32[]{:S(2)}, u32[]{:S(2)}) collective-permute-start(s16[528,128]{1,0:T(8,128)(2,1)S(1)} %get-tuple-element.61), channel_id=1, source_target_pairs={{0,2},{1,3},{4,0},{5,1},{8,4},{9,5},{12,8},{13,9},{14,12},{15,13},... | collective-permute-start | bytes 405512 | tf_op jit(solution)/shard_map/ppermute | solution.py:284
  17.9 10.2 %collective-permute-start.9 = (s16[1040,128]{1,0:T(8,128)(2,1)S(1)}, s16[1040,128]{1,0:T(8,128)(2,1)S(1)}, u32[]{:S(2)}, u32[]{:S(2)}) collective-permute-start(s16[1040,128]{1,0:T(8,128)(2,1)S(1)} %get-tuple-element.63), channel_id=1, source_target_pairs={{0,2},{1,3},{4,0},{5,1},{8,4},{9,5},{12,8},{13,9},{14,12},{15,13},... | collective-permute-start | bytes 798728 | tf_op jit(solution)/shard_map/ppermute | solution.py:284
  19.5 9.2 %collective-permute-start.8 = (s16[1040,128]{1,0:T(8,128)(2,1)S(1)}, s16[1040,128]{1,0:T(8,128)(2,1)S(1)}, u32[]{:S(2)}, u32[]{:S(2)}) collective-permute-start(s16[1040,128]{1,0:T(8,128)(2,1)S(1)} %get-tuple-element.60.before_ref), channel_id=1, source_target_pairs={{0,4},{1,5},{4,8},{5,9},{8,12},{9,13},{12,14},{13,15},{14,10},{15,... | collective-permute-start | bytes 798728 | tf_op jit(solution)/shard_map/ppermute | solution.py:284
  23.3 10.5 %collective-permute-start.11 = (s16[1040,128]{1,0:T(8,128)(2,1)S(1)}, s16[1040,128]{1,0:T(8,128)(2,1)S(1)}, u32[]{:S(2)}, u32[]{:S(2)}) collective-permute-start(s16[1040,128]{1,0:T(8,128)(2,1)S(1)} %get-tuple-element.65), channel_id=1, source_target_pairs={{0,2},{1,3},{4,0},{5,1},{8,4},{9,5},{12,8},{13,9},{14,12},{15,13},... | collective-permute-start | bytes 798728 | tf_op jit(solution)/shard_map/ppermute | solution.py:284
  23.4 11.1 %collective-permute-start.10 = (s16[1040,128]{1,0:T(8,128)(2,1)S(1)}, s16[1040,128]{1,0:T(8,128)(2,1)S(1)}, u32[]{:S(2)}, u32[]{:S(2)}) collective-permute-start(s16[1040,128]{1,0:T(8,128)(2,1)S(1)} %get-tuple-element.62.before_ref), channel_id=1, source_target_pairs={{0,4},{1,5},{4,8},{5,9},{8,12},{9,13},{12,14},{13,15},{14,10},{15,... | collective-permute-start | bytes 798728 | tf_op jit(solution)/shard_map/ppermute | solution.py:284
  29.6 9.9 %collective-permute-start.13 = (s16[1040,128]{1,0:T(8,128)(2,1)S(1)}, s16[1040,128]{1,0:T(8,128)(2,1)S(1)}, u32[]{:S(2)}, u32[]{:S(2)}) collective-permute-start(s16[1040,128]{1,0:T(8,128)(2,1)S(1)} %get-tuple-element.67), channel_id=1, source_target_pairs={{0,2},{1,3},{4,0},{5,1},{8,4},{9,5},{12,8},{13,9},{14,12},{15,13},... | collective-permute-start | bytes 798728 | tf_op jit(solution)/shard_map/ppermute | solution.py:284
  31.1 9.2 %collective-permute-start.12 = (s16[1040,128]{1,0:T(8,128)(2,1)S(1)}, s16[1040,128]{1,0:T(8,128)(2,1)S(1)}, u32[]{:S(2)}, u32[]{:S(2)}) collective-permute-start(s16[1040,128]{1,0:T(8,128)(2,1)S(1)} %get-tuple-element.64.before_ref), channel_id=1, source_target_pairs={{0,4},{1,5},{4,8},{5,9},{8,12},{9,13},{12,14},{13,15},{14,10},{15,... | collective-permute-start | bytes 798728 | tf_op jit(solution)/shard_map/ppermute | solution.py:284
  35.3 9.9 %collective-permute-start.15 = (s16[1040,128]{1,0:T(8,128)(2,1)S(1)}, s16[1040,128]{1,0:T(8,128)(2,1)S(1)}, u32[]{:S(2)}, u32[]{:S(2)}) collective-permute-start(s16[1040,128]{1,0:T(8,128)(2,1)S(1)} %get-tuple-element.69), channel_id=1, source_target_pairs={{0,2},{1,3},{4,0},{5,1},{8,4},{9,5},{12,8},{13,9},{14,12},{15,13},... | collective-permute-start | bytes 798728 | tf_op jit(solution)/shard_map/ppermute | solution.py:284
  36.8 9.2 %collective-permute-start.14 = (s16[1040,128]{1,0:T(8,128)(2,1)S(1)}, s16[1040,128]{1,0:T(8,128)(2,1)S(1)}, u32[]{:S(2)}, u32[]{:S(2)}) collective-permute-start(s16[1040,128]{1,0:T(8,128)(2,1)S(1)} %get-tuple-element.66.before_ref), channel_id=1, source_target_pairs={{0,4},{1,5},{4,8},{5,9},{8,12},{9,13},{12,14},{13,15},{14,10},{15,... | collective-permute-start | bytes 798728 | tf_op jit(solution)/shard_map/ppermute | solution.py:284
  41.2 9.8 %collective-permute-start.17 = (s16[1040,128]{1,0:T(8,128)(2,1)S(1)}, s16[1040,128]{1,0:T(8,128)(2,1)S(1)}, u32[]{:S(2)}, u32[]{:S(2)}) collective-permute-start(s16[1040,128]{1,0:T(8,128)(2,1)S(1)} %get-tuple-element.71), channel_id=1, source_target_pairs={{0,2},{1,3},{4,0},{5,1},{8,4},{9,5},{12,8},{13,9},{14,12},{15,13},... | collective-permute-start | bytes 798728 | tf_op jit(solution)/shard_map/ppermute | solution.py:284
  42.7 8.8 %collective-permute-start.16 = (s16[1040,128]{1,0:T(8,128)(2,1)S(1)}, s16[1040,128]{1,0:T(8,128)(2,1)S(1)}, u32[]{:S(2)}, u32[]{:S(2)}) collective-permute-start(s16[1040,128]{1,0:T(8,128)(2,1)S(1)} %get-tuple-element.68.before_ref), channel_id=1, source_target_pairs={{0,4},{1,5},{4,8},{5,9},{8,12},{9,13},{12,14},{13,15},{14,10},{15,... | collective-permute-start | bytes 798728 | tf_op jit(solution)/shard_map/ppermute | solution.py:284
  46.9 9.8 %collective-permute-start.19 = (s16[1040,128]{1,0:T(8,128)(2,1)S(1)}, s16[1040,128]{1,0:T(8,128)(2,1)S(1)}, u32[]{:S(2)}, u32[]{:S(2)}) collective-permute-start(s16[1040,128]{1,0:T(8,128)(2,1)S(1)} %get-tuple-element.73), channel_id=1, source_target_pairs={{0,2},{1,3},{4,0},{5,1},{8,4},{9,5},{12,8},{13,9},{14,12},{15,13},... | collective-permute-start | bytes 798728 | tf_op jit(solution)/shard_map/ppermute | solution.py:284
  48.3 8.8 %collective-permute-start.18 = (s16[1040,128]{1,0:T(8,128)(2,1)S(1)}, s16[1040,128]{1,0:T(8,128)(2,1)S(1)}, u32[]{:S(2)}, u32[]{:S(2)}) collective-permute-start(s16[1040,128]{1,0:T(8,128)(2,1)S(1)} %get-tuple-element.70.before_ref), channel_id=1, source_target_pairs={{0,4},{1,5},{4,8},{5,9},{8,12},{9,13},{12,14},{13,15},{14,10},{15,... | collective-permute-start | bytes 798728 | tf_op jit(solution)/shard_map/ppermute | solution.py:284
  52.8 9.5 %collective-permute-start.21 = (bf16[512,256]{1,0:T(8,128)(2,1)S(1)}, bf16[512,256]{1,0:T(8,128)(2,1)S(1)}, u32[]{:S(2)}, u32[]{:S(2)}) collective-permute-start(bf16[512,256]{1,0:T(8,128)(2,1)S(1)} %get-tuple-element.72.before_ref.refs_0_), channel_id=1, source_target_pairs={{0,2},{1,3},{4,0},{5,1},{8,4},{9,5},{12,8},{13,9},{14,12},{15,13},... | collective-permute-start | bytes 786440 | tf_op jit(solution)/shard_map/ppermute | solution.py:356
  54.4 9.1 %collective-permute-start.20 = (bf16[512,256]{1,0:T(8,128)(2,1)S(1)}, bf16[512,256]{1,0:T(8,128)(2,1)S(1)}, u32[]{:S(2)}, u32[]{:S(2)}) collective-permute-start(bf16[512,256]{1,0:T(8,128)(2,1)S(1)} %get-tuple-element.72.before_ref.refs_0_), channel_id=1, source_target_pairs={{0,4},{1,5},{4,8},{5,9},{8,12},{9,13},{12,14},{13,15},{14,10},{15,... | collective-permute-start | bytes 786440 | tf_op jit(solution)/shard_map/ppermute | solution.py:356
  58.5 9.4 %collective-permute-start.23 = (bf16[512,256]{1,0:T(8,128)(2,1)S(1)}, bf16[512,256]{1,0:T(8,128)(2,1)S(1)}, u32[]{:S(2)}, u32[]{:S(2)}) collective-permute-start(bf16[512,256]{1,0:T(8,128)(2,1)S(1)} %get-tuple-element.78.before_ref.refs_3_), channel_id=1, source_target_pairs={{0,2},{1,3},{4,0},{5,1},{8,4},{9,5},{12,8},{13,9},{14,12},{15,13},... | collective-permute-start | bytes 786440 | tf_op jit(solution)/shard_map/ppermute | solution.py:356
  59.8 9.4 %collective-permute-start.22 = (bf16[512,256]{1,0:T(8,128)(2,1)S(1)}, bf16[512,256]{1,0:T(8,128)(2,1)S(1)}, u32[]{:S(2)}, u32[]{:S(2)}) collective-permute-start(bf16[512,256]{1,0:T(8,128)(2,1)S(1)} %get-tuple-element.78.before_ref.refs_3_), channel_id=1, source_target_pairs={{0,4},{1,5},{4,8},{5,9},{8,12},{9,13},{12,14},{13,15},{14,10},{15,... | collective-permute-start | bytes 786440 | tf_op jit(solution)/shard_map/ppermute | solution.py:356
  63.5 11.2 %collective-permute-start.24 = (bf16[512,256]{1,0:T(8,128)(2,1)S(1)}, bf16[512,256]{1,0:T(8,128)(2,1)S(1)}, u32[]{:S(2)}, u32[]{:S(2)}) collective-permute-start(bf16[512,256]{1,0:T(8,128)(2,1)S(1)} %collective-permute-done.20.refs_0_), channel_id=1, source_target_pairs={{0,4},{1,5},{4,8},{5,9},{8,12},{9,13},{12,14},{13,15},{14,10},{15,... | collective-permute-start | bytes 786440 | tf_op jit(solution)/shard_map/ppermute | solution.py:356
  63.9 9.7 %collective-permute-start.25 = (bf16[512,256]{1,0:T(8,128)(2,1)S(1)}, bf16[512,256]{1,0:T(8,128)(2,1)S(1)}, u32[]{:S(2)}, u32[]{:S(2)}) collective-permute-start(bf16[512,256]{1,0:T(8,128)(2,1)S(1)} %collective-permute-done.21.refs_3_), channel_id=1, source_target_pairs={{0,2},{1,3},{4,0},{5,1},{8,4},{9,5},{12,8},{13,9},{14,12},{15,13},... | collective-permute-start | bytes 786440 | tf_op jit(solution)/shard_map/ppermute | solution.py:356
  69.2 11.2 %collective-permute-start.26 = (bf16[512,256]{1,0:T(8,128)(2,1)S(1)}, bf16[512,256]{1,0:T(8,128)(2,1)S(1)}, u32[]{:S(2)}, u32[]{:S(2)}) collective-permute-start(bf16[512,256]{1,0:T(8,128)(2,1)S(1)} %collective-permute-done.22.refs_0_), channel_id=1, source_target_pairs={{0,4},{1,5},{4,8},{5,9},{8,12},{9,13},{12,14},{13,15},{14,10},{15,... | collective-permute-start | bytes 786440 | tf_op jit(solution)/shard_map/ppermute | solution.py:356
  69.8 9.4 %collective-permute-start.27 = (bf16[512,256]{1,0:T(8,128)(2,1)S(1)}, bf16[512,256]{1,0:T(8,128)(2,1)S(1)}, u32[]{:S(2)}, u32[]{:S(2)}) collective-permute-start(bf16[512,256]{1,0:T(8,128)(2,1)S(1)} %collective-permute-done.23.refs_3_), channel_id=1, source_target_pairs={{0,2},{1,3},{4,0},{5,1},{8,4},{9,5},{12,8},{13,9},{14,12},{15,13},... | collective-permute-start | bytes 786440 | tf_op jit(solution)/shard_map/ppermute | solution.py:356
  74.8 10.5 %collective-permute-start.28 = (bf16[512,256]{1,0:T(8,128)(2,1)S(1)}, bf16[512,256]{1,0:T(8,128)(2,1)S(1)}, u32[]{:S(2)}, u32[]{:S(2)}) collective-permute-start(bf16[512,256]{1,0:T(8,128)(2,1)S(1)} %collective-permute-done.24.refs_0_), channel_id=1, source_target_pairs={{0,4},{1,5},{4,8},{5,9},{8,12},{9,13},{12,14},{13,15},{14,10},{15,... | collective-permute-start | bytes 786440 | tf_op jit(solution)/shard_map/ppermute | solution.py:356
  75.4 15.2 %collective-permute-start.29 = (bf16[512,256]{1,0:T(8,128)(2,1)S(1)}, bf16[512,256]{1,0:T(8,128)(2,1)S(1)}, u32[]{:S(2)}, u32[]{:S(2)}) collective-permute-start(bf16[512,256]{1,0:T(8,128)(2,1)S(1)} %collective-permute-done.25.refs_3_), channel_id=1, source_target_pairs={{0,2},{1,3},{4,0},{5,1},{8,4},{9,5},{12,8},{13,9},{14,12},{15,13},... | collective-permute-start | bytes 786440 | tf_op jit(solution)/shard_map/ppermute | solution.py:356
  80.4 10.8 %collective-permute-start.30 = (bf16[512,256]{1,0:T(8,128)(2,1)S(1)}, bf16[512,256]{1,0:T(8,128)(2,1)S(1)}, u32[]{:S(2)}, u32[]{:S(2)}) collective-permute-start(bf16[512,256]{1,0:T(8,128)(2,1)S(1)} %collective-permute-done.26.refs_0_), channel_id=1, source_target_pairs={{0,4},{1,5},{4,8},{5,9},{8,12},{9,13},{12,14},{13,15},{14,10},{15,... | collective-permute-start | bytes 786440 | tf_op jit(solution)/shard_map/ppermute | solution.py:356
  81.0 7.6 %collective-permute-start.31 = (bf16[512,256]{1,0:T(8,128)(2,1)S(1)}, bf16[512,256]{1,0:T(8,128)(2,1)S(1)}, u32[]{:S(2)}, u32[]{:S(2)}) collective-permute-start(bf16[512,256]{1,0:T(8,128)(2,1)S(1)} %collective-permute-done.27.refs_3_), channel_id=1, source_target_pairs={{0,2},{1,3},{4,0},{5,1},{8,4},{9,5},{12,8},{13,9},{14,12},{15,13},... | collective-permute-start | bytes 786440 | tf_op jit(solution)/shard_map/ppermute | solution.py:356
  88.6 6.5 %collective-permute-start.33 = (bf16[512,256]{1,0:T(8,128)(2,1)S(1)}, bf16[512,256]{1,0:T(8,128)(2,1)S(1)}, u32[]{:S(2)}, u32[]{:S(2)}) collective-permute-start(bf16[512,256]{1,0:T(8,128)(2,1)S(1)} %collective-permute-done.31.refs_3_), channel_id=1, source_target_pairs={{0,2},{1,3},{4,0},{5,1},{8,4},{9,5},{12,8},{13,9},{14,12},{15,13},... | collective-permute-start | bytes 786440 | tf_op jit(solution)/shard_map/ppermute | solution.py:356
  88.9 6.4 %collective-permute-start.32 = (bf16[512,256]{1,0:T(8,128)(2,1)S(1)}, bf16[512,256]{1,0:T(8,128)(2,1)S(1)}, u32[]{:S(2)}, u32[]{:S(2)}) collective-permute-start(bf16[512,256]{1,0:T(8,128)(2,1)S(1)} %collective-permute-done.28.refs_0_), channel_id=1, source_target_pairs={{0,4},{1,5},{4,8},{5,9},{8,12},{9,13},{12,14},{13,15},{14,10},{15,... | collective-permute-start | bytes 786440 | tf_op jit(solution)/shard_map/ppermute | solution.py:356
  (10 other events, 32.6 us)

commit v4 on v3

--- a/solution.py
+++ b/solution.py
@@ -200,6 +200,7 @@
     f32, bf16 = jnp.float32, jnp.bfloat16
     params = pltpu.CompilerParams(vmem_limit_bytes=VMEM)
     heavy = pl.CostEstimate(flops=10**10, bytes_accessed=10**6, transcendentals=0)
+    longest = pl.CostEstimate(flops=10**11, bytes_accessed=10**6, transcendentals=0)
     light = pl.CostEstimate(flops=2 * 10**9, bytes_accessed=10**6, transcendentals=0)
 
     swap = [(k, k ^ 1) for k in range(n)]
@@ -214,7 +215,7 @@
     def after(before, args):
         return [anywhere] + [pl.BlockSpec()] * len(args)
 
-    def pick(wanted, *before):
+    def pick(wanted, cost, *before):
         return pl.pallas_call(
             functools.partial(pick_kernel, ring, wanted, block),
             in_specs=[pl.BlockSpec(memory_space=pltpu.HBM)] + [anywhere] * len(before),
@@ -225,7 +226,7 @@
             ],
             scratch_shapes=[pltpu.SemaphoreType.DMA((sum(len(d) for d, _ in wanted),))],
             compiler_params=params,
-            cost_estimate=heavy,
+            cost_estimate=cost,
             name="pick_blocks",
         )(pltpu.with_memory_space_constraint(genotype, pltpu.HBM), *before)
 
@@ -233,18 +234,19 @@
     for d in range(reach - 1, 0, -1):
         order += [d, size - d]
     order += [0]
-    batches = [b for b in (order[:1], order[1:3], order[3:]) if b]
     own, peer = {}, {}
+
+    def swapped(distances, sent):
+        got = lax.ppermute(sent, "ind", swap)
+        peer.update({d: (got, k) for k, d in enumerate(distances)})
+
     residual_other = lax.ppermute(residual, "ind", swap)
-    last = None
-    for k, batch in enumerate(batches):
-        if k == 0:
-            last, mine = pick([(batch, True), (batch, False)])
-            own[reach] = (mine, 0)
-        else:
-            last = pick([(batch, True)], last)[0]
-        sent = lax.ppermute(last, "ind", swap)
-        peer.update({d: (sent, j) for j, d in enumerate(batch)})
+    (last,) = pick([(order[:1], True)], heavy)
+    swapped(order[:1], last)
+    next_two, others = order[1:3], order[3:]
+    mine, last = pick([(order[:3], False), (next_two, True)], heavy, last)
+    own.update({d: (mine, k) for k, d in enumerate(order[:3])})
+    swapped(next_two, last)
     res = last = pl.pallas_call(
         flip_kernel,
         in_specs=after(last, (residual, residual_other)),
@@ -277,14 +279,18 @@
                 in_specs=after(last, args),
                 out_shape=[shape_of(width)] * 2,
                 compiler_params=params,
-                cost_estimate=heavy,
+                cost_estimate=longest,
                 name=name,
             )(last, *args)
             last = sent[0]
             got[piece] = (lax.ppermute(sent[0], "ind", right), lax.ppermute(sent[1], "ind", left))
-        if d == reach:
-            last = pick([(order[1:], False)], last)[0]
-            own.update({w: (last, j) for j, w in enumerate(order[1:])})
+            if others and d == max(reach - 1, 1):
+                if piece == 0:
+                    (last,) = pick([(others, True)], light, last)
+                    swapped(others, last)
+                if piece == pieces - 1:
+                    (last,) = pick([(others, False)], light, last)
+                    own.update({w: (last, k) for k, w in enumerate(others)})
 
     near = last = pl.pallas_call(
         functools.partial(near_kernel, (own[0][1], peer[0][1])),
@@ -331,7 +337,7 @@
     eta_shape = jax.ShapeDtypeStruct((people, cols), f32)
     def product(found, eta, before):
         args = [v for d, _, effect in found for v in (effect, own[d][0], peer[d][0])] + list(eta)
-        places = [((own[d][1], peer[d][1]), piece * part) for d, piece, _ in found]
+        places = [((own[d][1], peer[d][1]), low) for d, low, _ in found]
         return pl.pallas_call(
             functools.partial(eta_kernel, places, not eta),
             in_specs=after(before, args),
@@ -341,28 +347,24 @@
             name="add_eta",
         )(before, *args)
 
-    eta = product([(0, piece, effects[piece]) for piece in range(pieces)], (), last)
+    eta = product([(0, piece * part, effects[piece]) for piece in range(pieces)], (), last)
     held = {(way, piece): effects[piece] for way in range(2) for piece in range(pieces)}
     etas = [eta[0]]
     for hop in range(1, reach + 1):
         for piece in range(pieces):
             found = []
             for way in range(2):
-                if hop == reach and way != piece % 2:
-                    continue
                 message = held[way, piece]
                 if hop > 1:
                     message, _ = lax.optimization_barrier((message, etas[-1 - pieces]))
+                low = 0
+                if hop == reach:
+                    low = way * (part // 2)
+                    message = message[low : low + part // 2]
                 held[way, piece] = lax.ppermute(message, "ind", left if way else right)
-                found.append((hop if way else size - hop, piece, held[way, piece]))
-            if hop == reach and pieces == 2:
-                tail = found if piece == 0 else tail + found
-                if piece == 0:
-                    continue
-                found = tail
-            if found:
-                eta = product(found, eta, eta[0])
-                etas.append(eta[0])
+                found.append((hop if way else size - hop, piece * part + low, held[way, piece]))
+            eta = product(found, eta, eta[0])
+            etas.append(eta[0])
 
     eta_got = lax.ppermute(eta[1], "ind", swap)
     resid_new = pl.pallas_call(

time: 98.7 us -> 98.7 us (level)
  waiting for transfers between devices: 41.7 us -> 38.6 us
  starting transfers between devices: 33.3 us -> 35.5 us
    ppermute x8, waiting for transfers between devices: 14.6 us -> 6.65 us  [on_device(): lax.ppermute(sent[1], 'ind', left)]
    ppermute x8, waiting for transfers between devices: 4.76 us -> 9.09 us  [on_device(): lax.ppermute(sent[0], 'ind', right)]
    ppermute x8, starting transfers between devices: 10.6 us -> 14.9 us  [on_device(): lax.ppermute(sent[1], 'ind', left)]
    ppermute x8, starting transfers between devices: 7.16 us -> 2.98 us  [on_device(): lax.ppermute(sent[0], 'ind', right)]
    ppermute x14 -> x16, starting transfers between devices: 14.2 us -> 16.3 us  [on_device(): held[way, piece] = lax.ppermute(message, 'ind', left if way else right)]
    ppermute x3, waiting for transfers between devices: 0.01 us -> 1.64 us  [swapped(): got = lax.ppermute(sent, 'ind', swap)]
    ppermute x14 -> x16, waiting for transfers between devices: 20.6 us -> 19.5 us  [on_device(): held[way, piece] = lax.ppermute(message, 'ind', left if way else right)]
    pallas_call x8 -> x9, Pallas kernels: 4.55 us -> 4.71 us  [product(): pl.pallas_call(functools.partial(eta_kernel, places, not eta), in_specs=a...]
  transfers between devices with their start and end apart: 35 -> 37, of which waited for: 27 -> 27; matrix products, arithmetic and copies ran while one was open for 0% -> 0% of each run, Pallas kernels for 22% -> 22%
where the time goes in v4:
time: 98.7 us; the launch traced here: 98.5 us
  waiting for transfers between devices  38.6 us (39%)
  starting transfers between devices  35.5 us (36%)
  Pallas kernels  22.8 us (23%)
  between operations  0.99 us (1%)
    ppermute x16, waiting for transfers between devices, on_device(): held[way, piece] = lax.ppermute(message, 'ind', left if way else right)  19.5 us
    ppermute x16, starting transfers between devices, on_device(): held[way, piece] = lax.ppermute(message, 'ind', left if way else right)  16.3 us
    ppermute x8, starting transfers between devices, on_device(): lax.ppermute(sent[1], 'ind', left)  14.9 us
    ppermute x8, waiting for transfers between devices, on_device(): lax.ppermute(sent[0], 'ind', right)  9.09 us
    pallas_call x4, Pallas kernels, pick(): pl.pallas_call(functools.partial(pick_kernel, ring, wanted, block), in_sp...  7.54 us
    ppermute x8, waiting for transfers between devices, on_device(): lax.ppermute(sent[1], 'ind', left)  6.65 us
    pallas_call x8, Pallas kernels, on_device(): pl.pallas_call(functools.partial(kernel, [(own[w][1], peer[w][1]) for w i...  6.13 us
    pallas_call x9, Pallas kernels, product(): pl.pallas_call(functools.partial(eta_kernel, places, not eta), in_specs=a...  4.71 us
  transfers between devices with their start and end apart: 37, of which 27 were waited for; matrix products, arithmetic and copies ran while one was open for 0% of the time, Pallas kernels for 22%

profile of v4, /device:TPU:0, one launch (start us, length us, event | category | flops | bytes accessed | tf_op | source)
XLA Modules:
  0.0 98.5 jit_solution(16304857839445453379)
XLA Ops:
  2.4 2.1 %pick_blocks.5 = (bf16[3,384,1024]{2,1,0:T(8,128)(2,1)S(1)}, bf16[2,384,1024]{2,1,0:T(8,128)(2,1)S(1)}) custom-call(bf16[384,16384]{1,0:T(8,128)(2,1)} %genotype_ref.7, bf16[1,384,1024]{2,1,0:T(8,128)(2,1)S(1)} %pick_blocks.4.refs_0_), custom_call_target="tpu_custom_call" | custom-call | flops 10000000000 | bytes 1000000 | tf_op jit(solution)/shard_map/pick_blocks/pallas_call | solution.py:219
  5.8 2.6 %collective-permute-start.4 = (s16[528,128]{1,0:T(8,128)(2,1)S(1)}, s16[528,128]{1,0:T(8,128)(2,1)S(1)}, u32[]{:S(2)}, u32[]{:S(2)}) collective-permute-start(s16[528,128]{1,0:T(8,128)(2,1)S(1)} %get-tuple-element.63), channel_id=1, source_target_pairs={{0,2},{1,3},{4,0},{5,1},{8,4},{9,5},{12,8},{13,9},{14,12},{15,13},... | collective-permute-start | bytes 405512 | tf_op jit(solution)/shard_map/ppermute | solution.py:286
  9.1 2.5 %collective-permute-start.6 = (s16[528,128]{1,0:T(8,128)(2,1)S(1)}, s16[528,128]{1,0:T(8,128)(2,1)S(1)}, u32[]{:S(2)}, u32[]{:S(2)}) collective-permute-start(s16[528,128]{1,0:T(8,128)(2,1)S(1)} %get-tuple-element.65), channel_id=1, source_target_pairs={{0,2},{1,3},{4,0},{5,1},{8,4},{9,5},{12,8},{13,9},{14,12},{15,13},... | collective-permute-start | bytes 405512 | tf_op jit(solution)/shard_map/ppermute | solution.py:286
  14.9 1.6 %collective-permute-start.9 = (s16[1040,128]{1,0:T(8,128)(2,1)S(1)}, s16[1040,128]{1,0:T(8,128)(2,1)S(1)}, u32[]{:S(2)}, u32[]{:S(2)}) collective-permute-start(s16[1040,128]{1,0:T(8,128)(2,1)S(1)} %get-tuple-element.67), channel_id=1, source_target_pairs={{0,2},{1,3},{4,0},{5,1},{8,4},{9,5},{12,8},{13,9},{14,12},{15,13},... | collective-permute-start | bytes 798728 | tf_op jit(solution)/shard_map/ppermute | solution.py:286
  17.0 2.1 %pick_blocks.6.before_ref = bf16[5,384,1024]{2,1,0:T(8,128)(2,1)S(1)} custom-call(bf16[384,16384]{1,0:T(8,128)(2,1)} %genotype_ref.7, s16[1040,128]{1,0:T(8,128)(2,1)S(1)} %get-tuple-element.64.refs_0_), custom_call_target="tpu_custom_call" | custom-call | flops 2000000000 | bytes 1000000 | tf_op jit(solution)/shard_map/pick_blocks/pallas_call | solution.py:219
  20.1 1.6 %collective-permute-start.11 = (s16[1040,128]{1,0:T(8,128)(2,1)S(1)}, s16[1040,128]{1,0:T(8,128)(2,1)S(1)}, u32[]{:S(2)}, u32[]{:S(2)}) collective-permute-start(s16[1040,128]{1,0:T(8,128)(2,1)S(1)} %get-tuple-element.69), channel_id=1, source_target_pairs={{0,2},{1,3},{4,0},{5,1},{8,4},{9,5},{12,8},{13,9},{14,12},{15,13},... | collective-permute-start | bytes 798728 | tf_op jit(solution)/shard_map/ppermute | solution.py:286
  22.2 2.1 %pick_blocks.7.before_ref.own_ref.own_left_ref.refs_1_.refs_4_ = bf16[5,384,1024]{2,1,0:T(8,128)(2,1)S(1)} custom-call(bf16[384,16384]{1,0:T(8,128)(2,1)} %genotype_ref.7, s16[1040,128]{1,0:T(8,128)(2,1)S(1)} %get-tuple-element.66.refs_0_), custom_call_target="tpu_custom_call" | custom-call | flops 2000000000 | bytes 1000000 | tf_op jit(solution)/shard_map/pick_blocks/pallas_call | solution.py:219
  24.4 1.6 %collective-permute-done.7.peer_ref.peer_left_ref.refs_2_.refs_5_ = bf16[5,384,1024]{2,1,0:T(8,128)(2,1)S(1)} collective-permute-done((bf16[5,384,1024]{2,1,0:T(8,128)(2,1)S(1)}, bf16[5,384,1024]{2,1,0:T(8,128)(2,1)S(1)}, u32[]{:S(2)}, u32[]{:S(2)}) %collective-permute-start.7) | collective-permute-done | bytes 3932192 | tf_op jit(solution)/shard_map/ppermute | solution.py:240
  26.9 1.6 %collective-permute-start.13 = (s16[1040,128]{1,0:T(8,128)(2,1)S(1)}, s16[1040,128]{1,0:T(8,128)(2,1)S(1)}, u32[]{:S(2)}, u32[]{:S(2)}) collective-permute-start(s16[1040,128]{1,0:T(8,128)(2,1)S(1)} %get-tuple-element.71), channel_id=1, source_target_pairs={{0,2},{1,3},{4,0},{5,1},{8,4},{9,5},{12,8},{13,9},{14,12},{15,13},... | collective-permute-start | bytes 798728 | tf_op jit(solution)/shard_map/ppermute | solution.py:286
  31.1 1.6 %collective-permute-start.15 = (s16[1040,128]{1,0:T(8,128)(2,1)S(1)}, s16[1040,128]{1,0:T(8,128)(2,1)S(1)}, u32[]{:S(2)}, u32[]{:S(2)}) collective-permute-start(s16[1040,128]{1,0:T(8,128)(2,1)S(1)} %get-tuple-element.73), channel_id=1, source_target_pairs={{0,2},{1,3},{4,0},{5,1},{8,4},{9,5},{12,8},{13,9},{14,12},{15,13},... | collective-permute-start | bytes 798728 | tf_op jit(solution)/shard_map/ppermute | solution.py:286
  33.2 3.0 %collective-permute-done.13.got_left_ref = s16[1040,128]{1,0:T(8,128)(2,1)S(1)} collective-permute-done((s16[1040,128]{1,0:T(8,128)(2,1)S(1)}, s16[1040,128]{1,0:T(8,128)(2,1)S(1)}, u32[]{:S(2)}, u32[]{:S(2)}) %collective-permute-start.13) | collective-permute-done | bytes 266272 | tf_op jit(solution)/shard_map/ppermute | solution.py:286
  36.2 1.6 %collective-permute-done.12.got_right_ref = s16[1040,128]{1,0:T(8,128)(2,1)S(1)} collective-permute-done((s16[1040,128]{1,0:T(8,128)(2,1)S(1)}, s16[1040,128]{1,0:T(8,128)(2,1)S(1)}, u32[]{:S(2)}, u32[]{:S(2)}) %collective-permute-start.12) | collective-permute-done | bytes 266272 | tf_op jit(solution)/shard_map/ppermute | solution.py:286
  38.6 1.6 %collective-permute-start.17 = (s16[1040,128]{1,0:T(8,128)(2,1)S(1)}, s16[1040,128]{1,0:T(8,128)(2,1)S(1)}, u32[]{:S(2)}, u32[]{:S(2)}) collective-permute-start(s16[1040,128]{1,0:T(8,128)(2,1)S(1)} %get-tuple-element.75), channel_id=1, source_target_pairs={{0,2},{1,3},{4,0},{5,1},{8,4},{9,5},{12,8},{13,9},{14,12},{15,13},... | collective-permute-start | bytes 798728 | tf_op jit(solution)/shard_map/ppermute | solution.py:286
  41.9 1.6 %collective-permute-done.14.got_right_ref = s16[1040,128]{1,0:T(8,128)(2,1)S(1)} collective-permute-done((s16[1040,128]{1,0:T(8,128)(2,1)S(1)}, s16[1040,128]{1,0:T(8,128)(2,1)S(1)}, u32[]{:S(2)}, u32[]{:S(2)}) %collective-permute-start.14) | collective-permute-done | bytes 266272 | tf_op jit(solution)/shard_map/ppermute | solution.py:286
  44.4 1.6 %collective-permute-start.19 = (s16[1040,128]{1,0:T(8,128)(2,1)S(1)}, s16[1040,128]{1,0:T(8,128)(2,1)S(1)}, u32[]{:S(2)}, u32[]{:S(2)}) collective-permute-start(s16[1040,128]{1,0:T(8,128)(2,1)S(1)} %get-tuple-element.77), channel_id=1, source_target_pairs={{0,2},{1,3},{4,0},{5,1},{8,4},{9,5},{12,8},{13,9},{14,12},{15,13},... | collective-permute-start | bytes 798728 | tf_op jit(solution)/shard_map/ppermute | solution.py:286
  48.0 1.6 %collective-permute-done.16.right_ref = s16[1040,128]{1,0:T(8,128)(2,1)S(1)} collective-permute-done((s16[1040,128]{1,0:T(8,128)(2,1)S(1)}, s16[1040,128]{1,0:T(8,128)(2,1)S(1)}, u32[]{:S(2)}, u32[]{:S(2)}) %collective-permute-start.16) | collective-permute-done | bytes 266272 | tf_op jit(solution)/shard_map/ppermute | solution.py:286
  51.0 1.6 %collective-permute-start.21 = (bf16[512,256]{1,0:T(8,128)(2,1)S(1)}, bf16[512,256]{1,0:T(8,128)(2,1)S(1)}, u32[]{:S(2)}, u32[]{:S(2)}) collective-permute-start(bf16[512,256]{1,0:T(8,128)(2,1)S(1)} %get-tuple-element.76.before_ref.refs_0_), channel_id=1, source_target_pairs={{0,2},{1,3},{4,0},{5,1},{8,4},{9,5},{12,8},{13,9},{14,12},{15,13},... | collective-permute-start | bytes 786440 | tf_op jit(solution)/shard_map/ppermute | solution.py:364
  53.7 1.6 %collective-permute-done.18.right_ref = s16[1040,128]{1,0:T(8,128)(2,1)S(1)} collective-permute-done((s16[1040,128]{1,0:T(8,128)(2,1)S(1)}, s16[1040,128]{1,0:T(8,128)(2,1)S(1)}, u32[]{:S(2)}, u32[]{:S(2)}) %collective-permute-start.18) | collective-permute-done | bytes 266272 | tf_op jit(solution)/shard_map/ppermute | solution.py:286
  56.7 1.4 %collective-permute-start.23 = (bf16[512,256]{1,0:T(8,128)(2,1)S(1)}, bf16[512,256]{1,0:T(8,128)(2,1)S(1)}, u32[]{:S(2)}, u32[]{:S(2)}) collective-permute-start(bf16[512,256]{1,0:T(8,128)(2,1)S(1)} %get-tuple-element.82.before_ref.refs_3_), channel_id=1, source_target_pairs={{0,2},{1,3},{4,0},{5,1},{8,4},{9,5},{12,8},{13,9},{14,12},{15,13},... | collective-permute-start | bytes 786440 | tf_op jit(solution)/shard_map/ppermute | solution.py:364
  63.5 2.4 %collective-permute-done.23.refs_3_ = bf16[512,256]{1,0:T(8,128)(2,1)S(1)} collective-permute-done((bf16[512,256]{1,0:T(8,128)(2,1)S(1)}, bf16[512,256]{1,0:T(8,128)(2,1)S(1)}, u32[]{:S(2)}, u32[]{:S(2)}) %collective-permute-start.23) | collective-permute-done | bytes 262176 | tf_op jit(solution)/shard_map/ppermute | solution.py:364
  65.9 1.4 %collective-permute-done.22.refs_0_ = bf16[512,256]{1,0:T(8,128)(2,1)S(1)} collective-permute-done((bf16[512,256]{1,0:T(8,128)(2,1)S(1)}, bf16[512,256]{1,0:T(8,128)(2,1)S(1)}, u32[]{:S(2)}, u32[]{:S(2)}) %collective-permute-start.22) | collective-permute-done | bytes 262176 | tf_op jit(solution)/shard_map/ppermute | solution.py:364
  67.9 1.4 %collective-permute-start.27 = (bf16[512,256]{1,0:T(8,128)(2,1)S(1)}, bf16[512,256]{1,0:T(8,128)(2,1)S(1)}, u32[]{:S(2)}, u32[]{:S(2)}) collective-permute-start(bf16[512,256]{1,0:T(8,128)(2,1)S(1)} %collective-permute-done.23.refs_3_), channel_id=1, source_target_pairs={{0,2},{1,3},{4,0},{5,1},{8,4},{9,5},{12,8},{13,9},{14,12},{15,13},... | collective-permute-start | bytes 786440 | tf_op jit(solution)/shard_map/ppermute | solution.py:364
  69.9 1.6 %collective-permute-done.25.refs_3_ = bf16[512,256]{1,0:T(8,128)(2,1)S(1)} collective-permute-done((bf16[512,256]{1,0:T(8,128)(2,1)S(1)}, bf16[512,256]{1,0:T(8,128)(2,1)S(1)}, u32[]{:S(2)}, u32[]{:S(2)}) %collective-permute-start.25) | collective-permute-done | bytes 262176 | tf_op jit(solution)/shard_map/ppermute | solution.py:364
  71.5 1.4 %collective-permute-done.24.refs_0_ = bf16[512,256]{1,0:T(8,128)(2,1)S(1)} collective-permute-done((bf16[512,256]{1,0:T(8,128)(2,1)S(1)}, bf16[512,256]{1,0:T(8,128)(2,1)S(1)}, u32[]{:S(2)}, u32[]{:S(2)}) %collective-permute-start.24) | collective-permute-done | bytes 262176 | tf_op jit(solution)/shard_map/ppermute | solution.py:364
  73.5 1.4 %collective-permute-start.29 = (bf16[512,256]{1,0:T(8,128)(2,1)S(1)}, bf16[512,256]{1,0:T(8,128)(2,1)S(1)}, u32[]{:S(2)}, u32[]{:S(2)}) collective-permute-start(bf16[512,256]{1,0:T(8,128)(2,1)S(1)} %collective-permute-done.25.refs_3_), channel_id=1, source_target_pairs={{0,2},{1,3},{4,0},{5,1},{8,4},{9,5},{12,8},{13,9},{14,12},{15,13},... | collective-permute-start | bytes 786440 | tf_op jit(solution)/shard_map/ppermute | solution.py:364
  75.6 1.6 %collective-permute-done.27.refs_3_ = bf16[512,256]{1,0:T(8,128)(2,1)S(1)} collective-permute-done((bf16[512,256]{1,0:T(8,128)(2,1)S(1)}, bf16[512,256]{1,0:T(8,128)(2,1)S(1)}, u32[]{:S(2)}, u32[]{:S(2)}) %collective-permute-start.27) | collective-permute-done | bytes 262176 | tf_op jit(solution)/shard_map/ppermute | solution.py:364
  77.1 1.4 %collective-permute-done.26.refs_0_ = bf16[512,256]{1,0:T(8,128)(2,1)S(1)} collective-permute-done((bf16[512,256]{1,0:T(8,128)(2,1)S(1)}, bf16[512,256]{1,0:T(8,128)(2,1)S(1)}, u32[]{:S(2)}, u32[]{:S(2)}) %collective-permute-start.26) | collective-permute-done | bytes 262176 | tf_op jit(solution)/shard_map/ppermute | solution.py:364
  79.2 1.4 %collective-permute-start.31 = (bf16[512,256]{1,0:T(8,128)(2,1)S(1)}, bf16[512,256]{1,0:T(8,128)(2,1)S(1)}, u32[]{:S(2)}, u32[]{:S(2)}) collective-permute-start(bf16[512,256]{1,0:T(8,128)(2,1)S(1)} %collective-permute-done.27.refs_3_), channel_id=1, source_target_pairs={{0,2},{1,3},{4,0},{5,1},{8,4},{9,5},{12,8},{13,9},{14,12},{15,13},... | collective-permute-start | bytes 786440 | tf_op jit(solution)/shard_map/ppermute | solution.py:364
  81.2 1.6 %collective-permute-done.29.refs_3_ = bf16[512,256]{1,0:T(8,128)(2,1)S(1)} collective-permute-done((bf16[512,256]{1,0:T(8,128)(2,1)S(1)}, bf16[512,256]{1,0:T(8,128)(2,1)S(1)}, u32[]{:S(2)}, u32[]{:S(2)}) %collective-permute-start.29) | collective-permute-done | bytes 262176 | tf_op jit(solution)/shard_map/ppermute | solution.py:364
  82.8 1.4 %collective-permute-done.28.refs_0_ = bf16[512,256]{1,0:T(8,128)(2,1)S(1)} collective-permute-done((bf16[512,256]{1,0:T(8,128)(2,1)S(1)}, bf16[512,256]{1,0:T(8,128)(2,1)S(1)}, u32[]{:S(2)}, u32[]{:S(2)}) %collective-permute-start.28) | collective-permute-done | bytes 262176 | tf_op jit(solution)/shard_map/ppermute | solution.py:364
  87.6 2.1 %collective-permute-done.30.refs_0_ = bf16[512,256]{1,0:T(8,128)(2,1)S(1)} collective-permute-done((bf16[512,256]{1,0:T(8,128)(2,1)S(1)}, bf16[512,256]{1,0:T(8,128)(2,1)S(1)}, u32[]{:S(2)}, u32[]{:S(2)}) %collective-permute-start.30) | collective-permute-done | bytes 262176 | tf_op jit(solution)/shard_map/ppermute | solution.py:364
  95.9 1.7 %collective-permute-done.36.got_ref = f32[384,256]{1,0:T(8,128)S(1)} collective-permute-done((f32[384,256]{1,0:T(8,128)S(1)}, f32[384,256]{1,0:T(8,128)S(1)}, u32[]{:S(2)}, u32[]{:S(2)}) %collective-permute-start.36) | collective-permute-done | bytes 393248 | tf_op jit(solution)/shard_map/ppermute | solution.py:369
  (98 shorter events, 41.2 us)
Async XLA Ops:
  5.8 6.9 %collective-permute-start.4 = (s16[528,128]{1,0:T(8,128)(2,1)S(1)}, s16[528,128]{1,0:T(8,128)(2,1)S(1)}, u32[]{:S(2)}, u32[]{:S(2)}) collective-permute-start(s16[528,128]{1,0:T(8,128)(2,1)S(1)} %get-tuple-element.63), channel_id=1, source_target_pairs={{0,2},{1,3},{4,0},{5,1},{8,4},{9,5},{12,8},{13,9},{14,12},{15,13},... | collective-permute-start | bytes 405512 | tf_op jit(solution)/shard_map/ppermute | solution.py:286
  8.4 5.7 %collective-permute-start.3 = (s16[528,128]{1,0:T(8,128)(2,1)S(1)}, s16[528,128]{1,0:T(8,128)(2,1)S(1)}, u32[]{:S(2)}, u32[]{:S(2)}) collective-permute-start(s16[528,128]{1,0:T(8,128)(2,1)S(1)} %get-tuple-element.61.before_ref), channel_id=1, source_target_pairs={{0,4},{1,5},{4,8},{5,9},{8,12},{9,13},{12,14},{13,15},{14,10},{15,... | collective-permute-start | bytes 405512 | tf_op jit(solution)/shard_map/ppermute | solution.py:286
  9.1 10.2 %collective-permute-start.6 = (s16[528,128]{1,0:T(8,128)(2,1)S(1)}, s16[528,128]{1,0:T(8,128)(2,1)S(1)}, u32[]{:S(2)}, u32[]{:S(2)}) collective-permute-start(s16[528,128]{1,0:T(8,128)(2,1)S(1)} %get-tuple-element.65), channel_id=1, source_target_pairs={{0,2},{1,3},{4,0},{5,1},{8,4},{9,5},{12,8},{13,9},{14,12},{15,13},... | collective-permute-start | bytes 405512 | tf_op jit(solution)/shard_map/ppermute | solution.py:286
  11.6 7.7 %collective-permute-start.5 = (s16[528,128]{1,0:T(8,128)(2,1)S(1)}, s16[528,128]{1,0:T(8,128)(2,1)S(1)}, u32[]{:S(2)}, u32[]{:S(2)}) collective-permute-start(s16[528,128]{1,0:T(8,128)(2,1)S(1)} %get-tuple-element.62.before_ref), channel_id=1, source_target_pairs={{0,4},{1,5},{4,8},{5,9},{8,12},{9,13},{12,14},{13,15},{14,10},{15,... | collective-permute-start | bytes 405512 | tf_op jit(solution)/shard_map/ppermute | solution.py:286
  14.9 9.4 %collective-permute-start.9 = (s16[1040,128]{1,0:T(8,128)(2,1)S(1)}, s16[1040,128]{1,0:T(8,128)(2,1)S(1)}, u32[]{:S(2)}, u32[]{:S(2)}) collective-permute-start(s16[1040,128]{1,0:T(8,128)(2,1)S(1)} %get-tuple-element.67), channel_id=1, source_target_pairs={{0,2},{1,3},{4,0},{5,1},{8,4},{9,5},{12,8},{13,9},{14,12},{15,13},... | collective-permute-start | bytes 798728 | tf_op jit(solution)/shard_map/ppermute | solution.py:286
  16.6 7.8 %collective-permute-start.8 = (s16[1040,128]{1,0:T(8,128)(2,1)S(1)}, s16[1040,128]{1,0:T(8,128)(2,1)S(1)}, u32[]{:S(2)}, u32[]{:S(2)}) collective-permute-start(s16[1040,128]{1,0:T(8,128)(2,1)S(1)} %get-tuple-element.64.refs_0_), channel_id=1, source_target_pairs={{0,4},{1,5},{4,8},{5,9},{8,12},{9,13},{12,14},{13,15},{14,10},{15,... | collective-permute-start | bytes 798728 | tf_op jit(solution)/shard_map/ppermute | solution.py:286
  19.2 6.8 %collective-permute-start.7 = (bf16[5,384,1024]{2,1,0:T(8,128)(2,1)S(1)}, bf16[5,384,1024]{2,1,0:T(8,128)(2,1)S(1)}, u32[]{:S(2)}, u32[]{:S(2)}) collective-permute-start(bf16[5,384,1024]{2,1,0:T(8,128)(2,1)S(1)} %pick_blocks.6.before_ref), channel_id=1, source_target_pairs={{0,1},{1,0},{2,3},{3,2},{4,5},{5,4},{6,7},{7,6},{8,9},{9,8},{10,11... | collective-permute-start | bytes 11796488 | tf_op jit(solution)/shard_map/ppermute | solution.py:240
  20.1 8.8 %collective-permute-start.11 = (s16[1040,128]{1,0:T(8,128)(2,1)S(1)}, s16[1040,128]{1,0:T(8,128)(2,1)S(1)}, u32[]{:S(2)}, u32[]{:S(2)}) collective-permute-start(s16[1040,128]{1,0:T(8,128)(2,1)S(1)} %get-tuple-element.69), channel_id=1, source_target_pairs={{0,2},{1,3},{4,0},{5,1},{8,4},{9,5},{12,8},{13,9},{14,12},{15,13},... | collective-permute-start | bytes 798728 | tf_op jit(solution)/shard_map/ppermute | solution.py:286
  21.8 8.5 %collective-permute-start.10 = (s16[1040,128]{1,0:T(8,128)(2,1)S(1)}, s16[1040,128]{1,0:T(8,128)(2,1)S(1)}, u32[]{:S(2)}, u32[]{:S(2)}) collective-permute-start(s16[1040,128]{1,0:T(8,128)(2,1)S(1)} %get-tuple-element.66.refs_0_), channel_id=1, source_target_pairs={{0,4},{1,5},{4,8},{5,9},{8,12},{9,13},{12,14},{13,15},{14,10},{15,... | collective-permute-start | bytes 798728 | tf_op jit(solution)/shard_map/ppermute | solution.py:286
  26.9 9.3 %collective-permute-start.13 = (s16[1040,128]{1,0:T(8,128)(2,1)S(1)}, s16[1040,128]{1,0:T(8,128)(2,1)S(1)}, u32[]{:S(2)}, u32[]{:S(2)}) collective-permute-start(s16[1040,128]{1,0:T(8,128)(2,1)S(1)} %get-tuple-element.71), channel_id=1, source_target_pairs={{0,2},{1,3},{4,0},{5,1},{8,4},{9,5},{12,8},{13,9},{14,12},{15,13},... | collective-permute-start | bytes 798728 | tf_op jit(solution)/shard_map/ppermute | solution.py:286
  28.5 9.3 %collective-permute-start.12 = (s16[1040,128]{1,0:T(8,128)(2,1)S(1)}, s16[1040,128]{1,0:T(8,128)(2,1)S(1)}, u32[]{:S(2)}, u32[]{:S(2)}) collective-permute-start(s16[1040,128]{1,0:T(8,128)(2,1)S(1)} %get-tuple-element.68.before_ref), channel_id=1, source_target_pairs={{0,4},{1,5},{4,8},{5,9},{8,12},{9,13},{12,14},{13,15},{14,10},{15,... | collective-permute-start | bytes 798728 | tf_op jit(solution)/shard_map/ppermute | solution.py:286
  31.1 10.7 %collective-permute-start.15 = (s16[1040,128]{1,0:T(8,128)(2,1)S(1)}, s16[1040,128]{1,0:T(8,128)(2,1)S(1)}, u32[]{:S(2)}, u32[]{:S(2)}) collective-permute-start(s16[1040,128]{1,0:T(8,128)(2,1)S(1)} %get-tuple-element.73), channel_id=1, source_target_pairs={{0,2},{1,3},{4,0},{5,1},{8,4},{9,5},{12,8},{13,9},{14,12},{15,13},... | collective-permute-start | bytes 798728 | tf_op jit(solution)/shard_map/ppermute | solution.py:286
  32.8 10.7 %collective-permute-start.14 = (s16[1040,128]{1,0:T(8,128)(2,1)S(1)}, s16[1040,128]{1,0:T(8,128)(2,1)S(1)}, u32[]{:S(2)}, u32[]{:S(2)}) collective-permute-start(s16[1040,128]{1,0:T(8,128)(2,1)S(1)} %get-tuple-element.70.before_ref), channel_id=1, source_target_pairs={{0,4},{1,5},{4,8},{5,9},{8,12},{9,13},{12,14},{13,15},{14,10},{15,... | collective-permute-start | bytes 798728 | tf_op jit(solution)/shard_map/ppermute | solution.py:286
  38.6 9.4 %collective-permute-start.17 = (s16[1040,128]{1,0:T(8,128)(2,1)S(1)}, s16[1040,128]{1,0:T(8,128)(2,1)S(1)}, u32[]{:S(2)}, u32[]{:S(2)}) collective-permute-start(s16[1040,128]{1,0:T(8,128)(2,1)S(1)} %get-tuple-element.75), channel_id=1, source_target_pairs={{0,2},{1,3},{4,0},{5,1},{8,4},{9,5},{12,8},{13,9},{14,12},{15,13},... | collective-permute-start | bytes 798728 | tf_op jit(solution)/shard_map/ppermute | solution.py:286
  40.3 9.3 %collective-permute-start.16 = (s16[1040,128]{1,0:T(8,128)(2,1)S(1)}, s16[1040,128]{1,0:T(8,128)(2,1)S(1)}, u32[]{:S(2)}, u32[]{:S(2)}) collective-permute-start(s16[1040,128]{1,0:T(8,128)(2,1)S(1)} %get-tuple-element.72.before_ref), channel_id=1, source_target_pairs={{0,4},{1,5},{4,8},{5,9},{8,12},{9,13},{12,14},{13,15},{14,10},{15,... | collective-permute-start | bytes 798728 | tf_op jit(solution)/shard_map/ppermute | solution.py:286
  44.4 9.4 %collective-permute-start.19 = (s16[1040,128]{1,0:T(8,128)(2,1)S(1)}, s16[1040,128]{1,0:T(8,128)(2,1)S(1)}, u32[]{:S(2)}, u32[]{:S(2)}) collective-permute-start(s16[1040,128]{1,0:T(8,128)(2,1)S(1)} %get-tuple-element.77), channel_id=1, source_target_pairs={{0,2},{1,3},{4,0},{5,1},{8,4},{9,5},{12,8},{13,9},{14,12},{15,13},... | collective-permute-start | bytes 798728 | tf_op jit(solution)/shard_map/ppermute | solution.py:286
  46.0 9.3 %collective-permute-start.18 = (s16[1040,128]{1,0:T(8,128)(2,1)S(1)}, s16[1040,128]{1,0:T(8,128)(2,1)S(1)}, u32[]{:S(2)}, u32[]{:S(2)}) collective-permute-start(s16[1040,128]{1,0:T(8,128)(2,1)S(1)} %get-tuple-element.74.before_ref), channel_id=1, source_target_pairs={{0,4},{1,5},{4,8},{5,9},{8,12},{9,13},{12,14},{13,15},{14,10},{15,... | collective-permute-start | bytes 798728 | tf_op jit(solution)/shard_map/ppermute | solution.py:286
  51.0 8.9 %collective-permute-start.21 = (bf16[512,256]{1,0:T(8,128)(2,1)S(1)}, bf16[512,256]{1,0:T(8,128)(2,1)S(1)}, u32[]{:S(2)}, u32[]{:S(2)}) collective-permute-start(bf16[512,256]{1,0:T(8,128)(2,1)S(1)} %get-tuple-element.76.before_ref.refs_0_), channel_id=1, source_target_pairs={{0,2},{1,3},{4,0},{5,1},{8,4},{9,5},{12,8},{13,9},{14,12},{15,13},... | collective-permute-start | bytes 786440 | tf_op jit(solution)/shard_map/ppermute | solution.py:364
  52.6 8.3 %collective-permute-start.20 = (bf16[512,256]{1,0:T(8,128)(2,1)S(1)}, bf16[512,256]{1,0:T(8,128)(2,1)S(1)}, u32[]{:S(2)}, u32[]{:S(2)}) collective-permute-start(bf16[512,256]{1,0:T(8,128)(2,1)S(1)} %get-tuple-element.76.before_ref.refs_0_), channel_id=1, source_target_pairs={{0,4},{1,5},{4,8},{5,9},{8,12},{9,13},{12,14},{13,15},{14,10},{15,... | collective-permute-start | bytes 786440 | tf_op jit(solution)/shard_map/ppermute | solution.py:364
  56.7 9.2 %collective-permute-start.23 = (bf16[512,256]{1,0:T(8,128)(2,1)S(1)}, bf16[512,256]{1,0:T(8,128)(2,1)S(1)}, u32[]{:S(2)}, u32[]{:S(2)}) collective-permute-start(bf16[512,256]{1,0:T(8,128)(2,1)S(1)} %get-tuple-element.82.before_ref.refs_3_), channel_id=1, source_target_pairs={{0,2},{1,3},{4,0},{5,1},{8,4},{9,5},{12,8},{13,9},{14,12},{15,13},... | collective-permute-start | bytes 786440 | tf_op jit(solution)/shard_map/ppermute | solution.py:364
  58.1 9.2 %collective-permute-start.22 = (bf16[512,256]{1,0:T(8,128)(2,1)S(1)}, bf16[512,256]{1,0:T(8,128)(2,1)S(1)}, u32[]{:S(2)}, u32[]{:S(2)}) collective-permute-start(bf16[512,256]{1,0:T(8,128)(2,1)S(1)} %get-tuple-element.82.before_ref.refs_3_), channel_id=1, source_target_pairs={{0,4},{1,5},{4,8},{5,9},{8,12},{9,13},{12,14},{13,15},{14,10},{15,... | collective-permute-start | bytes 786440 | tf_op jit(solution)/shard_map/ppermute | solution.py:364
  60.9 12.1 %collective-permute-start.24 = (bf16[512,256]{1,0:T(8,128)(2,1)S(1)}, bf16[512,256]{1,0:T(8,128)(2,1)S(1)}, u32[]{:S(2)}, u32[]{:S(2)}) collective-permute-start(bf16[512,256]{1,0:T(8,128)(2,1)S(1)} %collective-permute-done.20.refs_0_), channel_id=1, source_target_pairs={{0,4},{1,5},{4,8},{5,9},{8,12},{9,13},{12,14},{13,15},{14,10},{15,... | collective-permute-start | bytes 786440 | tf_op jit(solution)/shard_map/ppermute | solution.py:364
  61.6 9.9 %collective-permute-start.25 = (bf16[512,256]{1,0:T(8,128)(2,1)S(1)}, bf16[512,256]{1,0:T(8,128)(2,1)S(1)}, u32[]{:S(2)}, u32[]{:S(2)}) collective-permute-start(bf16[512,256]{1,0:T(8,128)(2,1)S(1)} %collective-permute-done.21.refs_3_), channel_id=1, source_target_pairs={{0,2},{1,3},{4,0},{5,1},{8,4},{9,5},{12,8},{13,9},{14,12},{15,13},... | collective-permute-start | bytes 786440 | tf_op jit(solution)/shard_map/ppermute | solution.py:364
  67.3 11.2 %collective-permute-start.26 = (bf16[512,256]{1,0:T(8,128)(2,1)S(1)}, bf16[512,256]{1,0:T(8,128)(2,1)S(1)}, u32[]{:S(2)}, u32[]{:S(2)}) collective-permute-start(bf16[512,256]{1,0:T(8,128)(2,1)S(1)} %collective-permute-done.22.refs_0_), channel_id=1, source_target_pairs={{0,4},{1,5},{4,8},{5,9},{8,12},{9,13},{12,14},{13,15},{14,10},{15,... | collective-permute-start | bytes 786440 | tf_op jit(solution)/shard_map/ppermute | solution.py:364
  67.9 9.2 %collective-permute-start.27 = (bf16[512,256]{1,0:T(8,128)(2,1)S(1)}, bf16[512,256]{1,0:T(8,128)(2,1)S(1)}, u32[]{:S(2)}, u32[]{:S(2)}) collective-permute-start(bf16[512,256]{1,0:T(8,128)(2,1)S(1)} %collective-permute-done.23.refs_3_), channel_id=1, source_target_pairs={{0,2},{1,3},{4,0},{5,1},{8,4},{9,5},{12,8},{13,9},{14,12},{15,13},... | collective-permute-start | bytes 786440 | tf_op jit(solution)/shard_map/ppermute | solution.py:364
  73.0 11.2 %collective-permute-start.28 = (bf16[512,256]{1,0:T(8,128)(2,1)S(1)}, bf16[512,256]{1,0:T(8,128)(2,1)S(1)}, u32[]{:S(2)}, u32[]{:S(2)}) collective-permute-start(bf16[512,256]{1,0:T(8,128)(2,1)S(1)} %collective-permute-done.24.refs_0_), channel_id=1, source_target_pairs={{0,4},{1,5},{4,8},{5,9},{8,12},{9,13},{12,14},{13,15},{14,10},{15,... | collective-permute-start | bytes 786440 | tf_op jit(solution)/shard_map/ppermute | solution.py:364
  73.5 9.2 %collective-permute-start.29 = (bf16[512,256]{1,0:T(8,128)(2,1)S(1)}, bf16[512,256]{1,0:T(8,128)(2,1)S(1)}, u32[]{:S(2)}, u32[]{:S(2)}) collective-permute-start(bf16[512,256]{1,0:T(8,128)(2,1)S(1)} %collective-permute-done.25.refs_3_), channel_id=1, source_target_pairs={{0,2},{1,3},{4,0},{5,1},{8,4},{9,5},{12,8},{13,9},{14,12},{15,13},... | collective-permute-start | bytes 786440 | tf_op jit(solution)/shard_map/ppermute | solution.py:364
  78.6 11.1 %collective-permute-start.30 = (bf16[512,256]{1,0:T(8,128)(2,1)S(1)}, bf16[512,256]{1,0:T(8,128)(2,1)S(1)}, u32[]{:S(2)}, u32[]{:S(2)}) collective-permute-start(bf16[512,256]{1,0:T(8,128)(2,1)S(1)} %collective-permute-done.26.refs_0_), channel_id=1, source_target_pairs={{0,4},{1,5},{4,8},{5,9},{8,12},{9,13},{12,14},{13,15},{14,10},{15,... | collective-permute-start | bytes 786440 | tf_op jit(solution)/shard_map/ppermute | solution.py:364
  79.2 8.4 %collective-permute-start.31 = (bf16[512,256]{1,0:T(8,128)(2,1)S(1)}, bf16[512,256]{1,0:T(8,128)(2,1)S(1)}, u32[]{:S(2)}, u32[]{:S(2)}) collective-permute-start(bf16[512,256]{1,0:T(8,128)(2,1)S(1)} %collective-permute-done.27.refs_3_), channel_id=1, source_target_pairs={{0,2},{1,3},{4,0},{5,1},{8,4},{9,5},{12,8},{13,9},{14,12},{15,13},... | collective-permute-start | bytes 786440 | tf_op jit(solution)/shard_map/ppermute | solution.py:364
  84.2 8.1 %collective-permute-start.33 = (bf16[256,256]{1,0:T(8,128)(2,1)S(1)}, bf16[256,256]{1,0:T(8,128)(2,1)S(1)}, u32[]{:S(2)}, u32[]{:S(2)}) collective-permute-start(bf16[256,256]{1,0:T(8,128)(2,1)S(1)} %slice.13), channel_id=1, source_target_pairs={{0,2},{1,3},{4,0},{5,1},{8,4},{9,5},{12,8},{13,9},{14,12},{15,13},... | collective-permute-start | bytes 393224 | tf_op jit(solution)/shard_map/ppermute | solution.py:364
  85.6 6.8 %collective-permute-start.32 = (bf16[256,256]{1,0:T(8,128)(2,1)S(1)}, bf16[256,256]{1,0:T(8,128)(2,1)S(1)}, u32[]{:S(2)}, u32[]{:S(2)}) collective-permute-start(bf16[256,256]{1,0:T(8,128)(2,1)S(1)} %slice.12), channel_id=1, source_target_pairs={{0,4},{1,5},{4,8},{5,9},{8,12},{9,13},{12,14},{13,15},{14,10},{15,... | collective-permute-start | bytes 393224 | tf_op jit(solution)/shard_map/ppermute | solution.py:364
  89.7 5.0 %collective-permute-start.34 = (bf16[256,256]{1,0:T(8,128)(2,1)S(1)}, bf16[256,256]{1,0:T(8,128)(2,1)S(1)}, u32[]{:S(2)}, u32[]{:S(2)}) collective-permute-start(bf16[256,256]{1,0:T(8,128)(2,1)S(1)} %slice.14), channel_id=1, source_target_pairs={{0,4},{1,5},{4,8},{5,9},{8,12},{9,13},{12,14},{13,15},{14,10},{15,... | collective-permute-start | bytes 393224 | tf_op jit(solution)/shard_map/ppermute | solution.py:364
  (18 other events, 81.1 us)

commit v5 on v4

--- a/solution.py
+++ b/solution.py
@@ -109,28 +109,21 @@
 
 
 def far_kernel(at, low, high, before_ref, res_ref, own_ref, peer_ref, right_ref, left_ref):
-    tiles = tiles_of(local_sum(res_ref, own_ref, peer_ref, at[0], low, high))
+    tiles = tiles_of(local_sum(res_ref, own_ref, peer_ref, at, low, high))
     half = len(tiles) // 2
     encode(right_ref, tiles[:half])
     encode(left_ref, tiles[half:])
 
 
-def hop_kernel(
-    at, low, high, before_ref, res_ref, own_ref, peer_ref, own_left_ref, peer_left_ref, got_right_ref,
-    got_left_ref, right_ref, left_ref
-):
-    for way, own, peer, got_ref, out_ref in (
-        (0, own_ref, peer_ref, got_right_ref, right_ref),
-        (1, own_left_ref, peer_left_ref, got_left_ref, left_ref),
-    ):
-        tiles = tiles_of(local_sum(res_ref, own, peer, at[way], low, high))
-        got = decode(got_ref)
-        height = tiles[0].shape[0]
-        count = got.shape[0] // height
-        first = 0 if way == 0 else len(tiles) - count
-        for k in range(count):
-            tiles[first + k] = tiles[first + k] + got[k * height : (k + 1) * height, :]
-        encode(out_ref, tiles)
+def hop_kernel(at, low, high, way, before_ref, res_ref, own_ref, peer_ref, got_ref, out_ref):
+    tiles = tiles_of(local_sum(res_ref, own_ref, peer_ref, at, low, high))
+    got = decode(got_ref)
+    height = tiles[0].shape[0]
+    count = got.shape[0] // height
+    first = 0 if way == 0 else len(tiles) - count
+    for k in range(count):
+        tiles[first + k] = tiles[first + k] + got[k * height : (k + 1) * height, :]
+    encode(out_ref, tiles)
 
 
 def near_kernel(at, before_ref, res_ref, own_ref, peer_ref, out_ref):
@@ -199,6 +192,7 @@
     part = block // pieces
     f32, bf16 = jnp.float32, jnp.bfloat16
     params = pltpu.CompilerParams(vmem_limit_bytes=VMEM)
+    small = pl.CostEstimate(flops=1, bytes_accessed=1, transcendentals=0)
     heavy = pl.CostEstimate(flops=10**10, bytes_accessed=10**6, transcendentals=0)
     longest = pl.CostEstimate(flops=10**11, bytes_accessed=10**6, transcendentals=0)
     light = pl.CostEstimate(flops=2 * 10**9, bytes_accessed=10**6, transcendentals=0)
@@ -266,24 +260,32 @@
             if d == reach > 1 and piece:
                 last, _ = lax.optimization_barrier((last, peer[d - 1][0]))
             if d == reach:
-                kernel, width, name, where = far_kernel, part // 2, "sum_far", (d,)
+                sent = last = pl.pallas_call(
+                    functools.partial(far_kernel, (own[d][1], peer[d][1]), low, high),
+                    in_specs=after(last, (res, own[d][0], peer[d][0])),
+                    out_shape=[shape_of(part // 2)] * 2,
+                    compiler_params=params,
+                    cost_estimate=longest,
+                    name="sum_far",
+                )(last, res, own[d][0], peer[d][0])
+                last = sent[0]
+                got[0, piece] = lax.ppermute(sent[0], "ind", right)
+                got[1, piece] = lax.ppermute(sent[1], "ind", left)
             else:
-                kernel, width, name, where = hop_kernel, part, "sum_hop", (d, size - d)
-            args = [res]
-            for w in where:
-                args += [own[w][0], peer[w][0]]
-            if d < reach:
-                args += got[piece]
-            sent = pl.pallas_call(
-                functools.partial(kernel, [(own[w][1], peer[w][1]) for w in where], low, high),
-                in_specs=after(last, args),
-                out_shape=[shape_of(width)] * 2,
-                compiler_params=params,
-                cost_estimate=longest,
-                name=name,
-            )(last, *args)
-            last = sent[0]
-            got[piece] = (lax.ppermute(sent[0], "ind", right), lax.ppermute(sent[1], "ind", left))
+                for way in (1, 0):
+                    w = size - d if way else d
+                    args = (res, own[w][0], peer[w][0], got[way, piece])
+                    last = pl.pallas_call(
+                        functools.partial(
+                            hop_kernel, (own[w][1], peer[w][1]), low, high, way
+                        ),
+                        in_specs=after(last, args),
+                        out_shape=shape_of(part),
+                        compiler_params=params,
+                        cost_estimate=longest,
+                        name="sum_hop",
+                    )(last, *args)
+                    got[way, piece] = lax.ppermute(last, "ind", left if way else right)
             if others and d == max(reach - 1, 1):
                 if piece == 0:
                     (last,) = pick([(others, True)], light, last)
@@ -315,7 +317,7 @@
             functools.partial(update_kernel, total, piece * part),
             grid=(1,),
             in_specs=[anywhere, full((cols, block))]
-            + [full(m.shape) for m in got[piece]]
+            + [full(got[way, piece].shape) for way in range(2)]
             + [rows] * 2
             + [full((1, cols))] * 2
             + [anywhere] * len(outs),
@@ -329,13 +331,13 @@
             compiler_params=params,
             cost_estimate=light,
             name="update",
-        )(last, near, *got[piece], incl_old, mean_old, prior, scale, *outs)
+        )(last, near, got[0, piece], got[1, piece], incl_old, mean_old, prior, scale, *outs)
         outs = (incl_new, mean_new)
         last = effect
         effects.append(effect)
 
     eta_shape = jax.ShapeDtypeStruct((people, cols), f32)
-    def product(found, eta, before):
+    def product(found, eta, before, cost):
         args = [v for d, _, effect in found for v in (effect, own[d][0], peer[d][0])] + list(eta)
         places = [((own[d][1], peer[d][1]), low) for d, low, _ in found]
         return pl.pallas_call(
@@ -343,28 +345,27 @@
             in_specs=after(before, args),
             out_shape=[eta_shape] * 2,
             compiler_params=params,
-            cost_estimate=heavy if eta else light,
+            cost_estimate=cost,
             name="add_eta",
         )(before, *args)
 
-    eta = product([(0, piece * part, effects[piece]) for piece in range(pieces)], (), last)
+    eta = product([(0, piece * part, effects[piece]) for piece in range(pieces)], (), last, small)
     held = {(way, piece): effects[piece] for way in range(2) for piece in range(pieces)}
     etas = [eta[0]]
     for hop in range(1, reach + 1):
         for piece in range(pieces):
-            found = []
-            for way in range(2):
+            for way in (1, 0):
                 message = held[way, piece]
                 if hop > 1:
-                    message, _ = lax.optimization_barrier((message, etas[-1 - pieces]))
+                    message, _ = lax.optimization_barrier((message, etas[-2 * pieces - 1]))
                 low = 0
                 if hop == reach:
                     low = way * (part // 2)
                     message = message[low : low + part // 2]
                 held[way, piece] = lax.ppermute(message, "ind", left if way else right)
-                found.append((hop if way else size - hop, piece * part + low, held[way, piece]))
-            eta = product(found, eta, eta[0])
-            etas.append(eta[0])
+                found = [(hop if way else size - hop, piece * part + low, held[way, piece])]
+                eta = product(found, eta, eta[0], small if len(etas) == 1 else light)
+                etas.append(eta[0])
 
     eta_got = lax.ppermute(eta[1], "ind", swap)
     resid_new = pl.pallas_call(

time: 98.7 us -> 239 us (2.42)
  Pallas kernels: 22.8 us -> 196 us
  waiting for transfers between devices: 38.6 us -> 5.53 us
    pallas_call x4, Pallas kernels: 7.54 us -> 126 us  [pick(): pl.pallas_call(functools.partial(pick_kernel, ring, wanted, block), in_sp...]
    pallas_call x8 -> x14, Pallas kernels: 6.13 us -> 35.9 us  [the longest x12 33.4 us: on_device(): pl.pallas_call(functools.partial(hop_kernel, (own[w][1], peer[w][1]), low...]
    pallas_call x9 -> x17, Pallas kernels: 4.71 us -> 26.4 us  [product(): pl.pallas_call(functools.partial(eta_kernel, places, not eta), in_specs=a...]
    ppermute x16, waiting for transfers between devices: 19.5 us -> 3.14 us  [on_device(): held[way, piece] = lax.ppermute(message, 'ind', left if way else right)]
    ppermute x16, waiting for transfers between devices: 15.7 us -> 0.68 us  [the longest x2 0.64 us: on_device(): got[1, piece] = lax.ppermute(sent[1], 'ind', left)]
  transfers between devices with their start and end apart: 37 -> 37, of which waited for: 27 -> 5; matrix products, arithmetic and copies ran while one was open for 0% -> 0% of each run, Pallas kernels for 22% -> 82%
where the time goes in v5:
time: 239 us; the launch traced here: 238 us
  Pallas kernels  196 us (82%)
  starting transfers between devices  35.6 us (15%)
  waiting for transfers between devices  5.53 us (2%)
    pallas_call x4, Pallas kernels, pick(): pl.pallas_call(functools.partial(pick_kernel, ring, wanted, block), in_sp...  126 us
    pallas_call x12, Pallas kernels, on_device(): pl.pallas_call(functools.partial(hop_kernel, (own[w][1], peer[w][1]), low...  33.4 us
    pallas_call x17, Pallas kernels, product(): pl.pallas_call(functools.partial(eta_kernel, places, not eta), in_specs=a...  26.4 us
    ppermute x16, starting transfers between devices, on_device(): held[way, piece] = lax.ppermute(message, 'ind', left if way else right)  17.2 us
    ppermute x12, starting transfers between devices, on_device(): got[way, piece] = lax.ppermute(last, 'ind', left if way else right)  12.3 us
  transfers between devices with their start and end apart: 37, of which 5 were waited for; matrix products, arithmetic and copies ran while one was open for 0% of the time, Pallas kernels for 82%

profile of v5, /device:TPU:0, one launch (start us, length us, event | category | flops | bytes accessed | tf_op | source)
XLA Modules:
  0.0 238.2 jit_solution(13869527252649571095)
XLA Ops:
  2.4 2.1 pick_blocks.5
  6.4 2.8 %collective-permute-start.3 = (s16[528,128]{1,0:T(8,128)(2,1)S(1)}, s16[528,128]{1,0:T(8,128)(2,1)S(1)}, u32[]{:S(2)}, u32[]{:S(2)}) collective-permute-start(s16[528,128]{1,0:T(8,128)(2,1)S(1)} %get-tuple-element.67), channel_id=1, source_target_pairs={{0,2},{1,3},{4,0},{5,1},{8,4},{9,5},{12,8},{13,9},{14,12},{15,13},... | collective-permute-start | bytes 405512 | tf_op jit(solution)/shard_map/ppermute | solution.py:273
  10.6 2.0 collective-permute-start.5
  14.5 1.7 collective-permute-start.8
  16.2 2.2 sum_hop.13.refs_0_
  18.7 120.3 %pick_blocks.6.before_ref = bf16[5,384,1024]{2,1,0:T(8,128)(2,1)} custom-call(bf16[384,16384]{1,0:T(8,128)(2,1)} %genotype_ref.7, s16[1040,128]{1,0:T(8,128)(2,1)} %sum_hop.13.refs_0_), custom_call_target="tpu_custom_call" | custom-call | flops 2000000000 | bytes 1000000 | tf_op jit(solution)/shard_map/pick_blocks/pallas_call | solution.py:213
  139.1 2.2 sum_hop.14.before_ref
  141.2 1.7 collective-permute-start.10
  142.9 2.1 sum_hop.15.refs_0_
  145.4 2.2 pick_blocks.7.before_ref.own_ref.refs_1_.refs_4_
  147.6 3.4 %sum_hop.16.before_ref = s16[1040,128]{1,0:T(8,128)(2,1)} custom-call(bf16[5,384,1024]{2,1,0:T(8,128)(2,1)S(1)} %pick_blocks.7.before_ref.own_ref.refs_1_.refs_4_, bf16[256,768]{1,0:T(8,128)(2,1)S(1)} %flip.1.before_ref.res_ref, bf16[5,384,1024]{2,1,0:T(8,128)(2,1)S(1)} %pick_blocks.7.before_ref.own_ref.refs_1_.refs_4_, ...), custom_call_target="tpu_custom_call" | custom-call | flops 99999997952 | bytes 1000000 | tf_op jit(solution)/shard_map/sum_hop/pallas_call | solution.py:278
  152.7 3.4 %sum_hop.17.before_ref = s16[1040,128]{1,0:T(8,128)(2,1)} custom-call(s16[1040,128]{1,0:T(8,128)(2,1)} %sum_hop.16.before_ref, bf16[256,768]{1,0:T(8,128)(2,1)S(1)} %flip.1.before_ref.res_ref, bf16[5,384,1024]{2,1,0:T(8,128)(2,1)S(1)} %pick_blocks.7.before_ref.own_ref.refs_1_.refs_4_, bf16[5,384,1024]{2,1,0:T(8,128)(2,1)} %collective-permute-done.7.peer_ref.refs_2_.refs_5_, ...), custom_call_target="tpu_custom_call" | custom-call | flops 99999997952 | bytes 1000000 | tf_op jit(solution)/shard_map/sum_hop/pallas_call | solution.py:278
  156.5 3.4 %sum_hop.18.before_ref = s16[1040,128]{1,0:T(8,128)(2,1)} custom-call(s16[1040,128]{1,0:T(8,128)(2,1)} %sum_hop.17.before_ref, bf16[256,768]{1,0:T(8,128)(2,1)S(1)} %flip.1.before_ref.res_ref, bf16[5,384,1024]{2,1,0:T(8,128)(2,1)S(1)} %pick_blocks.7.before_ref.own_ref.refs_1_.refs_4_, bf16[5,384,1024]{2,1,0:T(8,128)(2,1)} %collective-permute-done.7.peer_ref.refs_2_.refs_5_, ...), custom_call_target="tpu_custom_call" | custom-call | flops 99999997952 | bytes 1000000 | tf_op jit(solution)/shard_map/sum_hop/pallas_call | solution.py:278
  161.5 3.4 %sum_hop.19.before_ref = s16[1040,128]{1,0:T(8,128)(2,1)} custom-call(s16[1040,128]{1,0:T(8,128)(2,1)} %sum_hop.18.before_ref, bf16[256,768]{1,0:T(8,128)(2,1)S(1)} %flip.1.before_ref.res_ref, bf16[5,384,1024]{2,1,0:T(8,128)(2,1)S(1)} %pick_blocks.7.before_ref.own_ref.refs_1_.refs_4_, bf16[5,384,1024]{2,1,0:T(8,128)(2,1)} %collective-permute-done.7.peer_ref.refs_2_.refs_5_, ...), custom_call_target="tpu_custom_call" | custom-call | flops 99999997952 | bytes 1000000 | tf_op jit(solution)/shard_map/sum_hop/pallas_call | solution.py:278
  165.3 3.4 %sum_hop.20.before_ref = s16[1040,128]{1,0:T(8,128)(2,1)} custom-call(s16[1040,128]{1,0:T(8,128)(2,1)} %sum_hop.19.before_ref, bf16[256,768]{1,0:T(8,128)(2,1)S(1)} %flip.1.before_ref.res_ref, bf16[5,384,1024]{2,1,0:T(8,128)(2,1)S(1)} %pick_blocks.7.before_ref.own_ref.refs_1_.refs_4_, bf16[5,384,1024]{2,1,0:T(8,128)(2,1)} %collective-permute-done.7.peer_ref.refs_2_.refs_5_, ...), custom_call_target="tpu_custom_call" | custom-call | flops 99999997952 | bytes 1000000 | tf_op jit(solution)/shard_map/sum_hop/pallas_call | solution.py:278
  170.3 3.4 %sum_hop.21.before_ref = s16[1040,128]{1,0:T(8,128)(2,1)} custom-call(s16[1040,128]{1,0:T(8,128)(2,1)} %sum_hop.20.before_ref, bf16[256,768]{1,0:T(8,128)(2,1)S(1)} %flip.1.before_ref.res_ref, bf16[5,384,1024]{2,1,0:T(8,128)(2,1)S(1)} %pick_blocks.7.before_ref.own_ref.refs_1_.refs_4_, bf16[5,384,1024]{2,1,0:T(8,128)(2,1)} %collective-permute-done.7.peer_ref.refs_2_.refs_5_, ...), custom_call_target="tpu_custom_call" | custom-call | flops 99999997952 | bytes 1000000 | tf_op jit(solution)/shard_map/sum_hop/pallas_call | solution.py:278
  174.1 2.7 %sum_hop.22.before_ref = s16[1040,128]{1,0:T(8,128)(2,1)S(1)} custom-call(s16[1040,128]{1,0:T(8,128)(2,1)} %sum_hop.21.before_ref, bf16[256,768]{1,0:T(8,128)(2,1)S(1)} %flip.1.before_ref.res_ref, bf16[5,384,1024]{2,1,0:T(8,128)(2,1)S(1)} %pick_blocks.7.before_ref.own_ref.refs_1_.refs_4_, ...), custom_call_target="tpu_custom_call" | custom-call | flops 99999997952 | bytes 1000000 | tf_op jit(solution)/shard_map/sum_hop/pallas_call | solution.py:278
  176.8 1.7 collective-permute-start.19
  178.5 2.7 %sum_hop.23.before_ref = s16[1040,128]{1,0:T(8,128)(2,1)S(1)} custom-call(s16[1040,128]{1,0:T(8,128)(2,1)S(1)} %sum_hop.22.before_ref, bf16[256,768]{1,0:T(8,128)(2,1)S(1)} %flip.1.before_ref.res_ref, bf16[5,384,1024]{2,1,0:T(8,128)(2,1)S(1)} %pick_blocks.7.before_ref.own_ref.refs_1_.refs_4_, ...), custom_call_target="tpu_custom_call" | custom-call | flops 99999997952 | bytes 1000000 | tf_op jit(solution)/shard_map/sum_hop/pallas_call | solution.py:278
  181.6 3.0 %sum_near.1.before_ref.corr_ref = f32[256,1024]{1,0:T(8,128)S(1)} custom-call(s16[1040,128]{1,0:T(8,128)(2,1)S(1)} %sum_hop.23.before_ref, bf16[256,768]{1,0:T(8,128)(2,1)S(1)} %flip.1.before_ref.res_ref, bf16[5,384,1024]{2,1,0:T(8,128)(2,1)S(1)} %pick_blocks.7.before_ref.own_ref.refs_1_.refs_4_, ...), custom_call_target="tpu_custom_call" | custom-call | flops 2000000000 | bytes 1000000 | tf_op jit(solution)/shard_map/sum_near/pallas_call | solution.py:297
  184.7 2.4 update.2
  192.5 3.9 %add_eta.17 = (f32[384,256]{1,0:T(8,128)S(1)}, f32[384,256]{1,0:T(8,128)S(1)}) custom-call(bf16[512,256]{1,0:T(8,128)(2,1)S(1)} %get-tuple-element.74.before_ref.refs_3_, bf16[512,256]{1,0:T(8,128)(2,1)S(1)} %get-tuple-element.69.before_ref.refs_0_, bf16[5,384,1024]{2,1,0:T(8,128)(2,1)S(1)} %pick_blocks.7.before_ref.own_ref.refs_1_.refs_4_, ...), custom_call_target="tpu_custom_call" | custom-call | flops 1 | bytes 1 | tf_op jit(solution)/shard_map/add_eta/pallas_call | solution.py:343
  198.0 2.5 %add_eta.18 = (f32[384,256]{1,0:T(8,128)S(1)}, f32[384,256]{1,0:T(8,128)S(1)}) custom-call(f32[384,256]{1,0:T(8,128)S(1)} %get-tuple-element.75.before_ref.refs_3_, bf16[512,256]{1,0:T(8,128)(2,1)S(1)} %collective-permute-done.20.refs_0_, bf16[5,384,1024]{2,1,0:T(8,128)(2,1)S(1)} %pick_blocks.7.before_ref.own_ref.refs_1_.refs_4_, ...), custom_call_target="tpu_custom_call" | custom-call | flops 1 | bytes 1 | tf_op jit(solution)/shard_map/add_eta/pallas_call | solution.py:343
  201.0 2.5 %add_eta.19 = (f32[384,256]{1,0:T(8,128)S(1)}, f32[384,256]{1,0:T(8,128)S(1)}) custom-call(f32[384,256]{1,0:T(8,128)S(1)} %get-tuple-element.77.before_ref.refs_3_, bf16[512,256]{1,0:T(8,128)(2,1)S(1)} %collective-permute-done.21.refs_0_, bf16[5,384,1024]{2,1,0:T(8,128)(2,1)S(1)} %pick_blocks.7.before_ref.own_ref.refs_1_.refs_4_, ...), custom_call_target="tpu_custom_call" | custom-call | flops 2000000000 | bytes 1000000 | tf_op jit(solution)/shard_map/add_eta/pallas_call | solution.py:343
  205.1 2.5 %add_eta.20 = (f32[384,256]{1,0:T(8,128)S(1)}, f32[384,256]{1,0:T(8,128)S(1)}) custom-call(f32[384,256]{1,0:T(8,128)S(1)} %get-tuple-element.79.before_ref.refs_3_, bf16[512,256]{1,0:T(8,128)(2,1)S(1)} %collective-permute-done.22.refs_0_, bf16[5,384,1024]{2,1,0:T(8,128)(2,1)S(1)} %pick_blocks.7.before_ref.own_ref.refs_1_.refs_4_, ...), custom_call_target="tpu_custom_call" | custom-call | flops 2000000000 | bytes 1000000 | tf_op jit(solution)/shard_map/add_eta/pallas_call | solution.py:343
  208.1 2.5 %add_eta.21 = (f32[384,256]{1,0:T(8,128)S(1)}, f32[384,256]{1,0:T(8,128)S(1)}) custom-call(f32[384,256]{1,0:T(8,128)S(1)} %get-tuple-element.81.before_ref.refs_3_, bf16[512,256]{1,0:T(8,128)(2,1)S(1)} %collective-permute-done.23.refs_0_, bf16[5,384,1024]{2,1,0:T(8,128)(2,1)S(1)} %pick_blocks.7.before_ref.own_ref.refs_1_.refs_4_, ...), custom_call_target="tpu_custom_call" | custom-call | flops 2000000000 | bytes 1000000 | tf_op jit(solution)/shard_map/add_eta/pallas_call | solution.py:343
  212.2 2.5 %add_eta.22 = (f32[384,256]{1,0:T(8,128)S(1)}, f32[384,256]{1,0:T(8,128)S(1)}) custom-call(f32[384,256]{1,0:T(8,128)S(1)} %get-tuple-element.83.before_ref.refs_3_, bf16[512,256]{1,0:T(8,128)(2,1)S(1)} %collective-permute-done.24.refs_0_, bf16[5,384,1024]{2,1,0:T(8,128)(2,1)S(1)} %pick_blocks.7.before_ref.own_ref.refs_1_.refs_4_, ...), custom_call_target="tpu_custom_call" | custom-call | flops 2000000000 | bytes 1000000 | tf_op jit(solution)/shard_map/add_eta/pallas_call | solution.py:343
  215.2 2.5 %add_eta.23 = (f32[384,256]{1,0:T(8,128)S(1)}, f32[384,256]{1,0:T(8,128)S(1)}) custom-call(f32[384,256]{1,0:T(8,128)S(1)} %get-tuple-element.86.before_ref.refs_3_, bf16[512,256]{1,0:T(8,128)(2,1)S(1)} %collective-permute-done.25.refs_0_, bf16[5,384,1024]{2,1,0:T(8,128)(2,1)S(1)} %pick_blocks.7.before_ref.own_ref.refs_1_.refs_4_, ...), custom_call_target="tpu_custom_call" | custom-call | flops 2000000000 | bytes 1000000 | tf_op jit(solution)/shard_map/add_eta/pallas_call | solution.py:343
  217.7 1.8 collective-permute-start.30
  219.6 2.5 %add_eta.24 = (f32[384,256]{1,0:T(8,128)S(1)}, f32[384,256]{1,0:T(8,128)S(1)}) custom-call(f32[384,256]{1,0:T(8,128)S(1)} %get-tuple-element.89.before_ref.refs_3_, bf16[512,256]{1,0:T(8,128)(2,1)S(1)} %collective-permute-done.26.refs_0_, bf16[5,384,1024]{2,1,0:T(8,128)(2,1)S(1)} %pick_blocks.7.before_ref.own_ref.refs_1_.refs_4_, ...), custom_call_target="tpu_custom_call" | custom-call | flops 2000000000 | bytes 1000000 | tf_op jit(solution)/shard_map/add_eta/pallas_call | solution.py:343
  222.6 2.6 %add_eta.25 = (f32[384,256]{1,0:T(8,128)S(1)}, f32[384,256]{1,0:T(8,128)S(1)}) custom-call(f32[384,256]{1,0:T(8,128)S(1)} %get-tuple-element.92.before_ref.refs_3_, bf16[512,256]{1,0:T(8,128)(2,1)S(1)} %collective-permute-done.27.refs_0_, bf16[5,384,1024]{2,1,0:T(8,128)(2,1)S(1)} %pick_blocks.7.before_ref.own_ref.refs_1_.refs_4_, ...), custom_call_target="tpu_custom_call" | custom-call | flops 2000000000 | bytes 1000000 | tf_op jit(solution)/shard_map/add_eta/pallas_call | solution.py:343
  235.6 1.7 collective-permute-done.36.got_ref
  (112 shorter events, 37.7 us)
Async XLA Ops:
  6.4 6.8 %collective-permute-start.3 = (s16[528,128]{1,0:T(8,128)(2,1)S(1)}, s16[528,128]{1,0:T(8,128)(2,1)S(1)}, u32[]{:S(2)}, u32[]{:S(2)}) collective-permute-start(s16[528,128]{1,0:T(8,128)(2,1)S(1)} %get-tuple-element.67), channel_id=1, source_target_pairs={{0,2},{1,3},{4,0},{5,1},{8,4},{9,5},{12,8},{13,9},{14,12},{15,13},... | collective-permute-start | bytes 405512 | tf_op jit(solution)/shard_map/ppermute | solution.py:273
  9.2 7.0 %collective-permute-start.4 = (s16[528,128]{1,0:T(8,128)(2,1)}, s16[528,128]{1,0:T(8,128)(2,1)}, u32[]{:S(2)}, u32[]{:S(2)}) collective-permute-start(s16[528,128]{1,0:T(8,128)(2,1)} %get-tuple-element.65.before_ref), channel_id=1, source_target_pairs={{0,4},{1,5},{4,8},{5,9},{8,12},{9,13},{12,14},{13,15},{14,10},{15,... | collective-permute-start | bytes 405512 | tf_op jit(solution)/shard_map/ppermute | solution.py:272
  10.6 128.5 %collective-permute-start.5 = (s16[528,128]{1,0:T(8,128)(2,1)}, s16[528,128]{1,0:T(8,128)(2,1)}, u32[]{:S(2)}, u32[]{:S(2)}) collective-permute-start(s16[528,128]{1,0:T(8,128)(2,1)} %get-tuple-element.68), channel_id=1, source_target_pairs={{0,2},{1,3},{4,0},{5,1},{8,4},{9,5},{12,8},{13,9},{14,12},{15,13},... | collective-permute-start | bytes 405512 | tf_op jit(solution)/shard_map/ppermute | solution.py:273
  12.6 130.4 %collective-permute-start.6 = (s16[528,128]{1,0:T(8,128)(2,1)}, s16[528,128]{1,0:T(8,128)(2,1)}, u32[]{:S(2)}, u32[]{:S(2)}) collective-permute-start(s16[528,128]{1,0:T(8,128)(2,1)} %get-tuple-element.66.before_ref), channel_id=1, source_target_pairs={{0,4},{1,5},{4,8},{5,9},{8,12},{9,13},{12,14},{13,15},{14,10},{15,... | collective-permute-start | bytes 405512 | tf_op jit(solution)/shard_map/ppermute | solution.py:272
  14.5 133.1 %collective-permute-start.8 = (s16[1040,128]{1,0:T(8,128)(2,1)}, s16[1040,128]{1,0:T(8,128)(2,1)}, u32[]{:S(2)}, u32[]{:S(2)}) collective-permute-start(s16[1040,128]{1,0:T(8,128)(2,1)} %sum_hop.12.before_ref), channel_id=1, source_target_pairs={{0,2},{1,3},{4,0},{5,1},{8,4},{9,5},{12,8},{13,9},{14,12},{15,13},... | collective-permute-start | bytes 798728 | tf_op jit(solution)/shard_map/ppermute | solution.py:288
  18.4 134.3 %collective-permute-start.9 = (s16[1040,128]{1,0:T(8,128)(2,1)}, s16[1040,128]{1,0:T(8,128)(2,1)}, u32[]{:S(2)}, u32[]{:S(2)}) collective-permute-start(s16[1040,128]{1,0:T(8,128)(2,1)} %sum_hop.13.refs_0_), channel_id=1, source_target_pairs={{0,4},{1,5},{4,8},{5,9},{8,12},{9,13},{12,14},{13,15},{14,10},{15,... | collective-permute-start | bytes 798728 | tf_op jit(solution)/shard_map/ppermute | solution.py:288
  139.0 8.7 %collective-permute-start.7 = (bf16[5,384,1024]{2,1,0:T(8,128)(2,1)}, bf16[5,384,1024]{2,1,0:T(8,128)(2,1)}, u32[]{:S(2)}, u32[]{:S(2)}) collective-permute-start(bf16[5,384,1024]{2,1,0:T(8,128)(2,1)} %pick_blocks.6.before_ref), channel_id=1, source_target_pairs={{0,1},{1,0},{2,3},{3,2},{4,5},{5,4},{6,7},{7,6},{8,9},{9,8},{10,11... | collective-permute-start | bytes 11796488 | tf_op jit(solution)/shard_map/ppermute | solution.py:234
  141.2 15.2 %collective-permute-start.10 = (s16[1040,128]{1,0:T(8,128)(2,1)}, s16[1040,128]{1,0:T(8,128)(2,1)}, u32[]{:S(2)}, u32[]{:S(2)}) collective-permute-start(s16[1040,128]{1,0:T(8,128)(2,1)} %sum_hop.14.before_ref), channel_id=1, source_target_pairs={{0,2},{1,3},{4,0},{5,1},{8,4},{9,5},{12,8},{13,9},{14,12},{15,13},... | collective-permute-start | bytes 798728 | tf_op jit(solution)/shard_map/ppermute | solution.py:288
  145.1 16.4 %collective-permute-start.11 = (s16[1040,128]{1,0:T(8,128)(2,1)}, s16[1040,128]{1,0:T(8,128)(2,1)}, u32[]{:S(2)}, u32[]{:S(2)}) collective-permute-start(s16[1040,128]{1,0:T(8,128)(2,1)} %sum_hop.15.refs_0_), channel_id=1, source_target_pairs={{0,4},{1,5},{4,8},{5,9},{8,12},{9,13},{12,14},{13,15},{14,10},{15,... | collective-permute-start | bytes 798728 | tf_op jit(solution)/shard_map/ppermute | solution.py:288
  151.0 14.2 %collective-permute-start.12 = (s16[1040,128]{1,0:T(8,128)(2,1)}, s16[1040,128]{1,0:T(8,128)(2,1)}, u32[]{:S(2)}, u32[]{:S(2)}) collective-permute-start(s16[1040,128]{1,0:T(8,128)(2,1)} %sum_hop.16.before_ref), channel_id=1, source_target_pairs={{0,2},{1,3},{4,0},{5,1},{8,4},{9,5},{12,8},{13,9},{14,12},{15,13},... | collective-permute-start | bytes 798728 | tf_op jit(solution)/shard_map/ppermute | solution.py:288
  156.1 14.2 %collective-permute-start.13 = (s16[1040,128]{1,0:T(8,128)(2,1)}, s16[1040,128]{1,0:T(8,128)(2,1)}, u32[]{:S(2)}, u32[]{:S(2)}) collective-permute-start(s16[1040,128]{1,0:T(8,128)(2,1)} %sum_hop.17.before_ref), channel_id=1, source_target_pairs={{0,4},{1,5},{4,8},{5,9},{8,12},{9,13},{12,14},{13,15},{14,10},{15,... | collective-permute-start | bytes 798728 | tf_op jit(solution)/shard_map/ppermute | solution.py:288
  159.9 14.2 %collective-permute-start.14 = (s16[1040,128]{1,0:T(8,128)(2,1)}, s16[1040,128]{1,0:T(8,128)(2,1)}, u32[]{:S(2)}, u32[]{:S(2)}) collective-permute-start(s16[1040,128]{1,0:T(8,128)(2,1)} %sum_hop.18.before_ref), channel_id=1, source_target_pairs={{0,2},{1,3},{4,0},{5,1},{8,4},{9,5},{12,8},{13,9},{14,12},{15,13},... | collective-permute-start | bytes 798728 | tf_op jit(solution)/shard_map/ppermute | solution.py:288
  164.9 13.6 %collective-permute-start.15 = (s16[1040,128]{1,0:T(8,128)(2,1)}, s16[1040,128]{1,0:T(8,128)(2,1)}, u32[]{:S(2)}, u32[]{:S(2)}) collective-permute-start(s16[1040,128]{1,0:T(8,128)(2,1)} %sum_hop.19.before_ref), channel_id=1, source_target_pairs={{0,4},{1,5},{4,8},{5,9},{8,12},{9,13},{12,14},{13,15},{14,10},{15,... | collective-permute-start | bytes 798728 | tf_op jit(solution)/shard_map/ppermute | solution.py:288
  168.7 16.0 %collective-permute-start.17 = (s16[1040,128]{1,0:T(8,128)(2,1)}, s16[1040,128]{1,0:T(8,128)(2,1)}, u32[]{:S(2)}, u32[]{:S(2)}) collective-permute-start(s16[1040,128]{1,0:T(8,128)(2,1)} %sum_hop.20.before_ref), channel_id=1, source_target_pairs={{0,2},{1,3},{4,0},{5,1},{8,4},{9,5},{12,8},{13,9},{14,12},{15,13},... | collective-permute-start | bytes 798728 | tf_op jit(solution)/shard_map/ppermute | solution.py:288
  173.7 11.0 %collective-permute-start.16 = (s16[1040,128]{1,0:T(8,128)(2,1)}, s16[1040,128]{1,0:T(8,128)(2,1)}, u32[]{:S(2)}, u32[]{:S(2)}) collective-permute-start(s16[1040,128]{1,0:T(8,128)(2,1)} %sum_hop.21.before_ref), channel_id=1, source_target_pairs={{0,4},{1,5},{4,8},{5,9},{8,12},{9,13},{12,14},{13,15},{14,10},{15,... | collective-permute-start | bytes 798728 | tf_op jit(solution)/shard_map/ppermute | solution.py:288
  176.8 12.3 %collective-permute-start.19 = (s16[1040,128]{1,0:T(8,128)(2,1)S(1)}, s16[1040,128]{1,0:T(8,128)(2,1)S(1)}, u32[]{:S(2)}, u32[]{:S(2)}) collective-permute-start(s16[1040,128]{1,0:T(8,128)(2,1)S(1)} %sum_hop.22.before_ref), channel_id=1, source_target_pairs={{0,2},{1,3},{4,0},{5,1},{8,4},{9,5},{12,8},{13,9},{14,12},{15,13},... | collective-permute-start | bytes 798728 | tf_op jit(solution)/shard_map/ppermute | solution.py:288
  181.2 7.9 %collective-permute-start.18 = (s16[1040,128]{1,0:T(8,128)(2,1)S(1)}, s16[1040,128]{1,0:T(8,128)(2,1)S(1)}, u32[]{:S(2)}, u32[]{:S(2)}) collective-permute-start(s16[1040,128]{1,0:T(8,128)(2,1)S(1)} %sum_hop.23.before_ref), channel_id=1, source_target_pairs={{0,4},{1,5},{4,8},{5,9},{8,12},{9,13},{12,14},{13,15},{14,10},{15,... | collective-permute-start | bytes 798728 | tf_op jit(solution)/shard_map/ppermute | solution.py:288
  187.1 9.3 %collective-permute-start.20 = (bf16[512,256]{1,0:T(8,128)(2,1)S(1)}, bf16[512,256]{1,0:T(8,128)(2,1)S(1)}, u32[]{:S(2)}, u32[]{:S(2)}) collective-permute-start(bf16[512,256]{1,0:T(8,128)(2,1)S(1)} %get-tuple-element.69.before_ref.refs_0_), channel_id=1, source_target_pairs={{0,2},{1,3},{4,0},{5,1},{8,4},{9,5},{12,8},{13,9},{14,12},{15,13},... | collective-permute-start | bytes 786440 | tf_op jit(solution)/shard_map/ppermute | solution.py:365
  188.6 11.8 %collective-permute-start.21 = (bf16[512,256]{1,0:T(8,128)(2,1)S(1)}, bf16[512,256]{1,0:T(8,128)(2,1)S(1)}, u32[]{:S(2)}, u32[]{:S(2)}) collective-permute-start(bf16[512,256]{1,0:T(8,128)(2,1)S(1)} %get-tuple-element.69.before_ref.refs_0_), channel_id=1, source_target_pairs={{0,4},{1,5},{4,8},{5,9},{8,12},{9,13},{12,14},{13,15},{14,10},{15,... | collective-permute-start | bytes 786440 | tf_op jit(solution)/shard_map/ppermute | solution.py:365
  190.4 13.0 %collective-permute-start.22 = (bf16[512,256]{1,0:T(8,128)(2,1)S(1)}, bf16[512,256]{1,0:T(8,128)(2,1)S(1)}, u32[]{:S(2)}, u32[]{:S(2)}) collective-permute-start(bf16[512,256]{1,0:T(8,128)(2,1)S(1)} %get-tuple-element.74.before_ref.refs_3_), channel_id=1, source_target_pairs={{0,2},{1,3},{4,0},{5,1},{8,4},{9,5},{12,8},{13,9},{14,12},{15,13},... | collective-permute-start | bytes 786440 | tf_op jit(solution)/shard_map/ppermute | solution.py:365
  192.0 15.6 %collective-permute-start.23 = (bf16[512,256]{1,0:T(8,128)(2,1)S(1)}, bf16[512,256]{1,0:T(8,128)(2,1)S(1)}, u32[]{:S(2)}, u32[]{:S(2)}) collective-permute-start(bf16[512,256]{1,0:T(8,128)(2,1)S(1)} %get-tuple-element.74.before_ref.refs_3_), channel_id=1, source_target_pairs={{0,4},{1,5},{4,8},{5,9},{8,12},{9,13},{12,14},{13,15},{14,10},{15,... | collective-permute-start | bytes 786440 | tf_op jit(solution)/shard_map/ppermute | solution.py:365
  196.4 14.3 %collective-permute-start.24 = (bf16[512,256]{1,0:T(8,128)(2,1)S(1)}, bf16[512,256]{1,0:T(8,128)(2,1)S(1)}, u32[]{:S(2)}, u32[]{:S(2)}) collective-permute-start(bf16[512,256]{1,0:T(8,128)(2,1)S(1)} %collective-permute-done.20.refs_0_), channel_id=1, source_target_pairs={{0,2},{1,3},{4,0},{5,1},{8,4},{9,5},{12,8},{13,9},{14,12},{15,13},... | collective-permute-start | bytes 786440 | tf_op jit(solution)/shard_map/ppermute | solution.py:365
  200.5 14.3 %collective-permute-start.25 = (bf16[512,256]{1,0:T(8,128)(2,1)S(1)}, bf16[512,256]{1,0:T(8,128)(2,1)S(1)}, u32[]{:S(2)}, u32[]{:S(2)}) collective-permute-start(bf16[512,256]{1,0:T(8,128)(2,1)S(1)} %collective-permute-done.21.refs_0_), channel_id=1, source_target_pairs={{0,4},{1,5},{4,8},{5,9},{8,12},{9,13},{12,14},{13,15},{14,10},{15,... | collective-permute-start | bytes 786440 | tf_op jit(solution)/shard_map/ppermute | solution.py:365
  203.5 14.2 %collective-permute-start.26 = (bf16[512,256]{1,0:T(8,128)(2,1)S(1)}, bf16[512,256]{1,0:T(8,128)(2,1)S(1)}, u32[]{:S(2)}, u32[]{:S(2)}) collective-permute-start(bf16[512,256]{1,0:T(8,128)(2,1)S(1)} %collective-permute-done.22.refs_0_), channel_id=1, source_target_pairs={{0,2},{1,3},{4,0},{5,1},{8,4},{9,5},{12,8},{13,9},{14,12},{15,13},... | collective-permute-start | bytes 786440 | tf_op jit(solution)/shard_map/ppermute | solution.py:365
  207.6 14.4 %collective-permute-start.27 = (bf16[512,256]{1,0:T(8,128)(2,1)S(1)}, bf16[512,256]{1,0:T(8,128)(2,1)S(1)}, u32[]{:S(2)}, u32[]{:S(2)}) collective-permute-start(bf16[512,256]{1,0:T(8,128)(2,1)S(1)} %collective-permute-done.23.refs_0_), channel_id=1, source_target_pairs={{0,4},{1,5},{4,8},{5,9},{8,12},{9,13},{12,14},{13,15},{14,10},{15,... | collective-permute-start | bytes 786440 | tf_op jit(solution)/shard_map/ppermute | solution.py:365
  210.6 14.6 %collective-permute-start.28 = (bf16[512,256]{1,0:T(8,128)(2,1)S(1)}, bf16[512,256]{1,0:T(8,128)(2,1)S(1)}, u32[]{:S(2)}, u32[]{:S(2)}) collective-permute-start(bf16[512,256]{1,0:T(8,128)(2,1)S(1)} %collective-permute-done.24.refs_0_), channel_id=1, source_target_pairs={{0,2},{1,3},{4,0},{5,1},{8,4},{9,5},{12,8},{13,9},{14,12},{15,13},... | collective-permute-start | bytes 786440 | tf_op jit(solution)/shard_map/ppermute | solution.py:365
  214.7 12.5 %collective-permute-start.29 = (bf16[512,256]{1,0:T(8,128)(2,1)S(1)}, bf16[512,256]{1,0:T(8,128)(2,1)S(1)}, u32[]{:S(2)}, u32[]{:S(2)}) collective-permute-start(bf16[512,256]{1,0:T(8,128)(2,1)S(1)} %collective-permute-done.25.refs_0_), channel_id=1, source_target_pairs={{0,4},{1,5},{4,8},{5,9},{8,12},{9,13},{12,14},{13,15},{14,10},{15,... | collective-permute-start | bytes 786440 | tf_op jit(solution)/shard_map/ppermute | solution.py:365
  217.7 10.6 %collective-permute-start.30 = (bf16[512,256]{1,0:T(8,128)(2,1)S(1)}, bf16[512,256]{1,0:T(8,128)(2,1)S(1)}, u32[]{:S(2)}, u32[]{:S(2)}) collective-permute-start(bf16[512,256]{1,0:T(8,128)(2,1)S(1)} %collective-permute-done.26.refs_0_), channel_id=1, source_target_pairs={{0,2},{1,3},{4,0},{5,1},{8,4},{9,5},{12,8},{13,9},{14,12},{15,13},... | collective-permute-start | bytes 786440 | tf_op jit(solution)/shard_map/ppermute | solution.py:365
  222.1 8.2 %collective-permute-start.31 = (bf16[512,256]{1,0:T(8,128)(2,1)S(1)}, bf16[512,256]{1,0:T(8,128)(2,1)S(1)}, u32[]{:S(2)}, u32[]{:S(2)}) collective-permute-start(bf16[512,256]{1,0:T(8,128)(2,1)S(1)} %collective-permute-done.27.refs_0_), channel_id=1, source_target_pairs={{0,4},{1,5},{4,8},{5,9},{8,12},{9,13},{12,14},{13,15},{14,10},{15,... | collective-permute-start | bytes 786440 | tf_op jit(solution)/shard_map/ppermute | solution.py:365
  225.2 6.0 %collective-permute-start.32 = (bf16[256,256]{1,0:T(8,128)(2,1)S(1)}, bf16[256,256]{1,0:T(8,128)(2,1)S(1)}, u32[]{:S(2)}, u32[]{:S(2)}) collective-permute-start(bf16[256,256]{1,0:T(8,128)(2,1)S(1)} %slice.12), channel_id=1, source_target_pairs={{0,2},{1,3},{4,0},{5,1},{8,4},{9,5},{12,8},{13,9},{14,12},{15,13},... | collective-permute-start | bytes 393224 | tf_op jit(solution)/shard_map/ppermute | solution.py:365
  227.3 5.0 %collective-permute-start.33 = (bf16[256,256]{1,0:T(8,128)(2,1)S(1)}, bf16[256,256]{1,0:T(8,128)(2,1)S(1)}, u32[]{:S(2)}, u32[]{:S(2)}) collective-permute-start(bf16[256,256]{1,0:T(8,128)(2,1)S(1)} %slice.13), channel_id=1, source_target_pairs={{0,4},{1,5},{4,8},{5,9},{8,12},{9,13},{12,14},{13,15},{14,10},{15,... | collective-permute-start | bytes 393224 | tf_op jit(solution)/shard_map/ppermute | solution.py:365
  228.3 5.0 %collective-permute-start.34 = (bf16[256,256]{1,0:T(8,128)(2,1)S(1)}, bf16[256,256]{1,0:T(8,128)(2,1)S(1)}, u32[]{:S(2)}, u32[]{:S(2)}) collective-permute-start(bf16[256,256]{1,0:T(8,128)(2,1)S(1)} %slice.14), channel_id=1, source_target_pairs={{0,2},{1,3},{4,0},{5,1},{8,4},{9,5},{12,8},{13,9},{14,12},{15,13},... | collective-permute-start | bytes 393224 | tf_op jit(solution)/shard_map/ppermute | solution.py:365
  (18 other events, 328.9 us)

commit v6 on v5

--- a/solution.py
+++ b/solution.py
@@ -194,7 +194,8 @@
     params = pltpu.CompilerParams(vmem_limit_bytes=VMEM)
     small = pl.CostEstimate(flops=1, bytes_accessed=1, transcendentals=0)
     heavy = pl.CostEstimate(flops=10**10, bytes_accessed=10**6, transcendentals=0)
-    longest = pl.CostEstimate(flops=10**11, bytes_accessed=10**6, transcendentals=0)
+    longest = pl.CostEstimate(flops=2 * 10**10, bytes_accessed=10**6, transcendentals=0)
+    middle = pl.CostEstimate(flops=4 * 10**9, bytes_accessed=10**6, transcendentals=0)
     light = pl.CostEstimate(flops=2 * 10**9, bytes_accessed=10**6, transcendentals=0)
 
     swap = [(k, k ^ 1) for k in range(n)]
@@ -282,7 +283,7 @@
                         in_specs=after(last, args),
                         out_shape=shape_of(part),
                         compiler_params=params,
-                        cost_estimate=longest,
+                        cost_estimate=longest if d == reach - 1 else middle,
                         name="sum_hop",
                     )(last, *args)
                     got[way, piece] = lax.ppermute(last, "ind", left if way else right)

time: 239 us -> 97.5 us (0.41)
  Pallas kernels: 196 us -> 25.6 us
  waiting for transfers between devices: 5.53 us -> 33 us
    pallas_call x4, Pallas kernels: 126 us -> 7.54 us  [pick(): pl.pallas_call(functools.partial(pick_kernel, ring, wanted, block), in_sp...]
    pallas_call x12, Pallas kernels: 33.4 us -> 6.62 us  [on_device(): pl.pallas_call(functools.partial(hop_kernel, (own[w][1], peer[w][1]), low...]
    pallas_call x17, Pallas kernels: 26.4 us -> 6.02 us  [product(): pl.pallas_call(functools.partial(eta_kernel, places, not eta), in_specs=a...]
    ppermute x16, waiting for transfers between devices: 3.14 us -> 16.8 us  [on_device(): held[way, piece] = lax.ppermute(message, 'ind', left if way else right)]
    ppermute x12, waiting for transfers between devices: 0.03 us -> 12.2 us  [on_device(): got[way, piece] = lax.ppermute(last, 'ind', left if way else right)]
  transfers between devices with their start and end apart: 37 -> 37, of which waited for: 5 -> 17; matrix products, arithmetic and copies ran while one was open for 0% -> 0% of each run, Pallas kernels for 82% -> 25%
where the time goes in v6:
time: 97.5 us; the launch traced here: 97.3 us
  starting transfers between devices  36.8 us (38%)
  waiting for transfers between devices  33 us (34%)
  Pallas kernels  25.6 us (26%)
  between operations  1.17 us (1%)
    ppermute x16, starting transfers between devices, on_device(): held[way, piece] = lax.ppermute(message, 'ind', left if way else right)  17.3 us
    ppermute x16, waiting for transfers between devices, on_device(): held[way, piece] = lax.ppermute(message, 'ind', left if way else right)  16.8 us
    ppermute x12, starting transfers between devices, on_device(): got[way, piece] = lax.ppermute(last, 'ind', left if way else right)  12.8 us
    ppermute x12, waiting for transfers between devices, on_device(): got[way, piece] = lax.ppermute(last, 'ind', left if way else right)  12.2 us
    pallas_call x4, Pallas kernels, pick(): pl.pallas_call(functools.partial(pick_kernel, ring, wanted, block), in_sp...  7.54 us
    pallas_call x12, Pallas kernels, on_device(): pl.pallas_call(functools.partial(hop_kernel, (own[w][1], peer[w][1]), low...  6.62 us
    pallas_call x17, Pallas kernels, product(): pl.pallas_call(functools.partial(eta_kernel, places, not eta), in_specs=a...  6.02 us
    ppermute x2, starting transfers between devices, on_device(): got[1, piece] = lax.ppermute(sent[1], 'ind', left)  5.15 us
  transfers between devices with their start and end apart: 37, of which 17 were waited for; matrix products, arithmetic and copies ran while one was open for 0% of the time, Pallas kernels for 25%

profile of v6, /device:TPU:0, one launch (start us, length us, event | category | flops | bytes accessed | tf_op | source)
XLA Modules:
  0.0 97.3 jit_solution(11999782047470205057)
XLA Ops:
  2.4 2.1 %pick_blocks.5 = (bf16[3,384,1024]{2,1,0:T(8,128)(2,1)S(1)}, bf16[2,384,1024]{2,1,0:T(8,128)(2,1)S(1)}) custom-call(bf16[384,16384]{1,0:T(8,128)(2,1)} %genotype_ref.7, bf16[1,384,1024]{2,1,0:T(8,128)(2,1)S(1)} %pick_blocks.4.refs_0_), custom_call_target="tpu_custom_call" | custom-call | flops 10000000000 | bytes 1000000 | tf_op jit(solution)/shard_map/pick_blocks/pallas_call | solution.py:214
  5.8 2.6 %collective-permute-start.3 = (s16[528,128]{1,0:T(8,128)(2,1)S(1)}, s16[528,128]{1,0:T(8,128)(2,1)S(1)}, u32[]{:S(2)}, u32[]{:S(2)}) collective-permute-start(s16[528,128]{1,0:T(8,128)(2,1)S(1)} %get-tuple-element.67), channel_id=1, source_target_pairs={{0,2},{1,3},{4,0},{5,1},{8,4},{9,5},{12,8},{13,9},{14,12},{15,13},... | collective-permute-start | bytes 405512 | tf_op jit(solution)/shard_map/ppermute | solution.py:274
  9.1 2.5 %collective-permute-start.5 = (s16[528,128]{1,0:T(8,128)(2,1)S(1)}, s16[528,128]{1,0:T(8,128)(2,1)S(1)}, u32[]{:S(2)}, u32[]{:S(2)}) collective-permute-start(s16[528,128]{1,0:T(8,128)(2,1)S(1)} %get-tuple-element.68), channel_id=1, source_target_pairs={{0,2},{1,3},{4,0},{5,1},{8,4},{9,5},{12,8},{13,9},{14,12},{15,13},... | collective-permute-start | bytes 405512 | tf_op jit(solution)/shard_map/ppermute | solution.py:274
  13.2 1.7 %collective-permute-start.8 = (s16[1040,128]{1,0:T(8,128)(2,1)S(1)}, s16[1040,128]{1,0:T(8,128)(2,1)S(1)}, u32[]{:S(2)}, u32[]{:S(2)}) collective-permute-start(s16[1040,128]{1,0:T(8,128)(2,1)S(1)} %sum_hop.12.before_ref), channel_id=1, source_target_pairs={{0,2},{1,3},{4,0},{5,1},{8,4},{9,5},{12,8},{13,9},{14,12},{15,13},... | collective-permute-start | bytes 798728 | tf_op jit(solution)/shard_map/ppermute | solution.py:289
  15.9 2.1 %pick_blocks.6.before_ref = bf16[5,384,1024]{2,1,0:T(8,128)(2,1)S(1)} custom-call(bf16[384,16384]{1,0:T(8,128)(2,1)} %genotype_ref.7, s16[1040,128]{1,0:T(8,128)(2,1)S(1)} %sum_hop.13.refs_0_), custom_call_target="tpu_custom_call" | custom-call | flops 2000000000 | bytes 1000000 | tf_op jit(solution)/shard_map/pick_blocks/pallas_call | solution.py:214
  18.7 1.7 %collective-permute-start.10 = (s16[1040,128]{1,0:T(8,128)(2,1)S(1)}, s16[1040,128]{1,0:T(8,128)(2,1)S(1)}, u32[]{:S(2)}, u32[]{:S(2)}) collective-permute-start(s16[1040,128]{1,0:T(8,128)(2,1)S(1)} %sum_hop.14.before_ref), channel_id=1, source_target_pairs={{0,2},{1,3},{4,0},{5,1},{8,4},{9,5},{12,8},{13,9},{14,12},{15,13},... | collective-permute-start | bytes 798728 | tf_op jit(solution)/shard_map/ppermute | solution.py:289
  21.4 2.1 %pick_blocks.7.before_ref.own_ref.refs_1_.refs_4_ = bf16[5,384,1024]{2,1,0:T(8,128)(2,1)S(1)} custom-call(bf16[384,16384]{1,0:T(8,128)(2,1)} %genotype_ref.7, s16[1040,128]{1,0:T(8,128)(2,1)S(1)} %sum_hop.15.refs_0_), custom_call_target="tpu_custom_call" | custom-call | flops 2000000000 | bytes 1000000 | tf_op jit(solution)/shard_map/pick_blocks/pallas_call | solution.py:214
  23.6 1.4 %collective-permute-done.7.peer_ref.refs_2_.refs_5_ = bf16[5,384,1024]{2,1,0:T(8,128)(2,1)S(1)} collective-permute-done((bf16[5,384,1024]{2,1,0:T(8,128)(2,1)S(1)}, bf16[5,384,1024]{2,1,0:T(8,128)(2,1)S(1)}, u32[]{:S(2)}, u32[]{:S(2)}) %collective-permute-start.7) | collective-permute-done | bytes 3932192 | tf_op jit(solution)/shard_map/ppermute | solution.py:235
  25.5 1.7 %collective-permute-start.12 = (s16[1040,128]{1,0:T(8,128)(2,1)S(1)}, s16[1040,128]{1,0:T(8,128)(2,1)S(1)}, u32[]{:S(2)}, u32[]{:S(2)}) collective-permute-start(s16[1040,128]{1,0:T(8,128)(2,1)S(1)} %sum_hop.16.before_ref), channel_id=1, source_target_pairs={{0,2},{1,3},{4,0},{5,1},{8,4},{9,5},{12,8},{13,9},{14,12},{15,13},... | collective-permute-start | bytes 798728 | tf_op jit(solution)/shard_map/ppermute | solution.py:289
  28.7 1.7 %collective-permute-start.14 = (s16[1040,128]{1,0:T(8,128)(2,1)S(1)}, s16[1040,128]{1,0:T(8,128)(2,1)S(1)}, u32[]{:S(2)}, u32[]{:S(2)}) collective-permute-start(s16[1040,128]{1,0:T(8,128)(2,1)S(1)} %sum_hop.18.before_ref), channel_id=1, source_target_pairs={{0,2},{1,3},{4,0},{5,1},{8,4},{9,5},{12,8},{13,9},{14,12},{15,13},... | collective-permute-start | bytes 798728 | tf_op jit(solution)/shard_map/ppermute | solution.py:289
  31.4 3.3 %collective-permute-done.12.got_ref = s16[1040,128]{1,0:T(8,128)(2,1)S(1)} collective-permute-done((s16[1040,128]{1,0:T(8,128)(2,1)S(1)}, s16[1040,128]{1,0:T(8,128)(2,1)S(1)}, u32[]{:S(2)}, u32[]{:S(2)}) %collective-permute-start.12) | collective-permute-done | bytes 266272 | tf_op jit(solution)/shard_map/ppermute | solution.py:289
  35.3 1.7 %collective-permute-start.17 = (s16[1040,128]{1,0:T(8,128)(2,1)S(1)}, s16[1040,128]{1,0:T(8,128)(2,1)S(1)}, u32[]{:S(2)}, u32[]{:S(2)}) collective-permute-start(s16[1040,128]{1,0:T(8,128)(2,1)S(1)} %sum_hop.20.before_ref), channel_id=1, source_target_pairs={{0,2},{1,3},{4,0},{5,1},{8,4},{9,5},{12,8},{13,9},{14,12},{15,13},... | collective-permute-start | bytes 798728 | tf_op jit(solution)/shard_map/ppermute | solution.py:289
  38.1 2.4 %collective-permute-done.14.got_ref = s16[1040,128]{1,0:T(8,128)(2,1)S(1)} collective-permute-done((s16[1040,128]{1,0:T(8,128)(2,1)S(1)}, s16[1040,128]{1,0:T(8,128)(2,1)S(1)}, u32[]{:S(2)}, u32[]{:S(2)}) %collective-permute-start.14) | collective-permute-done | bytes 266272 | tf_op jit(solution)/shard_map/ppermute | solution.py:289
  41.0 1.7 %collective-permute-start.19 = (s16[1040,128]{1,0:T(8,128)(2,1)S(1)}, s16[1040,128]{1,0:T(8,128)(2,1)S(1)}, u32[]{:S(2)}, u32[]{:S(2)}) collective-permute-start(s16[1040,128]{1,0:T(8,128)(2,1)S(1)} %sum_hop.22.before_ref), channel_id=1, source_target_pairs={{0,2},{1,3},{4,0},{5,1},{8,4},{9,5},{12,8},{13,9},{14,12},{15,13},... | collective-permute-start | bytes 798728 | tf_op jit(solution)/shard_map/ppermute | solution.py:289
  44.5 4.0 %collective-permute-done.16.right_ref = s16[1040,128]{1,0:T(8,128)(2,1)S(1)} collective-permute-done((s16[1040,128]{1,0:T(8,128)(2,1)S(1)}, s16[1040,128]{1,0:T(8,128)(2,1)S(1)}, u32[]{:S(2)}, u32[]{:S(2)}) %collective-permute-start.16) | collective-permute-done | bytes 266272 | tf_op jit(solution)/shard_map/ppermute | solution.py:289
  48.6 1.3 %update.2 = (f32[1024,256]{1,0:T(8,128)}, f32[1024,256]{1,0:T(8,128)}, bf16[512,256]{1,0:T(8,128)(2,1)S(1)}) custom-call(f32[256,1024]{1,0:T(8,128)S(1)} %sum_near.1.before_ref.corr_ref, f32[256,1024]{1,0:T(8,128)S(1)} %sum_near.1.before_ref.corr_ref, s16[1040,128]{1,0:T(8,128)(2,1)S(1)} %collective-permute-done.16.right_ref, ...), custom_call_target="tpu_custom_call" | custom-call | flops 2000000000 | bytes 1000000 | tf_op jit(solution)/shard_map/update/pallas_call | solution.py:317
  49.9 1.6 %collective-permute-start.20 = (bf16[512,256]{1,0:T(8,128)(2,1)S(1)}, bf16[512,256]{1,0:T(8,128)(2,1)S(1)}, u32[]{:S(2)}, u32[]{:S(2)}) collective-permute-start(bf16[512,256]{1,0:T(8,128)(2,1)S(1)} %get-tuple-element.69.before_ref.refs_0_), channel_id=1, source_target_pairs={{0,2},{1,3},{4,0},{5,1},{8,4},{9,5},{12,8},{13,9},{14,12},{15,13},... | collective-permute-start | bytes 786440 | tf_op jit(solution)/shard_map/ppermute | solution.py:366
  51.9 2.3 %collective-permute-done.18.right_ref = s16[1040,128]{1,0:T(8,128)(2,1)S(1)} collective-permute-done((s16[1040,128]{1,0:T(8,128)(2,1)S(1)}, s16[1040,128]{1,0:T(8,128)(2,1)S(1)}, u32[]{:S(2)}, u32[]{:S(2)}) %collective-permute-start.18) | collective-permute-done | bytes 266272 | tf_op jit(solution)/shard_map/ppermute | solution.py:289
  55.6 1.6 %collective-permute-start.22 = (bf16[512,256]{1,0:T(8,128)(2,1)S(1)}, bf16[512,256]{1,0:T(8,128)(2,1)S(1)}, u32[]{:S(2)}, u32[]{:S(2)}) collective-permute-start(bf16[512,256]{1,0:T(8,128)(2,1)S(1)} %get-tuple-element.74.before_ref.refs_3_), channel_id=1, source_target_pairs={{0,2},{1,3},{4,0},{5,1},{8,4},{9,5},{12,8},{13,9},{14,12},{15,13},... | collective-permute-start | bytes 786440 | tf_op jit(solution)/shard_map/ppermute | solution.py:366
  58.2 1.6 %collective-permute-start.24 = (bf16[512,256]{1,0:T(8,128)(2,1)S(1)}, bf16[512,256]{1,0:T(8,128)(2,1)S(1)}, u32[]{:S(2)}, u32[]{:S(2)}) collective-permute-start(bf16[512,256]{1,0:T(8,128)(2,1)S(1)} %collective-permute-done.20.refs_0_), channel_id=1, source_target_pairs={{0,2},{1,3},{4,0},{5,1},{8,4},{9,5},{12,8},{13,9},{14,12},{15,13},... | collective-permute-start | bytes 786440 | tf_op jit(solution)/shard_map/ppermute | solution.py:366
  61.1 3.7 %collective-permute-done.22.refs_0_ = bf16[512,256]{1,0:T(8,128)(2,1)S(1)} collective-permute-done((bf16[512,256]{1,0:T(8,128)(2,1)S(1)}, bf16[512,256]{1,0:T(8,128)(2,1)S(1)}, u32[]{:S(2)}, u32[]{:S(2)}) %collective-permute-start.22) | collective-permute-done | bytes 262176 | tf_op jit(solution)/shard_map/ppermute | solution.py:366
  64.8 1.6 %collective-permute-start.26 = (bf16[512,256]{1,0:T(8,128)(2,1)S(1)}, bf16[512,256]{1,0:T(8,128)(2,1)S(1)}, u32[]{:S(2)}, u32[]{:S(2)}) collective-permute-start(bf16[512,256]{1,0:T(8,128)(2,1)S(1)} %collective-permute-done.22.refs_0_), channel_id=1, source_target_pairs={{0,2},{1,3},{4,0},{5,1},{8,4},{9,5},{12,8},{13,9},{14,12},{15,13},... | collective-permute-start | bytes 786440 | tf_op jit(solution)/shard_map/ppermute | solution.py:366
  67.7 2.8 %collective-permute-done.24.refs_0_ = bf16[512,256]{1,0:T(8,128)(2,1)S(1)} collective-permute-done((bf16[512,256]{1,0:T(8,128)(2,1)S(1)}, bf16[512,256]{1,0:T(8,128)(2,1)S(1)}, u32[]{:S(2)}, u32[]{:S(2)}) %collective-permute-start.24) | collective-permute-done | bytes 262176 | tf_op jit(solution)/shard_map/ppermute | solution.py:366
  70.4 1.6 %collective-permute-start.28 = (bf16[512,256]{1,0:T(8,128)(2,1)S(1)}, bf16[512,256]{1,0:T(8,128)(2,1)S(1)}, u32[]{:S(2)}, u32[]{:S(2)}) collective-permute-start(bf16[512,256]{1,0:T(8,128)(2,1)S(1)} %collective-permute-done.24.refs_0_), channel_id=1, source_target_pairs={{0,2},{1,3},{4,0},{5,1},{8,4},{9,5},{12,8},{13,9},{14,12},{15,13},... | collective-permute-start | bytes 786440 | tf_op jit(solution)/shard_map/ppermute | solution.py:366
  73.3 2.8 %collective-permute-done.26.refs_0_ = bf16[512,256]{1,0:T(8,128)(2,1)S(1)} collective-permute-done((bf16[512,256]{1,0:T(8,128)(2,1)S(1)}, bf16[512,256]{1,0:T(8,128)(2,1)S(1)}, u32[]{:S(2)}, u32[]{:S(2)}) %collective-permute-start.26) | collective-permute-done | bytes 262176 | tf_op jit(solution)/shard_map/ppermute | solution.py:366
  76.1 1.6 %collective-permute-start.30 = (bf16[512,256]{1,0:T(8,128)(2,1)S(1)}, bf16[512,256]{1,0:T(8,128)(2,1)S(1)}, u32[]{:S(2)}, u32[]{:S(2)}) collective-permute-start(bf16[512,256]{1,0:T(8,128)(2,1)S(1)} %collective-permute-done.26.refs_0_), channel_id=1, source_target_pairs={{0,2},{1,3},{4,0},{5,1},{8,4},{9,5},{12,8},{13,9},{14,12},{15,13},... | collective-permute-start | bytes 786440 | tf_op jit(solution)/shard_map/ppermute | solution.py:366
  79.1 2.6 %collective-permute-done.28.refs_0_ = bf16[512,256]{1,0:T(8,128)(2,1)S(1)} collective-permute-done((bf16[512,256]{1,0:T(8,128)(2,1)S(1)}, bf16[512,256]{1,0:T(8,128)(2,1)S(1)}, u32[]{:S(2)}, u32[]{:S(2)}) %collective-permute-start.28) | collective-permute-done | bytes 262176 | tf_op jit(solution)/shard_map/ppermute | solution.py:366
  81.7 1.6 %collective-permute-start.32 = (bf16[256,256]{1,0:T(8,128)(2,1)S(1)}, bf16[256,256]{1,0:T(8,128)(2,1)S(1)}, u32[]{:S(2)}, u32[]{:S(2)}) collective-permute-start(bf16[256,256]{1,0:T(8,128)(2,1)S(1)} %slice.12), channel_id=1, source_target_pairs={{0,2},{1,3},{4,0},{5,1},{8,4},{9,5},{12,8},{13,9},{14,12},{15,13},... | collective-permute-start | bytes 393224 | tf_op jit(solution)/shard_map/ppermute | solution.py:366
  84.6 1.8 %collective-permute-done.30.refs_0_ = bf16[512,256]{1,0:T(8,128)(2,1)S(1)} collective-permute-done((bf16[512,256]{1,0:T(8,128)(2,1)S(1)}, bf16[512,256]{1,0:T(8,128)(2,1)S(1)}, u32[]{:S(2)}, u32[]{:S(2)}) %collective-permute-start.30) | collective-permute-done | bytes 262176 | tf_op jit(solution)/shard_map/ppermute | solution.py:366
  86.4 2.5 %collective-permute-start.34 = (bf16[256,256]{1,0:T(8,128)(2,1)S(1)}, bf16[256,256]{1,0:T(8,128)(2,1)S(1)}, u32[]{:S(2)}, u32[]{:S(2)}) collective-permute-start(bf16[256,256]{1,0:T(8,128)(2,1)S(1)} %slice.14), channel_id=1, source_target_pairs={{0,2},{1,3},{4,0},{5,1},{8,4},{9,5},{12,8},{13,9},{14,12},{15,13},... | collective-permute-start | bytes 393224 | tf_op jit(solution)/shard_map/ppermute | solution.py:366
  91.8 2.6 %collective-permute-done.35.refs_0_ = bf16[256,256]{1,0:T(8,128)(2,1)S(1)} collective-permute-done((bf16[256,256]{1,0:T(8,128)(2,1)S(1)}, bf16[256,256]{1,0:T(8,128)(2,1)S(1)}, u32[]{:S(2)}, u32[]{:S(2)}) %collective-permute-start.35) | collective-permute-done | bytes 131104 | tf_op jit(solution)/shard_map/ppermute | solution.py:366
  94.7 1.7 %collective-permute-done.36.got_ref = f32[384,256]{1,0:T(8,128)S(1)} collective-permute-done((f32[384,256]{1,0:T(8,128)S(1)}, f32[384,256]{1,0:T(8,128)S(1)}, u32[]{:S(2)}, u32[]{:S(2)}) %collective-permute-start.36) | collective-permute-done | bytes 393248 | tf_op jit(solution)/shard_map/ppermute | solution.py:371
  (104 shorter events, 27.8 us)
Async XLA Ops:
  5.8 6.9 %collective-permute-start.3 = (s16[528,128]{1,0:T(8,128)(2,1)S(1)}, s16[528,128]{1,0:T(8,128)(2,1)S(1)}, u32[]{:S(2)}, u32[]{:S(2)}) collective-permute-start(s16[528,128]{1,0:T(8,128)(2,1)S(1)} %get-tuple-element.67), channel_id=1, source_target_pairs={{0,2},{1,3},{4,0},{5,1},{8,4},{9,5},{12,8},{13,9},{14,12},{15,13},... | collective-permute-start | bytes 405512 | tf_op jit(solution)/shard_map/ppermute | solution.py:274
  8.4 6.6 %collective-permute-start.4 = (s16[528,128]{1,0:T(8,128)(2,1)S(1)}, s16[528,128]{1,0:T(8,128)(2,1)S(1)}, u32[]{:S(2)}, u32[]{:S(2)}) collective-permute-start(s16[528,128]{1,0:T(8,128)(2,1)S(1)} %get-tuple-element.65.before_ref), channel_id=1, source_target_pairs={{0,4},{1,5},{4,8},{5,9},{8,12},{9,13},{12,14},{13,15},{14,10},{15,... | collective-permute-start | bytes 405512 | tf_op jit(solution)/shard_map/ppermute | solution.py:273
  9.1 9.1 %collective-permute-start.5 = (s16[528,128]{1,0:T(8,128)(2,1)S(1)}, s16[528,128]{1,0:T(8,128)(2,1)S(1)}, u32[]{:S(2)}, u32[]{:S(2)}) collective-permute-start(s16[528,128]{1,0:T(8,128)(2,1)S(1)} %get-tuple-element.68), channel_id=1, source_target_pairs={{0,2},{1,3},{4,0},{5,1},{8,4},{9,5},{12,8},{13,9},{14,12},{15,13},... | collective-permute-start | bytes 405512 | tf_op jit(solution)/shard_map/ppermute | solution.py:274
  11.6 8.9 %collective-permute-start.6 = (s16[528,128]{1,0:T(8,128)(2,1)S(1)}, s16[528,128]{1,0:T(8,128)(2,1)S(1)}, u32[]{:S(2)}, u32[]{:S(2)}) collective-permute-start(s16[528,128]{1,0:T(8,128)(2,1)S(1)} %get-tuple-element.66.before_ref), channel_id=1, source_target_pairs={{0,4},{1,5},{4,8},{5,9},{8,12},{9,13},{12,14},{13,15},{14,10},{15,... | collective-permute-start | bytes 405512 | tf_op jit(solution)/shard_map/ppermute | solution.py:273
  13.2 10.3 %collective-permute-start.8 = (s16[1040,128]{1,0:T(8,128)(2,1)S(1)}, s16[1040,128]{1,0:T(8,128)(2,1)S(1)}, u32[]{:S(2)}, u32[]{:S(2)}) collective-permute-start(s16[1040,128]{1,0:T(8,128)(2,1)S(1)} %sum_hop.12.before_ref), channel_id=1, source_target_pairs={{0,2},{1,3},{4,0},{5,1},{8,4},{9,5},{12,8},{13,9},{14,12},{15,13},... | collective-permute-start | bytes 798728 | tf_op jit(solution)/shard_map/ppermute | solution.py:289
  15.5 11.7 %collective-permute-start.9 = (s16[1040,128]{1,0:T(8,128)(2,1)S(1)}, s16[1040,128]{1,0:T(8,128)(2,1)S(1)}, u32[]{:S(2)}, u32[]{:S(2)}) collective-permute-start(s16[1040,128]{1,0:T(8,128)(2,1)S(1)} %sum_hop.13.refs_0_), channel_id=1, source_target_pairs={{0,4},{1,5},{4,8},{5,9},{8,12},{9,13},{12,14},{13,15},{14,10},{15,... | collective-permute-start | bytes 798728 | tf_op jit(solution)/shard_map/ppermute | solution.py:289
  18.1 6.8 %collective-permute-start.7 = (bf16[5,384,1024]{2,1,0:T(8,128)(2,1)S(1)}, bf16[5,384,1024]{2,1,0:T(8,128)(2,1)S(1)}, u32[]{:S(2)}, u32[]{:S(2)}) collective-permute-start(bf16[5,384,1024]{2,1,0:T(8,128)(2,1)S(1)} %pick_blocks.6.before_ref), channel_id=1, source_target_pairs={{0,1},{1,0},{2,3},{3,2},{4,5},{5,4},{6,7},{7,6},{8,9},{9,8},{10,11... | collective-permute-start | bytes 11796488 | tf_op jit(solution)/shard_map/ppermute | solution.py:235
  18.7 9.5 %collective-permute-start.10 = (s16[1040,128]{1,0:T(8,128)(2,1)S(1)}, s16[1040,128]{1,0:T(8,128)(2,1)S(1)}, u32[]{:S(2)}, u32[]{:S(2)}) collective-permute-start(s16[1040,128]{1,0:T(8,128)(2,1)S(1)} %sum_hop.14.before_ref), channel_id=1, source_target_pairs={{0,2},{1,3},{4,0},{5,1},{8,4},{9,5},{12,8},{13,9},{14,12},{15,13},... | collective-permute-start | bytes 798728 | tf_op jit(solution)/shard_map/ppermute | solution.py:289
  21.0 9.5 %collective-permute-start.11 = (s16[1040,128]{1,0:T(8,128)(2,1)S(1)}, s16[1040,128]{1,0:T(8,128)(2,1)S(1)}, u32[]{:S(2)}, u32[]{:S(2)}) collective-permute-start(s16[1040,128]{1,0:T(8,128)(2,1)S(1)} %sum_hop.15.refs_0_), channel_id=1, source_target_pairs={{0,4},{1,5},{4,8},{5,9},{8,12},{9,13},{12,14},{13,15},{14,10},{15,... | collective-permute-start | bytes 798728 | tf_op jit(solution)/shard_map/ppermute | solution.py:289
  25.5 9.3 %collective-permute-start.12 = (s16[1040,128]{1,0:T(8,128)(2,1)S(1)}, s16[1040,128]{1,0:T(8,128)(2,1)S(1)}, u32[]{:S(2)}, u32[]{:S(2)}) collective-permute-start(s16[1040,128]{1,0:T(8,128)(2,1)S(1)} %sum_hop.16.before_ref), channel_id=1, source_target_pairs={{0,2},{1,3},{4,0},{5,1},{8,4},{9,5},{12,8},{13,9},{14,12},{15,13},... | collective-permute-start | bytes 798728 | tf_op jit(solution)/shard_map/ppermute | solution.py:289
  27.8 9.3 %collective-permute-start.13 = (s16[1040,128]{1,0:T(8,128)(2,1)S(1)}, s16[1040,128]{1,0:T(8,128)(2,1)S(1)}, u32[]{:S(2)}, u32[]{:S(2)}) collective-permute-start(s16[1040,128]{1,0:T(8,128)(2,1)S(1)} %sum_hop.17.before_ref), channel_id=1, source_target_pairs={{0,4},{1,5},{4,8},{5,9},{8,12},{9,13},{12,14},{13,15},{14,10},{15,... | collective-permute-start | bytes 798728 | tf_op jit(solution)/shard_map/ppermute | solution.py:289
  28.7 11.7 %collective-permute-start.14 = (s16[1040,128]{1,0:T(8,128)(2,1)S(1)}, s16[1040,128]{1,0:T(8,128)(2,1)S(1)}, u32[]{:S(2)}, u32[]{:S(2)}) collective-permute-start(s16[1040,128]{1,0:T(8,128)(2,1)S(1)} %sum_hop.18.before_ref), channel_id=1, source_target_pairs={{0,2},{1,3},{4,0},{5,1},{8,4},{9,5},{12,8},{13,9},{14,12},{15,13},... | collective-permute-start | bytes 798728 | tf_op jit(solution)/shard_map/ppermute | solution.py:289
  31.0 11.8 %collective-permute-start.15 = (s16[1040,128]{1,0:T(8,128)(2,1)S(1)}, s16[1040,128]{1,0:T(8,128)(2,1)S(1)}, u32[]{:S(2)}, u32[]{:S(2)}) collective-permute-start(s16[1040,128]{1,0:T(8,128)(2,1)S(1)} %sum_hop.19.before_ref), channel_id=1, source_target_pairs={{0,4},{1,5},{4,8},{5,9},{8,12},{9,13},{12,14},{13,15},{14,10},{15,... | collective-permute-start | bytes 798728 | tf_op jit(solution)/shard_map/ppermute | solution.py:289
  35.3 13.2 %collective-permute-start.17 = (s16[1040,128]{1,0:T(8,128)(2,1)S(1)}, s16[1040,128]{1,0:T(8,128)(2,1)S(1)}, u32[]{:S(2)}, u32[]{:S(2)}) collective-permute-start(s16[1040,128]{1,0:T(8,128)(2,1)S(1)} %sum_hop.20.before_ref), channel_id=1, source_target_pairs={{0,2},{1,3},{4,0},{5,1},{8,4},{9,5},{12,8},{13,9},{14,12},{15,13},... | collective-permute-start | bytes 798728 | tf_op jit(solution)/shard_map/ppermute | solution.py:289
  37.7 10.9 %collective-permute-start.16 = (s16[1040,128]{1,0:T(8,128)(2,1)S(1)}, s16[1040,128]{1,0:T(8,128)(2,1)S(1)}, u32[]{:S(2)}, u32[]{:S(2)}) collective-permute-start(s16[1040,128]{1,0:T(8,128)(2,1)S(1)} %sum_hop.21.before_ref), channel_id=1, source_target_pairs={{0,4},{1,5},{4,8},{5,9},{8,12},{9,13},{12,14},{13,15},{14,10},{15,... | collective-permute-start | bytes 798728 | tf_op jit(solution)/shard_map/ppermute | solution.py:289
  41.0 13.2 %collective-permute-start.19 = (s16[1040,128]{1,0:T(8,128)(2,1)S(1)}, s16[1040,128]{1,0:T(8,128)(2,1)S(1)}, u32[]{:S(2)}, u32[]{:S(2)}) collective-permute-start(s16[1040,128]{1,0:T(8,128)(2,1)S(1)} %sum_hop.22.before_ref), channel_id=1, source_target_pairs={{0,2},{1,3},{4,0},{5,1},{8,4},{9,5},{12,8},{13,9},{14,12},{15,13},... | collective-permute-start | bytes 798728 | tf_op jit(solution)/shard_map/ppermute | solution.py:289
  43.4 10.8 %collective-permute-start.18 = (s16[1040,128]{1,0:T(8,128)(2,1)S(1)}, s16[1040,128]{1,0:T(8,128)(2,1)S(1)}, u32[]{:S(2)}, u32[]{:S(2)}) collective-permute-start(s16[1040,128]{1,0:T(8,128)(2,1)S(1)} %sum_hop.23.before_ref), channel_id=1, source_target_pairs={{0,4},{1,5},{4,8},{5,9},{8,12},{9,13},{12,14},{13,15},{14,10},{15,... | collective-permute-start | bytes 798728 | tf_op jit(solution)/shard_map/ppermute | solution.py:289
  49.9 8.3 %collective-permute-start.20 = (bf16[512,256]{1,0:T(8,128)(2,1)S(1)}, bf16[512,256]{1,0:T(8,128)(2,1)S(1)}, u32[]{:S(2)}, u32[]{:S(2)}) collective-permute-start(bf16[512,256]{1,0:T(8,128)(2,1)S(1)} %get-tuple-element.69.before_ref.refs_0_), channel_id=1, source_target_pairs={{0,2},{1,3},{4,0},{5,1},{8,4},{9,5},{12,8},{13,9},{14,12},{15,13},... | collective-permute-start | bytes 786440 | tf_op jit(solution)/shard_map/ppermute | solution.py:366
  51.5 8.7 %collective-permute-start.21 = (bf16[512,256]{1,0:T(8,128)(2,1)S(1)}, bf16[512,256]{1,0:T(8,128)(2,1)S(1)}, u32[]{:S(2)}, u32[]{:S(2)}) collective-permute-start(bf16[512,256]{1,0:T(8,128)(2,1)S(1)} %get-tuple-element.69.before_ref.refs_0_), channel_id=1, source_target_pairs={{0,4},{1,5},{4,8},{5,9},{8,12},{9,13},{12,14},{13,15},{14,10},{15,... | collective-permute-start | bytes 786440 | tf_op jit(solution)/shard_map/ppermute | solution.py:366
  55.6 9.2 %collective-permute-start.22 = (bf16[512,256]{1,0:T(8,128)(2,1)S(1)}, bf16[512,256]{1,0:T(8,128)(2,1)S(1)}, u32[]{:S(2)}, u32[]{:S(2)}) collective-permute-start(bf16[512,256]{1,0:T(8,128)(2,1)S(1)} %get-tuple-element.74.before_ref.refs_3_), channel_id=1, source_target_pairs={{0,2},{1,3},{4,0},{5,1},{8,4},{9,5},{12,8},{13,9},{14,12},{15,13},... | collective-permute-start | bytes 786440 | tf_op jit(solution)/shard_map/ppermute | solution.py:366
  57.2 9.6 %collective-permute-start.23 = (bf16[512,256]{1,0:T(8,128)(2,1)S(1)}, bf16[512,256]{1,0:T(8,128)(2,1)S(1)}, u32[]{:S(2)}, u32[]{:S(2)}) collective-permute-start(bf16[512,256]{1,0:T(8,128)(2,1)S(1)} %get-tuple-element.74.before_ref.refs_3_), channel_id=1, source_target_pairs={{0,4},{1,5},{4,8},{5,9},{8,12},{9,13},{12,14},{13,15},{14,10},{15,... | collective-permute-start | bytes 786440 | tf_op jit(solution)/shard_map/ppermute | solution.py:366
  58.2 12.3 %collective-permute-start.24 = (bf16[512,256]{1,0:T(8,128)(2,1)S(1)}, bf16[512,256]{1,0:T(8,128)(2,1)S(1)}, u32[]{:S(2)}, u32[]{:S(2)}) collective-permute-start(bf16[512,256]{1,0:T(8,128)(2,1)S(1)} %collective-permute-done.20.refs_0_), channel_id=1, source_target_pairs={{0,2},{1,3},{4,0},{5,1},{8,4},{9,5},{12,8},{13,9},{14,12},{15,13},... | collective-permute-start | bytes 786440 | tf_op jit(solution)/shard_map/ppermute | solution.py:366
  60.2 12.2 %collective-permute-start.25 = (bf16[512,256]{1,0:T(8,128)(2,1)S(1)}, bf16[512,256]{1,0:T(8,128)(2,1)S(1)}, u32[]{:S(2)}, u32[]{:S(2)}) collective-permute-start(bf16[512,256]{1,0:T(8,128)(2,1)S(1)} %collective-permute-done.21.refs_0_), channel_id=1, source_target_pairs={{0,4},{1,5},{4,8},{5,9},{8,12},{9,13},{12,14},{13,15},{14,10},{15,... | collective-permute-start | bytes 786440 | tf_op jit(solution)/shard_map/ppermute | solution.py:366
  64.8 11.2 %collective-permute-start.26 = (bf16[512,256]{1,0:T(8,128)(2,1)S(1)}, bf16[512,256]{1,0:T(8,128)(2,1)S(1)}, u32[]{:S(2)}, u32[]{:S(2)}) collective-permute-start(bf16[512,256]{1,0:T(8,128)(2,1)S(1)} %collective-permute-done.22.refs_0_), channel_id=1, source_target_pairs={{0,2},{1,3},{4,0},{5,1},{8,4},{9,5},{12,8},{13,9},{14,12},{15,13},... | collective-permute-start | bytes 786440 | tf_op jit(solution)/shard_map/ppermute | solution.py:366
  66.8 11.2 %collective-permute-start.27 = (bf16[512,256]{1,0:T(8,128)(2,1)S(1)}, bf16[512,256]{1,0:T(8,128)(2,1)S(1)}, u32[]{:S(2)}, u32[]{:S(2)}) collective-permute-start(bf16[512,256]{1,0:T(8,128)(2,1)S(1)} %collective-permute-done.23.refs_0_), channel_id=1, source_target_pairs={{0,4},{1,5},{4,8},{5,9},{8,12},{9,13},{12,14},{13,15},{14,10},{15,... | collective-permute-start | bytes 786440 | tf_op jit(solution)/shard_map/ppermute | solution.py:366
  70.4 11.2 %collective-permute-start.28 = (bf16[512,256]{1,0:T(8,128)(2,1)S(1)}, bf16[512,256]{1,0:T(8,128)(2,1)S(1)}, u32[]{:S(2)}, u32[]{:S(2)}) collective-permute-start(bf16[512,256]{1,0:T(8,128)(2,1)S(1)} %collective-permute-done.24.refs_0_), channel_id=1, source_target_pairs={{0,2},{1,3},{4,0},{5,1},{8,4},{9,5},{12,8},{13,9},{14,12},{15,13},... | collective-permute-start | bytes 786440 | tf_op jit(solution)/shard_map/ppermute | solution.py:366
  72.4 11.3 %collective-permute-start.29 = (bf16[512,256]{1,0:T(8,128)(2,1)S(1)}, bf16[512,256]{1,0:T(8,128)(2,1)S(1)}, u32[]{:S(2)}, u32[]{:S(2)}) collective-permute-start(bf16[512,256]{1,0:T(8,128)(2,1)S(1)} %collective-permute-done.25.refs_0_), channel_id=1, source_target_pairs={{0,4},{1,5},{4,8},{5,9},{8,12},{9,13},{12,14},{13,15},{14,10},{15,... | collective-permute-start | bytes 786440 | tf_op jit(solution)/shard_map/ppermute | solution.py:366
  76.1 10.3 %collective-permute-start.30 = (bf16[512,256]{1,0:T(8,128)(2,1)S(1)}, bf16[512,256]{1,0:T(8,128)(2,1)S(1)}, u32[]{:S(2)}, u32[]{:S(2)}) collective-permute-start(bf16[512,256]{1,0:T(8,128)(2,1)S(1)} %collective-permute-done.26.refs_0_), channel_id=1, source_target_pairs={{0,2},{1,3},{4,0},{5,1},{8,4},{9,5},{12,8},{13,9},{14,12},{15,13},... | collective-permute-start | bytes 786440 | tf_op jit(solution)/shard_map/ppermute | solution.py:366
  78.0 11.3 %collective-permute-start.31 = (bf16[512,256]{1,0:T(8,128)(2,1)S(1)}, bf16[512,256]{1,0:T(8,128)(2,1)S(1)}, u32[]{:S(2)}, u32[]{:S(2)}) collective-permute-start(bf16[512,256]{1,0:T(8,128)(2,1)S(1)} %collective-permute-done.27.refs_0_), channel_id=1, source_target_pairs={{0,4},{1,5},{4,8},{5,9},{8,12},{9,13},{12,14},{13,15},{14,10},{15,... | collective-permute-start | bytes 786440 | tf_op jit(solution)/shard_map/ppermute | solution.py:366
  81.7 8.1 %collective-permute-start.32 = (bf16[256,256]{1,0:T(8,128)(2,1)S(1)}, bf16[256,256]{1,0:T(8,128)(2,1)S(1)}, u32[]{:S(2)}, u32[]{:S(2)}) collective-permute-start(bf16[256,256]{1,0:T(8,128)(2,1)S(1)} %slice.12), channel_id=1, source_target_pairs={{0,2},{1,3},{4,0},{5,1},{8,4},{9,5},{12,8},{13,9},{14,12},{15,13},... | collective-permute-start | bytes 393224 | tf_op jit(solution)/shard_map/ppermute | solution.py:366
  83.7 7.3 %collective-permute-start.33 = (bf16[256,256]{1,0:T(8,128)(2,1)S(1)}, bf16[256,256]{1,0:T(8,128)(2,1)S(1)}, u32[]{:S(2)}, u32[]{:S(2)}) collective-permute-start(bf16[256,256]{1,0:T(8,128)(2,1)S(1)} %slice.13), channel_id=1, source_target_pairs={{0,4},{1,5},{4,8},{5,9},{8,12},{9,13},{12,14},{13,15},{14,10},{15,... | collective-permute-start | bytes 393224 | tf_op jit(solution)/shard_map/ppermute | solution.py:366
  86.4 5.1 %collective-permute-start.34 = (bf16[256,256]{1,0:T(8,128)(2,1)S(1)}, bf16[256,256]{1,0:T(8,128)(2,1)S(1)}, u32[]{:S(2)}, u32[]{:S(2)}) collective-permute-start(bf16[256,256]{1,0:T(8,128)(2,1)S(1)} %slice.14), channel_id=1, source_target_pairs={{0,2},{1,3},{4,0},{5,1},{8,4},{9,5},{12,8},{13,9},{14,12},{15,13},... | collective-permute-start | bytes 393224 | tf_op jit(solution)/shard_map/ppermute | solution.py:366
  (14 other events, 55.3 us)

commit v7 on v6

--- a/solution.py
+++ b/solution.py
@@ -50,14 +50,11 @@
 
 def pick_kernel(ring, wanted, block, genotype_ref, *refs):
     outs, sems = refs[-1 - len(wanted) : -1], refs[-1]
-    core = lax.rem(lax.axis_index("ind"), 2)
-    needed = sorted({d for distances, _ in wanted for d in distances})
-    owners = dict(zip(needed, owners_of(ring, needed)))
+    other = 1 - lax.rem(lax.axis_index("ind"), 2)
     copies = []
-    for out_ref, (distances, swapped) in zip(outs, wanted):
-        parity = 1 - core if swapped else core
-        for k, d in enumerate(distances):
-            at = pl.multiple_of((2 * owners[d] + parity) * block, LANES)
+    for out_ref, distances in zip(outs, wanted):
+        for k, owner in enumerate(owners_of(ring, distances)):
+            at = pl.multiple_of((2 * owner + other) * block, LANES)
             copies.append(
                 pltpu.make_async_copy(
                     genotype_ref.at[:, pl.ds(at, block)], out_ref.at[k], sems.at[len(copies)]
@@ -74,10 +71,18 @@
     out_ref[:, people:] = other_ref[...].T
 
 
-def local_sum(res_ref, own_ref, peer_ref, at, low, high):
-    people = own_ref.shape[1]
+def own_columns(ring, own_ref, peer_ref, d, low, high):
+    (owner,) = owners_of(ring, [d])
+    block = peer_ref.shape[2]
+    at = (2 * owner + lax.rem(lax.axis_index("ind"), 2)) * block + low
+    return own_ref[:, pl.ds(pl.multiple_of(at, LANES), high - low)]
+
+
+def local_sum(ring, res_ref, own_ref, peer_ref, at, low, high):
+    people = own_ref.shape[0]
+    own = own_columns(ring, own_ref, peer_ref, at[0], low, high)
     return jnp.dot(
-        res_ref[:, :people], own_ref[at[0], :, low:high], preferred_element_type=jnp.float32
+        res_ref[:, :people], own, preferred_element_type=jnp.float32
     ) + jnp.dot(
         res_ref[:, people:], peer_ref[at[1], :, low:high], preferred_element_type=jnp.float32
     )
@@ -108,15 +113,17 @@
     return [total[:, k : k + LANES] for k in range(0, total.shape[1], LANES)]
 
 
-def far_kernel(at, low, high, before_ref, res_ref, own_ref, peer_ref, right_ref, left_ref):
-    tiles = tiles_of(local_sum(res_ref, own_ref, peer_ref, at, low, high))
+def far_kernel(ring, at, low, high, before_ref, res_ref, own_ref, peer_ref, right_ref, left_ref):
+    tiles = tiles_of(local_sum(ring, res_ref, own_ref, peer_ref, at, low, high))
     half = len(tiles) // 2
     encode(right_ref, tiles[:half])
     encode(left_ref, tiles[half:])
 
 
-def hop_kernel(at, low, high, way, before_ref, res_ref, own_ref, peer_ref, got_ref, out_ref):
-    tiles = tiles_of(local_sum(res_ref, own_ref, peer_ref, at, low, high))
+def hop_kernel(
+    ring, at, low, high, way, before_ref, res_ref, own_ref, peer_ref, got_ref, out_ref
+):
+    tiles = tiles_of(local_sum(ring, res_ref, own_ref, peer_ref, at, low, high))
     got = decode(got_ref)
     height = tiles[0].shape[0]
     count = got.shape[0] // height
@@ -126,8 +133,8 @@
     encode(out_ref, tiles)
 
 
-def near_kernel(at, before_ref, res_ref, own_ref, peer_ref, out_ref):
-    out_ref[...] = local_sum(res_ref, own_ref, peer_ref, at, 0, own_ref.shape[2])
+def near_kernel(ring, at, before_ref, res_ref, own_ref, peer_ref, out_ref):
+    out_ref[...] = local_sum(ring, res_ref, own_ref, peer_ref, at, 0, peer_ref.shape[2])
 
 
 def update_kernel(total, low, before_ref, corr_ref, right_ref, left_ref, incl_ref, mean_ref, prior_ref,
@@ -158,14 +165,15 @@
         effect_ref[rows, :] = (incl_new * mean_new).astype(jnp.bfloat16)
 
 
-def eta_kernel(places, first, before_ref, *refs):
+def eta_kernel(ring, places, first, before_ref, *refs):
     out_ref, out_other_ref = refs[-2:]
     mine = other = None
     for k, (at, low) in enumerate(places):
         effect_ref, own_ref, peer_ref = refs[3 * k : 3 * k + 3]
         effect = effect_ref[...]
         high = low + effect.shape[0]
-        a = jnp.dot(own_ref[at[0], :, low:high], effect, preferred_element_type=jnp.float32)
+        own = own_columns(ring, own_ref, peer_ref, at[0], low, high)
+        a = jnp.dot(own, effect, preferred_element_type=jnp.float32)
         b = jnp.dot(peer_ref[at[1], :, low:high], effect, preferred_element_type=jnp.float32)
         mine = a if mine is None else mine + a
         other = b if other is None else other + b
@@ -194,7 +202,6 @@
     params = pltpu.CompilerParams(vmem_limit_bytes=VMEM)
     small = pl.CostEstimate(flops=1, bytes_accessed=1, transcendentals=0)
     heavy = pl.CostEstimate(flops=10**10, bytes_accessed=10**6, transcendentals=0)
-    longest = pl.CostEstimate(flops=2 * 10**10, bytes_accessed=10**6, transcendentals=0)
     middle = pl.CostEstimate(flops=4 * 10**9, bytes_accessed=10**6, transcendentals=0)
     light = pl.CostEstimate(flops=2 * 10**9, bytes_accessed=10**6, transcendentals=0)
 
@@ -210,44 +217,44 @@
     def after(before, args):
         return [anywhere] + [pl.BlockSpec()] * len(args)
 
-    def pick(wanted, cost, *before):
+    def pick(wanted, source, cost, *before):
         return pl.pallas_call(
             functools.partial(pick_kernel, ring, wanted, block),
-            in_specs=[pl.BlockSpec(memory_space=pltpu.HBM)] + [anywhere] * len(before),
+            in_specs=[anywhere] * (1 + len(before)),
             out_specs=[anywhere] * len(wanted),
             out_shape=[
                 jax.ShapeDtypeStruct((len(distances), people, block), bf16)
-                for distances, _ in wanted
+                for distances in wanted
             ],
-            scratch_shapes=[pltpu.SemaphoreType.DMA((sum(len(d) for d, _ in wanted),))],
+            scratch_shapes=[pltpu.SemaphoreType.DMA((sum(len(d) for d in wanted),))],
             compiler_params=params,
             cost_estimate=cost,
             name="pick_blocks",
-        )(pltpu.with_memory_space_constraint(genotype, pltpu.HBM), *before)
+        )(pltpu.with_memory_space_constraint(genotype, source), *before)
 
     order = [reach]
     for d in range(reach - 1, 0, -1):
         order += [d, size - d]
     order += [0]
-    own, peer = {}, {}
+    peer = {}
 
     def swapped(distances, sent):
         got = lax.ppermute(sent, "ind", swap)
         peer.update({d: (got, k) for k, d in enumerate(distances)})
 
-    residual_other = lax.ppermute(residual, "ind", swap)
-    (last,) = pick([(order[:1], True)], heavy)
-    swapped(order[:1], last)
-    next_two, others = order[1:3], order[3:]
-    mine, last = pick([(order[:3], False), (next_two, True)], heavy, last)
-    own.update({d: (mine, k) for k, d in enumerate(order[:3])})
-    swapped(next_two, last)
+    first, later = [b for b in (order[:1], order[1:3]) if b], [b for b in (order[3:5], order[5:]) if b]
+    sent = pick(first, pltpu.HBM, light)
+    last = sent[0]
+    for distances, array in zip(first, sent):
+        swapped(distances, array)
+    mine, _ = lax.optimization_barrier((residual, last))
+    residual_other = lax.ppermute(mine, "ind", swap)
     res = last = pl.pallas_call(
         flip_kernel,
         in_specs=after(last, (residual, residual_other)),
         out_shape=jax.ShapeDtypeStruct((cols, 2 * people), bf16),
         compiler_params=params,
-        cost_estimate=heavy,
+        cost_estimate=light,
         name="flip",
     )(last, residual, residual_other)
 
@@ -262,47 +269,46 @@
                 last, _ = lax.optimization_barrier((last, peer[d - 1][0]))
             if d == reach:
                 sent = last = pl.pallas_call(
-                    functools.partial(far_kernel, (own[d][1], peer[d][1]), low, high),
-                    in_specs=after(last, (res, own[d][0], peer[d][0])),
+                    functools.partial(far_kernel, ring, (d, peer[d][1]), low, high),
+                    in_specs=after(last, (res, genotype, peer[d][0])),
                     out_shape=[shape_of(part // 2)] * 2,
                     compiler_params=params,
-                    cost_estimate=longest,
+                    cost_estimate=heavy,
                     name="sum_far",
-                )(last, res, own[d][0], peer[d][0])
+                )(last, res, genotype, peer[d][0])
                 last = sent[0]
                 got[0, piece] = lax.ppermute(sent[0], "ind", right)
                 got[1, piece] = lax.ppermute(sent[1], "ind", left)
             else:
+                if d == reach - 1 > 1 and piece == pieces - 1:
+                    last, _ = lax.optimization_barrier((last, peer[d - 1][0]))
                 for way in (1, 0):
                     w = size - d if way else d
-                    args = (res, own[w][0], peer[w][0], got[way, piece])
+                    args = (res, genotype, peer[w][0], got[way, piece])
                     last = pl.pallas_call(
                         functools.partial(
-                            hop_kernel, (own[w][1], peer[w][1]), low, high, way
+                            hop_kernel, ring, (w, peer[w][1]), low, high, way
                         ),
                         in_specs=after(last, args),
                         out_shape=shape_of(part),
                         compiler_params=params,
-                        cost_estimate=longest if d == reach - 1 else middle,
+                        cost_estimate=heavy if d == reach - 1 else middle,
                         name="sum_hop",
                     )(last, *args)
                     got[way, piece] = lax.ppermute(last, "ind", left if way else right)
-            if others and d == max(reach - 1, 1):
-                if piece == 0:
-                    (last,) = pick([(others, True)], light, last)
-                    swapped(others, last)
-                if piece == pieces - 1:
-                    (last,) = pick([(others, False)], light, last)
-                    own.update({w: (last, k) for k, w in enumerate(others)})
+            if later and (d, piece) in ((reach, pieces - 1), (reach - 1, 0)):
+                distances = later.pop(0)
+                (last,) = pick([distances], pltpu.VMEM, light, last)
+                swapped(distances, last)
 
     near = last = pl.pallas_call(
-        functools.partial(near_kernel, (own[0][1], peer[0][1])),
-        in_specs=after(last, (res, own[0], peer[0])),
+        functools.partial(near_kernel, ring, (0, peer[0][1])),
+        in_specs=after(last, (res, genotype, peer[0][0])),
         out_shape=jax.ShapeDtypeStruct((cols, block), f32),
         compiler_params=params,
         cost_estimate=light,
         name="sum_near",
-    )(last, res, own[0][0], peer[0][0])
+    )(last, res, genotype, peer[0][0])
 
     prior = prior_logit.reshape(1, cols)
     scale = slab_scale.reshape(1, cols)
@@ -339,10 +345,10 @@
 
     eta_shape = jax.ShapeDtypeStruct((people, cols), f32)
     def product(found, eta, before, cost):
-        args = [v for d, _, effect in found for v in (effect, own[d][0], peer[d][0])] + list(eta)
-        places = [((own[d][1], peer[d][1]), low) for d, low, _ in found]
+        args = [v for d, _, effect in found for v in (effect, genotype, peer[d][0])] + list(eta)
+        places = [((d, peer[d][1]), low) for d, low, _ in found]
         return pl.pallas_call(
-            functools.partial(eta_kernel, places, not eta),
+            functools.partial(eta_kernel, ring, places, not eta),
             in_specs=after(before, args),
             out_shape=[eta_shape] * 2,
             compiler_params=params,

time: 97.5 us -> 97.9 us (level)
  waiting for transfers between devices: 33 us -> 39.6 us
  Pallas kernels: 25.6 us -> 20.2 us
    pallas_call x4 -> x3, Pallas kernels: 7.54 us -> 2.13 us  [pick(): pl.pallas_call(functools.partial(pick_kernel, ring, wanted, block), in_sp...]
    ppermute x1, waiting for transfers between devices: 0.01 us -> 3.93 us  [on_device(): residual_other = lax.ppermute(mine, 'ind', swap)]
    ppermute x12, waiting for transfers between devices: 12.2 us -> 15.3 us  [on_device(): got[way, piece] = lax.ppermute(last, 'ind', left if way else right)]
    ppermute x3 -> x4, waiting for transfers between devices: 1.36 us -> 0.01 us  [swapped(): got = lax.ppermute(sent, 'ind', swap)]
  transfers between devices with their start and end apart: 37 -> 38, of which waited for: 17 -> 16; matrix products, arithmetic and copies ran while one was open for 0% -> 0% of each run, Pallas kernels for 25% -> 18%
where the time goes in v7:
time: 97.9 us; the launch traced here: 97.8 us
  waiting for transfers between devices  39.6 us (40%)
  starting transfers between devices  35.9 us (37%)
  Pallas kernels  20.2 us (21%)
  between operations  1.19 us (1%)
    ppermute x16, waiting for transfers between devices, on_device(): held[way, piece] = lax.ppermute(message, 'ind', left if way else right)  17.2 us
    ppermute x16, starting transfers between devices, on_device(): held[way, piece] = lax.ppermute(message, 'ind', left if way else right)  16.7 us
    ppermute x12, waiting for transfers between devices, on_device(): got[way, piece] = lax.ppermute(last, 'ind', left if way else right)  15.3 us
    ppermute x12, starting transfers between devices, on_device(): got[way, piece] = lax.ppermute(last, 'ind', left if way else right)  12.8 us
    pallas_call x12, Pallas kernels, on_device(): pl.pallas_call(functools.partial(hop_kernel, ring, (w, peer[w][1]), low,...  6.57 us
    pallas_call x17, Pallas kernels, product(): pl.pallas_call(functools.partial(eta_kernel, ring, places, not eta), in_s...  6.08 us
    ppermute x2, starting transfers between devices, on_device(): got[1, piece] = lax.ppermute(sent[1], 'ind', left)  4.9 us
    ppermute x1, waiting for transfers between devices, on_device(): residual_other = lax.ppermute(mine, 'ind', swap)  3.93 us
  transfers between devices with their start and end apart: 38, of which 16 were waited for; matrix products, arithmetic and copies ran while one was open for 0% of the time, Pallas kernels for 18%

profile of v7, /device:TPU:0, one launch (start us, length us, event | category | flops | bytes accessed | tf_op | source)
XLA Modules:
  0.0 97.8 jit_solution(11832125254534750488)
XLA Ops:
  0.6 1.8 %pick_blocks.3 = (bf16[1,384,1024]{2,1,0:T(8,128)(2,1)S(1)}, bf16[2,384,1024]{2,1,0:T(8,128)(2,1)S(1)}) custom-call(bf16[384,16384]{1,0:T(8,128)(2,1)} %refs_1_.33), custom_call_target="tpu_custom_call" | custom-call | flops 2000000000 | bytes 1000000 | tf_op jit(solution)/shard_map/pick_blocks/pallas_call | solution.py:221
  3.5 3.9 %collective-permute-done.other_ref = bf16[384,256]{1,0:T(8,128)(2,1)S(1)} collective-permute-done((bf16[384,256]{1,0:T(8,128)(2,1)S(1)}, bf16[384,256]{1,0:T(8,128)(2,1)S(1)}, u32[]{:S(2)}, u32[]{:S(2)}) %collective-permute-start) | collective-permute-done | bytes 196640 | tf_op jit(solution)/shard_map/ppermute | solution.py:251
  8.2 2.9 %collective-permute-start.3 = (s16[528,128]{1,0:T(8,128)(2,1)S(1)}, s16[528,128]{1,0:T(8,128)(2,1)S(1)}, u32[]{:S(2)}, u32[]{:S(2)}) collective-permute-start(s16[528,128]{1,0:T(8,128)(2,1)S(1)} %get-tuple-element.70), channel_id=1, source_target_pairs={{0,2},{1,3},{4,0},{5,1},{8,4},{9,5},{12,8},{13,9},{14,12},{15,13},... | collective-permute-start | bytes 405512 | tf_op jit(solution)/shard_map/ppermute | solution.py:281
  11.7 2.0 %collective-permute-start.6 = (s16[528,128]{1,0:T(8,128)(2,1)S(1)}, s16[528,128]{1,0:T(8,128)(2,1)S(1)}, u32[]{:S(2)}, u32[]{:S(2)}) collective-permute-start(s16[528,128]{1,0:T(8,128)(2,1)S(1)} %get-tuple-element.72), channel_id=1, source_target_pairs={{0,2},{1,3},{4,0},{5,1},{8,4},{9,5},{12,8},{13,9},{14,12},{15,13},... | collective-permute-start | bytes 405512 | tf_op jit(solution)/shard_map/ppermute | solution.py:281
  14.0 1.5 %collective-permute-done.3.got_ref = s16[528,128]{1,0:T(8,128)(2,1)S(1)} collective-permute-done((s16[528,128]{1,0:T(8,128)(2,1)S(1)}, s16[528,128]{1,0:T(8,128)(2,1)S(1)}, u32[]{:S(2)}, u32[]{:S(2)}) %collective-permute-start.3) | collective-permute-done | bytes 135200 | tf_op jit(solution)/shard_map/ppermute | solution.py:281
  16.1 2.1 %collective-permute-start.8 = (s16[1040,128]{1,0:T(8,128)(2,1)S(1)}, s16[1040,128]{1,0:T(8,128)(2,1)S(1)}, u32[]{:S(2)}, u32[]{:S(2)}) collective-permute-start(s16[1040,128]{1,0:T(8,128)(2,1)S(1)} %sum_hop.12.before_ref), channel_id=1, source_target_pairs={{0,2},{1,3},{4,0},{5,1},{8,4},{9,5},{12,8},{13,9},{14,12},{15,13},... | collective-permute-start | bytes 798728 | tf_op jit(solution)/shard_map/ppermute | solution.py:298
  19.7 2.0 %collective-permute-start.10 = (s16[1040,128]{1,0:T(8,128)(2,1)S(1)}, s16[1040,128]{1,0:T(8,128)(2,1)S(1)}, u32[]{:S(2)}, u32[]{:S(2)}) collective-permute-start(s16[1040,128]{1,0:T(8,128)(2,1)S(1)} %sum_hop.14.before_ref), channel_id=1, source_target_pairs={{0,2},{1,3},{4,0},{5,1},{8,4},{9,5},{12,8},{13,9},{14,12},{15,13},... | collective-permute-start | bytes 798728 | tf_op jit(solution)/shard_map/ppermute | solution.py:298
  22.4 1.8 %collective-permute-done.8.got_ref = s16[1040,128]{1,0:T(8,128)(2,1)S(1)} collective-permute-done((s16[1040,128]{1,0:T(8,128)(2,1)S(1)}, s16[1040,128]{1,0:T(8,128)(2,1)S(1)}, u32[]{:S(2)}, u32[]{:S(2)}) %collective-permute-start.8) | collective-permute-done | bytes 266272 | tf_op jit(solution)/shard_map/ppermute | solution.py:298
  24.7 1.7 %collective-permute-start.13 = (s16[1040,128]{1,0:T(8,128)(2,1)S(1)}, s16[1040,128]{1,0:T(8,128)(2,1)S(1)}, u32[]{:S(2)}, u32[]{:S(2)}) collective-permute-start(s16[1040,128]{1,0:T(8,128)(2,1)S(1)} %sum_hop.16.before_ref), channel_id=1, source_target_pairs={{0,2},{1,3},{4,0},{5,1},{8,4},{9,5},{12,8},{13,9},{14,12},{15,13},... | collective-permute-start | bytes 798728 | tf_op jit(solution)/shard_map/ppermute | solution.py:298
  27.4 2.5 %collective-permute-done.10.got_ref = s16[1040,128]{1,0:T(8,128)(2,1)S(1)} collective-permute-done((s16[1040,128]{1,0:T(8,128)(2,1)S(1)}, s16[1040,128]{1,0:T(8,128)(2,1)S(1)}, u32[]{:S(2)}, u32[]{:S(2)}) %collective-permute-start.10) | collective-permute-done | bytes 266272 | tf_op jit(solution)/shard_map/ppermute | solution.py:298
  30.4 1.7 %collective-permute-start.15 = (s16[1040,128]{1,0:T(8,128)(2,1)S(1)}, s16[1040,128]{1,0:T(8,128)(2,1)S(1)}, u32[]{:S(2)}, u32[]{:S(2)}) collective-permute-start(s16[1040,128]{1,0:T(8,128)(2,1)S(1)} %sum_hop.18.before_ref), channel_id=1, source_target_pairs={{0,2},{1,3},{4,0},{5,1},{8,4},{9,5},{12,8},{13,9},{14,12},{15,13},... | collective-permute-start | bytes 798728 | tf_op jit(solution)/shard_map/ppermute | solution.py:298
  33.1 2.5 %collective-permute-done.13.got_ref = s16[1040,128]{1,0:T(8,128)(2,1)S(1)} collective-permute-done((s16[1040,128]{1,0:T(8,128)(2,1)S(1)}, s16[1040,128]{1,0:T(8,128)(2,1)S(1)}, u32[]{:S(2)}, u32[]{:S(2)}) %collective-permute-start.13) | collective-permute-done | bytes 266272 | tf_op jit(solution)/shard_map/ppermute | solution.py:298
  36.2 1.7 %collective-permute-start.18 = (s16[1040,128]{1,0:T(8,128)(2,1)S(1)}, s16[1040,128]{1,0:T(8,128)(2,1)S(1)}, u32[]{:S(2)}, u32[]{:S(2)}) collective-permute-start(s16[1040,128]{1,0:T(8,128)(2,1)S(1)} %sum_hop.20.before_ref), channel_id=1, source_target_pairs={{0,2},{1,3},{4,0},{5,1},{8,4},{9,5},{12,8},{13,9},{14,12},{15,13},... | collective-permute-start | bytes 798728 | tf_op jit(solution)/shard_map/ppermute | solution.py:298
  38.8 2.5 %collective-permute-done.15.got_ref = s16[1040,128]{1,0:T(8,128)(2,1)S(1)} collective-permute-done((s16[1040,128]{1,0:T(8,128)(2,1)S(1)}, s16[1040,128]{1,0:T(8,128)(2,1)S(1)}, u32[]{:S(2)}, u32[]{:S(2)}) %collective-permute-start.15) | collective-permute-done | bytes 266272 | tf_op jit(solution)/shard_map/ppermute | solution.py:298
  41.9 1.7 %collective-permute-start.20 = (s16[1040,128]{1,0:T(8,128)(2,1)S(1)}, s16[1040,128]{1,0:T(8,128)(2,1)S(1)}, u32[]{:S(2)}, u32[]{:S(2)}) collective-permute-start(s16[1040,128]{1,0:T(8,128)(2,1)S(1)} %sum_hop.22.before_ref), channel_id=1, source_target_pairs={{0,2},{1,3},{4,0},{5,1},{8,4},{9,5},{12,8},{13,9},{14,12},{15,13},... | collective-permute-start | bytes 798728 | tf_op jit(solution)/shard_map/ppermute | solution.py:298
  45.3 3.7 %collective-permute-done.17.right_ref = s16[1040,128]{1,0:T(8,128)(2,1)S(1)} collective-permute-done((s16[1040,128]{1,0:T(8,128)(2,1)S(1)}, s16[1040,128]{1,0:T(8,128)(2,1)S(1)}, u32[]{:S(2)}, u32[]{:S(2)}) %collective-permute-start.17) | collective-permute-done | bytes 266272 | tf_op jit(solution)/shard_map/ppermute | solution.py:298
  50.4 1.6 %collective-permute-start.21 = (bf16[512,256]{1,0:T(8,128)(2,1)S(1)}, bf16[512,256]{1,0:T(8,128)(2,1)S(1)}, u32[]{:S(2)}, u32[]{:S(2)}) collective-permute-start(bf16[512,256]{1,0:T(8,128)(2,1)S(1)} %get-tuple-element.73.before_ref.refs_0_), channel_id=1, source_target_pairs={{0,2},{1,3},{4,0},{5,1},{8,4},{9,5},{12,8},{13,9},{14,12},{15,13},... | collective-permute-start | bytes 786440 | tf_op jit(solution)/shard_map/ppermute | solution.py:372
  52.4 2.3 %collective-permute-done.19.right_ref = s16[1040,128]{1,0:T(8,128)(2,1)S(1)} collective-permute-done((s16[1040,128]{1,0:T(8,128)(2,1)S(1)}, s16[1040,128]{1,0:T(8,128)(2,1)S(1)}, u32[]{:S(2)}, u32[]{:S(2)}) %collective-permute-start.19) | collective-permute-done | bytes 266272 | tf_op jit(solution)/shard_map/ppermute | solution.py:298
  56.1 1.6 %collective-permute-start.23 = (bf16[512,256]{1,0:T(8,128)(2,1)S(1)}, bf16[512,256]{1,0:T(8,128)(2,1)S(1)}, u32[]{:S(2)}, u32[]{:S(2)}) collective-permute-start(bf16[512,256]{1,0:T(8,128)(2,1)S(1)} %get-tuple-element.78.before_ref.refs_3_), channel_id=1, source_target_pairs={{0,2},{1,3},{4,0},{5,1},{8,4},{9,5},{12,8},{13,9},{14,12},{15,13},... | collective-permute-start | bytes 786440 | tf_op jit(solution)/shard_map/ppermute | solution.py:372
  58.7 1.6 %collective-permute-start.25 = (bf16[512,256]{1,0:T(8,128)(2,1)S(1)}, bf16[512,256]{1,0:T(8,128)(2,1)S(1)}, u32[]{:S(2)}, u32[]{:S(2)}) collective-permute-start(bf16[512,256]{1,0:T(8,128)(2,1)S(1)} %collective-permute-done.21.refs_0_), channel_id=1, source_target_pairs={{0,2},{1,3},{4,0},{5,1},{8,4},{9,5},{12,8},{13,9},{14,12},{15,13},... | collective-permute-start | bytes 786440 | tf_op jit(solution)/shard_map/ppermute | solution.py:372
  61.6 3.7 %collective-permute-done.23.refs_0_ = bf16[512,256]{1,0:T(8,128)(2,1)S(1)} collective-permute-done((bf16[512,256]{1,0:T(8,128)(2,1)S(1)}, bf16[512,256]{1,0:T(8,128)(2,1)S(1)}, u32[]{:S(2)}, u32[]{:S(2)}) %collective-permute-start.23) | collective-permute-done | bytes 262176 | tf_op jit(solution)/shard_map/ppermute | solution.py:372
  65.3 1.6 %collective-permute-start.27 = (bf16[512,256]{1,0:T(8,128)(2,1)S(1)}, bf16[512,256]{1,0:T(8,128)(2,1)S(1)}, u32[]{:S(2)}, u32[]{:S(2)}) collective-permute-start(bf16[512,256]{1,0:T(8,128)(2,1)S(1)} %collective-permute-done.23.refs_0_), channel_id=1, source_target_pairs={{0,2},{1,3},{4,0},{5,1},{8,4},{9,5},{12,8},{13,9},{14,12},{15,13},... | collective-permute-start | bytes 786440 | tf_op jit(solution)/shard_map/ppermute | solution.py:372
  68.2 2.8 %collective-permute-done.25.refs_0_ = bf16[512,256]{1,0:T(8,128)(2,1)S(1)} collective-permute-done((bf16[512,256]{1,0:T(8,128)(2,1)S(1)}, bf16[512,256]{1,0:T(8,128)(2,1)S(1)}, u32[]{:S(2)}, u32[]{:S(2)}) %collective-permute-start.25) | collective-permute-done | bytes 262176 | tf_op jit(solution)/shard_map/ppermute | solution.py:372
  70.9 1.6 %collective-permute-start.29 = (bf16[512,256]{1,0:T(8,128)(2,1)S(1)}, bf16[512,256]{1,0:T(8,128)(2,1)S(1)}, u32[]{:S(2)}, u32[]{:S(2)}) collective-permute-start(bf16[512,256]{1,0:T(8,128)(2,1)S(1)} %collective-permute-done.25.refs_0_), channel_id=1, source_target_pairs={{0,2},{1,3},{4,0},{5,1},{8,4},{9,5},{12,8},{13,9},{14,12},{15,13},... | collective-permute-start | bytes 786440 | tf_op jit(solution)/shard_map/ppermute | solution.py:372
  73.8 2.8 %collective-permute-done.27.refs_0_ = bf16[512,256]{1,0:T(8,128)(2,1)S(1)} collective-permute-done((bf16[512,256]{1,0:T(8,128)(2,1)S(1)}, bf16[512,256]{1,0:T(8,128)(2,1)S(1)}, u32[]{:S(2)}, u32[]{:S(2)}) %collective-permute-start.27) | collective-permute-done | bytes 262176 | tf_op jit(solution)/shard_map/ppermute | solution.py:372
  76.6 1.6 %collective-permute-start.31 = (bf16[512,256]{1,0:T(8,128)(2,1)S(1)}, bf16[512,256]{1,0:T(8,128)(2,1)S(1)}, u32[]{:S(2)}, u32[]{:S(2)}) collective-permute-start(bf16[512,256]{1,0:T(8,128)(2,1)S(1)} %collective-permute-done.27.refs_0_), channel_id=1, source_target_pairs={{0,2},{1,3},{4,0},{5,1},{8,4},{9,5},{12,8},{13,9},{14,12},{15,13},... | collective-permute-start | bytes 786440 | tf_op jit(solution)/shard_map/ppermute | solution.py:372
  79.4 2.8 %collective-permute-done.29.refs_0_ = bf16[512,256]{1,0:T(8,128)(2,1)S(1)} collective-permute-done((bf16[512,256]{1,0:T(8,128)(2,1)S(1)}, bf16[512,256]{1,0:T(8,128)(2,1)S(1)}, u32[]{:S(2)}, u32[]{:S(2)}) %collective-permute-start.29) | collective-permute-done | bytes 262176 | tf_op jit(solution)/shard_map/ppermute | solution.py:372
  82.2 1.6 %collective-permute-start.33 = (bf16[256,256]{1,0:T(8,128)(2,1)S(1)}, bf16[256,256]{1,0:T(8,128)(2,1)S(1)}, u32[]{:S(2)}, u32[]{:S(2)}) collective-permute-start(bf16[256,256]{1,0:T(8,128)(2,1)S(1)} %slice.12), channel_id=1, source_target_pairs={{0,2},{1,3},{4,0},{5,1},{8,4},{9,5},{12,8},{13,9},{14,12},{15,13},... | collective-permute-start | bytes 393224 | tf_op jit(solution)/shard_map/ppermute | solution.py:372
  85.1 2.2 %collective-permute-done.31.refs_0_ = bf16[512,256]{1,0:T(8,128)(2,1)S(1)} collective-permute-done((bf16[512,256]{1,0:T(8,128)(2,1)S(1)}, bf16[512,256]{1,0:T(8,128)(2,1)S(1)}, u32[]{:S(2)}, u32[]{:S(2)}) %collective-permute-start.31) | collective-permute-done | bytes 262176 | tf_op jit(solution)/shard_map/ppermute | solution.py:372
  87.3 2.1 %collective-permute-start.35 = (bf16[256,256]{1,0:T(8,128)(2,1)S(1)}, bf16[256,256]{1,0:T(8,128)(2,1)S(1)}, u32[]{:S(2)}, u32[]{:S(2)}) collective-permute-start(bf16[256,256]{1,0:T(8,128)(2,1)S(1)} %slice.14), channel_id=1, source_target_pairs={{0,2},{1,3},{4,0},{5,1},{8,4},{9,5},{12,8},{13,9},{14,12},{15,13},... | collective-permute-start | bytes 393224 | tf_op jit(solution)/shard_map/ppermute | solution.py:372
  92.7 2.2 %collective-permute-done.36.refs_0_ = bf16[256,256]{1,0:T(8,128)(2,1)S(1)} collective-permute-done((bf16[256,256]{1,0:T(8,128)(2,1)S(1)}, bf16[256,256]{1,0:T(8,128)(2,1)S(1)}, u32[]{:S(2)}, u32[]{:S(2)}) %collective-permute-start.36) | collective-permute-done | bytes 131104 | tf_op jit(solution)/shard_map/ppermute | solution.py:372
  95.2 1.7 %collective-permute-done.37.got_ref = f32[384,256]{1,0:T(8,128)S(1)} collective-permute-done((f32[384,256]{1,0:T(8,128)S(1)}, f32[384,256]{1,0:T(8,128)S(1)}, u32[]{:S(2)}, u32[]{:S(2)}) %collective-permute-start.37) | collective-permute-done | bytes 393248 | tf_op jit(solution)/shard_map/ppermute | solution.py:377
  (107 shorter events, 26.8 us)
Async XLA Ops:
  3.0 8.2 %collective-permute-start.2 = (bf16[2,384,1024]{2,1,0:T(8,128)(2,1)S(1)}, bf16[2,384,1024]{2,1,0:T(8,128)(2,1)S(1)}, u32[]{:S(2)}, u32[]{:S(2)}) collective-permute-start(bf16[2,384,1024]{2,1,0:T(8,128)(2,1)S(1)} %get-tuple-element.67), channel_id=1, source_target_pairs={{0,1},{1,0},{2,3},{3,2},{4,5},{5,4},{6,7},{7,6},{8,9},{9,8},{10,11... | collective-permute-start | bytes 4718600 | tf_op jit(solution)/shard_map/ppermute | solution.py:242
  8.2 7.4 %collective-permute-start.3 = (s16[528,128]{1,0:T(8,128)(2,1)S(1)}, s16[528,128]{1,0:T(8,128)(2,1)S(1)}, u32[]{:S(2)}, u32[]{:S(2)}) collective-permute-start(s16[528,128]{1,0:T(8,128)(2,1)S(1)} %get-tuple-element.70), channel_id=1, source_target_pairs={{0,2},{1,3},{4,0},{5,1},{8,4},{9,5},{12,8},{13,9},{14,12},{15,13},... | collective-permute-start | bytes 405512 | tf_op jit(solution)/shard_map/ppermute | solution.py:281
  11.1 7.0 %collective-permute-start.4 = (s16[528,128]{1,0:T(8,128)(2,1)S(1)}, s16[528,128]{1,0:T(8,128)(2,1)S(1)}, u32[]{:S(2)}, u32[]{:S(2)}) collective-permute-start(s16[528,128]{1,0:T(8,128)(2,1)S(1)} %get-tuple-element.68.before_ref), channel_id=1, source_target_pairs={{0,4},{1,5},{4,8},{5,9},{8,12},{9,13},{12,14},{13,15},{14,10},{15,... | collective-permute-start | bytes 405512 | tf_op jit(solution)/shard_map/ppermute | solution.py:280
  11.7 7.4 %collective-permute-start.6 = (s16[528,128]{1,0:T(8,128)(2,1)S(1)}, s16[528,128]{1,0:T(8,128)(2,1)S(1)}, u32[]{:S(2)}, u32[]{:S(2)}) collective-permute-start(s16[528,128]{1,0:T(8,128)(2,1)S(1)} %get-tuple-element.72), channel_id=1, source_target_pairs={{0,2},{1,3},{4,0},{5,1},{8,4},{9,5},{12,8},{13,9},{14,12},{15,13},... | collective-permute-start | bytes 405512 | tf_op jit(solution)/shard_map/ppermute | solution.py:281
  13.7 8.0 %collective-permute-start.7 = (s16[528,128]{1,0:T(8,128)(2,1)S(1)}, s16[528,128]{1,0:T(8,128)(2,1)S(1)}, u32[]{:S(2)}, u32[]{:S(2)}) collective-permute-start(s16[528,128]{1,0:T(8,128)(2,1)S(1)} %get-tuple-element.69.refs_0_), channel_id=1, source_target_pairs={{0,4},{1,5},{4,8},{5,9},{8,12},{9,13},{12,14},{13,15},{14,10},{15,... | collective-permute-start | bytes 405512 | tf_op jit(solution)/shard_map/ppermute | solution.py:280
  16.1 8.1 %collective-permute-start.8 = (s16[1040,128]{1,0:T(8,128)(2,1)S(1)}, s16[1040,128]{1,0:T(8,128)(2,1)S(1)}, u32[]{:S(2)}, u32[]{:S(2)}) collective-permute-start(s16[1040,128]{1,0:T(8,128)(2,1)S(1)} %sum_hop.12.before_ref), channel_id=1, source_target_pairs={{0,2},{1,3},{4,0},{5,1},{8,4},{9,5},{12,8},{13,9},{14,12},{15,13},... | collective-permute-start | bytes 798728 | tf_op jit(solution)/shard_map/ppermute | solution.py:298
  18.7 7.8 %collective-permute-start.9 = (s16[1040,128]{1,0:T(8,128)(2,1)S(1)}, s16[1040,128]{1,0:T(8,128)(2,1)S(1)}, u32[]{:S(2)}, u32[]{:S(2)}) collective-permute-start(s16[1040,128]{1,0:T(8,128)(2,1)S(1)} %sum_hop.13.refs_0_), channel_id=1, source_target_pairs={{0,4},{1,5},{4,8},{5,9},{8,12},{9,13},{12,14},{13,15},{14,10},{15,... | collective-permute-start | bytes 798728 | tf_op jit(solution)/shard_map/ppermute | solution.py:298
  19.0 16.6 %collective-permute-start.12 = (bf16[3,384,1024]{2,1,0:T(8,128)(2,1)S(1)}, bf16[3,384,1024]{2,1,0:T(8,128)(2,1)S(1)}, u32[]{:S(2)}, u32[]{:S(2)}) collective-permute-start(bf16[3,384,1024]{2,1,0:T(8,128)(2,1)S(1)} %pick_blocks.5.before_ref), channel_id=1, source_target_pairs={{0,1},{1,0},{2,3},{3,2},{4,5},{5,4},{6,7},{7,6},{8,9},{9,8},{10,11... | collective-permute-start | bytes 7077896 | tf_op jit(solution)/shard_map/ppermute | solution.py:242
  19.7 10.2 %collective-permute-start.10 = (s16[1040,128]{1,0:T(8,128)(2,1)S(1)}, s16[1040,128]{1,0:T(8,128)(2,1)S(1)}, u32[]{:S(2)}, u32[]{:S(2)}) collective-permute-start(s16[1040,128]{1,0:T(8,128)(2,1)S(1)} %sum_hop.14.before_ref), channel_id=1, source_target_pairs={{0,2},{1,3},{4,0},{5,1},{8,4},{9,5},{12,8},{13,9},{14,12},{15,13},... | collective-permute-start | bytes 798728 | tf_op jit(solution)/shard_map/ppermute | solution.py:298
  22.2 10.0 %collective-permute-start.11 = (s16[1040,128]{1,0:T(8,128)(2,1)S(1)}, s16[1040,128]{1,0:T(8,128)(2,1)S(1)}, u32[]{:S(2)}, u32[]{:S(2)}) collective-permute-start(s16[1040,128]{1,0:T(8,128)(2,1)S(1)} %sum_hop.15.before_ref), channel_id=1, source_target_pairs={{0,4},{1,5},{4,8},{5,9},{8,12},{9,13},{12,14},{13,15},{14,10},{15,... | collective-permute-start | bytes 798728 | tf_op jit(solution)/shard_map/ppermute | solution.py:298
  24.7 10.9 %collective-permute-start.13 = (s16[1040,128]{1,0:T(8,128)(2,1)S(1)}, s16[1040,128]{1,0:T(8,128)(2,1)S(1)}, u32[]{:S(2)}, u32[]{:S(2)}) collective-permute-start(s16[1040,128]{1,0:T(8,128)(2,1)S(1)} %sum_hop.16.before_ref), channel_id=1, source_target_pairs={{0,2},{1,3},{4,0},{5,1},{8,4},{9,5},{12,8},{13,9},{14,12},{15,13},... | collective-permute-start | bytes 798728 | tf_op jit(solution)/shard_map/ppermute | solution.py:298
  27.0 10.9 %collective-permute-start.14 = (s16[1040,128]{1,0:T(8,128)(2,1)S(1)}, s16[1040,128]{1,0:T(8,128)(2,1)S(1)}, u32[]{:S(2)}, u32[]{:S(2)}) collective-permute-start(s16[1040,128]{1,0:T(8,128)(2,1)S(1)} %sum_hop.17.before_ref), channel_id=1, source_target_pairs={{0,4},{1,5},{4,8},{5,9},{8,12},{9,13},{12,14},{13,15},{14,10},{15,... | collective-permute-start | bytes 798728 | tf_op jit(solution)/shard_map/ppermute | solution.py:298
  30.4 10.9 %collective-permute-start.15 = (s16[1040,128]{1,0:T(8,128)(2,1)S(1)}, s16[1040,128]{1,0:T(8,128)(2,1)S(1)}, u32[]{:S(2)}, u32[]{:S(2)}) collective-permute-start(s16[1040,128]{1,0:T(8,128)(2,1)S(1)} %sum_hop.18.before_ref), channel_id=1, source_target_pairs={{0,2},{1,3},{4,0},{5,1},{8,4},{9,5},{12,8},{13,9},{14,12},{15,13},... | collective-permute-start | bytes 798728 | tf_op jit(solution)/shard_map/ppermute | solution.py:298
  32.7 10.9 %collective-permute-start.16 = (s16[1040,128]{1,0:T(8,128)(2,1)S(1)}, s16[1040,128]{1,0:T(8,128)(2,1)S(1)}, u32[]{:S(2)}, u32[]{:S(2)}) collective-permute-start(s16[1040,128]{1,0:T(8,128)(2,1)S(1)} %sum_hop.19.before_ref), channel_id=1, source_target_pairs={{0,4},{1,5},{4,8},{5,9},{8,12},{9,13},{12,14},{13,15},{14,10},{15,... | collective-permute-start | bytes 798728 | tf_op jit(solution)/shard_map/ppermute | solution.py:298
  36.2 12.9 %collective-permute-start.18 = (s16[1040,128]{1,0:T(8,128)(2,1)S(1)}, s16[1040,128]{1,0:T(8,128)(2,1)S(1)}, u32[]{:S(2)}, u32[]{:S(2)}) collective-permute-start(s16[1040,128]{1,0:T(8,128)(2,1)S(1)} %sum_hop.20.before_ref), channel_id=1, source_target_pairs={{0,2},{1,3},{4,0},{5,1},{8,4},{9,5},{12,8},{13,9},{14,12},{15,13},... | collective-permute-start | bytes 798728 | tf_op jit(solution)/shard_map/ppermute | solution.py:298
  38.5 10.6 %collective-permute-start.17 = (s16[1040,128]{1,0:T(8,128)(2,1)S(1)}, s16[1040,128]{1,0:T(8,128)(2,1)S(1)}, u32[]{:S(2)}, u32[]{:S(2)}) collective-permute-start(s16[1040,128]{1,0:T(8,128)(2,1)S(1)} %sum_hop.21.before_ref), channel_id=1, source_target_pairs={{0,4},{1,5},{4,8},{5,9},{8,12},{9,13},{12,14},{13,15},{14,10},{15,... | collective-permute-start | bytes 798728 | tf_op jit(solution)/shard_map/ppermute | solution.py:298
  41.9 12.9 %collective-permute-start.20 = (s16[1040,128]{1,0:T(8,128)(2,1)S(1)}, s16[1040,128]{1,0:T(8,128)(2,1)S(1)}, u32[]{:S(2)}, u32[]{:S(2)}) collective-permute-start(s16[1040,128]{1,0:T(8,128)(2,1)S(1)} %sum_hop.22.before_ref), channel_id=1, source_target_pairs={{0,2},{1,3},{4,0},{5,1},{8,4},{9,5},{12,8},{13,9},{14,12},{15,13},... | collective-permute-start | bytes 798728 | tf_op jit(solution)/shard_map/ppermute | solution.py:298
  44.2 10.5 %collective-permute-start.19 = (s16[1040,128]{1,0:T(8,128)(2,1)S(1)}, s16[1040,128]{1,0:T(8,128)(2,1)S(1)}, u32[]{:S(2)}, u32[]{:S(2)}) collective-permute-start(s16[1040,128]{1,0:T(8,128)(2,1)S(1)} %sum_hop.23.before_ref), channel_id=1, source_target_pairs={{0,4},{1,5},{4,8},{5,9},{8,12},{9,13},{12,14},{13,15},{14,10},{15,... | collective-permute-start | bytes 798728 | tf_op jit(solution)/shard_map/ppermute | solution.py:298
  50.4 8.3 %collective-permute-start.21 = (bf16[512,256]{1,0:T(8,128)(2,1)S(1)}, bf16[512,256]{1,0:T(8,128)(2,1)S(1)}, u32[]{:S(2)}, u32[]{:S(2)}) collective-permute-start(bf16[512,256]{1,0:T(8,128)(2,1)S(1)} %get-tuple-element.73.before_ref.refs_0_), channel_id=1, source_target_pairs={{0,2},{1,3},{4,0},{5,1},{8,4},{9,5},{12,8},{13,9},{14,12},{15,13},... | collective-permute-start | bytes 786440 | tf_op jit(solution)/shard_map/ppermute | solution.py:372
  52.0 8.7 %collective-permute-start.22 = (bf16[512,256]{1,0:T(8,128)(2,1)S(1)}, bf16[512,256]{1,0:T(8,128)(2,1)S(1)}, u32[]{:S(2)}, u32[]{:S(2)}) collective-permute-start(bf16[512,256]{1,0:T(8,128)(2,1)S(1)} %get-tuple-element.73.before_ref.refs_0_), channel_id=1, source_target_pairs={{0,4},{1,5},{4,8},{5,9},{8,12},{9,13},{12,14},{13,15},{14,10},{15,... | collective-permute-start | bytes 786440 | tf_op jit(solution)/shard_map/ppermute | solution.py:372
  56.1 9.2 %collective-permute-start.23 = (bf16[512,256]{1,0:T(8,128)(2,1)S(1)}, bf16[512,256]{1,0:T(8,128)(2,1)S(1)}, u32[]{:S(2)}, u32[]{:S(2)}) collective-permute-start(bf16[512,256]{1,0:T(8,128)(2,1)S(1)} %get-tuple-element.78.before_ref.refs_3_), channel_id=1, source_target_pairs={{0,2},{1,3},{4,0},{5,1},{8,4},{9,5},{12,8},{13,9},{14,12},{15,13},... | collective-permute-start | bytes 786440 | tf_op jit(solution)/shard_map/ppermute | solution.py:372
  57.7 9.6 %collective-permute-start.24 = (bf16[512,256]{1,0:T(8,128)(2,1)S(1)}, bf16[512,256]{1,0:T(8,128)(2,1)S(1)}, u32[]{:S(2)}, u32[]{:S(2)}) collective-permute-start(bf16[512,256]{1,0:T(8,128)(2,1)S(1)} %get-tuple-element.78.before_ref.refs_3_), channel_id=1, source_target_pairs={{0,4},{1,5},{4,8},{5,9},{8,12},{9,13},{12,14},{13,15},{14,10},{15,... | collective-permute-start | bytes 786440 | tf_op jit(solution)/shard_map/ppermute | solution.py:372
  58.7 12.2 %collective-permute-start.25 = (bf16[512,256]{1,0:T(8,128)(2,1)S(1)}, bf16[512,256]{1,0:T(8,128)(2,1)S(1)}, u32[]{:S(2)}, u32[]{:S(2)}) collective-permute-start(bf16[512,256]{1,0:T(8,128)(2,1)S(1)} %collective-permute-done.21.refs_0_), channel_id=1, source_target_pairs={{0,2},{1,3},{4,0},{5,1},{8,4},{9,5},{12,8},{13,9},{14,12},{15,13},... | collective-permute-start | bytes 786440 | tf_op jit(solution)/shard_map/ppermute | solution.py:372
  60.7 12.2 %collective-permute-start.26 = (bf16[512,256]{1,0:T(8,128)(2,1)S(1)}, bf16[512,256]{1,0:T(8,128)(2,1)S(1)}, u32[]{:S(2)}, u32[]{:S(2)}) collective-permute-start(bf16[512,256]{1,0:T(8,128)(2,1)S(1)} %collective-permute-done.22.refs_0_), channel_id=1, source_target_pairs={{0,4},{1,5},{4,8},{5,9},{8,12},{9,13},{12,14},{13,15},{14,10},{15,... | collective-permute-start | bytes 786440 | tf_op jit(solution)/shard_map/ppermute | solution.py:372
  65.3 11.2 %collective-permute-start.27 = (bf16[512,256]{1,0:T(8,128)(2,1)S(1)}, bf16[512,256]{1,0:T(8,128)(2,1)S(1)}, u32[]{:S(2)}, u32[]{:S(2)}) collective-permute-start(bf16[512,256]{1,0:T(8,128)(2,1)S(1)} %collective-permute-done.23.refs_0_), channel_id=1, source_target_pairs={{0,2},{1,3},{4,0},{5,1},{8,4},{9,5},{12,8},{13,9},{14,12},{15,13},... | collective-permute-start | bytes 786440 | tf_op jit(solution)/shard_map/ppermute | solution.py:372
  67.3 11.2 %collective-permute-start.28 = (bf16[512,256]{1,0:T(8,128)(2,1)S(1)}, bf16[512,256]{1,0:T(8,128)(2,1)S(1)}, u32[]{:S(2)}, u32[]{:S(2)}) collective-permute-start(bf16[512,256]{1,0:T(8,128)(2,1)S(1)} %collective-permute-done.24.refs_0_), channel_id=1, source_target_pairs={{0,4},{1,5},{4,8},{5,9},{8,12},{9,13},{12,14},{13,15},{14,10},{15,... | collective-permute-start | bytes 786440 | tf_op jit(solution)/shard_map/ppermute | solution.py:372
  70.9 11.2 %collective-permute-start.29 = (bf16[512,256]{1,0:T(8,128)(2,1)S(1)}, bf16[512,256]{1,0:T(8,128)(2,1)S(1)}, u32[]{:S(2)}, u32[]{:S(2)}) collective-permute-start(bf16[512,256]{1,0:T(8,128)(2,1)S(1)} %collective-permute-done.25.refs_0_), channel_id=1, source_target_pairs={{0,2},{1,3},{4,0},{5,1},{8,4},{9,5},{12,8},{13,9},{14,12},{15,13},... | collective-permute-start | bytes 786440 | tf_op jit(solution)/shard_map/ppermute | solution.py:372
  72.9 11.3 %collective-permute-start.30 = (bf16[512,256]{1,0:T(8,128)(2,1)S(1)}, bf16[512,256]{1,0:T(8,128)(2,1)S(1)}, u32[]{:S(2)}, u32[]{:S(2)}) collective-permute-start(bf16[512,256]{1,0:T(8,128)(2,1)S(1)} %collective-permute-done.26.refs_0_), channel_id=1, source_target_pairs={{0,4},{1,5},{4,8},{5,9},{8,12},{9,13},{12,14},{13,15},{14,10},{15,... | collective-permute-start | bytes 786440 | tf_op jit(solution)/shard_map/ppermute | solution.py:372
  76.6 10.7 %collective-permute-start.31 = (bf16[512,256]{1,0:T(8,128)(2,1)S(1)}, bf16[512,256]{1,0:T(8,128)(2,1)S(1)}, u32[]{:S(2)}, u32[]{:S(2)}) collective-permute-start(bf16[512,256]{1,0:T(8,128)(2,1)S(1)} %collective-permute-done.27.refs_0_), channel_id=1, source_target_pairs={{0,2},{1,3},{4,0},{5,1},{8,4},{9,5},{12,8},{13,9},{14,12},{15,13},... | collective-permute-start | bytes 786440 | tf_op jit(solution)/shard_map/ppermute | solution.py:372
  78.5 11.3 %collective-permute-start.32 = (bf16[512,256]{1,0:T(8,128)(2,1)S(1)}, bf16[512,256]{1,0:T(8,128)(2,1)S(1)}, u32[]{:S(2)}, u32[]{:S(2)}) collective-permute-start(bf16[512,256]{1,0:T(8,128)(2,1)S(1)} %collective-permute-done.28.refs_0_), channel_id=1, source_target_pairs={{0,4},{1,5},{4,8},{5,9},{8,12},{9,13},{12,14},{13,15},{14,10},{15,... | collective-permute-start | bytes 786440 | tf_op jit(solution)/shard_map/ppermute | solution.py:372
  82.2 8.1 %collective-permute-start.33 = (bf16[256,256]{1,0:T(8,128)(2,1)S(1)}, bf16[256,256]{1,0:T(8,128)(2,1)S(1)}, u32[]{:S(2)}, u32[]{:S(2)}) collective-permute-start(bf16[256,256]{1,0:T(8,128)(2,1)S(1)} %slice.12), channel_id=1, source_target_pairs={{0,2},{1,3},{4,0},{5,1},{8,4},{9,5},{12,8},{13,9},{14,12},{15,13},... | collective-permute-start | bytes 393224 | tf_op jit(solution)/shard_map/ppermute | solution.py:372
  84.2 7.9 %collective-permute-start.34 = (bf16[256,256]{1,0:T(8,128)(2,1)S(1)}, bf16[256,256]{1,0:T(8,128)(2,1)S(1)}, u32[]{:S(2)}, u32[]{:S(2)}) collective-permute-start(bf16[256,256]{1,0:T(8,128)(2,1)S(1)} %slice.13), channel_id=1, source_target_pairs={{0,4},{1,5},{4,8},{5,9},{8,12},{9,13},{12,14},{13,15},{14,10},{15,... | collective-permute-start | bytes 393224 | tf_op jit(solution)/shard_map/ppermute | solution.py:372
  (16 other events, 64.2 us)

commit v8 on v7

--- a/solution.py
+++ b/solution.py
@@ -242,13 +242,10 @@
         got = lax.ppermute(sent, "ind", swap)
         peer.update({d: (got, k) for k, d in enumerate(distances)})
 
-    first, later = [b for b in (order[:1], order[1:3]) if b], [b for b in (order[3:5], order[5:]) if b]
-    sent = pick(first, pltpu.HBM, light)
-    last = sent[0]
-    for distances, array in zip(first, sent):
-        swapped(distances, array)
-    mine, _ = lax.optimization_barrier((residual, last))
-    residual_other = lax.ppermute(mine, "ind", swap)
+    later = [b for b in (order[3:5], order[5:]) if b]
+    residual_other = lax.ppermute(residual, "ind", swap)
+    (last,) = pick([order[:1]], pltpu.HBM, light)
+    swapped(order[:1], last)
     res = last = pl.pallas_call(
         flip_kernel,
         in_specs=after(last, (residual, residual_other)),
@@ -257,6 +254,10 @@
         cost_estimate=light,
         name="flip",
     )(last, residual, residual_other)
+
+    if order[1:3]:
+        (last,) = pick([order[1:3]], pltpu.VMEM, light, last)
+        swapped(order[1:3], last)
 
     def shape_of(width):
         return jax.ShapeDtypeStruct((width // LANES * cols + PAD, LANES), jnp.int16)

time: 97.9 us -> 97.6 us (level)
  waiting for transfers between devices: 39.6 us -> 35.8 us
  local copies, waits for them, and re-layouts: 0.82 us -> 4.07 us
    ppermute x1, waiting for transfers between devices: 3.93 us -> 0.01 us  [on_device(): residual_other = lax.ppermute(residual, 'ind', swap)]
    unnamed x20, local copies, waits for them, and re-layouts: 0.78 us -> 4.03 us
    ppermute x12, waiting for transfers between devices: 15.3 us -> 16.8 us  [on_device(): got[way, piece] = lax.ppermute(last, 'ind', left if way else right)]
    ppermute x2, waiting for transfers between devices: 1.49 us -> 0.4 us  [on_device(): got[1, piece] = lax.ppermute(sent[1], 'ind', left)]
    pallas_call x3 -> x4, Pallas kernels: 2.13 us -> 1.73 us  [pick(): pl.pallas_call(functools.partial(pick_kernel, ring, wanted, block), in_sp...]
  transfers between devices with their start and end apart: 38 -> 38, of which waited for: 16 -> 15; matrix products, arithmetic and copies ran while one was open for 0% -> 0% of each run, Pallas kernels for 18% -> 19%
where the time goes in v8:
time: 97.6 us; the launch traced here: 97.4 us
  starting transfers between devices  36.6 us (38%)
  waiting for transfers between devices  35.8 us (37%)
  Pallas kernels  19.8 us (20%)
  local copies, waits for them, and re-layouts  4.07 us (4%)
  between operations  1.15 us (1%)
    ppermute x16, starting transfers between devices, on_device(): held[way, piece] = lax.ppermute(message, 'ind', left if way else right)  17.1 us
    ppermute x16, waiting for transfers between devices, on_device(): held[way, piece] = lax.ppermute(message, 'ind', left if way else right)  16.9 us
    ppermute x12, waiting for transfers between devices, on_device(): got[way, piece] = lax.ppermute(last, 'ind', left if way else right)  16.8 us
    ppermute x12, starting transfers between devices, on_device(): got[way, piece] = lax.ppermute(last, 'ind', left if way else right)  12.8 us
    pallas_call x12, Pallas kernels, on_device(): pl.pallas_call(functools.partial(hop_kernel, ring, (w, peer[w][1]), low,...  6.58 us
    pallas_call x17, Pallas kernels, product(): pl.pallas_call(functools.partial(eta_kernel, ring, places, not eta), in_s...  6.06 us
    ppermute x2, starting transfers between devices, on_device(): got[1, piece] = lax.ppermute(sent[1], 'ind', left)  5.4 us
    unnamed x20, local copies, waits for them, and re-layouts  4.03 us
  transfers between devices with their start and end apart: 38, of which 15 were waited for; matrix products, arithmetic and copies ran while one was open for 0% of the time, Pallas kernels for 19%

profile of v8, /device:TPU:0, one launch (start us, length us, event | category | flops | bytes accessed | tf_op | source)
XLA Modules:
  0.0 97.4 jit_solution(6411944457992713684)
XLA Ops:
  2.7 3.3 %copy-done = bf16[384,16384]{1,0:T(8,128)(2,1)S(1)} copy-done((bf16[384,16384]{1,0:T(8,128)(2,1)S(1)}, bf16[384,16384]{1,0:T(8,128)(2,1)}, u32[]{:S(2)}) %copy-start) | copy-done | bytes 12582936
  6.8 3.0 %collective-permute-start.3 = (s16[528,128]{1,0:T(8,128)(2,1)S(1)}, s16[528,128]{1,0:T(8,128)(2,1)S(1)}, u32[]{:S(2)}, u32[]{:S(2)}) collective-permute-start(s16[528,128]{1,0:T(8,128)(2,1)S(1)} %get-tuple-element.64), channel_id=1, source_target_pairs={{0,2},{1,3},{4,0},{5,1},{8,4},{9,5},{12,8},{13,9},{14,12},{15,13},... | collective-permute-start | bytes 405512 | tf_op jit(solution)/shard_map/ppermute | solution.py:282
  10.5 2.4 %collective-permute-start.6 = (s16[528,128]{1,0:T(8,128)(2,1)S(1)}, s16[528,128]{1,0:T(8,128)(2,1)S(1)}, u32[]{:S(2)}, u32[]{:S(2)}) collective-permute-start(s16[528,128]{1,0:T(8,128)(2,1)S(1)} %get-tuple-element.66), channel_id=1, source_target_pairs={{0,2},{1,3},{4,0},{5,1},{8,4},{9,5},{12,8},{13,9},{14,12},{15,13},... | collective-permute-start | bytes 405512 | tf_op jit(solution)/shard_map/ppermute | solution.py:282
  14.2 1.7 %collective-permute-start.8 = (s16[1040,128]{1,0:T(8,128)(2,1)S(1)}, s16[1040,128]{1,0:T(8,128)(2,1)S(1)}, u32[]{:S(2)}, u32[]{:S(2)}) collective-permute-start(s16[1040,128]{1,0:T(8,128)(2,1)S(1)} %sum_hop.12.before_ref), channel_id=1, source_target_pairs={{0,2},{1,3},{4,0},{5,1},{8,4},{9,5},{12,8},{13,9},{14,12},{15,13},... | collective-permute-start | bytes 798728 | tf_op jit(solution)/shard_map/ppermute | solution.py:299
  17.7 1.7 %collective-permute-start.10 = (s16[1040,128]{1,0:T(8,128)(2,1)S(1)}, s16[1040,128]{1,0:T(8,128)(2,1)S(1)}, u32[]{:S(2)}, u32[]{:S(2)}) collective-permute-start(s16[1040,128]{1,0:T(8,128)(2,1)S(1)} %sum_hop.14.before_ref), channel_id=1, source_target_pairs={{0,2},{1,3},{4,0},{5,1},{8,4},{9,5},{12,8},{13,9},{14,12},{15,13},... | collective-permute-start | bytes 798728 | tf_op jit(solution)/shard_map/ppermute | solution.py:299
  20.4 3.0 %collective-permute-done.8.got_ref = s16[1040,128]{1,0:T(8,128)(2,1)S(1)} collective-permute-done((s16[1040,128]{1,0:T(8,128)(2,1)S(1)}, s16[1040,128]{1,0:T(8,128)(2,1)S(1)}, u32[]{:S(2)}, u32[]{:S(2)}) %collective-permute-start.8) | collective-permute-done | bytes 266272 | tf_op jit(solution)/shard_map/ppermute | solution.py:299
  24.0 1.7 %collective-permute-start.13 = (s16[1040,128]{1,0:T(8,128)(2,1)S(1)}, s16[1040,128]{1,0:T(8,128)(2,1)S(1)}, u32[]{:S(2)}, u32[]{:S(2)}) collective-permute-start(s16[1040,128]{1,0:T(8,128)(2,1)S(1)} %sum_hop.16.before_ref), channel_id=1, source_target_pairs={{0,2},{1,3},{4,0},{5,1},{8,4},{9,5},{12,8},{13,9},{14,12},{15,13},... | collective-permute-start | bytes 798728 | tf_op jit(solution)/shard_map/ppermute | solution.py:299
  26.8 2.4 %collective-permute-done.10.got_ref = s16[1040,128]{1,0:T(8,128)(2,1)S(1)} collective-permute-done((s16[1040,128]{1,0:T(8,128)(2,1)S(1)}, s16[1040,128]{1,0:T(8,128)(2,1)S(1)}, u32[]{:S(2)}, u32[]{:S(2)}) %collective-permute-start.10) | collective-permute-done | bytes 266272 | tf_op jit(solution)/shard_map/ppermute | solution.py:299
  29.7 1.7 %collective-permute-start.15 = (s16[1040,128]{1,0:T(8,128)(2,1)S(1)}, s16[1040,128]{1,0:T(8,128)(2,1)S(1)}, u32[]{:S(2)}, u32[]{:S(2)}) collective-permute-start(s16[1040,128]{1,0:T(8,128)(2,1)S(1)} %sum_hop.18.before_ref), channel_id=1, source_target_pairs={{0,2},{1,3},{4,0},{5,1},{8,4},{9,5},{12,8},{13,9},{14,12},{15,13},... | collective-permute-start | bytes 798728 | tf_op jit(solution)/shard_map/ppermute | solution.py:299
  32.5 2.4 %collective-permute-done.13.got_ref = s16[1040,128]{1,0:T(8,128)(2,1)S(1)} collective-permute-done((s16[1040,128]{1,0:T(8,128)(2,1)S(1)}, s16[1040,128]{1,0:T(8,128)(2,1)S(1)}, u32[]{:S(2)}, u32[]{:S(2)}) %collective-permute-start.13) | collective-permute-done | bytes 266272 | tf_op jit(solution)/shard_map/ppermute | solution.py:299
  35.5 1.7 %collective-permute-start.18 = (s16[1040,128]{1,0:T(8,128)(2,1)S(1)}, s16[1040,128]{1,0:T(8,128)(2,1)S(1)}, u32[]{:S(2)}, u32[]{:S(2)}) collective-permute-start(s16[1040,128]{1,0:T(8,128)(2,1)S(1)} %sum_hop.20.before_ref), channel_id=1, source_target_pairs={{0,2},{1,3},{4,0},{5,1},{8,4},{9,5},{12,8},{13,9},{14,12},{15,13},... | collective-permute-start | bytes 798728 | tf_op jit(solution)/shard_map/ppermute | solution.py:299
  38.2 2.4 %collective-permute-done.15.got_ref = s16[1040,128]{1,0:T(8,128)(2,1)S(1)} collective-permute-done((s16[1040,128]{1,0:T(8,128)(2,1)S(1)}, s16[1040,128]{1,0:T(8,128)(2,1)S(1)}, u32[]{:S(2)}, u32[]{:S(2)}) %collective-permute-start.15) | collective-permute-done | bytes 266272 | tf_op jit(solution)/shard_map/ppermute | solution.py:299
  41.2 1.7 %collective-permute-start.20 = (s16[1040,128]{1,0:T(8,128)(2,1)S(1)}, s16[1040,128]{1,0:T(8,128)(2,1)S(1)}, u32[]{:S(2)}, u32[]{:S(2)}) collective-permute-start(s16[1040,128]{1,0:T(8,128)(2,1)S(1)} %sum_hop.22.before_ref), channel_id=1, source_target_pairs={{0,2},{1,3},{4,0},{5,1},{8,4},{9,5},{12,8},{13,9},{14,12},{15,13},... | collective-permute-start | bytes 798728 | tf_op jit(solution)/shard_map/ppermute | solution.py:299
  44.6 4.0 %collective-permute-done.17.right_ref = s16[1040,128]{1,0:T(8,128)(2,1)S(1)} collective-permute-done((s16[1040,128]{1,0:T(8,128)(2,1)S(1)}, s16[1040,128]{1,0:T(8,128)(2,1)S(1)}, u32[]{:S(2)}, u32[]{:S(2)}) %collective-permute-start.17) | collective-permute-done | bytes 266272 | tf_op jit(solution)/shard_map/ppermute | solution.py:299
  48.7 1.3 %update.2 = (f32[1024,256]{1,0:T(8,128)}, f32[1024,256]{1,0:T(8,128)}, bf16[512,256]{1,0:T(8,128)(2,1)S(1)}) custom-call(f32[256,1024]{1,0:T(8,128)S(1)} %sum_near.1.before_ref.corr_ref, f32[256,1024]{1,0:T(8,128)S(1)} %sum_near.1.before_ref.corr_ref, s16[1040,128]{1,0:T(8,128)(2,1)S(1)} %collective-permute-done.17.right_ref, ...), custom_call_target="tpu_custom_call" | custom-call | flops 2000000000 | bytes 1000000 | tf_op jit(solution)/shard_map/update/pallas_call | solution.py:324
  50.0 1.6 %collective-permute-start.21 = (bf16[512,256]{1,0:T(8,128)(2,1)S(1)}, bf16[512,256]{1,0:T(8,128)(2,1)S(1)}, u32[]{:S(2)}, u32[]{:S(2)}) collective-permute-start(bf16[512,256]{1,0:T(8,128)(2,1)S(1)} %get-tuple-element.67.before_ref.refs_0_), channel_id=1, source_target_pairs={{0,2},{1,3},{4,0},{5,1},{8,4},{9,5},{12,8},{13,9},{14,12},{15,13},... | collective-permute-start | bytes 786440 | tf_op jit(solution)/shard_map/ppermute | solution.py:373
  52.0 2.3 %collective-permute-done.19.right_ref = s16[1040,128]{1,0:T(8,128)(2,1)S(1)} collective-permute-done((s16[1040,128]{1,0:T(8,128)(2,1)S(1)}, s16[1040,128]{1,0:T(8,128)(2,1)S(1)}, u32[]{:S(2)}, u32[]{:S(2)}) %collective-permute-start.19) | collective-permute-done | bytes 266272 | tf_op jit(solution)/shard_map/ppermute | solution.py:299
  54.3 1.3 %update.3 = (f32[1024,256]{1,0:T(8,128)}, f32[1024,256]{1,0:T(8,128)}, bf16[512,256]{1,0:T(8,128)(2,1)S(1)}) custom-call(bf16[512,256]{1,0:T(8,128)(2,1)S(1)} %get-tuple-element.67.before_ref.refs_0_, f32[256,1024]{1,0:T(8,128)S(1)} %sum_near.1.before_ref.corr_ref, ...), custom_call_target="tpu_custom_call", output_to_operand_aliasing={{0}: (8, {}), {1}: (9, {})} | custom-call | flops 2000000000 | bytes 1000000 | tf_op jit(solution)/shard_map/update/pallas_call | solution.py:324
  55.7 1.6 %collective-permute-start.23 = (bf16[512,256]{1,0:T(8,128)(2,1)S(1)}, bf16[512,256]{1,0:T(8,128)(2,1)S(1)}, u32[]{:S(2)}, u32[]{:S(2)}) collective-permute-start(bf16[512,256]{1,0:T(8,128)(2,1)S(1)} %get-tuple-element.72.before_ref.refs_3_), channel_id=1, source_target_pairs={{0,2},{1,3},{4,0},{5,1},{8,4},{9,5},{12,8},{13,9},{14,12},{15,13},... | collective-permute-start | bytes 786440 | tf_op jit(solution)/shard_map/ppermute | solution.py:373
  58.3 1.6 %collective-permute-start.25 = (bf16[512,256]{1,0:T(8,128)(2,1)S(1)}, bf16[512,256]{1,0:T(8,128)(2,1)S(1)}, u32[]{:S(2)}, u32[]{:S(2)}) collective-permute-start(bf16[512,256]{1,0:T(8,128)(2,1)S(1)} %collective-permute-done.21.refs_0_), channel_id=1, source_target_pairs={{0,2},{1,3},{4,0},{5,1},{8,4},{9,5},{12,8},{13,9},{14,12},{15,13},... | collective-permute-start | bytes 786440 | tf_op jit(solution)/shard_map/ppermute | solution.py:373
  61.2 3.7 %collective-permute-done.23.refs_0_ = bf16[512,256]{1,0:T(8,128)(2,1)S(1)} collective-permute-done((bf16[512,256]{1,0:T(8,128)(2,1)S(1)}, bf16[512,256]{1,0:T(8,128)(2,1)S(1)}, u32[]{:S(2)}, u32[]{:S(2)}) %collective-permute-start.23) | collective-permute-done | bytes 262176 | tf_op jit(solution)/shard_map/ppermute | solution.py:373
  64.9 1.6 %collective-permute-start.27 = (bf16[512,256]{1,0:T(8,128)(2,1)S(1)}, bf16[512,256]{1,0:T(8,128)(2,1)S(1)}, u32[]{:S(2)}, u32[]{:S(2)}) collective-permute-start(bf16[512,256]{1,0:T(8,128)(2,1)S(1)} %collective-permute-done.23.refs_0_), channel_id=1, source_target_pairs={{0,2},{1,3},{4,0},{5,1},{8,4},{9,5},{12,8},{13,9},{14,12},{15,13},... | collective-permute-start | bytes 786440 | tf_op jit(solution)/shard_map/ppermute | solution.py:373
  67.8 2.8 %collective-permute-done.25.refs_0_ = bf16[512,256]{1,0:T(8,128)(2,1)S(1)} collective-permute-done((bf16[512,256]{1,0:T(8,128)(2,1)S(1)}, bf16[512,256]{1,0:T(8,128)(2,1)S(1)}, u32[]{:S(2)}, u32[]{:S(2)}) %collective-permute-start.25) | collective-permute-done | bytes 262176 | tf_op jit(solution)/shard_map/ppermute | solution.py:373
  70.5 1.6 %collective-permute-start.29 = (bf16[512,256]{1,0:T(8,128)(2,1)S(1)}, bf16[512,256]{1,0:T(8,128)(2,1)S(1)}, u32[]{:S(2)}, u32[]{:S(2)}) collective-permute-start(bf16[512,256]{1,0:T(8,128)(2,1)S(1)} %collective-permute-done.25.refs_0_), channel_id=1, source_target_pairs={{0,2},{1,3},{4,0},{5,1},{8,4},{9,5},{12,8},{13,9},{14,12},{15,13},... | collective-permute-start | bytes 786440 | tf_op jit(solution)/shard_map/ppermute | solution.py:373
  73.4 2.8 %collective-permute-done.27.refs_0_ = bf16[512,256]{1,0:T(8,128)(2,1)S(1)} collective-permute-done((bf16[512,256]{1,0:T(8,128)(2,1)S(1)}, bf16[512,256]{1,0:T(8,128)(2,1)S(1)}, u32[]{:S(2)}, u32[]{:S(2)}) %collective-permute-start.27) | collective-permute-done | bytes 262176 | tf_op jit(solution)/shard_map/ppermute | solution.py:373
  76.2 1.6 %collective-permute-start.31 = (bf16[512,256]{1,0:T(8,128)(2,1)S(1)}, bf16[512,256]{1,0:T(8,128)(2,1)S(1)}, u32[]{:S(2)}, u32[]{:S(2)}) collective-permute-start(bf16[512,256]{1,0:T(8,128)(2,1)S(1)} %collective-permute-done.27.refs_0_), channel_id=1, source_target_pairs={{0,2},{1,3},{4,0},{5,1},{8,4},{9,5},{12,8},{13,9},{14,12},{15,13},... | collective-permute-start | bytes 786440 | tf_op jit(solution)/shard_map/ppermute | solution.py:373
  79.0 2.8 %collective-permute-done.29.refs_0_ = bf16[512,256]{1,0:T(8,128)(2,1)S(1)} collective-permute-done((bf16[512,256]{1,0:T(8,128)(2,1)S(1)}, bf16[512,256]{1,0:T(8,128)(2,1)S(1)}, u32[]{:S(2)}, u32[]{:S(2)}) %collective-permute-start.29) | collective-permute-done | bytes 262176 | tf_op jit(solution)/shard_map/ppermute | solution.py:373
  81.8 1.6 %collective-permute-start.33 = (bf16[256,256]{1,0:T(8,128)(2,1)S(1)}, bf16[256,256]{1,0:T(8,128)(2,1)S(1)}, u32[]{:S(2)}, u32[]{:S(2)}) collective-permute-start(bf16[256,256]{1,0:T(8,128)(2,1)S(1)} %slice.12), channel_id=1, source_target_pairs={{0,2},{1,3},{4,0},{5,1},{8,4},{9,5},{12,8},{13,9},{14,12},{15,13},... | collective-permute-start | bytes 393224 | tf_op jit(solution)/shard_map/ppermute | solution.py:373
  84.7 1.8 %collective-permute-done.31.refs_0_ = bf16[512,256]{1,0:T(8,128)(2,1)S(1)} collective-permute-done((bf16[512,256]{1,0:T(8,128)(2,1)S(1)}, bf16[512,256]{1,0:T(8,128)(2,1)S(1)}, u32[]{:S(2)}, u32[]{:S(2)}) %collective-permute-start.31) | collective-permute-done | bytes 262176 | tf_op jit(solution)/shard_map/ppermute | solution.py:373
  86.5 2.5 %collective-permute-start.35 = (bf16[256,256]{1,0:T(8,128)(2,1)S(1)}, bf16[256,256]{1,0:T(8,128)(2,1)S(1)}, u32[]{:S(2)}, u32[]{:S(2)}) collective-permute-start(bf16[256,256]{1,0:T(8,128)(2,1)S(1)} %slice.14), channel_id=1, source_target_pairs={{0,2},{1,3},{4,0},{5,1},{8,4},{9,5},{12,8},{13,9},{14,12},{15,13},... | collective-permute-start | bytes 393224 | tf_op jit(solution)/shard_map/ppermute | solution.py:373
  91.8 2.6 %collective-permute-done.36.refs_0_ = bf16[256,256]{1,0:T(8,128)(2,1)S(1)} collective-permute-done((bf16[256,256]{1,0:T(8,128)(2,1)S(1)}, bf16[256,256]{1,0:T(8,128)(2,1)S(1)}, u32[]{:S(2)}, u32[]{:S(2)}) %collective-permute-start.36) | collective-permute-done | bytes 131104 | tf_op jit(solution)/shard_map/ppermute | solution.py:373
  94.8 1.7 %collective-permute-done.37.got_ref = f32[384,256]{1,0:T(8,128)S(1)} collective-permute-done((f32[384,256]{1,0:T(8,128)S(1)}, f32[384,256]{1,0:T(8,128)S(1)}, u32[]{:S(2)}, u32[]{:S(2)}) %collective-permute-start.37) | collective-permute-done | bytes 393248 | tf_op jit(solution)/shard_map/ppermute | solution.py:378
  (108 shorter events, 26.1 us)
Async XLA Ops:
  6.8 6.9 %collective-permute-start.3 = (s16[528,128]{1,0:T(8,128)(2,1)S(1)}, s16[528,128]{1,0:T(8,128)(2,1)S(1)}, u32[]{:S(2)}, u32[]{:S(2)}) collective-permute-start(s16[528,128]{1,0:T(8,128)(2,1)S(1)} %get-tuple-element.64), channel_id=1, source_target_pairs={{0,2},{1,3},{4,0},{5,1},{8,4},{9,5},{12,8},{13,9},{14,12},{15,13},... | collective-permute-start | bytes 405512 | tf_op jit(solution)/shard_map/ppermute | solution.py:282
  9.8 6.1 %collective-permute-start.4 = (s16[528,128]{1,0:T(8,128)(2,1)S(1)}, s16[528,128]{1,0:T(8,128)(2,1)S(1)}, u32[]{:S(2)}, u32[]{:S(2)}) collective-permute-start(s16[528,128]{1,0:T(8,128)(2,1)S(1)} %get-tuple-element.62.before_ref), channel_id=1, source_target_pairs={{0,4},{1,5},{4,8},{5,9},{8,12},{9,13},{12,14},{13,15},{14,10},{15,... | collective-permute-start | bytes 405512 | tf_op jit(solution)/shard_map/ppermute | solution.py:281
  10.5 6.7 %collective-permute-start.6 = (s16[528,128]{1,0:T(8,128)(2,1)S(1)}, s16[528,128]{1,0:T(8,128)(2,1)S(1)}, u32[]{:S(2)}, u32[]{:S(2)}) collective-permute-start(s16[528,128]{1,0:T(8,128)(2,1)S(1)} %get-tuple-element.66), channel_id=1, source_target_pairs={{0,2},{1,3},{4,0},{5,1},{8,4},{9,5},{12,8},{13,9},{14,12},{15,13},... | collective-permute-start | bytes 405512 | tf_op jit(solution)/shard_map/ppermute | solution.py:282
  12.8 6.6 %collective-permute-start.7 = (s16[528,128]{1,0:T(8,128)(2,1)S(1)}, s16[528,128]{1,0:T(8,128)(2,1)S(1)}, u32[]{:S(2)}, u32[]{:S(2)}) collective-permute-start(s16[528,128]{1,0:T(8,128)(2,1)S(1)} %get-tuple-element.63.refs_0_), channel_id=1, source_target_pairs={{0,4},{1,5},{4,8},{5,9},{8,12},{9,13},{12,14},{13,15},{14,10},{15,... | collective-permute-start | bytes 405512 | tf_op jit(solution)/shard_map/ppermute | solution.py:281
  14.2 9.3 %collective-permute-start.8 = (s16[1040,128]{1,0:T(8,128)(2,1)S(1)}, s16[1040,128]{1,0:T(8,128)(2,1)S(1)}, u32[]{:S(2)}, u32[]{:S(2)}) collective-permute-start(s16[1040,128]{1,0:T(8,128)(2,1)S(1)} %sum_hop.12.before_ref), channel_id=1, source_target_pairs={{0,2},{1,3},{4,0},{5,1},{8,4},{9,5},{12,8},{13,9},{14,12},{15,13},... | collective-permute-start | bytes 798728 | tf_op jit(solution)/shard_map/ppermute | solution.py:299
  16.5 9.3 %collective-permute-start.9 = (s16[1040,128]{1,0:T(8,128)(2,1)S(1)}, s16[1040,128]{1,0:T(8,128)(2,1)S(1)}, u32[]{:S(2)}, u32[]{:S(2)}) collective-permute-start(s16[1040,128]{1,0:T(8,128)(2,1)S(1)} %sum_hop.13.refs_0_), channel_id=1, source_target_pairs={{0,4},{1,5},{4,8},{5,9},{8,12},{9,13},{12,14},{13,15},{14,10},{15,... | collective-permute-start | bytes 798728 | tf_op jit(solution)/shard_map/ppermute | solution.py:299
  17.1 17.8 %collective-permute-start.12 = (bf16[3,384,1024]{2,1,0:T(8,128)(2,1)S(1)}, bf16[3,384,1024]{2,1,0:T(8,128)(2,1)S(1)}, u32[]{:S(2)}, u32[]{:S(2)}) collective-permute-start(bf16[3,384,1024]{2,1,0:T(8,128)(2,1)S(1)} %pick_blocks.7.before_ref), channel_id=1, source_target_pairs={{0,1},{1,0},{2,3},{3,2},{4,5},{5,4},{6,7},{7,6},{8,9},{9,8},{10,11... | collective-permute-start | bytes 7077896 | tf_op jit(solution)/shard_map/ppermute | solution.py:242
  17.7 11.4 %collective-permute-start.10 = (s16[1040,128]{1,0:T(8,128)(2,1)S(1)}, s16[1040,128]{1,0:T(8,128)(2,1)S(1)}, u32[]{:S(2)}, u32[]{:S(2)}) collective-permute-start(s16[1040,128]{1,0:T(8,128)(2,1)S(1)} %sum_hop.14.before_ref), channel_id=1, source_target_pairs={{0,2},{1,3},{4,0},{5,1},{8,4},{9,5},{12,8},{13,9},{14,12},{15,13},... | collective-permute-start | bytes 798728 | tf_op jit(solution)/shard_map/ppermute | solution.py:299
  20.0 11.5 %collective-permute-start.11 = (s16[1040,128]{1,0:T(8,128)(2,1)S(1)}, s16[1040,128]{1,0:T(8,128)(2,1)S(1)}, u32[]{:S(2)}, u32[]{:S(2)}) collective-permute-start(s16[1040,128]{1,0:T(8,128)(2,1)S(1)} %sum_hop.15.before_ref), channel_id=1, source_target_pairs={{0,4},{1,5},{4,8},{5,9},{8,12},{9,13},{12,14},{13,15},{14,10},{15,... | collective-permute-start | bytes 798728 | tf_op jit(solution)/shard_map/ppermute | solution.py:299
  24.0 10.9 %collective-permute-start.13 = (s16[1040,128]{1,0:T(8,128)(2,1)S(1)}, s16[1040,128]{1,0:T(8,128)(2,1)S(1)}, u32[]{:S(2)}, u32[]{:S(2)}) collective-permute-start(s16[1040,128]{1,0:T(8,128)(2,1)S(1)} %sum_hop.16.before_ref), channel_id=1, source_target_pairs={{0,2},{1,3},{4,0},{5,1},{8,4},{9,5},{12,8},{13,9},{14,12},{15,13},... | collective-permute-start | bytes 798728 | tf_op jit(solution)/shard_map/ppermute | solution.py:299
  26.4 10.9 %collective-permute-start.14 = (s16[1040,128]{1,0:T(8,128)(2,1)S(1)}, s16[1040,128]{1,0:T(8,128)(2,1)S(1)}, u32[]{:S(2)}, u32[]{:S(2)}) collective-permute-start(s16[1040,128]{1,0:T(8,128)(2,1)S(1)} %sum_hop.17.before_ref), channel_id=1, source_target_pairs={{0,4},{1,5},{4,8},{5,9},{8,12},{9,13},{12,14},{13,15},{14,10},{15,... | collective-permute-start | bytes 798728 | tf_op jit(solution)/shard_map/ppermute | solution.py:299
  29.7 10.9 %collective-permute-start.15 = (s16[1040,128]{1,0:T(8,128)(2,1)S(1)}, s16[1040,128]{1,0:T(8,128)(2,1)S(1)}, u32[]{:S(2)}, u32[]{:S(2)}) collective-permute-start(s16[1040,128]{1,0:T(8,128)(2,1)S(1)} %sum_hop.18.before_ref), channel_id=1, source_target_pairs={{0,2},{1,3},{4,0},{5,1},{8,4},{9,5},{12,8},{13,9},{14,12},{15,13},... | collective-permute-start | bytes 798728 | tf_op jit(solution)/shard_map/ppermute | solution.py:299
  32.1 10.9 %collective-permute-start.16 = (s16[1040,128]{1,0:T(8,128)(2,1)S(1)}, s16[1040,128]{1,0:T(8,128)(2,1)S(1)}, u32[]{:S(2)}, u32[]{:S(2)}) collective-permute-start(s16[1040,128]{1,0:T(8,128)(2,1)S(1)} %sum_hop.19.before_ref), channel_id=1, source_target_pairs={{0,4},{1,5},{4,8},{5,9},{8,12},{9,13},{12,14},{13,15},{14,10},{15,... | collective-permute-start | bytes 798728 | tf_op jit(solution)/shard_map/ppermute | solution.py:299
  35.5 13.2 %collective-permute-start.18 = (s16[1040,128]{1,0:T(8,128)(2,1)S(1)}, s16[1040,128]{1,0:T(8,128)(2,1)S(1)}, u32[]{:S(2)}, u32[]{:S(2)}) collective-permute-start(s16[1040,128]{1,0:T(8,128)(2,1)S(1)} %sum_hop.20.before_ref), channel_id=1, source_target_pairs={{0,2},{1,3},{4,0},{5,1},{8,4},{9,5},{12,8},{13,9},{14,12},{15,13},... | collective-permute-start | bytes 798728 | tf_op jit(solution)/shard_map/ppermute | solution.py:299
  37.8 10.9 %collective-permute-start.17 = (s16[1040,128]{1,0:T(8,128)(2,1)S(1)}, s16[1040,128]{1,0:T(8,128)(2,1)S(1)}, u32[]{:S(2)}, u32[]{:S(2)}) collective-permute-start(s16[1040,128]{1,0:T(8,128)(2,1)S(1)} %sum_hop.21.before_ref), channel_id=1, source_target_pairs={{0,4},{1,5},{4,8},{5,9},{8,12},{9,13},{12,14},{13,15},{14,10},{15,... | collective-permute-start | bytes 798728 | tf_op jit(solution)/shard_map/ppermute | solution.py:299
  41.2 13.2 %collective-permute-start.20 = (s16[1040,128]{1,0:T(8,128)(2,1)S(1)}, s16[1040,128]{1,0:T(8,128)(2,1)S(1)}, u32[]{:S(2)}, u32[]{:S(2)}) collective-permute-start(s16[1040,128]{1,0:T(8,128)(2,1)S(1)} %sum_hop.22.before_ref), channel_id=1, source_target_pairs={{0,2},{1,3},{4,0},{5,1},{8,4},{9,5},{12,8},{13,9},{14,12},{15,13},... | collective-permute-start | bytes 798728 | tf_op jit(solution)/shard_map/ppermute | solution.py:299
  43.5 10.8 %collective-permute-start.19 = (s16[1040,128]{1,0:T(8,128)(2,1)S(1)}, s16[1040,128]{1,0:T(8,128)(2,1)S(1)}, u32[]{:S(2)}, u32[]{:S(2)}) collective-permute-start(s16[1040,128]{1,0:T(8,128)(2,1)S(1)} %sum_hop.23.before_ref), channel_id=1, source_target_pairs={{0,4},{1,5},{4,8},{5,9},{8,12},{9,13},{12,14},{13,15},{14,10},{15,... | collective-permute-start | bytes 798728 | tf_op jit(solution)/shard_map/ppermute | solution.py:299
  50.0 8.3 %collective-permute-start.21 = (bf16[512,256]{1,0:T(8,128)(2,1)S(1)}, bf16[512,256]{1,0:T(8,128)(2,1)S(1)}, u32[]{:S(2)}, u32[]{:S(2)}) collective-permute-start(bf16[512,256]{1,0:T(8,128)(2,1)S(1)} %get-tuple-element.67.before_ref.refs_0_), channel_id=1, source_target_pairs={{0,2},{1,3},{4,0},{5,1},{8,4},{9,5},{12,8},{13,9},{14,12},{15,13},... | collective-permute-start | bytes 786440 | tf_op jit(solution)/shard_map/ppermute | solution.py:373
  51.6 8.7 %collective-permute-start.22 = (bf16[512,256]{1,0:T(8,128)(2,1)S(1)}, bf16[512,256]{1,0:T(8,128)(2,1)S(1)}, u32[]{:S(2)}, u32[]{:S(2)}) collective-permute-start(bf16[512,256]{1,0:T(8,128)(2,1)S(1)} %get-tuple-element.67.before_ref.refs_0_), channel_id=1, source_target_pairs={{0,4},{1,5},{4,8},{5,9},{8,12},{9,13},{12,14},{13,15},{14,10},{15,... | collective-permute-start | bytes 786440 | tf_op jit(solution)/shard_map/ppermute | solution.py:373
  55.7 9.2 %collective-permute-start.23 = (bf16[512,256]{1,0:T(8,128)(2,1)S(1)}, bf16[512,256]{1,0:T(8,128)(2,1)S(1)}, u32[]{:S(2)}, u32[]{:S(2)}) collective-permute-start(bf16[512,256]{1,0:T(8,128)(2,1)S(1)} %get-tuple-element.72.before_ref.refs_3_), channel_id=1, source_target_pairs={{0,2},{1,3},{4,0},{5,1},{8,4},{9,5},{12,8},{13,9},{14,12},{15,13},... | collective-permute-start | bytes 786440 | tf_op jit(solution)/shard_map/ppermute | solution.py:373
  57.3 9.6 %collective-permute-start.24 = (bf16[512,256]{1,0:T(8,128)(2,1)S(1)}, bf16[512,256]{1,0:T(8,128)(2,1)S(1)}, u32[]{:S(2)}, u32[]{:S(2)}) collective-permute-start(bf16[512,256]{1,0:T(8,128)(2,1)S(1)} %get-tuple-element.72.before_ref.refs_3_), channel_id=1, source_target_pairs={{0,4},{1,5},{4,8},{5,9},{8,12},{9,13},{12,14},{13,15},{14,10},{15,... | collective-permute-start | bytes 786440 | tf_op jit(solution)/shard_map/ppermute | solution.py:373
  58.3 12.2 %collective-permute-start.25 = (bf16[512,256]{1,0:T(8,128)(2,1)S(1)}, bf16[512,256]{1,0:T(8,128)(2,1)S(1)}, u32[]{:S(2)}, u32[]{:S(2)}) collective-permute-start(bf16[512,256]{1,0:T(8,128)(2,1)S(1)} %collective-permute-done.21.refs_0_), channel_id=1, source_target_pairs={{0,2},{1,3},{4,0},{5,1},{8,4},{9,5},{12,8},{13,9},{14,12},{15,13},... | collective-permute-start | bytes 786440 | tf_op jit(solution)/shard_map/ppermute | solution.py:373
  60.3 12.2 %collective-permute-start.26 = (bf16[512,256]{1,0:T(8,128)(2,1)S(1)}, bf16[512,256]{1,0:T(8,128)(2,1)S(1)}, u32[]{:S(2)}, u32[]{:S(2)}) collective-permute-start(bf16[512,256]{1,0:T(8,128)(2,1)S(1)} %collective-permute-done.22.refs_0_), channel_id=1, source_target_pairs={{0,4},{1,5},{4,8},{5,9},{8,12},{9,13},{12,14},{13,15},{14,10},{15,... | collective-permute-start | bytes 786440 | tf_op jit(solution)/shard_map/ppermute | solution.py:373
  64.9 11.2 %collective-permute-start.27 = (bf16[512,256]{1,0:T(8,128)(2,1)S(1)}, bf16[512,256]{1,0:T(8,128)(2,1)S(1)}, u32[]{:S(2)}, u32[]{:S(2)}) collective-permute-start(bf16[512,256]{1,0:T(8,128)(2,1)S(1)} %collective-permute-done.23.refs_0_), channel_id=1, source_target_pairs={{0,2},{1,3},{4,0},{5,1},{8,4},{9,5},{12,8},{13,9},{14,12},{15,13},... | collective-permute-start | bytes 786440 | tf_op jit(solution)/shard_map/ppermute | solution.py:373
  66.9 11.2 %collective-permute-start.28 = (bf16[512,256]{1,0:T(8,128)(2,1)S(1)}, bf16[512,256]{1,0:T(8,128)(2,1)S(1)}, u32[]{:S(2)}, u32[]{:S(2)}) collective-permute-start(bf16[512,256]{1,0:T(8,128)(2,1)S(1)} %collective-permute-done.24.refs_0_), channel_id=1, source_target_pairs={{0,4},{1,5},{4,8},{5,9},{8,12},{9,13},{12,14},{13,15},{14,10},{15,... | collective-permute-start | bytes 786440 | tf_op jit(solution)/shard_map/ppermute | solution.py:373
  70.5 11.2 %collective-permute-start.29 = (bf16[512,256]{1,0:T(8,128)(2,1)S(1)}, bf16[512,256]{1,0:T(8,128)(2,1)S(1)}, u32[]{:S(2)}, u32[]{:S(2)}) collective-permute-start(bf16[512,256]{1,0:T(8,128)(2,1)S(1)} %collective-permute-done.25.refs_0_), channel_id=1, source_target_pairs={{0,2},{1,3},{4,0},{5,1},{8,4},{9,5},{12,8},{13,9},{14,12},{15,13},... | collective-permute-start | bytes 786440 | tf_op jit(solution)/shard_map/ppermute | solution.py:373
  72.5 11.3 %collective-permute-start.30 = (bf16[512,256]{1,0:T(8,128)(2,1)S(1)}, bf16[512,256]{1,0:T(8,128)(2,1)S(1)}, u32[]{:S(2)}, u32[]{:S(2)}) collective-permute-start(bf16[512,256]{1,0:T(8,128)(2,1)S(1)} %collective-permute-done.26.refs_0_), channel_id=1, source_target_pairs={{0,4},{1,5},{4,8},{5,9},{8,12},{9,13},{12,14},{13,15},{14,10},{15,... | collective-permute-start | bytes 786440 | tf_op jit(solution)/shard_map/ppermute | solution.py:373
  76.2 10.3 %collective-permute-start.31 = (bf16[512,256]{1,0:T(8,128)(2,1)S(1)}, bf16[512,256]{1,0:T(8,128)(2,1)S(1)}, u32[]{:S(2)}, u32[]{:S(2)}) collective-permute-start(bf16[512,256]{1,0:T(8,128)(2,1)S(1)} %collective-permute-done.27.refs_0_), channel_id=1, source_target_pairs={{0,2},{1,3},{4,0},{5,1},{8,4},{9,5},{12,8},{13,9},{14,12},{15,13},... | collective-permute-start | bytes 786440 | tf_op jit(solution)/shard_map/ppermute | solution.py:373
  78.1 11.3 %collective-permute-start.32 = (bf16[512,256]{1,0:T(8,128)(2,1)S(1)}, bf16[512,256]{1,0:T(8,128)(2,1)S(1)}, u32[]{:S(2)}, u32[]{:S(2)}) collective-permute-start(bf16[512,256]{1,0:T(8,128)(2,1)S(1)} %collective-permute-done.28.refs_0_), channel_id=1, source_target_pairs={{0,4},{1,5},{4,8},{5,9},{8,12},{9,13},{12,14},{13,15},{14,10},{15,... | collective-permute-start | bytes 786440 | tf_op jit(solution)/shard_map/ppermute | solution.py:373
  81.8 8.1 %collective-permute-start.33 = (bf16[256,256]{1,0:T(8,128)(2,1)S(1)}, bf16[256,256]{1,0:T(8,128)(2,1)S(1)}, u32[]{:S(2)}, u32[]{:S(2)}) collective-permute-start(bf16[256,256]{1,0:T(8,128)(2,1)S(1)} %slice.12), channel_id=1, source_target_pairs={{0,2},{1,3},{4,0},{5,1},{8,4},{9,5},{12,8},{13,9},{14,12},{15,13},... | collective-permute-start | bytes 393224 | tf_op jit(solution)/shard_map/ppermute | solution.py:373
  83.8 7.4 %collective-permute-start.34 = (bf16[256,256]{1,0:T(8,128)(2,1)S(1)}, bf16[256,256]{1,0:T(8,128)(2,1)S(1)}, u32[]{:S(2)}, u32[]{:S(2)}) collective-permute-start(bf16[256,256]{1,0:T(8,128)(2,1)S(1)} %slice.13), channel_id=1, source_target_pairs={{0,4},{1,5},{4,8},{5,9},{8,12},{9,13},{12,14},{13,15},{14,10},{15,... | collective-permute-start | bytes 393224 | tf_op jit(solution)/shard_map/ppermute | solution.py:373
  86.5 5.1 %collective-permute-start.35 = (bf16[256,256]{1,0:T(8,128)(2,1)S(1)}, bf16[256,256]{1,0:T(8,128)(2,1)S(1)}, u32[]{:S(2)}, u32[]{:S(2)}) collective-permute-start(bf16[256,256]{1,0:T(8,128)(2,1)S(1)} %slice.14), channel_id=1, source_target_pairs={{0,2},{1,3},{4,0},{5,1},{8,4},{9,5},{12,8},{13,9},{14,12},{15,13},... | collective-permute-start | bytes 393224 | tf_op jit(solution)/shard_map/ppermute | solution.py:373
  (16 other events, 56.7 us)

commit v9 on v7

--- a/solution.py
+++ b/solution.py
@@ -50,14 +50,16 @@
 
 def pick_kernel(ring, wanted, block, genotype_ref, *refs):
     outs, sems = refs[-1 - len(wanted) : -1], refs[-1]
-    other = 1 - lax.rem(lax.axis_index("ind"), 2)
+    core = lax.rem(lax.axis_index("ind"), 2)
     copies = []
-    for out_ref, distances in zip(outs, wanted):
+    for out_ref, (distances, swapped, low, _) in zip(outs, wanted):
+        parity = 1 - core if swapped else core
+        width = out_ref.shape[2]
         for k, owner in enumerate(owners_of(ring, distances)):
-            at = pl.multiple_of((2 * owner + other) * block, LANES)
+            at = pl.multiple_of((2 * owner + parity) * block + low, LANES)
             copies.append(
                 pltpu.make_async_copy(
-                    genotype_ref.at[:, pl.ds(at, block)], out_ref.at[k], sems.at[len(copies)]
+                    genotype_ref.at[:, pl.ds(at, width)], out_ref.at[k], sems.at[len(copies)]
                 )
             )
             copies[-1].start()
@@ -71,21 +73,18 @@
     out_ref[:, people:] = other_ref[...].T
 
 
-def own_columns(ring, own_ref, peer_ref, d, low, high):
+def own_columns(ring, own_ref, d, low, high):
     (owner,) = owners_of(ring, [d])
-    block = peer_ref.shape[2]
+    block = own_ref.shape[1] // (2 * len(ring))
     at = (2 * owner + lax.rem(lax.axis_index("ind"), 2)) * block + low
     return own_ref[:, pl.ds(pl.multiple_of(at, LANES), high - low)]
 
 
-def local_sum(ring, res_ref, own_ref, peer_ref, at, low, high):
-    people = own_ref.shape[0]
-    own = own_columns(ring, own_ref, peer_ref, at[0], low, high)
+def local_sum(res_ref, own, other):
+    people = own.shape[0]
     return jnp.dot(
         res_ref[:, :people], own, preferred_element_type=jnp.float32
-    ) + jnp.dot(
-        res_ref[:, people:], peer_ref[at[1], :, low:high], preferred_element_type=jnp.float32
-    )
+    ) + jnp.dot(res_ref[:, people:], other, preferred_element_type=jnp.float32)
 
 
 def decode(ref):
@@ -113,8 +112,8 @@
     return [total[:, k : k + LANES] for k in range(0, total.shape[1], LANES)]
 
 
-def far_kernel(ring, at, low, high, before_ref, res_ref, own_ref, peer_ref, right_ref, left_ref):
-    tiles = tiles_of(local_sum(ring, res_ref, own_ref, peer_ref, at, low, high))
+def far_kernel(before_ref, res_ref, own_ref, peer_ref, right_ref, left_ref):
+    tiles = tiles_of(local_sum(res_ref, own_ref[0], peer_ref[0]))
     half = len(tiles) // 2
     encode(right_ref, tiles[:half])
     encode(left_ref, tiles[half:])
@@ -123,7 +122,8 @@
 def hop_kernel(
     ring, at, low, high, way, before_ref, res_ref, own_ref, peer_ref, got_ref, out_ref
 ):
-    tiles = tiles_of(local_sum(ring, res_ref, own_ref, peer_ref, at, low, high))
+    own = own_columns(ring, own_ref, at[0], low, high)
+    tiles = tiles_of(local_sum(res_ref, own, peer_ref[at[1], :, low:high]))
     got = decode(got_ref)
     height = tiles[0].shape[0]
     count = got.shape[0] // height
@@ -134,7 +134,8 @@
 
 
 def near_kernel(ring, at, before_ref, res_ref, own_ref, peer_ref, out_ref):
-    out_ref[...] = local_sum(ring, res_ref, own_ref, peer_ref, at, 0, peer_ref.shape[2])
+    own = own_columns(ring, own_ref, at[0], 0, peer_ref.shape[2])
+    out_ref[...] = local_sum(res_ref, own, peer_ref[at[1]])
 
 
 def update_kernel(total, low, before_ref, corr_ref, right_ref, left_ref, incl_ref, mean_ref, prior_ref,
@@ -172,9 +173,9 @@
         effect_ref, own_ref, peer_ref = refs[3 * k : 3 * k + 3]
         effect = effect_ref[...]
         high = low + effect.shape[0]
-        own = own_columns(ring, own_ref, peer_ref, at[0], low, high)
+        own = own_columns(ring, own_ref, at[0], low, high)
         a = jnp.dot(own, effect, preferred_element_type=jnp.float32)
-        b = jnp.dot(peer_ref[at[1], :, low:high], effect, preferred_element_type=jnp.float32)
+        b = jnp.dot(peer_ref[at[1], :, low - at[2] : high - at[2]], effect, preferred_element_type=jnp.float32)
         mine = a if mine is None else mine + a
         other = b if other is None else other + b
     if not first:
@@ -201,6 +202,7 @@
     f32, bf16 = jnp.float32, jnp.bfloat16
     params = pltpu.CompilerParams(vmem_limit_bytes=VMEM)
     small = pl.CostEstimate(flops=1, bytes_accessed=1, transcendentals=0)
+    longest = pl.CostEstimate(flops=25 * 10**9, bytes_accessed=10**6, transcendentals=0)
     heavy = pl.CostEstimate(flops=10**10, bytes_accessed=10**6, transcendentals=0)
     middle = pl.CostEstimate(flops=4 * 10**9, bytes_accessed=10**6, transcendentals=0)
     light = pl.CostEstimate(flops=2 * 10**9, bytes_accessed=10**6, transcendentals=0)
@@ -223,10 +225,10 @@
             in_specs=[anywhere] * (1 + len(before)),
             out_specs=[anywhere] * len(wanted),
             out_shape=[
-                jax.ShapeDtypeStruct((len(distances), people, block), bf16)
-                for distances in wanted
+                jax.ShapeDtypeStruct((len(distances), people, width), bf16)
+                for distances, _, _, width in wanted
             ],
-            scratch_shapes=[pltpu.SemaphoreType.DMA((sum(len(d) for d in wanted),))],
+            scratch_shapes=[pltpu.SemaphoreType.DMA((sum(len(w[0]) for w in wanted),))],
             compiler_params=params,
             cost_estimate=cost,
             name="pick_blocks",
@@ -236,25 +238,37 @@
     for d in range(reach - 1, 0, -1):
         order += [d, size - d]
     order += [0]
-    peer = {}
+    peer, own_far, peer_far = {}, {}, {}
 
     def swapped(distances, sent):
         got = lax.ppermute(sent, "ind", swap)
-        peer.update({d: (got, k) for k, d in enumerate(distances)})
-
-    first, later = [b for b in (order[:1], order[1:3]) if b], [b for b in (order[3:5], order[5:]) if b]
-    sent = pick(first, pltpu.HBM, light)
-    last = sent[0]
-    for distances, array in zip(first, sent):
-        swapped(distances, array)
+        peer.update({d: (got, k, 0) for k, d in enumerate(distances)})
+
+    def far(piece):
+        return [(order[:1], True, piece * part, part), (order[:1], False, piece * part, part)]
+
+    def whole(distances):
+        return [(distances, True, 0, block)] if distances else []
+
+    later = [b for b in (order[3:5], order[5:]) if b]
+    last, own_far[0] = pick(far(0), pltpu.HBM, small)
+    peer_far[0] = lax.ppermute(last, "ind", swap)
     mine, _ = lax.optimization_barrier((residual, last))
     residual_other = lax.ppermute(mine, "ind", swap)
+    wanted = (far(1) if pieces > 1 else []) + whole(order[1:3])
+    if wanted:
+        found = pick(wanted, pltpu.HBM, heavy, last)
+        last = found[0]
+        if pieces > 1:
+            peer_far[1], own_far[1] = lax.ppermute(found[0], "ind", swap), found[1]
+        if order[1:3]:
+            swapped(order[1:3], found[-1])
     res = last = pl.pallas_call(
         flip_kernel,
         in_specs=after(last, (residual, residual_other)),
         out_shape=jax.ShapeDtypeStruct((cols, 2 * people), bf16),
         compiler_params=params,
-        cost_estimate=light,
+        cost_estimate=small,
         name="flip",
     )(last, residual, residual_other)
 
@@ -265,17 +279,18 @@
     for d in range(reach, 0, -1):
         for piece in range(pieces):
             low, high = piece * part, (piece + 1) * part
-            if d == reach > 1 and piece:
+            if d == reach > 1 and piece == pieces - 1:
                 last, _ = lax.optimization_barrier((last, peer[d - 1][0]))
             if d == reach:
-                sent = last = pl.pallas_call(
-                    functools.partial(far_kernel, ring, (d, peer[d][1]), low, high),
-                    in_specs=after(last, (res, genotype, peer[d][0])),
+                args = (res, own_far[piece], peer_far[piece])
+                sent = pl.pallas_call(
+                    far_kernel,
+                    in_specs=after(last, args),
                     out_shape=[shape_of(part // 2)] * 2,
                     compiler_params=params,
-                    cost_estimate=heavy,
+                    cost_estimate=small if piece else longest,
                     name="sum_far",
-                )(last, res, genotype, peer[d][0])
+                )(last, *args)
                 last = sent[0]
                 got[0, piece] = lax.ppermute(sent[0], "ind", right)
                 got[1, piece] = lax.ppermute(sent[1], "ind", left)
@@ -298,7 +313,7 @@
                     got[way, piece] = lax.ppermute(last, "ind", left if way else right)
             if later and (d, piece) in ((reach, pieces - 1), (reach - 1, 0)):
                 distances = later.pop(0)
-                (last,) = pick([distances], pltpu.VMEM, light, last)
+                (last,) = pick(whole(distances), pltpu.VMEM, light, last)
                 swapped(distances, last)
 
     near = last = pl.pallas_call(
@@ -345,8 +360,12 @@
 
     eta_shape = jax.ShapeDtypeStruct((people, cols), f32)
     def product(found, eta, before, cost):
-        args = [v for d, _, effect in found for v in (effect, genotype, peer[d][0])] + list(eta)
-        places = [((d, peer[d][1]), low) for d, low, _ in found]
+        args, places = list(eta), []
+        for d, low, effect in reversed(found):
+            piece = low // part
+            there = (peer_far[piece], 0, piece * part) if d == reach else peer[d]
+            args = [effect, genotype, there[0]] + args
+            places = [((d, *there[1:]), low)] + places
         return pl.pallas_call(
             functools.partial(eta_kernel, ring, places, not eta),
             in_specs=after(before, args),

time: 97.9 us -> 96.4 us (0.985)
  waiting for transfers between devices: 39.6 us -> 35 us
  starting transfers between devices: 35.9 us -> 37.1 us
  Pallas kernels: 20.2 us -> 21.3 us
    ppermute x1, waiting for transfers between devices: 3.93 us -> 0.01 us  [on_device(): residual_other = lax.ppermute(mine, 'ind', swap)]
    ppermute x12, waiting for transfers between devices: 15.3 us -> 16.7 us  [on_device(): got[way, piece] = lax.ppermute(last, 'ind', left if way else right)]
    ppermute x16, waiting for transfers between devices: 17.2 us -> 16.1 us  [on_device(): held[way, piece] = lax.ppermute(message, 'ind', left if way else right)]
    ppermute x2, waiting for transfers between devices: 1.49 us -> 0.38 us  [on_device(): got[1, piece] = lax.ppermute(sent[1], 'ind', left)]
    pallas_call x3 -> x4, Pallas kernels: 2.13 us -> 3.21 us  [pick(): pl.pallas_call(functools.partial(pick_kernel, ring, wanted, block), in_sp...]
    ppermute x0 -> x2, starting transfers between devices: none -> 1.01 us  [the longest x1 0.52 us: on_device(): peer_far[0] = lax.ppermute(last, 'ind', swap)]
  transfers between devices with their start and end apart: 38 -> 39, of which waited for: 16 -> 15; matrix products, arithmetic and copies ran while one was open for 0% -> 0% of each run, Pallas kernels for 18% -> 20%
where the time goes in v9:
time: 96.4 us; the launch traced here: 96.2 us
  starting transfers between devices  37.1 us (38%)
  waiting for transfers between devices  35 us (36%)
  Pallas kernels  21.3 us (22%)
  local copies, waits for them, and re-layouts  1.6 us (2%)
  between operations  1.22 us (1%)
    ppermute x16, starting transfers between devices, on_device(): held[way, piece] = lax.ppermute(message, 'ind', left if way else right)  17.3 us
    ppermute x12, waiting for transfers between devices, on_device(): got[way, piece] = lax.ppermute(last, 'ind', left if way else right)  16.7 us
    ppermute x16, waiting for transfers between devices, on_device(): held[way, piece] = lax.ppermute(message, 'ind', left if way else right)  16.1 us
    ppermute x12, starting transfers between devices, on_device(): got[way, piece] = lax.ppermute(last, 'ind', left if way else right)  12.8 us
    pallas_call x12, Pallas kernels, on_device(): pl.pallas_call(functools.partial(hop_kernel, ring, (w, peer[w][1]), low,...  6.61 us
    pallas_call x17, Pallas kernels, product(): pl.pallas_call(functools.partial(eta_kernel, ring, places, not eta), in_s...  6.09 us
    ppermute x2, starting transfers between devices, on_device(): got[1, piece] = lax.ppermute(sent[1], 'ind', left)  5.47 us
    pallas_call x4, Pallas kernels, pick(): pl.pallas_call(functools.partial(pick_kernel, ring, wanted, block), in_sp...  3.21 us
  transfers between devices with their start and end apart: 39, of which 15 were waited for; matrix products, arithmetic and copies ran while one was open for 0% of the time, Pallas kernels for 20%

profile of v9, /device:TPU:0, one launch (start us, length us, event | category | flops | bytes accessed | tf_op | source)
XLA Modules:
  0.0 96.2 jit_solution(8724587575459412258)
XLA Ops:
  2.5 1.7 %pick_blocks.5 = (bf16[1,384,512]{2,1,0:T(8,128)(2,1)S(1)}, bf16[1,384,512]{2,1,0:T(8,128)(2,1)S(1)}, bf16[2,384,1024]{2,1,0:T(8,128)(2,1)S(1)}) custom-call(bf16[384,16384]{1,0:T(8,128)(2,1)} %refs_1_.33, bf16[1,384,512]{2,1,0:T(8,128)(2,1)S(1)} %get-tuple-element.67.refs_0_), custom_call_target="tpu_custom_call" | custom-call | flops 10000000000 | bytes 1000000 | tf_op jit(solution)/shard_map/pick_blocks/pallas_call | solution.py:223
  5.6 2.9 %collective-permute-start.4 = (s16[528,128]{1,0:T(8,128)(2,1)S(1)}, s16[528,128]{1,0:T(8,128)(2,1)S(1)}, u32[]{:S(2)}, u32[]{:S(2)}) collective-permute-start(s16[528,128]{1,0:T(8,128)(2,1)S(1)} %get-tuple-element.76), channel_id=1, source_target_pairs={{0,2},{1,3},{4,0},{5,1},{8,4},{9,5},{12,8},{13,9},{14,12},{15,13},... | collective-permute-start | bytes 405512 | tf_op jit(solution)/shard_map/ppermute | solution.py:296
  9.2 2.5 %collective-permute-start.7 = (s16[528,128]{1,0:T(8,128)(2,1)S(1)}, s16[528,128]{1,0:T(8,128)(2,1)S(1)}, u32[]{:S(2)}, u32[]{:S(2)}) collective-permute-start(s16[528,128]{1,0:T(8,128)(2,1)S(1)} %get-tuple-element.78), channel_id=1, source_target_pairs={{0,2},{1,3},{4,0},{5,1},{8,4},{9,5},{12,8},{13,9},{14,12},{15,13},... | collective-permute-start | bytes 405512 | tf_op jit(solution)/shard_map/ppermute | solution.py:296
  13.0 1.7 %collective-permute-start.9 = (s16[1040,128]{1,0:T(8,128)(2,1)S(1)}, s16[1040,128]{1,0:T(8,128)(2,1)S(1)}, u32[]{:S(2)}, u32[]{:S(2)}) collective-permute-start(s16[1040,128]{1,0:T(8,128)(2,1)S(1)} %sum_hop.12.before_ref), channel_id=1, source_target_pairs={{0,2},{1,3},{4,0},{5,1},{8,4},{9,5},{12,8},{13,9},{14,12},{15,13},... | collective-permute-start | bytes 798728 | tf_op jit(solution)/shard_map/ppermute | solution.py:313
  16.6 1.7 %collective-permute-start.11 = (s16[1040,128]{1,0:T(8,128)(2,1)S(1)}, s16[1040,128]{1,0:T(8,128)(2,1)S(1)}, u32[]{:S(2)}, u32[]{:S(2)}) collective-permute-start(s16[1040,128]{1,0:T(8,128)(2,1)S(1)} %sum_hop.14.before_ref), channel_id=1, source_target_pairs={{0,2},{1,3},{4,0},{5,1},{8,4},{9,5},{12,8},{13,9},{14,12},{15,13},... | collective-permute-start | bytes 798728 | tf_op jit(solution)/shard_map/ppermute | solution.py:313
  19.2 3.0 %collective-permute-done.9.got_ref = s16[1040,128]{1,0:T(8,128)(2,1)S(1)} collective-permute-done((s16[1040,128]{1,0:T(8,128)(2,1)S(1)}, s16[1040,128]{1,0:T(8,128)(2,1)S(1)}, u32[]{:S(2)}, u32[]{:S(2)}) %collective-permute-start.9) | collective-permute-done | bytes 266272 | tf_op jit(solution)/shard_map/ppermute | solution.py:313
  22.8 1.7 %collective-permute-start.14 = (s16[1040,128]{1,0:T(8,128)(2,1)S(1)}, s16[1040,128]{1,0:T(8,128)(2,1)S(1)}, u32[]{:S(2)}, u32[]{:S(2)}) collective-permute-start(s16[1040,128]{1,0:T(8,128)(2,1)S(1)} %sum_hop.16.before_ref), channel_id=1, source_target_pairs={{0,2},{1,3},{4,0},{5,1},{8,4},{9,5},{12,8},{13,9},{14,12},{15,13},... | collective-permute-start | bytes 798728 | tf_op jit(solution)/shard_map/ppermute | solution.py:313
  25.6 2.4 %collective-permute-done.11.got_ref = s16[1040,128]{1,0:T(8,128)(2,1)S(1)} collective-permute-done((s16[1040,128]{1,0:T(8,128)(2,1)S(1)}, s16[1040,128]{1,0:T(8,128)(2,1)S(1)}, u32[]{:S(2)}, u32[]{:S(2)}) %collective-permute-start.11) | collective-permute-done | bytes 266272 | tf_op jit(solution)/shard_map/ppermute | solution.py:313
  28.5 1.7 %collective-permute-start.16 = (s16[1040,128]{1,0:T(8,128)(2,1)S(1)}, s16[1040,128]{1,0:T(8,128)(2,1)S(1)}, u32[]{:S(2)}, u32[]{:S(2)}) collective-permute-start(s16[1040,128]{1,0:T(8,128)(2,1)S(1)} %sum_hop.18.before_ref), channel_id=1, source_target_pairs={{0,2},{1,3},{4,0},{5,1},{8,4},{9,5},{12,8},{13,9},{14,12},{15,13},... | collective-permute-start | bytes 798728 | tf_op jit(solution)/shard_map/ppermute | solution.py:313
  31.3 2.4 %collective-permute-done.14.got_ref = s16[1040,128]{1,0:T(8,128)(2,1)S(1)} collective-permute-done((s16[1040,128]{1,0:T(8,128)(2,1)S(1)}, s16[1040,128]{1,0:T(8,128)(2,1)S(1)}, u32[]{:S(2)}, u32[]{:S(2)}) %collective-permute-start.14) | collective-permute-done | bytes 266272 | tf_op jit(solution)/shard_map/ppermute | solution.py:313
  34.2 1.7 %collective-permute-start.19 = (s16[1040,128]{1,0:T(8,128)(2,1)S(1)}, s16[1040,128]{1,0:T(8,128)(2,1)S(1)}, u32[]{:S(2)}, u32[]{:S(2)}) collective-permute-start(s16[1040,128]{1,0:T(8,128)(2,1)S(1)} %sum_hop.20.before_ref), channel_id=1, source_target_pairs={{0,2},{1,3},{4,0},{5,1},{8,4},{9,5},{12,8},{13,9},{14,12},{15,13},... | collective-permute-start | bytes 798728 | tf_op jit(solution)/shard_map/ppermute | solution.py:313
  37.0 2.4 %collective-permute-done.16.got_ref = s16[1040,128]{1,0:T(8,128)(2,1)S(1)} collective-permute-done((s16[1040,128]{1,0:T(8,128)(2,1)S(1)}, s16[1040,128]{1,0:T(8,128)(2,1)S(1)}, u32[]{:S(2)}, u32[]{:S(2)}) %collective-permute-start.16) | collective-permute-done | bytes 266272 | tf_op jit(solution)/shard_map/ppermute | solution.py:313
  39.9 1.7 %collective-permute-start.21 = (s16[1040,128]{1,0:T(8,128)(2,1)S(1)}, s16[1040,128]{1,0:T(8,128)(2,1)S(1)}, u32[]{:S(2)}, u32[]{:S(2)}) collective-permute-start(s16[1040,128]{1,0:T(8,128)(2,1)S(1)} %sum_hop.22.before_ref), channel_id=1, source_target_pairs={{0,2},{1,3},{4,0},{5,1},{8,4},{9,5},{12,8},{13,9},{14,12},{15,13},... | collective-permute-start | bytes 798728 | tf_op jit(solution)/shard_map/ppermute | solution.py:313
  43.4 4.0 %collective-permute-done.18.right_ref = s16[1040,128]{1,0:T(8,128)(2,1)S(1)} collective-permute-done((s16[1040,128]{1,0:T(8,128)(2,1)S(1)}, s16[1040,128]{1,0:T(8,128)(2,1)S(1)}, u32[]{:S(2)}, u32[]{:S(2)}) %collective-permute-start.18) | collective-permute-done | bytes 266272 | tf_op jit(solution)/shard_map/ppermute | solution.py:313
  47.5 1.3 %update.2 = (f32[1024,256]{1,0:T(8,128)}, f32[1024,256]{1,0:T(8,128)}, bf16[512,256]{1,0:T(8,128)(2,1)S(1)}) custom-call(f32[256,1024]{1,0:T(8,128)S(1)} %sum_near.1.before_ref.corr_ref, f32[256,1024]{1,0:T(8,128)S(1)} %sum_near.1.before_ref.corr_ref, s16[1040,128]{1,0:T(8,128)(2,1)S(1)} %collective-permute-done.18.right_ref, ...), custom_call_target="tpu_custom_call" | custom-call | flops 2000000000 | bytes 1000000 | tf_op jit(solution)/shard_map/update/pallas_call | solution.py:338
  48.8 1.6 %collective-permute-start.22 = (bf16[512,256]{1,0:T(8,128)(2,1)S(1)}, bf16[512,256]{1,0:T(8,128)(2,1)S(1)}, u32[]{:S(2)}, u32[]{:S(2)}) collective-permute-start(bf16[512,256]{1,0:T(8,128)(2,1)S(1)} %get-tuple-element.79.before_ref.refs_0_), channel_id=1, source_target_pairs={{0,2},{1,3},{4,0},{5,1},{8,4},{9,5},{12,8},{13,9},{14,12},{15,13},... | collective-permute-start | bytes 786440 | tf_op jit(solution)/shard_map/ppermute | solution.py:391
  50.8 2.3 %collective-permute-done.20.right_ref = s16[1040,128]{1,0:T(8,128)(2,1)S(1)} collective-permute-done((s16[1040,128]{1,0:T(8,128)(2,1)S(1)}, s16[1040,128]{1,0:T(8,128)(2,1)S(1)}, u32[]{:S(2)}, u32[]{:S(2)}) %collective-permute-start.20) | collective-permute-done | bytes 266272 | tf_op jit(solution)/shard_map/ppermute | solution.py:313
  53.1 1.3 %update.3 = (f32[1024,256]{1,0:T(8,128)}, f32[1024,256]{1,0:T(8,128)}, bf16[512,256]{1,0:T(8,128)(2,1)S(1)}) custom-call(bf16[512,256]{1,0:T(8,128)(2,1)S(1)} %get-tuple-element.79.before_ref.refs_0_, f32[256,1024]{1,0:T(8,128)S(1)} %sum_near.1.before_ref.corr_ref, ...), custom_call_target="tpu_custom_call", output_to_operand_aliasing={{0}: (8, {}), {1}: (9, {})} | custom-call | flops 2000000000 | bytes 1000000 | tf_op jit(solution)/shard_map/update/pallas_call | solution.py:338
  54.5 1.6 %collective-permute-start.24 = (bf16[512,256]{1,0:T(8,128)(2,1)S(1)}, bf16[512,256]{1,0:T(8,128)(2,1)S(1)}, u32[]{:S(2)}, u32[]{:S(2)}) collective-permute-start(bf16[512,256]{1,0:T(8,128)(2,1)S(1)} %get-tuple-element.84.before_ref.refs_3_), channel_id=1, source_target_pairs={{0,2},{1,3},{4,0},{5,1},{8,4},{9,5},{12,8},{13,9},{14,12},{15,13},... | collective-permute-start | bytes 786440 | tf_op jit(solution)/shard_map/ppermute | solution.py:391
  57.1 1.6 %collective-permute-start.26 = (bf16[512,256]{1,0:T(8,128)(2,1)S(1)}, bf16[512,256]{1,0:T(8,128)(2,1)S(1)}, u32[]{:S(2)}, u32[]{:S(2)}) collective-permute-start(bf16[512,256]{1,0:T(8,128)(2,1)S(1)} %collective-permute-done.22.refs_0_), channel_id=1, source_target_pairs={{0,2},{1,3},{4,0},{5,1},{8,4},{9,5},{12,8},{13,9},{14,12},{15,13},... | collective-permute-start | bytes 786440 | tf_op jit(solution)/shard_map/ppermute | solution.py:391
  60.0 3.7 %collective-permute-done.24.refs_0_ = bf16[512,256]{1,0:T(8,128)(2,1)S(1)} collective-permute-done((bf16[512,256]{1,0:T(8,128)(2,1)S(1)}, bf16[512,256]{1,0:T(8,128)(2,1)S(1)}, u32[]{:S(2)}, u32[]{:S(2)}) %collective-permute-start.24) | collective-permute-done | bytes 262176 | tf_op jit(solution)/shard_map/ppermute | solution.py:391
  63.7 1.6 %collective-permute-start.28 = (bf16[512,256]{1,0:T(8,128)(2,1)S(1)}, bf16[512,256]{1,0:T(8,128)(2,1)S(1)}, u32[]{:S(2)}, u32[]{:S(2)}) collective-permute-start(bf16[512,256]{1,0:T(8,128)(2,1)S(1)} %collective-permute-done.24.refs_0_), channel_id=1, source_target_pairs={{0,2},{1,3},{4,0},{5,1},{8,4},{9,5},{12,8},{13,9},{14,12},{15,13},... | collective-permute-start | bytes 786440 | tf_op jit(solution)/shard_map/ppermute | solution.py:391
  66.6 2.8 %collective-permute-done.26.refs_0_ = bf16[512,256]{1,0:T(8,128)(2,1)S(1)} collective-permute-done((bf16[512,256]{1,0:T(8,128)(2,1)S(1)}, bf16[512,256]{1,0:T(8,128)(2,1)S(1)}, u32[]{:S(2)}, u32[]{:S(2)}) %collective-permute-start.26) | collective-permute-done | bytes 262176 | tf_op jit(solution)/shard_map/ppermute | solution.py:391
  69.3 1.6 %collective-permute-start.30 = (bf16[512,256]{1,0:T(8,128)(2,1)S(1)}, bf16[512,256]{1,0:T(8,128)(2,1)S(1)}, u32[]{:S(2)}, u32[]{:S(2)}) collective-permute-start(bf16[512,256]{1,0:T(8,128)(2,1)S(1)} %collective-permute-done.26.refs_0_), channel_id=1, source_target_pairs={{0,2},{1,3},{4,0},{5,1},{8,4},{9,5},{12,8},{13,9},{14,12},{15,13},... | collective-permute-start | bytes 786440 | tf_op jit(solution)/shard_map/ppermute | solution.py:391
  72.4 2.6 %collective-permute-done.28.refs_0_ = bf16[512,256]{1,0:T(8,128)(2,1)S(1)} collective-permute-done((bf16[512,256]{1,0:T(8,128)(2,1)S(1)}, bf16[512,256]{1,0:T(8,128)(2,1)S(1)}, u32[]{:S(2)}, u32[]{:S(2)}) %collective-permute-start.28) | collective-permute-done | bytes 262176 | tf_op jit(solution)/shard_map/ppermute | solution.py:391
  75.0 1.6 %collective-permute-start.32 = (bf16[512,256]{1,0:T(8,128)(2,1)S(1)}, bf16[512,256]{1,0:T(8,128)(2,1)S(1)}, u32[]{:S(2)}, u32[]{:S(2)}) collective-permute-start(bf16[512,256]{1,0:T(8,128)(2,1)S(1)} %collective-permute-done.28.refs_0_), channel_id=1, source_target_pairs={{0,2},{1,3},{4,0},{5,1},{8,4},{9,5},{12,8},{13,9},{14,12},{15,13},... | collective-permute-start | bytes 786440 | tf_op jit(solution)/shard_map/ppermute | solution.py:391
  77.8 2.8 %collective-permute-done.30.refs_0_ = bf16[512,256]{1,0:T(8,128)(2,1)S(1)} collective-permute-done((bf16[512,256]{1,0:T(8,128)(2,1)S(1)}, bf16[512,256]{1,0:T(8,128)(2,1)S(1)}, u32[]{:S(2)}, u32[]{:S(2)}) %collective-permute-start.30) | collective-permute-done | bytes 262176 | tf_op jit(solution)/shard_map/ppermute | solution.py:391
  80.6 1.6 %collective-permute-start.34 = (bf16[256,256]{1,0:T(8,128)(2,1)S(1)}, bf16[256,256]{1,0:T(8,128)(2,1)S(1)}, u32[]{:S(2)}, u32[]{:S(2)}) collective-permute-start(bf16[256,256]{1,0:T(8,128)(2,1)S(1)} %slice.12), channel_id=1, source_target_pairs={{0,2},{1,3},{4,0},{5,1},{8,4},{9,5},{12,8},{13,9},{14,12},{15,13},... | collective-permute-start | bytes 393224 | tf_op jit(solution)/shard_map/ppermute | solution.py:391
  83.5 1.8 %collective-permute-done.32.refs_0_ = bf16[512,256]{1,0:T(8,128)(2,1)S(1)} collective-permute-done((bf16[512,256]{1,0:T(8,128)(2,1)S(1)}, bf16[512,256]{1,0:T(8,128)(2,1)S(1)}, u32[]{:S(2)}, u32[]{:S(2)}) %collective-permute-start.32) | collective-permute-done | bytes 262176 | tf_op jit(solution)/shard_map/ppermute | solution.py:391
  85.4 2.5 %collective-permute-start.36 = (bf16[256,256]{1,0:T(8,128)(2,1)S(1)}, bf16[256,256]{1,0:T(8,128)(2,1)S(1)}, u32[]{:S(2)}, u32[]{:S(2)}) collective-permute-start(bf16[256,256]{1,0:T(8,128)(2,1)S(1)} %slice.14), channel_id=1, source_target_pairs={{0,2},{1,3},{4,0},{5,1},{8,4},{9,5},{12,8},{13,9},{14,12},{15,13},... | collective-permute-start | bytes 393224 | tf_op jit(solution)/shard_map/ppermute | solution.py:391
  91.4 1.8 %collective-permute-done.37.refs_0_ = bf16[256,256]{1,0:T(8,128)(2,1)S(1)} collective-permute-done((bf16[256,256]{1,0:T(8,128)(2,1)S(1)}, bf16[256,256]{1,0:T(8,128)(2,1)S(1)}, u32[]{:S(2)}, u32[]{:S(2)}) %collective-permute-start.37) | collective-permute-done | bytes 131104 | tf_op jit(solution)/shard_map/ppermute | solution.py:391
  93.6 1.7 %collective-permute-done.38.got_ref = f32[384,256]{1,0:T(8,128)S(1)} collective-permute-done((f32[384,256]{1,0:T(8,128)S(1)}, f32[384,256]{1,0:T(8,128)S(1)}, u32[]{:S(2)}, u32[]{:S(2)}) %collective-permute-start.38) | collective-permute-done | bytes 393248 | tf_op jit(solution)/shard_map/ppermute | solution.py:396
  (119 shorter events, 27.3 us)
Async XLA Ops:
  5.6 6.8 %collective-permute-start.4 = (s16[528,128]{1,0:T(8,128)(2,1)S(1)}, s16[528,128]{1,0:T(8,128)(2,1)S(1)}, u32[]{:S(2)}, u32[]{:S(2)}) collective-permute-start(s16[528,128]{1,0:T(8,128)(2,1)S(1)} %get-tuple-element.76), channel_id=1, source_target_pairs={{0,2},{1,3},{4,0},{5,1},{8,4},{9,5},{12,8},{13,9},{14,12},{15,13},... | collective-permute-start | bytes 405512 | tf_op jit(solution)/shard_map/ppermute | solution.py:296
  8.6 6.2 %collective-permute-start.5 = (s16[528,128]{1,0:T(8,128)(2,1)S(1)}, s16[528,128]{1,0:T(8,128)(2,1)S(1)}, u32[]{:S(2)}, u32[]{:S(2)}) collective-permute-start(s16[528,128]{1,0:T(8,128)(2,1)S(1)} %get-tuple-element.73.before_ref), channel_id=1, source_target_pairs={{0,4},{1,5},{4,8},{5,9},{8,12},{9,13},{12,14},{13,15},{14,10},{15,... | collective-permute-start | bytes 405512 | tf_op jit(solution)/shard_map/ppermute | solution.py:295
  9.2 6.8 %collective-permute-start.7 = (s16[528,128]{1,0:T(8,128)(2,1)S(1)}, s16[528,128]{1,0:T(8,128)(2,1)S(1)}, u32[]{:S(2)}, u32[]{:S(2)}) collective-permute-start(s16[528,128]{1,0:T(8,128)(2,1)S(1)} %get-tuple-element.78), channel_id=1, source_target_pairs={{0,2},{1,3},{4,0},{5,1},{8,4},{9,5},{12,8},{13,9},{14,12},{15,13},... | collective-permute-start | bytes 405512 | tf_op jit(solution)/shard_map/ppermute | solution.py:296
  11.7 6.6 %collective-permute-start.8 = (s16[528,128]{1,0:T(8,128)(2,1)S(1)}, s16[528,128]{1,0:T(8,128)(2,1)S(1)}, u32[]{:S(2)}, u32[]{:S(2)}) collective-permute-start(s16[528,128]{1,0:T(8,128)(2,1)S(1)} %get-tuple-element.75.refs_0_), channel_id=1, source_target_pairs={{0,4},{1,5},{4,8},{5,9},{8,12},{9,13},{12,14},{13,15},{14,10},{15,... | collective-permute-start | bytes 405512 | tf_op jit(solution)/shard_map/ppermute | solution.py:295
  13.0 9.3 %collective-permute-start.9 = (s16[1040,128]{1,0:T(8,128)(2,1)S(1)}, s16[1040,128]{1,0:T(8,128)(2,1)S(1)}, u32[]{:S(2)}, u32[]{:S(2)}) collective-permute-start(s16[1040,128]{1,0:T(8,128)(2,1)S(1)} %sum_hop.12.before_ref), channel_id=1, source_target_pairs={{0,2},{1,3},{4,0},{5,1},{8,4},{9,5},{12,8},{13,9},{14,12},{15,13},... | collective-permute-start | bytes 798728 | tf_op jit(solution)/shard_map/ppermute | solution.py:313
  15.3 9.3 %collective-permute-start.10 = (s16[1040,128]{1,0:T(8,128)(2,1)S(1)}, s16[1040,128]{1,0:T(8,128)(2,1)S(1)}, u32[]{:S(2)}, u32[]{:S(2)}) collective-permute-start(s16[1040,128]{1,0:T(8,128)(2,1)S(1)} %sum_hop.13.refs_0_), channel_id=1, source_target_pairs={{0,4},{1,5},{4,8},{5,9},{8,12},{9,13},{12,14},{13,15},{14,10},{15,... | collective-permute-start | bytes 798728 | tf_op jit(solution)/shard_map/ppermute | solution.py:313
  15.9 17.8 %collective-permute-start.13 = (bf16[3,384,1024]{2,1,0:T(8,128)(2,1)S(1)}, bf16[3,384,1024]{2,1,0:T(8,128)(2,1)S(1)}, u32[]{:S(2)}, u32[]{:S(2)}) collective-permute-start(bf16[3,384,1024]{2,1,0:T(8,128)(2,1)S(1)} %pick_blocks.7.before_ref), channel_id=1, source_target_pairs={{0,1},{1,0},{2,3},{3,2},{4,5},{5,4},{6,7},{7,6},{8,9},{9,8},{10,11... | collective-permute-start | bytes 7077896 | tf_op jit(solution)/shard_map/ppermute | solution.py:244
  16.6 11.4 %collective-permute-start.11 = (s16[1040,128]{1,0:T(8,128)(2,1)S(1)}, s16[1040,128]{1,0:T(8,128)(2,1)S(1)}, u32[]{:S(2)}, u32[]{:S(2)}) collective-permute-start(s16[1040,128]{1,0:T(8,128)(2,1)S(1)} %sum_hop.14.before_ref), channel_id=1, source_target_pairs={{0,2},{1,3},{4,0},{5,1},{8,4},{9,5},{12,8},{13,9},{14,12},{15,13},... | collective-permute-start | bytes 798728 | tf_op jit(solution)/shard_map/ppermute | solution.py:313
  18.9 11.5 %collective-permute-start.12 = (s16[1040,128]{1,0:T(8,128)(2,1)S(1)}, s16[1040,128]{1,0:T(8,128)(2,1)S(1)}, u32[]{:S(2)}, u32[]{:S(2)}) collective-permute-start(s16[1040,128]{1,0:T(8,128)(2,1)S(1)} %sum_hop.15.before_ref), channel_id=1, source_target_pairs={{0,4},{1,5},{4,8},{5,9},{8,12},{9,13},{12,14},{13,15},{14,10},{15,... | collective-permute-start | bytes 798728 | tf_op jit(solution)/shard_map/ppermute | solution.py:313
  22.8 10.9 %collective-permute-start.14 = (s16[1040,128]{1,0:T(8,128)(2,1)S(1)}, s16[1040,128]{1,0:T(8,128)(2,1)S(1)}, u32[]{:S(2)}, u32[]{:S(2)}) collective-permute-start(s16[1040,128]{1,0:T(8,128)(2,1)S(1)} %sum_hop.16.before_ref), channel_id=1, source_target_pairs={{0,2},{1,3},{4,0},{5,1},{8,4},{9,5},{12,8},{13,9},{14,12},{15,13},... | collective-permute-start | bytes 798728 | tf_op jit(solution)/shard_map/ppermute | solution.py:313
  25.2 10.9 %collective-permute-start.15 = (s16[1040,128]{1,0:T(8,128)(2,1)S(1)}, s16[1040,128]{1,0:T(8,128)(2,1)S(1)}, u32[]{:S(2)}, u32[]{:S(2)}) collective-permute-start(s16[1040,128]{1,0:T(8,128)(2,1)S(1)} %sum_hop.17.before_ref), channel_id=1, source_target_pairs={{0,4},{1,5},{4,8},{5,9},{8,12},{9,13},{12,14},{13,15},{14,10},{15,... | collective-permute-start | bytes 798728 | tf_op jit(solution)/shard_map/ppermute | solution.py:313
  28.5 10.9 %collective-permute-start.16 = (s16[1040,128]{1,0:T(8,128)(2,1)S(1)}, s16[1040,128]{1,0:T(8,128)(2,1)S(1)}, u32[]{:S(2)}, u32[]{:S(2)}) collective-permute-start(s16[1040,128]{1,0:T(8,128)(2,1)S(1)} %sum_hop.18.before_ref), channel_id=1, source_target_pairs={{0,2},{1,3},{4,0},{5,1},{8,4},{9,5},{12,8},{13,9},{14,12},{15,13},... | collective-permute-start | bytes 798728 | tf_op jit(solution)/shard_map/ppermute | solution.py:313
  30.9 10.9 %collective-permute-start.17 = (s16[1040,128]{1,0:T(8,128)(2,1)S(1)}, s16[1040,128]{1,0:T(8,128)(2,1)S(1)}, u32[]{:S(2)}, u32[]{:S(2)}) collective-permute-start(s16[1040,128]{1,0:T(8,128)(2,1)S(1)} %sum_hop.19.before_ref), channel_id=1, source_target_pairs={{0,4},{1,5},{4,8},{5,9},{8,12},{9,13},{12,14},{13,15},{14,10},{15,... | collective-permute-start | bytes 798728 | tf_op jit(solution)/shard_map/ppermute | solution.py:313
  34.2 13.2 %collective-permute-start.19 = (s16[1040,128]{1,0:T(8,128)(2,1)S(1)}, s16[1040,128]{1,0:T(8,128)(2,1)S(1)}, u32[]{:S(2)}, u32[]{:S(2)}) collective-permute-start(s16[1040,128]{1,0:T(8,128)(2,1)S(1)} %sum_hop.20.before_ref), channel_id=1, source_target_pairs={{0,2},{1,3},{4,0},{5,1},{8,4},{9,5},{12,8},{13,9},{14,12},{15,13},... | collective-permute-start | bytes 798728 | tf_op jit(solution)/shard_map/ppermute | solution.py:313
  36.6 10.8 %collective-permute-start.18 = (s16[1040,128]{1,0:T(8,128)(2,1)S(1)}, s16[1040,128]{1,0:T(8,128)(2,1)S(1)}, u32[]{:S(2)}, u32[]{:S(2)}) collective-permute-start(s16[1040,128]{1,0:T(8,128)(2,1)S(1)} %sum_hop.21.before_ref), channel_id=1, source_target_pairs={{0,4},{1,5},{4,8},{5,9},{8,12},{9,13},{12,14},{13,15},{14,10},{15,... | collective-permute-start | bytes 798728 | tf_op jit(solution)/shard_map/ppermute | solution.py:313
  39.9 13.2 %collective-permute-start.21 = (s16[1040,128]{1,0:T(8,128)(2,1)S(1)}, s16[1040,128]{1,0:T(8,128)(2,1)S(1)}, u32[]{:S(2)}, u32[]{:S(2)}) collective-permute-start(s16[1040,128]{1,0:T(8,128)(2,1)S(1)} %sum_hop.22.before_ref), channel_id=1, source_target_pairs={{0,2},{1,3},{4,0},{5,1},{8,4},{9,5},{12,8},{13,9},{14,12},{15,13},... | collective-permute-start | bytes 798728 | tf_op jit(solution)/shard_map/ppermute | solution.py:313
  42.3 10.8 %collective-permute-start.20 = (s16[1040,128]{1,0:T(8,128)(2,1)S(1)}, s16[1040,128]{1,0:T(8,128)(2,1)S(1)}, u32[]{:S(2)}, u32[]{:S(2)}) collective-permute-start(s16[1040,128]{1,0:T(8,128)(2,1)S(1)} %sum_hop.23.before_ref), channel_id=1, source_target_pairs={{0,4},{1,5},{4,8},{5,9},{8,12},{9,13},{12,14},{13,15},{14,10},{15,... | collective-permute-start | bytes 798728 | tf_op jit(solution)/shard_map/ppermute | solution.py:313
  48.8 8.3 %collective-permute-start.22 = (bf16[512,256]{1,0:T(8,128)(2,1)S(1)}, bf16[512,256]{1,0:T(8,128)(2,1)S(1)}, u32[]{:S(2)}, u32[]{:S(2)}) collective-permute-start(bf16[512,256]{1,0:T(8,128)(2,1)S(1)} %get-tuple-element.79.before_ref.refs_0_), channel_id=1, source_target_pairs={{0,2},{1,3},{4,0},{5,1},{8,4},{9,5},{12,8},{13,9},{14,12},{15,13},... | collective-permute-start | bytes 786440 | tf_op jit(solution)/shard_map/ppermute | solution.py:391
  50.4 8.7 %collective-permute-start.23 = (bf16[512,256]{1,0:T(8,128)(2,1)S(1)}, bf16[512,256]{1,0:T(8,128)(2,1)S(1)}, u32[]{:S(2)}, u32[]{:S(2)}) collective-permute-start(bf16[512,256]{1,0:T(8,128)(2,1)S(1)} %get-tuple-element.79.before_ref.refs_0_), channel_id=1, source_target_pairs={{0,4},{1,5},{4,8},{5,9},{8,12},{9,13},{12,14},{13,15},{14,10},{15,... | collective-permute-start | bytes 786440 | tf_op jit(solution)/shard_map/ppermute | solution.py:391
  54.5 9.2 %collective-permute-start.24 = (bf16[512,256]{1,0:T(8,128)(2,1)S(1)}, bf16[512,256]{1,0:T(8,128)(2,1)S(1)}, u32[]{:S(2)}, u32[]{:S(2)}) collective-permute-start(bf16[512,256]{1,0:T(8,128)(2,1)S(1)} %get-tuple-element.84.before_ref.refs_3_), channel_id=1, source_target_pairs={{0,2},{1,3},{4,0},{5,1},{8,4},{9,5},{12,8},{13,9},{14,12},{15,13},... | collective-permute-start | bytes 786440 | tf_op jit(solution)/shard_map/ppermute | solution.py:391
  56.1 9.6 %collective-permute-start.25 = (bf16[512,256]{1,0:T(8,128)(2,1)S(1)}, bf16[512,256]{1,0:T(8,128)(2,1)S(1)}, u32[]{:S(2)}, u32[]{:S(2)}) collective-permute-start(bf16[512,256]{1,0:T(8,128)(2,1)S(1)} %get-tuple-element.84.before_ref.refs_3_), channel_id=1, source_target_pairs={{0,4},{1,5},{4,8},{5,9},{8,12},{9,13},{12,14},{13,15},{14,10},{15,... | collective-permute-start | bytes 786440 | tf_op jit(solution)/shard_map/ppermute | solution.py:391
  57.1 12.2 %collective-permute-start.26 = (bf16[512,256]{1,0:T(8,128)(2,1)S(1)}, bf16[512,256]{1,0:T(8,128)(2,1)S(1)}, u32[]{:S(2)}, u32[]{:S(2)}) collective-permute-start(bf16[512,256]{1,0:T(8,128)(2,1)S(1)} %collective-permute-done.22.refs_0_), channel_id=1, source_target_pairs={{0,2},{1,3},{4,0},{5,1},{8,4},{9,5},{12,8},{13,9},{14,12},{15,13},... | collective-permute-start | bytes 786440 | tf_op jit(solution)/shard_map/ppermute | solution.py:391
  59.1 12.2 %collective-permute-start.27 = (bf16[512,256]{1,0:T(8,128)(2,1)S(1)}, bf16[512,256]{1,0:T(8,128)(2,1)S(1)}, u32[]{:S(2)}, u32[]{:S(2)}) collective-permute-start(bf16[512,256]{1,0:T(8,128)(2,1)S(1)} %collective-permute-done.23.refs_0_), channel_id=1, source_target_pairs={{0,4},{1,5},{4,8},{5,9},{8,12},{9,13},{12,14},{13,15},{14,10},{15,... | collective-permute-start | bytes 786440 | tf_op jit(solution)/shard_map/ppermute | solution.py:391
  63.7 11.2 %collective-permute-start.28 = (bf16[512,256]{1,0:T(8,128)(2,1)S(1)}, bf16[512,256]{1,0:T(8,128)(2,1)S(1)}, u32[]{:S(2)}, u32[]{:S(2)}) collective-permute-start(bf16[512,256]{1,0:T(8,128)(2,1)S(1)} %collective-permute-done.24.refs_0_), channel_id=1, source_target_pairs={{0,2},{1,3},{4,0},{5,1},{8,4},{9,5},{12,8},{13,9},{14,12},{15,13},... | collective-permute-start | bytes 786440 | tf_op jit(solution)/shard_map/ppermute | solution.py:391
  65.7 11.2 %collective-permute-start.29 = (bf16[512,256]{1,0:T(8,128)(2,1)S(1)}, bf16[512,256]{1,0:T(8,128)(2,1)S(1)}, u32[]{:S(2)}, u32[]{:S(2)}) collective-permute-start(bf16[512,256]{1,0:T(8,128)(2,1)S(1)} %collective-permute-done.25.refs_0_), channel_id=1, source_target_pairs={{0,4},{1,5},{4,8},{5,9},{8,12},{9,13},{12,14},{13,15},{14,10},{15,... | collective-permute-start | bytes 786440 | tf_op jit(solution)/shard_map/ppermute | solution.py:391
  69.3 11.2 %collective-permute-start.30 = (bf16[512,256]{1,0:T(8,128)(2,1)S(1)}, bf16[512,256]{1,0:T(8,128)(2,1)S(1)}, u32[]{:S(2)}, u32[]{:S(2)}) collective-permute-start(bf16[512,256]{1,0:T(8,128)(2,1)S(1)} %collective-permute-done.26.refs_0_), channel_id=1, source_target_pairs={{0,2},{1,3},{4,0},{5,1},{8,4},{9,5},{12,8},{13,9},{14,12},{15,13},... | collective-permute-start | bytes 786440 | tf_op jit(solution)/shard_map/ppermute | solution.py:391
  71.3 11.3 %collective-permute-start.31 = (bf16[512,256]{1,0:T(8,128)(2,1)S(1)}, bf16[512,256]{1,0:T(8,128)(2,1)S(1)}, u32[]{:S(2)}, u32[]{:S(2)}) collective-permute-start(bf16[512,256]{1,0:T(8,128)(2,1)S(1)} %collective-permute-done.27.refs_0_), channel_id=1, source_target_pairs={{0,4},{1,5},{4,8},{5,9},{8,12},{9,13},{12,14},{13,15},{14,10},{15,... | collective-permute-start | bytes 786440 | tf_op jit(solution)/shard_map/ppermute | solution.py:391
  75.0 10.4 %collective-permute-start.32 = (bf16[512,256]{1,0:T(8,128)(2,1)S(1)}, bf16[512,256]{1,0:T(8,128)(2,1)S(1)}, u32[]{:S(2)}, u32[]{:S(2)}) collective-permute-start(bf16[512,256]{1,0:T(8,128)(2,1)S(1)} %collective-permute-done.28.refs_0_), channel_id=1, source_target_pairs={{0,2},{1,3},{4,0},{5,1},{8,4},{9,5},{12,8},{13,9},{14,12},{15,13},... | collective-permute-start | bytes 786440 | tf_op jit(solution)/shard_map/ppermute | solution.py:391
  76.9 11.3 %collective-permute-start.33 = (bf16[512,256]{1,0:T(8,128)(2,1)S(1)}, bf16[512,256]{1,0:T(8,128)(2,1)S(1)}, u32[]{:S(2)}, u32[]{:S(2)}) collective-permute-start(bf16[512,256]{1,0:T(8,128)(2,1)S(1)} %collective-permute-done.29.refs_0_), channel_id=1, source_target_pairs={{0,4},{1,5},{4,8},{5,9},{8,12},{9,13},{12,14},{13,15},{14,10},{15,... | collective-permute-start | bytes 786440 | tf_op jit(solution)/shard_map/ppermute | solution.py:391
  80.6 8.1 %collective-permute-start.34 = (bf16[256,256]{1,0:T(8,128)(2,1)S(1)}, bf16[256,256]{1,0:T(8,128)(2,1)S(1)}, u32[]{:S(2)}, u32[]{:S(2)}) collective-permute-start(bf16[256,256]{1,0:T(8,128)(2,1)S(1)} %slice.12), channel_id=1, source_target_pairs={{0,2},{1,3},{4,0},{5,1},{8,4},{9,5},{12,8},{13,9},{14,12},{15,13},... | collective-permute-start | bytes 393224 | tf_op jit(solution)/shard_map/ppermute | solution.py:391
  82.6 7.5 %collective-permute-start.35 = (bf16[256,256]{1,0:T(8,128)(2,1)S(1)}, bf16[256,256]{1,0:T(8,128)(2,1)S(1)}, u32[]{:S(2)}, u32[]{:S(2)}) collective-permute-start(bf16[256,256]{1,0:T(8,128)(2,1)S(1)} %slice.13), channel_id=1, source_target_pairs={{0,4},{1,5},{4,8},{5,9},{8,12},{9,13},{12,14},{13,15},{14,10},{15,... | collective-permute-start | bytes 393224 | tf_op jit(solution)/shard_map/ppermute | solution.py:391
  85.4 5.1 %collective-permute-start.36 = (bf16[256,256]{1,0:T(8,128)(2,1)S(1)}, bf16[256,256]{1,0:T(8,128)(2,1)S(1)}, u32[]{:S(2)}, u32[]{:S(2)}) collective-permute-start(bf16[256,256]{1,0:T(8,128)(2,1)S(1)} %slice.14), channel_id=1, source_target_pairs={{0,2},{1,3},{4,0},{5,1},{8,4},{9,5},{12,8},{13,9},{14,12},{15,13},... | collective-permute-start | bytes 393224 | tf_op jit(solution)/shard_map/ppermute | solution.py:391
  (21 other events, 77.8 us)

commit v10 on v9

--- a/solution.py
+++ b/solution.py
@@ -73,10 +73,11 @@
     out_ref[:, people:] = other_ref[...].T
 
 
-def own_columns(ring, own_ref, d, low, high):
+def own_columns(ring, own_ref, d, low, high, swapped=False):
     (owner,) = owners_of(ring, [d])
     block = own_ref.shape[1] // (2 * len(ring))
-    at = (2 * owner + lax.rem(lax.axis_index("ind"), 2)) * block + low
+    core = lax.rem(lax.axis_index("ind"), 2)
+    at = (2 * owner + (1 - core if swapped else core)) * block + low
     return own_ref[:, pl.ds(pl.multiple_of(at, LANES), high - low)]
 
 
@@ -138,32 +139,42 @@
     out_ref[...] = local_sum(res_ref, own, peer_ref[at[1]])
 
 
-def update_kernel(total, low, before_ref, corr_ref, right_ref, left_ref, incl_ref, mean_ref, prior_ref,
-                  scale_ref, *rest):
-    incl_new_ref, mean_new_ref, effect_ref = rest[-3:]
+def new_state(total, low, first, rows, refs):
+    corr_ref, right_ref, left_ref, incl_ref, mean_ref, prior_ref, scale_ref = refs
     height = corr_ref.shape[0]
     right, left = decode(right_ref), decode(left_ref)
     scale = scale_ref[...]
     shrink = scale / (1.0 + scale)
     start = prior_ref[...] - 0.5 * jnp.log1p(scale)
     steep = 0.5 * total * shrink
-    halves = [(right, 0), (left, 1)]
-    tiles = effect_ref.shape[0] // LANES
+    tiles = rows // LANES
     for k in range(tiles):
         corr = corr_ref[:, low + k * LANES : low + (k + 1) * LANES]
-        for got, way in halves:
+        for got, way in ((right, 0), (left, 1)):
             count = got.shape[0] // height
-            first = 0 if way == 0 else tiles - count
-            if first <= k < first + count:
-                corr = corr + got[(k - first) * height : (k - first + 1) * height, :]
-        rows = slice(k * LANES, (k + 1) * LANES)
-        incl = incl_ref[rows, :]
-        stat = corr.T / total + incl * mean_ref[rows, :]
+            skip = 0 if way == 0 else tiles - count
+            if skip <= k < skip + count:
+                corr = corr + got[(k - skip) * height : (k - skip + 1) * height, :]
+        at = slice(first + k * LANES, first + (k + 1) * LANES)
+        incl = incl_ref[at, :]
+        stat = corr.T * (1.0 / total) + incl * mean_ref[at, :]
         mean_new = stat * shrink
         incl_new = 0.5 * incl + 0.5 * jax.nn.sigmoid(start + steep * stat * stat)
+        yield slice(k * LANES, (k + 1) * LANES), incl_new, mean_new
+
+
+def effect_kernel(total, low, before_ref, *refs):
+    out_ref = refs[-1]
+    for rows, incl_new, mean_new in new_state(total, low, low, out_ref.shape[0], refs[:7]):
+        out_ref[rows, :] = (incl_new * mean_new).astype(jnp.bfloat16)
+
+
+def update_kernel(total, low, before_ref, *refs):
+    incl_new_ref, mean_new_ref = refs[-2:]
+    rows_all = incl_new_ref.shape[0]
+    for rows, incl_new, mean_new in new_state(total, low, 0, rows_all, refs[:7]):
         incl_new_ref[rows, :] = incl_new
         mean_new_ref[rows, :] = mean_new
-        effect_ref[rows, :] = (incl_new * mean_new).astype(jnp.bfloat16)
 
 
 def eta_kernel(ring, places, first, before_ref, *refs):
@@ -185,8 +196,15 @@
     out_other_ref[...] = other
 
 
-def end_kernel(eta_ref, got_ref, labels_ref, offset_ref, out_ref):
-    eta = eta_ref[...] + got_ref[...] + offset_ref[...]
+def end_kernel(
+    ring, places, genotype_ref, eta_ref, upper_ref, lower_ref, labels_ref, offset_ref, *refs
+):
+    out_ref = refs[-1]
+    got = jnp.concatenate([upper_ref[...], lower_ref[...]], axis=0)
+    eta = eta_ref[...] + got + offset_ref[...]
+    for effect_ref, (d, low, swapped) in zip(refs, places):
+        own = own_columns(ring, genotype_ref, d, low, low + effect_ref.shape[0], swapped)
+        eta = eta + jnp.dot(own, effect_ref[...], preferred_element_type=jnp.float32)
     out_ref[...] = 4.0 * (labels_ref[...].astype(jnp.float32) - jax.nn.sigmoid(eta))
 
 
@@ -331,11 +349,22 @@
     def full(shape):
         return pl.BlockSpec(shape, lambda i: (0,) * len(shape))
 
-    outs = ()
     effects = []
     for piece in range(pieces):
+        args = (near, got[0, piece], got[1, piece], incl_old, mean_old, prior, scale)
+        last = pl.pallas_call(
+            functools.partial(effect_kernel, total, piece * part),
+            in_specs=after(last, args),
+            out_shape=jax.ShapeDtypeStruct((part, cols), bf16),
+            compiler_params=params,
+            cost_estimate=light,
+            name="effect",
+        )(last, *args)
+        effects.append(last)
+
+    def update(piece, outs, before):
         rows = pl.BlockSpec((part, cols), lambda i, piece=piece: (piece, 0))
-        incl_new, mean_new, effect = pl.pallas_call(
+        return pl.pallas_call(
             functools.partial(update_kernel, total, piece * part),
             grid=(1,),
             in_specs=[anywhere, full((cols, block))]
@@ -343,20 +372,13 @@
             + [rows] * 2
             + [full((1, cols))] * 2
             + [anywhere] * len(outs),
-            out_specs=[rows, rows, full((part, cols))],
-            out_shape=[
-                jax.ShapeDtypeStruct((block, cols), f32),
-                jax.ShapeDtypeStruct((block, cols), f32),
-                jax.ShapeDtypeStruct((part, cols), bf16),
-            ],
+            out_specs=[rows, rows],
+            out_shape=[jax.ShapeDtypeStruct((block, cols), f32)] * 2,
             input_output_aliases={8: 0, 9: 1} if outs else {},
             compiler_params=params,
-            cost_estimate=light,
+            cost_estimate=small,
             name="update",
-        )(last, near, got[0, piece], got[1, piece], incl_old, mean_old, prior, scale, *outs)
-        outs = (incl_new, mean_new)
-        last = effect
-        effects.append(effect)
+        )(before, near, got[0, piece], got[1, piece], incl_old, mean_old, prior, scale, *outs)
 
     eta_shape = jax.ShapeDtypeStruct((people, cols), f32)
     def product(found, eta, before, cost):
@@ -376,8 +398,10 @@
         )(before, *args)
 
     eta = product([(0, piece * part, effects[piece]) for piece in range(pieces)], (), last, small)
+    last = eta[0]
     held = {(way, piece): effects[piece] for way in range(2) for piece in range(pieces)}
     etas = [eta[0]]
+    outs, updated, final = (), 0, []
     for hop in range(1, reach + 1):
         for piece in range(pieces):
             for way in (1, 0):
@@ -389,18 +413,35 @@
                     low = way * (part // 2)
                     message = message[low : low + part // 2]
                 held[way, piece] = lax.ppermute(message, "ind", left if way else right)
-                found = [(hop if way else size - hop, piece * part + low, held[way, piece])]
-                eta = product(found, eta, eta[0], small if len(etas) == 1 else light)
-                etas.append(eta[0])
-
-    eta_got = lax.ppermute(eta[1], "ind", swap)
+                found = (hop if way else size - hop, piece * part + low, held[way, piece])
+                if hop == reach and piece == pieces - 1:
+                    final.append(found)
+                    continue
+                eta = product([found], eta, last, small if len(etas) == 1 else light)
+                last = eta[0]
+                etas.append(last)
+        if updated < pieces and hop < reach:
+            outs = update(updated, outs, last)
+            last = outs[0]
+            updated += 1
+    while updated < pieces:
+        outs = update(updated, outs, last)
+        last = outs[0]
+        updated += 1
+
+    half = people // 2
+    eta_got = [lax.ppermute(eta[1][k : k + half], "ind", swap) for k in (0, half)]
+    places = [(d, low, False) for d, low, _ in final] + [(d, low, True) for d, low, _ in final]
+    args = (genotype, eta[0], *eta_got, labels, offset.reshape(1, cols))
+    args += tuple(effect for _, _, effect in final)
+    args += tuple(lax.ppermute(effect, "ind", swap) for _, _, effect in final)
     resid_new = pl.pallas_call(
-        end_kernel,
+        functools.partial(end_kernel, ring, places),
         out_shape=eta_shape,
         compiler_params=params,
         cost_estimate=light,
         name="new_residual",
-    )(eta[0], eta_got, labels, offset.reshape(1, cols))
+    )(*args)
     return (outs[0], outs[1], resid_new)
 
 

time: 96.4 us -> 95 us (0.985)
  waiting for transfers between devices: 35 us -> 31.9 us
  local copies, waits for them, and re-layouts: 1.6 us -> 2.58 us
    ppermute x16, waiting for transfers between devices: 16.1 us -> 12.7 us  [on_device(): held[way, piece] = lax.ppermute(message, 'ind', left if way else right)]
    pallas_call x3 -> x5, Pallas kernels: 3.55 us -> 4.55 us  [the longest x2 2.63 us: update(): pl.pallas_call(functools.partial(update_kernel, total, piece * part), gri...]
    unnamed x28 -> x24, local copies, waits for them, and re-layouts: 1.56 us -> 2.51 us
    pallas_call x17 -> x15, Pallas kernels: 6.09 us -> 5.56 us  [product(): pl.pallas_call(functools.partial(eta_kernel, ring, places, not eta), in_s...]
  transfers between devices with their start and end apart: 39 -> 42, of which waited for: 15 -> 17; matrix products, arithmetic and copies ran while one was open for 0% -> 0% of each run, Pallas kernels for 20% -> 21%
where the time goes in v10:
time: 95 us; the launch traced here: 94.7 us
  starting transfers between devices  37.3 us (39%)
  waiting for transfers between devices  31.9 us (34%)
  Pallas kernels  21.8 us (23%)
  local copies, waits for them, and re-layouts  2.58 us (3%)
  between operations  1.2 us (1%)
    ppermute x12, waiting for transfers between devices, on_device(): got[way, piece] = lax.ppermute(last, 'ind', left if way else right)  17.6 us
    ppermute x16, starting transfers between devices, on_device(): held[way, piece] = lax.ppermute(message, 'ind', left if way else right)  16.7 us
    ppermute x12, starting transfers between devices, on_device(): got[way, piece] = lax.ppermute(last, 'ind', left if way else right)  12.8 us
    ppermute x16, waiting for transfers between devices, on_device(): held[way, piece] = lax.ppermute(message, 'ind', left if way else right)  12.7 us
    pallas_call x12, Pallas kernels, on_device(): pl.pallas_call(functools.partial(hop_kernel, ring, (w, peer[w][1]), low,...  6.62 us
    ppermute x2, starting transfers between devices, on_device(): got[1, piece] = lax.ppermute(sent[1], 'ind', left)  5.61 us
    pallas_call x15, Pallas kernels, product(): pl.pallas_call(functools.partial(eta_kernel, ring, places, not eta), in_s...  5.56 us
    pallas_call x4, Pallas kernels, pick(): pl.pallas_call(functools.partial(pick_kernel, ring, wanted, block), in_sp...  3.21 us
  transfers between devices with their start and end apart: 42, of which 17 were waited for; matrix products, arithmetic and copies ran while one was open for 0% of the time, Pallas kernels for 21%

profile of v10, /device:TPU:0, one launch (start us, length us, event | category | flops | bytes accessed | tf_op | source)
XLA Modules:
  0.0 94.7 jit_solution(180375537889152063)
XLA Ops:
  2.5 1.7 %pick_blocks.5 = (bf16[1,384,512]{2,1,0:T(8,128)(2,1)S(1)}, bf16[1,384,512]{2,1,0:T(8,128)(2,1)S(1)}, bf16[2,384,1024]{2,1,0:T(8,128)(2,1)S(1)}) custom-call(bf16[384,16384]{1,0:T(8,128)(2,1)} %genotype_ref.9, bf16[1,384,512]{2,1,0:T(8,128)(2,1)S(1)} %get-tuple-element.61.refs_0_), custom_call_target="tpu_custom_call" | custom-call | flops 10000000000 | bytes 1000000 | tf_op jit(solution)/shard_map/pick_blocks/pallas_call | solution.py:241
  5.4 3.0 %collective-permute-start.4 = (s16[528,128]{1,0:T(8,128)(2,1)S(1)}, s16[528,128]{1,0:T(8,128)(2,1)S(1)}, u32[]{:S(2)}, u32[]{:S(2)}) collective-permute-start(s16[528,128]{1,0:T(8,128)(2,1)S(1)} %get-tuple-element.70), channel_id=1, source_target_pairs={{0,2},{1,3},{4,0},{5,1},{8,4},{9,5},{12,8},{13,9},{14,12},{15,13},... | collective-permute-start | bytes 405512 | tf_op jit(solution)/shard_map/ppermute | solution.py:314
  9.1 2.6 %collective-permute-start.7 = (s16[528,128]{1,0:T(8,128)(2,1)S(1)}, s16[528,128]{1,0:T(8,128)(2,1)S(1)}, u32[]{:S(2)}, u32[]{:S(2)}) collective-permute-start(s16[528,128]{1,0:T(8,128)(2,1)S(1)} %get-tuple-element.72), channel_id=1, source_target_pairs={{0,2},{1,3},{4,0},{5,1},{8,4},{9,5},{12,8},{13,9},{14,12},{15,13},... | collective-permute-start | bytes 405512 | tf_op jit(solution)/shard_map/ppermute | solution.py:314
  12.9 1.7 %collective-permute-start.9 = (s16[1040,128]{1,0:T(8,128)(2,1)S(1)}, s16[1040,128]{1,0:T(8,128)(2,1)S(1)}, u32[]{:S(2)}, u32[]{:S(2)}) collective-permute-start(s16[1040,128]{1,0:T(8,128)(2,1)S(1)} %sum_hop.12.before_ref), channel_id=1, source_target_pairs={{0,2},{1,3},{4,0},{5,1},{8,4},{9,5},{12,8},{13,9},{14,12},{15,13},... | collective-permute-start | bytes 798728 | tf_op jit(solution)/shard_map/ppermute | solution.py:331
  16.4 1.7 %collective-permute-start.11 = (s16[1040,128]{1,0:T(8,128)(2,1)S(1)}, s16[1040,128]{1,0:T(8,128)(2,1)S(1)}, u32[]{:S(2)}, u32[]{:S(2)}) collective-permute-start(s16[1040,128]{1,0:T(8,128)(2,1)S(1)} %sum_hop.14.before_ref), channel_id=1, source_target_pairs={{0,2},{1,3},{4,0},{5,1},{8,4},{9,5},{12,8},{13,9},{14,12},{15,13},... | collective-permute-start | bytes 798728 | tf_op jit(solution)/shard_map/ppermute | solution.py:331
  19.1 3.0 %collective-permute-done.9.got_ref = s16[1040,128]{1,0:T(8,128)(2,1)S(1)} collective-permute-done((s16[1040,128]{1,0:T(8,128)(2,1)S(1)}, s16[1040,128]{1,0:T(8,128)(2,1)S(1)}, u32[]{:S(2)}, u32[]{:S(2)}) %collective-permute-start.9) | collective-permute-done | bytes 266272 | tf_op jit(solution)/shard_map/ppermute | solution.py:331
  22.7 1.7 %collective-permute-start.14 = (s16[1040,128]{1,0:T(8,128)(2,1)S(1)}, s16[1040,128]{1,0:T(8,128)(2,1)S(1)}, u32[]{:S(2)}, u32[]{:S(2)}) collective-permute-start(s16[1040,128]{1,0:T(8,128)(2,1)S(1)} %sum_hop.16.before_ref), channel_id=1, source_target_pairs={{0,2},{1,3},{4,0},{5,1},{8,4},{9,5},{12,8},{13,9},{14,12},{15,13},... | collective-permute-start | bytes 798728 | tf_op jit(solution)/shard_map/ppermute | solution.py:331
  25.4 2.4 %collective-permute-done.11.got_ref = s16[1040,128]{1,0:T(8,128)(2,1)S(1)} collective-permute-done((s16[1040,128]{1,0:T(8,128)(2,1)S(1)}, s16[1040,128]{1,0:T(8,128)(2,1)S(1)}, u32[]{:S(2)}, u32[]{:S(2)}) %collective-permute-start.11) | collective-permute-done | bytes 266272 | tf_op jit(solution)/shard_map/ppermute | solution.py:331
  28.4 1.7 %collective-permute-start.16 = (s16[1040,128]{1,0:T(8,128)(2,1)S(1)}, s16[1040,128]{1,0:T(8,128)(2,1)S(1)}, u32[]{:S(2)}, u32[]{:S(2)}) collective-permute-start(s16[1040,128]{1,0:T(8,128)(2,1)S(1)} %sum_hop.18.before_ref), channel_id=1, source_target_pairs={{0,2},{1,3},{4,0},{5,1},{8,4},{9,5},{12,8},{13,9},{14,12},{15,13},... | collective-permute-start | bytes 798728 | tf_op jit(solution)/shard_map/ppermute | solution.py:331
  31.1 2.4 %collective-permute-done.14.got_ref = s16[1040,128]{1,0:T(8,128)(2,1)S(1)} collective-permute-done((s16[1040,128]{1,0:T(8,128)(2,1)S(1)}, s16[1040,128]{1,0:T(8,128)(2,1)S(1)}, u32[]{:S(2)}, u32[]{:S(2)}) %collective-permute-start.14) | collective-permute-done | bytes 266272 | tf_op jit(solution)/shard_map/ppermute | solution.py:331
  34.1 1.7 %collective-permute-start.19 = (s16[1040,128]{1,0:T(8,128)(2,1)S(1)}, s16[1040,128]{1,0:T(8,128)(2,1)S(1)}, u32[]{:S(2)}, u32[]{:S(2)}) collective-permute-start(s16[1040,128]{1,0:T(8,128)(2,1)S(1)} %sum_hop.20.before_ref), channel_id=1, source_target_pairs={{0,2},{1,3},{4,0},{5,1},{8,4},{9,5},{12,8},{13,9},{14,12},{15,13},... | collective-permute-start | bytes 798728 | tf_op jit(solution)/shard_map/ppermute | solution.py:331
  36.8 2.4 %collective-permute-done.16.got_ref = s16[1040,128]{1,0:T(8,128)(2,1)S(1)} collective-permute-done((s16[1040,128]{1,0:T(8,128)(2,1)S(1)}, s16[1040,128]{1,0:T(8,128)(2,1)S(1)}, u32[]{:S(2)}, u32[]{:S(2)}) %collective-permute-start.16) | collective-permute-done | bytes 266272 | tf_op jit(solution)/shard_map/ppermute | solution.py:331
  39.8 1.7 %collective-permute-start.21 = (s16[1040,128]{1,0:T(8,128)(2,1)S(1)}, s16[1040,128]{1,0:T(8,128)(2,1)S(1)}, u32[]{:S(2)}, u32[]{:S(2)}) collective-permute-start(s16[1040,128]{1,0:T(8,128)(2,1)S(1)} %sum_hop.22.before_ref), channel_id=1, source_target_pairs={{0,2},{1,3},{4,0},{5,1},{8,4},{9,5},{12,8},{13,9},{14,12},{15,13},... | collective-permute-start | bytes 798728 | tf_op jit(solution)/shard_map/ppermute | solution.py:331
  43.3 4.0 %collective-permute-done.18.refs_1_ = s16[1040,128]{1,0:T(8,128)(2,1)S(1)} collective-permute-done((s16[1040,128]{1,0:T(8,128)(2,1)S(1)}, s16[1040,128]{1,0:T(8,128)(2,1)S(1)}, u32[]{:S(2)}, u32[]{:S(2)}) %collective-permute-start.18) | collective-permute-done | bytes 266272 | tf_op jit(solution)/shard_map/ppermute | solution.py:331
  47.7 1.6 %collective-permute-start.22 = (bf16[512,256]{1,0:T(8,128)(2,1)S(1)}, bf16[512,256]{1,0:T(8,128)(2,1)S(1)}, u32[]{:S(2)}, u32[]{:S(2)}) collective-permute-start(bf16[512,256]{1,0:T(8,128)(2,1)S(1)} %effect.2.before_ref.refs_0_), channel_id=1, source_target_pairs={{0,2},{1,3},{4,0},{5,1},{8,4},{9,5},{12,8},{13,9},{14,12},{15,13},... | collective-permute-start | bytes 786440 | tf_op jit(solution)/shard_map/ppermute | solution.py:415
  49.8 3.2 %collective-permute-done.20.refs_1_ = s16[1040,128]{1,0:T(8,128)(2,1)S(1)} collective-permute-done((s16[1040,128]{1,0:T(8,128)(2,1)S(1)}, s16[1040,128]{1,0:T(8,128)(2,1)S(1)}, u32[]{:S(2)}, u32[]{:S(2)}) %collective-permute-start.20) | collective-permute-done | bytes 266272 | tf_op jit(solution)/shard_map/ppermute | solution.py:331
  53.4 1.6 %collective-permute-start.24 = (bf16[512,256]{1,0:T(8,128)(2,1)S(1)}, bf16[512,256]{1,0:T(8,128)(2,1)S(1)}, u32[]{:S(2)}, u32[]{:S(2)}) collective-permute-start(bf16[512,256]{1,0:T(8,128)(2,1)S(1)} %effect.3.before_ref.refs_3_), channel_id=1, source_target_pairs={{0,2},{1,3},{4,0},{5,1},{8,4},{9,5},{12,8},{13,9},{14,12},{15,13},... | collective-permute-start | bytes 786440 | tf_op jit(solution)/shard_map/ppermute | solution.py:415
  57.0 1.6 %collective-permute-start.26 = (bf16[512,256]{1,0:T(8,128)(2,1)S(1)}, bf16[512,256]{1,0:T(8,128)(2,1)S(1)}, u32[]{:S(2)}, u32[]{:S(2)}) collective-permute-start(bf16[512,256]{1,0:T(8,128)(2,1)S(1)} %collective-permute-done.22.refs_0_), channel_id=1, source_target_pairs={{0,2},{1,3},{4,0},{5,1},{8,4},{9,5},{12,8},{13,9},{14,12},{15,13},... | collective-permute-start | bytes 786440 | tf_op jit(solution)/shard_map/ppermute | solution.py:415
  59.8 2.8 %collective-permute-done.24.refs_0_ = bf16[512,256]{1,0:T(8,128)(2,1)S(1)} collective-permute-done((bf16[512,256]{1,0:T(8,128)(2,1)S(1)}, bf16[512,256]{1,0:T(8,128)(2,1)S(1)}, u32[]{:S(2)}, u32[]{:S(2)}) %collective-permute-start.24) | collective-permute-done | bytes 262176 | tf_op jit(solution)/shard_map/ppermute | solution.py:415
  62.7 1.5 %collective-permute-start.28 = (bf16[512,256]{1,0:T(8,128)(2,1)S(1)}, bf16[512,256]{1,0:T(8,128)(2,1)S(1)}, u32[]{:S(2)}, u32[]{:S(2)}) collective-permute-start(bf16[512,256]{1,0:T(8,128)(2,1)S(1)} %collective-permute-done.24.refs_0_), channel_id=1, source_target_pairs={{0,2},{1,3},{4,0},{5,1},{8,4},{9,5},{12,8},{13,9},{14,12},{15,13},... | collective-permute-start | bytes 786440 | tf_op jit(solution)/shard_map/ppermute | solution.py:415
  65.5 1.3 %update.2 = (f32[1024,256]{1,0:T(8,128)}, f32[1024,256]{1,0:T(8,128)}) custom-call(f32[384,256]{1,0:T(8,128)S(1)} %get-tuple-element.81.before_ref.refs_3_, f32[256,1024]{1,0:T(8,128)S(1)} %sum_near.1.before_ref.refs_0_, s16[1040,128]{1,0:T(8,128)(2,1)S(1)} %collective-permute-done.18.refs_1_, s16[1040,128]{1,0:T(8,128)(2,1)S(1)} %collective-permute-done.19.refs_2_, ...), custom_call_target="tpu_custom_call" | custom-call | flops 1 | bytes 1 | tf_op jit(solution)/shard_map/update/pallas_call | solution.py:367
  66.8 1.5 %collective-permute-done.26.refs_0_ = bf16[512,256]{1,0:T(8,128)(2,1)S(1)} collective-permute-done((bf16[512,256]{1,0:T(8,128)(2,1)S(1)}, bf16[512,256]{1,0:T(8,128)(2,1)S(1)}, u32[]{:S(2)}, u32[]{:S(2)}) %collective-permute-start.26) | collective-permute-done | bytes 262176 | tf_op jit(solution)/shard_map/ppermute | solution.py:415
  68.3 1.5 %collective-permute-start.30 = (bf16[512,256]{1,0:T(8,128)(2,1)S(1)}, bf16[512,256]{1,0:T(8,128)(2,1)S(1)}, u32[]{:S(2)}, u32[]{:S(2)}) collective-permute-start(bf16[512,256]{1,0:T(8,128)(2,1)S(1)} %collective-permute-done.26.refs_0_), channel_id=1, source_target_pairs={{0,2},{1,3},{4,0},{5,1},{8,4},{9,5},{12,8},{13,9},{14,12},{15,13},... | collective-permute-start | bytes 786440 | tf_op jit(solution)/shard_map/ppermute | solution.py:415
  69.8 1.2 %copy-done = f32[1024,256]{1,0:T(8,128)S(1)} copy-done((f32[1024,256]{1,0:T(8,128)S(1)}, f32[1024,256]{1,0:T(8,128)}, u32[]{:S(2)}) %copy-start) | copy-done | bytes 1048600
  72.4 1.5 %collective-permute-done.28.refs_0_ = bf16[512,256]{1,0:T(8,128)(2,1)S(1)} collective-permute-done((bf16[512,256]{1,0:T(8,128)(2,1)S(1)}, bf16[512,256]{1,0:T(8,128)(2,1)S(1)}, u32[]{:S(2)}, u32[]{:S(2)}) %collective-permute-start.28) | collective-permute-done | bytes 262176 | tf_op jit(solution)/shard_map/ppermute | solution.py:415
  73.9 1.5 %collective-permute-start.32 = (bf16[512,256]{1,0:T(8,128)(2,1)S(1)}, bf16[512,256]{1,0:T(8,128)(2,1)S(1)}, u32[]{:S(2)}, u32[]{:S(2)}) collective-permute-start(bf16[512,256]{1,0:T(8,128)(2,1)S(1)} %collective-permute-done.28.refs_0_), channel_id=1, source_target_pairs={{0,2},{1,3},{4,0},{5,1},{8,4},{9,5},{12,8},{13,9},{14,12},{15,13},... | collective-permute-start | bytes 786440 | tf_op jit(solution)/shard_map/ppermute | solution.py:415
  76.7 1.3 %update.3 = (f32[1024,256]{1,0:T(8,128)}, f32[1024,256]{1,0:T(8,128)}) custom-call(f32[384,256]{1,0:T(8,128)S(1)} %get-tuple-element.94.before_ref.refs_3_, f32[256,1024]{1,0:T(8,128)S(1)} %sum_near.1.before_ref.refs_0_, s16[1040,128]{1,0:T(8,128)(2,1)S(1)} %collective-permute-done.20.refs_1_, ...), custom_call_target="tpu_custom_call", output_to_operand_aliasing={{0}: (8, {}), {1}: (9, {})} | custom-call | flops 1 | bytes 1 | tf_op jit(solution)/shard_map/update/pallas_call | solution.py:367
  78.1 1.4 %collective-permute-done.30.refs_0_ = bf16[512,256]{1,0:T(8,128)(2,1)S(1)} collective-permute-done((bf16[512,256]{1,0:T(8,128)(2,1)S(1)}, bf16[512,256]{1,0:T(8,128)(2,1)S(1)}, u32[]{:S(2)}, u32[]{:S(2)}) %collective-permute-start.30) | collective-permute-done | bytes 262176 | tf_op jit(solution)/shard_map/ppermute | solution.py:415
  79.5 1.6 %collective-permute-start.34 = (bf16[256,256]{1,0:T(8,128)(2,1)S(1)}, bf16[256,256]{1,0:T(8,128)(2,1)S(1)}, u32[]{:S(2)}, u32[]{:S(2)}) collective-permute-start(bf16[256,256]{1,0:T(8,128)(2,1)S(1)} %slice.18), channel_id=1, source_target_pairs={{0,2},{1,3},{4,0},{5,1},{8,4},{9,5},{12,8},{13,9},{14,12},{15,13},... | collective-permute-start | bytes 393224 | tf_op jit(solution)/shard_map/ppermute | solution.py:415
  81.1 1.2 %copy-done.1 = f32[1024,256]{1,0:T(8,128)S(1)} copy-done((f32[1024,256]{1,0:T(8,128)S(1)}, f32[1024,256]{1,0:T(8,128)}, u32[]{:S(2)}) %copy-start.1) | copy-done | bytes 1048600
  83.7 3.0 %collective-permute-done.33.refs_0_ = bf16[512,256]{1,0:T(8,128)(2,1)S(1)} collective-permute-done((bf16[512,256]{1,0:T(8,128)(2,1)S(1)}, bf16[512,256]{1,0:T(8,128)(2,1)S(1)}, u32[]{:S(2)}, u32[]{:S(2)}) %collective-permute-start.33) | collective-permute-done | bytes 262176 | tf_op jit(solution)/shard_map/ppermute | solution.py:415
  87.2 1.5 %collective-permute-start.38 = (bf16[256,256]{1,0:T(8,128)(2,1)S(1)}, bf16[256,256]{1,0:T(8,128)(2,1)S(1)}, u32[]{:S(2)}, u32[]{:S(2)}) collective-permute-start(bf16[256,256]{1,0:T(8,128)(2,1)S(1)} %slice.22), channel_id=1, source_target_pairs={{0,2},{1,3},{4,0},{5,1},{8,4},{9,5},{12,8},{13,9},{14,12},{15,13},... | collective-permute-start | bytes 393224 | tf_op jit(solution)/shard_map/ppermute | solution.py:415
  (122 shorter events, 30.5 us)
Async XLA Ops:
  5.4 6.9 %collective-permute-start.4 = (s16[528,128]{1,0:T(8,128)(2,1)S(1)}, s16[528,128]{1,0:T(8,128)(2,1)S(1)}, u32[]{:S(2)}, u32[]{:S(2)}) collective-permute-start(s16[528,128]{1,0:T(8,128)(2,1)S(1)} %get-tuple-element.70), channel_id=1, source_target_pairs={{0,2},{1,3},{4,0},{5,1},{8,4},{9,5},{12,8},{13,9},{14,12},{15,13},... | collective-permute-start | bytes 405512 | tf_op jit(solution)/shard_map/ppermute | solution.py:314
  8.4 6.2 %collective-permute-start.5 = (s16[528,128]{1,0:T(8,128)(2,1)S(1)}, s16[528,128]{1,0:T(8,128)(2,1)S(1)}, u32[]{:S(2)}, u32[]{:S(2)}) collective-permute-start(s16[528,128]{1,0:T(8,128)(2,1)S(1)} %get-tuple-element.67.before_ref), channel_id=1, source_target_pairs={{0,4},{1,5},{4,8},{5,9},{8,12},{9,13},{12,14},{13,15},{14,10},{15,... | collective-permute-start | bytes 405512 | tf_op jit(solution)/shard_map/ppermute | solution.py:313
  9.1 6.8 %collective-permute-start.7 = (s16[528,128]{1,0:T(8,128)(2,1)S(1)}, s16[528,128]{1,0:T(8,128)(2,1)S(1)}, u32[]{:S(2)}, u32[]{:S(2)}) collective-permute-start(s16[528,128]{1,0:T(8,128)(2,1)S(1)} %get-tuple-element.72), channel_id=1, source_target_pairs={{0,2},{1,3},{4,0},{5,1},{8,4},{9,5},{12,8},{13,9},{14,12},{15,13},... | collective-permute-start | bytes 405512 | tf_op jit(solution)/shard_map/ppermute | solution.py:314
  11.7 6.5 %collective-permute-start.8 = (s16[528,128]{1,0:T(8,128)(2,1)S(1)}, s16[528,128]{1,0:T(8,128)(2,1)S(1)}, u32[]{:S(2)}, u32[]{:S(2)}) collective-permute-start(s16[528,128]{1,0:T(8,128)(2,1)S(1)} %get-tuple-element.69.refs_0_), channel_id=1, source_target_pairs={{0,4},{1,5},{4,8},{5,9},{8,12},{9,13},{12,14},{13,15},{14,10},{15,... | collective-permute-start | bytes 405512 | tf_op jit(solution)/shard_map/ppermute | solution.py:313
  12.9 9.2 %collective-permute-start.9 = (s16[1040,128]{1,0:T(8,128)(2,1)S(1)}, s16[1040,128]{1,0:T(8,128)(2,1)S(1)}, u32[]{:S(2)}, u32[]{:S(2)}) collective-permute-start(s16[1040,128]{1,0:T(8,128)(2,1)S(1)} %sum_hop.12.before_ref), channel_id=1, source_target_pairs={{0,2},{1,3},{4,0},{5,1},{8,4},{9,5},{12,8},{13,9},{14,12},{15,13},... | collective-permute-start | bytes 798728 | tf_op jit(solution)/shard_map/ppermute | solution.py:331
  15.2 9.3 %collective-permute-start.10 = (s16[1040,128]{1,0:T(8,128)(2,1)S(1)}, s16[1040,128]{1,0:T(8,128)(2,1)S(1)}, u32[]{:S(2)}, u32[]{:S(2)}) collective-permute-start(s16[1040,128]{1,0:T(8,128)(2,1)S(1)} %sum_hop.13.refs_0_), channel_id=1, source_target_pairs={{0,4},{1,5},{4,8},{5,9},{8,12},{9,13},{12,14},{13,15},{14,10},{15,... | collective-permute-start | bytes 798728 | tf_op jit(solution)/shard_map/ppermute | solution.py:331
  15.8 17.8 %collective-permute-start.13 = (bf16[3,384,1024]{2,1,0:T(8,128)(2,1)S(1)}, bf16[3,384,1024]{2,1,0:T(8,128)(2,1)S(1)}, u32[]{:S(2)}, u32[]{:S(2)}) collective-permute-start(bf16[3,384,1024]{2,1,0:T(8,128)(2,1)S(1)} %pick_blocks.7.before_ref), channel_id=1, source_target_pairs={{0,1},{1,0},{2,3},{3,2},{4,5},{5,4},{6,7},{7,6},{8,9},{9,8},{10,11... | collective-permute-start | bytes 7077896 | tf_op jit(solution)/shard_map/ppermute | solution.py:262
  16.4 11.4 %collective-permute-start.11 = (s16[1040,128]{1,0:T(8,128)(2,1)S(1)}, s16[1040,128]{1,0:T(8,128)(2,1)S(1)}, u32[]{:S(2)}, u32[]{:S(2)}) collective-permute-start(s16[1040,128]{1,0:T(8,128)(2,1)S(1)} %sum_hop.14.before_ref), channel_id=1, source_target_pairs={{0,2},{1,3},{4,0},{5,1},{8,4},{9,5},{12,8},{13,9},{14,12},{15,13},... | collective-permute-start | bytes 798728 | tf_op jit(solution)/shard_map/ppermute | solution.py:331
  18.7 11.4 %collective-permute-start.12 = (s16[1040,128]{1,0:T(8,128)(2,1)S(1)}, s16[1040,128]{1,0:T(8,128)(2,1)S(1)}, u32[]{:S(2)}, u32[]{:S(2)}) collective-permute-start(s16[1040,128]{1,0:T(8,128)(2,1)S(1)} %sum_hop.15.before_ref), channel_id=1, source_target_pairs={{0,4},{1,5},{4,8},{5,9},{8,12},{9,13},{12,14},{13,15},{14,10},{15,... | collective-permute-start | bytes 798728 | tf_op jit(solution)/shard_map/ppermute | solution.py:331
  22.7 10.8 %collective-permute-start.14 = (s16[1040,128]{1,0:T(8,128)(2,1)S(1)}, s16[1040,128]{1,0:T(8,128)(2,1)S(1)}, u32[]{:S(2)}, u32[]{:S(2)}) collective-permute-start(s16[1040,128]{1,0:T(8,128)(2,1)S(1)} %sum_hop.16.before_ref), channel_id=1, source_target_pairs={{0,2},{1,3},{4,0},{5,1},{8,4},{9,5},{12,8},{13,9},{14,12},{15,13},... | collective-permute-start | bytes 798728 | tf_op jit(solution)/shard_map/ppermute | solution.py:331
  25.0 10.8 %collective-permute-start.15 = (s16[1040,128]{1,0:T(8,128)(2,1)S(1)}, s16[1040,128]{1,0:T(8,128)(2,1)S(1)}, u32[]{:S(2)}, u32[]{:S(2)}) collective-permute-start(s16[1040,128]{1,0:T(8,128)(2,1)S(1)} %sum_hop.17.before_ref), channel_id=1, source_target_pairs={{0,4},{1,5},{4,8},{5,9},{8,12},{9,13},{12,14},{13,15},{14,10},{15,... | collective-permute-start | bytes 798728 | tf_op jit(solution)/shard_map/ppermute | solution.py:331
  28.4 10.9 %collective-permute-start.16 = (s16[1040,128]{1,0:T(8,128)(2,1)S(1)}, s16[1040,128]{1,0:T(8,128)(2,1)S(1)}, u32[]{:S(2)}, u32[]{:S(2)}) collective-permute-start(s16[1040,128]{1,0:T(8,128)(2,1)S(1)} %sum_hop.18.before_ref), channel_id=1, source_target_pairs={{0,2},{1,3},{4,0},{5,1},{8,4},{9,5},{12,8},{13,9},{14,12},{15,13},... | collective-permute-start | bytes 798728 | tf_op jit(solution)/shard_map/ppermute | solution.py:331
  30.7 10.9 %collective-permute-start.17 = (s16[1040,128]{1,0:T(8,128)(2,1)S(1)}, s16[1040,128]{1,0:T(8,128)(2,1)S(1)}, u32[]{:S(2)}, u32[]{:S(2)}) collective-permute-start(s16[1040,128]{1,0:T(8,128)(2,1)S(1)} %sum_hop.19.before_ref), channel_id=1, source_target_pairs={{0,4},{1,5},{4,8},{5,9},{8,12},{9,13},{12,14},{13,15},{14,10},{15,... | collective-permute-start | bytes 798728 | tf_op jit(solution)/shard_map/ppermute | solution.py:331
  34.1 13.2 %collective-permute-start.19 = (s16[1040,128]{1,0:T(8,128)(2,1)S(1)}, s16[1040,128]{1,0:T(8,128)(2,1)S(1)}, u32[]{:S(2)}, u32[]{:S(2)}) collective-permute-start(s16[1040,128]{1,0:T(8,128)(2,1)S(1)} %sum_hop.20.before_ref), channel_id=1, source_target_pairs={{0,2},{1,3},{4,0},{5,1},{8,4},{9,5},{12,8},{13,9},{14,12},{15,13},... | collective-permute-start | bytes 798728 | tf_op jit(solution)/shard_map/ppermute | solution.py:331
  36.4 10.8 %collective-permute-start.18 = (s16[1040,128]{1,0:T(8,128)(2,1)S(1)}, s16[1040,128]{1,0:T(8,128)(2,1)S(1)}, u32[]{:S(2)}, u32[]{:S(2)}) collective-permute-start(s16[1040,128]{1,0:T(8,128)(2,1)S(1)} %sum_hop.21.before_ref), channel_id=1, source_target_pairs={{0,4},{1,5},{4,8},{5,9},{8,12},{9,13},{12,14},{13,15},{14,10},{15,... | collective-permute-start | bytes 798728 | tf_op jit(solution)/shard_map/ppermute | solution.py:331
  39.8 13.2 %collective-permute-start.21 = (s16[1040,128]{1,0:T(8,128)(2,1)S(1)}, s16[1040,128]{1,0:T(8,128)(2,1)S(1)}, u32[]{:S(2)}, u32[]{:S(2)}) collective-permute-start(s16[1040,128]{1,0:T(8,128)(2,1)S(1)} %sum_hop.22.before_ref), channel_id=1, source_target_pairs={{0,2},{1,3},{4,0},{5,1},{8,4},{9,5},{12,8},{13,9},{14,12},{15,13},... | collective-permute-start | bytes 798728 | tf_op jit(solution)/shard_map/ppermute | solution.py:331
  42.2 10.8 %collective-permute-start.20 = (s16[1040,128]{1,0:T(8,128)(2,1)S(1)}, s16[1040,128]{1,0:T(8,128)(2,1)S(1)}, u32[]{:S(2)}, u32[]{:S(2)}) collective-permute-start(s16[1040,128]{1,0:T(8,128)(2,1)S(1)} %sum_hop.23.before_ref), channel_id=1, source_target_pairs={{0,4},{1,5},{4,8},{5,9},{8,12},{9,13},{12,14},{13,15},{14,10},{15,... | collective-permute-start | bytes 798728 | tf_op jit(solution)/shard_map/ppermute | solution.py:331
  47.7 9.3 %collective-permute-start.22 = (bf16[512,256]{1,0:T(8,128)(2,1)S(1)}, bf16[512,256]{1,0:T(8,128)(2,1)S(1)}, u32[]{:S(2)}, u32[]{:S(2)}) collective-permute-start(bf16[512,256]{1,0:T(8,128)(2,1)S(1)} %effect.2.before_ref.refs_0_), channel_id=1, source_target_pairs={{0,2},{1,3},{4,0},{5,1},{8,4},{9,5},{12,8},{13,9},{14,12},{15,13},... | collective-permute-start | bytes 786440 | tf_op jit(solution)/shard_map/ppermute | solution.py:415
  49.3 9.6 %collective-permute-start.23 = (bf16[512,256]{1,0:T(8,128)(2,1)S(1)}, bf16[512,256]{1,0:T(8,128)(2,1)S(1)}, u32[]{:S(2)}, u32[]{:S(2)}) collective-permute-start(bf16[512,256]{1,0:T(8,128)(2,1)S(1)} %effect.2.before_ref.refs_0_), channel_id=1, source_target_pairs={{0,4},{1,5},{4,8},{5,9},{8,12},{9,13},{12,14},{13,15},{14,10},{15,... | collective-permute-start | bytes 786440 | tf_op jit(solution)/shard_map/ppermute | solution.py:415
  53.4 9.3 %collective-permute-start.24 = (bf16[512,256]{1,0:T(8,128)(2,1)S(1)}, bf16[512,256]{1,0:T(8,128)(2,1)S(1)}, u32[]{:S(2)}, u32[]{:S(2)}) collective-permute-start(bf16[512,256]{1,0:T(8,128)(2,1)S(1)} %effect.3.before_ref.refs_3_), channel_id=1, source_target_pairs={{0,2},{1,3},{4,0},{5,1},{8,4},{9,5},{12,8},{13,9},{14,12},{15,13},... | collective-permute-start | bytes 786440 | tf_op jit(solution)/shard_map/ppermute | solution.py:415
  55.0 9.6 %collective-permute-start.25 = (bf16[512,256]{1,0:T(8,128)(2,1)S(1)}, bf16[512,256]{1,0:T(8,128)(2,1)S(1)}, u32[]{:S(2)}, u32[]{:S(2)}) collective-permute-start(bf16[512,256]{1,0:T(8,128)(2,1)S(1)} %effect.3.before_ref.refs_3_), channel_id=1, source_target_pairs={{0,4},{1,5},{4,8},{5,9},{8,12},{9,13},{12,14},{13,15},{14,10},{15,... | collective-permute-start | bytes 786440 | tf_op jit(solution)/shard_map/ppermute | solution.py:415
  57.0 11.3 %collective-permute-start.26 = (bf16[512,256]{1,0:T(8,128)(2,1)S(1)}, bf16[512,256]{1,0:T(8,128)(2,1)S(1)}, u32[]{:S(2)}, u32[]{:S(2)}) collective-permute-start(bf16[512,256]{1,0:T(8,128)(2,1)S(1)} %collective-permute-done.22.refs_0_), channel_id=1, source_target_pairs={{0,2},{1,3},{4,0},{5,1},{8,4},{9,5},{12,8},{13,9},{14,12},{15,13},... | collective-permute-start | bytes 786440 | tf_op jit(solution)/shard_map/ppermute | solution.py:415
  59.0 12.5 %collective-permute-start.27 = (bf16[512,256]{1,0:T(8,128)(2,1)S(1)}, bf16[512,256]{1,0:T(8,128)(2,1)S(1)}, u32[]{:S(2)}, u32[]{:S(2)}) collective-permute-start(bf16[512,256]{1,0:T(8,128)(2,1)S(1)} %collective-permute-done.23.refs_0_), channel_id=1, source_target_pairs={{0,4},{1,5},{4,8},{5,9},{8,12},{9,13},{12,14},{13,15},{14,10},{15,... | collective-permute-start | bytes 786440 | tf_op jit(solution)/shard_map/ppermute | solution.py:415
  62.7 11.2 %collective-permute-start.28 = (bf16[512,256]{1,0:T(8,128)(2,1)S(1)}, bf16[512,256]{1,0:T(8,128)(2,1)S(1)}, u32[]{:S(2)}, u32[]{:S(2)}) collective-permute-start(bf16[512,256]{1,0:T(8,128)(2,1)S(1)} %collective-permute-done.24.refs_0_), channel_id=1, source_target_pairs={{0,2},{1,3},{4,0},{5,1},{8,4},{9,5},{12,8},{13,9},{14,12},{15,13},... | collective-permute-start | bytes 786440 | tf_op jit(solution)/shard_map/ppermute | solution.py:415
  64.6 11.2 %collective-permute-start.29 = (bf16[512,256]{1,0:T(8,128)(2,1)S(1)}, bf16[512,256]{1,0:T(8,128)(2,1)S(1)}, u32[]{:S(2)}, u32[]{:S(2)}) collective-permute-start(bf16[512,256]{1,0:T(8,128)(2,1)S(1)} %collective-permute-done.25.refs_0_), channel_id=1, source_target_pairs={{0,4},{1,5},{4,8},{5,9},{8,12},{9,13},{12,14},{13,15},{14,10},{15,... | collective-permute-start | bytes 786440 | tf_op jit(solution)/shard_map/ppermute | solution.py:415
  68.3 11.2 %collective-permute-start.30 = (bf16[512,256]{1,0:T(8,128)(2,1)S(1)}, bf16[512,256]{1,0:T(8,128)(2,1)S(1)}, u32[]{:S(2)}, u32[]{:S(2)}) collective-permute-start(bf16[512,256]{1,0:T(8,128)(2,1)S(1)} %collective-permute-done.26.refs_0_), channel_id=1, source_target_pairs={{0,2},{1,3},{4,0},{5,1},{8,4},{9,5},{12,8},{13,9},{14,12},{15,13},... | collective-permute-start | bytes 786440 | tf_op jit(solution)/shard_map/ppermute | solution.py:415
  71.4 11.3 %collective-permute-start.31 = (bf16[512,256]{1,0:T(8,128)(2,1)S(1)}, bf16[512,256]{1,0:T(8,128)(2,1)S(1)}, u32[]{:S(2)}, u32[]{:S(2)}) collective-permute-start(bf16[512,256]{1,0:T(8,128)(2,1)S(1)} %collective-permute-done.27.refs_0_), channel_id=1, source_target_pairs={{0,4},{1,5},{4,8},{5,9},{8,12},{9,13},{12,14},{13,15},{14,10},{15,... | collective-permute-start | bytes 786440 | tf_op jit(solution)/shard_map/ppermute | solution.py:415
  73.9 12.8 %collective-permute-start.32 = (bf16[512,256]{1,0:T(8,128)(2,1)S(1)}, bf16[512,256]{1,0:T(8,128)(2,1)S(1)}, u32[]{:S(2)}, u32[]{:S(2)}) collective-permute-start(bf16[512,256]{1,0:T(8,128)(2,1)S(1)} %collective-permute-done.28.refs_0_), channel_id=1, source_target_pairs={{0,2},{1,3},{4,0},{5,1},{8,4},{9,5},{12,8},{13,9},{14,12},{15,13},... | collective-permute-start | bytes 786440 | tf_op jit(solution)/shard_map/ppermute | solution.py:415
  75.8 10.9 %collective-permute-start.33 = (bf16[512,256]{1,0:T(8,128)(2,1)S(1)}, bf16[512,256]{1,0:T(8,128)(2,1)S(1)}, u32[]{:S(2)}, u32[]{:S(2)}) collective-permute-start(bf16[512,256]{1,0:T(8,128)(2,1)S(1)} %collective-permute-done.29.refs_0_), channel_id=1, source_target_pairs={{0,4},{1,5},{4,8},{5,9},{8,12},{9,13},{12,14},{13,15},{14,10},{15,... | collective-permute-start | bytes 786440 | tf_op jit(solution)/shard_map/ppermute | solution.py:415
  79.5 10.0 %collective-permute-start.34 = (bf16[256,256]{1,0:T(8,128)(2,1)S(1)}, bf16[256,256]{1,0:T(8,128)(2,1)S(1)}, u32[]{:S(2)}, u32[]{:S(2)}) collective-permute-start(bf16[256,256]{1,0:T(8,128)(2,1)S(1)} %slice.18), channel_id=1, source_target_pairs={{0,2},{1,3},{4,0},{5,1},{8,4},{9,5},{12,8},{13,9},{14,12},{15,13},... | collective-permute-start | bytes 393224 | tf_op jit(solution)/shard_map/ppermute | solution.py:415
  82.7 7.1 %collective-permute-start.35 = (bf16[256,256]{1,0:T(8,128)(2,1)S(1)}, bf16[256,256]{1,0:T(8,128)(2,1)S(1)}, u32[]{:S(2)}, u32[]{:S(2)}) collective-permute-start(bf16[256,256]{1,0:T(8,128)(2,1)S(1)} %slice.19), channel_id=1, source_target_pairs={{0,4},{1,5},{4,8},{5,9},{8,12},{9,13},{12,14},{13,15},{14,10},{15,... | collective-permute-start | bytes 393224 | tf_op jit(solution)/shard_map/ppermute | solution.py:415
  86.7 5.0 %collective-permute-start.39 = (bf16[256,256]{1,0:T(8,128)(2,1)S(1)}, bf16[256,256]{1,0:T(8,128)(2,1)S(1)}, u32[]{:S(2)}, u32[]{:S(2)}) collective-permute-start(bf16[256,256]{1,0:T(8,128)(2,1)S(1)} %slice.23), channel_id=1, source_target_pairs={{0,4},{1,5},{4,8},{5,9},{8,12},{9,13},{12,14},{13,15},{14,10},{15,... | collective-permute-start | bytes 393224 | tf_op jit(solution)/shard_map/ppermute | solution.py:415
  (22 other events, 84.8 us)

commit v11 on v10

--- a/solution.py
+++ b/solution.py
@@ -170,7 +170,8 @@
 
 
 def update_kernel(total, low, before_ref, *refs):
-    incl_new_ref, mean_new_ref = refs[-2:]
+    incl_new_ref, mean_new_ref, token_ref = refs[-3:]
+    token_ref[...] = jnp.zeros_like(token_ref)
     rows_all = incl_new_ref.shape[0]
     for rows, incl_new, mean_new in new_state(total, low, 0, rows_all, refs[:7]):
         incl_new_ref[rows, :] = incl_new
@@ -196,16 +197,22 @@
     out_other_ref[...] = other
 
 
-def end_kernel(
-    ring, places, genotype_ref, eta_ref, upper_ref, lower_ref, labels_ref, offset_ref, *refs
-):
-    out_ref = refs[-1]
-    got = jnp.concatenate([upper_ref[...], lower_ref[...]], axis=0)
-    eta = eta_ref[...] + got + offset_ref[...]
+def columns_product(ring, places, genotype_ref, refs, eta):
     for effect_ref, (d, low, swapped) in zip(refs, places):
         own = own_columns(ring, genotype_ref, d, low, low + effect_ref.shape[0], swapped)
         eta = eta + jnp.dot(own, effect_ref[...], preferred_element_type=jnp.float32)
-    out_ref[...] = 4.0 * (labels_ref[...].astype(jnp.float32) - jax.nn.sigmoid(eta))
+    return eta
+
+
+def own_kernel(ring, places, genotype_ref, eta_ref, offset_ref, *refs):
+    eta = eta_ref[...] + offset_ref[...]
+    refs[-1][...] = columns_product(ring, places, genotype_ref, refs, eta)
+
+
+def end_kernel(ring, places, genotype_ref, eta_ref, upper_ref, lower_ref, labels_ref, *refs):
+    got = jnp.concatenate([upper_ref[...], lower_ref[...]], axis=0)
+    eta = columns_product(ring, places, genotype_ref, refs, eta_ref[...] + got)
+    refs[-1][...] = 4.0 * (labels_ref[...].astype(jnp.float32) - jax.nn.sigmoid(eta))
 
 
 def on_device(ring, genotype, residual, labels, incl_old, mean_old, prior_logit, slab_scale, offset):
@@ -372,8 +379,9 @@
             + [rows] * 2
             + [full((1, cols))] * 2
             + [anywhere] * len(outs),
-            out_specs=[rows, rows],
-            out_shape=[jax.ShapeDtypeStruct((block, cols), f32)] * 2,
+            out_specs=[rows, rows, full((8, LANES))],
+            out_shape=[jax.ShapeDtypeStruct((block, cols), f32)] * 2
+            + [jax.ShapeDtypeStruct((8, LANES), f32)],
             input_output_aliases={8: 0, 9: 1} if outs else {},
             compiler_params=params,
             cost_estimate=small,
@@ -406,42 +414,58 @@
         for piece in range(pieces):
             for way in (1, 0):
                 message = held[way, piece]
+                perm = left if way else right
+                d, low = (hop if way else size - hop), piece * part
                 if hop > 1:
                     message, _ = lax.optimization_barrier((message, etas[-2 * pieces - 1]))
-                low = 0
+                near_half = way * (part // 2)
+                halved = message.shape[0] != part
                 if hop == reach:
-                    low = way * (part // 2)
-                    message = message[low : low + part // 2]
-                held[way, piece] = lax.ppermute(message, "ind", left if way else right)
-                found = (hop if way else size - hop, piece * part + low, held[way, piece])
+                    if not halved:
+                        message = message[near_half : near_half + part // 2]
+                    held[way, piece] = lax.ppermute(message, "ind", perm)
+                    found = [(d, low + near_half, held[way, piece])]
+                elif hop == reach - 1 and piece == pieces - 1:
+                    far_half = part // 2 - near_half
+                    first = message[near_half : near_half + part // 2]
+                    first = held[way, piece] = lax.ppermute(first, "ind", perm)
+                    message, _ = lax.optimization_barrier((message, etas[-2 * pieces]))
+                    second = message[far_half : far_half + part // 2]
+                    second = lax.ppermute(second, "ind", perm)
+                    found = [(d, low + near_half, first), (d, low + far_half, second)]
+                else:
+                    held[way, piece] = lax.ppermute(message, "ind", perm)
+                    found = [(d, low, held[way, piece])]
                 if hop == reach and piece == pieces - 1:
-                    final.append(found)
+                    final += found
                     continue
-                eta = product([found], eta, last, small if len(etas) == 1 else light)
+                eta = product(found, eta, last, small if len(etas) == 1 or (hop, piece) >= (reach - 1, pieces - 1) else light)
                 last = eta[0]
                 etas.append(last)
         if updated < pieces and hop < reach:
-            outs = update(updated, outs, last)
-            last = outs[0]
+            *outs, last = update(updated, outs, last)
             updated += 1
     while updated < pieces:
-        outs = update(updated, outs, last)
-        last = outs[0]
+        *outs, last = update(updated, outs, last)
         updated += 1
 
     half = people // 2
     eta_got = [lax.ppermute(eta[1][k : k + half], "ind", swap) for k in (0, half)]
-    places = [(d, low, False) for d, low, _ in final] + [(d, low, True) for d, low, _ in final]
-    args = (genotype, eta[0], *eta_got, labels, offset.reshape(1, cols))
-    args += tuple(effect for _, _, effect in final)
-    args += tuple(lax.ppermute(effect, "ind", swap) for _, _, effect in final)
+    others = [lax.ppermute(effect, "ind", swap) for _, _, effect in final]
+    mine = pl.pallas_call(
+        functools.partial(own_kernel, ring, [(d, low, False) for d, low, _ in final]),
+        out_shape=eta_shape,
+        compiler_params=params,
+        cost_estimate=heavy,
+        name="own_last",
+    )(genotype, eta[0], offset.reshape(1, cols), *[effect for _, _, effect in final])
     resid_new = pl.pallas_call(
-        functools.partial(end_kernel, ring, places),
+        functools.partial(end_kernel, ring, [(d, low, True) for d, low, _ in final]),
         out_shape=eta_shape,
         compiler_params=params,
         cost_estimate=light,
         name="new_residual",
-    )(*args)
+    )(genotype, mine, *eta_got, labels, *others)
     return (outs[0], outs[1], resid_new)
 
 

time: 95 us -> 94.1 us (level)
  starting transfers between devices: 37.3 us -> 40.4 us
  local copies, waits for them, and re-layouts: 2.58 us -> 0.14 us
  waiting for transfers between devices: 31.9 us -> 30.3 us
    ppermute x18 -> x20, starting transfers between devices: 16.7 us -> 19.8 us  [the longest x14 14.8 us: on_device(): held[way, piece] = lax.ppermute(message, 'ind', perm)]
    unnamed x24 -> x20, local copies, waits for them, and re-layouts: 2.51 us -> 0.05 us
    ppermute x18 -> x20, waiting for transfers between devices: 14 us -> 12.4 us  [the longest x14 10.5 us: on_device(): held[way, piece] = lax.ppermute(message, 'ind', perm)]
  transfers between devices with their start and end apart: 42 -> 44, of which waited for: 17 -> 17; matrix products, arithmetic and copies ran while one was open for 0% -> 0% of each run, Pallas kernels for 21% -> 21%
where the time goes in v11:
time: 94.1 us; the launch traced here: 94 us
  starting transfers between devices  40.4 us (43%)
  waiting for transfers between devices  30.3 us (32%)
  Pallas kernels  22 us (23%)
  between operations  1.21 us (1%)
    ppermute x12, waiting for transfers between devices, on_device(): got[way, piece] = lax.ppermute(last, 'ind', left if way else right)  17.6 us
    ppermute x14, starting transfers between devices, on_device(): held[way, piece] = lax.ppermute(message, 'ind', perm)  14.8 us
    ppermute x12, starting transfers between devices, on_device(): got[way, piece] = lax.ppermute(last, 'ind', left if way else right)  12.8 us
    ppermute x14, waiting for transfers between devices, on_device(): held[way, piece] = lax.ppermute(message, 'ind', perm)  10.5 us
    pallas_call x12, Pallas kernels, on_device(): pl.pallas_call(functools.partial(hop_kernel, ring, (w, peer[w][1]), low,...  6.62 us
    ppermute x2, starting transfers between devices, on_device(): got[1, piece] = lax.ppermute(sent[1], 'ind', left)  5.61 us
    pallas_call x15, Pallas kernels, product(): pl.pallas_call(functools.partial(eta_kernel, ring, places, not eta), in_s...  5.6 us
    pallas_call x4, Pallas kernels, pick(): pl.pallas_call(functools.partial(pick_kernel, ring, wanted, block), in_sp...  3.21 us
  transfers between devices with their start and end apart: 44, of which 17 were waited for; matrix products, arithmetic and copies ran while one was open for 0% of the time, Pallas kernels for 21%

profile of v11, /device:TPU:0, one launch (start us, length us, event | category | flops | bytes accessed | tf_op | source)
XLA Modules:
  0.0 94.0 jit_solution(7690246663257399998)
XLA Ops:
  0.6 1.2 %pick_blocks.4 = (bf16[1,384,512]{2,1,0:T(8,128)(2,1)S(1)}, bf16[1,384,512]{2,1,0:T(8,128)(2,1)S(1)}) custom-call(bf16[384,16384]{1,0:T(8,128)(2,1)} %genotype_ref.11), custom_call_target="tpu_custom_call" | custom-call | flops 1 | bytes 1 | tf_op jit(solution)/shard_map/pick_blocks/pallas_call | solution.py:248
  2.5 1.7 %pick_blocks.5 = (bf16[1,384,512]{2,1,0:T(8,128)(2,1)S(1)}, bf16[1,384,512]{2,1,0:T(8,128)(2,1)S(1)}, bf16[2,384,1024]{2,1,0:T(8,128)(2,1)S(1)}) custom-call(bf16[384,16384]{1,0:T(8,128)(2,1)} %genotype_ref.11, bf16[1,384,512]{2,1,0:T(8,128)(2,1)S(1)} %get-tuple-element.65.refs_0_), custom_call_target="tpu_custom_call" | custom-call | flops 10000000000 | bytes 1000000 | tf_op jit(solution)/shard_map/pick_blocks/pallas_call | solution.py:248
  5.4 3.0 %collective-permute-start.4 = (s16[528,128]{1,0:T(8,128)(2,1)S(1)}, s16[528,128]{1,0:T(8,128)(2,1)S(1)}, u32[]{:S(2)}, u32[]{:S(2)}) collective-permute-start(s16[528,128]{1,0:T(8,128)(2,1)S(1)} %get-tuple-element.74), channel_id=1, source_target_pairs={{0,2},{1,3},{4,0},{5,1},{8,4},{9,5},{12,8},{13,9},{14,12},{15,13},... | collective-permute-start | bytes 405512 | tf_op jit(solution)/shard_map/ppermute | solution.py:321
  9.1 2.6 %collective-permute-start.7 = (s16[528,128]{1,0:T(8,128)(2,1)S(1)}, s16[528,128]{1,0:T(8,128)(2,1)S(1)}, u32[]{:S(2)}, u32[]{:S(2)}) collective-permute-start(s16[528,128]{1,0:T(8,128)(2,1)S(1)} %get-tuple-element.76), channel_id=1, source_target_pairs={{0,2},{1,3},{4,0},{5,1},{8,4},{9,5},{12,8},{13,9},{14,12},{15,13},... | collective-permute-start | bytes 405512 | tf_op jit(solution)/shard_map/ppermute | solution.py:321
  12.9 1.7 %collective-permute-start.9 = (s16[1040,128]{1,0:T(8,128)(2,1)S(1)}, s16[1040,128]{1,0:T(8,128)(2,1)S(1)}, u32[]{:S(2)}, u32[]{:S(2)}) collective-permute-start(s16[1040,128]{1,0:T(8,128)(2,1)S(1)} %sum_hop.12.before_ref), channel_id=1, source_target_pairs={{0,2},{1,3},{4,0},{5,1},{8,4},{9,5},{12,8},{13,9},{14,12},{15,13},... | collective-permute-start | bytes 798728 | tf_op jit(solution)/shard_map/ppermute | solution.py:338
  16.4 1.7 %collective-permute-start.11 = (s16[1040,128]{1,0:T(8,128)(2,1)S(1)}, s16[1040,128]{1,0:T(8,128)(2,1)S(1)}, u32[]{:S(2)}, u32[]{:S(2)}) collective-permute-start(s16[1040,128]{1,0:T(8,128)(2,1)S(1)} %sum_hop.14.before_ref), channel_id=1, source_target_pairs={{0,2},{1,3},{4,0},{5,1},{8,4},{9,5},{12,8},{13,9},{14,12},{15,13},... | collective-permute-start | bytes 798728 | tf_op jit(solution)/shard_map/ppermute | solution.py:338
  19.1 3.0 %collective-permute-done.9.got_ref = s16[1040,128]{1,0:T(8,128)(2,1)S(1)} collective-permute-done((s16[1040,128]{1,0:T(8,128)(2,1)S(1)}, s16[1040,128]{1,0:T(8,128)(2,1)S(1)}, u32[]{:S(2)}, u32[]{:S(2)}) %collective-permute-start.9) | collective-permute-done | bytes 266272 | tf_op jit(solution)/shard_map/ppermute | solution.py:338
  22.7 1.7 %collective-permute-start.14 = (s16[1040,128]{1,0:T(8,128)(2,1)S(1)}, s16[1040,128]{1,0:T(8,128)(2,1)S(1)}, u32[]{:S(2)}, u32[]{:S(2)}) collective-permute-start(s16[1040,128]{1,0:T(8,128)(2,1)S(1)} %sum_hop.16.before_ref), channel_id=1, source_target_pairs={{0,2},{1,3},{4,0},{5,1},{8,4},{9,5},{12,8},{13,9},{14,12},{15,13},... | collective-permute-start | bytes 798728 | tf_op jit(solution)/shard_map/ppermute | solution.py:338
  25.4 2.4 %collective-permute-done.11.got_ref = s16[1040,128]{1,0:T(8,128)(2,1)S(1)} collective-permute-done((s16[1040,128]{1,0:T(8,128)(2,1)S(1)}, s16[1040,128]{1,0:T(8,128)(2,1)S(1)}, u32[]{:S(2)}, u32[]{:S(2)}) %collective-permute-start.11) | collective-permute-done | bytes 266272 | tf_op jit(solution)/shard_map/ppermute | solution.py:338
  28.4 1.7 %collective-permute-start.16 = (s16[1040,128]{1,0:T(8,128)(2,1)S(1)}, s16[1040,128]{1,0:T(8,128)(2,1)S(1)}, u32[]{:S(2)}, u32[]{:S(2)}) collective-permute-start(s16[1040,128]{1,0:T(8,128)(2,1)S(1)} %sum_hop.18.before_ref), channel_id=1, source_target_pairs={{0,2},{1,3},{4,0},{5,1},{8,4},{9,5},{12,8},{13,9},{14,12},{15,13},... | collective-permute-start | bytes 798728 | tf_op jit(solution)/shard_map/ppermute | solution.py:338
  31.1 2.4 %collective-permute-done.14.got_ref = s16[1040,128]{1,0:T(8,128)(2,1)S(1)} collective-permute-done((s16[1040,128]{1,0:T(8,128)(2,1)S(1)}, s16[1040,128]{1,0:T(8,128)(2,1)S(1)}, u32[]{:S(2)}, u32[]{:S(2)}) %collective-permute-start.14) | collective-permute-done | bytes 266272 | tf_op jit(solution)/shard_map/ppermute | solution.py:338
  34.1 1.7 %collective-permute-start.19 = (s16[1040,128]{1,0:T(8,128)(2,1)S(1)}, s16[1040,128]{1,0:T(8,128)(2,1)S(1)}, u32[]{:S(2)}, u32[]{:S(2)}) collective-permute-start(s16[1040,128]{1,0:T(8,128)(2,1)S(1)} %sum_hop.20.before_ref), channel_id=1, source_target_pairs={{0,2},{1,3},{4,0},{5,1},{8,4},{9,5},{12,8},{13,9},{14,12},{15,13},... | collective-permute-start | bytes 798728 | tf_op jit(solution)/shard_map/ppermute | solution.py:338
  36.8 2.4 %collective-permute-done.16.got_ref = s16[1040,128]{1,0:T(8,128)(2,1)S(1)} collective-permute-done((s16[1040,128]{1,0:T(8,128)(2,1)S(1)}, s16[1040,128]{1,0:T(8,128)(2,1)S(1)}, u32[]{:S(2)}, u32[]{:S(2)}) %collective-permute-start.16) | collective-permute-done | bytes 266272 | tf_op jit(solution)/shard_map/ppermute | solution.py:338
  39.8 1.7 %collective-permute-start.21 = (s16[1040,128]{1,0:T(8,128)(2,1)S(1)}, s16[1040,128]{1,0:T(8,128)(2,1)S(1)}, u32[]{:S(2)}, u32[]{:S(2)}) collective-permute-start(s16[1040,128]{1,0:T(8,128)(2,1)S(1)} %sum_hop.22.before_ref), channel_id=1, source_target_pairs={{0,2},{1,3},{4,0},{5,1},{8,4},{9,5},{12,8},{13,9},{14,12},{15,13},... | collective-permute-start | bytes 798728 | tf_op jit(solution)/shard_map/ppermute | solution.py:338
  43.3 4.0 %collective-permute-done.18.refs_1_ = s16[1040,128]{1,0:T(8,128)(2,1)S(1)} collective-permute-done((s16[1040,128]{1,0:T(8,128)(2,1)S(1)}, s16[1040,128]{1,0:T(8,128)(2,1)S(1)}, u32[]{:S(2)}, u32[]{:S(2)}) %collective-permute-start.18) | collective-permute-done | bytes 266272 | tf_op jit(solution)/shard_map/ppermute | solution.py:338
  47.7 1.6 %collective-permute-start.22 = (bf16[512,256]{1,0:T(8,128)(2,1)S(1)}, bf16[512,256]{1,0:T(8,128)(2,1)S(1)}, u32[]{:S(2)}, u32[]{:S(2)}) collective-permute-start(bf16[512,256]{1,0:T(8,128)(2,1)S(1)} %effect.2.before_ref.refs_0_), channel_id=1, source_target_pairs={{0,2},{1,3},{4,0},{5,1},{8,4},{9,5},{12,8},{13,9},{14,12},{15,13},... | collective-permute-start | bytes 786440 | tf_op jit(solution)/shard_map/ppermute | solution.py:437
  49.8 3.2 %collective-permute-done.20.refs_1_ = s16[1040,128]{1,0:T(8,128)(2,1)S(1)} collective-permute-done((s16[1040,128]{1,0:T(8,128)(2,1)S(1)}, s16[1040,128]{1,0:T(8,128)(2,1)S(1)}, u32[]{:S(2)}, u32[]{:S(2)}) %collective-permute-start.20) | collective-permute-done | bytes 266272 | tf_op jit(solution)/shard_map/ppermute | solution.py:338
  53.4 1.6 %collective-permute-start.24 = (bf16[512,256]{1,0:T(8,128)(2,1)S(1)}, bf16[512,256]{1,0:T(8,128)(2,1)S(1)}, u32[]{:S(2)}, u32[]{:S(2)}) collective-permute-start(bf16[512,256]{1,0:T(8,128)(2,1)S(1)} %effect.3.before_ref.refs_3_), channel_id=1, source_target_pairs={{0,2},{1,3},{4,0},{5,1},{8,4},{9,5},{12,8},{13,9},{14,12},{15,13},... | collective-permute-start | bytes 786440 | tf_op jit(solution)/shard_map/ppermute | solution.py:437
  57.0 1.6 %collective-permute-start.26 = (bf16[512,256]{1,0:T(8,128)(2,1)S(1)}, bf16[512,256]{1,0:T(8,128)(2,1)S(1)}, u32[]{:S(2)}, u32[]{:S(2)}) collective-permute-start(bf16[512,256]{1,0:T(8,128)(2,1)S(1)} %collective-permute-done.22.refs_0_), channel_id=1, source_target_pairs={{0,2},{1,3},{4,0},{5,1},{8,4},{9,5},{12,8},{13,9},{14,12},{15,13},... | collective-permute-start | bytes 786440 | tf_op jit(solution)/shard_map/ppermute | solution.py:437
  59.8 2.8 %collective-permute-done.24.refs_0_ = bf16[512,256]{1,0:T(8,128)(2,1)S(1)} collective-permute-done((bf16[512,256]{1,0:T(8,128)(2,1)S(1)}, bf16[512,256]{1,0:T(8,128)(2,1)S(1)}, u32[]{:S(2)}, u32[]{:S(2)}) %collective-permute-start.24) | collective-permute-done | bytes 262176 | tf_op jit(solution)/shard_map/ppermute | solution.py:437
  62.6 1.6 %collective-permute-start.28 = (bf16[512,256]{1,0:T(8,128)(2,1)S(1)}, bf16[512,256]{1,0:T(8,128)(2,1)S(1)}, u32[]{:S(2)}, u32[]{:S(2)}) collective-permute-start(bf16[512,256]{1,0:T(8,128)(2,1)S(1)} %collective-permute-done.24.refs_0_), channel_id=1, source_target_pairs={{0,2},{1,3},{4,0},{5,1},{8,4},{9,5},{12,8},{13,9},{14,12},{15,13},... | collective-permute-start | bytes 786440 | tf_op jit(solution)/shard_map/ppermute | solution.py:437
  65.5 1.3 %update.2 = (f32[1024,256]{1,0:T(8,128)}, f32[1024,256]{1,0:T(8,128)}, f32[8,128]{1,0:T(8,128)S(1)}) custom-call(f32[384,256]{1,0:T(8,128)S(1)} %get-tuple-element.85.before_ref.refs_3_, f32[256,1024]{1,0:T(8,128)S(1)} %sum_near.1.before_ref.refs_0_, s16[1040,128]{1,0:T(8,128)(2,1)S(1)} %collective-permute-done.18.refs_1_, ...), custom_call_target="tpu_custom_call" | custom-call | flops 1 | bytes 1 | tf_op jit(solution)/shard_map/update/pallas_call | solution.py:374
  66.8 1.4 %collective-permute-done.26.refs_0_ = bf16[512,256]{1,0:T(8,128)(2,1)S(1)} collective-permute-done((bf16[512,256]{1,0:T(8,128)(2,1)S(1)}, bf16[512,256]{1,0:T(8,128)(2,1)S(1)}, u32[]{:S(2)}, u32[]{:S(2)}) %collective-permute-start.26) | collective-permute-done | bytes 262176 | tf_op jit(solution)/shard_map/ppermute | solution.py:437
  68.2 1.6 %collective-permute-start.30 = (bf16[512,256]{1,0:T(8,128)(2,1)S(1)}, bf16[512,256]{1,0:T(8,128)(2,1)S(1)}, u32[]{:S(2)}, u32[]{:S(2)}) collective-permute-start(bf16[512,256]{1,0:T(8,128)(2,1)S(1)} %collective-permute-done.26.refs_0_), channel_id=1, source_target_pairs={{0,2},{1,3},{4,0},{5,1},{8,4},{9,5},{12,8},{13,9},{14,12},{15,13},... | collective-permute-start | bytes 786440 | tf_op jit(solution)/shard_map/ppermute | solution.py:437
  71.1 2.8 %collective-permute-done.28.refs_0_ = bf16[512,256]{1,0:T(8,128)(2,1)S(1)} collective-permute-done((bf16[512,256]{1,0:T(8,128)(2,1)S(1)}, bf16[512,256]{1,0:T(8,128)(2,1)S(1)}, u32[]{:S(2)}, u32[]{:S(2)}) %collective-permute-start.28) | collective-permute-done | bytes 262176 | tf_op jit(solution)/shard_map/ppermute | solution.py:437
  73.8 1.6 %collective-permute-start.32 = (bf16[256,256]{1,0:T(8,128)(2,1)S(1)}, bf16[256,256]{1,0:T(8,128)(2,1)S(1)}, u32[]{:S(2)}, u32[]{:S(2)}) collective-permute-start(bf16[256,256]{1,0:T(8,128)(2,1)S(1)} %slice.24), channel_id=1, source_target_pairs={{0,2},{1,3},{4,0},{5,1},{8,4},{9,5},{12,8},{13,9},{14,12},{15,13},... | collective-permute-start | bytes 393224 | tf_op jit(solution)/shard_map/ppermute | solution.py:431
  76.8 1.2 %collective-permute-start.35 = (bf16[256,256]{1,0:T(8,128)(2,1)S(1)}, bf16[256,256]{1,0:T(8,128)(2,1)S(1)}, u32[]{:S(2)}, u32[]{:S(2)}) collective-permute-start(bf16[256,256]{1,0:T(8,128)(2,1)S(1)} %slice.27), channel_id=1, source_target_pairs={{0,4},{1,5},{4,8},{5,9},{8,12},{9,13},{12,14},{13,15},{14,10},{15,... | collective-permute-start | bytes 393224 | tf_op jit(solution)/shard_map/ppermute | solution.py:434
  78.0 1.3 %update.3 = (f32[1024,256]{1,0:T(8,128)}, f32[1024,256]{1,0:T(8,128)}, f32[8,128]{1,0:T(8,128)S(1)}) custom-call(f32[384,256]{1,0:T(8,128)S(1)} %get-tuple-element.98.before_ref.refs_3_, f32[256,1024]{1,0:T(8,128)S(1)} %sum_near.1.before_ref.refs_0_, ...), custom_call_target="tpu_custom_call", output_to_operand_aliasing={{0}: (8, {}), {1}: (9, {})} | custom-call | flops 1 | bytes 1 | tf_op jit(solution)/shard_map/update/pallas_call | solution.py:374
  79.5 1.6 %collective-permute-start.33 = (bf16[256,256]{1,0:T(8,128)(2,1)S(1)}, bf16[256,256]{1,0:T(8,128)(2,1)S(1)}, u32[]{:S(2)}, u32[]{:S(2)}) collective-permute-start(bf16[256,256]{1,0:T(8,128)(2,1)S(1)} %slice.25), channel_id=1, source_target_pairs={{0,2},{1,3},{4,0},{5,1},{8,4},{9,5},{12,8},{13,9},{14,12},{15,13},... | collective-permute-start | bytes 393224 | tf_op jit(solution)/shard_map/ppermute | solution.py:434
  81.4 1.6 %collective-permute-start.36 = (bf16[256,256]{1,0:T(8,128)(2,1)S(1)}, bf16[256,256]{1,0:T(8,128)(2,1)S(1)}, u32[]{:S(2)}, u32[]{:S(2)}) collective-permute-start(bf16[256,256]{1,0:T(8,128)(2,1)S(1)} %slice.28), channel_id=1, source_target_pairs={{0,2},{1,3},{4,0},{5,1},{8,4},{9,5},{12,8},{13,9},{14,12},{15,13},... | collective-permute-start | bytes 393224 | tf_op jit(solution)/shard_map/ppermute | solution.py:426
  84.7 1.7 %collective-permute-start.38 = (bf16[256,256]{1,0:T(8,128)(2,1)S(1)}, bf16[256,256]{1,0:T(8,128)(2,1)S(1)}, u32[]{:S(2)}, u32[]{:S(2)}) collective-permute-start(bf16[256,256]{1,0:T(8,128)(2,1)S(1)} %collective-permute-done.32.refs_0_), channel_id=1, source_target_pairs={{0,2},{1,3},{4,0},{5,1},{8,4},{9,5},{12,8},{13,9},{14,12},{15,13},... | collective-permute-start | bytes 393224 | tf_op jit(solution)/shard_map/ppermute | solution.py:426
  88.1 2.0 %collective-permute-done.37.refs_0_ = bf16[256,256]{1,0:T(8,128)(2,1)S(1)} collective-permute-done((bf16[256,256]{1,0:T(8,128)(2,1)S(1)}, bf16[256,256]{1,0:T(8,128)(2,1)S(1)}, u32[]{:S(2)}, u32[]{:S(2)}) %collective-permute-start.37) | collective-permute-done | bytes 131104 | tf_op jit(solution)/shard_map/ppermute | solution.py:426
  (125 shorter events, 29.1 us)
Async XLA Ops:
  5.4 6.9 %collective-permute-start.4 = (s16[528,128]{1,0:T(8,128)(2,1)S(1)}, s16[528,128]{1,0:T(8,128)(2,1)S(1)}, u32[]{:S(2)}, u32[]{:S(2)}) collective-permute-start(s16[528,128]{1,0:T(8,128)(2,1)S(1)} %get-tuple-element.74), channel_id=1, source_target_pairs={{0,2},{1,3},{4,0},{5,1},{8,4},{9,5},{12,8},{13,9},{14,12},{15,13},... | collective-permute-start | bytes 405512 | tf_op jit(solution)/shard_map/ppermute | solution.py:321
  9.1 6.8 %collective-permute-start.7 = (s16[528,128]{1,0:T(8,128)(2,1)S(1)}, s16[528,128]{1,0:T(8,128)(2,1)S(1)}, u32[]{:S(2)}, u32[]{:S(2)}) collective-permute-start(s16[528,128]{1,0:T(8,128)(2,1)S(1)} %get-tuple-element.76), channel_id=1, source_target_pairs={{0,2},{1,3},{4,0},{5,1},{8,4},{9,5},{12,8},{13,9},{14,12},{15,13},... | collective-permute-start | bytes 405512 | tf_op jit(solution)/shard_map/ppermute | solution.py:321
  11.7 6.5 %collective-permute-start.8 = (s16[528,128]{1,0:T(8,128)(2,1)S(1)}, s16[528,128]{1,0:T(8,128)(2,1)S(1)}, u32[]{:S(2)}, u32[]{:S(2)}) collective-permute-start(s16[528,128]{1,0:T(8,128)(2,1)S(1)} %get-tuple-element.73.refs_0_), channel_id=1, source_target_pairs={{0,4},{1,5},{4,8},{5,9},{8,12},{9,13},{12,14},{13,15},{14,10},{15,... | collective-permute-start | bytes 405512 | tf_op jit(solution)/shard_map/ppermute | solution.py:320
  12.9 9.2 %collective-permute-start.9 = (s16[1040,128]{1,0:T(8,128)(2,1)S(1)}, s16[1040,128]{1,0:T(8,128)(2,1)S(1)}, u32[]{:S(2)}, u32[]{:S(2)}) collective-permute-start(s16[1040,128]{1,0:T(8,128)(2,1)S(1)} %sum_hop.12.before_ref), channel_id=1, source_target_pairs={{0,2},{1,3},{4,0},{5,1},{8,4},{9,5},{12,8},{13,9},{14,12},{15,13},... | collective-permute-start | bytes 798728 | tf_op jit(solution)/shard_map/ppermute | solution.py:338
  15.2 9.3 %collective-permute-start.10 = (s16[1040,128]{1,0:T(8,128)(2,1)S(1)}, s16[1040,128]{1,0:T(8,128)(2,1)S(1)}, u32[]{:S(2)}, u32[]{:S(2)}) collective-permute-start(s16[1040,128]{1,0:T(8,128)(2,1)S(1)} %sum_hop.13.refs_0_), channel_id=1, source_target_pairs={{0,4},{1,5},{4,8},{5,9},{8,12},{9,13},{12,14},{13,15},{14,10},{15,... | collective-permute-start | bytes 798728 | tf_op jit(solution)/shard_map/ppermute | solution.py:338
  15.8 17.8 %collective-permute-start.13 = (bf16[3,384,1024]{2,1,0:T(8,128)(2,1)S(1)}, bf16[3,384,1024]{2,1,0:T(8,128)(2,1)S(1)}, u32[]{:S(2)}, u32[]{:S(2)}) collective-permute-start(bf16[3,384,1024]{2,1,0:T(8,128)(2,1)S(1)} %pick_blocks.7.before_ref), channel_id=1, source_target_pairs={{0,1},{1,0},{2,3},{3,2},{4,5},{5,4},{6,7},{7,6},{8,9},{9,8},{10,11... | collective-permute-start | bytes 7077896 | tf_op jit(solution)/shard_map/ppermute | solution.py:269
  16.4 11.4 %collective-permute-start.11 = (s16[1040,128]{1,0:T(8,128)(2,1)S(1)}, s16[1040,128]{1,0:T(8,128)(2,1)S(1)}, u32[]{:S(2)}, u32[]{:S(2)}) collective-permute-start(s16[1040,128]{1,0:T(8,128)(2,1)S(1)} %sum_hop.14.before_ref), channel_id=1, source_target_pairs={{0,2},{1,3},{4,0},{5,1},{8,4},{9,5},{12,8},{13,9},{14,12},{15,13},... | collective-permute-start | bytes 798728 | tf_op jit(solution)/shard_map/ppermute | solution.py:338
  18.7 11.4 %collective-permute-start.12 = (s16[1040,128]{1,0:T(8,128)(2,1)S(1)}, s16[1040,128]{1,0:T(8,128)(2,1)S(1)}, u32[]{:S(2)}, u32[]{:S(2)}) collective-permute-start(s16[1040,128]{1,0:T(8,128)(2,1)S(1)} %sum_hop.15.before_ref), channel_id=1, source_target_pairs={{0,4},{1,5},{4,8},{5,9},{8,12},{9,13},{12,14},{13,15},{14,10},{15,... | collective-permute-start | bytes 798728 | tf_op jit(solution)/shard_map/ppermute | solution.py:338
  22.7 10.8 %collective-permute-start.14 = (s16[1040,128]{1,0:T(8,128)(2,1)S(1)}, s16[1040,128]{1,0:T(8,128)(2,1)S(1)}, u32[]{:S(2)}, u32[]{:S(2)}) collective-permute-start(s16[1040,128]{1,0:T(8,128)(2,1)S(1)} %sum_hop.16.before_ref), channel_id=1, source_target_pairs={{0,2},{1,3},{4,0},{5,1},{8,4},{9,5},{12,8},{13,9},{14,12},{15,13},... | collective-permute-start | bytes 798728 | tf_op jit(solution)/shard_map/ppermute | solution.py:338
  25.0 10.8 %collective-permute-start.15 = (s16[1040,128]{1,0:T(8,128)(2,1)S(1)}, s16[1040,128]{1,0:T(8,128)(2,1)S(1)}, u32[]{:S(2)}, u32[]{:S(2)}) collective-permute-start(s16[1040,128]{1,0:T(8,128)(2,1)S(1)} %sum_hop.17.before_ref), channel_id=1, source_target_pairs={{0,4},{1,5},{4,8},{5,9},{8,12},{9,13},{12,14},{13,15},{14,10},{15,... | collective-permute-start | bytes 798728 | tf_op jit(solution)/shard_map/ppermute | solution.py:338
  28.4 10.9 %collective-permute-start.16 = (s16[1040,128]{1,0:T(8,128)(2,1)S(1)}, s16[1040,128]{1,0:T(8,128)(2,1)S(1)}, u32[]{:S(2)}, u32[]{:S(2)}) collective-permute-start(s16[1040,128]{1,0:T(8,128)(2,1)S(1)} %sum_hop.18.before_ref), channel_id=1, source_target_pairs={{0,2},{1,3},{4,0},{5,1},{8,4},{9,5},{12,8},{13,9},{14,12},{15,13},... | collective-permute-start | bytes 798728 | tf_op jit(solution)/shard_map/ppermute | solution.py:338
  30.7 10.9 %collective-permute-start.17 = (s16[1040,128]{1,0:T(8,128)(2,1)S(1)}, s16[1040,128]{1,0:T(8,128)(2,1)S(1)}, u32[]{:S(2)}, u32[]{:S(2)}) collective-permute-start(s16[1040,128]{1,0:T(8,128)(2,1)S(1)} %sum_hop.19.before_ref), channel_id=1, source_target_pairs={{0,4},{1,5},{4,8},{5,9},{8,12},{9,13},{12,14},{13,15},{14,10},{15,... | collective-permute-start | bytes 798728 | tf_op jit(solution)/shard_map/ppermute | solution.py:338
  34.1 13.2 %collective-permute-start.19 = (s16[1040,128]{1,0:T(8,128)(2,1)S(1)}, s16[1040,128]{1,0:T(8,128)(2,1)S(1)}, u32[]{:S(2)}, u32[]{:S(2)}) collective-permute-start(s16[1040,128]{1,0:T(8,128)(2,1)S(1)} %sum_hop.20.before_ref), channel_id=1, source_target_pairs={{0,2},{1,3},{4,0},{5,1},{8,4},{9,5},{12,8},{13,9},{14,12},{15,13},... | collective-permute-start | bytes 798728 | tf_op jit(solution)/shard_map/ppermute | solution.py:338
  36.4 10.8 %collective-permute-start.18 = (s16[1040,128]{1,0:T(8,128)(2,1)S(1)}, s16[1040,128]{1,0:T(8,128)(2,1)S(1)}, u32[]{:S(2)}, u32[]{:S(2)}) collective-permute-start(s16[1040,128]{1,0:T(8,128)(2,1)S(1)} %sum_hop.21.before_ref), channel_id=1, source_target_pairs={{0,4},{1,5},{4,8},{5,9},{8,12},{9,13},{12,14},{13,15},{14,10},{15,... | collective-permute-start | bytes 798728 | tf_op jit(solution)/shard_map/ppermute | solution.py:338
  39.8 13.2 %collective-permute-start.21 = (s16[1040,128]{1,0:T(8,128)(2,1)S(1)}, s16[1040,128]{1,0:T(8,128)(2,1)S(1)}, u32[]{:S(2)}, u32[]{:S(2)}) collective-permute-start(s16[1040,128]{1,0:T(8,128)(2,1)S(1)} %sum_hop.22.before_ref), channel_id=1, source_target_pairs={{0,2},{1,3},{4,0},{5,1},{8,4},{9,5},{12,8},{13,9},{14,12},{15,13},... | collective-permute-start | bytes 798728 | tf_op jit(solution)/shard_map/ppermute | solution.py:338
  42.2 10.8 %collective-permute-start.20 = (s16[1040,128]{1,0:T(8,128)(2,1)S(1)}, s16[1040,128]{1,0:T(8,128)(2,1)S(1)}, u32[]{:S(2)}, u32[]{:S(2)}) collective-permute-start(s16[1040,128]{1,0:T(8,128)(2,1)S(1)} %sum_hop.23.before_ref), channel_id=1, source_target_pairs={{0,4},{1,5},{4,8},{5,9},{8,12},{9,13},{12,14},{13,15},{14,10},{15,... | collective-permute-start | bytes 798728 | tf_op jit(solution)/shard_map/ppermute | solution.py:338
  47.7 9.3 %collective-permute-start.22 = (bf16[512,256]{1,0:T(8,128)(2,1)S(1)}, bf16[512,256]{1,0:T(8,128)(2,1)S(1)}, u32[]{:S(2)}, u32[]{:S(2)}) collective-permute-start(bf16[512,256]{1,0:T(8,128)(2,1)S(1)} %effect.2.before_ref.refs_0_), channel_id=1, source_target_pairs={{0,2},{1,3},{4,0},{5,1},{8,4},{9,5},{12,8},{13,9},{14,12},{15,13},... | collective-permute-start | bytes 786440 | tf_op jit(solution)/shard_map/ppermute | solution.py:437
  49.3 9.6 %collective-permute-start.23 = (bf16[512,256]{1,0:T(8,128)(2,1)S(1)}, bf16[512,256]{1,0:T(8,128)(2,1)S(1)}, u32[]{:S(2)}, u32[]{:S(2)}) collective-permute-start(bf16[512,256]{1,0:T(8,128)(2,1)S(1)} %effect.2.before_ref.refs_0_), channel_id=1, source_target_pairs={{0,4},{1,5},{4,8},{5,9},{8,12},{9,13},{12,14},{13,15},{14,10},{15,... | collective-permute-start | bytes 786440 | tf_op jit(solution)/shard_map/ppermute | solution.py:437
  53.4 9.2 %collective-permute-start.24 = (bf16[512,256]{1,0:T(8,128)(2,1)S(1)}, bf16[512,256]{1,0:T(8,128)(2,1)S(1)}, u32[]{:S(2)}, u32[]{:S(2)}) collective-permute-start(bf16[512,256]{1,0:T(8,128)(2,1)S(1)} %effect.3.before_ref.refs_3_), channel_id=1, source_target_pairs={{0,2},{1,3},{4,0},{5,1},{8,4},{9,5},{12,8},{13,9},{14,12},{15,13},... | collective-permute-start | bytes 786440 | tf_op jit(solution)/shard_map/ppermute | solution.py:437
  55.0 9.6 %collective-permute-start.25 = (bf16[512,256]{1,0:T(8,128)(2,1)S(1)}, bf16[512,256]{1,0:T(8,128)(2,1)S(1)}, u32[]{:S(2)}, u32[]{:S(2)}) collective-permute-start(bf16[512,256]{1,0:T(8,128)(2,1)S(1)} %effect.3.before_ref.refs_3_), channel_id=1, source_target_pairs={{0,4},{1,5},{4,8},{5,9},{8,12},{9,13},{12,14},{13,15},{14,10},{15,... | collective-permute-start | bytes 786440 | tf_op jit(solution)/shard_map/ppermute | solution.py:437
  57.0 11.2 %collective-permute-start.26 = (bf16[512,256]{1,0:T(8,128)(2,1)S(1)}, bf16[512,256]{1,0:T(8,128)(2,1)S(1)}, u32[]{:S(2)}, u32[]{:S(2)}) collective-permute-start(bf16[512,256]{1,0:T(8,128)(2,1)S(1)} %collective-permute-done.22.refs_0_), channel_id=1, source_target_pairs={{0,2},{1,3},{4,0},{5,1},{8,4},{9,5},{12,8},{13,9},{14,12},{15,13},... | collective-permute-start | bytes 786440 | tf_op jit(solution)/shard_map/ppermute | solution.py:437
  59.0 11.2 %collective-permute-start.27 = (bf16[512,256]{1,0:T(8,128)(2,1)S(1)}, bf16[512,256]{1,0:T(8,128)(2,1)S(1)}, u32[]{:S(2)}, u32[]{:S(2)}) collective-permute-start(bf16[512,256]{1,0:T(8,128)(2,1)S(1)} %collective-permute-done.23.refs_0_), channel_id=1, source_target_pairs={{0,4},{1,5},{4,8},{5,9},{8,12},{9,13},{12,14},{13,15},{14,10},{15,... | collective-permute-start | bytes 786440 | tf_op jit(solution)/shard_map/ppermute | solution.py:437
  62.6 11.2 %collective-permute-start.28 = (bf16[512,256]{1,0:T(8,128)(2,1)S(1)}, bf16[512,256]{1,0:T(8,128)(2,1)S(1)}, u32[]{:S(2)}, u32[]{:S(2)}) collective-permute-start(bf16[512,256]{1,0:T(8,128)(2,1)S(1)} %collective-permute-done.24.refs_0_), channel_id=1, source_target_pairs={{0,2},{1,3},{4,0},{5,1},{8,4},{9,5},{12,8},{13,9},{14,12},{15,13},... | collective-permute-start | bytes 786440 | tf_op jit(solution)/shard_map/ppermute | solution.py:437
  64.6 11.3 %collective-permute-start.29 = (bf16[512,256]{1,0:T(8,128)(2,1)S(1)}, bf16[512,256]{1,0:T(8,128)(2,1)S(1)}, u32[]{:S(2)}, u32[]{:S(2)}) collective-permute-start(bf16[512,256]{1,0:T(8,128)(2,1)S(1)} %collective-permute-done.25.refs_0_), channel_id=1, source_target_pairs={{0,4},{1,5},{4,8},{5,9},{8,12},{9,13},{12,14},{13,15},{14,10},{15,... | collective-permute-start | bytes 786440 | tf_op jit(solution)/shard_map/ppermute | solution.py:437
  68.2 11.2 %collective-permute-start.30 = (bf16[512,256]{1,0:T(8,128)(2,1)S(1)}, bf16[512,256]{1,0:T(8,128)(2,1)S(1)}, u32[]{:S(2)}, u32[]{:S(2)}) collective-permute-start(bf16[512,256]{1,0:T(8,128)(2,1)S(1)} %collective-permute-done.26.refs_0_), channel_id=1, source_target_pairs={{0,2},{1,3},{4,0},{5,1},{8,4},{9,5},{12,8},{13,9},{14,12},{15,13},... | collective-permute-start | bytes 786440 | tf_op jit(solution)/shard_map/ppermute | solution.py:437
  70.2 11.2 %collective-permute-start.31 = (bf16[512,256]{1,0:T(8,128)(2,1)S(1)}, bf16[512,256]{1,0:T(8,128)(2,1)S(1)}, u32[]{:S(2)}, u32[]{:S(2)}) collective-permute-start(bf16[512,256]{1,0:T(8,128)(2,1)S(1)} %collective-permute-done.27.refs_0_), channel_id=1, source_target_pairs={{0,4},{1,5},{4,8},{5,9},{8,12},{9,13},{12,14},{13,15},{14,10},{15,... | collective-permute-start | bytes 786440 | tf_op jit(solution)/shard_map/ppermute | solution.py:437
  73.8 10.8 %collective-permute-start.32 = (bf16[256,256]{1,0:T(8,128)(2,1)S(1)}, bf16[256,256]{1,0:T(8,128)(2,1)S(1)}, u32[]{:S(2)}, u32[]{:S(2)}) collective-permute-start(bf16[256,256]{1,0:T(8,128)(2,1)S(1)} %slice.24), channel_id=1, source_target_pairs={{0,2},{1,3},{4,0},{5,1},{8,4},{9,5},{12,8},{13,9},{14,12},{15,13},... | collective-permute-start | bytes 393224 | tf_op jit(solution)/shard_map/ppermute | solution.py:431
  76.3 7.6 %collective-permute-start.34 = (bf16[256,256]{1,0:T(8,128)(2,1)S(1)}, bf16[256,256]{1,0:T(8,128)(2,1)S(1)}, u32[]{:S(2)}, u32[]{:S(2)}) collective-permute-start(bf16[256,256]{1,0:T(8,128)(2,1)S(1)} %slice.26), channel_id=1, source_target_pairs={{0,4},{1,5},{4,8},{5,9},{8,12},{9,13},{12,14},{13,15},{14,10},{15,... | collective-permute-start | bytes 393224 | tf_op jit(solution)/shard_map/ppermute | solution.py:431
  76.8 10.6 %collective-permute-start.35 = (bf16[256,256]{1,0:T(8,128)(2,1)S(1)}, bf16[256,256]{1,0:T(8,128)(2,1)S(1)}, u32[]{:S(2)}, u32[]{:S(2)}) collective-permute-start(bf16[256,256]{1,0:T(8,128)(2,1)S(1)} %slice.27), channel_id=1, source_target_pairs={{0,4},{1,5},{4,8},{5,9},{8,12},{9,13},{12,14},{13,15},{14,10},{15,... | collective-permute-start | bytes 393224 | tf_op jit(solution)/shard_map/ppermute | solution.py:434
  79.5 6.9 %collective-permute-start.33 = (bf16[256,256]{1,0:T(8,128)(2,1)S(1)}, bf16[256,256]{1,0:T(8,128)(2,1)S(1)}, u32[]{:S(2)}, u32[]{:S(2)}) collective-permute-start(bf16[256,256]{1,0:T(8,128)(2,1)S(1)} %slice.25), channel_id=1, source_target_pairs={{0,2},{1,3},{4,0},{5,1},{8,4},{9,5},{12,8},{13,9},{14,12},{15,13},... | collective-permute-start | bytes 393224 | tf_op jit(solution)/shard_map/ppermute | solution.py:434
  81.4 6.4 %collective-permute-start.36 = (bf16[256,256]{1,0:T(8,128)(2,1)S(1)}, bf16[256,256]{1,0:T(8,128)(2,1)S(1)}, u32[]{:S(2)}, u32[]{:S(2)}) collective-permute-start(bf16[256,256]{1,0:T(8,128)(2,1)S(1)} %slice.28), channel_id=1, source_target_pairs={{0,2},{1,3},{4,0},{5,1},{8,4},{9,5},{12,8},{13,9},{14,12},{15,13},... | collective-permute-start | bytes 393224 | tf_op jit(solution)/shard_map/ppermute | solution.py:426
  84.7 6.4 %collective-permute-start.38 = (bf16[256,256]{1,0:T(8,128)(2,1)S(1)}, bf16[256,256]{1,0:T(8,128)(2,1)S(1)}, u32[]{:S(2)}, u32[]{:S(2)}) collective-permute-start(bf16[256,256]{1,0:T(8,128)(2,1)S(1)} %collective-permute-done.32.refs_0_), channel_id=1, source_target_pairs={{0,2},{1,3},{4,0},{5,1},{8,4},{9,5},{12,8},{13,9},{14,12},{15,13},... | collective-permute-start | bytes 393224 | tf_op jit(solution)/shard_map/ppermute | solution.py:426
  (22 other events, 88.5 us)

commit v12 on v11

--- a/solution.py
+++ b/solution.py
@@ -304,8 +304,6 @@
     for d in range(reach, 0, -1):
         for piece in range(pieces):
             low, high = piece * part, (piece + 1) * part
-            if d == reach > 1 and piece == pieces - 1:
-                last, _ = lax.optimization_barrier((last, peer[d - 1][0]))
             if d == reach:
                 args = (res, own_far[piece], peer_far[piece])
                 sent = pl.pallas_call(
@@ -337,6 +335,8 @@
                     )(last, *args)
                     got[way, piece] = lax.ppermute(last, "ind", left if way else right)
             if later and (d, piece) in ((reach, pieces - 1), (reach - 1, 0)):
+                if d == reach > 1:
+                    last, _ = lax.optimization_barrier((last, peer[d - 1][0]))
                 distances = later.pop(0)
                 (last,) = pick(whole(distances), pltpu.VMEM, light, last)
                 swapped(distances, last)

time: 94.1 us -> 93.5 us (level)
    ppermute x12, waiting for transfers between devices: 17.6 us -> 16.2 us  [on_device(): got[way, piece] = lax.ppermute(last, 'ind', left if way else right)]
    ppermute x2, waiting for transfers between devices: 0.26 us -> 1.43 us  [on_device(): got[1, piece] = lax.ppermute(sent[1], 'ind', left)]
  transfers between devices with their start and end apart: 44 -> 44, of which waited for: 17 -> 16; matrix products, arithmetic and copies ran while one was open for 0% -> 0% of each run, Pallas kernels for 21% -> 21%
where the time goes in v12:
time: 93.5 us; the launch traced here: 93.3 us
  starting transfers between devices  40 us (43%)
  waiting for transfers between devices  30 us (32%)
  Pallas kernels  22 us (24%)
  between operations  1.22 us (1%)
    ppermute x12, waiting for transfers between devices, on_device(): got[way, piece] = lax.ppermute(last, 'ind', left if way else right)  16.2 us
    ppermute x14, starting transfers between devices, on_device(): held[way, piece] = lax.ppermute(message, 'ind', perm)  15 us
    ppermute x12, starting transfers between devices, on_device(): got[way, piece] = lax.ppermute(last, 'ind', left if way else right)  12.8 us
    ppermute x14, waiting for transfers between devices, on_device(): held[way, piece] = lax.ppermute(message, 'ind', perm)  10.4 us
    pallas_call x12, Pallas kernels, on_device(): pl.pallas_call(functools.partial(hop_kernel, ring, (w, peer[w][1]), low,...  6.61 us
    pallas_call x15, Pallas kernels, product(): pl.pallas_call(functools.partial(eta_kernel, ring, places, not eta), in_s...  5.6 us
    ppermute x2, starting transfers between devices, on_device(): got[1, piece] = lax.ppermute(sent[1], 'ind', left)  4.95 us
    pallas_call x4, Pallas kernels, pick(): pl.pallas_call(functools.partial(pick_kernel, ring, wanted, block), in_sp...  3.21 us
  transfers between devices with their start and end apart: 44, of which 16 were waited for; matrix products, arithmetic and copies ran while one was open for 0% of the time, Pallas kernels for 21%

profile of v12, /device:TPU:0, one launch (start us, length us, event | category | flops | bytes accessed | tf_op | source)
XLA Modules:
  0.0 93.3 jit_solution(5464161762300428448)
XLA Ops:
  2.5 1.7 %pick_blocks.5 = (bf16[1,384,512]{2,1,0:T(8,128)(2,1)S(1)}, bf16[1,384,512]{2,1,0:T(8,128)(2,1)S(1)}, bf16[2,384,1024]{2,1,0:T(8,128)(2,1)S(1)}) custom-call(bf16[384,16384]{1,0:T(8,128)(2,1)} %genotype_ref.11, bf16[1,384,512]{2,1,0:T(8,128)(2,1)S(1)} %get-tuple-element.65.refs_0_), custom_call_target="tpu_custom_call" | custom-call | flops 10000000000 | bytes 1000000 | tf_op jit(solution)/shard_map/pick_blocks/pallas_call | solution.py:248
  5.4 3.0 %collective-permute-start.4 = (s16[528,128]{1,0:T(8,128)(2,1)S(1)}, s16[528,128]{1,0:T(8,128)(2,1)S(1)}, u32[]{:S(2)}, u32[]{:S(2)}) collective-permute-start(s16[528,128]{1,0:T(8,128)(2,1)S(1)} %get-tuple-element.74), channel_id=1, source_target_pairs={{0,2},{1,3},{4,0},{5,1},{8,4},{9,5},{12,8},{13,9},{14,12},{15,13},... | collective-permute-start | bytes 405512 | tf_op jit(solution)/shard_map/ppermute | solution.py:319
  9.1 2.0 %collective-permute-start.7 = (s16[528,128]{1,0:T(8,128)(2,1)S(1)}, s16[528,128]{1,0:T(8,128)(2,1)S(1)}, u32[]{:S(2)}, u32[]{:S(2)}) collective-permute-start(s16[528,128]{1,0:T(8,128)(2,1)S(1)} %get-tuple-element.76), channel_id=1, source_target_pairs={{0,2},{1,3},{4,0},{5,1},{8,4},{9,5},{12,8},{13,9},{14,12},{15,13},... | collective-permute-start | bytes 405512 | tf_op jit(solution)/shard_map/ppermute | solution.py:319
  11.4 1.4 %collective-permute-done.4.got_ref = s16[528,128]{1,0:T(8,128)(2,1)S(1)} collective-permute-done((s16[528,128]{1,0:T(8,128)(2,1)S(1)}, s16[528,128]{1,0:T(8,128)(2,1)S(1)}, u32[]{:S(2)}, u32[]{:S(2)}) %collective-permute-start.4) | collective-permute-done | bytes 135200 | tf_op jit(solution)/shard_map/ppermute | solution.py:319
  13.4 2.0 %collective-permute-start.9 = (s16[1040,128]{1,0:T(8,128)(2,1)S(1)}, s16[1040,128]{1,0:T(8,128)(2,1)S(1)}, u32[]{:S(2)}, u32[]{:S(2)}) collective-permute-start(s16[1040,128]{1,0:T(8,128)(2,1)S(1)} %sum_hop.12.before_ref), channel_id=1, source_target_pairs={{0,2},{1,3},{4,0},{5,1},{8,4},{9,5},{12,8},{13,9},{14,12},{15,13},... | collective-permute-start | bytes 798728 | tf_op jit(solution)/shard_map/ppermute | solution.py:336
  17.0 2.0 %collective-permute-start.11 = (s16[1040,128]{1,0:T(8,128)(2,1)S(1)}, s16[1040,128]{1,0:T(8,128)(2,1)S(1)}, u32[]{:S(2)}, u32[]{:S(2)}) collective-permute-start(s16[1040,128]{1,0:T(8,128)(2,1)S(1)} %sum_hop.14.before_ref), channel_id=1, source_target_pairs={{0,2},{1,3},{4,0},{5,1},{8,4},{9,5},{12,8},{13,9},{14,12},{15,13},... | collective-permute-start | bytes 798728 | tf_op jit(solution)/shard_map/ppermute | solution.py:336
  19.7 1.9 %collective-permute-done.9.got_ref = s16[1040,128]{1,0:T(8,128)(2,1)S(1)} collective-permute-done((s16[1040,128]{1,0:T(8,128)(2,1)S(1)}, s16[1040,128]{1,0:T(8,128)(2,1)S(1)}, u32[]{:S(2)}, u32[]{:S(2)}) %collective-permute-start.9) | collective-permute-done | bytes 266272 | tf_op jit(solution)/shard_map/ppermute | solution.py:336
  22.2 1.7 %collective-permute-start.14 = (s16[1040,128]{1,0:T(8,128)(2,1)S(1)}, s16[1040,128]{1,0:T(8,128)(2,1)S(1)}, u32[]{:S(2)}, u32[]{:S(2)}) collective-permute-start(s16[1040,128]{1,0:T(8,128)(2,1)S(1)} %sum_hop.16.before_ref), channel_id=1, source_target_pairs={{0,2},{1,3},{4,0},{5,1},{8,4},{9,5},{12,8},{13,9},{14,12},{15,13},... | collective-permute-start | bytes 798728 | tf_op jit(solution)/shard_map/ppermute | solution.py:336
  24.9 2.5 %collective-permute-done.11.got_ref = s16[1040,128]{1,0:T(8,128)(2,1)S(1)} collective-permute-done((s16[1040,128]{1,0:T(8,128)(2,1)S(1)}, s16[1040,128]{1,0:T(8,128)(2,1)S(1)}, u32[]{:S(2)}, u32[]{:S(2)}) %collective-permute-start.11) | collective-permute-done | bytes 266272 | tf_op jit(solution)/shard_map/ppermute | solution.py:336
  27.9 1.7 %collective-permute-start.16 = (s16[1040,128]{1,0:T(8,128)(2,1)S(1)}, s16[1040,128]{1,0:T(8,128)(2,1)S(1)}, u32[]{:S(2)}, u32[]{:S(2)}) collective-permute-start(s16[1040,128]{1,0:T(8,128)(2,1)S(1)} %sum_hop.18.before_ref), channel_id=1, source_target_pairs={{0,2},{1,3},{4,0},{5,1},{8,4},{9,5},{12,8},{13,9},{14,12},{15,13},... | collective-permute-start | bytes 798728 | tf_op jit(solution)/shard_map/ppermute | solution.py:336
  30.6 2.4 %collective-permute-done.14.got_ref = s16[1040,128]{1,0:T(8,128)(2,1)S(1)} collective-permute-done((s16[1040,128]{1,0:T(8,128)(2,1)S(1)}, s16[1040,128]{1,0:T(8,128)(2,1)S(1)}, u32[]{:S(2)}, u32[]{:S(2)}) %collective-permute-start.14) | collective-permute-done | bytes 266272 | tf_op jit(solution)/shard_map/ppermute | solution.py:336
  33.6 1.7 %collective-permute-start.19 = (s16[1040,128]{1,0:T(8,128)(2,1)S(1)}, s16[1040,128]{1,0:T(8,128)(2,1)S(1)}, u32[]{:S(2)}, u32[]{:S(2)}) collective-permute-start(s16[1040,128]{1,0:T(8,128)(2,1)S(1)} %sum_hop.20.before_ref), channel_id=1, source_target_pairs={{0,2},{1,3},{4,0},{5,1},{8,4},{9,5},{12,8},{13,9},{14,12},{15,13},... | collective-permute-start | bytes 798728 | tf_op jit(solution)/shard_map/ppermute | solution.py:336
  36.3 2.4 %collective-permute-done.16.got_ref = s16[1040,128]{1,0:T(8,128)(2,1)S(1)} collective-permute-done((s16[1040,128]{1,0:T(8,128)(2,1)S(1)}, s16[1040,128]{1,0:T(8,128)(2,1)S(1)}, u32[]{:S(2)}, u32[]{:S(2)}) %collective-permute-start.16) | collective-permute-done | bytes 266272 | tf_op jit(solution)/shard_map/ppermute | solution.py:336
  39.3 1.7 %collective-permute-start.21 = (s16[1040,128]{1,0:T(8,128)(2,1)S(1)}, s16[1040,128]{1,0:T(8,128)(2,1)S(1)}, u32[]{:S(2)}, u32[]{:S(2)}) collective-permute-start(s16[1040,128]{1,0:T(8,128)(2,1)S(1)} %sum_hop.22.before_ref), channel_id=1, source_target_pairs={{0,2},{1,3},{4,0},{5,1},{8,4},{9,5},{12,8},{13,9},{14,12},{15,13},... | collective-permute-start | bytes 798728 | tf_op jit(solution)/shard_map/ppermute | solution.py:336
  42.8 3.7 %collective-permute-done.18.refs_1_ = s16[1040,128]{1,0:T(8,128)(2,1)S(1)} collective-permute-done((s16[1040,128]{1,0:T(8,128)(2,1)S(1)}, s16[1040,128]{1,0:T(8,128)(2,1)S(1)}, u32[]{:S(2)}, u32[]{:S(2)}) %collective-permute-start.18) | collective-permute-done | bytes 266272 | tf_op jit(solution)/shard_map/ppermute | solution.py:336
  46.9 1.6 %collective-permute-start.22 = (bf16[512,256]{1,0:T(8,128)(2,1)S(1)}, bf16[512,256]{1,0:T(8,128)(2,1)S(1)}, u32[]{:S(2)}, u32[]{:S(2)}) collective-permute-start(bf16[512,256]{1,0:T(8,128)(2,1)S(1)} %effect.2.before_ref.refs_0_), channel_id=1, source_target_pairs={{0,2},{1,3},{4,0},{5,1},{8,4},{9,5},{12,8},{13,9},{14,12},{15,13},... | collective-permute-start | bytes 786440 | tf_op jit(solution)/shard_map/ppermute | solution.py:437
  49.0 3.2 %collective-permute-done.20.refs_1_ = s16[1040,128]{1,0:T(8,128)(2,1)S(1)} collective-permute-done((s16[1040,128]{1,0:T(8,128)(2,1)S(1)}, s16[1040,128]{1,0:T(8,128)(2,1)S(1)}, u32[]{:S(2)}, u32[]{:S(2)}) %collective-permute-start.20) | collective-permute-done | bytes 266272 | tf_op jit(solution)/shard_map/ppermute | solution.py:336
  52.6 1.6 %collective-permute-start.24 = (bf16[512,256]{1,0:T(8,128)(2,1)S(1)}, bf16[512,256]{1,0:T(8,128)(2,1)S(1)}, u32[]{:S(2)}, u32[]{:S(2)}) collective-permute-start(bf16[512,256]{1,0:T(8,128)(2,1)S(1)} %effect.3.before_ref.refs_3_), channel_id=1, source_target_pairs={{0,2},{1,3},{4,0},{5,1},{8,4},{9,5},{12,8},{13,9},{14,12},{15,13},... | collective-permute-start | bytes 786440 | tf_op jit(solution)/shard_map/ppermute | solution.py:437
  56.2 1.6 %collective-permute-start.26 = (bf16[512,256]{1,0:T(8,128)(2,1)S(1)}, bf16[512,256]{1,0:T(8,128)(2,1)S(1)}, u32[]{:S(2)}, u32[]{:S(2)}) collective-permute-start(bf16[512,256]{1,0:T(8,128)(2,1)S(1)} %collective-permute-done.22.refs_0_), channel_id=1, source_target_pairs={{0,2},{1,3},{4,0},{5,1},{8,4},{9,5},{12,8},{13,9},{14,12},{15,13},... | collective-permute-start | bytes 786440 | tf_op jit(solution)/shard_map/ppermute | solution.py:437
  59.0 2.8 %collective-permute-done.24.refs_0_ = bf16[512,256]{1,0:T(8,128)(2,1)S(1)} collective-permute-done((bf16[512,256]{1,0:T(8,128)(2,1)S(1)}, bf16[512,256]{1,0:T(8,128)(2,1)S(1)}, u32[]{:S(2)}, u32[]{:S(2)}) %collective-permute-start.24) | collective-permute-done | bytes 262176 | tf_op jit(solution)/shard_map/ppermute | solution.py:437
  61.8 1.6 %collective-permute-start.28 = (bf16[512,256]{1,0:T(8,128)(2,1)S(1)}, bf16[512,256]{1,0:T(8,128)(2,1)S(1)}, u32[]{:S(2)}, u32[]{:S(2)}) collective-permute-start(bf16[512,256]{1,0:T(8,128)(2,1)S(1)} %collective-permute-done.24.refs_0_), channel_id=1, source_target_pairs={{0,2},{1,3},{4,0},{5,1},{8,4},{9,5},{12,8},{13,9},{14,12},{15,13},... | collective-permute-start | bytes 786440 | tf_op jit(solution)/shard_map/ppermute | solution.py:437
  64.7 1.3 %update.2 = (f32[1024,256]{1,0:T(8,128)}, f32[1024,256]{1,0:T(8,128)}, f32[8,128]{1,0:T(8,128)S(1)}) custom-call(f32[384,256]{1,0:T(8,128)S(1)} %get-tuple-element.85.before_ref.refs_3_, f32[256,1024]{1,0:T(8,128)S(1)} %sum_near.1.before_ref.refs_0_, s16[1040,128]{1,0:T(8,128)(2,1)S(1)} %collective-permute-done.18.refs_1_, ...), custom_call_target="tpu_custom_call" | custom-call | flops 1 | bytes 1 | tf_op jit(solution)/shard_map/update/pallas_call | solution.py:374
  66.0 1.4 %collective-permute-done.26.refs_0_ = bf16[512,256]{1,0:T(8,128)(2,1)S(1)} collective-permute-done((bf16[512,256]{1,0:T(8,128)(2,1)S(1)}, bf16[512,256]{1,0:T(8,128)(2,1)S(1)}, u32[]{:S(2)}, u32[]{:S(2)}) %collective-permute-start.26) | collective-permute-done | bytes 262176 | tf_op jit(solution)/shard_map/ppermute | solution.py:437
  67.4 1.6 %collective-permute-start.30 = (bf16[512,256]{1,0:T(8,128)(2,1)S(1)}, bf16[512,256]{1,0:T(8,128)(2,1)S(1)}, u32[]{:S(2)}, u32[]{:S(2)}) collective-permute-start(bf16[512,256]{1,0:T(8,128)(2,1)S(1)} %collective-permute-done.26.refs_0_), channel_id=1, source_target_pairs={{0,2},{1,3},{4,0},{5,1},{8,4},{9,5},{12,8},{13,9},{14,12},{15,13},... | collective-permute-start | bytes 786440 | tf_op jit(solution)/shard_map/ppermute | solution.py:437
  70.3 2.8 %collective-permute-done.28.refs_0_ = bf16[512,256]{1,0:T(8,128)(2,1)S(1)} collective-permute-done((bf16[512,256]{1,0:T(8,128)(2,1)S(1)}, bf16[512,256]{1,0:T(8,128)(2,1)S(1)}, u32[]{:S(2)}, u32[]{:S(2)}) %collective-permute-start.28) | collective-permute-done | bytes 262176 | tf_op jit(solution)/shard_map/ppermute | solution.py:437
  73.1 1.6 %collective-permute-start.32 = (bf16[256,256]{1,0:T(8,128)(2,1)S(1)}, bf16[256,256]{1,0:T(8,128)(2,1)S(1)}, u32[]{:S(2)}, u32[]{:S(2)}) collective-permute-start(bf16[256,256]{1,0:T(8,128)(2,1)S(1)} %slice.24), channel_id=1, source_target_pairs={{0,2},{1,3},{4,0},{5,1},{8,4},{9,5},{12,8},{13,9},{14,12},{15,13},... | collective-permute-start | bytes 393224 | tf_op jit(solution)/shard_map/ppermute | solution.py:431
  76.0 1.3 %collective-permute-start.35 = (bf16[256,256]{1,0:T(8,128)(2,1)S(1)}, bf16[256,256]{1,0:T(8,128)(2,1)S(1)}, u32[]{:S(2)}, u32[]{:S(2)}) collective-permute-start(bf16[256,256]{1,0:T(8,128)(2,1)S(1)} %slice.27), channel_id=1, source_target_pairs={{0,4},{1,5},{4,8},{5,9},{8,12},{9,13},{12,14},{13,15},{14,10},{15,... | collective-permute-start | bytes 393224 | tf_op jit(solution)/shard_map/ppermute | solution.py:434
  77.3 1.3 %update.3 = (f32[1024,256]{1,0:T(8,128)}, f32[1024,256]{1,0:T(8,128)}, f32[8,128]{1,0:T(8,128)S(1)}) custom-call(f32[384,256]{1,0:T(8,128)S(1)} %get-tuple-element.98.before_ref.refs_3_, f32[256,1024]{1,0:T(8,128)S(1)} %sum_near.1.before_ref.refs_0_, ...), custom_call_target="tpu_custom_call", output_to_operand_aliasing={{0}: (8, {}), {1}: (9, {})} | custom-call | flops 1 | bytes 1 | tf_op jit(solution)/shard_map/update/pallas_call | solution.py:374
  78.7 1.6 %collective-permute-start.33 = (bf16[256,256]{1,0:T(8,128)(2,1)S(1)}, bf16[256,256]{1,0:T(8,128)(2,1)S(1)}, u32[]{:S(2)}, u32[]{:S(2)}) collective-permute-start(bf16[256,256]{1,0:T(8,128)(2,1)S(1)} %slice.25), channel_id=1, source_target_pairs={{0,2},{1,3},{4,0},{5,1},{8,4},{9,5},{12,8},{13,9},{14,12},{15,13},... | collective-permute-start | bytes 393224 | tf_op jit(solution)/shard_map/ppermute | solution.py:434
  80.6 1.6 %collective-permute-start.36 = (bf16[256,256]{1,0:T(8,128)(2,1)S(1)}, bf16[256,256]{1,0:T(8,128)(2,1)S(1)}, u32[]{:S(2)}, u32[]{:S(2)}) collective-permute-start(bf16[256,256]{1,0:T(8,128)(2,1)S(1)} %slice.28), channel_id=1, source_target_pairs={{0,2},{1,3},{4,0},{5,1},{8,4},{9,5},{12,8},{13,9},{14,12},{15,13},... | collective-permute-start | bytes 393224 | tf_op jit(solution)/shard_map/ppermute | solution.py:426
  83.9 1.7 %collective-permute-start.38 = (bf16[256,256]{1,0:T(8,128)(2,1)S(1)}, bf16[256,256]{1,0:T(8,128)(2,1)S(1)}, u32[]{:S(2)}, u32[]{:S(2)}) collective-permute-start(bf16[256,256]{1,0:T(8,128)(2,1)S(1)} %collective-permute-done.32.refs_0_), channel_id=1, source_target_pairs={{0,2},{1,3},{4,0},{5,1},{8,4},{9,5},{12,8},{13,9},{14,12},{15,13},... | collective-permute-start | bytes 393224 | tf_op jit(solution)/shard_map/ppermute | solution.py:426
  87.5 2.0 %collective-permute-done.37.refs_0_ = bf16[256,256]{1,0:T(8,128)(2,1)S(1)} collective-permute-done((bf16[256,256]{1,0:T(8,128)(2,1)S(1)}, bf16[256,256]{1,0:T(8,128)(2,1)S(1)}, u32[]{:S(2)}, u32[]{:S(2)}) %collective-permute-start.37) | collective-permute-done | bytes 131104 | tf_op jit(solution)/shard_map/ppermute | solution.py:426
  (125 shorter events, 29.4 us)
Async XLA Ops:
  5.4 7.4 %collective-permute-start.4 = (s16[528,128]{1,0:T(8,128)(2,1)S(1)}, s16[528,128]{1,0:T(8,128)(2,1)S(1)}, u32[]{:S(2)}, u32[]{:S(2)}) collective-permute-start(s16[528,128]{1,0:T(8,128)(2,1)S(1)} %get-tuple-element.74), channel_id=1, source_target_pairs={{0,2},{1,3},{4,0},{5,1},{8,4},{9,5},{12,8},{13,9},{14,12},{15,13},... | collective-permute-start | bytes 405512 | tf_op jit(solution)/shard_map/ppermute | solution.py:319
  8.4 7.0 %collective-permute-start.5 = (s16[528,128]{1,0:T(8,128)(2,1)S(1)}, s16[528,128]{1,0:T(8,128)(2,1)S(1)}, u32[]{:S(2)}, u32[]{:S(2)}) collective-permute-start(s16[528,128]{1,0:T(8,128)(2,1)S(1)} %get-tuple-element.69.before_ref), channel_id=1, source_target_pairs={{0,4},{1,5},{4,8},{5,9},{8,12},{9,13},{12,14},{13,15},{14,10},{15,... | collective-permute-start | bytes 405512 | tf_op jit(solution)/shard_map/ppermute | solution.py:318
  9.1 7.3 %collective-permute-start.7 = (s16[528,128]{1,0:T(8,128)(2,1)S(1)}, s16[528,128]{1,0:T(8,128)(2,1)S(1)}, u32[]{:S(2)}, u32[]{:S(2)}) collective-permute-start(s16[528,128]{1,0:T(8,128)(2,1)S(1)} %get-tuple-element.76), channel_id=1, source_target_pairs={{0,2},{1,3},{4,0},{5,1},{8,4},{9,5},{12,8},{13,9},{14,12},{15,13},... | collective-permute-start | bytes 405512 | tf_op jit(solution)/shard_map/ppermute | solution.py:319
  11.0 8.0 %collective-permute-start.8 = (s16[528,128]{1,0:T(8,128)(2,1)S(1)}, s16[528,128]{1,0:T(8,128)(2,1)S(1)}, u32[]{:S(2)}, u32[]{:S(2)}) collective-permute-start(s16[528,128]{1,0:T(8,128)(2,1)S(1)} %get-tuple-element.73.refs_0_), channel_id=1, source_target_pairs={{0,4},{1,5},{4,8},{5,9},{8,12},{9,13},{12,14},{13,15},{14,10},{15,... | collective-permute-start | bytes 405512 | tf_op jit(solution)/shard_map/ppermute | solution.py:318
  13.4 8.2 %collective-permute-start.9 = (s16[1040,128]{1,0:T(8,128)(2,1)S(1)}, s16[1040,128]{1,0:T(8,128)(2,1)S(1)}, u32[]{:S(2)}, u32[]{:S(2)}) collective-permute-start(s16[1040,128]{1,0:T(8,128)(2,1)S(1)} %sum_hop.12.before_ref), channel_id=1, source_target_pairs={{0,2},{1,3},{4,0},{5,1},{8,4},{9,5},{12,8},{13,9},{14,12},{15,13},... | collective-permute-start | bytes 798728 | tf_op jit(solution)/shard_map/ppermute | solution.py:336
  16.0 7.9 %collective-permute-start.10 = (s16[1040,128]{1,0:T(8,128)(2,1)S(1)}, s16[1040,128]{1,0:T(8,128)(2,1)S(1)}, u32[]{:S(2)}, u32[]{:S(2)}) collective-permute-start(s16[1040,128]{1,0:T(8,128)(2,1)S(1)} %sum_hop.13.refs_0_), channel_id=1, source_target_pairs={{0,4},{1,5},{4,8},{5,9},{8,12},{9,13},{12,14},{13,15},{14,10},{15,... | collective-permute-start | bytes 798728 | tf_op jit(solution)/shard_map/ppermute | solution.py:336
  16.3 16.7 %collective-permute-start.13 = (bf16[3,384,1024]{2,1,0:T(8,128)(2,1)S(1)}, bf16[3,384,1024]{2,1,0:T(8,128)(2,1)S(1)}, u32[]{:S(2)}, u32[]{:S(2)}) collective-permute-start(bf16[3,384,1024]{2,1,0:T(8,128)(2,1)S(1)} %pick_blocks.7.before_ref), channel_id=1, source_target_pairs={{0,1},{1,0},{2,3},{3,2},{4,5},{5,4},{6,7},{7,6},{8,9},{9,8},{10,11... | collective-permute-start | bytes 7077896 | tf_op jit(solution)/shard_map/ppermute | solution.py:269
  17.0 10.3 %collective-permute-start.11 = (s16[1040,128]{1,0:T(8,128)(2,1)S(1)}, s16[1040,128]{1,0:T(8,128)(2,1)S(1)}, u32[]{:S(2)}, u32[]{:S(2)}) collective-permute-start(s16[1040,128]{1,0:T(8,128)(2,1)S(1)} %sum_hop.14.before_ref), channel_id=1, source_target_pairs={{0,2},{1,3},{4,0},{5,1},{8,4},{9,5},{12,8},{13,9},{14,12},{15,13},... | collective-permute-start | bytes 798728 | tf_op jit(solution)/shard_map/ppermute | solution.py:336
  19.5 10.1 %collective-permute-start.12 = (s16[1040,128]{1,0:T(8,128)(2,1)S(1)}, s16[1040,128]{1,0:T(8,128)(2,1)S(1)}, u32[]{:S(2)}, u32[]{:S(2)}) collective-permute-start(s16[1040,128]{1,0:T(8,128)(2,1)S(1)} %sum_hop.15.before_ref), channel_id=1, source_target_pairs={{0,4},{1,5},{4,8},{5,9},{8,12},{9,13},{12,14},{13,15},{14,10},{15,... | collective-permute-start | bytes 798728 | tf_op jit(solution)/shard_map/ppermute | solution.py:336
  22.2 10.8 %collective-permute-start.14 = (s16[1040,128]{1,0:T(8,128)(2,1)S(1)}, s16[1040,128]{1,0:T(8,128)(2,1)S(1)}, u32[]{:S(2)}, u32[]{:S(2)}) collective-permute-start(s16[1040,128]{1,0:T(8,128)(2,1)S(1)} %sum_hop.16.before_ref), channel_id=1, source_target_pairs={{0,2},{1,3},{4,0},{5,1},{8,4},{9,5},{12,8},{13,9},{14,12},{15,13},... | collective-permute-start | bytes 798728 | tf_op jit(solution)/shard_map/ppermute | solution.py:336
  24.5 10.9 %collective-permute-start.15 = (s16[1040,128]{1,0:T(8,128)(2,1)S(1)}, s16[1040,128]{1,0:T(8,128)(2,1)S(1)}, u32[]{:S(2)}, u32[]{:S(2)}) collective-permute-start(s16[1040,128]{1,0:T(8,128)(2,1)S(1)} %sum_hop.17.before_ref), channel_id=1, source_target_pairs={{0,4},{1,5},{4,8},{5,9},{8,12},{9,13},{12,14},{13,15},{14,10},{15,... | collective-permute-start | bytes 798728 | tf_op jit(solution)/shard_map/ppermute | solution.py:336
  27.9 10.9 %collective-permute-start.16 = (s16[1040,128]{1,0:T(8,128)(2,1)S(1)}, s16[1040,128]{1,0:T(8,128)(2,1)S(1)}, u32[]{:S(2)}, u32[]{:S(2)}) collective-permute-start(s16[1040,128]{1,0:T(8,128)(2,1)S(1)} %sum_hop.18.before_ref), channel_id=1, source_target_pairs={{0,2},{1,3},{4,0},{5,1},{8,4},{9,5},{12,8},{13,9},{14,12},{15,13},... | collective-permute-start | bytes 798728 | tf_op jit(solution)/shard_map/ppermute | solution.py:336
  30.2 10.8 %collective-permute-start.17 = (s16[1040,128]{1,0:T(8,128)(2,1)S(1)}, s16[1040,128]{1,0:T(8,128)(2,1)S(1)}, u32[]{:S(2)}, u32[]{:S(2)}) collective-permute-start(s16[1040,128]{1,0:T(8,128)(2,1)S(1)} %sum_hop.19.before_ref), channel_id=1, source_target_pairs={{0,4},{1,5},{4,8},{5,9},{8,12},{9,13},{12,14},{13,15},{14,10},{15,... | collective-permute-start | bytes 798728 | tf_op jit(solution)/shard_map/ppermute | solution.py:336
  33.6 12.9 %collective-permute-start.19 = (s16[1040,128]{1,0:T(8,128)(2,1)S(1)}, s16[1040,128]{1,0:T(8,128)(2,1)S(1)}, u32[]{:S(2)}, u32[]{:S(2)}) collective-permute-start(s16[1040,128]{1,0:T(8,128)(2,1)S(1)} %sum_hop.20.before_ref), channel_id=1, source_target_pairs={{0,2},{1,3},{4,0},{5,1},{8,4},{9,5},{12,8},{13,9},{14,12},{15,13},... | collective-permute-start | bytes 798728 | tf_op jit(solution)/shard_map/ppermute | solution.py:336
  35.9 10.6 %collective-permute-start.18 = (s16[1040,128]{1,0:T(8,128)(2,1)S(1)}, s16[1040,128]{1,0:T(8,128)(2,1)S(1)}, u32[]{:S(2)}, u32[]{:S(2)}) collective-permute-start(s16[1040,128]{1,0:T(8,128)(2,1)S(1)} %sum_hop.21.before_ref), channel_id=1, source_target_pairs={{0,4},{1,5},{4,8},{5,9},{8,12},{9,13},{12,14},{13,15},{14,10},{15,... | collective-permute-start | bytes 798728 | tf_op jit(solution)/shard_map/ppermute | solution.py:336
  39.3 12.9 %collective-permute-start.21 = (s16[1040,128]{1,0:T(8,128)(2,1)S(1)}, s16[1040,128]{1,0:T(8,128)(2,1)S(1)}, u32[]{:S(2)}, u32[]{:S(2)}) collective-permute-start(s16[1040,128]{1,0:T(8,128)(2,1)S(1)} %sum_hop.22.before_ref), channel_id=1, source_target_pairs={{0,2},{1,3},{4,0},{5,1},{8,4},{9,5},{12,8},{13,9},{14,12},{15,13},... | collective-permute-start | bytes 798728 | tf_op jit(solution)/shard_map/ppermute | solution.py:336
  41.7 10.5 %collective-permute-start.20 = (s16[1040,128]{1,0:T(8,128)(2,1)S(1)}, s16[1040,128]{1,0:T(8,128)(2,1)S(1)}, u32[]{:S(2)}, u32[]{:S(2)}) collective-permute-start(s16[1040,128]{1,0:T(8,128)(2,1)S(1)} %sum_hop.23.before_ref), channel_id=1, source_target_pairs={{0,4},{1,5},{4,8},{5,9},{8,12},{9,13},{12,14},{13,15},{14,10},{15,... | collective-permute-start | bytes 798728 | tf_op jit(solution)/shard_map/ppermute | solution.py:336
  46.9 9.3 %collective-permute-start.22 = (bf16[512,256]{1,0:T(8,128)(2,1)S(1)}, bf16[512,256]{1,0:T(8,128)(2,1)S(1)}, u32[]{:S(2)}, u32[]{:S(2)}) collective-permute-start(bf16[512,256]{1,0:T(8,128)(2,1)S(1)} %effect.2.before_ref.refs_0_), channel_id=1, source_target_pairs={{0,2},{1,3},{4,0},{5,1},{8,4},{9,5},{12,8},{13,9},{14,12},{15,13},... | collective-permute-start | bytes 786440 | tf_op jit(solution)/shard_map/ppermute | solution.py:437
  48.5 9.6 %collective-permute-start.23 = (bf16[512,256]{1,0:T(8,128)(2,1)S(1)}, bf16[512,256]{1,0:T(8,128)(2,1)S(1)}, u32[]{:S(2)}, u32[]{:S(2)}) collective-permute-start(bf16[512,256]{1,0:T(8,128)(2,1)S(1)} %effect.2.before_ref.refs_0_), channel_id=1, source_target_pairs={{0,4},{1,5},{4,8},{5,9},{8,12},{9,13},{12,14},{13,15},{14,10},{15,... | collective-permute-start | bytes 786440 | tf_op jit(solution)/shard_map/ppermute | solution.py:437
  52.6 9.2 %collective-permute-start.24 = (bf16[512,256]{1,0:T(8,128)(2,1)S(1)}, bf16[512,256]{1,0:T(8,128)(2,1)S(1)}, u32[]{:S(2)}, u32[]{:S(2)}) collective-permute-start(bf16[512,256]{1,0:T(8,128)(2,1)S(1)} %effect.3.before_ref.refs_3_), channel_id=1, source_target_pairs={{0,2},{1,3},{4,0},{5,1},{8,4},{9,5},{12,8},{13,9},{14,12},{15,13},... | collective-permute-start | bytes 786440 | tf_op jit(solution)/shard_map/ppermute | solution.py:437
  54.2 9.6 %collective-permute-start.25 = (bf16[512,256]{1,0:T(8,128)(2,1)S(1)}, bf16[512,256]{1,0:T(8,128)(2,1)S(1)}, u32[]{:S(2)}, u32[]{:S(2)}) collective-permute-start(bf16[512,256]{1,0:T(8,128)(2,1)S(1)} %effect.3.before_ref.refs_3_), channel_id=1, source_target_pairs={{0,4},{1,5},{4,8},{5,9},{8,12},{9,13},{12,14},{13,15},{14,10},{15,... | collective-permute-start | bytes 786440 | tf_op jit(solution)/shard_map/ppermute | solution.py:437
  56.2 11.2 %collective-permute-start.26 = (bf16[512,256]{1,0:T(8,128)(2,1)S(1)}, bf16[512,256]{1,0:T(8,128)(2,1)S(1)}, u32[]{:S(2)}, u32[]{:S(2)}) collective-permute-start(bf16[512,256]{1,0:T(8,128)(2,1)S(1)} %collective-permute-done.22.refs_0_), channel_id=1, source_target_pairs={{0,2},{1,3},{4,0},{5,1},{8,4},{9,5},{12,8},{13,9},{14,12},{15,13},... | collective-permute-start | bytes 786440 | tf_op jit(solution)/shard_map/ppermute | solution.py:437
  58.2 11.2 %collective-permute-start.27 = (bf16[512,256]{1,0:T(8,128)(2,1)S(1)}, bf16[512,256]{1,0:T(8,128)(2,1)S(1)}, u32[]{:S(2)}, u32[]{:S(2)}) collective-permute-start(bf16[512,256]{1,0:T(8,128)(2,1)S(1)} %collective-permute-done.23.refs_0_), channel_id=1, source_target_pairs={{0,4},{1,5},{4,8},{5,9},{8,12},{9,13},{12,14},{13,15},{14,10},{15,... | collective-permute-start | bytes 786440 | tf_op jit(solution)/shard_map/ppermute | solution.py:437
  61.8 11.2 %collective-permute-start.28 = (bf16[512,256]{1,0:T(8,128)(2,1)S(1)}, bf16[512,256]{1,0:T(8,128)(2,1)S(1)}, u32[]{:S(2)}, u32[]{:S(2)}) collective-permute-start(bf16[512,256]{1,0:T(8,128)(2,1)S(1)} %collective-permute-done.24.refs_0_), channel_id=1, source_target_pairs={{0,2},{1,3},{4,0},{5,1},{8,4},{9,5},{12,8},{13,9},{14,12},{15,13},... | collective-permute-start | bytes 786440 | tf_op jit(solution)/shard_map/ppermute | solution.py:437
  63.8 11.3 %collective-permute-start.29 = (bf16[512,256]{1,0:T(8,128)(2,1)S(1)}, bf16[512,256]{1,0:T(8,128)(2,1)S(1)}, u32[]{:S(2)}, u32[]{:S(2)}) collective-permute-start(bf16[512,256]{1,0:T(8,128)(2,1)S(1)} %collective-permute-done.25.refs_0_), channel_id=1, source_target_pairs={{0,4},{1,5},{4,8},{5,9},{8,12},{9,13},{12,14},{13,15},{14,10},{15,... | collective-permute-start | bytes 786440 | tf_op jit(solution)/shard_map/ppermute | solution.py:437
  67.4 11.2 %collective-permute-start.30 = (bf16[512,256]{1,0:T(8,128)(2,1)S(1)}, bf16[512,256]{1,0:T(8,128)(2,1)S(1)}, u32[]{:S(2)}, u32[]{:S(2)}) collective-permute-start(bf16[512,256]{1,0:T(8,128)(2,1)S(1)} %collective-permute-done.26.refs_0_), channel_id=1, source_target_pairs={{0,2},{1,3},{4,0},{5,1},{8,4},{9,5},{12,8},{13,9},{14,12},{15,13},... | collective-permute-start | bytes 786440 | tf_op jit(solution)/shard_map/ppermute | solution.py:437
  69.4 11.2 %collective-permute-start.31 = (bf16[512,256]{1,0:T(8,128)(2,1)S(1)}, bf16[512,256]{1,0:T(8,128)(2,1)S(1)}, u32[]{:S(2)}, u32[]{:S(2)}) collective-permute-start(bf16[512,256]{1,0:T(8,128)(2,1)S(1)} %collective-permute-done.27.refs_0_), channel_id=1, source_target_pairs={{0,4},{1,5},{4,8},{5,9},{8,12},{9,13},{12,14},{13,15},{14,10},{15,... | collective-permute-start | bytes 786440 | tf_op jit(solution)/shard_map/ppermute | solution.py:437
  73.1 10.8 %collective-permute-start.32 = (bf16[256,256]{1,0:T(8,128)(2,1)S(1)}, bf16[256,256]{1,0:T(8,128)(2,1)S(1)}, u32[]{:S(2)}, u32[]{:S(2)}) collective-permute-start(bf16[256,256]{1,0:T(8,128)(2,1)S(1)} %slice.24), channel_id=1, source_target_pairs={{0,2},{1,3},{4,0},{5,1},{8,4},{9,5},{12,8},{13,9},{14,12},{15,13},... | collective-permute-start | bytes 393224 | tf_op jit(solution)/shard_map/ppermute | solution.py:431
  75.5 7.6 %collective-permute-start.34 = (bf16[256,256]{1,0:T(8,128)(2,1)S(1)}, bf16[256,256]{1,0:T(8,128)(2,1)S(1)}, u32[]{:S(2)}, u32[]{:S(2)}) collective-permute-start(bf16[256,256]{1,0:T(8,128)(2,1)S(1)} %slice.26), channel_id=1, source_target_pairs={{0,4},{1,5},{4,8},{5,9},{8,12},{9,13},{12,14},{13,15},{14,10},{15,... | collective-permute-start | bytes 393224 | tf_op jit(solution)/shard_map/ppermute | solution.py:431
  76.0 10.8 %collective-permute-start.35 = (bf16[256,256]{1,0:T(8,128)(2,1)S(1)}, bf16[256,256]{1,0:T(8,128)(2,1)S(1)}, u32[]{:S(2)}, u32[]{:S(2)}) collective-permute-start(bf16[256,256]{1,0:T(8,128)(2,1)S(1)} %slice.27), channel_id=1, source_target_pairs={{0,4},{1,5},{4,8},{5,9},{8,12},{9,13},{12,14},{13,15},{14,10},{15,... | collective-permute-start | bytes 393224 | tf_op jit(solution)/shard_map/ppermute | solution.py:434
  78.7 6.9 %collective-permute-start.33 = (bf16[256,256]{1,0:T(8,128)(2,1)S(1)}, bf16[256,256]{1,0:T(8,128)(2,1)S(1)}, u32[]{:S(2)}, u32[]{:S(2)}) collective-permute-start(bf16[256,256]{1,0:T(8,128)(2,1)S(1)} %slice.25), channel_id=1, source_target_pairs={{0,2},{1,3},{4,0},{5,1},{8,4},{9,5},{12,8},{13,9},{14,12},{15,13},... | collective-permute-start | bytes 393224 | tf_op jit(solution)/shard_map/ppermute | solution.py:434
  80.6 6.6 %collective-permute-start.36 = (bf16[256,256]{1,0:T(8,128)(2,1)S(1)}, bf16[256,256]{1,0:T(8,128)(2,1)S(1)}, u32[]{:S(2)}, u32[]{:S(2)}) collective-permute-start(bf16[256,256]{1,0:T(8,128)(2,1)S(1)} %slice.28), channel_id=1, source_target_pairs={{0,2},{1,3},{4,0},{5,1},{8,4},{9,5},{12,8},{13,9},{14,12},{15,13},... | collective-permute-start | bytes 393224 | tf_op jit(solution)/shard_map/ppermute | solution.py:426
  (22 other events, 89.9 us)

commit v13 on v12

--- a/solution.py
+++ b/solution.py
@@ -120,11 +120,17 @@
     encode(left_ref, tiles[half:])
 
 
-def hop_kernel(
-    ring, at, low, high, way, before_ref, res_ref, own_ref, peer_ref, got_ref, out_ref
-):
+def hop_kernel(ring, at, low, high, way, before_ref, res_ref, own_ref, peer_ref, got_ref, out_ref):
     own = own_columns(ring, own_ref, at[0], low, high)
-    tiles = tiles_of(local_sum(res_ref, own, peer_ref[at[1], :, low:high]))
+    add_and_send(local_sum(res_ref, own, peer_ref[at[1], :, low:high]), way, got_ref, out_ref)
+
+
+def add_kernel(way, before_ref, local_ref, got_ref, out_ref):
+    add_and_send(local_ref[...], way, got_ref, out_ref)
+
+
+def add_and_send(local, way, got_ref, out_ref):
+    tiles = tiles_of(local)
     got = decode(got_ref)
     height = tiles[0].shape[0]
     count = got.shape[0] // height
@@ -134,9 +140,9 @@
     encode(out_ref, tiles)
 
 
-def near_kernel(ring, at, before_ref, res_ref, own_ref, peer_ref, out_ref):
-    own = own_columns(ring, own_ref, at[0], 0, peer_ref.shape[2])
-    out_ref[...] = local_sum(res_ref, own, peer_ref[at[1]])
+def local_kernel(ring, at, low, high, before_ref, res_ref, own_ref, peer_ref, out_ref):
+    own = own_columns(ring, own_ref, at[0], low, high)
+    out_ref[...] = local_sum(res_ref, own, peer_ref[at[1], :, low:high])
 
 
 def new_state(total, low, first, rows, refs):
@@ -209,9 +215,13 @@
     refs[-1][...] = columns_product(ring, places, genotype_ref, refs, eta)
 
 
-def end_kernel(ring, places, genotype_ref, eta_ref, upper_ref, lower_ref, labels_ref, *refs):
+def other_kernel(ring, places, genotype_ref, eta_ref, upper_ref, lower_ref, *refs):
     got = jnp.concatenate([upper_ref[...], lower_ref[...]], axis=0)
-    eta = columns_product(ring, places, genotype_ref, refs, eta_ref[...] + got)
+    refs[-1][...] = columns_product(ring, places, genotype_ref, refs, eta_ref[...] + got)
+
+
+def end_kernel(ring, places, genotype_ref, eta_ref, labels_ref, *refs):
+    eta = columns_product(ring, places, genotype_ref, refs, eta_ref[...])
     refs[-1][...] = 4.0 * (labels_ref[...].astype(jnp.float32) - jax.nn.sigmoid(eta))
 
 
@@ -300,6 +310,17 @@
     def shape_of(width):
         return jax.ShapeDtypeStruct((width // LANES * cols + PAD, LANES), jnp.int16)
 
+    def local(d, low, high, before, cost):
+        args = (res, genotype, peer[d][0])
+        return pl.pallas_call(
+            functools.partial(local_kernel, ring, (d, peer[d][1]), low, high),
+            in_specs=after(before, args),
+            out_shape=jax.ShapeDtypeStruct((cols, high - low), f32),
+            compiler_params=params,
+            cost_estimate=cost,
+            name="sum_local",
+        )(before, *args)
+
     got = {}
     for d in range(reach, 0, -1):
         for piece in range(pieces):
@@ -320,13 +341,23 @@
             else:
                 if d == reach - 1 > 1 and piece == pieces - 1:
                     last, _ = lax.optimization_barrier((last, peer[d - 1][0]))
+                ahead = {}
+                if d == reach - 1 and piece == 0:
+                    for way in (1, 0):
+                        w = size - d if way else d
+                        ahead[way] = last = local(w, low, high, last, light)
                 for way in (1, 0):
                     w = size - d if way else d
-                    args = (res, genotype, peer[w][0], got[way, piece])
+                    if ahead:
+                        kernel = functools.partial(add_kernel, way)
+                        args = (ahead[way], got[way, piece])
+                    else:
+                        kernel = functools.partial(
+                            hop_kernel, ring, (w, peer[w][1]), low, high, way
+                        )
+                        args = (res, genotype, peer[w][0], got[way, piece])
                     last = pl.pallas_call(
-                        functools.partial(
-                            hop_kernel, ring, (w, peer[w][1]), low, high, way
-                        ),
+                        kernel,
                         in_specs=after(last, args),
                         out_shape=shape_of(part),
                         compiler_params=params,
@@ -341,14 +372,7 @@
                 (last,) = pick(whole(distances), pltpu.VMEM, light, last)
                 swapped(distances, last)
 
-    near = last = pl.pallas_call(
-        functools.partial(near_kernel, ring, (0, peer[0][1])),
-        in_specs=after(last, (res, genotype, peer[0][0])),
-        out_shape=jax.ShapeDtypeStruct((cols, block), f32),
-        compiler_params=params,
-        cost_estimate=light,
-        name="sum_near",
-    )(last, res, genotype, peer[0][0])
+    near = last = local(0, 0, block, last, light)
 
     prior = prior_logit.reshape(1, cols)
     scale = slab_scale.reshape(1, cols)
@@ -459,13 +483,21 @@
         cost_estimate=heavy,
         name="own_last",
     )(genotype, eta[0], offset.reshape(1, cols), *[effect for _, _, effect in final])
+    there = [(d, low, True) for d, low, _ in final]
+    mine = pl.pallas_call(
+        functools.partial(other_kernel, ring, there[:1]),
+        out_shape=eta_shape,
+        compiler_params=params,
+        cost_estimate=heavy,
+        name="other_last",
+    )(genotype, mine, *eta_got, others[0])
     resid_new = pl.pallas_call(
-        functools.partial(end_kernel, ring, [(d, low, True) for d, low, _ in final]),
+        functools.partial(end_kernel, ring, there[1:]),
         out_shape=eta_shape,
         compiler_params=params,
         cost_estimate=light,
         name="new_residual",
-    )(genotype, mine, *eta_got, labels, *others)
+    )(genotype, mine, labels, *others[1:])
     return (outs[0], outs[1], resid_new)
 
 

time: 93.5 us -> 94 us (level)
    ppermute x12, waiting for transfers between devices: 16.2 us -> 17.7 us  [on_device(): got[way, piece] = lax.ppermute(last, 'ind', left if way else right)]
    pallas_call x14 -> x17, Pallas kernels: 8.35 us -> 8.6 us  [the longest x12 5.83 us: on_device(): pl.pallas_call(kernel, in_specs=after(last, args), out_shape=shape_of(par...]
where the time goes in v13:
time: 94 us; the launch traced here: 93.8 us
  starting transfers between devices  40.5 us (43%)
  waiting for transfers between devices  29.6 us (31%)
  Pallas kernels  22.3 us (24%)
  between operations  1.24 us (1%)
    ppermute x12, waiting for transfers between devices, on_device(): got[way, piece] = lax.ppermute(last, 'ind', left if way else right)  17.7 us
    ppermute x14, starting transfers between devices, on_device(): held[way, piece] = lax.ppermute(message, 'ind', perm)  15.3 us
    ppermute x12, starting transfers between devices, on_device(): got[way, piece] = lax.ppermute(last, 'ind', left if way else right)  13 us
    ppermute x14, waiting for transfers between devices, on_device(): held[way, piece] = lax.ppermute(message, 'ind', perm)  9.7 us
    pallas_call x12, Pallas kernels, on_device(): pl.pallas_call(kernel, in_specs=after(last, args), out_shape=shape_of(par...  5.83 us
    pallas_call x15, Pallas kernels, product(): pl.pallas_call(functools.partial(eta_kernel, ring, places, not eta), in_s...  5.59 us
    ppermute x2, starting transfers between devices, on_device(): got[1, piece] = lax.ppermute(sent[1], 'ind', left)  4.95 us
    pallas_call x4, Pallas kernels, pick(): pl.pallas_call(functools.partial(pick_kernel, ring, wanted, block), in_sp...  3.27 us
  transfers between devices with their start and end apart: 44, of which 16 were waited for; matrix products, arithmetic and copies ran while one was open for 0% of the time, Pallas kernels for 21%

profile of v13, /device:TPU:0, one launch (start us, length us, event | category | flops | bytes accessed | tf_op | source)
XLA Modules:
  0.0 93.8 jit_solution(7970065713670341426)
XLA Ops:
  0.6 1.2 %pick_blocks.4 = (bf16[1,384,512]{2,1,0:T(8,128)(2,1)S(1)}, bf16[1,384,512]{2,1,0:T(8,128)(2,1)S(1)}) custom-call(bf16[384,16384]{1,0:T(8,128)(2,1)} %genotype_ref.13), custom_call_target="tpu_custom_call" | custom-call | flops 1 | bytes 1 | tf_op jit(solution)/shard_map/pick_blocks/pallas_call | solution.py:258
  2.5 1.7 %pick_blocks.5 = (bf16[1,384,512]{2,1,0:T(8,128)(2,1)S(1)}, bf16[1,384,512]{2,1,0:T(8,128)(2,1)S(1)}, bf16[2,384,1024]{2,1,0:T(8,128)(2,1)S(1)}) custom-call(bf16[384,16384]{1,0:T(8,128)(2,1)} %genotype_ref.13, bf16[1,384,512]{2,1,0:T(8,128)(2,1)S(1)} %get-tuple-element.65.refs_0_), custom_call_target="tpu_custom_call" | custom-call | flops 10000000000 | bytes 1000000 | tf_op jit(solution)/shard_map/pick_blocks/pallas_call | solution.py:258
  5.4 3.0 %collective-permute-start.4 = (s16[528,128]{1,0:T(8,128)(2,1)S(1)}, s16[528,128]{1,0:T(8,128)(2,1)S(1)}, u32[]{:S(2)}, u32[]{:S(2)}) collective-permute-start(s16[528,128]{1,0:T(8,128)(2,1)S(1)} %get-tuple-element.74), channel_id=1, source_target_pairs={{0,2},{1,3},{4,0},{5,1},{8,4},{9,5},{12,8},{13,9},{14,12},{15,13},... | collective-permute-start | bytes 405512 | tf_op jit(solution)/shard_map/ppermute | solution.py:340
  9.1 2.0 %collective-permute-start.7 = (s16[528,128]{1,0:T(8,128)(2,1)S(1)}, s16[528,128]{1,0:T(8,128)(2,1)S(1)}, u32[]{:S(2)}, u32[]{:S(2)}) collective-permute-start(s16[528,128]{1,0:T(8,128)(2,1)S(1)} %get-tuple-element.76), channel_id=1, source_target_pairs={{0,2},{1,3},{4,0},{5,1},{8,4},{9,5},{12,8},{13,9},{14,12},{15,13},... | collective-permute-start | bytes 405512 | tf_op jit(solution)/shard_map/ppermute | solution.py:340
  13.0 2.0 %collective-permute-start.9 = (s16[1040,128]{1,0:T(8,128)(2,1)S(1)}, s16[1040,128]{1,0:T(8,128)(2,1)S(1)}, u32[]{:S(2)}, u32[]{:S(2)}) collective-permute-start(s16[1040,128]{1,0:T(8,128)(2,1)S(1)} %sum_hop.12.before_ref), channel_id=1, source_target_pairs={{0,2},{1,3},{4,0},{5,1},{8,4},{9,5},{12,8},{13,9},{14,12},{15,13},... | collective-permute-start | bytes 798728 | tf_op jit(solution)/shard_map/ppermute | solution.py:367
  16.3 2.0 %collective-permute-start.11 = (s16[1040,128]{1,0:T(8,128)(2,1)S(1)}, s16[1040,128]{1,0:T(8,128)(2,1)S(1)}, u32[]{:S(2)}, u32[]{:S(2)}) collective-permute-start(s16[1040,128]{1,0:T(8,128)(2,1)S(1)} %sum_hop.14.before_ref), channel_id=1, source_target_pairs={{0,2},{1,3},{4,0},{5,1},{8,4},{9,5},{12,8},{13,9},{14,12},{15,13},... | collective-permute-start | bytes 798728 | tf_op jit(solution)/shard_map/ppermute | solution.py:367
  19.0 3.4 %collective-permute-done.9.got_ref = s16[1040,128]{1,0:T(8,128)(2,1)S(1)} collective-permute-done((s16[1040,128]{1,0:T(8,128)(2,1)S(1)}, s16[1040,128]{1,0:T(8,128)(2,1)S(1)}, u32[]{:S(2)}, u32[]{:S(2)}) %collective-permute-start.9) | collective-permute-done | bytes 266272 | tf_op jit(solution)/shard_map/ppermute | solution.py:367
  22.9 2.1 %collective-permute-start.14 = (s16[1040,128]{1,0:T(8,128)(2,1)S(1)}, s16[1040,128]{1,0:T(8,128)(2,1)S(1)}, u32[]{:S(2)}, u32[]{:S(2)}) collective-permute-start(s16[1040,128]{1,0:T(8,128)(2,1)S(1)} %sum_hop.16.before_ref), channel_id=1, source_target_pairs={{0,2},{1,3},{4,0},{5,1},{8,4},{9,5},{12,8},{13,9},{14,12},{15,13},... | collective-permute-start | bytes 798728 | tf_op jit(solution)/shard_map/ppermute | solution.py:367
  25.6 2.4 %collective-permute-done.11.got_ref = s16[1040,128]{1,0:T(8,128)(2,1)S(1)} collective-permute-done((s16[1040,128]{1,0:T(8,128)(2,1)S(1)}, s16[1040,128]{1,0:T(8,128)(2,1)S(1)}, u32[]{:S(2)}, u32[]{:S(2)}) %collective-permute-start.11) | collective-permute-done | bytes 266272 | tf_op jit(solution)/shard_map/ppermute | solution.py:367
  28.6 2.1 %collective-permute-start.16 = (s16[1040,128]{1,0:T(8,128)(2,1)S(1)}, s16[1040,128]{1,0:T(8,128)(2,1)S(1)}, u32[]{:S(2)}, u32[]{:S(2)}) collective-permute-start(s16[1040,128]{1,0:T(8,128)(2,1)S(1)} %sum_hop.18.before_ref), channel_id=1, source_target_pairs={{0,2},{1,3},{4,0},{5,1},{8,4},{9,5},{12,8},{13,9},{14,12},{15,13},... | collective-permute-start | bytes 798728 | tf_op jit(solution)/shard_map/ppermute | solution.py:367
  31.3 2.4 %collective-permute-done.14.got_ref = s16[1040,128]{1,0:T(8,128)(2,1)S(1)} collective-permute-done((s16[1040,128]{1,0:T(8,128)(2,1)S(1)}, s16[1040,128]{1,0:T(8,128)(2,1)S(1)}, u32[]{:S(2)}, u32[]{:S(2)}) %collective-permute-start.14) | collective-permute-done | bytes 266272 | tf_op jit(solution)/shard_map/ppermute | solution.py:367
  34.3 2.1 %collective-permute-start.19 = (s16[1040,128]{1,0:T(8,128)(2,1)S(1)}, s16[1040,128]{1,0:T(8,128)(2,1)S(1)}, u32[]{:S(2)}, u32[]{:S(2)}) collective-permute-start(s16[1040,128]{1,0:T(8,128)(2,1)S(1)} %sum_hop.20.before_ref), channel_id=1, source_target_pairs={{0,2},{1,3},{4,0},{5,1},{8,4},{9,5},{12,8},{13,9},{14,12},{15,13},... | collective-permute-start | bytes 798728 | tf_op jit(solution)/shard_map/ppermute | solution.py:367
  37.0 2.4 %collective-permute-done.16.got_ref = s16[1040,128]{1,0:T(8,128)(2,1)S(1)} collective-permute-done((s16[1040,128]{1,0:T(8,128)(2,1)S(1)}, s16[1040,128]{1,0:T(8,128)(2,1)S(1)}, u32[]{:S(2)}, u32[]{:S(2)}) %collective-permute-start.16) | collective-permute-done | bytes 266272 | tf_op jit(solution)/shard_map/ppermute | solution.py:367
  40.0 2.1 %collective-permute-start.21 = (s16[1040,128]{1,0:T(8,128)(2,1)S(1)}, s16[1040,128]{1,0:T(8,128)(2,1)S(1)}, u32[]{:S(2)}, u32[]{:S(2)}) collective-permute-start(s16[1040,128]{1,0:T(8,128)(2,1)S(1)} %sum_hop.22.before_ref), channel_id=1, source_target_pairs={{0,2},{1,3},{4,0},{5,1},{8,4},{9,5},{12,8},{13,9},{14,12},{15,13},... | collective-permute-start | bytes 798728 | tf_op jit(solution)/shard_map/ppermute | solution.py:367
  43.5 3.9 %collective-permute-done.18.refs_1_ = s16[1040,128]{1,0:T(8,128)(2,1)S(1)} collective-permute-done((s16[1040,128]{1,0:T(8,128)(2,1)S(1)}, s16[1040,128]{1,0:T(8,128)(2,1)S(1)}, u32[]{:S(2)}, u32[]{:S(2)}) %collective-permute-start.18) | collective-permute-done | bytes 266272 | tf_op jit(solution)/shard_map/ppermute | solution.py:367
  47.8 1.6 %collective-permute-start.22 = (bf16[512,256]{1,0:T(8,128)(2,1)S(1)}, bf16[512,256]{1,0:T(8,128)(2,1)S(1)}, u32[]{:S(2)}, u32[]{:S(2)}) collective-permute-start(bf16[512,256]{1,0:T(8,128)(2,1)S(1)} %effect.2.before_ref.refs_0_), channel_id=1, source_target_pairs={{0,2},{1,3},{4,0},{5,1},{8,4},{9,5},{12,8},{13,9},{14,12},{15,13},... | collective-permute-start | bytes 786440 | tf_op jit(solution)/shard_map/ppermute | solution.py:461
  49.9 3.2 %collective-permute-done.20.refs_1_ = s16[1040,128]{1,0:T(8,128)(2,1)S(1)} collective-permute-done((s16[1040,128]{1,0:T(8,128)(2,1)S(1)}, s16[1040,128]{1,0:T(8,128)(2,1)S(1)}, u32[]{:S(2)}, u32[]{:S(2)}) %collective-permute-start.20) | collective-permute-done | bytes 266272 | tf_op jit(solution)/shard_map/ppermute | solution.py:367
  53.5 1.6 %collective-permute-start.24 = (bf16[512,256]{1,0:T(8,128)(2,1)S(1)}, bf16[512,256]{1,0:T(8,128)(2,1)S(1)}, u32[]{:S(2)}, u32[]{:S(2)}) collective-permute-start(bf16[512,256]{1,0:T(8,128)(2,1)S(1)} %effect.3.before_ref.refs_3_), channel_id=1, source_target_pairs={{0,2},{1,3},{4,0},{5,1},{8,4},{9,5},{12,8},{13,9},{14,12},{15,13},... | collective-permute-start | bytes 786440 | tf_op jit(solution)/shard_map/ppermute | solution.py:461
  57.1 1.6 %collective-permute-start.26 = (bf16[512,256]{1,0:T(8,128)(2,1)S(1)}, bf16[512,256]{1,0:T(8,128)(2,1)S(1)}, u32[]{:S(2)}, u32[]{:S(2)}) collective-permute-start(bf16[512,256]{1,0:T(8,128)(2,1)S(1)} %collective-permute-done.22.refs_0_), channel_id=1, source_target_pairs={{0,2},{1,3},{4,0},{5,1},{8,4},{9,5},{12,8},{13,9},{14,12},{15,13},... | collective-permute-start | bytes 786440 | tf_op jit(solution)/shard_map/ppermute | solution.py:461
  60.0 2.8 %collective-permute-done.24.refs_0_ = bf16[512,256]{1,0:T(8,128)(2,1)S(1)} collective-permute-done((bf16[512,256]{1,0:T(8,128)(2,1)S(1)}, bf16[512,256]{1,0:T(8,128)(2,1)S(1)}, u32[]{:S(2)}, u32[]{:S(2)}) %collective-permute-start.24) | collective-permute-done | bytes 262176 | tf_op jit(solution)/shard_map/ppermute | solution.py:461
  62.7 1.6 %collective-permute-start.28 = (bf16[512,256]{1,0:T(8,128)(2,1)S(1)}, bf16[512,256]{1,0:T(8,128)(2,1)S(1)}, u32[]{:S(2)}, u32[]{:S(2)}) collective-permute-start(bf16[512,256]{1,0:T(8,128)(2,1)S(1)} %collective-permute-done.24.refs_0_), channel_id=1, source_target_pairs={{0,2},{1,3},{4,0},{5,1},{8,4},{9,5},{12,8},{13,9},{14,12},{15,13},... | collective-permute-start | bytes 786440 | tf_op jit(solution)/shard_map/ppermute | solution.py:461
  65.6 1.3 %update.2 = (f32[1024,256]{1,0:T(8,128)}, f32[1024,256]{1,0:T(8,128)}, f32[8,128]{1,0:T(8,128)S(1)}) custom-call(f32[384,256]{1,0:T(8,128)S(1)} %get-tuple-element.85.before_ref.refs_3_, f32[256,1024]{1,0:T(8,128)S(1)} %sum_local.5.before_ref.refs_0_, s16[1040,128]{1,0:T(8,128)(2,1)S(1)} %collective-permute-done.18.refs_1_, ...), custom_call_target="tpu_custom_call" | custom-call | flops 1 | bytes 1 | tf_op jit(solution)/shard_map/update/pallas_call | solution.py:398
  66.9 1.4 %collective-permute-done.26.refs_0_ = bf16[512,256]{1,0:T(8,128)(2,1)S(1)} collective-permute-done((bf16[512,256]{1,0:T(8,128)(2,1)S(1)}, bf16[512,256]{1,0:T(8,128)(2,1)S(1)}, u32[]{:S(2)}, u32[]{:S(2)}) %collective-permute-start.26) | collective-permute-done | bytes 262176 | tf_op jit(solution)/shard_map/ppermute | solution.py:461
  68.3 1.6 %collective-permute-start.30 = (bf16[512,256]{1,0:T(8,128)(2,1)S(1)}, bf16[512,256]{1,0:T(8,128)(2,1)S(1)}, u32[]{:S(2)}, u32[]{:S(2)}) collective-permute-start(bf16[512,256]{1,0:T(8,128)(2,1)S(1)} %collective-permute-done.26.refs_0_), channel_id=1, source_target_pairs={{0,2},{1,3},{4,0},{5,1},{8,4},{9,5},{12,8},{13,9},{14,12},{15,13},... | collective-permute-start | bytes 786440 | tf_op jit(solution)/shard_map/ppermute | solution.py:461
  71.2 2.8 %collective-permute-done.28.refs_0_ = bf16[512,256]{1,0:T(8,128)(2,1)S(1)} collective-permute-done((bf16[512,256]{1,0:T(8,128)(2,1)S(1)}, bf16[512,256]{1,0:T(8,128)(2,1)S(1)}, u32[]{:S(2)}, u32[]{:S(2)}) %collective-permute-start.28) | collective-permute-done | bytes 262176 | tf_op jit(solution)/shard_map/ppermute | solution.py:461
  74.0 1.6 %collective-permute-start.32 = (bf16[256,256]{1,0:T(8,128)(2,1)S(1)}, bf16[256,256]{1,0:T(8,128)(2,1)S(1)}, u32[]{:S(2)}, u32[]{:S(2)}) collective-permute-start(bf16[256,256]{1,0:T(8,128)(2,1)S(1)} %slice.24), channel_id=1, source_target_pairs={{0,2},{1,3},{4,0},{5,1},{8,4},{9,5},{12,8},{13,9},{14,12},{15,13},... | collective-permute-start | bytes 393224 | tf_op jit(solution)/shard_map/ppermute | solution.py:455
  76.9 1.4 %collective-permute-start.35 = (bf16[256,256]{1,0:T(8,128)(2,1)S(1)}, bf16[256,256]{1,0:T(8,128)(2,1)S(1)}, u32[]{:S(2)}, u32[]{:S(2)}) collective-permute-start(bf16[256,256]{1,0:T(8,128)(2,1)S(1)} %slice.27), channel_id=1, source_target_pairs={{0,4},{1,5},{4,8},{5,9},{8,12},{9,13},{12,14},{13,15},{14,10},{15,... | collective-permute-start | bytes 393224 | tf_op jit(solution)/shard_map/ppermute | solution.py:458
  78.3 1.3 %update.3 = (f32[1024,256]{1,0:T(8,128)}, f32[1024,256]{1,0:T(8,128)}, f32[8,128]{1,0:T(8,128)S(1)}) custom-call(f32[384,256]{1,0:T(8,128)S(1)} %get-tuple-element.98.before_ref.refs_3_, f32[256,1024]{1,0:T(8,128)S(1)} %sum_local.5.before_ref.refs_0_, ...), custom_call_target="tpu_custom_call", output_to_operand_aliasing={{0}: (8, {}), {1}: (9, {})} | custom-call | flops 1 | bytes 1 | tf_op jit(solution)/shard_map/update/pallas_call | solution.py:398
  79.7 1.5 %collective-permute-start.33 = (bf16[256,256]{1,0:T(8,128)(2,1)S(1)}, bf16[256,256]{1,0:T(8,128)(2,1)S(1)}, u32[]{:S(2)}, u32[]{:S(2)}) collective-permute-start(bf16[256,256]{1,0:T(8,128)(2,1)S(1)} %slice.25), channel_id=1, source_target_pairs={{0,2},{1,3},{4,0},{5,1},{8,4},{9,5},{12,8},{13,9},{14,12},{15,13},... | collective-permute-start | bytes 393224 | tf_op jit(solution)/shard_map/ppermute | solution.py:458
  81.6 1.6 %collective-permute-start.36 = (bf16[256,256]{1,0:T(8,128)(2,1)S(1)}, bf16[256,256]{1,0:T(8,128)(2,1)S(1)}, u32[]{:S(2)}, u32[]{:S(2)}) collective-permute-start(bf16[256,256]{1,0:T(8,128)(2,1)S(1)} %slice.28), channel_id=1, source_target_pairs={{0,2},{1,3},{4,0},{5,1},{8,4},{9,5},{12,8},{13,9},{14,12},{15,13},... | collective-permute-start | bytes 393224 | tf_op jit(solution)/shard_map/ppermute | solution.py:450
  84.8 1.7 %collective-permute-start.38 = (bf16[256,256]{1,0:T(8,128)(2,1)S(1)}, bf16[256,256]{1,0:T(8,128)(2,1)S(1)}, u32[]{:S(2)}, u32[]{:S(2)}) collective-permute-start(bf16[256,256]{1,0:T(8,128)(2,1)S(1)} %collective-permute-done.32.refs_0_), channel_id=1, source_target_pairs={{0,2},{1,3},{4,0},{5,1},{8,4},{9,5},{12,8},{13,9},{14,12},{15,13},... | collective-permute-start | bytes 393224 | tf_op jit(solution)/shard_map/ppermute | solution.py:450
  86.5 1.2 %collective-permute-start.39 = (bf16[256,256]{1,0:T(8,128)(2,1)S(1)}, bf16[256,256]{1,0:T(8,128)(2,1)S(1)}, u32[]{:S(2)}, u32[]{:S(2)}) collective-permute-start(bf16[256,256]{1,0:T(8,128)(2,1)S(1)} %collective-permute-done.34.refs_0_), channel_id=1, source_target_pairs={{0,4},{1,5},{4,8},{5,9},{8,12},{9,13},{12,14},{13,15},{14,10},{15,... | collective-permute-start | bytes 393224 | tf_op jit(solution)/shard_map/ppermute | solution.py:450
  (128 shorter events, 28.1 us)
Async XLA Ops:
  5.4 7.4 %collective-permute-start.4 = (s16[528,128]{1,0:T(8,128)(2,1)S(1)}, s16[528,128]{1,0:T(8,128)(2,1)S(1)}, u32[]{:S(2)}, u32[]{:S(2)}) collective-permute-start(s16[528,128]{1,0:T(8,128)(2,1)S(1)} %get-tuple-element.74), channel_id=1, source_target_pairs={{0,2},{1,3},{4,0},{5,1},{8,4},{9,5},{12,8},{13,9},{14,12},{15,13},... | collective-permute-start | bytes 405512 | tf_op jit(solution)/shard_map/ppermute | solution.py:340
  8.4 6.6 %collective-permute-start.5 = (s16[528,128]{1,0:T(8,128)(2,1)S(1)}, s16[528,128]{1,0:T(8,128)(2,1)S(1)}, u32[]{:S(2)}, u32[]{:S(2)}) collective-permute-start(s16[528,128]{1,0:T(8,128)(2,1)S(1)} %get-tuple-element.69.before_ref), channel_id=1, source_target_pairs={{0,4},{1,5},{4,8},{5,9},{8,12},{9,13},{12,14},{13,15},{14,10},{15,... | collective-permute-start | bytes 405512 | tf_op jit(solution)/shard_map/ppermute | solution.py:339
  9.1 6.6 %collective-permute-start.7 = (s16[528,128]{1,0:T(8,128)(2,1)S(1)}, s16[528,128]{1,0:T(8,128)(2,1)S(1)}, u32[]{:S(2)}, u32[]{:S(2)}) collective-permute-start(s16[528,128]{1,0:T(8,128)(2,1)S(1)} %get-tuple-element.76), channel_id=1, source_target_pairs={{0,2},{1,3},{4,0},{5,1},{8,4},{9,5},{12,8},{13,9},{14,12},{15,13},... | collective-permute-start | bytes 405512 | tf_op jit(solution)/shard_map/ppermute | solution.py:340
  11.0 7.2 %collective-permute-start.8 = (s16[528,128]{1,0:T(8,128)(2,1)S(1)}, s16[528,128]{1,0:T(8,128)(2,1)S(1)}, u32[]{:S(2)}, u32[]{:S(2)}) collective-permute-start(s16[528,128]{1,0:T(8,128)(2,1)S(1)} %get-tuple-element.73.refs_0_), channel_id=1, source_target_pairs={{0,4},{1,5},{4,8},{5,9},{8,12},{9,13},{12,14},{13,15},{14,10},{15,... | collective-permute-start | bytes 405512 | tf_op jit(solution)/shard_map/ppermute | solution.py:339
  13.0 9.3 %collective-permute-start.9 = (s16[1040,128]{1,0:T(8,128)(2,1)S(1)}, s16[1040,128]{1,0:T(8,128)(2,1)S(1)}, u32[]{:S(2)}, u32[]{:S(2)}) collective-permute-start(s16[1040,128]{1,0:T(8,128)(2,1)S(1)} %sum_hop.12.before_ref), channel_id=1, source_target_pairs={{0,2},{1,3},{4,0},{5,1},{8,4},{9,5},{12,8},{13,9},{14,12},{15,13},... | collective-permute-start | bytes 798728 | tf_op jit(solution)/shard_map/ppermute | solution.py:367
  15.2 9.7 %collective-permute-start.10 = (s16[1040,128]{1,0:T(8,128)(2,1)S(1)}, s16[1040,128]{1,0:T(8,128)(2,1)S(1)}, u32[]{:S(2)}, u32[]{:S(2)}) collective-permute-start(s16[1040,128]{1,0:T(8,128)(2,1)S(1)} %sum_hop.13.refs_0_), channel_id=1, source_target_pairs={{0,4},{1,5},{4,8},{5,9},{8,12},{9,13},{12,14},{13,15},{14,10},{15,... | collective-permute-start | bytes 798728 | tf_op jit(solution)/shard_map/ppermute | solution.py:367
  15.6 18.1 %collective-permute-start.13 = (bf16[3,384,1024]{2,1,0:T(8,128)(2,1)S(1)}, bf16[3,384,1024]{2,1,0:T(8,128)(2,1)S(1)}, u32[]{:S(2)}, u32[]{:S(2)}) collective-permute-start(bf16[3,384,1024]{2,1,0:T(8,128)(2,1)S(1)} %pick_blocks.7.before_ref), channel_id=1, source_target_pairs={{0,1},{1,0},{2,3},{3,2},{4,5},{5,4},{6,7},{7,6},{8,9},{9,8},{10,11... | collective-permute-start | bytes 7077896 | tf_op jit(solution)/shard_map/ppermute | solution.py:279
  16.3 11.8 %collective-permute-start.11 = (s16[1040,128]{1,0:T(8,128)(2,1)S(1)}, s16[1040,128]{1,0:T(8,128)(2,1)S(1)}, u32[]{:S(2)}, u32[]{:S(2)}) collective-permute-start(s16[1040,128]{1,0:T(8,128)(2,1)S(1)} %sum_hop.14.before_ref), channel_id=1, source_target_pairs={{0,2},{1,3},{4,0},{5,1},{8,4},{9,5},{12,8},{13,9},{14,12},{15,13},... | collective-permute-start | bytes 798728 | tf_op jit(solution)/shard_map/ppermute | solution.py:367
  18.8 11.8 %collective-permute-start.12 = (s16[1040,128]{1,0:T(8,128)(2,1)S(1)}, s16[1040,128]{1,0:T(8,128)(2,1)S(1)}, u32[]{:S(2)}, u32[]{:S(2)}) collective-permute-start(s16[1040,128]{1,0:T(8,128)(2,1)S(1)} %sum_hop.15.before_ref), channel_id=1, source_target_pairs={{0,4},{1,5},{4,8},{5,9},{8,12},{9,13},{12,14},{13,15},{14,10},{15,... | collective-permute-start | bytes 798728 | tf_op jit(solution)/shard_map/ppermute | solution.py:367
  22.9 10.8 %collective-permute-start.14 = (s16[1040,128]{1,0:T(8,128)(2,1)S(1)}, s16[1040,128]{1,0:T(8,128)(2,1)S(1)}, u32[]{:S(2)}, u32[]{:S(2)}) collective-permute-start(s16[1040,128]{1,0:T(8,128)(2,1)S(1)} %sum_hop.16.before_ref), channel_id=1, source_target_pairs={{0,2},{1,3},{4,0},{5,1},{8,4},{9,5},{12,8},{13,9},{14,12},{15,13},... | collective-permute-start | bytes 798728 | tf_op jit(solution)/shard_map/ppermute | solution.py:367
  25.5 10.9 %collective-permute-start.15 = (s16[1040,128]{1,0:T(8,128)(2,1)S(1)}, s16[1040,128]{1,0:T(8,128)(2,1)S(1)}, u32[]{:S(2)}, u32[]{:S(2)}) collective-permute-start(s16[1040,128]{1,0:T(8,128)(2,1)S(1)} %sum_hop.17.before_ref), channel_id=1, source_target_pairs={{0,4},{1,5},{4,8},{5,9},{8,12},{9,13},{12,14},{13,15},{14,10},{15,... | collective-permute-start | bytes 798728 | tf_op jit(solution)/shard_map/ppermute | solution.py:367
  28.6 10.9 %collective-permute-start.16 = (s16[1040,128]{1,0:T(8,128)(2,1)S(1)}, s16[1040,128]{1,0:T(8,128)(2,1)S(1)}, u32[]{:S(2)}, u32[]{:S(2)}) collective-permute-start(s16[1040,128]{1,0:T(8,128)(2,1)S(1)} %sum_hop.18.before_ref), channel_id=1, source_target_pairs={{0,2},{1,3},{4,0},{5,1},{8,4},{9,5},{12,8},{13,9},{14,12},{15,13},... | collective-permute-start | bytes 798728 | tf_op jit(solution)/shard_map/ppermute | solution.py:367
  31.2 10.9 %collective-permute-start.17 = (s16[1040,128]{1,0:T(8,128)(2,1)S(1)}, s16[1040,128]{1,0:T(8,128)(2,1)S(1)}, u32[]{:S(2)}, u32[]{:S(2)}) collective-permute-start(s16[1040,128]{1,0:T(8,128)(2,1)S(1)} %sum_hop.19.before_ref), channel_id=1, source_target_pairs={{0,4},{1,5},{4,8},{5,9},{8,12},{9,13},{12,14},{13,15},{14,10},{15,... | collective-permute-start | bytes 798728 | tf_op jit(solution)/shard_map/ppermute | solution.py:367
  34.3 13.1 %collective-permute-start.19 = (s16[1040,128]{1,0:T(8,128)(2,1)S(1)}, s16[1040,128]{1,0:T(8,128)(2,1)S(1)}, u32[]{:S(2)}, u32[]{:S(2)}) collective-permute-start(s16[1040,128]{1,0:T(8,128)(2,1)S(1)} %sum_hop.20.before_ref), channel_id=1, source_target_pairs={{0,2},{1,3},{4,0},{5,1},{8,4},{9,5},{12,8},{13,9},{14,12},{15,13},... | collective-permute-start | bytes 798728 | tf_op jit(solution)/shard_map/ppermute | solution.py:367
  36.9 10.5 %collective-permute-start.18 = (s16[1040,128]{1,0:T(8,128)(2,1)S(1)}, s16[1040,128]{1,0:T(8,128)(2,1)S(1)}, u32[]{:S(2)}, u32[]{:S(2)}) collective-permute-start(s16[1040,128]{1,0:T(8,128)(2,1)S(1)} %sum_hop.21.before_ref), channel_id=1, source_target_pairs={{0,4},{1,5},{4,8},{5,9},{8,12},{9,13},{12,14},{13,15},{14,10},{15,... | collective-permute-start | bytes 798728 | tf_op jit(solution)/shard_map/ppermute | solution.py:367
  40.0 13.1 %collective-permute-start.21 = (s16[1040,128]{1,0:T(8,128)(2,1)S(1)}, s16[1040,128]{1,0:T(8,128)(2,1)S(1)}, u32[]{:S(2)}, u32[]{:S(2)}) collective-permute-start(s16[1040,128]{1,0:T(8,128)(2,1)S(1)} %sum_hop.22.before_ref), channel_id=1, source_target_pairs={{0,2},{1,3},{4,0},{5,1},{8,4},{9,5},{12,8},{13,9},{14,12},{15,13},... | collective-permute-start | bytes 798728 | tf_op jit(solution)/shard_map/ppermute | solution.py:367
  42.7 10.4 %collective-permute-start.20 = (s16[1040,128]{1,0:T(8,128)(2,1)S(1)}, s16[1040,128]{1,0:T(8,128)(2,1)S(1)}, u32[]{:S(2)}, u32[]{:S(2)}) collective-permute-start(s16[1040,128]{1,0:T(8,128)(2,1)S(1)} %sum_hop.23.before_ref), channel_id=1, source_target_pairs={{0,4},{1,5},{4,8},{5,9},{8,12},{9,13},{12,14},{13,15},{14,10},{15,... | collective-permute-start | bytes 798728 | tf_op jit(solution)/shard_map/ppermute | solution.py:367
  47.8 9.3 %collective-permute-start.22 = (bf16[512,256]{1,0:T(8,128)(2,1)S(1)}, bf16[512,256]{1,0:T(8,128)(2,1)S(1)}, u32[]{:S(2)}, u32[]{:S(2)}) collective-permute-start(bf16[512,256]{1,0:T(8,128)(2,1)S(1)} %effect.2.before_ref.refs_0_), channel_id=1, source_target_pairs={{0,2},{1,3},{4,0},{5,1},{8,4},{9,5},{12,8},{13,9},{14,12},{15,13},... | collective-permute-start | bytes 786440 | tf_op jit(solution)/shard_map/ppermute | solution.py:461
  49.5 9.6 %collective-permute-start.23 = (bf16[512,256]{1,0:T(8,128)(2,1)S(1)}, bf16[512,256]{1,0:T(8,128)(2,1)S(1)}, u32[]{:S(2)}, u32[]{:S(2)}) collective-permute-start(bf16[512,256]{1,0:T(8,128)(2,1)S(1)} %effect.2.before_ref.refs_0_), channel_id=1, source_target_pairs={{0,4},{1,5},{4,8},{5,9},{8,12},{9,13},{12,14},{13,15},{14,10},{15,... | collective-permute-start | bytes 786440 | tf_op jit(solution)/shard_map/ppermute | solution.py:461
  53.5 9.2 %collective-permute-start.24 = (bf16[512,256]{1,0:T(8,128)(2,1)S(1)}, bf16[512,256]{1,0:T(8,128)(2,1)S(1)}, u32[]{:S(2)}, u32[]{:S(2)}) collective-permute-start(bf16[512,256]{1,0:T(8,128)(2,1)S(1)} %effect.3.before_ref.refs_3_), channel_id=1, source_target_pairs={{0,2},{1,3},{4,0},{5,1},{8,4},{9,5},{12,8},{13,9},{14,12},{15,13},... | collective-permute-start | bytes 786440 | tf_op jit(solution)/shard_map/ppermute | solution.py:461
  55.1 9.6 %collective-permute-start.25 = (bf16[512,256]{1,0:T(8,128)(2,1)S(1)}, bf16[512,256]{1,0:T(8,128)(2,1)S(1)}, u32[]{:S(2)}, u32[]{:S(2)}) collective-permute-start(bf16[512,256]{1,0:T(8,128)(2,1)S(1)} %effect.3.before_ref.refs_3_), channel_id=1, source_target_pairs={{0,4},{1,5},{4,8},{5,9},{8,12},{9,13},{12,14},{13,15},{14,10},{15,... | collective-permute-start | bytes 786440 | tf_op jit(solution)/shard_map/ppermute | solution.py:461
  57.1 11.2 %collective-permute-start.26 = (bf16[512,256]{1,0:T(8,128)(2,1)S(1)}, bf16[512,256]{1,0:T(8,128)(2,1)S(1)}, u32[]{:S(2)}, u32[]{:S(2)}) collective-permute-start(bf16[512,256]{1,0:T(8,128)(2,1)S(1)} %collective-permute-done.22.refs_0_), channel_id=1, source_target_pairs={{0,2},{1,3},{4,0},{5,1},{8,4},{9,5},{12,8},{13,9},{14,12},{15,13},... | collective-permute-start | bytes 786440 | tf_op jit(solution)/shard_map/ppermute | solution.py:461
  59.1 11.2 %collective-permute-start.27 = (bf16[512,256]{1,0:T(8,128)(2,1)S(1)}, bf16[512,256]{1,0:T(8,128)(2,1)S(1)}, u32[]{:S(2)}, u32[]{:S(2)}) collective-permute-start(bf16[512,256]{1,0:T(8,128)(2,1)S(1)} %collective-permute-done.23.refs_0_), channel_id=1, source_target_pairs={{0,4},{1,5},{4,8},{5,9},{8,12},{9,13},{12,14},{13,15},{14,10},{15,... | collective-permute-start | bytes 786440 | tf_op jit(solution)/shard_map/ppermute | solution.py:461
  62.7 11.2 %collective-permute-start.28 = (bf16[512,256]{1,0:T(8,128)(2,1)S(1)}, bf16[512,256]{1,0:T(8,128)(2,1)S(1)}, u32[]{:S(2)}, u32[]{:S(2)}) collective-permute-start(bf16[512,256]{1,0:T(8,128)(2,1)S(1)} %collective-permute-done.24.refs_0_), channel_id=1, source_target_pairs={{0,2},{1,3},{4,0},{5,1},{8,4},{9,5},{12,8},{13,9},{14,12},{15,13},... | collective-permute-start | bytes 786440 | tf_op jit(solution)/shard_map/ppermute | solution.py:461
  64.7 11.3 %collective-permute-start.29 = (bf16[512,256]{1,0:T(8,128)(2,1)S(1)}, bf16[512,256]{1,0:T(8,128)(2,1)S(1)}, u32[]{:S(2)}, u32[]{:S(2)}) collective-permute-start(bf16[512,256]{1,0:T(8,128)(2,1)S(1)} %collective-permute-done.25.refs_0_), channel_id=1, source_target_pairs={{0,4},{1,5},{4,8},{5,9},{8,12},{9,13},{12,14},{13,15},{14,10},{15,... | collective-permute-start | bytes 786440 | tf_op jit(solution)/shard_map/ppermute | solution.py:461
  68.3 11.3 %collective-permute-start.30 = (bf16[512,256]{1,0:T(8,128)(2,1)S(1)}, bf16[512,256]{1,0:T(8,128)(2,1)S(1)}, u32[]{:S(2)}, u32[]{:S(2)}) collective-permute-start(bf16[512,256]{1,0:T(8,128)(2,1)S(1)} %collective-permute-done.26.refs_0_), channel_id=1, source_target_pairs={{0,2},{1,3},{4,0},{5,1},{8,4},{9,5},{12,8},{13,9},{14,12},{15,13},... | collective-permute-start | bytes 786440 | tf_op jit(solution)/shard_map/ppermute | solution.py:461
  70.3 11.2 %collective-permute-start.31 = (bf16[512,256]{1,0:T(8,128)(2,1)S(1)}, bf16[512,256]{1,0:T(8,128)(2,1)S(1)}, u32[]{:S(2)}, u32[]{:S(2)}) collective-permute-start(bf16[512,256]{1,0:T(8,128)(2,1)S(1)} %collective-permute-done.27.refs_0_), channel_id=1, source_target_pairs={{0,4},{1,5},{4,8},{5,9},{8,12},{9,13},{12,14},{13,15},{14,10},{15,... | collective-permute-start | bytes 786440 | tf_op jit(solution)/shard_map/ppermute | solution.py:461
  74.0 10.8 %collective-permute-start.32 = (bf16[256,256]{1,0:T(8,128)(2,1)S(1)}, bf16[256,256]{1,0:T(8,128)(2,1)S(1)}, u32[]{:S(2)}, u32[]{:S(2)}) collective-permute-start(bf16[256,256]{1,0:T(8,128)(2,1)S(1)} %slice.24), channel_id=1, source_target_pairs={{0,2},{1,3},{4,0},{5,1},{8,4},{9,5},{12,8},{13,9},{14,12},{15,13},... | collective-permute-start | bytes 393224 | tf_op jit(solution)/shard_map/ppermute | solution.py:455
  76.4 7.6 %collective-permute-start.34 = (bf16[256,256]{1,0:T(8,128)(2,1)S(1)}, bf16[256,256]{1,0:T(8,128)(2,1)S(1)}, u32[]{:S(2)}, u32[]{:S(2)}) collective-permute-start(bf16[256,256]{1,0:T(8,128)(2,1)S(1)} %slice.26), channel_id=1, source_target_pairs={{0,4},{1,5},{4,8},{5,9},{8,12},{9,13},{12,14},{13,15},{14,10},{15,... | collective-permute-start | bytes 393224 | tf_op jit(solution)/shard_map/ppermute | solution.py:455
  76.9 11.1 %collective-permute-start.35 = (bf16[256,256]{1,0:T(8,128)(2,1)S(1)}, bf16[256,256]{1,0:T(8,128)(2,1)S(1)}, u32[]{:S(2)}, u32[]{:S(2)}) collective-permute-start(bf16[256,256]{1,0:T(8,128)(2,1)S(1)} %slice.27), channel_id=1, source_target_pairs={{0,4},{1,5},{4,8},{5,9},{8,12},{9,13},{12,14},{13,15},{14,10},{15,... | collective-permute-start | bytes 393224 | tf_op jit(solution)/shard_map/ppermute | solution.py:458
  79.7 6.8 %collective-permute-start.33 = (bf16[256,256]{1,0:T(8,128)(2,1)S(1)}, bf16[256,256]{1,0:T(8,128)(2,1)S(1)}, u32[]{:S(2)}, u32[]{:S(2)}) collective-permute-start(bf16[256,256]{1,0:T(8,128)(2,1)S(1)} %slice.25), channel_id=1, source_target_pairs={{0,2},{1,3},{4,0},{5,1},{8,4},{9,5},{12,8},{13,9},{14,12},{15,13},... | collective-permute-start | bytes 393224 | tf_op jit(solution)/shard_map/ppermute | solution.py:458
  81.6 6.9 %collective-permute-start.36 = (bf16[256,256]{1,0:T(8,128)(2,1)S(1)}, bf16[256,256]{1,0:T(8,128)(2,1)S(1)}, u32[]{:S(2)}, u32[]{:S(2)}) collective-permute-start(bf16[256,256]{1,0:T(8,128)(2,1)S(1)} %slice.28), channel_id=1, source_target_pairs={{0,2},{1,3},{4,0},{5,1},{8,4},{9,5},{12,8},{13,9},{14,12},{15,13},... | collective-permute-start | bytes 393224 | tf_op jit(solution)/shard_map/ppermute | solution.py:450
  (22 other events, 86.0 us)

commit v14 on v12

--- a/solution.py
+++ b/solution.py
@@ -209,9 +209,13 @@
     refs[-1][...] = columns_product(ring, places, genotype_ref, refs, eta)
 
 
-def end_kernel(ring, places, genotype_ref, eta_ref, upper_ref, lower_ref, labels_ref, *refs):
+def other_kernel(ring, places, genotype_ref, eta_ref, upper_ref, lower_ref, *refs):
     got = jnp.concatenate([upper_ref[...], lower_ref[...]], axis=0)
-    eta = columns_product(ring, places, genotype_ref, refs, eta_ref[...] + got)
+    refs[-1][...] = columns_product(ring, places, genotype_ref, refs, eta_ref[...] + got)
+
+
+def end_kernel(ring, places, genotype_ref, eta_ref, labels_ref, *refs):
+    eta = columns_product(ring, places, genotype_ref, refs, eta_ref[...])
     refs[-1][...] = 4.0 * (labels_ref[...].astype(jnp.float32) - jax.nn.sigmoid(eta))
 
 
@@ -276,18 +280,17 @@
         return [(distances, True, 0, block)] if distances else []
 
     later = [b for b in (order[3:5], order[5:]) if b]
-    last, own_far[0] = pick(far(0), pltpu.HBM, small)
-    peer_far[0] = lax.ppermute(last, "ind", swap)
-    mine, _ = lax.optimization_barrier((residual, last))
-    residual_other = lax.ppermute(mine, "ind", swap)
-    wanted = (far(1) if pieces > 1 else []) + whole(order[1:3])
-    if wanted:
-        found = pick(wanted, pltpu.HBM, heavy, last)
-        last = found[0]
-        if pieces > 1:
-            peer_far[1], own_far[1] = lax.ppermute(found[0], "ind", swap), found[1]
-        if order[1:3]:
-            swapped(order[1:3], found[-1])
+    wanted = [w for piece in range(pieces) for w in far(piece)] + whole(order[1:3])
+    found = pick(wanted, pltpu.HBM, small)
+    last = found[0]
+    for piece in range(pieces):
+        peer_far[piece] = lax.ppermute(found[2 * piece], "ind", swap)
+        own_far[piece] = found[2 * piece + 1]
+        if piece == 0:
+            mine, _ = lax.optimization_barrier((residual, last))
+            residual_other = lax.ppermute(mine, "ind", swap)
+    if order[1:3]:
+        swapped(order[1:3], found[-1])
     res = last = pl.pallas_call(
         flip_kernel,
         in_specs=after(last, (residual, residual_other)),
@@ -338,7 +341,7 @@
                 if d == reach > 1:
                     last, _ = lax.optimization_barrier((last, peer[d - 1][0]))
                 distances = later.pop(0)
-                (last,) = pick(whole(distances), pltpu.VMEM, light, last)
+                (last,) = pick(whole(distances), pltpu.VMEM, small, last)
                 swapped(distances, last)
 
     near = last = pl.pallas_call(
@@ -459,13 +462,21 @@
         cost_estimate=heavy,
         name="own_last",
     )(genotype, eta[0], offset.reshape(1, cols), *[effect for _, _, effect in final])
+    there = [(d, low, True) for d, low, _ in final]
+    mine = pl.pallas_call(
+        functools.partial(other_kernel, ring, there[:1]),
+        out_shape=eta_shape,
+        compiler_params=params,
+        cost_estimate=heavy,
+        name="other_last",
+    )(genotype, mine, *eta_got, others[0])
     resid_new = pl.pallas_call(
-        functools.partial(end_kernel, ring, [(d, low, True) for d, low, _ in final]),
+        functools.partial(end_kernel, ring, there[1:]),
         out_shape=eta_shape,
         compiler_params=params,
         cost_estimate=light,
         name="new_residual",
-    )(genotype, mine, *eta_got, labels, *others)
+    )(genotype, mine, labels, *others[1:])
     return (outs[0], outs[1], resid_new)
 
 

time: 93.5 us -> 93.4 us (level)
    ppermute x1, waiting for transfers between devices: 0.01 us -> 1.03 us  [on_device(): residual_other = lax.ppermute(mine, 'ind', swap)]
    pallas_call x4 -> x3, Pallas kernels: 3.21 us -> 2.34 us  [pick(): pl.pallas_call(functools.partial(pick_kernel, ring, wanted, block), in_sp...]
  transfers between devices with their start and end apart: 44 -> 44, of which waited for: 16 -> 17; matrix products, arithmetic and copies ran while one was open for 0% -> 0% of each run, Pallas kernels for 21% -> 20%
where the time goes in v14:
time: 93.4 us; the launch traced here: 93.3 us
  starting transfers between devices  40.1 us (43%)
  waiting for transfers between devices  30.5 us (33%)
  Pallas kernels  21.3 us (23%)
  between operations  1.22 us (1%)
    ppermute x12, waiting for transfers between devices, on_device(): got[way, piece] = lax.ppermute(last, 'ind', left if way else right)  16.2 us
    ppermute x14, starting transfers between devices, on_device(): held[way, piece] = lax.ppermute(message, 'ind', perm)  15.2 us
    ppermute x12, starting transfers between devices, on_device(): got[way, piece] = lax.ppermute(last, 'ind', left if way else right)  12.8 us
    ppermute x14, waiting for transfers between devices, on_device(): held[way, piece] = lax.ppermute(message, 'ind', perm)  10.2 us
    pallas_call x12, Pallas kernels, on_device(): pl.pallas_call(functools.partial(hop_kernel, ring, (w, peer[w][1]), low,...  6.63 us
    pallas_call x15, Pallas kernels, product(): pl.pallas_call(functools.partial(eta_kernel, ring, places, not eta), in_s...  5.64 us
    ppermute x2, starting transfers between devices, on_device(): got[1, piece] = lax.ppermute(sent[1], 'ind', left)  4.9 us
    ppermute x2, starting transfers between devices, on_device(): second = lax.ppermute(second, 'ind', perm)  2.88 us
  transfers between devices with their start and end apart: 44, of which 17 were waited for; matrix products, arithmetic and copies ran while one was open for 0% of the time, Pallas kernels for 20%

profile of v14, /device:TPU:0, one launch (start us, length us, event | category | flops | bytes accessed | tf_op | source)
XLA Modules:
  0.0 93.3 jit_solution(14318632384601196309)
XLA Ops:
  0.6 2.0 %pick_blocks.3 = (bf16[1,384,512]{2,1,0:T(8,128)(2,1)S(1)}, bf16[1,384,512]{2,1,0:T(8,128)(2,1)S(1)}, bf16[1,384,512]{2,1,0:T(8,128)(2,1)S(1)}, bf16[1,384,512]{...) custom-call(bf16[384,16384]{1,0:T(8,128)(2,1)} %genotype_ref.11), custom_call_target="tpu_custom_call" | custom-call | flops 1 | bytes 1 | tf_op jit(solution)/shard_map/pick_blocks/pallas_call | solution.py:252
  5.5 2.9 %collective-permute-start.4 = (s16[528,128]{1,0:T(8,128)(2,1)S(1)}, s16[528,128]{1,0:T(8,128)(2,1)S(1)}, u32[]{:S(2)}, u32[]{:S(2)}) collective-permute-start(s16[528,128]{1,0:T(8,128)(2,1)S(1)} %get-tuple-element.74), channel_id=1, source_target_pairs={{0,2},{1,3},{4,0},{5,1},{8,4},{9,5},{12,8},{13,9},{14,12},{15,13},... | collective-permute-start | bytes 405512 | tf_op jit(solution)/shard_map/ppermute | solution.py:322
  9.1 2.0 %collective-permute-start.7 = (s16[528,128]{1,0:T(8,128)(2,1)S(1)}, s16[528,128]{1,0:T(8,128)(2,1)S(1)}, u32[]{:S(2)}, u32[]{:S(2)}) collective-permute-start(s16[528,128]{1,0:T(8,128)(2,1)S(1)} %get-tuple-element.76), channel_id=1, source_target_pairs={{0,2},{1,3},{4,0},{5,1},{8,4},{9,5},{12,8},{13,9},{14,12},{15,13},... | collective-permute-start | bytes 405512 | tf_op jit(solution)/shard_map/ppermute | solution.py:322
  11.5 1.4 %collective-permute-done.4.got_ref = s16[528,128]{1,0:T(8,128)(2,1)S(1)} collective-permute-done((s16[528,128]{1,0:T(8,128)(2,1)S(1)}, s16[528,128]{1,0:T(8,128)(2,1)S(1)}, u32[]{:S(2)}, u32[]{:S(2)}) %collective-permute-start.4) | collective-permute-done | bytes 135200 | tf_op jit(solution)/shard_map/ppermute | solution.py:322
  13.4 2.1 %collective-permute-start.9 = (s16[1040,128]{1,0:T(8,128)(2,1)S(1)}, s16[1040,128]{1,0:T(8,128)(2,1)S(1)}, u32[]{:S(2)}, u32[]{:S(2)}) collective-permute-start(s16[1040,128]{1,0:T(8,128)(2,1)S(1)} %sum_hop.12.before_ref), channel_id=1, source_target_pairs={{0,2},{1,3},{4,0},{5,1},{8,4},{9,5},{12,8},{13,9},{14,12},{15,13},... | collective-permute-start | bytes 798728 | tf_op jit(solution)/shard_map/ppermute | solution.py:339
  17.0 2.0 %collective-permute-start.11 = (s16[1040,128]{1,0:T(8,128)(2,1)S(1)}, s16[1040,128]{1,0:T(8,128)(2,1)S(1)}, u32[]{:S(2)}, u32[]{:S(2)}) collective-permute-start(s16[1040,128]{1,0:T(8,128)(2,1)S(1)} %sum_hop.14.before_ref), channel_id=1, source_target_pairs={{0,2},{1,3},{4,0},{5,1},{8,4},{9,5},{12,8},{13,9},{14,12},{15,13},... | collective-permute-start | bytes 798728 | tf_op jit(solution)/shard_map/ppermute | solution.py:339
  19.7 1.9 %collective-permute-done.9.got_ref = s16[1040,128]{1,0:T(8,128)(2,1)S(1)} collective-permute-done((s16[1040,128]{1,0:T(8,128)(2,1)S(1)}, s16[1040,128]{1,0:T(8,128)(2,1)S(1)}, u32[]{:S(2)}, u32[]{:S(2)}) %collective-permute-start.9) | collective-permute-done | bytes 266272 | tf_op jit(solution)/shard_map/ppermute | solution.py:339
  22.2 1.7 %collective-permute-start.14 = (s16[1040,128]{1,0:T(8,128)(2,1)S(1)}, s16[1040,128]{1,0:T(8,128)(2,1)S(1)}, u32[]{:S(2)}, u32[]{:S(2)}) collective-permute-start(s16[1040,128]{1,0:T(8,128)(2,1)S(1)} %sum_hop.16.before_ref), channel_id=1, source_target_pairs={{0,2},{1,3},{4,0},{5,1},{8,4},{9,5},{12,8},{13,9},{14,12},{15,13},... | collective-permute-start | bytes 798728 | tf_op jit(solution)/shard_map/ppermute | solution.py:339
  24.9 2.5 %collective-permute-done.11.got_ref = s16[1040,128]{1,0:T(8,128)(2,1)S(1)} collective-permute-done((s16[1040,128]{1,0:T(8,128)(2,1)S(1)}, s16[1040,128]{1,0:T(8,128)(2,1)S(1)}, u32[]{:S(2)}, u32[]{:S(2)}) %collective-permute-start.11) | collective-permute-done | bytes 266272 | tf_op jit(solution)/shard_map/ppermute | solution.py:339
  27.9 1.7 %collective-permute-start.16 = (s16[1040,128]{1,0:T(8,128)(2,1)S(1)}, s16[1040,128]{1,0:T(8,128)(2,1)S(1)}, u32[]{:S(2)}, u32[]{:S(2)}) collective-permute-start(s16[1040,128]{1,0:T(8,128)(2,1)S(1)} %sum_hop.18.before_ref), channel_id=1, source_target_pairs={{0,2},{1,3},{4,0},{5,1},{8,4},{9,5},{12,8},{13,9},{14,12},{15,13},... | collective-permute-start | bytes 798728 | tf_op jit(solution)/shard_map/ppermute | solution.py:339
  30.6 2.4 %collective-permute-done.14.got_ref = s16[1040,128]{1,0:T(8,128)(2,1)S(1)} collective-permute-done((s16[1040,128]{1,0:T(8,128)(2,1)S(1)}, s16[1040,128]{1,0:T(8,128)(2,1)S(1)}, u32[]{:S(2)}, u32[]{:S(2)}) %collective-permute-start.14) | collective-permute-done | bytes 266272 | tf_op jit(solution)/shard_map/ppermute | solution.py:339
  33.6 1.7 %collective-permute-start.19 = (s16[1040,128]{1,0:T(8,128)(2,1)S(1)}, s16[1040,128]{1,0:T(8,128)(2,1)S(1)}, u32[]{:S(2)}, u32[]{:S(2)}) collective-permute-start(s16[1040,128]{1,0:T(8,128)(2,1)S(1)} %sum_hop.20.before_ref), channel_id=1, source_target_pairs={{0,2},{1,3},{4,0},{5,1},{8,4},{9,5},{12,8},{13,9},{14,12},{15,13},... | collective-permute-start | bytes 798728 | tf_op jit(solution)/shard_map/ppermute | solution.py:339
  36.3 2.4 %collective-permute-done.16.got_ref = s16[1040,128]{1,0:T(8,128)(2,1)S(1)} collective-permute-done((s16[1040,128]{1,0:T(8,128)(2,1)S(1)}, s16[1040,128]{1,0:T(8,128)(2,1)S(1)}, u32[]{:S(2)}, u32[]{:S(2)}) %collective-permute-start.16) | collective-permute-done | bytes 266272 | tf_op jit(solution)/shard_map/ppermute | solution.py:339
  39.3 1.7 %collective-permute-start.21 = (s16[1040,128]{1,0:T(8,128)(2,1)S(1)}, s16[1040,128]{1,0:T(8,128)(2,1)S(1)}, u32[]{:S(2)}, u32[]{:S(2)}) collective-permute-start(s16[1040,128]{1,0:T(8,128)(2,1)S(1)} %sum_hop.22.before_ref), channel_id=1, source_target_pairs={{0,2},{1,3},{4,0},{5,1},{8,4},{9,5},{12,8},{13,9},{14,12},{15,13},... | collective-permute-start | bytes 798728 | tf_op jit(solution)/shard_map/ppermute | solution.py:339
  42.8 3.7 %collective-permute-done.18.refs_1_ = s16[1040,128]{1,0:T(8,128)(2,1)S(1)} collective-permute-done((s16[1040,128]{1,0:T(8,128)(2,1)S(1)}, s16[1040,128]{1,0:T(8,128)(2,1)S(1)}, u32[]{:S(2)}, u32[]{:S(2)}) %collective-permute-start.18) | collective-permute-done | bytes 266272 | tf_op jit(solution)/shard_map/ppermute | solution.py:339
  46.9 1.6 %collective-permute-start.22 = (bf16[512,256]{1,0:T(8,128)(2,1)S(1)}, bf16[512,256]{1,0:T(8,128)(2,1)S(1)}, u32[]{:S(2)}, u32[]{:S(2)}) collective-permute-start(bf16[512,256]{1,0:T(8,128)(2,1)S(1)} %effect.2.before_ref.refs_0_), channel_id=1, source_target_pairs={{0,2},{1,3},{4,0},{5,1},{8,4},{9,5},{12,8},{13,9},{14,12},{15,13},... | collective-permute-start | bytes 786440 | tf_op jit(solution)/shard_map/ppermute | solution.py:440
  49.0 3.2 %collective-permute-done.20.refs_1_ = s16[1040,128]{1,0:T(8,128)(2,1)S(1)} collective-permute-done((s16[1040,128]{1,0:T(8,128)(2,1)S(1)}, s16[1040,128]{1,0:T(8,128)(2,1)S(1)}, u32[]{:S(2)}, u32[]{:S(2)}) %collective-permute-start.20) | collective-permute-done | bytes 266272 | tf_op jit(solution)/shard_map/ppermute | solution.py:339
  52.6 1.6 %collective-permute-start.24 = (bf16[512,256]{1,0:T(8,128)(2,1)S(1)}, bf16[512,256]{1,0:T(8,128)(2,1)S(1)}, u32[]{:S(2)}, u32[]{:S(2)}) collective-permute-start(bf16[512,256]{1,0:T(8,128)(2,1)S(1)} %effect.3.before_ref.refs_3_), channel_id=1, source_target_pairs={{0,2},{1,3},{4,0},{5,1},{8,4},{9,5},{12,8},{13,9},{14,12},{15,13},... | collective-permute-start | bytes 786440 | tf_op jit(solution)/shard_map/ppermute | solution.py:440
  56.2 1.6 %collective-permute-start.26 = (bf16[512,256]{1,0:T(8,128)(2,1)S(1)}, bf16[512,256]{1,0:T(8,128)(2,1)S(1)}, u32[]{:S(2)}, u32[]{:S(2)}) collective-permute-start(bf16[512,256]{1,0:T(8,128)(2,1)S(1)} %collective-permute-done.22.refs_0_), channel_id=1, source_target_pairs={{0,2},{1,3},{4,0},{5,1},{8,4},{9,5},{12,8},{13,9},{14,12},{15,13},... | collective-permute-start | bytes 786440 | tf_op jit(solution)/shard_map/ppermute | solution.py:440
  59.1 2.8 %collective-permute-done.24.refs_0_ = bf16[512,256]{1,0:T(8,128)(2,1)S(1)} collective-permute-done((bf16[512,256]{1,0:T(8,128)(2,1)S(1)}, bf16[512,256]{1,0:T(8,128)(2,1)S(1)}, u32[]{:S(2)}, u32[]{:S(2)}) %collective-permute-start.24) | collective-permute-done | bytes 262176 | tf_op jit(solution)/shard_map/ppermute | solution.py:440
  61.8 1.6 %collective-permute-start.28 = (bf16[512,256]{1,0:T(8,128)(2,1)S(1)}, bf16[512,256]{1,0:T(8,128)(2,1)S(1)}, u32[]{:S(2)}, u32[]{:S(2)}) collective-permute-start(bf16[512,256]{1,0:T(8,128)(2,1)S(1)} %collective-permute-done.24.refs_0_), channel_id=1, source_target_pairs={{0,2},{1,3},{4,0},{5,1},{8,4},{9,5},{12,8},{13,9},{14,12},{15,13},... | collective-permute-start | bytes 786440 | tf_op jit(solution)/shard_map/ppermute | solution.py:440
  64.7 1.3 %update.2 = (f32[1024,256]{1,0:T(8,128)}, f32[1024,256]{1,0:T(8,128)}, f32[8,128]{1,0:T(8,128)S(1)}) custom-call(f32[384,256]{1,0:T(8,128)S(1)} %get-tuple-element.85.before_ref.refs_3_, f32[256,1024]{1,0:T(8,128)S(1)} %sum_near.1.before_ref.refs_0_, s16[1040,128]{1,0:T(8,128)(2,1)S(1)} %collective-permute-done.18.refs_1_, ...), custom_call_target="tpu_custom_call" | custom-call | flops 1 | bytes 1 | tf_op jit(solution)/shard_map/update/pallas_call | solution.py:377
  66.0 1.4 %collective-permute-done.26.refs_0_ = bf16[512,256]{1,0:T(8,128)(2,1)S(1)} collective-permute-done((bf16[512,256]{1,0:T(8,128)(2,1)S(1)}, bf16[512,256]{1,0:T(8,128)(2,1)S(1)}, u32[]{:S(2)}, u32[]{:S(2)}) %collective-permute-start.26) | collective-permute-done | bytes 262176 | tf_op jit(solution)/shard_map/ppermute | solution.py:440
  67.4 1.6 %collective-permute-start.30 = (bf16[512,256]{1,0:T(8,128)(2,1)S(1)}, bf16[512,256]{1,0:T(8,128)(2,1)S(1)}, u32[]{:S(2)}, u32[]{:S(2)}) collective-permute-start(bf16[512,256]{1,0:T(8,128)(2,1)S(1)} %collective-permute-done.26.refs_0_), channel_id=1, source_target_pairs={{0,2},{1,3},{4,0},{5,1},{8,4},{9,5},{12,8},{13,9},{14,12},{15,13},... | collective-permute-start | bytes 786440 | tf_op jit(solution)/shard_map/ppermute | solution.py:440
  70.5 2.6 %collective-permute-done.28.refs_0_ = bf16[512,256]{1,0:T(8,128)(2,1)S(1)} collective-permute-done((bf16[512,256]{1,0:T(8,128)(2,1)S(1)}, bf16[512,256]{1,0:T(8,128)(2,1)S(1)}, u32[]{:S(2)}, u32[]{:S(2)}) %collective-permute-start.28) | collective-permute-done | bytes 262176 | tf_op jit(solution)/shard_map/ppermute | solution.py:440
  73.1 1.6 %collective-permute-start.32 = (bf16[256,256]{1,0:T(8,128)(2,1)S(1)}, bf16[256,256]{1,0:T(8,128)(2,1)S(1)}, u32[]{:S(2)}, u32[]{:S(2)}) collective-permute-start(bf16[256,256]{1,0:T(8,128)(2,1)S(1)} %slice.24), channel_id=1, source_target_pairs={{0,2},{1,3},{4,0},{5,1},{8,4},{9,5},{12,8},{13,9},{14,12},{15,13},... | collective-permute-start | bytes 393224 | tf_op jit(solution)/shard_map/ppermute | solution.py:434
  76.0 1.3 %collective-permute-start.35 = (bf16[256,256]{1,0:T(8,128)(2,1)S(1)}, bf16[256,256]{1,0:T(8,128)(2,1)S(1)}, u32[]{:S(2)}, u32[]{:S(2)}) collective-permute-start(bf16[256,256]{1,0:T(8,128)(2,1)S(1)} %slice.27), channel_id=1, source_target_pairs={{0,4},{1,5},{4,8},{5,9},{8,12},{9,13},{12,14},{13,15},{14,10},{15,... | collective-permute-start | bytes 393224 | tf_op jit(solution)/shard_map/ppermute | solution.py:437
  77.4 1.3 %update.3 = (f32[1024,256]{1,0:T(8,128)}, f32[1024,256]{1,0:T(8,128)}, f32[8,128]{1,0:T(8,128)S(1)}) custom-call(f32[384,256]{1,0:T(8,128)S(1)} %get-tuple-element.98.before_ref.refs_3_, f32[256,1024]{1,0:T(8,128)S(1)} %sum_near.1.before_ref.refs_0_, ...), custom_call_target="tpu_custom_call", output_to_operand_aliasing={{0}: (8, {}), {1}: (9, {})} | custom-call | flops 1 | bytes 1 | tf_op jit(solution)/shard_map/update/pallas_call | solution.py:377
  78.7 1.5 %collective-permute-start.33 = (bf16[256,256]{1,0:T(8,128)(2,1)S(1)}, bf16[256,256]{1,0:T(8,128)(2,1)S(1)}, u32[]{:S(2)}, u32[]{:S(2)}) collective-permute-start(bf16[256,256]{1,0:T(8,128)(2,1)S(1)} %slice.25), channel_id=1, source_target_pairs={{0,2},{1,3},{4,0},{5,1},{8,4},{9,5},{12,8},{13,9},{14,12},{15,13},... | collective-permute-start | bytes 393224 | tf_op jit(solution)/shard_map/ppermute | solution.py:437
  80.7 1.7 %collective-permute-start.36 = (bf16[256,256]{1,0:T(8,128)(2,1)S(1)}, bf16[256,256]{1,0:T(8,128)(2,1)S(1)}, u32[]{:S(2)}, u32[]{:S(2)}) collective-permute-start(bf16[256,256]{1,0:T(8,128)(2,1)S(1)} %slice.28), channel_id=1, source_target_pairs={{0,2},{1,3},{4,0},{5,1},{8,4},{9,5},{12,8},{13,9},{14,12},{15,13},... | collective-permute-start | bytes 393224 | tf_op jit(solution)/shard_map/ppermute | solution.py:429
  84.0 1.6 %collective-permute-start.38 = (bf16[256,256]{1,0:T(8,128)(2,1)S(1)}, bf16[256,256]{1,0:T(8,128)(2,1)S(1)}, u32[]{:S(2)}, u32[]{:S(2)}) collective-permute-start(bf16[256,256]{1,0:T(8,128)(2,1)S(1)} %collective-permute-done.32.refs_0_), channel_id=1, source_target_pairs={{0,2},{1,3},{4,0},{5,1},{8,4},{9,5},{12,8},{13,9},{14,12},{15,13},... | collective-permute-start | bytes 393224 | tf_op jit(solution)/shard_map/ppermute | solution.py:429
  87.5 2.0 %collective-permute-done.37.refs_0_ = bf16[256,256]{1,0:T(8,128)(2,1)S(1)} collective-permute-done((bf16[256,256]{1,0:T(8,128)(2,1)S(1)}, bf16[256,256]{1,0:T(8,128)(2,1)S(1)}, u32[]{:S(2)}, u32[]{:S(2)}) %collective-permute-start.37) | collective-permute-done | bytes 131104 | tf_op jit(solution)/shard_map/ppermute | solution.py:429
  (125 shorter events, 29.4 us)
Async XLA Ops:
  3.7 7.5 %collective-permute-start.3 = (bf16[2,384,1024]{2,1,0:T(8,128)(2,1)S(1)}, bf16[2,384,1024]{2,1,0:T(8,128)(2,1)S(1)}, u32[]{:S(2)}, u32[]{:S(2)}) collective-permute-start(bf16[2,384,1024]{2,1,0:T(8,128)(2,1)S(1)} %get-tuple-element.72), channel_id=1, source_target_pairs={{0,1},{1,0},{2,3},{3,2},{4,5},{5,4},{6,7},{7,6},{8,9},{9,8},{10,11... | collective-permute-start | bytes 4718600 | tf_op jit(solution)/shard_map/ppermute | solution.py:273
  5.5 7.4 %collective-permute-start.4 = (s16[528,128]{1,0:T(8,128)(2,1)S(1)}, s16[528,128]{1,0:T(8,128)(2,1)S(1)}, u32[]{:S(2)}, u32[]{:S(2)}) collective-permute-start(s16[528,128]{1,0:T(8,128)(2,1)S(1)} %get-tuple-element.74), channel_id=1, source_target_pairs={{0,2},{1,3},{4,0},{5,1},{8,4},{9,5},{12,8},{13,9},{14,12},{15,13},... | collective-permute-start | bytes 405512 | tf_op jit(solution)/shard_map/ppermute | solution.py:322
  8.5 7.0 %collective-permute-start.5 = (s16[528,128]{1,0:T(8,128)(2,1)S(1)}, s16[528,128]{1,0:T(8,128)(2,1)S(1)}, u32[]{:S(2)}, u32[]{:S(2)}) collective-permute-start(s16[528,128]{1,0:T(8,128)(2,1)S(1)} %get-tuple-element.68.before_ref), channel_id=1, source_target_pairs={{0,4},{1,5},{4,8},{5,9},{8,12},{9,13},{12,14},{13,15},{14,10},{15,... | collective-permute-start | bytes 405512 | tf_op jit(solution)/shard_map/ppermute | solution.py:321
  9.1 7.4 %collective-permute-start.7 = (s16[528,128]{1,0:T(8,128)(2,1)S(1)}, s16[528,128]{1,0:T(8,128)(2,1)S(1)}, u32[]{:S(2)}, u32[]{:S(2)}) collective-permute-start(s16[528,128]{1,0:T(8,128)(2,1)S(1)} %get-tuple-element.76), channel_id=1, source_target_pairs={{0,2},{1,3},{4,0},{5,1},{8,4},{9,5},{12,8},{13,9},{14,12},{15,13},... | collective-permute-start | bytes 405512 | tf_op jit(solution)/shard_map/ppermute | solution.py:322
  11.1 8.0 %collective-permute-start.8 = (s16[528,128]{1,0:T(8,128)(2,1)S(1)}, s16[528,128]{1,0:T(8,128)(2,1)S(1)}, u32[]{:S(2)}, u32[]{:S(2)}) collective-permute-start(s16[528,128]{1,0:T(8,128)(2,1)S(1)} %get-tuple-element.73.refs_0_), channel_id=1, source_target_pairs={{0,4},{1,5},{4,8},{5,9},{8,12},{9,13},{12,14},{13,15},{14,10},{15,... | collective-permute-start | bytes 405512 | tf_op jit(solution)/shard_map/ppermute | solution.py:321
  13.4 8.2 %collective-permute-start.9 = (s16[1040,128]{1,0:T(8,128)(2,1)S(1)}, s16[1040,128]{1,0:T(8,128)(2,1)S(1)}, u32[]{:S(2)}, u32[]{:S(2)}) collective-permute-start(s16[1040,128]{1,0:T(8,128)(2,1)S(1)} %sum_hop.12.before_ref), channel_id=1, source_target_pairs={{0,2},{1,3},{4,0},{5,1},{8,4},{9,5},{12,8},{13,9},{14,12},{15,13},... | collective-permute-start | bytes 798728 | tf_op jit(solution)/shard_map/ppermute | solution.py:339
  16.1 7.9 %collective-permute-start.10 = (s16[1040,128]{1,0:T(8,128)(2,1)S(1)}, s16[1040,128]{1,0:T(8,128)(2,1)S(1)}, u32[]{:S(2)}, u32[]{:S(2)}) collective-permute-start(s16[1040,128]{1,0:T(8,128)(2,1)S(1)} %sum_hop.13.refs_0_), channel_id=1, source_target_pairs={{0,4},{1,5},{4,8},{5,9},{8,12},{9,13},{12,14},{13,15},{14,10},{15,... | collective-permute-start | bytes 798728 | tf_op jit(solution)/shard_map/ppermute | solution.py:339
  16.4 16.7 %collective-permute-start.13 = (bf16[3,384,1024]{2,1,0:T(8,128)(2,1)S(1)}, bf16[3,384,1024]{2,1,0:T(8,128)(2,1)S(1)}, u32[]{:S(2)}, u32[]{:S(2)}) collective-permute-start(bf16[3,384,1024]{2,1,0:T(8,128)(2,1)S(1)} %pick_blocks.5.before_ref), channel_id=1, source_target_pairs={{0,1},{1,0},{2,3},{3,2},{4,5},{5,4},{6,7},{7,6},{8,9},{9,8},{10,11... | collective-permute-start | bytes 7077896 | tf_op jit(solution)/shard_map/ppermute | solution.py:273
  17.0 10.3 %collective-permute-start.11 = (s16[1040,128]{1,0:T(8,128)(2,1)S(1)}, s16[1040,128]{1,0:T(8,128)(2,1)S(1)}, u32[]{:S(2)}, u32[]{:S(2)}) collective-permute-start(s16[1040,128]{1,0:T(8,128)(2,1)S(1)} %sum_hop.14.before_ref), channel_id=1, source_target_pairs={{0,2},{1,3},{4,0},{5,1},{8,4},{9,5},{12,8},{13,9},{14,12},{15,13},... | collective-permute-start | bytes 798728 | tf_op jit(solution)/shard_map/ppermute | solution.py:339
  19.6 10.1 %collective-permute-start.12 = (s16[1040,128]{1,0:T(8,128)(2,1)S(1)}, s16[1040,128]{1,0:T(8,128)(2,1)S(1)}, u32[]{:S(2)}, u32[]{:S(2)}) collective-permute-start(s16[1040,128]{1,0:T(8,128)(2,1)S(1)} %sum_hop.15.before_ref), channel_id=1, source_target_pairs={{0,4},{1,5},{4,8},{5,9},{8,12},{9,13},{12,14},{13,15},{14,10},{15,... | collective-permute-start | bytes 798728 | tf_op jit(solution)/shard_map/ppermute | solution.py:339
  22.2 10.9 %collective-permute-start.14 = (s16[1040,128]{1,0:T(8,128)(2,1)S(1)}, s16[1040,128]{1,0:T(8,128)(2,1)S(1)}, u32[]{:S(2)}, u32[]{:S(2)}) collective-permute-start(s16[1040,128]{1,0:T(8,128)(2,1)S(1)} %sum_hop.16.before_ref), channel_id=1, source_target_pairs={{0,2},{1,3},{4,0},{5,1},{8,4},{9,5},{12,8},{13,9},{14,12},{15,13},... | collective-permute-start | bytes 798728 | tf_op jit(solution)/shard_map/ppermute | solution.py:339
  24.5 10.9 %collective-permute-start.15 = (s16[1040,128]{1,0:T(8,128)(2,1)S(1)}, s16[1040,128]{1,0:T(8,128)(2,1)S(1)}, u32[]{:S(2)}, u32[]{:S(2)}) collective-permute-start(s16[1040,128]{1,0:T(8,128)(2,1)S(1)} %sum_hop.17.before_ref), channel_id=1, source_target_pairs={{0,4},{1,5},{4,8},{5,9},{8,12},{9,13},{12,14},{13,15},{14,10},{15,... | collective-permute-start | bytes 798728 | tf_op jit(solution)/shard_map/ppermute | solution.py:339
  27.9 10.8 %collective-permute-start.16 = (s16[1040,128]{1,0:T(8,128)(2,1)S(1)}, s16[1040,128]{1,0:T(8,128)(2,1)S(1)}, u32[]{:S(2)}, u32[]{:S(2)}) collective-permute-start(s16[1040,128]{1,0:T(8,128)(2,1)S(1)} %sum_hop.18.before_ref), channel_id=1, source_target_pairs={{0,2},{1,3},{4,0},{5,1},{8,4},{9,5},{12,8},{13,9},{14,12},{15,13},... | collective-permute-start | bytes 798728 | tf_op jit(solution)/shard_map/ppermute | solution.py:339
  30.2 10.9 %collective-permute-start.17 = (s16[1040,128]{1,0:T(8,128)(2,1)S(1)}, s16[1040,128]{1,0:T(8,128)(2,1)S(1)}, u32[]{:S(2)}, u32[]{:S(2)}) collective-permute-start(s16[1040,128]{1,0:T(8,128)(2,1)S(1)} %sum_hop.19.before_ref), channel_id=1, source_target_pairs={{0,4},{1,5},{4,8},{5,9},{8,12},{9,13},{12,14},{13,15},{14,10},{15,... | collective-permute-start | bytes 798728 | tf_op jit(solution)/shard_map/ppermute | solution.py:339
  33.6 12.9 %collective-permute-start.19 = (s16[1040,128]{1,0:T(8,128)(2,1)S(1)}, s16[1040,128]{1,0:T(8,128)(2,1)S(1)}, u32[]{:S(2)}, u32[]{:S(2)}) collective-permute-start(s16[1040,128]{1,0:T(8,128)(2,1)S(1)} %sum_hop.20.before_ref), channel_id=1, source_target_pairs={{0,2},{1,3},{4,0},{5,1},{8,4},{9,5},{12,8},{13,9},{14,12},{15,13},... | collective-permute-start | bytes 798728 | tf_op jit(solution)/shard_map/ppermute | solution.py:339
  35.9 10.6 %collective-permute-start.18 = (s16[1040,128]{1,0:T(8,128)(2,1)S(1)}, s16[1040,128]{1,0:T(8,128)(2,1)S(1)}, u32[]{:S(2)}, u32[]{:S(2)}) collective-permute-start(s16[1040,128]{1,0:T(8,128)(2,1)S(1)} %sum_hop.21.before_ref), channel_id=1, source_target_pairs={{0,4},{1,5},{4,8},{5,9},{8,12},{9,13},{12,14},{13,15},{14,10},{15,... | collective-permute-start | bytes 798728 | tf_op jit(solution)/shard_map/ppermute | solution.py:339
  39.3 12.9 %collective-permute-start.21 = (s16[1040,128]{1,0:T(8,128)(2,1)S(1)}, s16[1040,128]{1,0:T(8,128)(2,1)S(1)}, u32[]{:S(2)}, u32[]{:S(2)}) collective-permute-start(s16[1040,128]{1,0:T(8,128)(2,1)S(1)} %sum_hop.22.before_ref), channel_id=1, source_target_pairs={{0,2},{1,3},{4,0},{5,1},{8,4},{9,5},{12,8},{13,9},{14,12},{15,13},... | collective-permute-start | bytes 798728 | tf_op jit(solution)/shard_map/ppermute | solution.py:339
  41.7 10.5 %collective-permute-start.20 = (s16[1040,128]{1,0:T(8,128)(2,1)S(1)}, s16[1040,128]{1,0:T(8,128)(2,1)S(1)}, u32[]{:S(2)}, u32[]{:S(2)}) collective-permute-start(s16[1040,128]{1,0:T(8,128)(2,1)S(1)} %sum_hop.23.before_ref), channel_id=1, source_target_pairs={{0,4},{1,5},{4,8},{5,9},{8,12},{9,13},{12,14},{13,15},{14,10},{15,... | collective-permute-start | bytes 798728 | tf_op jit(solution)/shard_map/ppermute | solution.py:339
  46.9 9.3 %collective-permute-start.22 = (bf16[512,256]{1,0:T(8,128)(2,1)S(1)}, bf16[512,256]{1,0:T(8,128)(2,1)S(1)}, u32[]{:S(2)}, u32[]{:S(2)}) collective-permute-start(bf16[512,256]{1,0:T(8,128)(2,1)S(1)} %effect.2.before_ref.refs_0_), channel_id=1, source_target_pairs={{0,2},{1,3},{4,0},{5,1},{8,4},{9,5},{12,8},{13,9},{14,12},{15,13},... | collective-permute-start | bytes 786440 | tf_op jit(solution)/shard_map/ppermute | solution.py:440
  48.5 9.6 %collective-permute-start.23 = (bf16[512,256]{1,0:T(8,128)(2,1)S(1)}, bf16[512,256]{1,0:T(8,128)(2,1)S(1)}, u32[]{:S(2)}, u32[]{:S(2)}) collective-permute-start(bf16[512,256]{1,0:T(8,128)(2,1)S(1)} %effect.2.before_ref.refs_0_), channel_id=1, source_target_pairs={{0,4},{1,5},{4,8},{5,9},{8,12},{9,13},{12,14},{13,15},{14,10},{15,... | collective-permute-start | bytes 786440 | tf_op jit(solution)/shard_map/ppermute | solution.py:440
  52.6 9.2 %collective-permute-start.24 = (bf16[512,256]{1,0:T(8,128)(2,1)S(1)}, bf16[512,256]{1,0:T(8,128)(2,1)S(1)}, u32[]{:S(2)}, u32[]{:S(2)}) collective-permute-start(bf16[512,256]{1,0:T(8,128)(2,1)S(1)} %effect.3.before_ref.refs_3_), channel_id=1, source_target_pairs={{0,2},{1,3},{4,0},{5,1},{8,4},{9,5},{12,8},{13,9},{14,12},{15,13},... | collective-permute-start | bytes 786440 | tf_op jit(solution)/shard_map/ppermute | solution.py:440
  54.2 9.6 %collective-permute-start.25 = (bf16[512,256]{1,0:T(8,128)(2,1)S(1)}, bf16[512,256]{1,0:T(8,128)(2,1)S(1)}, u32[]{:S(2)}, u32[]{:S(2)}) collective-permute-start(bf16[512,256]{1,0:T(8,128)(2,1)S(1)} %effect.3.before_ref.refs_3_), channel_id=1, source_target_pairs={{0,4},{1,5},{4,8},{5,9},{8,12},{9,13},{12,14},{13,15},{14,10},{15,... | collective-permute-start | bytes 786440 | tf_op jit(solution)/shard_map/ppermute | solution.py:440
  56.2 11.2 %collective-permute-start.26 = (bf16[512,256]{1,0:T(8,128)(2,1)S(1)}, bf16[512,256]{1,0:T(8,128)(2,1)S(1)}, u32[]{:S(2)}, u32[]{:S(2)}) collective-permute-start(bf16[512,256]{1,0:T(8,128)(2,1)S(1)} %collective-permute-done.22.refs_0_), channel_id=1, source_target_pairs={{0,2},{1,3},{4,0},{5,1},{8,4},{9,5},{12,8},{13,9},{14,12},{15,13},... | collective-permute-start | bytes 786440 | tf_op jit(solution)/shard_map/ppermute | solution.py:440
  58.2 11.2 %collective-permute-start.27 = (bf16[512,256]{1,0:T(8,128)(2,1)S(1)}, bf16[512,256]{1,0:T(8,128)(2,1)S(1)}, u32[]{:S(2)}, u32[]{:S(2)}) collective-permute-start(bf16[512,256]{1,0:T(8,128)(2,1)S(1)} %collective-permute-done.23.refs_0_), channel_id=1, source_target_pairs={{0,4},{1,5},{4,8},{5,9},{8,12},{9,13},{12,14},{13,15},{14,10},{15,... | collective-permute-start | bytes 786440 | tf_op jit(solution)/shard_map/ppermute | solution.py:440
  61.8 11.2 %collective-permute-start.28 = (bf16[512,256]{1,0:T(8,128)(2,1)S(1)}, bf16[512,256]{1,0:T(8,128)(2,1)S(1)}, u32[]{:S(2)}, u32[]{:S(2)}) collective-permute-start(bf16[512,256]{1,0:T(8,128)(2,1)S(1)} %collective-permute-done.24.refs_0_), channel_id=1, source_target_pairs={{0,2},{1,3},{4,0},{5,1},{8,4},{9,5},{12,8},{13,9},{14,12},{15,13},... | collective-permute-start | bytes 786440 | tf_op jit(solution)/shard_map/ppermute | solution.py:440
  63.8 11.3 %collective-permute-start.29 = (bf16[512,256]{1,0:T(8,128)(2,1)S(1)}, bf16[512,256]{1,0:T(8,128)(2,1)S(1)}, u32[]{:S(2)}, u32[]{:S(2)}) collective-permute-start(bf16[512,256]{1,0:T(8,128)(2,1)S(1)} %collective-permute-done.25.refs_0_), channel_id=1, source_target_pairs={{0,4},{1,5},{4,8},{5,9},{8,12},{9,13},{12,14},{13,15},{14,10},{15,... | collective-permute-start | bytes 786440 | tf_op jit(solution)/shard_map/ppermute | solution.py:440
  67.4 11.3 %collective-permute-start.30 = (bf16[512,256]{1,0:T(8,128)(2,1)S(1)}, bf16[512,256]{1,0:T(8,128)(2,1)S(1)}, u32[]{:S(2)}, u32[]{:S(2)}) collective-permute-start(bf16[512,256]{1,0:T(8,128)(2,1)S(1)} %collective-permute-done.26.refs_0_), channel_id=1, source_target_pairs={{0,2},{1,3},{4,0},{5,1},{8,4},{9,5},{12,8},{13,9},{14,12},{15,13},... | collective-permute-start | bytes 786440 | tf_op jit(solution)/shard_map/ppermute | solution.py:440
  69.4 11.2 %collective-permute-start.31 = (bf16[512,256]{1,0:T(8,128)(2,1)S(1)}, bf16[512,256]{1,0:T(8,128)(2,1)S(1)}, u32[]{:S(2)}, u32[]{:S(2)}) collective-permute-start(bf16[512,256]{1,0:T(8,128)(2,1)S(1)} %collective-permute-done.27.refs_0_), channel_id=1, source_target_pairs={{0,4},{1,5},{4,8},{5,9},{8,12},{9,13},{12,14},{13,15},{14,10},{15,... | collective-permute-start | bytes 786440 | tf_op jit(solution)/shard_map/ppermute | solution.py:440
  73.1 10.9 %collective-permute-start.32 = (bf16[256,256]{1,0:T(8,128)(2,1)S(1)}, bf16[256,256]{1,0:T(8,128)(2,1)S(1)}, u32[]{:S(2)}, u32[]{:S(2)}) collective-permute-start(bf16[256,256]{1,0:T(8,128)(2,1)S(1)} %slice.24), channel_id=1, source_target_pairs={{0,2},{1,3},{4,0},{5,1},{8,4},{9,5},{12,8},{13,9},{14,12},{15,13},... | collective-permute-start | bytes 393224 | tf_op jit(solution)/shard_map/ppermute | solution.py:434
  75.5 7.5 %collective-permute-start.34 = (bf16[256,256]{1,0:T(8,128)(2,1)S(1)}, bf16[256,256]{1,0:T(8,128)(2,1)S(1)}, u32[]{:S(2)}, u32[]{:S(2)}) collective-permute-start(bf16[256,256]{1,0:T(8,128)(2,1)S(1)} %slice.26), channel_id=1, source_target_pairs={{0,4},{1,5},{4,8},{5,9},{8,12},{9,13},{12,14},{13,15},{14,10},{15,... | collective-permute-start | bytes 393224 | tf_op jit(solution)/shard_map/ppermute | solution.py:434
  76.0 10.8 %collective-permute-start.35 = (bf16[256,256]{1,0:T(8,128)(2,1)S(1)}, bf16[256,256]{1,0:T(8,128)(2,1)S(1)}, u32[]{:S(2)}, u32[]{:S(2)}) collective-permute-start(bf16[256,256]{1,0:T(8,128)(2,1)S(1)} %slice.27), channel_id=1, source_target_pairs={{0,4},{1,5},{4,8},{5,9},{8,12},{9,13},{12,14},{13,15},{14,10},{15,... | collective-permute-start | bytes 393224 | tf_op jit(solution)/shard_map/ppermute | solution.py:437
  78.7 6.9 %collective-permute-start.33 = (bf16[256,256]{1,0:T(8,128)(2,1)S(1)}, bf16[256,256]{1,0:T(8,128)(2,1)S(1)}, u32[]{:S(2)}, u32[]{:S(2)}) collective-permute-start(bf16[256,256]{1,0:T(8,128)(2,1)S(1)} %slice.25), channel_id=1, source_target_pairs={{0,2},{1,3},{4,0},{5,1},{8,4},{9,5},{12,8},{13,9},{14,12},{15,13},... | collective-permute-start | bytes 393224 | tf_op jit(solution)/shard_map/ppermute | solution.py:437
  (22 other events, 88.8 us)

commit v15 on v12

--- a/solution.py
+++ b/solution.py
@@ -209,9 +209,13 @@
     refs[-1][...] = columns_product(ring, places, genotype_ref, refs, eta)
 
 
-def end_kernel(ring, places, genotype_ref, eta_ref, upper_ref, lower_ref, labels_ref, *refs):
+def other_kernel(ring, places, genotype_ref, eta_ref, upper_ref, lower_ref, *refs):
     got = jnp.concatenate([upper_ref[...], lower_ref[...]], axis=0)
-    eta = columns_product(ring, places, genotype_ref, refs, eta_ref[...] + got)
+    refs[-1][...] = columns_product(ring, places, genotype_ref, refs, eta_ref[...] + got)
+
+
+def end_kernel(ring, places, genotype_ref, eta_ref, labels_ref, *refs):
+    eta = columns_product(ring, places, genotype_ref, refs, eta_ref[...])
     refs[-1][...] = 4.0 * (labels_ref[...].astype(jnp.float32) - jax.nn.sigmoid(eta))
 
 
@@ -320,7 +324,7 @@
             else:
                 if d == reach - 1 > 1 and piece == pieces - 1:
                     last, _ = lax.optimization_barrier((last, peer[d - 1][0]))
-                for way in (1, 0):
+                for way in (0, 1):
                     w = size - d if way else d
                     args = (res, genotype, peer[w][0], got[way, piece])
                     last = pl.pallas_call(
@@ -338,7 +342,7 @@
                 if d == reach > 1:
                     last, _ = lax.optimization_barrier((last, peer[d - 1][0]))
                 distances = later.pop(0)
-                (last,) = pick(whole(distances), pltpu.VMEM, light, last)
+                (last,) = pick(whole(distances), pltpu.VMEM, small, last)
                 swapped(distances, last)
 
     near = last = pl.pallas_call(
@@ -412,7 +416,7 @@
     outs, updated, final = (), 0, []
     for hop in range(1, reach + 1):
         for piece in range(pieces):
-            for way in (1, 0):
+            for way in (0, 1):
                 message = held[way, piece]
                 perm = left if way else right
                 d, low = (hop if way else size - hop), piece * part
@@ -459,13 +463,21 @@
         cost_estimate=heavy,
         name="own_last",
     )(genotype, eta[0], offset.reshape(1, cols), *[effect for _, _, effect in final])
+    there = [(d, low, True) for d, low, _ in final]
+    mine = pl.pallas_call(
+        functools.partial(other_kernel, ring, there[:1]),
+        out_shape=eta_shape,
+        compiler_params=params,
+        cost_estimate=heavy,
+        name="other_last",
+    )(genotype, mine, *eta_got, others[0])
     resid_new = pl.pallas_call(
-        functools.partial(end_kernel, ring, [(d, low, True) for d, low, _ in final]),
+        functools.partial(end_kernel, ring, there[1:]),
         out_shape=eta_shape,
         compiler_params=params,
         cost_estimate=light,
         name="new_residual",
-    )(genotype, mine, *eta_got, labels, *others)
+    )(genotype, mine, labels, *others[1:])
     return (outs[0], outs[1], resid_new)
 
 

time: 93.5 us -> 93.5 us (level)
    ppermute x2, starting transfers between devices: 0.24 us -> 3.19 us  [on_device(): got[0, piece] = lax.ppermute(sent[0], 'ind', right)]
    ppermute x2, starting transfers between devices: 4.95 us -> 2.02 us  [on_device(): got[1, piece] = lax.ppermute(sent[1], 'ind', left)]
    ppermute x2, waiting for transfers between devices: 1.43 us -> 0.01 us  [on_device(): got[1, piece] = lax.ppermute(sent[1], 'ind', left)]
    ppermute x2, waiting for transfers between devices: 0.01 us -> 1.35 us  [on_device(): got[0, piece] = lax.ppermute(sent[0], 'ind', right)]
  transfers between devices with their start and end apart: 44 -> 44, of which waited for: 16 -> 18; matrix products, arithmetic and copies ran while one was open for 0% -> 0% of each run, Pallas kernels for 21% -> 21%
where the time goes in v15:
time: 93.5 us; the launch traced here: 93.3 us
  starting transfers between devices  40.7 us (44%)
  waiting for transfers between devices  29.1 us (31%)
  Pallas kernels  22.2 us (24%)
  between operations  1.22 us (1%)
    ppermute x12, waiting for transfers between devices, on_device(): got[way, piece] = lax.ppermute(last, 'ind', left if way else right)  16 us
    ppermute x14, starting transfers between devices, on_device(): held[way, piece] = lax.ppermute(message, 'ind', perm)  15.5 us
    ppermute x12, starting transfers between devices, on_device(): got[way, piece] = lax.ppermute(last, 'ind', left if way else right)  13.2 us
    ppermute x14, waiting for transfers between devices, on_device(): held[way, piece] = lax.ppermute(message, 'ind', perm)  10.1 us
    pallas_call x12, Pallas kernels, on_device(): pl.pallas_call(functools.partial(hop_kernel, ring, (w, peer[w][1]), low,...  6.62 us
    pallas_call x15, Pallas kernels, product(): pl.pallas_call(functools.partial(eta_kernel, ring, places, not eta), in_s...  5.58 us
    pallas_call x4, Pallas kernels, pick(): pl.pallas_call(functools.partial(pick_kernel, ring, wanted, block), in_sp...  3.25 us
    ppermute x2, starting transfers between devices, on_device(): got[0, piece] = lax.ppermute(sent[0], 'ind', right)  3.19 us
  transfers between devices with their start and end apart: 44, of which 18 were waited for; matrix products, arithmetic and copies ran while one was open for 0% of the time, Pallas kernels for 21%

profile of v15, /device:TPU:0, one launch (start us, length us, event | category | flops | bytes accessed | tf_op | source)
XLA Modules:
  0.0 93.3 jit_solution(10567269727907986879)
XLA Ops:
  0.6 1.2 %pick_blocks.4 = (bf16[1,384,512]{2,1,0:T(8,128)(2,1)S(1)}, bf16[1,384,512]{2,1,0:T(8,128)(2,1)S(1)}) custom-call(bf16[384,16384]{1,0:T(8,128)(2,1)} %genotype_ref.13), custom_call_target="tpu_custom_call" | custom-call | flops 1 | bytes 1 | tf_op jit(solution)/shard_map/pick_blocks/pallas_call | solution.py:252
  2.5 1.7 %pick_blocks.5 = (bf16[1,384,512]{2,1,0:T(8,128)(2,1)S(1)}, bf16[1,384,512]{2,1,0:T(8,128)(2,1)S(1)}, bf16[2,384,1024]{2,1,0:T(8,128)(2,1)S(1)}) custom-call(bf16[384,16384]{1,0:T(8,128)(2,1)} %genotype_ref.13, bf16[1,384,512]{2,1,0:T(8,128)(2,1)S(1)} %get-tuple-element.65.refs_0_), custom_call_target="tpu_custom_call" | custom-call | flops 10000000000 | bytes 1000000 | tf_op jit(solution)/shard_map/pick_blocks/pallas_call | solution.py:252
  5.4 3.0 %collective-permute-start.4 = (s16[528,128]{1,0:T(8,128)(2,1)S(1)}, s16[528,128]{1,0:T(8,128)(2,1)S(1)}, u32[]{:S(2)}, u32[]{:S(2)}) collective-permute-start(s16[528,128]{1,0:T(8,128)(2,1)S(1)} %get-tuple-element.69.before_ref), channel_id=1, source_target_pairs={{0,4},{1,5},{4,8},{5,9},{8,12},{9,13},{12,14},{13,15},{14,10},{15,... | collective-permute-start | bytes 405512 | tf_op jit(solution)/shard_map/ppermute | solution.py:322
  9.0 2.0 %collective-permute-start.8 = (s16[528,128]{1,0:T(8,128)(2,1)S(1)}, s16[528,128]{1,0:T(8,128)(2,1)S(1)}, u32[]{:S(2)}, u32[]{:S(2)}) collective-permute-start(s16[528,128]{1,0:T(8,128)(2,1)S(1)} %get-tuple-element.76), channel_id=1, source_target_pairs={{0,2},{1,3},{4,0},{5,1},{8,4},{9,5},{12,8},{13,9},{14,12},{15,13},... | collective-permute-start | bytes 405512 | tf_op jit(solution)/shard_map/ppermute | solution.py:323
  12.9 2.5 %collective-permute-start.9 = (s16[1040,128]{1,0:T(8,128)(2,1)S(1)}, s16[1040,128]{1,0:T(8,128)(2,1)S(1)}, u32[]{:S(2)}, u32[]{:S(2)}) collective-permute-start(s16[1040,128]{1,0:T(8,128)(2,1)S(1)} %sum_hop.12.before_ref), channel_id=1, source_target_pairs={{0,4},{1,5},{4,8},{5,9},{8,12},{9,13},{12,14},{13,15},{14,10},{15,... | collective-permute-start | bytes 798728 | tf_op jit(solution)/shard_map/ppermute | solution.py:340
  17.4 1.6 %collective-permute-start.11 = (s16[1040,128]{1,0:T(8,128)(2,1)S(1)}, s16[1040,128]{1,0:T(8,128)(2,1)S(1)}, u32[]{:S(2)}, u32[]{:S(2)}) collective-permute-start(s16[1040,128]{1,0:T(8,128)(2,1)S(1)} %sum_hop.14.before_ref), channel_id=1, source_target_pairs={{0,4},{1,5},{4,8},{5,9},{8,12},{9,13},{12,14},{13,15},{14,10},{15,... | collective-permute-start | bytes 798728 | tf_op jit(solution)/shard_map/ppermute | solution.py:340
  20.1 2.5 %collective-permute-done.9.got_ref = s16[1040,128]{1,0:T(8,128)(2,1)S(1)} collective-permute-done((s16[1040,128]{1,0:T(8,128)(2,1)S(1)}, s16[1040,128]{1,0:T(8,128)(2,1)S(1)}, u32[]{:S(2)}, u32[]{:S(2)}) %collective-permute-start.9) | collective-permute-done | bytes 266272 | tf_op jit(solution)/shard_map/ppermute | solution.py:340
  24.7 1.1 %collective-permute-start.15 = (s16[1040,128]{1,0:T(8,128)(2,1)S(1)}, s16[1040,128]{1,0:T(8,128)(2,1)S(1)}, u32[]{:S(2)}, u32[]{:S(2)}) collective-permute-start(s16[1040,128]{1,0:T(8,128)(2,1)S(1)} %sum_hop.17.before_ref), channel_id=1, source_target_pairs={{0,2},{1,3},{4,0},{5,1},{8,4},{9,5},{12,8},{13,9},{14,12},{15,13},... | collective-permute-start | bytes 798728 | tf_op jit(solution)/shard_map/ppermute | solution.py:340
  25.8 2.4 %collective-permute-done.11.got_ref = s16[1040,128]{1,0:T(8,128)(2,1)S(1)} collective-permute-done((s16[1040,128]{1,0:T(8,128)(2,1)S(1)}, s16[1040,128]{1,0:T(8,128)(2,1)S(1)}, u32[]{:S(2)}, u32[]{:S(2)}) %collective-permute-start.11) | collective-permute-done | bytes 266272 | tf_op jit(solution)/shard_map/ppermute | solution.py:340
  30.4 1.1 %collective-permute-start.17 = (s16[1040,128]{1,0:T(8,128)(2,1)S(1)}, s16[1040,128]{1,0:T(8,128)(2,1)S(1)}, u32[]{:S(2)}, u32[]{:S(2)}) collective-permute-start(s16[1040,128]{1,0:T(8,128)(2,1)S(1)} %sum_hop.19.before_ref), channel_id=1, source_target_pairs={{0,2},{1,3},{4,0},{5,1},{8,4},{9,5},{12,8},{13,9},{14,12},{15,13},... | collective-permute-start | bytes 798728 | tf_op jit(solution)/shard_map/ppermute | solution.py:340
  31.5 2.4 %collective-permute-done.14.got_ref = s16[1040,128]{1,0:T(8,128)(2,1)S(1)} collective-permute-done((s16[1040,128]{1,0:T(8,128)(2,1)S(1)}, s16[1040,128]{1,0:T(8,128)(2,1)S(1)}, u32[]{:S(2)}, u32[]{:S(2)}) %collective-permute-start.14) | collective-permute-done | bytes 266272 | tf_op jit(solution)/shard_map/ppermute | solution.py:340
  37.2 2.4 %collective-permute-done.16.got_ref = s16[1040,128]{1,0:T(8,128)(2,1)S(1)} collective-permute-done((s16[1040,128]{1,0:T(8,128)(2,1)S(1)}, s16[1040,128]{1,0:T(8,128)(2,1)S(1)}, u32[]{:S(2)}, u32[]{:S(2)}) %collective-permute-start.16) | collective-permute-done | bytes 266272 | tf_op jit(solution)/shard_map/ppermute | solution.py:340
  43.7 3.0 %collective-permute-done.19.refs_2_ = s16[1040,128]{1,0:T(8,128)(2,1)S(1)} collective-permute-done((s16[1040,128]{1,0:T(8,128)(2,1)S(1)}, s16[1040,128]{1,0:T(8,128)(2,1)S(1)}, u32[]{:S(2)}, u32[]{:S(2)}) %collective-permute-start.19) | collective-permute-done | bytes 266272 | tf_op jit(solution)/shard_map/ppermute | solution.py:340
  47.1 1.7 %collective-permute-start.22 = (bf16[512,256]{1,0:T(8,128)(2,1)S(1)}, bf16[512,256]{1,0:T(8,128)(2,1)S(1)}, u32[]{:S(2)}, u32[]{:S(2)}) collective-permute-start(bf16[512,256]{1,0:T(8,128)(2,1)S(1)} %effect.2.before_ref.refs_0_), channel_id=1, source_target_pairs={{0,4},{1,5},{4,8},{5,9},{8,12},{9,13},{12,14},{13,15},{14,10},{15,... | collective-permute-start | bytes 786440 | tf_op jit(solution)/shard_map/ppermute | solution.py:441
  49.1 3.2 %collective-permute-done.21.refs_2_ = s16[1040,128]{1,0:T(8,128)(2,1)S(1)} collective-permute-done((s16[1040,128]{1,0:T(8,128)(2,1)S(1)}, s16[1040,128]{1,0:T(8,128)(2,1)S(1)}, u32[]{:S(2)}, u32[]{:S(2)}) %collective-permute-start.21) | collective-permute-done | bytes 266272 | tf_op jit(solution)/shard_map/ppermute | solution.py:340
  52.7 1.7 %collective-permute-start.24 = (bf16[512,256]{1,0:T(8,128)(2,1)S(1)}, bf16[512,256]{1,0:T(8,128)(2,1)S(1)}, u32[]{:S(2)}, u32[]{:S(2)}) collective-permute-start(bf16[512,256]{1,0:T(8,128)(2,1)S(1)} %effect.3.before_ref.refs_3_), channel_id=1, source_target_pairs={{0,4},{1,5},{4,8},{5,9},{8,12},{9,13},{12,14},{13,15},{14,10},{15,... | collective-permute-start | bytes 786440 | tf_op jit(solution)/shard_map/ppermute | solution.py:441
  55.4 1.3 %collective-permute-done.22.refs_0_ = bf16[512,256]{1,0:T(8,128)(2,1)S(1)} collective-permute-done((bf16[512,256]{1,0:T(8,128)(2,1)S(1)}, bf16[512,256]{1,0:T(8,128)(2,1)S(1)}, u32[]{:S(2)}, u32[]{:S(2)}) %collective-permute-start.22) | collective-permute-done | bytes 262176 | tf_op jit(solution)/shard_map/ppermute | solution.py:441
  56.7 1.3 %collective-permute-start.26 = (bf16[512,256]{1,0:T(8,128)(2,1)S(1)}, bf16[512,256]{1,0:T(8,128)(2,1)S(1)}, u32[]{:S(2)}, u32[]{:S(2)}) collective-permute-start(bf16[512,256]{1,0:T(8,128)(2,1)S(1)} %collective-permute-done.22.refs_0_), channel_id=1, source_target_pairs={{0,4},{1,5},{4,8},{5,9},{8,12},{9,13},{12,14},{13,15},{14,10},{15,... | collective-permute-start | bytes 786440 | tf_op jit(solution)/shard_map/ppermute | solution.py:441
  59.5 2.8 %collective-permute-done.24.refs_0_ = bf16[512,256]{1,0:T(8,128)(2,1)S(1)} collective-permute-done((bf16[512,256]{1,0:T(8,128)(2,1)S(1)}, bf16[512,256]{1,0:T(8,128)(2,1)S(1)}, u32[]{:S(2)}, u32[]{:S(2)}) %collective-permute-start.24) | collective-permute-done | bytes 262176 | tf_op jit(solution)/shard_map/ppermute | solution.py:441
  62.3 1.3 %collective-permute-start.28 = (bf16[512,256]{1,0:T(8,128)(2,1)S(1)}, bf16[512,256]{1,0:T(8,128)(2,1)S(1)}, u32[]{:S(2)}, u32[]{:S(2)}) collective-permute-start(bf16[512,256]{1,0:T(8,128)(2,1)S(1)} %collective-permute-done.24.refs_0_), channel_id=1, source_target_pairs={{0,4},{1,5},{4,8},{5,9},{8,12},{9,13},{12,14},{13,15},{14,10},{15,... | collective-permute-start | bytes 786440 | tf_op jit(solution)/shard_map/ppermute | solution.py:441
  65.2 1.3 %update.2 = (f32[1024,256]{1,0:T(8,128)}, f32[1024,256]{1,0:T(8,128)}, f32[8,128]{1,0:T(8,128)S(1)}) custom-call(f32[384,256]{1,0:T(8,128)S(1)} %get-tuple-element.85.before_ref.refs_3_, f32[256,1024]{1,0:T(8,128)S(1)} %sum_near.1.before_ref.refs_0_, s16[1040,128]{1,0:T(8,128)(2,1)S(1)} %collective-permute-done.18.refs_1_, ...), custom_call_target="tpu_custom_call" | custom-call | flops 1 | bytes 1 | tf_op jit(solution)/shard_map/update/pallas_call | solution.py:378
  66.5 1.4 %collective-permute-done.26.refs_0_ = bf16[512,256]{1,0:T(8,128)(2,1)S(1)} collective-permute-done((bf16[512,256]{1,0:T(8,128)(2,1)S(1)}, bf16[512,256]{1,0:T(8,128)(2,1)S(1)}, u32[]{:S(2)}, u32[]{:S(2)}) %collective-permute-start.26) | collective-permute-done | bytes 262176 | tf_op jit(solution)/shard_map/ppermute | solution.py:441
  67.9 1.3 %collective-permute-start.30 = (bf16[512,256]{1,0:T(8,128)(2,1)S(1)}, bf16[512,256]{1,0:T(8,128)(2,1)S(1)}, u32[]{:S(2)}, u32[]{:S(2)}) collective-permute-start(bf16[512,256]{1,0:T(8,128)(2,1)S(1)} %collective-permute-done.26.refs_0_), channel_id=1, source_target_pairs={{0,4},{1,5},{4,8},{5,9},{8,12},{9,13},{12,14},{13,15},{14,10},{15,... | collective-permute-start | bytes 786440 | tf_op jit(solution)/shard_map/ppermute | solution.py:441
  70.8 2.8 %collective-permute-done.28.refs_0_ = bf16[512,256]{1,0:T(8,128)(2,1)S(1)} collective-permute-done((bf16[512,256]{1,0:T(8,128)(2,1)S(1)}, bf16[512,256]{1,0:T(8,128)(2,1)S(1)}, u32[]{:S(2)}, u32[]{:S(2)}) %collective-permute-start.28) | collective-permute-done | bytes 262176 | tf_op jit(solution)/shard_map/ppermute | solution.py:441
  73.5 1.4 %collective-permute-start.32 = (bf16[256,256]{1,0:T(8,128)(2,1)S(1)}, bf16[256,256]{1,0:T(8,128)(2,1)S(1)}, u32[]{:S(2)}, u32[]{:S(2)}) collective-permute-start(bf16[256,256]{1,0:T(8,128)(2,1)S(1)} %slice.24), channel_id=1, source_target_pairs={{0,4},{1,5},{4,8},{5,9},{8,12},{9,13},{12,14},{13,15},{14,10},{15,... | collective-permute-start | bytes 393224 | tf_op jit(solution)/shard_map/ppermute | solution.py:435
  76.5 1.4 %collective-permute-start.35 = (bf16[256,256]{1,0:T(8,128)(2,1)S(1)}, bf16[256,256]{1,0:T(8,128)(2,1)S(1)}, u32[]{:S(2)}, u32[]{:S(2)}) collective-permute-start(bf16[256,256]{1,0:T(8,128)(2,1)S(1)} %slice.27), channel_id=1, source_target_pairs={{0,2},{1,3},{4,0},{5,1},{8,4},{9,5},{12,8},{13,9},{14,12},{15,13},... | collective-permute-start | bytes 393224 | tf_op jit(solution)/shard_map/ppermute | solution.py:438
  77.9 1.3 %update.3 = (f32[1024,256]{1,0:T(8,128)}, f32[1024,256]{1,0:T(8,128)}, f32[8,128]{1,0:T(8,128)S(1)}) custom-call(f32[384,256]{1,0:T(8,128)S(1)} %get-tuple-element.98.before_ref.refs_3_, f32[256,1024]{1,0:T(8,128)S(1)} %sum_near.1.before_ref.refs_0_, ...), custom_call_target="tpu_custom_call", output_to_operand_aliasing={{0}: (8, {}), {1}: (9, {})} | custom-call | flops 1 | bytes 1 | tf_op jit(solution)/shard_map/update/pallas_call | solution.py:378
  79.2 1.3 %collective-permute-start.33 = (bf16[256,256]{1,0:T(8,128)(2,1)S(1)}, bf16[256,256]{1,0:T(8,128)(2,1)S(1)}, u32[]{:S(2)}, u32[]{:S(2)}) collective-permute-start(bf16[256,256]{1,0:T(8,128)(2,1)S(1)} %slice.25), channel_id=1, source_target_pairs={{0,4},{1,5},{4,8},{5,9},{8,12},{9,13},{12,14},{13,15},{14,10},{15,... | collective-permute-start | bytes 393224 | tf_op jit(solution)/shard_map/ppermute | solution.py:438
  80.9 1.6 %collective-permute-start.36 = (bf16[256,256]{1,0:T(8,128)(2,1)S(1)}, bf16[256,256]{1,0:T(8,128)(2,1)S(1)}, u32[]{:S(2)}, u32[]{:S(2)}) collective-permute-start(bf16[256,256]{1,0:T(8,128)(2,1)S(1)} %slice.28), channel_id=1, source_target_pairs={{0,4},{1,5},{4,8},{5,9},{8,12},{9,13},{12,14},{13,15},{14,10},{15,... | collective-permute-start | bytes 393224 | tf_op jit(solution)/shard_map/ppermute | solution.py:430
  84.1 1.8 %collective-permute-start.38 = (bf16[256,256]{1,0:T(8,128)(2,1)S(1)}, bf16[256,256]{1,0:T(8,128)(2,1)S(1)}, u32[]{:S(2)}, u32[]{:S(2)}) collective-permute-start(bf16[256,256]{1,0:T(8,128)(2,1)S(1)} %collective-permute-done.32.refs_0_), channel_id=1, source_target_pairs={{0,4},{1,5},{4,8},{5,9},{8,12},{9,13},{12,14},{13,15},{14,10},{15,... | collective-permute-start | bytes 393224 | tf_op jit(solution)/shard_map/ppermute | solution.py:430
  85.8 1.4 %collective-permute-start.39 = (bf16[256,256]{1,0:T(8,128)(2,1)S(1)}, bf16[256,256]{1,0:T(8,128)(2,1)S(1)}, u32[]{:S(2)}, u32[]{:S(2)}) collective-permute-start(bf16[256,256]{1,0:T(8,128)(2,1)S(1)} %collective-permute-done.34.refs_0_), channel_id=1, source_target_pairs={{0,2},{1,3},{4,0},{5,1},{8,4},{9,5},{12,8},{13,9},{14,12},{15,13},... | collective-permute-start | bytes 393224 | tf_op jit(solution)/shard_map/ppermute | solution.py:430
  88.5 1.1 %collective-permute-done.37.refs_0_ = bf16[256,256]{1,0:T(8,128)(2,1)S(1)} collective-permute-done((bf16[256,256]{1,0:T(8,128)(2,1)S(1)}, bf16[256,256]{1,0:T(8,128)(2,1)S(1)}, u32[]{:S(2)}, u32[]{:S(2)}) %collective-permute-start.37) | collective-permute-done | bytes 131104 | tf_op jit(solution)/shard_map/ppermute | solution.py:430
  (126 shorter events, 33.6 us)
Async XLA Ops:
  4.6 6.6 %collective-permute-start.3 = (bf16[2,384,1024]{2,1,0:T(8,128)(2,1)S(1)}, bf16[2,384,1024]{2,1,0:T(8,128)(2,1)S(1)}, u32[]{:S(2)}, u32[]{:S(2)}) collective-permute-start(bf16[2,384,1024]{2,1,0:T(8,128)(2,1)S(1)} %get-tuple-element.72), channel_id=1, source_target_pairs={{0,1},{1,0},{2,3},{3,2},{4,5},{5,4},{6,7},{7,6},{8,9},{9,8},{10,11... | collective-permute-start | bytes 4718600 | tf_op jit(solution)/shard_map/ppermute | solution.py:273
  5.4 6.9 %collective-permute-start.4 = (s16[528,128]{1,0:T(8,128)(2,1)S(1)}, s16[528,128]{1,0:T(8,128)(2,1)S(1)}, u32[]{:S(2)}, u32[]{:S(2)}) collective-permute-start(s16[528,128]{1,0:T(8,128)(2,1)S(1)} %get-tuple-element.69.before_ref), channel_id=1, source_target_pairs={{0,4},{1,5},{4,8},{5,9},{8,12},{9,13},{12,14},{13,15},{14,10},{15,... | collective-permute-start | bytes 405512 | tf_op jit(solution)/shard_map/ppermute | solution.py:322
  8.5 6.9 %collective-permute-start.5 = (s16[528,128]{1,0:T(8,128)(2,1)S(1)}, s16[528,128]{1,0:T(8,128)(2,1)S(1)}, u32[]{:S(2)}, u32[]{:S(2)}) collective-permute-start(s16[528,128]{1,0:T(8,128)(2,1)S(1)} %get-tuple-element.74), channel_id=1, source_target_pairs={{0,2},{1,3},{4,0},{5,1},{8,4},{9,5},{12,8},{13,9},{14,12},{15,13},... | collective-permute-start | bytes 405512 | tf_op jit(solution)/shard_map/ppermute | solution.py:323
  9.0 10.0 %collective-permute-start.8 = (s16[528,128]{1,0:T(8,128)(2,1)S(1)}, s16[528,128]{1,0:T(8,128)(2,1)S(1)}, u32[]{:S(2)}, u32[]{:S(2)}) collective-permute-start(s16[528,128]{1,0:T(8,128)(2,1)S(1)} %get-tuple-element.76), channel_id=1, source_target_pairs={{0,2},{1,3},{4,0},{5,1},{8,4},{9,5},{12,8},{13,9},{14,12},{15,13},... | collective-permute-start | bytes 405512 | tf_op jit(solution)/shard_map/ppermute | solution.py:323
  12.9 9.6 %collective-permute-start.9 = (s16[1040,128]{1,0:T(8,128)(2,1)S(1)}, s16[1040,128]{1,0:T(8,128)(2,1)S(1)}, u32[]{:S(2)}, u32[]{:S(2)}) collective-permute-start(s16[1040,128]{1,0:T(8,128)(2,1)S(1)} %sum_hop.12.before_ref), channel_id=1, source_target_pairs={{0,4},{1,5},{4,8},{5,9},{8,12},{9,13},{12,14},{13,15},{14,10},{15,... | collective-permute-start | bytes 798728 | tf_op jit(solution)/shard_map/ppermute | solution.py:340
  16.0 8.1 %collective-permute-start.10 = (s16[1040,128]{1,0:T(8,128)(2,1)S(1)}, s16[1040,128]{1,0:T(8,128)(2,1)S(1)}, u32[]{:S(2)}, u32[]{:S(2)}) collective-permute-start(s16[1040,128]{1,0:T(8,128)(2,1)S(1)} %sum_hop.13.refs_0_), channel_id=1, source_target_pairs={{0,2},{1,3},{4,0},{5,1},{8,4},{9,5},{12,8},{13,9},{14,12},{15,13},... | collective-permute-start | bytes 798728 | tf_op jit(solution)/shard_map/ppermute | solution.py:340
  16.3 17.7 %collective-permute-start.13 = (bf16[3,384,1024]{2,1,0:T(8,128)(2,1)S(1)}, bf16[3,384,1024]{2,1,0:T(8,128)(2,1)S(1)}, u32[]{:S(2)}, u32[]{:S(2)}) collective-permute-start(bf16[3,384,1024]{2,1,0:T(8,128)(2,1)S(1)} %pick_blocks.7.before_ref), channel_id=1, source_target_pairs={{0,1},{1,0},{2,3},{3,2},{4,5},{5,4},{6,7},{7,6},{8,9},{9,8},{10,11... | collective-permute-start | bytes 7077896 | tf_op jit(solution)/shard_map/ppermute | solution.py:273
  17.4 10.9 %collective-permute-start.11 = (s16[1040,128]{1,0:T(8,128)(2,1)S(1)}, s16[1040,128]{1,0:T(8,128)(2,1)S(1)}, u32[]{:S(2)}, u32[]{:S(2)}) collective-permute-start(s16[1040,128]{1,0:T(8,128)(2,1)S(1)} %sum_hop.14.before_ref), channel_id=1, source_target_pairs={{0,4},{1,5},{4,8},{5,9},{8,12},{9,13},{12,14},{13,15},{14,10},{15,... | collective-permute-start | bytes 798728 | tf_op jit(solution)/shard_map/ppermute | solution.py:340
  19.5 10.3 %collective-permute-start.12 = (s16[1040,128]{1,0:T(8,128)(2,1)S(1)}, s16[1040,128]{1,0:T(8,128)(2,1)S(1)}, u32[]{:S(2)}, u32[]{:S(2)}) collective-permute-start(s16[1040,128]{1,0:T(8,128)(2,1)S(1)} %sum_hop.15.before_ref), channel_id=1, source_target_pairs={{0,2},{1,3},{4,0},{5,1},{8,4},{9,5},{12,8},{13,9},{14,12},{15,13},... | collective-permute-start | bytes 798728 | tf_op jit(solution)/shard_map/ppermute | solution.py:340
  23.1 10.9 %collective-permute-start.14 = (s16[1040,128]{1,0:T(8,128)(2,1)S(1)}, s16[1040,128]{1,0:T(8,128)(2,1)S(1)}, u32[]{:S(2)}, u32[]{:S(2)}) collective-permute-start(s16[1040,128]{1,0:T(8,128)(2,1)S(1)} %sum_hop.16.before_ref), channel_id=1, source_target_pairs={{0,4},{1,5},{4,8},{5,9},{8,12},{9,13},{12,14},{13,15},{14,10},{15,... | collective-permute-start | bytes 798728 | tf_op jit(solution)/shard_map/ppermute | solution.py:340
  24.7 10.9 %collective-permute-start.15 = (s16[1040,128]{1,0:T(8,128)(2,1)S(1)}, s16[1040,128]{1,0:T(8,128)(2,1)S(1)}, u32[]{:S(2)}, u32[]{:S(2)}) collective-permute-start(s16[1040,128]{1,0:T(8,128)(2,1)S(1)} %sum_hop.17.before_ref), channel_id=1, source_target_pairs={{0,2},{1,3},{4,0},{5,1},{8,4},{9,5},{12,8},{13,9},{14,12},{15,13},... | collective-permute-start | bytes 798728 | tf_op jit(solution)/shard_map/ppermute | solution.py:340
  28.8 10.8 %collective-permute-start.16 = (s16[1040,128]{1,0:T(8,128)(2,1)S(1)}, s16[1040,128]{1,0:T(8,128)(2,1)S(1)}, u32[]{:S(2)}, u32[]{:S(2)}) collective-permute-start(s16[1040,128]{1,0:T(8,128)(2,1)S(1)} %sum_hop.18.before_ref), channel_id=1, source_target_pairs={{0,4},{1,5},{4,8},{5,9},{8,12},{9,13},{12,14},{13,15},{14,10},{15,... | collective-permute-start | bytes 798728 | tf_op jit(solution)/shard_map/ppermute | solution.py:340
  30.4 10.8 %collective-permute-start.17 = (s16[1040,128]{1,0:T(8,128)(2,1)S(1)}, s16[1040,128]{1,0:T(8,128)(2,1)S(1)}, u32[]{:S(2)}, u32[]{:S(2)}) collective-permute-start(s16[1040,128]{1,0:T(8,128)(2,1)S(1)} %sum_hop.19.before_ref), channel_id=1, source_target_pairs={{0,2},{1,3},{4,0},{5,1},{8,4},{9,5},{12,8},{13,9},{14,12},{15,13},... | collective-permute-start | bytes 798728 | tf_op jit(solution)/shard_map/ppermute | solution.py:340
  34.5 12.1 %collective-permute-start.18 = (s16[1040,128]{1,0:T(8,128)(2,1)S(1)}, s16[1040,128]{1,0:T(8,128)(2,1)S(1)}, u32[]{:S(2)}, u32[]{:S(2)}) collective-permute-start(s16[1040,128]{1,0:T(8,128)(2,1)S(1)} %sum_hop.20.before_ref), channel_id=1, source_target_pairs={{0,4},{1,5},{4,8},{5,9},{8,12},{9,13},{12,14},{13,15},{14,10},{15,... | collective-permute-start | bytes 798728 | tf_op jit(solution)/shard_map/ppermute | solution.py:340
  36.1 10.6 %collective-permute-start.19 = (s16[1040,128]{1,0:T(8,128)(2,1)S(1)}, s16[1040,128]{1,0:T(8,128)(2,1)S(1)}, u32[]{:S(2)}, u32[]{:S(2)}) collective-permute-start(s16[1040,128]{1,0:T(8,128)(2,1)S(1)} %sum_hop.21.before_ref), channel_id=1, source_target_pairs={{0,2},{1,3},{4,0},{5,1},{8,4},{9,5},{12,8},{13,9},{14,12},{15,13},... | collective-permute-start | bytes 798728 | tf_op jit(solution)/shard_map/ppermute | solution.py:340
  40.2 12.1 %collective-permute-start.20 = (s16[1040,128]{1,0:T(8,128)(2,1)S(1)}, s16[1040,128]{1,0:T(8,128)(2,1)S(1)}, u32[]{:S(2)}, u32[]{:S(2)}) collective-permute-start(s16[1040,128]{1,0:T(8,128)(2,1)S(1)} %sum_hop.22.before_ref), channel_id=1, source_target_pairs={{0,4},{1,5},{4,8},{5,9},{8,12},{9,13},{12,14},{13,15},{14,10},{15,... | collective-permute-start | bytes 798728 | tf_op jit(solution)/shard_map/ppermute | solution.py:340
  41.8 10.5 %collective-permute-start.21 = (s16[1040,128]{1,0:T(8,128)(2,1)S(1)}, s16[1040,128]{1,0:T(8,128)(2,1)S(1)}, u32[]{:S(2)}, u32[]{:S(2)}) collective-permute-start(s16[1040,128]{1,0:T(8,128)(2,1)S(1)} %sum_hop.23.before_ref), channel_id=1, source_target_pairs={{0,2},{1,3},{4,0},{5,1},{8,4},{9,5},{12,8},{13,9},{14,12},{15,13},... | collective-permute-start | bytes 798728 | tf_op jit(solution)/shard_map/ppermute | solution.py:340
  47.1 9.6 %collective-permute-start.22 = (bf16[512,256]{1,0:T(8,128)(2,1)S(1)}, bf16[512,256]{1,0:T(8,128)(2,1)S(1)}, u32[]{:S(2)}, u32[]{:S(2)}) collective-permute-start(bf16[512,256]{1,0:T(8,128)(2,1)S(1)} %effect.2.before_ref.refs_0_), channel_id=1, source_target_pairs={{0,4},{1,5},{4,8},{5,9},{8,12},{9,13},{12,14},{13,15},{14,10},{15,... | collective-permute-start | bytes 786440 | tf_op jit(solution)/shard_map/ppermute | solution.py:441
  48.8 9.6 %collective-permute-start.23 = (bf16[512,256]{1,0:T(8,128)(2,1)S(1)}, bf16[512,256]{1,0:T(8,128)(2,1)S(1)}, u32[]{:S(2)}, u32[]{:S(2)}) collective-permute-start(bf16[512,256]{1,0:T(8,128)(2,1)S(1)} %effect.2.before_ref.refs_0_), channel_id=1, source_target_pairs={{0,2},{1,3},{4,0},{5,1},{8,4},{9,5},{12,8},{13,9},{14,12},{15,13},... | collective-permute-start | bytes 786440 | tf_op jit(solution)/shard_map/ppermute | solution.py:441
  52.7 9.6 %collective-permute-start.24 = (bf16[512,256]{1,0:T(8,128)(2,1)S(1)}, bf16[512,256]{1,0:T(8,128)(2,1)S(1)}, u32[]{:S(2)}, u32[]{:S(2)}) collective-permute-start(bf16[512,256]{1,0:T(8,128)(2,1)S(1)} %effect.3.before_ref.refs_3_), channel_id=1, source_target_pairs={{0,4},{1,5},{4,8},{5,9},{8,12},{9,13},{12,14},{13,15},{14,10},{15,... | collective-permute-start | bytes 786440 | tf_op jit(solution)/shard_map/ppermute | solution.py:441
  54.4 9.6 %collective-permute-start.25 = (bf16[512,256]{1,0:T(8,128)(2,1)S(1)}, bf16[512,256]{1,0:T(8,128)(2,1)S(1)}, u32[]{:S(2)}, u32[]{:S(2)}) collective-permute-start(bf16[512,256]{1,0:T(8,128)(2,1)S(1)} %effect.3.before_ref.refs_3_), channel_id=1, source_target_pairs={{0,2},{1,3},{4,0},{5,1},{8,4},{9,5},{12,8},{13,9},{14,12},{15,13},... | collective-permute-start | bytes 786440 | tf_op jit(solution)/shard_map/ppermute | solution.py:441
  56.7 11.2 %collective-permute-start.26 = (bf16[512,256]{1,0:T(8,128)(2,1)S(1)}, bf16[512,256]{1,0:T(8,128)(2,1)S(1)}, u32[]{:S(2)}, u32[]{:S(2)}) collective-permute-start(bf16[512,256]{1,0:T(8,128)(2,1)S(1)} %collective-permute-done.22.refs_0_), channel_id=1, source_target_pairs={{0,4},{1,5},{4,8},{5,9},{8,12},{9,13},{12,14},{13,15},{14,10},{15,... | collective-permute-start | bytes 786440 | tf_op jit(solution)/shard_map/ppermute | solution.py:441
  58.4 11.2 %collective-permute-start.27 = (bf16[512,256]{1,0:T(8,128)(2,1)S(1)}, bf16[512,256]{1,0:T(8,128)(2,1)S(1)}, u32[]{:S(2)}, u32[]{:S(2)}) collective-permute-start(bf16[512,256]{1,0:T(8,128)(2,1)S(1)} %collective-permute-done.23.refs_0_), channel_id=1, source_target_pairs={{0,2},{1,3},{4,0},{5,1},{8,4},{9,5},{12,8},{13,9},{14,12},{15,13},... | collective-permute-start | bytes 786440 | tf_op jit(solution)/shard_map/ppermute | solution.py:441
  62.3 11.2 %collective-permute-start.28 = (bf16[512,256]{1,0:T(8,128)(2,1)S(1)}, bf16[512,256]{1,0:T(8,128)(2,1)S(1)}, u32[]{:S(2)}, u32[]{:S(2)}) collective-permute-start(bf16[512,256]{1,0:T(8,128)(2,1)S(1)} %collective-permute-done.24.refs_0_), channel_id=1, source_target_pairs={{0,4},{1,5},{4,8},{5,9},{8,12},{9,13},{12,14},{13,15},{14,10},{15,... | collective-permute-start | bytes 786440 | tf_op jit(solution)/shard_map/ppermute | solution.py:441
  64.0 11.3 %collective-permute-start.29 = (bf16[512,256]{1,0:T(8,128)(2,1)S(1)}, bf16[512,256]{1,0:T(8,128)(2,1)S(1)}, u32[]{:S(2)}, u32[]{:S(2)}) collective-permute-start(bf16[512,256]{1,0:T(8,128)(2,1)S(1)} %collective-permute-done.25.refs_0_), channel_id=1, source_target_pairs={{0,2},{1,3},{4,0},{5,1},{8,4},{9,5},{12,8},{13,9},{14,12},{15,13},... | collective-permute-start | bytes 786440 | tf_op jit(solution)/shard_map/ppermute | solution.py:441
  67.9 11.3 %collective-permute-start.30 = (bf16[512,256]{1,0:T(8,128)(2,1)S(1)}, bf16[512,256]{1,0:T(8,128)(2,1)S(1)}, u32[]{:S(2)}, u32[]{:S(2)}) collective-permute-start(bf16[512,256]{1,0:T(8,128)(2,1)S(1)} %collective-permute-done.26.refs_0_), channel_id=1, source_target_pairs={{0,4},{1,5},{4,8},{5,9},{8,12},{9,13},{12,14},{13,15},{14,10},{15,... | collective-permute-start | bytes 786440 | tf_op jit(solution)/shard_map/ppermute | solution.py:441
  69.6 11.2 %collective-permute-start.31 = (bf16[512,256]{1,0:T(8,128)(2,1)S(1)}, bf16[512,256]{1,0:T(8,128)(2,1)S(1)}, u32[]{:S(2)}, u32[]{:S(2)}) collective-permute-start(bf16[512,256]{1,0:T(8,128)(2,1)S(1)} %collective-permute-done.27.refs_0_), channel_id=1, source_target_pairs={{0,2},{1,3},{4,0},{5,1},{8,4},{9,5},{12,8},{13,9},{14,12},{15,13},... | collective-permute-start | bytes 786440 | tf_op jit(solution)/shard_map/ppermute | solution.py:441
  73.5 10.5 %collective-permute-start.32 = (bf16[256,256]{1,0:T(8,128)(2,1)S(1)}, bf16[256,256]{1,0:T(8,128)(2,1)S(1)}, u32[]{:S(2)}, u32[]{:S(2)}) collective-permute-start(bf16[256,256]{1,0:T(8,128)(2,1)S(1)} %slice.24), channel_id=1, source_target_pairs={{0,4},{1,5},{4,8},{5,9},{8,12},{9,13},{12,14},{13,15},{14,10},{15,... | collective-permute-start | bytes 393224 | tf_op jit(solution)/shard_map/ppermute | solution.py:435
  75.7 7.6 %collective-permute-start.34 = (bf16[256,256]{1,0:T(8,128)(2,1)S(1)}, bf16[256,256]{1,0:T(8,128)(2,1)S(1)}, u32[]{:S(2)}, u32[]{:S(2)}) collective-permute-start(bf16[256,256]{1,0:T(8,128)(2,1)S(1)} %slice.26), channel_id=1, source_target_pairs={{0,2},{1,3},{4,0},{5,1},{8,4},{9,5},{12,8},{13,9},{14,12},{15,13},... | collective-permute-start | bytes 393224 | tf_op jit(solution)/shard_map/ppermute | solution.py:435
  76.5 11.1 %collective-permute-start.35 = (bf16[256,256]{1,0:T(8,128)(2,1)S(1)}, bf16[256,256]{1,0:T(8,128)(2,1)S(1)}, u32[]{:S(2)}, u32[]{:S(2)}) collective-permute-start(bf16[256,256]{1,0:T(8,128)(2,1)S(1)} %slice.27), channel_id=1, source_target_pairs={{0,2},{1,3},{4,0},{5,1},{8,4},{9,5},{12,8},{13,9},{14,12},{15,13},... | collective-permute-start | bytes 393224 | tf_op jit(solution)/shard_map/ppermute | solution.py:438
  79.2 6.6 %collective-permute-start.33 = (bf16[256,256]{1,0:T(8,128)(2,1)S(1)}, bf16[256,256]{1,0:T(8,128)(2,1)S(1)}, u32[]{:S(2)}, u32[]{:S(2)}) collective-permute-start(bf16[256,256]{1,0:T(8,128)(2,1)S(1)} %slice.25), channel_id=1, source_target_pairs={{0,4},{1,5},{4,8},{5,9},{8,12},{9,13},{12,14},{13,15},{14,10},{15,... | collective-permute-start | bytes 393224 | tf_op jit(solution)/shard_map/ppermute | solution.py:438
  80.9 7.3 %collective-permute-start.36 = (bf16[256,256]{1,0:T(8,128)(2,1)S(1)}, bf16[256,256]{1,0:T(8,128)(2,1)S(1)}, u32[]{:S(2)}, u32[]{:S(2)}) collective-permute-start(bf16[256,256]{1,0:T(8,128)(2,1)S(1)} %slice.28), channel_id=1, source_target_pairs={{0,4},{1,5},{4,8},{5,9},{8,12},{9,13},{12,14},{13,15},{14,10},{15,... | collective-permute-start | bytes 393224 | tf_op jit(solution)/shard_map/ppermute | solution.py:430
  (22 other events, 87.4 us)

commit v16 on v15

--- a/solution.py
+++ b/solution.py
@@ -446,9 +446,9 @@
                 eta = product(found, eta, last, small if len(etas) == 1 or (hop, piece) >= (reach - 1, pieces - 1) else light)
                 last = eta[0]
                 etas.append(last)
-        if updated < pieces and hop < reach:
-            *outs, last = update(updated, outs, last)
-            updated += 1
+            if updated < pieces and hop < reach and piece == (pieces - 1 if hop == 1 else 0):
+                *outs, last = update(updated, outs, last)
+                updated += 1
     while updated < pieces:
         *outs, last = update(updated, outs, last)
         updated += 1

time: 93.5 us -> 93.5 us (level)
  no operation moved by 1% of the time
where the time goes in v16:
time: 93.5 us; the launch traced here: 93.3 us
  starting transfers between devices  40.5 us (43%)
  waiting for transfers between devices  29.3 us (31%)
  Pallas kernels  22.2 us (24%)
  between operations  1.22 us (1%)
    ppermute x12, waiting for transfers between devices, on_device(): got[way, piece] = lax.ppermute(last, 'ind', left if way else right)  16 us
    ppermute x14, starting transfers between devices, on_device(): held[way, piece] = lax.ppermute(message, 'ind', perm)  15.3 us
    ppermute x12, starting transfers between devices, on_device(): got[way, piece] = lax.ppermute(last, 'ind', left if way else right)  13.2 us
    ppermute x14, waiting for transfers between devices, on_device(): held[way, piece] = lax.ppermute(message, 'ind', perm)  10.1 us
    pallas_call x12, Pallas kernels, on_device(): pl.pallas_call(functools.partial(hop_kernel, ring, (w, peer[w][1]), low,...  6.62 us
    pallas_call x15, Pallas kernels, product(): pl.pallas_call(functools.partial(eta_kernel, ring, places, not eta), in_s...  5.57 us
    pallas_call x4, Pallas kernels, pick(): pl.pallas_call(functools.partial(pick_kernel, ring, wanted, block), in_sp...  3.25 us
    ppermute x2, starting transfers between devices, on_device(): got[0, piece] = lax.ppermute(sent[0], 'ind', right)  3.19 us
  transfers between devices with their start and end apart: 44, of which 18 were waited for; matrix products, arithmetic and copies ran while one was open for 0% of the time, Pallas kernels for 21%

profile of v16, /device:TPU:0, one launch (start us, length us, event | category | flops | bytes accessed | tf_op | source)
XLA Modules:
  0.0 93.3 jit_solution(5740542957765587538)
XLA Ops:
  0.6 1.2 %pick_blocks.4 = (bf16[1,384,512]{2,1,0:T(8,128)(2,1)S(1)}, bf16[1,384,512]{2,1,0:T(8,128)(2,1)S(1)}) custom-call(bf16[384,16384]{1,0:T(8,128)(2,1)} %genotype_ref.13), custom_call_target="tpu_custom_call" | custom-call | flops 1 | bytes 1 | tf_op jit(solution)/shard_map/pick_blocks/pallas_call | solution.py:252
  2.5 1.7 %pick_blocks.5 = (bf16[1,384,512]{2,1,0:T(8,128)(2,1)S(1)}, bf16[1,384,512]{2,1,0:T(8,128)(2,1)S(1)}, bf16[2,384,1024]{2,1,0:T(8,128)(2,1)S(1)}) custom-call(bf16[384,16384]{1,0:T(8,128)(2,1)} %genotype_ref.13, bf16[1,384,512]{2,1,0:T(8,128)(2,1)S(1)} %get-tuple-element.65.refs_0_), custom_call_target="tpu_custom_call" | custom-call | flops 10000000000 | bytes 1000000 | tf_op jit(solution)/shard_map/pick_blocks/pallas_call | solution.py:252
  5.4 3.0 %collective-permute-start.4 = (s16[528,128]{1,0:T(8,128)(2,1)S(1)}, s16[528,128]{1,0:T(8,128)(2,1)S(1)}, u32[]{:S(2)}, u32[]{:S(2)}) collective-permute-start(s16[528,128]{1,0:T(8,128)(2,1)S(1)} %get-tuple-element.69.before_ref), channel_id=1, source_target_pairs={{0,4},{1,5},{4,8},{5,9},{8,12},{9,13},{12,14},{13,15},{14,10},{15,... | collective-permute-start | bytes 405512 | tf_op jit(solution)/shard_map/ppermute | solution.py:322
  9.0 2.0 %collective-permute-start.8 = (s16[528,128]{1,0:T(8,128)(2,1)S(1)}, s16[528,128]{1,0:T(8,128)(2,1)S(1)}, u32[]{:S(2)}, u32[]{:S(2)}) collective-permute-start(s16[528,128]{1,0:T(8,128)(2,1)S(1)} %get-tuple-element.76), channel_id=1, source_target_pairs={{0,2},{1,3},{4,0},{5,1},{8,4},{9,5},{12,8},{13,9},{14,12},{15,13},... | collective-permute-start | bytes 405512 | tf_op jit(solution)/shard_map/ppermute | solution.py:323
  12.9 2.5 %collective-permute-start.9 = (s16[1040,128]{1,0:T(8,128)(2,1)S(1)}, s16[1040,128]{1,0:T(8,128)(2,1)S(1)}, u32[]{:S(2)}, u32[]{:S(2)}) collective-permute-start(s16[1040,128]{1,0:T(8,128)(2,1)S(1)} %sum_hop.12.before_ref), channel_id=1, source_target_pairs={{0,4},{1,5},{4,8},{5,9},{8,12},{9,13},{12,14},{13,15},{14,10},{15,... | collective-permute-start | bytes 798728 | tf_op jit(solution)/shard_map/ppermute | solution.py:340
  17.4 1.6 %collective-permute-start.11 = (s16[1040,128]{1,0:T(8,128)(2,1)S(1)}, s16[1040,128]{1,0:T(8,128)(2,1)S(1)}, u32[]{:S(2)}, u32[]{:S(2)}) collective-permute-start(s16[1040,128]{1,0:T(8,128)(2,1)S(1)} %sum_hop.14.before_ref), channel_id=1, source_target_pairs={{0,4},{1,5},{4,8},{5,9},{8,12},{9,13},{12,14},{13,15},{14,10},{15,... | collective-permute-start | bytes 798728 | tf_op jit(solution)/shard_map/ppermute | solution.py:340
  20.1 2.5 %collective-permute-done.9.got_ref = s16[1040,128]{1,0:T(8,128)(2,1)S(1)} collective-permute-done((s16[1040,128]{1,0:T(8,128)(2,1)S(1)}, s16[1040,128]{1,0:T(8,128)(2,1)S(1)}, u32[]{:S(2)}, u32[]{:S(2)}) %collective-permute-start.9) | collective-permute-done | bytes 266272 | tf_op jit(solution)/shard_map/ppermute | solution.py:340
  24.7 1.1 %collective-permute-start.15 = (s16[1040,128]{1,0:T(8,128)(2,1)S(1)}, s16[1040,128]{1,0:T(8,128)(2,1)S(1)}, u32[]{:S(2)}, u32[]{:S(2)}) collective-permute-start(s16[1040,128]{1,0:T(8,128)(2,1)S(1)} %sum_hop.17.before_ref), channel_id=1, source_target_pairs={{0,2},{1,3},{4,0},{5,1},{8,4},{9,5},{12,8},{13,9},{14,12},{15,13},... | collective-permute-start | bytes 798728 | tf_op jit(solution)/shard_map/ppermute | solution.py:340
  25.8 2.4 %collective-permute-done.11.got_ref = s16[1040,128]{1,0:T(8,128)(2,1)S(1)} collective-permute-done((s16[1040,128]{1,0:T(8,128)(2,1)S(1)}, s16[1040,128]{1,0:T(8,128)(2,1)S(1)}, u32[]{:S(2)}, u32[]{:S(2)}) %collective-permute-start.11) | collective-permute-done | bytes 266272 | tf_op jit(solution)/shard_map/ppermute | solution.py:340
  30.4 1.1 %collective-permute-start.17 = (s16[1040,128]{1,0:T(8,128)(2,1)S(1)}, s16[1040,128]{1,0:T(8,128)(2,1)S(1)}, u32[]{:S(2)}, u32[]{:S(2)}) collective-permute-start(s16[1040,128]{1,0:T(8,128)(2,1)S(1)} %sum_hop.19.before_ref), channel_id=1, source_target_pairs={{0,2},{1,3},{4,0},{5,1},{8,4},{9,5},{12,8},{13,9},{14,12},{15,13},... | collective-permute-start | bytes 798728 | tf_op jit(solution)/shard_map/ppermute | solution.py:340
  31.5 2.4 %collective-permute-done.14.got_ref = s16[1040,128]{1,0:T(8,128)(2,1)S(1)} collective-permute-done((s16[1040,128]{1,0:T(8,128)(2,1)S(1)}, s16[1040,128]{1,0:T(8,128)(2,1)S(1)}, u32[]{:S(2)}, u32[]{:S(2)}) %collective-permute-start.14) | collective-permute-done | bytes 266272 | tf_op jit(solution)/shard_map/ppermute | solution.py:340
  37.2 2.4 %collective-permute-done.16.got_ref = s16[1040,128]{1,0:T(8,128)(2,1)S(1)} collective-permute-done((s16[1040,128]{1,0:T(8,128)(2,1)S(1)}, s16[1040,128]{1,0:T(8,128)(2,1)S(1)}, u32[]{:S(2)}, u32[]{:S(2)}) %collective-permute-start.16) | collective-permute-done | bytes 266272 | tf_op jit(solution)/shard_map/ppermute | solution.py:340
  43.7 3.0 %collective-permute-done.19.refs_2_ = s16[1040,128]{1,0:T(8,128)(2,1)S(1)} collective-permute-done((s16[1040,128]{1,0:T(8,128)(2,1)S(1)}, s16[1040,128]{1,0:T(8,128)(2,1)S(1)}, u32[]{:S(2)}, u32[]{:S(2)}) %collective-permute-start.19) | collective-permute-done | bytes 266272 | tf_op jit(solution)/shard_map/ppermute | solution.py:340
  47.1 1.7 %collective-permute-start.22 = (bf16[512,256]{1,0:T(8,128)(2,1)S(1)}, bf16[512,256]{1,0:T(8,128)(2,1)S(1)}, u32[]{:S(2)}, u32[]{:S(2)}) collective-permute-start(bf16[512,256]{1,0:T(8,128)(2,1)S(1)} %effect.2.before_ref.refs_0_), channel_id=1, source_target_pairs={{0,4},{1,5},{4,8},{5,9},{8,12},{9,13},{12,14},{13,15},{14,10},{15,... | collective-permute-start | bytes 786440 | tf_op jit(solution)/shard_map/ppermute | solution.py:441
  49.1 3.2 %collective-permute-done.21.refs_2_ = s16[1040,128]{1,0:T(8,128)(2,1)S(1)} collective-permute-done((s16[1040,128]{1,0:T(8,128)(2,1)S(1)}, s16[1040,128]{1,0:T(8,128)(2,1)S(1)}, u32[]{:S(2)}, u32[]{:S(2)}) %collective-permute-start.21) | collective-permute-done | bytes 266272 | tf_op jit(solution)/shard_map/ppermute | solution.py:340
  52.7 1.7 %collective-permute-start.24 = (bf16[512,256]{1,0:T(8,128)(2,1)S(1)}, bf16[512,256]{1,0:T(8,128)(2,1)S(1)}, u32[]{:S(2)}, u32[]{:S(2)}) collective-permute-start(bf16[512,256]{1,0:T(8,128)(2,1)S(1)} %effect.3.before_ref.refs_3_), channel_id=1, source_target_pairs={{0,4},{1,5},{4,8},{5,9},{8,12},{9,13},{12,14},{13,15},{14,10},{15,... | collective-permute-start | bytes 786440 | tf_op jit(solution)/shard_map/ppermute | solution.py:441
  55.4 1.3 %collective-permute-done.22.refs_0_ = bf16[512,256]{1,0:T(8,128)(2,1)S(1)} collective-permute-done((bf16[512,256]{1,0:T(8,128)(2,1)S(1)}, bf16[512,256]{1,0:T(8,128)(2,1)S(1)}, u32[]{:S(2)}, u32[]{:S(2)}) %collective-permute-start.22) | collective-permute-done | bytes 262176 | tf_op jit(solution)/shard_map/ppermute | solution.py:441
  56.7 1.3 %collective-permute-start.26 = (bf16[512,256]{1,0:T(8,128)(2,1)S(1)}, bf16[512,256]{1,0:T(8,128)(2,1)S(1)}, u32[]{:S(2)}, u32[]{:S(2)}) collective-permute-start(bf16[512,256]{1,0:T(8,128)(2,1)S(1)} %collective-permute-done.22.refs_0_), channel_id=1, source_target_pairs={{0,4},{1,5},{4,8},{5,9},{8,12},{9,13},{12,14},{13,15},{14,10},{15,... | collective-permute-start | bytes 786440 | tf_op jit(solution)/shard_map/ppermute | solution.py:441
  59.5 2.8 %collective-permute-done.24.refs_0_ = bf16[512,256]{1,0:T(8,128)(2,1)S(1)} collective-permute-done((bf16[512,256]{1,0:T(8,128)(2,1)S(1)}, bf16[512,256]{1,0:T(8,128)(2,1)S(1)}, u32[]{:S(2)}, u32[]{:S(2)}) %collective-permute-start.24) | collective-permute-done | bytes 262176 | tf_op jit(solution)/shard_map/ppermute | solution.py:441
  62.3 1.3 %collective-permute-start.28 = (bf16[512,256]{1,0:T(8,128)(2,1)S(1)}, bf16[512,256]{1,0:T(8,128)(2,1)S(1)}, u32[]{:S(2)}, u32[]{:S(2)}) collective-permute-start(bf16[512,256]{1,0:T(8,128)(2,1)S(1)} %collective-permute-done.24.refs_0_), channel_id=1, source_target_pairs={{0,4},{1,5},{4,8},{5,9},{8,12},{9,13},{12,14},{13,15},{14,10},{15,... | collective-permute-start | bytes 786440 | tf_op jit(solution)/shard_map/ppermute | solution.py:441
  65.1 1.3 %update.2 = (f32[1024,256]{1,0:T(8,128)}, f32[1024,256]{1,0:T(8,128)}, f32[8,128]{1,0:T(8,128)S(1)}) custom-call(f32[384,256]{1,0:T(8,128)S(1)} %get-tuple-element.85.before_ref.refs_3_, f32[256,1024]{1,0:T(8,128)S(1)} %sum_near.1.before_ref.refs_0_, s16[1040,128]{1,0:T(8,128)(2,1)S(1)} %collective-permute-done.18.refs_1_, ...), custom_call_target="tpu_custom_call" | custom-call | flops 1 | bytes 1 | tf_op jit(solution)/shard_map/update/pallas_call | solution.py:378
  66.5 1.5 %collective-permute-done.26.refs_0_ = bf16[512,256]{1,0:T(8,128)(2,1)S(1)} collective-permute-done((bf16[512,256]{1,0:T(8,128)(2,1)S(1)}, bf16[512,256]{1,0:T(8,128)(2,1)S(1)}, u32[]{:S(2)}, u32[]{:S(2)}) %collective-permute-start.26) | collective-permute-done | bytes 262176 | tf_op jit(solution)/shard_map/ppermute | solution.py:441
  67.9 1.3 %collective-permute-start.30 = (bf16[512,256]{1,0:T(8,128)(2,1)S(1)}, bf16[512,256]{1,0:T(8,128)(2,1)S(1)}, u32[]{:S(2)}, u32[]{:S(2)}) collective-permute-start(bf16[512,256]{1,0:T(8,128)(2,1)S(1)} %collective-permute-done.26.refs_0_), channel_id=1, source_target_pairs={{0,4},{1,5},{4,8},{5,9},{8,12},{9,13},{12,14},{13,15},{14,10},{15,... | collective-permute-start | bytes 786440 | tf_op jit(solution)/shard_map/ppermute | solution.py:441
  70.8 2.8 %collective-permute-done.28.refs_0_ = bf16[512,256]{1,0:T(8,128)(2,1)S(1)} collective-permute-done((bf16[512,256]{1,0:T(8,128)(2,1)S(1)}, bf16[512,256]{1,0:T(8,128)(2,1)S(1)}, u32[]{:S(2)}, u32[]{:S(2)}) %collective-permute-start.28) | collective-permute-done | bytes 262176 | tf_op jit(solution)/shard_map/ppermute | solution.py:441
  73.5 1.4 %collective-permute-start.32 = (bf16[256,256]{1,0:T(8,128)(2,1)S(1)}, bf16[256,256]{1,0:T(8,128)(2,1)S(1)}, u32[]{:S(2)}, u32[]{:S(2)}) collective-permute-start(bf16[256,256]{1,0:T(8,128)(2,1)S(1)} %slice.24), channel_id=1, source_target_pairs={{0,4},{1,5},{4,8},{5,9},{8,12},{9,13},{12,14},{13,15},{14,10},{15,... | collective-permute-start | bytes 393224 | tf_op jit(solution)/shard_map/ppermute | solution.py:435
  74.9 1.3 %update.3 = (f32[1024,256]{1,0:T(8,128)}, f32[1024,256]{1,0:T(8,128)}, f32[8,128]{1,0:T(8,128)S(1)}) custom-call(f32[384,256]{1,0:T(8,128)S(1)} %get-tuple-element.92.before_ref.refs_3_, f32[256,1024]{1,0:T(8,128)S(1)} %sum_near.1.before_ref.refs_0_, ...), custom_call_target="tpu_custom_call", output_to_operand_aliasing={{0}: (8, {}), {1}: (9, {})} | custom-call | flops 1 | bytes 1 | tf_op jit(solution)/shard_map/update/pallas_call | solution.py:378
  77.8 1.4 %collective-permute-start.35 = (bf16[256,256]{1,0:T(8,128)(2,1)S(1)}, bf16[256,256]{1,0:T(8,128)(2,1)S(1)}, u32[]{:S(2)}, u32[]{:S(2)}) collective-permute-start(bf16[256,256]{1,0:T(8,128)(2,1)S(1)} %slice.27), channel_id=1, source_target_pairs={{0,2},{1,3},{4,0},{5,1},{8,4},{9,5},{12,8},{13,9},{14,12},{15,13},... | collective-permute-start | bytes 393224 | tf_op jit(solution)/shard_map/ppermute | solution.py:438
  79.2 1.3 %collective-permute-start.33 = (bf16[256,256]{1,0:T(8,128)(2,1)S(1)}, bf16[256,256]{1,0:T(8,128)(2,1)S(1)}, u32[]{:S(2)}, u32[]{:S(2)}) collective-permute-start(bf16[256,256]{1,0:T(8,128)(2,1)S(1)} %slice.25), channel_id=1, source_target_pairs={{0,4},{1,5},{4,8},{5,9},{8,12},{9,13},{12,14},{13,15},{14,10},{15,... | collective-permute-start | bytes 393224 | tf_op jit(solution)/shard_map/ppermute | solution.py:438
  80.9 1.6 %collective-permute-start.36 = (bf16[256,256]{1,0:T(8,128)(2,1)S(1)}, bf16[256,256]{1,0:T(8,128)(2,1)S(1)}, u32[]{:S(2)}, u32[]{:S(2)}) collective-permute-start(bf16[256,256]{1,0:T(8,128)(2,1)S(1)} %slice.28), channel_id=1, source_target_pairs={{0,4},{1,5},{4,8},{5,9},{8,12},{9,13},{12,14},{13,15},{14,10},{15,... | collective-permute-start | bytes 393224 | tf_op jit(solution)/shard_map/ppermute | solution.py:430
  84.6 1.4 %collective-permute-start.38 = (bf16[256,256]{1,0:T(8,128)(2,1)S(1)}, bf16[256,256]{1,0:T(8,128)(2,1)S(1)}, u32[]{:S(2)}, u32[]{:S(2)}) collective-permute-start(bf16[256,256]{1,0:T(8,128)(2,1)S(1)} %collective-permute-done.32.refs_0_), channel_id=1, source_target_pairs={{0,4},{1,5},{4,8},{5,9},{8,12},{9,13},{12,14},{13,15},{14,10},{15,... | collective-permute-start | bytes 393224 | tf_op jit(solution)/shard_map/ppermute | solution.py:430
  86.0 1.2 %collective-permute-start.39 = (bf16[256,256]{1,0:T(8,128)(2,1)S(1)}, bf16[256,256]{1,0:T(8,128)(2,1)S(1)}, u32[]{:S(2)}, u32[]{:S(2)}) collective-permute-start(bf16[256,256]{1,0:T(8,128)(2,1)S(1)} %collective-permute-done.34.refs_0_), channel_id=1, source_target_pairs={{0,2},{1,3},{4,0},{5,1},{8,4},{9,5},{12,8},{13,9},{14,12},{15,13},... | collective-permute-start | bytes 393224 | tf_op jit(solution)/shard_map/ppermute | solution.py:430
  88.5 1.1 %collective-permute-done.37.refs_0_ = bf16[256,256]{1,0:T(8,128)(2,1)S(1)} collective-permute-done((bf16[256,256]{1,0:T(8,128)(2,1)S(1)}, bf16[256,256]{1,0:T(8,128)(2,1)S(1)}, u32[]{:S(2)}, u32[]{:S(2)}) %collective-permute-start.37) | collective-permute-done | bytes 131104 | tf_op jit(solution)/shard_map/ppermute | solution.py:430
  (126 shorter events, 34.2 us)
Async XLA Ops:
  4.6 6.6 %collective-permute-start.3 = (bf16[2,384,1024]{2,1,0:T(8,128)(2,1)S(1)}, bf16[2,384,1024]{2,1,0:T(8,128)(2,1)S(1)}, u32[]{:S(2)}, u32[]{:S(2)}) collective-permute-start(bf16[2,384,1024]{2,1,0:T(8,128)(2,1)S(1)} %get-tuple-element.72), channel_id=1, source_target_pairs={{0,1},{1,0},{2,3},{3,2},{4,5},{5,4},{6,7},{7,6},{8,9},{9,8},{10,11... | collective-permute-start | bytes 4718600 | tf_op jit(solution)/shard_map/ppermute | solution.py:273
  5.4 6.9 %collective-permute-start.4 = (s16[528,128]{1,0:T(8,128)(2,1)S(1)}, s16[528,128]{1,0:T(8,128)(2,1)S(1)}, u32[]{:S(2)}, u32[]{:S(2)}) collective-permute-start(s16[528,128]{1,0:T(8,128)(2,1)S(1)} %get-tuple-element.69.before_ref), channel_id=1, source_target_pairs={{0,4},{1,5},{4,8},{5,9},{8,12},{9,13},{12,14},{13,15},{14,10},{15,... | collective-permute-start | bytes 405512 | tf_op jit(solution)/shard_map/ppermute | solution.py:322
  8.5 6.9 %collective-permute-start.5 = (s16[528,128]{1,0:T(8,128)(2,1)S(1)}, s16[528,128]{1,0:T(8,128)(2,1)S(1)}, u32[]{:S(2)}, u32[]{:S(2)}) collective-permute-start(s16[528,128]{1,0:T(8,128)(2,1)S(1)} %get-tuple-element.74), channel_id=1, source_target_pairs={{0,2},{1,3},{4,0},{5,1},{8,4},{9,5},{12,8},{13,9},{14,12},{15,13},... | collective-permute-start | bytes 405512 | tf_op jit(solution)/shard_map/ppermute | solution.py:323
  9.0 10.0 %collective-permute-start.8 = (s16[528,128]{1,0:T(8,128)(2,1)S(1)}, s16[528,128]{1,0:T(8,128)(2,1)S(1)}, u32[]{:S(2)}, u32[]{:S(2)}) collective-permute-start(s16[528,128]{1,0:T(8,128)(2,1)S(1)} %get-tuple-element.76), channel_id=1, source_target_pairs={{0,2},{1,3},{4,0},{5,1},{8,4},{9,5},{12,8},{13,9},{14,12},{15,13},... | collective-permute-start | bytes 405512 | tf_op jit(solution)/shard_map/ppermute | solution.py:323
  12.9 9.6 %collective-permute-start.9 = (s16[1040,128]{1,0:T(8,128)(2,1)S(1)}, s16[1040,128]{1,0:T(8,128)(2,1)S(1)}, u32[]{:S(2)}, u32[]{:S(2)}) collective-permute-start(s16[1040,128]{1,0:T(8,128)(2,1)S(1)} %sum_hop.12.before_ref), channel_id=1, source_target_pairs={{0,4},{1,5},{4,8},{5,9},{8,12},{9,13},{12,14},{13,15},{14,10},{15,... | collective-permute-start | bytes 798728 | tf_op jit(solution)/shard_map/ppermute | solution.py:340
  16.0 8.1 %collective-permute-start.10 = (s16[1040,128]{1,0:T(8,128)(2,1)S(1)}, s16[1040,128]{1,0:T(8,128)(2,1)S(1)}, u32[]{:S(2)}, u32[]{:S(2)}) collective-permute-start(s16[1040,128]{1,0:T(8,128)(2,1)S(1)} %sum_hop.13.refs_0_), channel_id=1, source_target_pairs={{0,2},{1,3},{4,0},{5,1},{8,4},{9,5},{12,8},{13,9},{14,12},{15,13},... | collective-permute-start | bytes 798728 | tf_op jit(solution)/shard_map/ppermute | solution.py:340
  16.3 17.7 %collective-permute-start.13 = (bf16[3,384,1024]{2,1,0:T(8,128)(2,1)S(1)}, bf16[3,384,1024]{2,1,0:T(8,128)(2,1)S(1)}, u32[]{:S(2)}, u32[]{:S(2)}) collective-permute-start(bf16[3,384,1024]{2,1,0:T(8,128)(2,1)S(1)} %pick_blocks.7.before_ref), channel_id=1, source_target_pairs={{0,1},{1,0},{2,3},{3,2},{4,5},{5,4},{6,7},{7,6},{8,9},{9,8},{10,11... | collective-permute-start | bytes 7077896 | tf_op jit(solution)/shard_map/ppermute | solution.py:273
  17.4 10.9 %collective-permute-start.11 = (s16[1040,128]{1,0:T(8,128)(2,1)S(1)}, s16[1040,128]{1,0:T(8,128)(2,1)S(1)}, u32[]{:S(2)}, u32[]{:S(2)}) collective-permute-start(s16[1040,128]{1,0:T(8,128)(2,1)S(1)} %sum_hop.14.before_ref), channel_id=1, source_target_pairs={{0,4},{1,5},{4,8},{5,9},{8,12},{9,13},{12,14},{13,15},{14,10},{15,... | collective-permute-start | bytes 798728 | tf_op jit(solution)/shard_map/ppermute | solution.py:340
  19.5 10.3 %collective-permute-start.12 = (s16[1040,128]{1,0:T(8,128)(2,1)S(1)}, s16[1040,128]{1,0:T(8,128)(2,1)S(1)}, u32[]{:S(2)}, u32[]{:S(2)}) collective-permute-start(s16[1040,128]{1,0:T(8,128)(2,1)S(1)} %sum_hop.15.before_ref), channel_id=1, source_target_pairs={{0,2},{1,3},{4,0},{5,1},{8,4},{9,5},{12,8},{13,9},{14,12},{15,13},... | collective-permute-start | bytes 798728 | tf_op jit(solution)/shard_map/ppermute | solution.py:340
  23.1 10.9 %collective-permute-start.14 = (s16[1040,128]{1,0:T(8,128)(2,1)S(1)}, s16[1040,128]{1,0:T(8,128)(2,1)S(1)}, u32[]{:S(2)}, u32[]{:S(2)}) collective-permute-start(s16[1040,128]{1,0:T(8,128)(2,1)S(1)} %sum_hop.16.before_ref), channel_id=1, source_target_pairs={{0,4},{1,5},{4,8},{5,9},{8,12},{9,13},{12,14},{13,15},{14,10},{15,... | collective-permute-start | bytes 798728 | tf_op jit(solution)/shard_map/ppermute | solution.py:340
  24.7 10.9 %collective-permute-start.15 = (s16[1040,128]{1,0:T(8,128)(2,1)S(1)}, s16[1040,128]{1,0:T(8,128)(2,1)S(1)}, u32[]{:S(2)}, u32[]{:S(2)}) collective-permute-start(s16[1040,128]{1,0:T(8,128)(2,1)S(1)} %sum_hop.17.before_ref), channel_id=1, source_target_pairs={{0,2},{1,3},{4,0},{5,1},{8,4},{9,5},{12,8},{13,9},{14,12},{15,13},... | collective-permute-start | bytes 798728 | tf_op jit(solution)/shard_map/ppermute | solution.py:340
  28.8 10.8 %collective-permute-start.16 = (s16[1040,128]{1,0:T(8,128)(2,1)S(1)}, s16[1040,128]{1,0:T(8,128)(2,1)S(1)}, u32[]{:S(2)}, u32[]{:S(2)}) collective-permute-start(s16[1040,128]{1,0:T(8,128)(2,1)S(1)} %sum_hop.18.before_ref), channel_id=1, source_target_pairs={{0,4},{1,5},{4,8},{5,9},{8,12},{9,13},{12,14},{13,15},{14,10},{15,... | collective-permute-start | bytes 798728 | tf_op jit(solution)/shard_map/ppermute | solution.py:340
  30.4 10.8 %collective-permute-start.17 = (s16[1040,128]{1,0:T(8,128)(2,1)S(1)}, s16[1040,128]{1,0:T(8,128)(2,1)S(1)}, u32[]{:S(2)}, u32[]{:S(2)}) collective-permute-start(s16[1040,128]{1,0:T(8,128)(2,1)S(1)} %sum_hop.19.before_ref), channel_id=1, source_target_pairs={{0,2},{1,3},{4,0},{5,1},{8,4},{9,5},{12,8},{13,9},{14,12},{15,13},... | collective-permute-start | bytes 798728 | tf_op jit(solution)/shard_map/ppermute | solution.py:340
  34.5 12.1 %collective-permute-start.18 = (s16[1040,128]{1,0:T(8,128)(2,1)S(1)}, s16[1040,128]{1,0:T(8,128)(2,1)S(1)}, u32[]{:S(2)}, u32[]{:S(2)}) collective-permute-start(s16[1040,128]{1,0:T(8,128)(2,1)S(1)} %sum_hop.20.before_ref), channel_id=1, source_target_pairs={{0,4},{1,5},{4,8},{5,9},{8,12},{9,13},{12,14},{13,15},{14,10},{15,... | collective-permute-start | bytes 798728 | tf_op jit(solution)/shard_map/ppermute | solution.py:340
  36.1 10.6 %collective-permute-start.19 = (s16[1040,128]{1,0:T(8,128)(2,1)S(1)}, s16[1040,128]{1,0:T(8,128)(2,1)S(1)}, u32[]{:S(2)}, u32[]{:S(2)}) collective-permute-start(s16[1040,128]{1,0:T(8,128)(2,1)S(1)} %sum_hop.21.before_ref), channel_id=1, source_target_pairs={{0,2},{1,3},{4,0},{5,1},{8,4},{9,5},{12,8},{13,9},{14,12},{15,13},... | collective-permute-start | bytes 798728 | tf_op jit(solution)/shard_map/ppermute | solution.py:340
  40.2 12.1 %collective-permute-start.20 = (s16[1040,128]{1,0:T(8,128)(2,1)S(1)}, s16[1040,128]{1,0:T(8,128)(2,1)S(1)}, u32[]{:S(2)}, u32[]{:S(2)}) collective-permute-start(s16[1040,128]{1,0:T(8,128)(2,1)S(1)} %sum_hop.22.before_ref), channel_id=1, source_target_pairs={{0,4},{1,5},{4,8},{5,9},{8,12},{9,13},{12,14},{13,15},{14,10},{15,... | collective-permute-start | bytes 798728 | tf_op jit(solution)/shard_map/ppermute | solution.py:340
  41.8 10.5 %collective-permute-start.21 = (s16[1040,128]{1,0:T(8,128)(2,1)S(1)}, s16[1040,128]{1,0:T(8,128)(2,1)S(1)}, u32[]{:S(2)}, u32[]{:S(2)}) collective-permute-start(s16[1040,128]{1,0:T(8,128)(2,1)S(1)} %sum_hop.23.before_ref), channel_id=1, source_target_pairs={{0,2},{1,3},{4,0},{5,1},{8,4},{9,5},{12,8},{13,9},{14,12},{15,13},... | collective-permute-start | bytes 798728 | tf_op jit(solution)/shard_map/ppermute | solution.py:340
  47.1 9.6 %collective-permute-start.22 = (bf16[512,256]{1,0:T(8,128)(2,1)S(1)}, bf16[512,256]{1,0:T(8,128)(2,1)S(1)}, u32[]{:S(2)}, u32[]{:S(2)}) collective-permute-start(bf16[512,256]{1,0:T(8,128)(2,1)S(1)} %effect.2.before_ref.refs_0_), channel_id=1, source_target_pairs={{0,4},{1,5},{4,8},{5,9},{8,12},{9,13},{12,14},{13,15},{14,10},{15,... | collective-permute-start | bytes 786440 | tf_op jit(solution)/shard_map/ppermute | solution.py:441
  48.8 9.6 %collective-permute-start.23 = (bf16[512,256]{1,0:T(8,128)(2,1)S(1)}, bf16[512,256]{1,0:T(8,128)(2,1)S(1)}, u32[]{:S(2)}, u32[]{:S(2)}) collective-permute-start(bf16[512,256]{1,0:T(8,128)(2,1)S(1)} %effect.2.before_ref.refs_0_), channel_id=1, source_target_pairs={{0,2},{1,3},{4,0},{5,1},{8,4},{9,5},{12,8},{13,9},{14,12},{15,13},... | collective-permute-start | bytes 786440 | tf_op jit(solution)/shard_map/ppermute | solution.py:441
  52.7 9.6 %collective-permute-start.24 = (bf16[512,256]{1,0:T(8,128)(2,1)S(1)}, bf16[512,256]{1,0:T(8,128)(2,1)S(1)}, u32[]{:S(2)}, u32[]{:S(2)}) collective-permute-start(bf16[512,256]{1,0:T(8,128)(2,1)S(1)} %effect.3.before_ref.refs_3_), channel_id=1, source_target_pairs={{0,4},{1,5},{4,8},{5,9},{8,12},{9,13},{12,14},{13,15},{14,10},{15,... | collective-permute-start | bytes 786440 | tf_op jit(solution)/shard_map/ppermute | solution.py:441
  54.4 9.6 %collective-permute-start.25 = (bf16[512,256]{1,0:T(8,128)(2,1)S(1)}, bf16[512,256]{1,0:T(8,128)(2,1)S(1)}, u32[]{:S(2)}, u32[]{:S(2)}) collective-permute-start(bf16[512,256]{1,0:T(8,128)(2,1)S(1)} %effect.3.before_ref.refs_3_), channel_id=1, source_target_pairs={{0,2},{1,3},{4,0},{5,1},{8,4},{9,5},{12,8},{13,9},{14,12},{15,13},... | collective-permute-start | bytes 786440 | tf_op jit(solution)/shard_map/ppermute | solution.py:441
  56.7 11.2 %collective-permute-start.26 = (bf16[512,256]{1,0:T(8,128)(2,1)S(1)}, bf16[512,256]{1,0:T(8,128)(2,1)S(1)}, u32[]{:S(2)}, u32[]{:S(2)}) collective-permute-start(bf16[512,256]{1,0:T(8,128)(2,1)S(1)} %collective-permute-done.22.refs_0_), channel_id=1, source_target_pairs={{0,4},{1,5},{4,8},{5,9},{8,12},{9,13},{12,14},{13,15},{14,10},{15,... | collective-permute-start | bytes 786440 | tf_op jit(solution)/shard_map/ppermute | solution.py:441
  58.4 11.2 %collective-permute-start.27 = (bf16[512,256]{1,0:T(8,128)(2,1)S(1)}, bf16[512,256]{1,0:T(8,128)(2,1)S(1)}, u32[]{:S(2)}, u32[]{:S(2)}) collective-permute-start(bf16[512,256]{1,0:T(8,128)(2,1)S(1)} %collective-permute-done.23.refs_0_), channel_id=1, source_target_pairs={{0,2},{1,3},{4,0},{5,1},{8,4},{9,5},{12,8},{13,9},{14,12},{15,13},... | collective-permute-start | bytes 786440 | tf_op jit(solution)/shard_map/ppermute | solution.py:441
  62.3 11.2 %collective-permute-start.28 = (bf16[512,256]{1,0:T(8,128)(2,1)S(1)}, bf16[512,256]{1,0:T(8,128)(2,1)S(1)}, u32[]{:S(2)}, u32[]{:S(2)}) collective-permute-start(bf16[512,256]{1,0:T(8,128)(2,1)S(1)} %collective-permute-done.24.refs_0_), channel_id=1, source_target_pairs={{0,4},{1,5},{4,8},{5,9},{8,12},{9,13},{12,14},{13,15},{14,10},{15,... | collective-permute-start | bytes 786440 | tf_op jit(solution)/shard_map/ppermute | solution.py:441
  64.0 12.6 %collective-permute-start.29 = (bf16[512,256]{1,0:T(8,128)(2,1)S(1)}, bf16[512,256]{1,0:T(8,128)(2,1)S(1)}, u32[]{:S(2)}, u32[]{:S(2)}) collective-permute-start(bf16[512,256]{1,0:T(8,128)(2,1)S(1)} %collective-permute-done.25.refs_0_), channel_id=1, source_target_pairs={{0,2},{1,3},{4,0},{5,1},{8,4},{9,5},{12,8},{13,9},{14,12},{15,13},... | collective-permute-start | bytes 786440 | tf_op jit(solution)/shard_map/ppermute | solution.py:441
  67.9 11.3 %collective-permute-start.30 = (bf16[512,256]{1,0:T(8,128)(2,1)S(1)}, bf16[512,256]{1,0:T(8,128)(2,1)S(1)}, u32[]{:S(2)}, u32[]{:S(2)}) collective-permute-start(bf16[512,256]{1,0:T(8,128)(2,1)S(1)} %collective-permute-done.26.refs_0_), channel_id=1, source_target_pairs={{0,4},{1,5},{4,8},{5,9},{8,12},{9,13},{12,14},{13,15},{14,10},{15,... | collective-permute-start | bytes 786440 | tf_op jit(solution)/shard_map/ppermute | solution.py:441
  69.6 11.2 %collective-permute-start.31 = (bf16[512,256]{1,0:T(8,128)(2,1)S(1)}, bf16[512,256]{1,0:T(8,128)(2,1)S(1)}, u32[]{:S(2)}, u32[]{:S(2)}) collective-permute-start(bf16[512,256]{1,0:T(8,128)(2,1)S(1)} %collective-permute-done.27.refs_0_), channel_id=1, source_target_pairs={{0,2},{1,3},{4,0},{5,1},{8,4},{9,5},{12,8},{13,9},{14,12},{15,13},... | collective-permute-start | bytes 786440 | tf_op jit(solution)/shard_map/ppermute | solution.py:441
  73.5 11.1 %collective-permute-start.32 = (bf16[256,256]{1,0:T(8,128)(2,1)S(1)}, bf16[256,256]{1,0:T(8,128)(2,1)S(1)}, u32[]{:S(2)}, u32[]{:S(2)}) collective-permute-start(bf16[256,256]{1,0:T(8,128)(2,1)S(1)} %slice.24), channel_id=1, source_target_pairs={{0,4},{1,5},{4,8},{5,9},{8,12},{9,13},{12,14},{13,15},{14,10},{15,... | collective-permute-start | bytes 393224 | tf_op jit(solution)/shard_map/ppermute | solution.py:435
  77.1 6.5 %collective-permute-start.34 = (bf16[256,256]{1,0:T(8,128)(2,1)S(1)}, bf16[256,256]{1,0:T(8,128)(2,1)S(1)}, u32[]{:S(2)}, u32[]{:S(2)}) collective-permute-start(bf16[256,256]{1,0:T(8,128)(2,1)S(1)} %slice.26), channel_id=1, source_target_pairs={{0,2},{1,3},{4,0},{5,1},{8,4},{9,5},{12,8},{13,9},{14,12},{15,13},... | collective-permute-start | bytes 393224 | tf_op jit(solution)/shard_map/ppermute | solution.py:435
  77.8 9.8 %collective-permute-start.35 = (bf16[256,256]{1,0:T(8,128)(2,1)S(1)}, bf16[256,256]{1,0:T(8,128)(2,1)S(1)}, u32[]{:S(2)}, u32[]{:S(2)}) collective-permute-start(bf16[256,256]{1,0:T(8,128)(2,1)S(1)} %slice.27), channel_id=1, source_target_pairs={{0,2},{1,3},{4,0},{5,1},{8,4},{9,5},{12,8},{13,9},{14,12},{15,13},... | collective-permute-start | bytes 393224 | tf_op jit(solution)/shard_map/ppermute | solution.py:438
  79.2 6.8 %collective-permute-start.33 = (bf16[256,256]{1,0:T(8,128)(2,1)S(1)}, bf16[256,256]{1,0:T(8,128)(2,1)S(1)}, u32[]{:S(2)}, u32[]{:S(2)}) collective-permute-start(bf16[256,256]{1,0:T(8,128)(2,1)S(1)} %slice.25), channel_id=1, source_target_pairs={{0,4},{1,5},{4,8},{5,9},{8,12},{9,13},{12,14},{13,15},{14,10},{15,... | collective-permute-start | bytes 393224 | tf_op jit(solution)/shard_map/ppermute | solution.py:438
  80.9 7.3 %collective-permute-start.36 = (bf16[256,256]{1,0:T(8,128)(2,1)S(1)}, bf16[256,256]{1,0:T(8,128)(2,1)S(1)}, u32[]{:S(2)}, u32[]{:S(2)}) collective-permute-start(bf16[256,256]{1,0:T(8,128)(2,1)S(1)} %slice.28), channel_id=1, source_target_pairs={{0,4},{1,5},{4,8},{5,9},{8,12},{9,13},{12,14},{13,15},{14,10},{15,... | collective-permute-start | bytes 393224 | tf_op jit(solution)/shard_map/ppermute | solution.py:430
  (22 other events, 86.4 us)

commit v17 on v15

--- a/solution.py
+++ b/solution.py
@@ -324,7 +324,7 @@
             else:
                 if d == reach - 1 > 1 and piece == pieces - 1:
                     last, _ = lax.optimization_barrier((last, peer[d - 1][0]))
-                for way in (0, 1):
+                for way in (1, 0):
                     w = size - d if way else d
                     args = (res, genotype, peer[w][0], got[way, piece])
                     last = pl.pallas_call(
@@ -342,7 +342,7 @@
                 if d == reach > 1:
                     last, _ = lax.optimization_barrier((last, peer[d - 1][0]))
                 distances = later.pop(0)
-                (last,) = pick(whole(distances), pltpu.VMEM, small, last)
+                (last,) = pick(whole(distances), pltpu.VMEM, light, last)
                 swapped(distances, last)
 
     near = last = pl.pallas_call(
@@ -416,7 +416,7 @@
     outs, updated, final = (), 0, []
     for hop in range(1, reach + 1):
         for piece in range(pieces):
-            for way in (0, 1):
+            for way in (1, 0):
                 message = held[way, piece]
                 perm = left if way else right
                 d, low = (hop if way else size - hop), piece * part

time: 93.5 us -> 93.4 us (level)
    ppermute x2, starting transfers between devices: 3.19 us -> 0.24 us  [on_device(): got[0, piece] = lax.ppermute(sent[0], 'ind', right)]
    ppermute x2, starting transfers between devices: 2.02 us -> 4.95 us  [on_device(): got[1, piece] = lax.ppermute(sent[1], 'ind', left)]
    ppermute x2, waiting for transfers between devices: 0.01 us -> 1.43 us  [on_device(): got[1, piece] = lax.ppermute(sent[1], 'ind', left)]
    ppermute x2, waiting for transfers between devices: 1.35 us -> 0.01 us  [on_device(): got[0, piece] = lax.ppermute(sent[0], 'ind', right)]
  transfers between devices with their start and end apart: 44 -> 44, of which waited for: 18 -> 16; matrix products, arithmetic and copies ran while one was open for 0% -> 0% of each run, Pallas kernels for 21% -> 21%
where the time goes in v17:
time: 93.4 us; the launch traced here: 93.3 us
  starting transfers between devices  40 us (43%)
  waiting for transfers between devices  29.8 us (32%)
  Pallas kernels  22.2 us (24%)
  between operations  1.23 us (1%)
    ppermute x12, waiting for transfers between devices, on_device(): got[way, piece] = lax.ppermute(last, 'ind', left if way else right)  16.2 us
    ppermute x14, starting transfers between devices, on_device(): held[way, piece] = lax.ppermute(message, 'ind', perm)  15 us
    ppermute x12, starting transfers between devices, on_device(): got[way, piece] = lax.ppermute(last, 'ind', left if way else right)  12.8 us
    ppermute x14, waiting for transfers between devices, on_device(): held[way, piece] = lax.ppermute(message, 'ind', perm)  10.4 us
    pallas_call x12, Pallas kernels, on_device(): pl.pallas_call(functools.partial(hop_kernel, ring, (w, peer[w][1]), low,...  6.61 us
    pallas_call x15, Pallas kernels, product(): pl.pallas_call(functools.partial(eta_kernel, ring, places, not eta), in_s...  5.6 us
    ppermute x2, starting transfers between devices, on_device(): got[1, piece] = lax.ppermute(sent[1], 'ind', left)  4.95 us
    pallas_call x4, Pallas kernels, pick(): pl.pallas_call(functools.partial(pick_kernel, ring, wanted, block), in_sp...  3.21 us
  transfers between devices with their start and end apart: 44, of which 16 were waited for; matrix products, arithmetic and copies ran while one was open for 0% of the time, Pallas kernels for 21%

profile of v17, /device:TPU:0, one launch (start us, length us, event | category | flops | bytes accessed | tf_op | source)
XLA Modules:
  0.0 93.3 jit_solution(1749601220929600989)
XLA Ops:
  2.5 1.7 %pick_blocks.5 = (bf16[1,384,512]{2,1,0:T(8,128)(2,1)S(1)}, bf16[1,384,512]{2,1,0:T(8,128)(2,1)S(1)}, bf16[2,384,1024]{2,1,0:T(8,128)(2,1)S(1)}) custom-call(bf16[384,16384]{1,0:T(8,128)(2,1)} %genotype_ref.13, bf16[1,384,512]{2,1,0:T(8,128)(2,1)S(1)} %get-tuple-element.65.refs_0_), custom_call_target="tpu_custom_call" | custom-call | flops 10000000000 | bytes 1000000 | tf_op jit(solution)/shard_map/pick_blocks/pallas_call | solution.py:252
  5.4 3.0 %collective-permute-start.4 = (s16[528,128]{1,0:T(8,128)(2,1)S(1)}, s16[528,128]{1,0:T(8,128)(2,1)S(1)}, u32[]{:S(2)}, u32[]{:S(2)}) collective-permute-start(s16[528,128]{1,0:T(8,128)(2,1)S(1)} %get-tuple-element.74), channel_id=1, source_target_pairs={{0,2},{1,3},{4,0},{5,1},{8,4},{9,5},{12,8},{13,9},{14,12},{15,13},... | collective-permute-start | bytes 405512 | tf_op jit(solution)/shard_map/ppermute | solution.py:323
  9.1 2.0 %collective-permute-start.7 = (s16[528,128]{1,0:T(8,128)(2,1)S(1)}, s16[528,128]{1,0:T(8,128)(2,1)S(1)}, u32[]{:S(2)}, u32[]{:S(2)}) collective-permute-start(s16[528,128]{1,0:T(8,128)(2,1)S(1)} %get-tuple-element.76), channel_id=1, source_target_pairs={{0,2},{1,3},{4,0},{5,1},{8,4},{9,5},{12,8},{13,9},{14,12},{15,13},... | collective-permute-start | bytes 405512 | tf_op jit(solution)/shard_map/ppermute | solution.py:323
  11.4 1.4 %collective-permute-done.4.got_ref = s16[528,128]{1,0:T(8,128)(2,1)S(1)} collective-permute-done((s16[528,128]{1,0:T(8,128)(2,1)S(1)}, s16[528,128]{1,0:T(8,128)(2,1)S(1)}, u32[]{:S(2)}, u32[]{:S(2)}) %collective-permute-start.4) | collective-permute-done | bytes 135200 | tf_op jit(solution)/shard_map/ppermute | solution.py:323
  13.4 2.0 %collective-permute-start.9 = (s16[1040,128]{1,0:T(8,128)(2,1)S(1)}, s16[1040,128]{1,0:T(8,128)(2,1)S(1)}, u32[]{:S(2)}, u32[]{:S(2)}) collective-permute-start(s16[1040,128]{1,0:T(8,128)(2,1)S(1)} %sum_hop.12.before_ref), channel_id=1, source_target_pairs={{0,2},{1,3},{4,0},{5,1},{8,4},{9,5},{12,8},{13,9},{14,12},{15,13},... | collective-permute-start | bytes 798728 | tf_op jit(solution)/shard_map/ppermute | solution.py:340
  17.0 2.0 %collective-permute-start.11 = (s16[1040,128]{1,0:T(8,128)(2,1)S(1)}, s16[1040,128]{1,0:T(8,128)(2,1)S(1)}, u32[]{:S(2)}, u32[]{:S(2)}) collective-permute-start(s16[1040,128]{1,0:T(8,128)(2,1)S(1)} %sum_hop.14.before_ref), channel_id=1, source_target_pairs={{0,2},{1,3},{4,0},{5,1},{8,4},{9,5},{12,8},{13,9},{14,12},{15,13},... | collective-permute-start | bytes 798728 | tf_op jit(solution)/shard_map/ppermute | solution.py:340
  19.7 1.9 %collective-permute-done.9.got_ref = s16[1040,128]{1,0:T(8,128)(2,1)S(1)} collective-permute-done((s16[1040,128]{1,0:T(8,128)(2,1)S(1)}, s16[1040,128]{1,0:T(8,128)(2,1)S(1)}, u32[]{:S(2)}, u32[]{:S(2)}) %collective-permute-start.9) | collective-permute-done | bytes 266272 | tf_op jit(solution)/shard_map/ppermute | solution.py:340
  22.2 1.7 %collective-permute-start.14 = (s16[1040,128]{1,0:T(8,128)(2,1)S(1)}, s16[1040,128]{1,0:T(8,128)(2,1)S(1)}, u32[]{:S(2)}, u32[]{:S(2)}) collective-permute-start(s16[1040,128]{1,0:T(8,128)(2,1)S(1)} %sum_hop.16.before_ref), channel_id=1, source_target_pairs={{0,2},{1,3},{4,0},{5,1},{8,4},{9,5},{12,8},{13,9},{14,12},{15,13},... | collective-permute-start | bytes 798728 | tf_op jit(solution)/shard_map/ppermute | solution.py:340
  24.9 2.5 %collective-permute-done.11.got_ref = s16[1040,128]{1,0:T(8,128)(2,1)S(1)} collective-permute-done((s16[1040,128]{1,0:T(8,128)(2,1)S(1)}, s16[1040,128]{1,0:T(8,128)(2,1)S(1)}, u32[]{:S(2)}, u32[]{:S(2)}) %collective-permute-start.11) | collective-permute-done | bytes 266272 | tf_op jit(solution)/shard_map/ppermute | solution.py:340
  27.9 1.7 %collective-permute-start.16 = (s16[1040,128]{1,0:T(8,128)(2,1)S(1)}, s16[1040,128]{1,0:T(8,128)(2,1)S(1)}, u32[]{:S(2)}, u32[]{:S(2)}) collective-permute-start(s16[1040,128]{1,0:T(8,128)(2,1)S(1)} %sum_hop.18.before_ref), channel_id=1, source_target_pairs={{0,2},{1,3},{4,0},{5,1},{8,4},{9,5},{12,8},{13,9},{14,12},{15,13},... | collective-permute-start | bytes 798728 | tf_op jit(solution)/shard_map/ppermute | solution.py:340
  30.6 2.4 %collective-permute-done.14.got_ref = s16[1040,128]{1,0:T(8,128)(2,1)S(1)} collective-permute-done((s16[1040,128]{1,0:T(8,128)(2,1)S(1)}, s16[1040,128]{1,0:T(8,128)(2,1)S(1)}, u32[]{:S(2)}, u32[]{:S(2)}) %collective-permute-start.14) | collective-permute-done | bytes 266272 | tf_op jit(solution)/shard_map/ppermute | solution.py:340
  33.6 1.7 %collective-permute-start.19 = (s16[1040,128]{1,0:T(8,128)(2,1)S(1)}, s16[1040,128]{1,0:T(8,128)(2,1)S(1)}, u32[]{:S(2)}, u32[]{:S(2)}) collective-permute-start(s16[1040,128]{1,0:T(8,128)(2,1)S(1)} %sum_hop.20.before_ref), channel_id=1, source_target_pairs={{0,2},{1,3},{4,0},{5,1},{8,4},{9,5},{12,8},{13,9},{14,12},{15,13},... | collective-permute-start | bytes 798728 | tf_op jit(solution)/shard_map/ppermute | solution.py:340
  36.3 2.4 %collective-permute-done.16.got_ref = s16[1040,128]{1,0:T(8,128)(2,1)S(1)} collective-permute-done((s16[1040,128]{1,0:T(8,128)(2,1)S(1)}, s16[1040,128]{1,0:T(8,128)(2,1)S(1)}, u32[]{:S(2)}, u32[]{:S(2)}) %collective-permute-start.16) | collective-permute-done | bytes 266272 | tf_op jit(solution)/shard_map/ppermute | solution.py:340
  39.3 1.7 %collective-permute-start.21 = (s16[1040,128]{1,0:T(8,128)(2,1)S(1)}, s16[1040,128]{1,0:T(8,128)(2,1)S(1)}, u32[]{:S(2)}, u32[]{:S(2)}) collective-permute-start(s16[1040,128]{1,0:T(8,128)(2,1)S(1)} %sum_hop.22.before_ref), channel_id=1, source_target_pairs={{0,2},{1,3},{4,0},{5,1},{8,4},{9,5},{12,8},{13,9},{14,12},{15,13},... | collective-permute-start | bytes 798728 | tf_op jit(solution)/shard_map/ppermute | solution.py:340
  42.8 3.7 %collective-permute-done.18.refs_1_ = s16[1040,128]{1,0:T(8,128)(2,1)S(1)} collective-permute-done((s16[1040,128]{1,0:T(8,128)(2,1)S(1)}, s16[1040,128]{1,0:T(8,128)(2,1)S(1)}, u32[]{:S(2)}, u32[]{:S(2)}) %collective-permute-start.18) | collective-permute-done | bytes 266272 | tf_op jit(solution)/shard_map/ppermute | solution.py:340
  46.9 1.6 %collective-permute-start.22 = (bf16[512,256]{1,0:T(8,128)(2,1)S(1)}, bf16[512,256]{1,0:T(8,128)(2,1)S(1)}, u32[]{:S(2)}, u32[]{:S(2)}) collective-permute-start(bf16[512,256]{1,0:T(8,128)(2,1)S(1)} %effect.2.before_ref.refs_0_), channel_id=1, source_target_pairs={{0,2},{1,3},{4,0},{5,1},{8,4},{9,5},{12,8},{13,9},{14,12},{15,13},... | collective-permute-start | bytes 786440 | tf_op jit(solution)/shard_map/ppermute | solution.py:441
  49.0 3.2 %collective-permute-done.20.refs_1_ = s16[1040,128]{1,0:T(8,128)(2,1)S(1)} collective-permute-done((s16[1040,128]{1,0:T(8,128)(2,1)S(1)}, s16[1040,128]{1,0:T(8,128)(2,1)S(1)}, u32[]{:S(2)}, u32[]{:S(2)}) %collective-permute-start.20) | collective-permute-done | bytes 266272 | tf_op jit(solution)/shard_map/ppermute | solution.py:340
  52.6 1.6 %collective-permute-start.24 = (bf16[512,256]{1,0:T(8,128)(2,1)S(1)}, bf16[512,256]{1,0:T(8,128)(2,1)S(1)}, u32[]{:S(2)}, u32[]{:S(2)}) collective-permute-start(bf16[512,256]{1,0:T(8,128)(2,1)S(1)} %effect.3.before_ref.refs_3_), channel_id=1, source_target_pairs={{0,2},{1,3},{4,0},{5,1},{8,4},{9,5},{12,8},{13,9},{14,12},{15,13},... | collective-permute-start | bytes 786440 | tf_op jit(solution)/shard_map/ppermute | solution.py:441
  56.2 1.6 %collective-permute-start.26 = (bf16[512,256]{1,0:T(8,128)(2,1)S(1)}, bf16[512,256]{1,0:T(8,128)(2,1)S(1)}, u32[]{:S(2)}, u32[]{:S(2)}) collective-permute-start(bf16[512,256]{1,0:T(8,128)(2,1)S(1)} %collective-permute-done.22.refs_0_), channel_id=1, source_target_pairs={{0,2},{1,3},{4,0},{5,1},{8,4},{9,5},{12,8},{13,9},{14,12},{15,13},... | collective-permute-start | bytes 786440 | tf_op jit(solution)/shard_map/ppermute | solution.py:441
  59.0 2.8 %collective-permute-done.24.refs_0_ = bf16[512,256]{1,0:T(8,128)(2,1)S(1)} collective-permute-done((bf16[512,256]{1,0:T(8,128)(2,1)S(1)}, bf16[512,256]{1,0:T(8,128)(2,1)S(1)}, u32[]{:S(2)}, u32[]{:S(2)}) %collective-permute-start.24) | collective-permute-done | bytes 262176 | tf_op jit(solution)/shard_map/ppermute | solution.py:441
  61.8 1.6 %collective-permute-start.28 = (bf16[512,256]{1,0:T(8,128)(2,1)S(1)}, bf16[512,256]{1,0:T(8,128)(2,1)S(1)}, u32[]{:S(2)}, u32[]{:S(2)}) collective-permute-start(bf16[512,256]{1,0:T(8,128)(2,1)S(1)} %collective-permute-done.24.refs_0_), channel_id=1, source_target_pairs={{0,2},{1,3},{4,0},{5,1},{8,4},{9,5},{12,8},{13,9},{14,12},{15,13},... | collective-permute-start | bytes 786440 | tf_op jit(solution)/shard_map/ppermute | solution.py:441
  64.7 1.3 %update.2 = (f32[1024,256]{1,0:T(8,128)}, f32[1024,256]{1,0:T(8,128)}, f32[8,128]{1,0:T(8,128)S(1)}) custom-call(f32[384,256]{1,0:T(8,128)S(1)} %get-tuple-element.85.before_ref.refs_3_, f32[256,1024]{1,0:T(8,128)S(1)} %sum_near.1.before_ref.refs_0_, s16[1040,128]{1,0:T(8,128)(2,1)S(1)} %collective-permute-done.18.refs_1_, ...), custom_call_target="tpu_custom_call" | custom-call | flops 1 | bytes 1 | tf_op jit(solution)/shard_map/update/pallas_call | solution.py:378
  66.0 1.4 %collective-permute-done.26.refs_0_ = bf16[512,256]{1,0:T(8,128)(2,1)S(1)} collective-permute-done((bf16[512,256]{1,0:T(8,128)(2,1)S(1)}, bf16[512,256]{1,0:T(8,128)(2,1)S(1)}, u32[]{:S(2)}, u32[]{:S(2)}) %collective-permute-start.26) | collective-permute-done | bytes 262176 | tf_op jit(solution)/shard_map/ppermute | solution.py:441
  67.4 1.6 %collective-permute-start.30 = (bf16[512,256]{1,0:T(8,128)(2,1)S(1)}, bf16[512,256]{1,0:T(8,128)(2,1)S(1)}, u32[]{:S(2)}, u32[]{:S(2)}) collective-permute-start(bf16[512,256]{1,0:T(8,128)(2,1)S(1)} %collective-permute-done.26.refs_0_), channel_id=1, source_target_pairs={{0,2},{1,3},{4,0},{5,1},{8,4},{9,5},{12,8},{13,9},{14,12},{15,13},... | collective-permute-start | bytes 786440 | tf_op jit(solution)/shard_map/ppermute | solution.py:441
  70.3 2.8 %collective-permute-done.28.refs_0_ = bf16[512,256]{1,0:T(8,128)(2,1)S(1)} collective-permute-done((bf16[512,256]{1,0:T(8,128)(2,1)S(1)}, bf16[512,256]{1,0:T(8,128)(2,1)S(1)}, u32[]{:S(2)}, u32[]{:S(2)}) %collective-permute-start.28) | collective-permute-done | bytes 262176 | tf_op jit(solution)/shard_map/ppermute | solution.py:441
  73.1 1.6 %collective-permute-start.32 = (bf16[256,256]{1,0:T(8,128)(2,1)S(1)}, bf16[256,256]{1,0:T(8,128)(2,1)S(1)}, u32[]{:S(2)}, u32[]{:S(2)}) collective-permute-start(bf16[256,256]{1,0:T(8,128)(2,1)S(1)} %slice.24), channel_id=1, source_target_pairs={{0,2},{1,3},{4,0},{5,1},{8,4},{9,5},{12,8},{13,9},{14,12},{15,13},... | collective-permute-start | bytes 393224 | tf_op jit(solution)/shard_map/ppermute | solution.py:435
  76.0 1.3 %collective-permute-start.35 = (bf16[256,256]{1,0:T(8,128)(2,1)S(1)}, bf16[256,256]{1,0:T(8,128)(2,1)S(1)}, u32[]{:S(2)}, u32[]{:S(2)}) collective-permute-start(bf16[256,256]{1,0:T(8,128)(2,1)S(1)} %slice.27), channel_id=1, source_target_pairs={{0,4},{1,5},{4,8},{5,9},{8,12},{9,13},{12,14},{13,15},{14,10},{15,... | collective-permute-start | bytes 393224 | tf_op jit(solution)/shard_map/ppermute | solution.py:438
  77.3 1.3 %update.3 = (f32[1024,256]{1,0:T(8,128)}, f32[1024,256]{1,0:T(8,128)}, f32[8,128]{1,0:T(8,128)S(1)}) custom-call(f32[384,256]{1,0:T(8,128)S(1)} %get-tuple-element.98.before_ref.refs_3_, f32[256,1024]{1,0:T(8,128)S(1)} %sum_near.1.before_ref.refs_0_, ...), custom_call_target="tpu_custom_call", output_to_operand_aliasing={{0}: (8, {}), {1}: (9, {})} | custom-call | flops 1 | bytes 1 | tf_op jit(solution)/shard_map/update/pallas_call | solution.py:378
  78.7 1.6 %collective-permute-start.33 = (bf16[256,256]{1,0:T(8,128)(2,1)S(1)}, bf16[256,256]{1,0:T(8,128)(2,1)S(1)}, u32[]{:S(2)}, u32[]{:S(2)}) collective-permute-start(bf16[256,256]{1,0:T(8,128)(2,1)S(1)} %slice.25), channel_id=1, source_target_pairs={{0,2},{1,3},{4,0},{5,1},{8,4},{9,5},{12,8},{13,9},{14,12},{15,13},... | collective-permute-start | bytes 393224 | tf_op jit(solution)/shard_map/ppermute | solution.py:438
  80.6 1.6 %collective-permute-start.36 = (bf16[256,256]{1,0:T(8,128)(2,1)S(1)}, bf16[256,256]{1,0:T(8,128)(2,1)S(1)}, u32[]{:S(2)}, u32[]{:S(2)}) collective-permute-start(bf16[256,256]{1,0:T(8,128)(2,1)S(1)} %slice.28), channel_id=1, source_target_pairs={{0,2},{1,3},{4,0},{5,1},{8,4},{9,5},{12,8},{13,9},{14,12},{15,13},... | collective-permute-start | bytes 393224 | tf_op jit(solution)/shard_map/ppermute | solution.py:430
  83.9 1.7 %collective-permute-start.38 = (bf16[256,256]{1,0:T(8,128)(2,1)S(1)}, bf16[256,256]{1,0:T(8,128)(2,1)S(1)}, u32[]{:S(2)}, u32[]{:S(2)}) collective-permute-start(bf16[256,256]{1,0:T(8,128)(2,1)S(1)} %collective-permute-done.32.refs_0_), channel_id=1, source_target_pairs={{0,2},{1,3},{4,0},{5,1},{8,4},{9,5},{12,8},{13,9},{14,12},{15,13},... | collective-permute-start | bytes 393224 | tf_op jit(solution)/shard_map/ppermute | solution.py:430
  87.5 2.0 %collective-permute-done.37.refs_0_ = bf16[256,256]{1,0:T(8,128)(2,1)S(1)} collective-permute-done((bf16[256,256]{1,0:T(8,128)(2,1)S(1)}, bf16[256,256]{1,0:T(8,128)(2,1)S(1)}, u32[]{:S(2)}, u32[]{:S(2)}) %collective-permute-start.37) | collective-permute-done | bytes 131104 | tf_op jit(solution)/shard_map/ppermute | solution.py:430
  (126 shorter events, 29.4 us)
Async XLA Ops:
  5.4 7.4 %collective-permute-start.4 = (s16[528,128]{1,0:T(8,128)(2,1)S(1)}, s16[528,128]{1,0:T(8,128)(2,1)S(1)}, u32[]{:S(2)}, u32[]{:S(2)}) collective-permute-start(s16[528,128]{1,0:T(8,128)(2,1)S(1)} %get-tuple-element.74), channel_id=1, source_target_pairs={{0,2},{1,3},{4,0},{5,1},{8,4},{9,5},{12,8},{13,9},{14,12},{15,13},... | collective-permute-start | bytes 405512 | tf_op jit(solution)/shard_map/ppermute | solution.py:323
  8.4 7.0 %collective-permute-start.5 = (s16[528,128]{1,0:T(8,128)(2,1)S(1)}, s16[528,128]{1,0:T(8,128)(2,1)S(1)}, u32[]{:S(2)}, u32[]{:S(2)}) collective-permute-start(s16[528,128]{1,0:T(8,128)(2,1)S(1)} %get-tuple-element.69.before_ref), channel_id=1, source_target_pairs={{0,4},{1,5},{4,8},{5,9},{8,12},{9,13},{12,14},{13,15},{14,10},{15,... | collective-permute-start | bytes 405512 | tf_op jit(solution)/shard_map/ppermute | solution.py:322
  9.1 7.3 %collective-permute-start.7 = (s16[528,128]{1,0:T(8,128)(2,1)S(1)}, s16[528,128]{1,0:T(8,128)(2,1)S(1)}, u32[]{:S(2)}, u32[]{:S(2)}) collective-permute-start(s16[528,128]{1,0:T(8,128)(2,1)S(1)} %get-tuple-element.76), channel_id=1, source_target_pairs={{0,2},{1,3},{4,0},{5,1},{8,4},{9,5},{12,8},{13,9},{14,12},{15,13},... | collective-permute-start | bytes 405512 | tf_op jit(solution)/shard_map/ppermute | solution.py:323
  11.0 8.0 %collective-permute-start.8 = (s16[528,128]{1,0:T(8,128)(2,1)S(1)}, s16[528,128]{1,0:T(8,128)(2,1)S(1)}, u32[]{:S(2)}, u32[]{:S(2)}) collective-permute-start(s16[528,128]{1,0:T(8,128)(2,1)S(1)} %get-tuple-element.73.refs_0_), channel_id=1, source_target_pairs={{0,4},{1,5},{4,8},{5,9},{8,12},{9,13},{12,14},{13,15},{14,10},{15,... | collective-permute-start | bytes 405512 | tf_op jit(solution)/shard_map/ppermute | solution.py:322
  13.4 8.2 %collective-permute-start.9 = (s16[1040,128]{1,0:T(8,128)(2,1)S(1)}, s16[1040,128]{1,0:T(8,128)(2,1)S(1)}, u32[]{:S(2)}, u32[]{:S(2)}) collective-permute-start(s16[1040,128]{1,0:T(8,128)(2,1)S(1)} %sum_hop.12.before_ref), channel_id=1, source_target_pairs={{0,2},{1,3},{4,0},{5,1},{8,4},{9,5},{12,8},{13,9},{14,12},{15,13},... | collective-permute-start | bytes 798728 | tf_op jit(solution)/shard_map/ppermute | solution.py:340
  16.0 7.9 %collective-permute-start.10 = (s16[1040,128]{1,0:T(8,128)(2,1)S(1)}, s16[1040,128]{1,0:T(8,128)(2,1)S(1)}, u32[]{:S(2)}, u32[]{:S(2)}) collective-permute-start(s16[1040,128]{1,0:T(8,128)(2,1)S(1)} %sum_hop.13.refs_0_), channel_id=1, source_target_pairs={{0,4},{1,5},{4,8},{5,9},{8,12},{9,13},{12,14},{13,15},{14,10},{15,... | collective-permute-start | bytes 798728 | tf_op jit(solution)/shard_map/ppermute | solution.py:340
  16.3 16.7 %collective-permute-start.13 = (bf16[3,384,1024]{2,1,0:T(8,128)(2,1)S(1)}, bf16[3,384,1024]{2,1,0:T(8,128)(2,1)S(1)}, u32[]{:S(2)}, u32[]{:S(2)}) collective-permute-start(bf16[3,384,1024]{2,1,0:T(8,128)(2,1)S(1)} %pick_blocks.7.before_ref), channel_id=1, source_target_pairs={{0,1},{1,0},{2,3},{3,2},{4,5},{5,4},{6,7},{7,6},{8,9},{9,8},{10,11... | collective-permute-start | bytes 7077896 | tf_op jit(solution)/shard_map/ppermute | solution.py:273
  17.0 10.3 %collective-permute-start.11 = (s16[1040,128]{1,0:T(8,128)(2,1)S(1)}, s16[1040,128]{1,0:T(8,128)(2,1)S(1)}, u32[]{:S(2)}, u32[]{:S(2)}) collective-permute-start(s16[1040,128]{1,0:T(8,128)(2,1)S(1)} %sum_hop.14.before_ref), channel_id=1, source_target_pairs={{0,2},{1,3},{4,0},{5,1},{8,4},{9,5},{12,8},{13,9},{14,12},{15,13},... | collective-permute-start | bytes 798728 | tf_op jit(solution)/shard_map/ppermute | solution.py:340
  19.5 10.1 %collective-permute-start.12 = (s16[1040,128]{1,0:T(8,128)(2,1)S(1)}, s16[1040,128]{1,0:T(8,128)(2,1)S(1)}, u32[]{:S(2)}, u32[]{:S(2)}) collective-permute-start(s16[1040,128]{1,0:T(8,128)(2,1)S(1)} %sum_hop.15.before_ref), channel_id=1, source_target_pairs={{0,4},{1,5},{4,8},{5,9},{8,12},{9,13},{12,14},{13,15},{14,10},{15,... | collective-permute-start | bytes 798728 | tf_op jit(solution)/shard_map/ppermute | solution.py:340
  22.2 10.8 %collective-permute-start.14 = (s16[1040,128]{1,0:T(8,128)(2,1)S(1)}, s16[1040,128]{1,0:T(8,128)(2,1)S(1)}, u32[]{:S(2)}, u32[]{:S(2)}) collective-permute-start(s16[1040,128]{1,0:T(8,128)(2,1)S(1)} %sum_hop.16.before_ref), channel_id=1, source_target_pairs={{0,2},{1,3},{4,0},{5,1},{8,4},{9,5},{12,8},{13,9},{14,12},{15,13},... | collective-permute-start | bytes 798728 | tf_op jit(solution)/shard_map/ppermute | solution.py:340
  24.5 10.9 %collective-permute-start.15 = (s16[1040,128]{1,0:T(8,128)(2,1)S(1)}, s16[1040,128]{1,0:T(8,128)(2,1)S(1)}, u32[]{:S(2)}, u32[]{:S(2)}) collective-permute-start(s16[1040,128]{1,0:T(8,128)(2,1)S(1)} %sum_hop.17.before_ref), channel_id=1, source_target_pairs={{0,4},{1,5},{4,8},{5,9},{8,12},{9,13},{12,14},{13,15},{14,10},{15,... | collective-permute-start | bytes 798728 | tf_op jit(solution)/shard_map/ppermute | solution.py:340
  27.9 10.9 %collective-permute-start.16 = (s16[1040,128]{1,0:T(8,128)(2,1)S(1)}, s16[1040,128]{1,0:T(8,128)(2,1)S(1)}, u32[]{:S(2)}, u32[]{:S(2)}) collective-permute-start(s16[1040,128]{1,0:T(8,128)(2,1)S(1)} %sum_hop.18.before_ref), channel_id=1, source_target_pairs={{0,2},{1,3},{4,0},{5,1},{8,4},{9,5},{12,8},{13,9},{14,12},{15,13},... | collective-permute-start | bytes 798728 | tf_op jit(solution)/shard_map/ppermute | solution.py:340
  30.2 10.8 %collective-permute-start.17 = (s16[1040,128]{1,0:T(8,128)(2,1)S(1)}, s16[1040,128]{1,0:T(8,128)(2,1)S(1)}, u32[]{:S(2)}, u32[]{:S(2)}) collective-permute-start(s16[1040,128]{1,0:T(8,128)(2,1)S(1)} %sum_hop.19.before_ref), channel_id=1, source_target_pairs={{0,4},{1,5},{4,8},{5,9},{8,12},{9,13},{12,14},{13,15},{14,10},{15,... | collective-permute-start | bytes 798728 | tf_op jit(solution)/shard_map/ppermute | solution.py:340
  33.6 12.9 %collective-permute-start.19 = (s16[1040,128]{1,0:T(8,128)(2,1)S(1)}, s16[1040,128]{1,0:T(8,128)(2,1)S(1)}, u32[]{:S(2)}, u32[]{:S(2)}) collective-permute-start(s16[1040,128]{1,0:T(8,128)(2,1)S(1)} %sum_hop.20.before_ref), channel_id=1, source_target_pairs={{0,2},{1,3},{4,0},{5,1},{8,4},{9,5},{12,8},{13,9},{14,12},{15,13},... | collective-permute-start | bytes 798728 | tf_op jit(solution)/shard_map/ppermute | solution.py:340
  35.9 10.6 %collective-permute-start.18 = (s16[1040,128]{1,0:T(8,128)(2,1)S(1)}, s16[1040,128]{1,0:T(8,128)(2,1)S(1)}, u32[]{:S(2)}, u32[]{:S(2)}) collective-permute-start(s16[1040,128]{1,0:T(8,128)(2,1)S(1)} %sum_hop.21.before_ref), channel_id=1, source_target_pairs={{0,4},{1,5},{4,8},{5,9},{8,12},{9,13},{12,14},{13,15},{14,10},{15,... | collective-permute-start | bytes 798728 | tf_op jit(solution)/shard_map/ppermute | solution.py:340
  39.3 12.9 %collective-permute-start.21 = (s16[1040,128]{1,0:T(8,128)(2,1)S(1)}, s16[1040,128]{1,0:T(8,128)(2,1)S(1)}, u32[]{:S(2)}, u32[]{:S(2)}) collective-permute-start(s16[1040,128]{1,0:T(8,128)(2,1)S(1)} %sum_hop.22.before_ref), channel_id=1, source_target_pairs={{0,2},{1,3},{4,0},{5,1},{8,4},{9,5},{12,8},{13,9},{14,12},{15,13},... | collective-permute-start | bytes 798728 | tf_op jit(solution)/shard_map/ppermute | solution.py:340
  41.7 10.5 %collective-permute-start.20 = (s16[1040,128]{1,0:T(8,128)(2,1)S(1)}, s16[1040,128]{1,0:T(8,128)(2,1)S(1)}, u32[]{:S(2)}, u32[]{:S(2)}) collective-permute-start(s16[1040,128]{1,0:T(8,128)(2,1)S(1)} %sum_hop.23.before_ref), channel_id=1, source_target_pairs={{0,4},{1,5},{4,8},{5,9},{8,12},{9,13},{12,14},{13,15},{14,10},{15,... | collective-permute-start | bytes 798728 | tf_op jit(solution)/shard_map/ppermute | solution.py:340
  46.9 9.3 %collective-permute-start.22 = (bf16[512,256]{1,0:T(8,128)(2,1)S(1)}, bf16[512,256]{1,0:T(8,128)(2,1)S(1)}, u32[]{:S(2)}, u32[]{:S(2)}) collective-permute-start(bf16[512,256]{1,0:T(8,128)(2,1)S(1)} %effect.2.before_ref.refs_0_), channel_id=1, source_target_pairs={{0,2},{1,3},{4,0},{5,1},{8,4},{9,5},{12,8},{13,9},{14,12},{15,13},... | collective-permute-start | bytes 786440 | tf_op jit(solution)/shard_map/ppermute | solution.py:441
  48.5 9.6 %collective-permute-start.23 = (bf16[512,256]{1,0:T(8,128)(2,1)S(1)}, bf16[512,256]{1,0:T(8,128)(2,1)S(1)}, u32[]{:S(2)}, u32[]{:S(2)}) collective-permute-start(bf16[512,256]{1,0:T(8,128)(2,1)S(1)} %effect.2.before_ref.refs_0_), channel_id=1, source_target_pairs={{0,4},{1,5},{4,8},{5,9},{8,12},{9,13},{12,14},{13,15},{14,10},{15,... | collective-permute-start | bytes 786440 | tf_op jit(solution)/shard_map/ppermute | solution.py:441
  52.6 9.2 %collective-permute-start.24 = (bf16[512,256]{1,0:T(8,128)(2,1)S(1)}, bf16[512,256]{1,0:T(8,128)(2,1)S(1)}, u32[]{:S(2)}, u32[]{:S(2)}) collective-permute-start(bf16[512,256]{1,0:T(8,128)(2,1)S(1)} %effect.3.before_ref.refs_3_), channel_id=1, source_target_pairs={{0,2},{1,3},{4,0},{5,1},{8,4},{9,5},{12,8},{13,9},{14,12},{15,13},... | collective-permute-start | bytes 786440 | tf_op jit(solution)/shard_map/ppermute | solution.py:441
  54.2 9.6 %collective-permute-start.25 = (bf16[512,256]{1,0:T(8,128)(2,1)S(1)}, bf16[512,256]{1,0:T(8,128)(2,1)S(1)}, u32[]{:S(2)}, u32[]{:S(2)}) collective-permute-start(bf16[512,256]{1,0:T(8,128)(2,1)S(1)} %effect.3.before_ref.refs_3_), channel_id=1, source_target_pairs={{0,4},{1,5},{4,8},{5,9},{8,12},{9,13},{12,14},{13,15},{14,10},{15,... | collective-permute-start | bytes 786440 | tf_op jit(solution)/shard_map/ppermute | solution.py:441
  56.2 11.2 %collective-permute-start.26 = (bf16[512,256]{1,0:T(8,128)(2,1)S(1)}, bf16[512,256]{1,0:T(8,128)(2,1)S(1)}, u32[]{:S(2)}, u32[]{:S(2)}) collective-permute-start(bf16[512,256]{1,0:T(8,128)(2,1)S(1)} %collective-permute-done.22.refs_0_), channel_id=1, source_target_pairs={{0,2},{1,3},{4,0},{5,1},{8,4},{9,5},{12,8},{13,9},{14,12},{15,13},... | collective-permute-start | bytes 786440 | tf_op jit(solution)/shard_map/ppermute | solution.py:441
  58.2 11.2 %collective-permute-start.27 = (bf16[512,256]{1,0:T(8,128)(2,1)S(1)}, bf16[512,256]{1,0:T(8,128)(2,1)S(1)}, u32[]{:S(2)}, u32[]{:S(2)}) collective-permute-start(bf16[512,256]{1,0:T(8,128)(2,1)S(1)} %collective-permute-done.23.refs_0_), channel_id=1, source_target_pairs={{0,4},{1,5},{4,8},{5,9},{8,12},{9,13},{12,14},{13,15},{14,10},{15,... | collective-permute-start | bytes 786440 | tf_op jit(solution)/shard_map/ppermute | solution.py:441
  61.8 11.2 %collective-permute-start.28 = (bf16[512,256]{1,0:T(8,128)(2,1)S(1)}, bf16[512,256]{1,0:T(8,128)(2,1)S(1)}, u32[]{:S(2)}, u32[]{:S(2)}) collective-permute-start(bf16[512,256]{1,0:T(8,128)(2,1)S(1)} %collective-permute-done.24.refs_0_), channel_id=1, source_target_pairs={{0,2},{1,3},{4,0},{5,1},{8,4},{9,5},{12,8},{13,9},{14,12},{15,13},... | collective-permute-start | bytes 786440 | tf_op jit(solution)/shard_map/ppermute | solution.py:441
  63.8 11.3 %collective-permute-start.29 = (bf16[512,256]{1,0:T(8,128)(2,1)S(1)}, bf16[512,256]{1,0:T(8,128)(2,1)S(1)}, u32[]{:S(2)}, u32[]{:S(2)}) collective-permute-start(bf16[512,256]{1,0:T(8,128)(2,1)S(1)} %collective-permute-done.25.refs_0_), channel_id=1, source_target_pairs={{0,4},{1,5},{4,8},{5,9},{8,12},{9,13},{12,14},{13,15},{14,10},{15,... | collective-permute-start | bytes 786440 | tf_op jit(solution)/shard_map/ppermute | solution.py:441
  67.4 11.2 %collective-permute-start.30 = (bf16[512,256]{1,0:T(8,128)(2,1)S(1)}, bf16[512,256]{1,0:T(8,128)(2,1)S(1)}, u32[]{:S(2)}, u32[]{:S(2)}) collective-permute-start(bf16[512,256]{1,0:T(8,128)(2,1)S(1)} %collective-permute-done.26.refs_0_), channel_id=1, source_target_pairs={{0,2},{1,3},{4,0},{5,1},{8,4},{9,5},{12,8},{13,9},{14,12},{15,13},... | collective-permute-start | bytes 786440 | tf_op jit(solution)/shard_map/ppermute | solution.py:441
  69.4 11.2 %collective-permute-start.31 = (bf16[512,256]{1,0:T(8,128)(2,1)S(1)}, bf16[512,256]{1,0:T(8,128)(2,1)S(1)}, u32[]{:S(2)}, u32[]{:S(2)}) collective-permute-start(bf16[512,256]{1,0:T(8,128)(2,1)S(1)} %collective-permute-done.27.refs_0_), channel_id=1, source_target_pairs={{0,4},{1,5},{4,8},{5,9},{8,12},{9,13},{12,14},{13,15},{14,10},{15,... | collective-permute-start | bytes 786440 | tf_op jit(solution)/shard_map/ppermute | solution.py:441
  73.1 10.8 %collective-permute-start.32 = (bf16[256,256]{1,0:T(8,128)(2,1)S(1)}, bf16[256,256]{1,0:T(8,128)(2,1)S(1)}, u32[]{:S(2)}, u32[]{:S(2)}) collective-permute-start(bf16[256,256]{1,0:T(8,128)(2,1)S(1)} %slice.24), channel_id=1, source_target_pairs={{0,2},{1,3},{4,0},{5,1},{8,4},{9,5},{12,8},{13,9},{14,12},{15,13},... | collective-permute-start | bytes 393224 | tf_op jit(solution)/shard_map/ppermute | solution.py:435
  75.5 7.6 %collective-permute-start.34 = (bf16[256,256]{1,0:T(8,128)(2,1)S(1)}, bf16[256,256]{1,0:T(8,128)(2,1)S(1)}, u32[]{:S(2)}, u32[]{:S(2)}) collective-permute-start(bf16[256,256]{1,0:T(8,128)(2,1)S(1)} %slice.26), channel_id=1, source_target_pairs={{0,4},{1,5},{4,8},{5,9},{8,12},{9,13},{12,14},{13,15},{14,10},{15,... | collective-permute-start | bytes 393224 | tf_op jit(solution)/shard_map/ppermute | solution.py:435
  76.0 10.8 %collective-permute-start.35 = (bf16[256,256]{1,0:T(8,128)(2,1)S(1)}, bf16[256,256]{1,0:T(8,128)(2,1)S(1)}, u32[]{:S(2)}, u32[]{:S(2)}) collective-permute-start(bf16[256,256]{1,0:T(8,128)(2,1)S(1)} %slice.27), channel_id=1, source_target_pairs={{0,4},{1,5},{4,8},{5,9},{8,12},{9,13},{12,14},{13,15},{14,10},{15,... | collective-permute-start | bytes 393224 | tf_op jit(solution)/shard_map/ppermute | solution.py:438
  78.7 6.9 %collective-permute-start.33 = (bf16[256,256]{1,0:T(8,128)(2,1)S(1)}, bf16[256,256]{1,0:T(8,128)(2,1)S(1)}, u32[]{:S(2)}, u32[]{:S(2)}) collective-permute-start(bf16[256,256]{1,0:T(8,128)(2,1)S(1)} %slice.25), channel_id=1, source_target_pairs={{0,2},{1,3},{4,0},{5,1},{8,4},{9,5},{12,8},{13,9},{14,12},{15,13},... | collective-permute-start | bytes 393224 | tf_op jit(solution)/shard_map/ppermute | solution.py:438
  80.6 6.6 %collective-permute-start.36 = (bf16[256,256]{1,0:T(8,128)(2,1)S(1)}, bf16[256,256]{1,0:T(8,128)(2,1)S(1)}, u32[]{:S(2)}, u32[]{:S(2)}) collective-permute-start(bf16[256,256]{1,0:T(8,128)(2,1)S(1)} %slice.28), channel_id=1, source_target_pairs={{0,2},{1,3},{4,0},{5,1},{8,4},{9,5},{12,8},{13,9},{14,12},{15,13},... | collective-permute-start | bytes 393224 | tf_op jit(solution)/shard_map/ppermute | solution.py:430
  (22 other events, 88.6 us)
